TPU v7x, 32 devices: a whole 2x2x4 slice. The times are simulated.
32 devices in a mesh: grp: 2 (over y), gx: 4 (over z), gy: 2 (over x), gz: 2 (over core).
Axes of the slice: x: 2, y: 2, z: 4, core: 2. Of those that a mesh axis runs over, the one named last changes fastest.
Arguments:
- tokens: bfloat16 [72, 8192], P(('grp', 'gy', 'gz'), 'gx'), parts along dimension 0, may hold values from -6 to 6
- gate_weight: bfloat16 [8192, 26624], P('gx', ('gy', 'gz')), may hold values from -0.0625 to 0.0625
- up_weight: bfloat16 [8192, 26624], P('gx', ('gy', 'gz')), may hold values from -0.0625 to 0.0625
- down_weight: bfloat16 [26624, 8192], P(('gy', 'gz'), 'gx'), may hold values from -0.0390625 to 0.0390625
Outputs:
- mixed: bfloat16 [72, 8192], P(('grp', 'gy', 'gz'), 'gx'), parts along dimension 0
There are 2 independent parts, one for each index of `grp`. A program takes and returns all parts, laid end to end along the dimension named above; an argument that names none is the same for every part. Nothing has to cross between parts.
All inputs are finite; a program needn't handle non-finite values.
Results may differ from a plain program's by a relative error of at most 0.019.
Values may be sent and summed in bfloat16 or wider, within the bound.
No kernel may reach another device: no remote copies, remote signals or barrier semaphores. Data moves between devices by JAX's collectives and lax.ppermute only.
A program may use at most 192 MiB of HBM per device.

v0:
```python
import jax
import jax.numpy as jnp
from jax import lax
from jax.sharding import PartitionSpec as P


def activate(gate, up):
    return (jax.nn.silu(gate) * up).astype(jnp.bfloat16)


def shards(tokens, gate_weight, up_weight, down_weight):
    features = lax.all_gather(tokens, ("gy", "gz"), axis=0, tiled=True)
    hidden_width = gate_weight.shape[1]
    gate_part = jnp.dot(features, gate_weight, preferred_element_type=jnp.float32)
    up_part = jnp.dot(features, up_weight, preferred_element_type=jnp.float32)
    summed = lax.psum(
        jnp.concatenate([gate_part, up_part], axis=1).astype(jnp.bfloat16), "gx"
    ).astype(jnp.float32)
    hidden = activate(summed[:, :hidden_width], summed[:, hidden_width:])
    partial_value = jnp.dot(hidden, down_weight, preferred_element_type=jnp.float32)
    return lax.psum_scatter(
        partial_value.astype(jnp.bfloat16), ("gy", "gz"), scatter_dimension=0, tiled=True
    )


def solution(mesh):
    return jax.shard_map(
        shards,
        mesh=mesh,
        in_specs=(
            P(("grp", "gy", "gz"), "gx"),
            P("gx", ("gy", "gz")),
            P("gx", ("gy", "gz")),
            P(("gy", "gz"), "gx"),
        ),
        out_specs=P(("grp", "gy", "gz"), "gx"),
        check_vma=False,
    )
```

profile of v0, /device:TPU:0, one launch (start us, length us, event | category | flops | bytes accessed | tf_op | source)
XLA Modules:
  0.0 144.6 jit_solution(15893588462923963197)
XLA Ops:
  6.5 0.0 all-reduce.4.cloned.1.call-start
  6.5 7.4 %all-gather = bf16[4,9,2048]{2,1,0:T(8,128)(2,1)S(1)} all-gather(bf16[1,9,2048]{2,1,0:T(8,128)(2,1)} %bitcast.7), channel_id=1, replica_groups=mesh['grp'=2,'gx'=4,'gy'=2,'gz'=2] {'gy','gz'}, dimensions={0}, use_global_device_ids=true | all-gather | bytes 184320 | tf_op jit(solution)/shard_map/all_gather | solution.py:12
  13.9 0.1 reshape.1
  14.0 11.3 %convolution_convert_fusion = bf16[36,6656]{1,0:T(8,128)(2,1)S(1)} fusion(bf16[36,2048]{1,0:T(8,128)(2,1)S(1)} %reshape.1, bf16[2048,6656]{1,0:T(8,128)(2,1)} %param.6), kind=kOutput, calls=%fused_computation | convolution fusion | flops 981706752 | bytes 27889664 | tf_op jit(solution)/shard_map/dot_general | solution.py:15
  25.3 11.3 %convolution_convert_fusion.1 = bf16[36,6656]{1,0:T(8,128)(2,1)S(1)} fusion(bf16[36,2048]{1,0:T(8,128)(2,1)S(1)} %reshape.1, bf16[2048,6656]{1,0:T(8,128)(2,1)} %param.5), kind=kOutput, calls=%fused_computation.1 | convolution fusion | flops 981706752 | bytes 27889664 | tf_op jit(solution)/shard_map/dot_general | solution.py:14
  36.5 1.1 pad_maximum_fusion
  37.6 0.0 all-reduce.4.cloned.1.call-update
  37.6 0.0 all-reduce.6.cloned.1.call-start
  37.7 54.1 %all-reduce.4.cloned.1.call-done = bf16[36,13312]{1,0:T(8,128)(2,1)} async-done(((bf16[36,13312]{1,0:T(8,128)(2,1)}), bf16[36,13312]{1,0:T(8,128)(2,1)}) %all-reduce.4.cloned.1.call-update) | async-done | bytes 958480 | tf_op jit(solution)/shard_map/psum | solution.py:16
  91.8 1.4 convert_element_type.10
  93.1 0.0 copy-start
  93.2 11.9 %convolution_convert_fusion.2 = bf16[36,2048]{1,0:T(8,128)(2,1)} fusion(bf16[6656,2048]{1,0:T(8,128)(2,1)} %param.7, f32[36,13312]{1,0:T(8,128)S(1)} %convert_element_type.10), kind=kOutput, calls=%fused_computation.2 | convolution fusion | flops 982978560 | bytes 29327360 | tf_op jit(solution)/shard_map/dot_general | solution.py:20
  105.0 0.0 all-reduce.6.cloned.1.call-update
  105.1 0.0 copy-done
  105.1 0.6 dynamic-slice
  106.3 29.9 %all-reduce.6.cloned.1.call-done = bf16[36,2048]{1,0:T(8,128)(2,1)} async-done(((bf16[36,2048]{1,0:T(8,128)(2,1)}), bf16[36,2048]{1,0:T(8,128)(2,1)}) %all-reduce.6.cloned.1.call-update) | async-done | bytes 147472
  136.2 1.5 %constant_dynamic-slice_fusion = bf16[9,2048]{1,0:T(8,128)(2,1)} fusion(bf16[36,2048]{1,0:T(8,128)(2,1)} %all-reduce.6.cloned.1.call-done, u32[]{:T(128)S(6)} %multiply.1), kind=kLoop, calls=%fused_computation.7 | loop fusion | bytes 73732
Async XLA Ops:
  6.5 85.2 %all-reduce.4.cloned.1.call-start = ((), (), s32[]{:S(2)}) async-start(), calls=%async_computation | async-start | bytes 2129920 | tf_op jit(solution)/shard_map/psum | solution.py:16
  37.6 98.6 %all-reduce.6.cloned.1.call-start = ((), (), s32[]{:S(2)}) async-start(), calls=%async_computation.1 | async-start | bytes 327680
  93.1 11.9 %copy-start = (u32[32]{0:T(128)S(1)}, u32[32]{0:T(128)}, u32[]{:S(2)}) copy-start(u32[32]{0:T(128)} %constant.6) | copy-start | bytes 388
Sparse Core Ops, SparseCore 0:
  37.8 53.9 all-reduce.3
  105.2 30.9 all-reduce.5
where the time goes:
time: 145 us
  waiting for transfers between devices  84 us (58%)
  matrix products  34.4 us (24%)
  between operations  14.1 us (10%)
  blocking collectives  7.39 us (5%)
  other arithmetic  2.46 us (2%)
  local copies, waits for them, and re-layouts  2.2 us (2%)
    psum x1, waiting for transfers between devices, shards(): lax.psum(jnp.concatenate([gate_part, up_part], axis=1).astype(jnp.bfloat1...  54.1 us
    unnamed x3, waiting for transfers between devices  29.9 us
    dot_general x1, matrix products, shards(): jnp.dot(hidden, down_weight, preferred_element_type=jnp.float32)  11.9 us
    dot_general x1, matrix products, shards(): up_part = jnp.dot(features, up_weight, preferred_element_type=jnp.float32)  11.3 us
    dot_general x1, matrix products, shards(): jnp.dot(features, gate_weight, preferred_element_type=jnp.float32)  11.3 us
    all_gather x1, blocking collectives, shards(): features = lax.all_gather(tokens, ('gy', 'gz'), axis=0, tiled=True)  7.39 us
  transfers between devices with their start and end apart: 2, of which 2 were waited for; matrix products, arithmetic and copies ran while one was open for 0% of the time, Pallas kernels for 0%

commit v1 on v0

v1 whole, which is shorter than its diff:
```python
import functools

import jax
import jax.numpy as jnp
from jax import lax
from jax.experimental import pallas as pl
from jax.experimental.pallas import tpu as pltpu
from jax.sharding import PartitionSpec as P

MIB = 1 << 20
TOKEN_AXES = ("gy", "gz")
ANY = pl.BlockSpec(memory_space=pl.ANY)
WHOLE = pl.BlockSpec(memory_space=pltpu.VMEM)
SCALARS = pl.BlockSpec(memory_space=pltpu.SMEM)


def activate(gate, up):
    return (jax.nn.silu(gate) * up).astype(jnp.bfloat16)


def pieces_of(total, step):
    return [(start, min(step, total - start)) for start in range(0, total, step)]


def gate_up_kernel(width, depth_step, starts, x_ref, gate_ref, up_ref, _, *rest):
    outs, (held, total, sems) = rest[:-3], rest[-3:]
    blocks = len(outs)
    parts = pieces_of(x_ref.shape[1], depth_step)
    copies = []
    for b in range(blocks):
        columns = pl.ds(pl.multiple_of(starts[b], 128), width)
        for k, (row, rows) in enumerate(parts):
            for w, weight in enumerate((gate_ref, up_ref)):
                copy = pltpu.make_async_copy(
                    weight.at[pl.ds(row, rows), columns],
                    held.at[b, w, pl.ds(row, rows)],
                    sems.at[b, w, k],
                )
                copy.start()
                copies.append((b, w, k, row, rows, copy))
    for b, w, k, row, rows, copy in copies:
        copy.wait()
        term = jnp.dot(
            x_ref[:, row : row + rows],
            held[b, w, row : row + rows, :],
            preferred_element_type=jnp.float32,
        )
        if k == 0:
            total[w] = term
        elif k < len(parts) - 1:
            total[w] += term
        else:
            outs[b][:, w * width : (w + 1) * width] = (total[w] + term).astype(jnp.bfloat16)


def gate_up(features, gate_weight, up_weight, starts, width, after):
    rows, depth = features.shape
    blocks = starts.shape[0]
    step = 256
    return pl.pallas_call(
        functools.partial(gate_up_kernel, width, step),
        out_shape=[jax.ShapeDtypeStruct((rows, 2 * width), jnp.bfloat16)] * blocks,
        in_specs=[SCALARS, WHOLE, ANY, ANY, ANY],
        out_specs=[WHOLE] * blocks,
        scratch_shapes=[
            pltpu.VMEM((blocks, 2, depth, width), jnp.bfloat16),
            pltpu.VMEM((2, rows, width), jnp.float32),
            pltpu.SemaphoreType.DMA((blocks, 2, len(pieces_of(depth, step)))),
        ],
        compiler_params=pltpu.CompilerParams(vmem_limit_bytes=48 * MIB),
        cost_estimate=pl.CostEstimate(
            flops=4 * rows * depth * width * blocks,
            bytes_accessed=4 * depth * width * blocks,
            transcendentals=0,
        ),
    )(starts, features, gate_weight, up_weight, after)


def down_kernel(first, depth_step, starts, *refs):
    blocks = starts.shape[0]
    hidden, refs = refs[:blocks], refs[blocks:]
    if not first:
        before, refs = refs[0], refs[1:]
    down_ref, outs, (held, total, sems) = refs[0], refs[1:-3], refs[-3:]
    width = hidden[0].shape[1]
    parts = pieces_of(width, depth_step)
    copies = []
    for b in range(blocks):
        for k, (row, rows) in enumerate(parts):
            source = pl.ds(pl.multiple_of(starts[b] + row, 128), rows)
            copy = pltpu.make_async_copy(
                down_ref.at[source], held.at[b, pl.ds(row, rows)], sems.at[b, k]
            )
            copy.start()
            copies.append((b, row, rows, copy))
    if first:
        total[...] = jnp.zeros_like(total)
    else:
        total[...] = before[...]
    for b, row, rows, copy in copies:
        copy.wait()
        total[...] += jnp.dot(
            hidden[b][:, row : row + rows],
            held[b, row : row + rows, :],
            preferred_element_type=jnp.float32,
        )
    if len(outs) == 1:
        outs[0][...] = total[...]
    else:
        tall = outs[0].shape[0]
        for r, out in enumerate(outs):
            out[...] = total[r * tall : (r + 1) * tall, :].astype(out.dtype)


def down(hidden, starts, before, down_weight, outs):
    rows, width = hidden[0].shape
    columns = down_weight.shape[1]
    blocks = len(hidden)
    step = 256
    if outs == 1:
        shapes = [jax.ShapeDtypeStruct((rows, columns), jnp.float32)]
    else:
        shapes = [jax.ShapeDtypeStruct((rows // outs, columns), jnp.bfloat16)] * outs
    carried = [] if before is None else [before]
    return pl.pallas_call(
        functools.partial(down_kernel, before is None, step),
        out_shape=shapes,
        in_specs=[SCALARS] + [WHOLE] * (blocks + len(carried)) + [ANY],
        out_specs=[WHOLE] * outs,
        scratch_shapes=[
            pltpu.VMEM((blocks, width, columns), jnp.bfloat16),
            pltpu.VMEM((rows, columns), jnp.float32),
            pltpu.SemaphoreType.DMA((blocks, len(pieces_of(width, step)))),
        ],
        compiler_params=pltpu.CompilerParams(vmem_limit_bytes=48 * MIB),
        cost_estimate=pl.CostEstimate(
            flops=2 * rows * columns * width * blocks,
            bytes_accessed=2 * columns * width * blocks,
            transcendentals=0,
        ),
    )(starts, *hidden, *carried, down_weight)


def swap(value, axes, size, distance):
    return lax.ppermute(value, axes, [(i, i ^ distance) for i in range(size)])


def direct(tokens, gate_weight, up_weight, down_weight):
    n_gx = lax.axis_size("gx")
    n_token = lax.axis_size(TOKEN_AXES)
    me = lax.axis_index("gx")
    width = gate_weight.shape[1] // n_gx
    features = jnp.concatenate(
        [tokens] + [swap(tokens, TOKEN_AXES, n_token, r) for r in range(1, n_token)], axis=0
    )

    def starts_of(distances):
        return jnp.stack([(me ^ d) * width for d in distances]).astype(jnp.int32)

    received = []
    after = tokens
    for d in range(n_gx - 1, 0, -1):
        (block,) = gate_up(features, gate_weight, up_weight, starts_of([d]), width, after)
        received.append(swap(block, "gx", n_gx, d))
        after = block
    (own,) = gate_up(features, gate_weight, up_weight, starts_of([0]), width, after)
    summed = own.astype(jnp.float32)
    for block in received:
        summed = summed + block.astype(jnp.float32)
    hidden = activate(summed[:, :width], summed[:, width:])

    blocks = [hidden] + [swap(hidden, "gx", n_gx, d) for d in range(1, n_gx)]
    half = n_gx // 2
    (partial_sum,) = down(blocks[:half], starts_of(range(half)), None, down_weight, 1)
    outs = down(blocks[half:], starts_of(range(half, n_gx)), partial_sum, down_weight, n_token)
    result = outs[0].astype(jnp.float32)
    for r in range(1, n_token):
        result = result + swap(outs[r], TOKEN_AXES, n_token, r).astype(jnp.float32)
    return result.astype(jnp.bfloat16)


def offloaded(tokens, gate_weight, up_weight, down_weight):
    features = lax.all_gather(tokens, TOKEN_AXES, axis=0, tiled=True)
    hidden_width = gate_weight.shape[1]
    gate_part = jnp.dot(features, gate_weight, preferred_element_type=jnp.float32)
    up_part = jnp.dot(features, up_weight, preferred_element_type=jnp.float32)
    summed = lax.psum(
        jnp.concatenate([gate_part, up_part], axis=1).astype(jnp.bfloat16), "gx"
    ).astype(jnp.float32)
    hidden = activate(summed[:, :hidden_width], summed[:, hidden_width:])
    partial_value = jnp.dot(hidden, down_weight, preferred_element_type=jnp.float32)
    return lax.psum_scatter(
        partial_value.astype(jnp.bfloat16), TOKEN_AXES, scatter_dimension=0, tiled=True
    )


def shards(tokens, gate_weight, up_weight, down_weight):
    n_gx = lax.axis_size("gx")
    n_token = lax.axis_size(TOKEN_AXES)
    powers = all(n > 1 and n & (n - 1) == 0 for n in (n_gx, n_token))
    blocks_fit = gate_weight.shape[1] % (128 * n_gx) == 0 and n_gx <= 4
    if powers and blocks_fit:
        return direct(tokens, gate_weight, up_weight, down_weight)
    return offloaded(tokens, gate_weight, up_weight, down_weight)


def solution(mesh):
    return jax.shard_map(
        shards,
        mesh=mesh,
        in_specs=(
            P(("grp", "gy", "gz"), "gx"),
            P("gx", ("gy", "gz")),
            P("gx", ("gy", "gz")),
            P(("gy", "gz"), "gx"),
        ),
        out_specs=P(("grp", "gy", "gz"), "gx"),
        check_vma=False,
    )
```

time: 145 us -> 80.8 us (0.56)
  waiting for transfers between devices: 84 us -> 25.8 us
  Pallas kernels: 0 us -> 35 us
  matrix products: 34.4 us -> 0 us
  starting transfers between devices: 0.04 us -> 17 us
  between operations: 14.1 us -> 0.1 us
  blocking collectives: 7.39 us -> 0 us
    psum x1 -> x0, waiting for transfers between devices: 54.1 us -> none  [shards(): lax.psum(jnp.concatenate([gate_part, up_part], axis=1).astype(jnp.bfloat1...]
    pallas_call x0 -> x6, Pallas kernels: none -> 35 us  [the longest x4 23 us: gate_up(): pl.pallas_call(functools.partial(gate_up_kernel, width, step), out_shape=...]
    dot_general x3 -> x0, matrix products: 34.4 us -> none  [the longest x1 11.9 us: shards(): jnp.dot(hidden, down_weight, preferred_element_type=jnp.float32)]
    unnamed x3 -> x0, waiting for transfers between devices: 29.9 us -> none
    ppermute x0 -> x12, waiting for transfers between devices: none -> 25.8 us  [swap(): return lax.ppermute(value, axes, [(i, i ^ distance) for i in range(size)])]
    ppermute x0 -> x12, starting transfers between devices: none -> 17 us  [swap(): return lax.ppermute(value, axes, [(i, i ^ distance) for i in range(size)])]
    all_gather x1 -> x0, blocking collectives: 7.39 us -> none  [shards(): features = lax.all_gather(tokens, ('gy', 'gz'), axis=0, tiled=True)]
  transfers between devices with their start and end apart: 2 -> 12, of which waited for: 2 -> 8; matrix products, arithmetic and copies ran while one was open for 0% -> 0% of each run, Pallas kernels for 0% -> 15%
where the time goes in v1:
time: 80.8 us; the launch traced here: 80.6 us
  Pallas kernels  35 us (43%)
  waiting for transfers between devices  25.8 us (32%)
  starting transfers between devices  17 us (21%)
  other arithmetic  1.94 us (2%)
  local copies, waits for them, and re-layouts  0.83 us (1%)
    ppermute x12, waiting for transfers between devices, swap(): return lax.ppermute(value, axes, [(i, i ^ distance) for i in range(size)])  25.8 us
    pallas_call x4, Pallas kernels, gate_up(): pl.pallas_call(functools.partial(gate_up_kernel, width, step), out_shape=...  23 us
    ppermute x12, starting transfers between devices, swap(): return lax.ppermute(value, axes, [(i, i ^ distance) for i in range(size)])  17 us
    pallas_call x2, Pallas kernels, down(): pl.pallas_call(functools.partial(down_kernel, before is None, step), out_...  12 us
  transfers between devices with their start and end apart: 12, of which 8 were waited for; matrix products, arithmetic and copies ran while one was open for 0% of the time, Pallas kernels for 15%

profile of v1, /device:TPU:0, one launch (start us, length us, event | category | flops | bytes accessed | tf_op | source)
XLA Modules:
  0.0 80.6 jit_solution(6462070465062469038)
XLA Ops:
  0.0 2.4 %collective-permute-start.2 = (bf16[9,2048]{1,0:T(8,128)(2,1)}, bf16[9,2048]{1,0:T(8,128)(2,1)S(1)}, u32[]{:S(2)}, u32[]{:S(2)}) collective-permute-start(bf16[9,2048]{1,0:T(8,128)(2,1)} %_.1), channel_id=1, source_target_pairs={{0,3},{1,2},{2,1},{3,0},{4,7},{5,6},{6,5},{7,4},{8,11},{9,10},{10,... | collective-permute-start | bytes 110600 | tf_op jit(solution)/shard_map/ppermute | solution.py:145
  2.4 0.6 collective-permute-start.1
  3.0 0.1 collective-permute-start
  3.1 2.1 %collective-permute-done.2 = bf16[9,2048]{1,0:T(8,128)(2,1)S(1)} collective-permute-done((bf16[9,2048]{1,0:T(8,128)(2,1)}, bf16[9,2048]{1,0:T(8,128)(2,1)S(1)}, u32[]{:S(2)}, u32[]{:S(2)}) %collective-permute-start.2) | collective-permute-done | bytes 36896 | tf_op jit(solution)/shard_map/ppermute | solution.py:145
  5.2 2.1 %collective-permute-done.1 = bf16[9,2048]{1,0:T(8,128)(2,1)S(1)} collective-permute-done((bf16[9,2048]{1,0:T(8,128)(2,1)}, bf16[9,2048]{1,0:T(8,128)(2,1)S(1)}, u32[]{:S(2)}, u32[]{:S(2)}) %collective-permute-start.1) | collective-permute-done | bytes 36896 | tf_op jit(solution)/shard_map/ppermute | solution.py:145
  7.3 0.0 collective-permute-done
  7.3 0.9 %pad_maximum_fusion.x_ref = bf16[36,2048]{1,0:T(8,128)(2,1)S(1)} fusion(bf16[9,2048]{1,0:T(8,128)(2,1)S(1)} %collective-permute-done.2, bf16[9,2048]{1,0:T(8,128)(2,1)S(1)} %collective-permute-done.1, bf16[9,2048]{1,0:T(8,128)(2,1)S(1)} %collective-permute-done, bf16[9,2048]{1,0:T(8,128)(2,1)} %_.1), kind=kLoop, calls=%fused_computation.3 | loop fusion | flops 589824 | bytes 294912 | tf_op jit(solution)/shard_map/concatenate | solution.py:153
  8.2 0.0 copy-start
  8.2 0.8 %copy-done = bf16[9,2048]{1,0:T(8,128)(2,1)S(1)} copy-done((bf16[9,2048]{1,0:T(8,128)(2,1)S(1)}, bf16[9,2048]{1,0:T(8,128)(2,1)}, u32[]{:S(2)}) %copy-start) | copy-done | bytes 36888
  9.0 5.7 %shard_map.46._ = bf16[36,3328]{1,0:T(8,128)(2,1)S(1)} custom-call(s32[1]{0:T(128)} %bitcast.1.starts, bf16[36,2048]{1,0:T(8,128)(2,1)S(1)} %pad_maximum_fusion.x_ref, bf16[2048,6656]{1,0:T(8,128)(2,1)} %gate_ref.7, bf16[2048,6656]{1,0:T(8,128)(2,1)} %up_ref.7, bf16[9,2048]{1,0:T(8,128)(2,1)S(1)} %copy-done), custom_call_target="tpu_custom_call" | custom-call | flops 490733568 | bytes 13631488 | tf_op jit(solution)/shard_map/pallas_call | solution.py:60
  14.8 5.7 %shard_map.47._ = bf16[36,3328]{1,0:T(8,128)(2,1)S(1)} custom-call(s32[1]{0:T(128)} %bitcast.starts, bf16[36,2048]{1,0:T(8,128)(2,1)S(1)} %pad_maximum_fusion.x_ref, bf16[2048,6656]{1,0:T(8,128)(2,1)} %gate_ref.7, bf16[2048,6656]{1,0:T(8,128)(2,1)} %up_ref.7, bf16[36,3328]{1,0:T(8,128)(2,1)S(1)} %shard_map.46._), custom_call_target="tpu_custom_call" | custom-call | flops 490733568 | bytes 13631488 | tf_op jit(solution)/shard_map/pallas_call | solution.py:60
  20.5 5.8 %shard_map.48._ = bf16[36,3328]{1,0:T(8,128)(2,1)S(1)} custom-call(s32[1]{0:T(128)} %bitcast.3.starts, bf16[36,2048]{1,0:T(8,128)(2,1)S(1)} %pad_maximum_fusion.x_ref, bf16[2048,6656]{1,0:T(8,128)(2,1)} %gate_ref.7, bf16[2048,6656]{1,0:T(8,128)(2,1)} %up_ref.7, bf16[36,3328]{1,0:T(8,128)(2,1)S(1)} %shard_map.47._), custom_call_target="tpu_custom_call" | custom-call | flops 490733568 | bytes 13631488 | tf_op jit(solution)/shard_map/pallas_call | solution.py:60
  26.3 1.8 %collective-permute-start.5 = (bf16[36,3328]{1,0:T(8,128)(2,1)S(1)}, bf16[36,3328]{1,0:T(8,128)(2,1)S(1)}, u32[]{:S(2)}, u32[]{:S(2)}) collective-permute-start(bf16[36,3328]{1,0:T(8,128)(2,1)S(1)} %shard_map.48._), channel_id=1, source_target_pairs={{0,4},{4,0},{8,12},{12,8},{1,5},{5,1},{9,13},{13,9},{2,6},{6,2},{1... | collective-permute-start | bytes 718856 | tf_op jit(solution)/shard_map/ppermute | solution.py:145
  28.1 2.6 %collective-permute-start.4 = (bf16[36,3328]{1,0:T(8,128)(2,1)S(1)}, bf16[36,3328]{1,0:T(8,128)(2,1)S(1)}, u32[]{:S(2)}, u32[]{:S(2)}) collective-permute-start(bf16[36,3328]{1,0:T(8,128)(2,1)S(1)} %shard_map.47._), channel_id=1, source_target_pairs={{0,8},{4,12},{8,0},{12,4},{1,9},{5,13},{9,1},{13,5},{2,10},{6,14},... | collective-permute-start | bytes 718856 | tf_op jit(solution)/shard_map/ppermute | solution.py:145
  30.7 0.0 collective-permute-start.3
  30.7 5.7 %shard_map.49 = bf16[36,3328]{1,0:T(8,128)(2,1)S(1)} custom-call(s32[1]{0:T(128)} %bitcast.2.starts, bf16[36,2048]{1,0:T(8,128)(2,1)S(1)} %pad_maximum_fusion.x_ref, bf16[2048,6656]{1,0:T(8,128)(2,1)} %gate_ref.7, bf16[2048,6656]{1,0:T(8,128)(2,1)} %up_ref.7, bf16[36,3328]{1,0:T(8,128)(2,1)S(1)} %shard_map.48._), custom_call_target="tpu_custom_call" | custom-call | flops 490733568 | bytes 13631488 | tf_op jit(solution)/shard_map/pallas_call | solution.py:60
  36.5 3.1 %collective-permute-done.5 = bf16[36,3328]{1,0:T(8,128)(2,1)S(1)} collective-permute-done((bf16[36,3328]{1,0:T(8,128)(2,1)S(1)}, bf16[36,3328]{1,0:T(8,128)(2,1)S(1)}, u32[]{:S(2)}, u32[]{:S(2)}) %collective-permute-start.5) | collective-permute-done | bytes 239648 | tf_op jit(solution)/shard_map/ppermute | solution.py:145
  39.6 10.1 %collective-permute-done.4 = bf16[36,3328]{1,0:T(8,128)(2,1)S(1)} collective-permute-done((bf16[36,3328]{1,0:T(8,128)(2,1)S(1)}, bf16[36,3328]{1,0:T(8,128)(2,1)S(1)}, u32[]{:S(2)}, u32[]{:S(2)}) %collective-permute-start.4) | collective-permute-done | bytes 239648 | tf_op jit(solution)/shard_map/ppermute | solution.py:145
  49.7 0.0 collective-permute-done.3
  49.7 0.1 convert_add_fusion
  49.9 0.1 fusion.refs_0_
  50.0 5.0 %collective-permute-start.8 = (bf16[36,1664]{1,0:T(8,128)(2,1)S(1)}, bf16[36,1664]{1,0:T(8,128)(2,1)S(1)}, u32[]{:S(2)}, u32[]{:S(2)}) collective-permute-start(bf16[36,1664]{1,0:T(8,128)(2,1)S(1)} %fusion.refs_0_), channel_id=1, source_target_pairs={{0,4},{4,0},{8,12},{12,8},{1,5},{5,1},{9,13},{13,9},{2,6},{6,2},{1... | collective-permute-start | bytes 359432 | tf_op jit(solution)/shard_map/ppermute | solution.py:145
  55.0 0.1 pad_add_fusion.starts
  55.1 2.5 %collective-permute-start.7 = (bf16[36,1664]{1,0:T(8,128)(2,1)S(1)}, bf16[36,1664]{1,0:T(8,128)(2,1)S(1)}, u32[]{:S(2)}, u32[]{:S(2)}) collective-permute-start(bf16[36,1664]{1,0:T(8,128)(2,1)S(1)} %fusion.refs_0_), channel_id=1, source_target_pairs={{0,12},{4,8},{8,4},{12,0},{1,13},{5,9},{9,5},{13,1},{2,14},{6,10},... | collective-permute-start | bytes 359432 | tf_op jit(solution)/shard_map/ppermute | solution.py:145
  57.6 0.0 collective-permute-start.6
  57.6 0.1 pad_add_fusion.1.starts
  57.6 1.2 %collective-permute-done.8.refs_1_ = bf16[36,1664]{1,0:T(8,128)(2,1)S(1)} collective-permute-done((bf16[36,1664]{1,0:T(8,128)(2,1)S(1)}, bf16[36,1664]{1,0:T(8,128)(2,1)S(1)}, u32[]{:S(2)}, u32[]{:S(2)}) %collective-permute-start.8) | collective-permute-done | bytes 119840 | tf_op jit(solution)/shard_map/ppermute | solution.py:145
  58.8 6.0 %shard_map.50.refs_2_ = f32[36,2048]{1,0:T(8,128)S(1)} custom-call(s32[2]{0:T(128)S(1)} %pad_add_fusion.1.starts, bf16[36,1664]{1,0:T(8,128)(2,1)S(1)} %fusion.refs_0_, bf16[36,1664]{1,0:T(8,128)(2,1)S(1)} %collective-permute-done.8.refs_1_, bf16[6656,2048]{1,0:T(8,128)(2,1)} %refs_3_.1), custom_call_target="tpu_custom_call" | custom-call | flops 490733568 | bytes 13631488 | tf_op jit(solution)/shard_map/pallas_call | solution.py:125
  64.8 0.0 collective-permute-done.7.refs_1_
  64.8 3.3 %collective-permute-done.6.refs_0_ = bf16[36,1664]{1,0:T(8,128)(2,1)S(1)} collective-permute-done((bf16[36,1664]{1,0:T(8,128)(2,1)S(1)}, bf16[36,1664]{1,0:T(8,128)(2,1)S(1)}, u32[]{:S(2)}, u32[]{:S(2)}) %collective-permute-start.6) | collective-permute-done | bytes 119840 | tf_op jit(solution)/shard_map/ppermute | solution.py:145
  68.1 6.0 %shard_map.51 = (bf16[9,2048]{1,0:T(8,128)(2,1)S(1)}, bf16[9,2048]{1,0:T(8,128)(2,1)S(1)}, bf16[9,2048]{1,0:T(8,128)(2,1)S(1)}, bf16[9,2048]{1,0:T(8,128)(2,1)S(1)}) custom-call(s32[2]{0:T(128)S(1)} %pad_add_fusion.starts, bf16[36,1664]{1,0:T(8,128)(2,1)S(1)} %collective-permute-done.6.refs_0_, bf16[36,1664]{1,0:T(8,128)(2,1)S(1)} %collective-permute-done.7.refs_1_, ...), custom_call_target="tpu_custom_call" | custom-call | flops 490733568 | bytes 13631488 | tf_op jit(solution)/shard_map/pallas_call | solution.py:125
  74.1 0.1 collective-permute-start.9
  74.2 1.7 %collective-permute-start.10 = (bf16[9,2048]{1,0:T(8,128)(2,1)S(1)}, bf16[9,2048]{1,0:T(8,128)(2,1)S(1)}, u32[]{:S(2)}, u32[]{:S(2)}) collective-permute-start(bf16[9,2048]{1,0:T(8,128)(2,1)S(1)} %get-tuple-element.11), channel_id=1, source_target_pairs={{0,2},{1,3},{2,0},{3,1},{4,6},{5,7},{6,4},{7,5},{8,10},{9,11},{10,... | collective-permute-start | bytes 110600 | tf_op jit(solution)/shard_map/ppermute | solution.py:145
  75.9 0.2 collective-permute-start.11
  76.1 0.0 collective-permute-done.9
  76.1 2.6 %collective-permute-done.10 = bf16[9,2048]{1,0:T(8,128)(2,1)S(1)} collective-permute-done((bf16[9,2048]{1,0:T(8,128)(2,1)S(1)}, bf16[9,2048]{1,0:T(8,128)(2,1)S(1)}, u32[]{:S(2)}, u32[]{:S(2)}) %collective-permute-start.10) | collective-permute-done | bytes 36896 | tf_op jit(solution)/shard_map/ppermute | solution.py:145
  78.7 1.2 %collective-permute-done.11 = bf16[9,2048]{1,0:T(8,128)(2,1)S(1)} collective-permute-done((bf16[9,2048]{1,0:T(8,128)(2,1)S(1)}, bf16[9,2048]{1,0:T(8,128)(2,1)S(1)}, u32[]{:S(2)}, u32[]{:S(2)}) %collective-permute-start.11) | collective-permute-done | bytes 36896 | tf_op jit(solution)/shard_map/ppermute | solution.py:145
  80.0 0.7 add_convert_fusion
Async XLA Ops:
  0.0 5.2 %collective-permute-start.2 = (bf16[9,2048]{1,0:T(8,128)(2,1)}, bf16[9,2048]{1,0:T(8,128)(2,1)S(1)}, u32[]{:S(2)}, u32[]{:S(2)}) collective-permute-start(bf16[9,2048]{1,0:T(8,128)(2,1)} %_.1), channel_id=1, source_target_pairs={{0,3},{1,2},{2,1},{3,0},{4,7},{5,6},{6,5},{7,4},{8,11},{9,10},{10,... | collective-permute-start | bytes 110600 | tf_op jit(solution)/shard_map/ppermute | solution.py:145
  2.4 4.9 %collective-permute-start.1 = (bf16[9,2048]{1,0:T(8,128)(2,1)}, bf16[9,2048]{1,0:T(8,128)(2,1)S(1)}, u32[]{:S(2)}, u32[]{:S(2)}) collective-permute-start(bf16[9,2048]{1,0:T(8,128)(2,1)} %_.1), channel_id=1, source_target_pairs={{0,2},{1,3},{2,0},{3,1},{4,6},{5,7},{6,4},{7,5},{8,10},{9,11},{10,... | collective-permute-start | bytes 110600 | tf_op jit(solution)/shard_map/ppermute | solution.py:145
  3.0 4.3 %collective-permute-start = (bf16[9,2048]{1,0:T(8,128)(2,1)}, bf16[9,2048]{1,0:T(8,128)(2,1)S(1)}, u32[]{:S(2)}, u32[]{:S(2)}) collective-permute-start(bf16[9,2048]{1,0:T(8,128)(2,1)} %_.1), channel_id=1, source_target_pairs={{0,1},{1,0},{2,3},{3,2},{4,5},{5,4},{6,7},{7,6},{8,9},{9,8},{10,11... | collective-permute-start | bytes 110600 | tf_op jit(solution)/shard_map/ppermute | solution.py:145
  8.2 0.8 %copy-start = (bf16[9,2048]{1,0:T(8,128)(2,1)S(1)}, bf16[9,2048]{1,0:T(8,128)(2,1)}, u32[]{:S(2)}) copy-start(bf16[9,2048]{1,0:T(8,128)(2,1)} %_.1) | copy-start | bytes 110596
  26.3 13.3 %collective-permute-start.5 = (bf16[36,3328]{1,0:T(8,128)(2,1)S(1)}, bf16[36,3328]{1,0:T(8,128)(2,1)S(1)}, u32[]{:S(2)}, u32[]{:S(2)}) collective-permute-start(bf16[36,3328]{1,0:T(8,128)(2,1)S(1)} %shard_map.48._), channel_id=1, source_target_pairs={{0,4},{4,0},{8,12},{12,8},{1,5},{5,1},{9,13},{13,9},{2,6},{6,2},{1... | collective-permute-start | bytes 718856 | tf_op jit(solution)/shard_map/ppermute | solution.py:145
  28.1 21.6 %collective-permute-start.4 = (bf16[36,3328]{1,0:T(8,128)(2,1)S(1)}, bf16[36,3328]{1,0:T(8,128)(2,1)S(1)}, u32[]{:S(2)}, u32[]{:S(2)}) collective-permute-start(bf16[36,3328]{1,0:T(8,128)(2,1)S(1)} %shard_map.47._), channel_id=1, source_target_pairs={{0,8},{4,12},{8,0},{12,4},{1,9},{5,13},{9,1},{13,5},{2,10},{6,14},... | collective-permute-start | bytes 718856 | tf_op jit(solution)/shard_map/ppermute | solution.py:145
  30.7 19.0 %collective-permute-start.3 = (bf16[36,3328]{1,0:T(8,128)(2,1)S(1)}, bf16[36,3328]{1,0:T(8,128)(2,1)S(1)}, u32[]{:S(2)}, u32[]{:S(2)}) collective-permute-start(bf16[36,3328]{1,0:T(8,128)(2,1)S(1)} %shard_map.46._), channel_id=1, source_target_pairs={{0,12},{4,8},{8,4},{12,0},{1,13},{5,9},{9,5},{13,1},{2,14},{6,10},... | collective-permute-start | bytes 718856 | tf_op jit(solution)/shard_map/ppermute | solution.py:145
  50.0 8.9 %collective-permute-start.8 = (bf16[36,1664]{1,0:T(8,128)(2,1)S(1)}, bf16[36,1664]{1,0:T(8,128)(2,1)S(1)}, u32[]{:S(2)}, u32[]{:S(2)}) collective-permute-start(bf16[36,1664]{1,0:T(8,128)(2,1)S(1)} %fusion.refs_0_), channel_id=1, source_target_pairs={{0,4},{4,0},{8,12},{12,8},{1,5},{5,1},{9,13},{13,9},{2,6},{6,2},{1... | collective-permute-start | bytes 359432 | tf_op jit(solution)/shard_map/ppermute | solution.py:145
  55.1 9.7 %collective-permute-start.7 = (bf16[36,1664]{1,0:T(8,128)(2,1)S(1)}, bf16[36,1664]{1,0:T(8,128)(2,1)S(1)}, u32[]{:S(2)}, u32[]{:S(2)}) collective-permute-start(bf16[36,1664]{1,0:T(8,128)(2,1)S(1)} %fusion.refs_0_), channel_id=1, source_target_pairs={{0,12},{4,8},{8,4},{12,0},{1,13},{5,9},{9,5},{13,1},{2,14},{6,10},... | collective-permute-start | bytes 359432 | tf_op jit(solution)/shard_map/ppermute | solution.py:145
  57.6 10.5 %collective-permute-start.6 = (bf16[36,1664]{1,0:T(8,128)(2,1)S(1)}, bf16[36,1664]{1,0:T(8,128)(2,1)S(1)}, u32[]{:S(2)}, u32[]{:S(2)}) collective-permute-start(bf16[36,1664]{1,0:T(8,128)(2,1)S(1)} %fusion.refs_0_), channel_id=1, source_target_pairs={{0,8},{4,12},{8,0},{12,4},{1,9},{5,13},{9,1},{13,5},{2,10},{6,14},... | collective-permute-start | bytes 359432 | tf_op jit(solution)/shard_map/ppermute | solution.py:145
  74.1 1.9 %collective-permute-start.9 = (bf16[9,2048]{1,0:T(8,128)(2,1)S(1)}, bf16[9,2048]{1,0:T(8,128)(2,1)S(1)}, u32[]{:S(2)}, u32[]{:S(2)}) collective-permute-start(bf16[9,2048]{1,0:T(8,128)(2,1)S(1)} %get-tuple-element.10), channel_id=1, source_target_pairs={{0,1},{1,0},{2,3},{3,2},{4,5},{5,4},{6,7},{7,6},{8,9},{9,8},{10,11... | collective-permute-start | bytes 110600 | tf_op jit(solution)/shard_map/ppermute | solution.py:145
  74.2 4.5 %collective-permute-start.10 = (bf16[9,2048]{1,0:T(8,128)(2,1)S(1)}, bf16[9,2048]{1,0:T(8,128)(2,1)S(1)}, u32[]{:S(2)}, u32[]{:S(2)}) collective-permute-start(bf16[9,2048]{1,0:T(8,128)(2,1)S(1)} %get-tuple-element.11), channel_id=1, source_target_pairs={{0,2},{1,3},{2,0},{3,1},{4,6},{5,7},{6,4},{7,5},{8,10},{9,11},{10,... | collective-permute-start | bytes 110600 | tf_op jit(solution)/shard_map/ppermute | solution.py:145
  75.9 4.0 %collective-permute-start.11 = (bf16[9,2048]{1,0:T(8,128)(2,1)S(1)}, bf16[9,2048]{1,0:T(8,128)(2,1)S(1)}, u32[]{:S(2)}, u32[]{:S(2)}) collective-permute-start(bf16[9,2048]{1,0:T(8,128)(2,1)S(1)} %get-tuple-element.12), channel_id=1, source_target_pairs={{0,3},{1,2},{2,1},{3,0},{4,7},{5,6},{6,5},{7,4},{8,11},{9,10},{10,... | collective-permute-start | bytes 110600 | tf_op jit(solution)/shard_map/ppermute | solution.py:145

commit v2 on v0

v2 whole, which is shorter than its diff:
```python
import functools

import jax
import jax.numpy as jnp
from jax import lax
from jax.experimental import pallas as pl
from jax.experimental.pallas import tpu as pltpu
from jax.sharding import PartitionSpec as P

MIB = 1 << 20
TOKEN_AXES = ("gy", "gz")
ANY = pl.BlockSpec(memory_space=pl.ANY)
IN_HBM = pl.BlockSpec(memory_space=pltpu.HBM)
WHOLE = pl.BlockSpec(memory_space=pltpu.VMEM)
SCALARS = pl.BlockSpec(memory_space=pltpu.SMEM)


def activate(gate, up):
    return (jax.nn.silu(gate) * up).astype(jnp.bfloat16)


def pieces_of(total, step):
    return [(start, min(step, total - start)) for start in range(0, total, step)]


def in_hbm(value):
    return pltpu.with_memory_space_constraint(value, pltpu.HBM)


def in_vmem(value):
    return pltpu.with_memory_space_constraint(value, pltpu.VMEM)


def cost(nbytes):
    return pl.CostEstimate(flops=0, bytes_accessed=nbytes, transcendentals=0)


def fetch_gate_up_kernel(width, step, start_ref, gate_ref, up_ref, held, sems):
    columns = pl.ds(pl.multiple_of(start_ref[0], 128), width)
    copies = []
    for k, (row, rows) in enumerate(pieces_of(held.shape[1], step)):
        for w, weight in enumerate((gate_ref, up_ref)):
            copy = pltpu.make_async_copy(
                weight.at[pl.ds(row, rows), columns], held.at[w, pl.ds(row, rows)], sems.at[w, k]
            )
            copy.start()
            copies.append(copy)
    for copy in copies:
        copy.wait()


def fetch_gate_up(gate_weight, up_weight, start, width):
    depth, step = gate_weight.shape[0], 256
    return pl.pallas_call(
        functools.partial(fetch_gate_up_kernel, width, step),
        out_shape=pltpu.VMEM((2, depth, width), jnp.bfloat16),
        in_specs=[SCALARS, IN_HBM, IN_HBM],
        out_specs=WHOLE,
        scratch_shapes=[pltpu.SemaphoreType.DMA((2, len(pieces_of(depth, step))))],
        compiler_params=pltpu.CompilerParams(vmem_limit_bytes=8 * MIB),
        cost_estimate=cost(MIB),
    )(start, in_hbm(gate_weight), in_hbm(up_weight))


def gate_up_held_kernel(step, x_ref, held, out, total):
    width = held.shape[2]
    parts = pieces_of(x_ref.shape[1], step)
    for w in range(2):
        for k, (row, rows) in enumerate(parts):
            term = jnp.dot(
                x_ref[:, row : row + rows],
                held[w, row : row + rows, :],
                preferred_element_type=jnp.float32,
            )
            if k == 0:
                total[...] = term
            elif k < len(parts) - 1:
                total[...] += term
            else:
                out[:, w * width : (w + 1) * width] = (total[...] + term).astype(jnp.bfloat16)


def gate_up_held(features, held):
    rows = features.shape[0]
    width = held.shape[2]
    return pl.pallas_call(
        functools.partial(gate_up_held_kernel, 256),
        out_shape=jax.ShapeDtypeStruct((rows, 2 * width), jnp.bfloat16),
        in_specs=[WHOLE, WHOLE],
        out_specs=WHOLE,
        scratch_shapes=[pltpu.VMEM((rows, width), jnp.float32)],
        compiler_params=pltpu.CompilerParams(vmem_limit_bytes=8 * MIB),
        cost_estimate=cost(MIB),
    )(features, in_vmem(held))


def gate_up_kernel(width, step, start_ref, x_ref, gate_ref, up_ref, _, out, held, total, sems):
    parts = pieces_of(x_ref.shape[1], step)
    columns = pl.ds(pl.multiple_of(start_ref[0], 128), width)
    copies = []
    for k, (row, rows) in enumerate(parts):
        for w, weight in enumerate((gate_ref, up_ref)):
            copy = pltpu.make_async_copy(
                weight.at[pl.ds(row, rows), columns], held.at[w, pl.ds(row, rows)], sems.at[w, k]
            )
            copy.start()
            copies.append((w, k, row, rows, copy))
    for w, k, row, rows, copy in copies:
        copy.wait()
        term = jnp.dot(
            x_ref[:, row : row + rows],
            held[w, row : row + rows, :],
            preferred_element_type=jnp.float32,
        )
        if k == 0:
            total[w] = term
        elif k < len(parts) - 1:
            total[w] += term
        else:
            out[:, w * width : (w + 1) * width] = (total[w] + term).astype(jnp.bfloat16)


def gate_up(features, gate_weight, up_weight, start, width, after):
    rows, depth = features.shape
    step = 256
    return pl.pallas_call(
        functools.partial(gate_up_kernel, width, step),
        out_shape=jax.ShapeDtypeStruct((rows, 2 * width), jnp.bfloat16),
        in_specs=[SCALARS, WHOLE, IN_HBM, IN_HBM, ANY],
        out_specs=WHOLE,
        scratch_shapes=[
            pltpu.VMEM((2, depth, width), jnp.bfloat16),
            pltpu.VMEM((2, rows, width), jnp.float32),
            pltpu.SemaphoreType.DMA((2, len(pieces_of(depth, step)))),
        ],
        compiler_params=pltpu.CompilerParams(vmem_limit_bytes=24 * MIB),
        cost_estimate=cost(MIB),
    )(start, features, in_hbm(gate_weight), in_hbm(up_weight), after)


def fetch_down_kernel(step, own_ref, down_ref, own_out, held, sems):
    copies = []
    for k, (row, rows) in enumerate(pieces_of(held.shape[0], step)):
        copy = pltpu.make_async_copy(
            down_ref.at[pl.ds(row, rows)], held.at[pl.ds(row, rows)], sems.at[k]
        )
        copy.start()
        copies.append(copy)
    own_out[...] = own_ref[...].astype(jnp.float32)
    for copy in copies:
        copy.wait()


def fetch_down(own, down_weight):
    step = 512
    return pl.pallas_call(
        functools.partial(fetch_down_kernel, step),
        out_shape=(
            jax.ShapeDtypeStruct(own.shape, jnp.float32),
            pltpu.VMEM(down_weight.shape, jnp.bfloat16),
        ),
        in_specs=[WHOLE, IN_HBM],
        out_specs=(WHOLE, WHOLE),
        scratch_shapes=[pltpu.SemaphoreType.DMA((len(pieces_of(down_weight.shape[0], step)),))],
        compiler_params=pltpu.CompilerParams(vmem_limit_bytes=8 * MIB),
        cost_estimate=cost(MIB),
    )(own, in_hbm(down_weight))


def down_kernel(first, starts, *refs):
    blocks = starts.shape[0]
    hidden, refs = refs[:blocks], refs[blocks:]
    if not first:
        before, refs = refs[0], refs[1:]
    held, outs, total = refs[0], refs[1:-1], refs[-1]
    width = hidden[0].shape[1]
    for b in range(blocks):
        rows = pl.ds(pl.multiple_of(starts[b], 128), width)
        term = jnp.dot(hidden[b][...], held[rows, :], preferred_element_type=jnp.float32)
        if b == 0 and first:
            total[...] = term
        elif b == 0:
            total[...] = before[...] + term
        else:
            total[...] += term
    if len(outs) == 1:
        outs[0][...] = total[...]
    else:
        tall = outs[0].shape[0]
        for r, out in enumerate(outs):
            out[...] = total[r * tall : (r + 1) * tall, :].astype(out.dtype)


def down(hidden, starts, before, held, outs):
    rows = hidden[0].shape[0]
    columns = held.shape[1]
    if outs == 1:
        shapes = [jax.ShapeDtypeStruct((rows, columns), jnp.float32)]
    else:
        shapes = [jax.ShapeDtypeStruct((rows // outs, columns), jnp.bfloat16)] * outs
    carried = [] if before is None else [before]
    return pl.pallas_call(
        functools.partial(down_kernel, before is None),
        out_shape=shapes,
        in_specs=[SCALARS] + [WHOLE] * (len(hidden) + len(carried) + 1),
        out_specs=[WHOLE] * outs,
        scratch_shapes=[pltpu.VMEM((rows, columns), jnp.float32)],
        compiler_params=pltpu.CompilerParams(vmem_limit_bytes=8 * MIB),
        cost_estimate=cost(MIB),
    )(starts, *hidden, *carried, in_vmem(held))


def swap(value, axes, size, distance):
    return lax.ppermute(value, axes, [(i, i ^ distance) for i in range(size)])


def direct(tokens, gate_weight, up_weight, down_weight):
    n_gx = lax.axis_size("gx")
    n_token = lax.axis_size(TOKEN_AXES)
    me = lax.axis_index("gx")
    width = gate_weight.shape[1] // n_gx

    def starts_of(distances):
        return jnp.stack([(me ^ d) * width for d in distances]).astype(jnp.int32)

    held = fetch_gate_up(gate_weight, up_weight, starts_of([n_gx - 1]), width)
    features = jnp.concatenate(
        [tokens] + [swap(tokens, TOKEN_AXES, n_token, r) for r in range(1, n_token)], axis=0
    )

    received = []
    for d in range(n_gx - 1, -1, -1):
        if d == n_gx - 1:
            block = gate_up_held(features, held)
        else:
            block = gate_up(features, gate_weight, up_weight, starts_of([d]), width, block)
        if d:
            received.append(swap(block, "gx", n_gx, d))
    summed, down_held = fetch_down(block, down_weight)
    for term in received:
        summed = lax.optimization_barrier(summed + term.astype(jnp.float32))
    hidden = activate(summed[:, :width], summed[:, width:])

    blocks = [hidden] + [swap(hidden, "gx", n_gx, d) for d in range(1, n_gx)]
    half = n_gx // 2
    (partial_sum,) = down(blocks[:half], starts_of(range(half)), None, down_held, 1)
    outs = down(blocks[half:], starts_of(range(half, n_gx)), partial_sum, down_held, n_token)
    result = outs[0].astype(jnp.float32)
    for r in range(1, n_token):
        result = result + swap(outs[r], TOKEN_AXES, n_token, r).astype(jnp.float32)
    return result.astype(jnp.bfloat16)


def offloaded(tokens, gate_weight, up_weight, down_weight):
    features = lax.all_gather(tokens, TOKEN_AXES, axis=0, tiled=True)
    hidden_width = gate_weight.shape[1]
    gate_part = jnp.dot(features, gate_weight, preferred_element_type=jnp.float32)
    up_part = jnp.dot(features, up_weight, preferred_element_type=jnp.float32)
    summed = lax.psum(
        jnp.concatenate([gate_part, up_part], axis=1).astype(jnp.bfloat16), "gx"
    ).astype(jnp.float32)
    hidden = activate(summed[:, :hidden_width], summed[:, hidden_width:])
    partial_value = jnp.dot(hidden, down_weight, preferred_element_type=jnp.float32)
    return lax.psum_scatter(
        partial_value.astype(jnp.bfloat16), TOKEN_AXES, scatter_dimension=0, tiled=True
    )


def shards(tokens, gate_weight, up_weight, down_weight):
    n_gx = lax.axis_size("gx")
    n_token = lax.axis_size(TOKEN_AXES)
    powers = all(n > 1 and n & (n - 1) == 0 for n in (n_gx, n_token))
    blocks_fit = gate_weight.shape[1] % (128 * n_gx) == 0 and n_gx <= 4
    if powers and blocks_fit:
        return direct(tokens, gate_weight, up_weight, down_weight)
    return offloaded(tokens, gate_weight, up_weight, down_weight)


def solution(mesh):
    return jax.shard_map(
        shards,
        mesh=mesh,
        in_specs=(
            P(("grp", "gy", "gz"), "gx"),
            P("gx", ("gy", "gz")),
            P("gx", ("gy", "gz")),
            P(("gy", "gz"), "gx"),
        ),
        out_specs=P(("grp", "gy", "gz"), "gx"),
        check_vma=False,
    )
```

time: 145 us -> 67.1 us (0.46)
  waiting for transfers between devices: 84 us -> 11.7 us
  Pallas kernels: 0 us -> 39.7 us
  matrix products: 34.4 us -> 0 us
  starting transfers between devices: 0.04 us -> 14.2 us
  between operations: 14.1 us -> 0.17 us
  blocking collectives: 7.39 us -> 0 us
  local copies, waits for them, and re-layouts: 2.2 us -> 0.01 us
    psum x1 -> x0, waiting for transfers between devices: 54.1 us -> none  [shards(): lax.psum(jnp.concatenate([gate_part, up_part], axis=1).astype(jnp.bfloat1...]
    pallas_call x0 -> x8, Pallas kernels: none -> 39.7 us  [the longest x3 17.2 us: gate_up(): pl.pallas_call(functools.partial(gate_up_kernel, width, step), out_shape=...]
    dot_general x3 -> x0, matrix products: 34.4 us -> none  [the longest x1 11.9 us: shards(): jnp.dot(hidden, down_weight, preferred_element_type=jnp.float32)]
    unnamed x3 -> x0, waiting for transfers between devices: 29.9 us -> none
    ppermute x0 -> x12, starting transfers between devices: none -> 14.2 us  [swap(): return lax.ppermute(value, axes, [(i, i ^ distance) for i in range(size)])]
    ppermute x0 -> x12, waiting for transfers between devices: none -> 11.7 us  [swap(): return lax.ppermute(value, axes, [(i, i ^ distance) for i in range(size)])]
    all_gather x1 -> x0, blocking collectives: 7.39 us -> none  [shards(): features = lax.all_gather(tokens, ('gy', 'gz'), axis=0, tiled=True)]
    unnamed x5 -> x2, local copies, waits for them, and re-layouts: 2.2 us -> 0.01 us
  transfers between devices with their start and end apart: 2 -> 12, of which waited for: 2 -> 5; matrix products, arithmetic and copies ran while one was open for 0% -> 0% of each run, Pallas kernels for 0% -> 51%
where the time goes in v2:
time: 67.1 us; the launch traced here: 67 us
  Pallas kernels  39.7 us (59%)
  starting transfers between devices  14.2 us (21%)
  waiting for transfers between devices  11.7 us (17%)
  other arithmetic  1.14 us (2%)
    pallas_call x3, Pallas kernels, gate_up(): pl.pallas_call(functools.partial(gate_up_kernel, width, step), out_shape=...  17.2 us
    ppermute x12, starting transfers between devices, swap(): return lax.ppermute(value, axes, [(i, i ^ distance) for i in range(size)])  14.2 us
    ppermute x12, waiting for transfers between devices, swap(): return lax.ppermute(value, axes, [(i, i ^ distance) for i in range(size)])  11.7 us
    pallas_call x1, Pallas kernels, fetch_down(): pl.pallas_call(functools.partial(fetch_down_kernel, step), out_shape=(jax...  8.96 us
    pallas_call x2, Pallas kernels, down(): pl.pallas_call(functools.partial(down_kernel, before is None), out_shape=...  6.09 us
    pallas_call x1, Pallas kernels, fetch_gate_up(): pl.pallas_call(functools.partial(fetch_gate_up_kernel, width, step), out_...  5.23 us
    pallas_call x1, Pallas kernels, gate_up_held(): pl.pallas_call(functools.partial(gate_up_held_kernel, 256), out_shape=jax...  2.16 us
  transfers between devices with their start and end apart: 12, of which 5 were waited for; matrix products, arithmetic and copies ran while one was open for 0% of the time, Pallas kernels for 51%

profile of v2, /device:TPU:0, one launch (start us, length us, event | category | flops | bytes accessed | tf_op | source)
XLA Modules:
  0.0 67.0 jit_solution(3008183227801144101)
XLA Ops:
  0.0 2.9 %collective-permute-start.1 = (bf16[9,2048]{1,0:T(8,128)(2,1)}, bf16[9,2048]{1,0:T(8,128)(2,1)S(1)}, u32[]{:S(2)}, u32[]{:S(2)}) collective-permute-start(bf16[9,2048]{1,0:T(8,128)(2,1)} %param.4), channel_id=1, source_target_pairs={{0,2},{1,3},{2,0},{3,1},{4,6},{5,7},{6,4},{7,5},{8,10},{9,11},{10,... | collective-permute-start | bytes 110600 | tf_op jit(solution)/shard_map/ppermute | solution.py:214
  2.9 0.0 collective-permute-start
  2.9 0.1 collective-permute-start.2
  3.1 0.0 copy-start
  3.1 5.2 %shard_map.46.held = bf16[2,2048,1664]{2,1,0:T(8,128)(2,1)S(1)} custom-call(s32[1]{0:T(128)} %bitcast.1.start_ref, bf16[2048,6656]{1,0:T(8,128)(2,1)} %gate_ref.7, bf16[2048,6656]{1,0:T(8,128)(2,1)} %up_ref.7), custom_call_target="tpu_custom_call" | custom-call | bytes 1048576 | tf_op jit(solution)/shard_map/pallas_call | solution.py:54
  8.3 0.0 collective-permute-done.1
  8.3 0.0 collective-permute-done
  8.3 0.0 collective-permute-done.2
  8.3 0.0 copy-done
  8.3 0.1 pad_maximum_fusion.x_ref
  8.4 2.2 %shard_map.47._ = bf16[36,3328]{1,0:T(8,128)(2,1)S(1)} custom-call(bf16[36,2048]{1,0:T(8,128)(2,1)S(1)} %pad_maximum_fusion.x_ref, bf16[2,2048,1664]{2,1,0:T(8,128)(2,1)S(1)} %shard_map.46.held), custom_call_target="tpu_custom_call" | custom-call | bytes 1048576 | tf_op jit(solution)/shard_map/pallas_call | solution.py:86
  10.6 4.1 %collective-permute-start.3 = (bf16[36,3328]{1,0:T(8,128)(2,1)S(1)}, bf16[36,3328]{1,0:T(8,128)(2,1)S(1)}, u32[]{:S(2)}, u32[]{:S(2)}) collective-permute-start(bf16[36,3328]{1,0:T(8,128)(2,1)S(1)} %shard_map.47._), channel_id=1, source_target_pairs={{0,12},{4,8},{8,4},{12,0},{1,13},{5,9},{9,5},{13,1},{2,14},{6,10},... | collective-permute-start | bytes 718856 | tf_op jit(solution)/shard_map/ppermute | solution.py:214
  14.7 5.7 %shard_map.48._ = bf16[36,3328]{1,0:T(8,128)(2,1)S(1)} custom-call(s32[1]{0:T(128)} %bitcast.start_ref, bf16[36,2048]{1,0:T(8,128)(2,1)S(1)} %pad_maximum_fusion.x_ref, bf16[2048,6656]{1,0:T(8,128)(2,1)} %gate_ref.7, bf16[2048,6656]{1,0:T(8,128)(2,1)} %up_ref.7, bf16[36,3328]{1,0:T(8,128)(2,1)S(1)} %shard_map.47._), custom_call_target="tpu_custom_call" | custom-call | bytes 1048576 | tf_op jit(solution)/shard_map/pallas_call | solution.py:126
  20.5 0.1 collective-permute-start.4
  20.6 5.7 %shard_map.49._ = bf16[36,3328]{1,0:T(8,128)(2,1)S(1)} custom-call(s32[1]{0:T(128)} %bitcast.3.start_ref, bf16[36,2048]{1,0:T(8,128)(2,1)S(1)} %pad_maximum_fusion.x_ref, bf16[2048,6656]{1,0:T(8,128)(2,1)} %gate_ref.7, bf16[2048,6656]{1,0:T(8,128)(2,1)} %up_ref.7, bf16[36,3328]{1,0:T(8,128)(2,1)S(1)} %shard_map.48._), custom_call_target="tpu_custom_call" | custom-call | bytes 1048576 | tf_op jit(solution)/shard_map/pallas_call | solution.py:126
  26.3 0.6 collective-permute-start.5
  26.9 5.7 %shard_map.50.own_ref = bf16[36,3328]{1,0:T(8,128)(2,1)S(1)} custom-call(s32[1]{0:T(128)} %bitcast.2.start_ref, bf16[36,2048]{1,0:T(8,128)(2,1)S(1)} %pad_maximum_fusion.x_ref, bf16[2048,6656]{1,0:T(8,128)(2,1)} %gate_ref.7, bf16[2048,6656]{1,0:T(8,128)(2,1)} %up_ref.7, bf16[36,3328]{1,0:T(8,128)(2,1)S(1)} %shard_map.49._), custom_call_target="tpu_custom_call" | custom-call | bytes 1048576 | tf_op jit(solution)/shard_map/pallas_call | solution.py:126
  32.7 9.0 %shard_map.51 = (f32[36,3328]{1,0:T(8,128)S(1)}, bf16[6656,2048]{1,0:T(8,128)(2,1)S(1)}) custom-call(bf16[36,3328]{1,0:T(8,128)(2,1)S(1)} %shard_map.50.own_ref, bf16[6656,2048]{1,0:T(8,128)(2,1)} %down_ref.1), custom_call_target="tpu_custom_call" | custom-call | bytes 1048576 | tf_op jit(solution)/shard_map/pallas_call | solution.py:156
  41.7 0.0 collective-permute-done.3
  41.7 0.1 convert_add_fusion.2
  41.7 0.0 collective-permute-done.4
  41.7 0.1 convert_add_fusion.1
  41.8 0.0 collective-permute-done.5
  41.9 0.1 fusion.refs_0_
  42.0 1.5 %collective-permute-start.8 = (bf16[36,1664]{1,0:T(8,128)(2,1)S(1)}, bf16[36,1664]{1,0:T(8,128)(2,1)S(1)}, u32[]{:S(2)}, u32[]{:S(2)}) collective-permute-start(bf16[36,1664]{1,0:T(8,128)(2,1)S(1)} %fusion.refs_0_), channel_id=1, source_target_pairs={{0,4},{4,0},{8,12},{12,8},{1,5},{5,1},{9,13},{13,9},{2,6},{6,2},{1... | collective-permute-start | bytes 359432 | tf_op jit(solution)/shard_map/ppermute | solution.py:214
  43.5 2.4 %collective-permute-start.7 = (bf16[36,1664]{1,0:T(8,128)(2,1)S(1)}, bf16[36,1664]{1,0:T(8,128)(2,1)S(1)}, u32[]{:S(2)}, u32[]{:S(2)}) collective-permute-start(bf16[36,1664]{1,0:T(8,128)(2,1)S(1)} %fusion.refs_0_), channel_id=1, source_target_pairs={{0,12},{4,8},{8,4},{12,0},{1,13},{5,9},{9,5},{13,1},{2,14},{6,10},... | collective-permute-start | bytes 359432 | tf_op jit(solution)/shard_map/ppermute | solution.py:214
  45.9 0.5 collective-permute-start.6
  46.4 0.1 pad_add_fusion.starts
  46.5 0.1 pad_add_fusion.1.starts
  46.5 0.5 collective-permute-done.8.refs_1_
  47.0 3.0 %shard_map.52.refs_2_ = f32[36,2048]{1,0:T(8,128)S(1)} custom-call(s32[2]{0:T(128)S(1)} %pad_add_fusion.1.starts, bf16[36,1664]{1,0:T(8,128)(2,1)S(1)} %fusion.refs_0_, bf16[36,1664]{1,0:T(8,128)(2,1)S(1)} %collective-permute-done.8.refs_1_, bf16[6656,2048]{1,0:T(8,128)(2,1)S(1)} %get-tuple-element.12.refs_2_.refs_3_), custom_call_target="tpu_custom_call" | custom-call | bytes 1048576 | tf_op jit(solution)/shard_map/pallas_call | solution.py:202
  50.0 2.9 %collective-permute-done.7.refs_1_ = bf16[36,1664]{1,0:T(8,128)(2,1)S(1)} collective-permute-done((bf16[36,1664]{1,0:T(8,128)(2,1)S(1)}, bf16[36,1664]{1,0:T(8,128)(2,1)S(1)}, u32[]{:S(2)}, u32[]{:S(2)}) %collective-permute-start.7) | collective-permute-done | bytes 119840 | tf_op jit(solution)/shard_map/ppermute | solution.py:214
  53.0 4.5 %collective-permute-done.6.refs_0_ = bf16[36,1664]{1,0:T(8,128)(2,1)S(1)} collective-permute-done((bf16[36,1664]{1,0:T(8,128)(2,1)S(1)}, bf16[36,1664]{1,0:T(8,128)(2,1)S(1)}, u32[]{:S(2)}, u32[]{:S(2)}) %collective-permute-start.6) | collective-permute-done | bytes 119840 | tf_op jit(solution)/shard_map/ppermute | solution.py:214
  57.5 3.1 %shard_map.53 = (bf16[9,2048]{1,0:T(8,128)(2,1)S(1)}, bf16[9,2048]{1,0:T(8,128)(2,1)S(1)}, bf16[9,2048]{1,0:T(8,128)(2,1)S(1)}, bf16[9,2048]{1,0:T(8,128)(2,1)S(1)}) custom-call(s32[2]{0:T(128)S(1)} %pad_add_fusion.starts, bf16[36,1664]{1,0:T(8,128)(2,1)S(1)} %collective-permute-done.6.refs_0_, bf16[36,1664]{1,0:T(8,128)(2,1)S(1)} %collective-permute-done.7.refs_1_, ...), custom_call_target="tpu_custom_call" | custom-call | bytes 1048576 | tf_op jit(solution)/shard_map/pallas_call | solution.py:202
  60.6 0.1 collective-permute-start.9
  60.7 1.6 %collective-permute-start.10 = (bf16[9,2048]{1,0:T(8,128)(2,1)S(1)}, bf16[9,2048]{1,0:T(8,128)(2,1)S(1)}, u32[]{:S(2)}, u32[]{:S(2)}) collective-permute-start(bf16[9,2048]{1,0:T(8,128)(2,1)S(1)} %get-tuple-element.15), channel_id=1, source_target_pairs={{0,2},{1,3},{2,0},{3,1},{4,6},{5,7},{6,4},{7,5},{8,10},{9,11},{10,... | collective-permute-start | bytes 110600 | tf_op jit(solution)/shard_map/ppermute | solution.py:214
  62.2 0.3 collective-permute-start.11
  62.5 0.0 collective-permute-done.9
  62.5 2.6 %collective-permute-done.10 = bf16[9,2048]{1,0:T(8,128)(2,1)S(1)} collective-permute-done((bf16[9,2048]{1,0:T(8,128)(2,1)S(1)}, bf16[9,2048]{1,0:T(8,128)(2,1)S(1)}, u32[]{:S(2)}, u32[]{:S(2)}) %collective-permute-start.10) | collective-permute-done | bytes 36896 | tf_op jit(solution)/shard_map/ppermute | solution.py:214
  65.2 1.1 %collective-permute-done.11 = bf16[9,2048]{1,0:T(8,128)(2,1)S(1)} collective-permute-done((bf16[9,2048]{1,0:T(8,128)(2,1)S(1)}, bf16[9,2048]{1,0:T(8,128)(2,1)S(1)}, u32[]{:S(2)}, u32[]{:S(2)}) %collective-permute-start.11) | collective-permute-done | bytes 36896 | tf_op jit(solution)/shard_map/ppermute | solution.py:214
  66.3 0.7 add_convert_fusion
  (1 shorter events, 0.0 us)
Async XLA Ops:
  0.0 8.3 %collective-permute-start.1 = (bf16[9,2048]{1,0:T(8,128)(2,1)}, bf16[9,2048]{1,0:T(8,128)(2,1)S(1)}, u32[]{:S(2)}, u32[]{:S(2)}) collective-permute-start(bf16[9,2048]{1,0:T(8,128)(2,1)} %param.4), channel_id=1, source_target_pairs={{0,2},{1,3},{2,0},{3,1},{4,6},{5,7},{6,4},{7,5},{8,10},{9,11},{10,... | collective-permute-start | bytes 110600 | tf_op jit(solution)/shard_map/ppermute | solution.py:214
  2.9 5.4 %collective-permute-start = (bf16[9,2048]{1,0:T(8,128)(2,1)}, bf16[9,2048]{1,0:T(8,128)(2,1)S(1)}, u32[]{:S(2)}, u32[]{:S(2)}) collective-permute-start(bf16[9,2048]{1,0:T(8,128)(2,1)} %param.4), channel_id=1, source_target_pairs={{0,1},{1,0},{2,3},{3,2},{4,5},{5,4},{6,7},{7,6},{8,9},{9,8},{10,11... | collective-permute-start | bytes 110600 | tf_op jit(solution)/shard_map/ppermute | solution.py:214
  2.9 5.4 %collective-permute-start.2 = (bf16[9,2048]{1,0:T(8,128)(2,1)}, bf16[9,2048]{1,0:T(8,128)(2,1)S(1)}, u32[]{:S(2)}, u32[]{:S(2)}) collective-permute-start(bf16[9,2048]{1,0:T(8,128)(2,1)} %param.4), channel_id=1, source_target_pairs={{0,3},{1,2},{2,1},{3,0},{4,7},{5,6},{6,5},{7,4},{8,11},{9,10},{10,... | collective-permute-start | bytes 110600 | tf_op jit(solution)/shard_map/ppermute | solution.py:214
  3.1 5.3 %copy-start = (bf16[9,2048]{1,0:T(8,128)(2,1)S(1)}, bf16[9,2048]{1,0:T(8,128)(2,1)}, u32[]{:S(2)}) copy-start(bf16[9,2048]{1,0:T(8,128)(2,1)} %param.4) | copy-start | bytes 110596
  10.6 31.1 %collective-permute-start.3 = (bf16[36,3328]{1,0:T(8,128)(2,1)S(1)}, bf16[36,3328]{1,0:T(8,128)(2,1)S(1)}, u32[]{:S(2)}, u32[]{:S(2)}) collective-permute-start(bf16[36,3328]{1,0:T(8,128)(2,1)S(1)} %shard_map.47._), channel_id=1, source_target_pairs={{0,12},{4,8},{8,4},{12,0},{1,13},{5,9},{9,5},{13,1},{2,14},{6,10},... | collective-permute-start | bytes 718856 | tf_op jit(solution)/shard_map/ppermute | solution.py:214
  20.5 21.3 %collective-permute-start.4 = (bf16[36,3328]{1,0:T(8,128)(2,1)S(1)}, bf16[36,3328]{1,0:T(8,128)(2,1)S(1)}, u32[]{:S(2)}, u32[]{:S(2)}) collective-permute-start(bf16[36,3328]{1,0:T(8,128)(2,1)S(1)} %shard_map.48._), channel_id=1, source_target_pairs={{0,8},{4,12},{8,0},{12,4},{1,9},{5,13},{9,1},{13,5},{2,10},{6,14},... | collective-permute-start | bytes 718856 | tf_op jit(solution)/shard_map/ppermute | solution.py:214
  26.3 15.5 %collective-permute-start.5 = (bf16[36,3328]{1,0:T(8,128)(2,1)S(1)}, bf16[36,3328]{1,0:T(8,128)(2,1)S(1)}, u32[]{:S(2)}, u32[]{:S(2)}) collective-permute-start(bf16[36,3328]{1,0:T(8,128)(2,1)S(1)} %shard_map.49._), channel_id=1, source_target_pairs={{0,4},{4,0},{8,12},{12,8},{1,5},{5,1},{9,13},{13,9},{2,6},{6,2},{1... | collective-permute-start | bytes 718856 | tf_op jit(solution)/shard_map/ppermute | solution.py:214
  42.0 5.1 %collective-permute-start.8 = (bf16[36,1664]{1,0:T(8,128)(2,1)S(1)}, bf16[36,1664]{1,0:T(8,128)(2,1)S(1)}, u32[]{:S(2)}, u32[]{:S(2)}) collective-permute-start(bf16[36,1664]{1,0:T(8,128)(2,1)S(1)} %fusion.refs_0_), channel_id=1, source_target_pairs={{0,4},{4,0},{8,12},{12,8},{1,5},{5,1},{9,13},{13,9},{2,6},{6,2},{1... | collective-permute-start | bytes 359432 | tf_op jit(solution)/shard_map/ppermute | solution.py:214
  43.5 9.5 %collective-permute-start.7 = (bf16[36,1664]{1,0:T(8,128)(2,1)S(1)}, bf16[36,1664]{1,0:T(8,128)(2,1)S(1)}, u32[]{:S(2)}, u32[]{:S(2)}) collective-permute-start(bf16[36,1664]{1,0:T(8,128)(2,1)S(1)} %fusion.refs_0_), channel_id=1, source_target_pairs={{0,12},{4,8},{8,4},{12,0},{1,13},{5,9},{9,5},{13,1},{2,14},{6,10},... | collective-permute-start | bytes 359432 | tf_op jit(solution)/shard_map/ppermute | solution.py:214
  45.9 11.6 %collective-permute-start.6 = (bf16[36,1664]{1,0:T(8,128)(2,1)S(1)}, bf16[36,1664]{1,0:T(8,128)(2,1)S(1)}, u32[]{:S(2)}, u32[]{:S(2)}) collective-permute-start(bf16[36,1664]{1,0:T(8,128)(2,1)S(1)} %fusion.refs_0_), channel_id=1, source_target_pairs={{0,8},{4,12},{8,0},{12,4},{1,9},{5,13},{9,1},{13,5},{2,10},{6,14},... | collective-permute-start | bytes 359432 | tf_op jit(solution)/shard_map/ppermute | solution.py:214
  60.6 1.9 %collective-permute-start.9 = (bf16[9,2048]{1,0:T(8,128)(2,1)S(1)}, bf16[9,2048]{1,0:T(8,128)(2,1)S(1)}, u32[]{:S(2)}, u32[]{:S(2)}) collective-permute-start(bf16[9,2048]{1,0:T(8,128)(2,1)S(1)} %get-tuple-element.14), channel_id=1, source_target_pairs={{0,1},{1,0},{2,3},{3,2},{4,5},{5,4},{6,7},{7,6},{8,9},{9,8},{10,11... | collective-permute-start | bytes 110600 | tf_op jit(solution)/shard_map/ppermute | solution.py:214
  60.7 4.5 %collective-permute-start.10 = (bf16[9,2048]{1,0:T(8,128)(2,1)S(1)}, bf16[9,2048]{1,0:T(8,128)(2,1)S(1)}, u32[]{:S(2)}, u32[]{:S(2)}) collective-permute-start(bf16[9,2048]{1,0:T(8,128)(2,1)S(1)} %get-tuple-element.15), channel_id=1, source_target_pairs={{0,2},{1,3},{2,0},{3,1},{4,6},{5,7},{6,4},{7,5},{8,10},{9,11},{10,... | collective-permute-start | bytes 110600 | tf_op jit(solution)/shard_map/ppermute | solution.py:214
  62.2 4.0 %collective-permute-start.11 = (bf16[9,2048]{1,0:T(8,128)(2,1)S(1)}, bf16[9,2048]{1,0:T(8,128)(2,1)S(1)}, u32[]{:S(2)}, u32[]{:S(2)}) collective-permute-start(bf16[9,2048]{1,0:T(8,128)(2,1)S(1)} %get-tuple-element.16), channel_id=1, source_target_pairs={{0,3},{1,2},{2,1},{3,0},{4,7},{5,6},{6,5},{7,4},{8,11},{9,10},{10,... | collective-permute-start | bytes 110600 | tf_op jit(solution)/shard_map/ppermute | solution.py:214

commit v3 on v0

v3 whole, which is shorter than its diff:
```python
import functools

import jax
import jax.numpy as jnp
from jax import lax
from jax.experimental import pallas as pl
from jax.experimental.pallas import tpu as pltpu
from jax.sharding import PartitionSpec as P

MIB = 1 << 20
STEP = 256
TOKEN_AXES = ("gy", "gz")
IN_HBM = pl.BlockSpec(memory_space=pltpu.HBM)
ANY = pl.BlockSpec(memory_space=pl.ANY)
WHOLE = pl.BlockSpec(memory_space=pltpu.VMEM)
SCALARS = pl.BlockSpec(memory_space=pltpu.SMEM)


def activate(gate, up):
    return (jax.nn.silu(gate) * up).astype(jnp.bfloat16)


def pieces_of(total, step):
    return [(start, min(step, total - start)) for start in range(0, total, step)]


def in_hbm(value):
    return pltpu.with_memory_space_constraint(value, pltpu.HBM)


def in_vmem(value):
    return pltpu.with_memory_space_constraint(value, pltpu.VMEM)


SMALL = pl.CostEstimate(flops=0, bytes_accessed=MIB, transcendentals=0)


def params(mib):
    return pltpu.CompilerParams(vmem_limit_bytes=mib * MIB)


def packed_pair_width(rows, width):
    return (rows // 8) * 2 * width + (width if rows % 8 else 0)


def pack_pair(out, gate, up):
    rows, width = gate.shape
    for g in range(rows // 8):
        for w, value in enumerate((gate, up)):
            at = (2 * g + w) * width
            out[:, at : at + width] = value[8 * g : 8 * g + 8].astype(out.dtype)
    if rows % 8:
        at = (rows // 8) * 2 * width
        tail = jnp.concatenate([gate[rows - 4 :], up[rows - 4 :]], axis=0)
        out[:, at : at + width] = tail.astype(out.dtype)


def start_copies(width, start_ref, gate_ref, up_ref, held, sems):
    columns = pl.ds(pl.multiple_of(start_ref[0], 128), width)
    copies = []
    for k, (row, rows) in enumerate(pieces_of(held.shape[1], STEP)):
        for w, weight in enumerate((gate_ref, up_ref)):
            copy = pltpu.make_async_copy(
                weight.at[pl.ds(row, rows), columns], held.at[w, pl.ds(row, rows)], sems.at[w, k]
            )
            copy.start()
            copies.append((w, row, rows, copy))
    return copies


def fetch_kernel(width, start_ref, gate_ref, up_ref, held, sems):
    for _, _, _, copy in start_copies(width, start_ref, gate_ref, up_ref, held, sems):
        copy.wait()


def fetch(gate_weight, up_weight, start, width):
    depth = gate_weight.shape[0]
    return pl.pallas_call(
        functools.partial(fetch_kernel, width),
        out_shape=pltpu.VMEM((2, depth, width), jnp.bfloat16),
        in_specs=[SCALARS, IN_HBM, IN_HBM],
        out_specs=WHOLE,
        scratch_shapes=[pltpu.SemaphoreType.DMA((2, len(pieces_of(depth, STEP))))],
        compiler_params=params(4),
        cost_estimate=SMALL,
    )(start, in_hbm(gate_weight), in_hbm(up_weight))


def multiply(x_ref, held, total, steps):
    for w, row, rows, copy in steps:
        if copy is not None:
            copy.wait()
        term = jnp.dot(
            x_ref[:, row : row + rows], held[w, row : row + rows, :], preferred_element_type=jnp.float32
        )
        if row == 0:
            total[w] = term
        else:
            total[w] += term


def held_kernel(x_ref, held, out, total):
    parts = pieces_of(x_ref.shape[1], STEP)
    multiply(x_ref, held, total, [(w, row, rows, None) for w in range(2) for row, rows in parts])
    pack_pair(out, total[0], total[1])


def gate_up_held(features, held):
    rows, width = features.shape[0], held.shape[2]
    return pl.pallas_call(
        held_kernel,
        out_shape=jax.ShapeDtypeStruct((8, packed_pair_width(rows, width)), jnp.bfloat16),
        in_specs=[WHOLE, WHOLE],
        out_specs=WHOLE,
        scratch_shapes=[pltpu.VMEM((2, rows, width), jnp.float32)],
        compiler_params=params(8),
        cost_estimate=SMALL,
    )(features, in_vmem(held))


def stream_kernel(width, start_ref, x_ref, gate_ref, up_ref, _, out, held, total, sems):
    copies = start_copies(width, start_ref, gate_ref, up_ref, held, sems)
    multiply(x_ref, held, total, copies)
    pack_pair(out, total[0], total[1])


def gate_up_stream(features, gate_weight, up_weight, start, width, after):
    rows, depth = features.shape
    return pl.pallas_call(
        functools.partial(stream_kernel, width),
        out_shape=jax.ShapeDtypeStruct((8, packed_pair_width(rows, width)), jnp.bfloat16),
        in_specs=[SCALARS, WHOLE, IN_HBM, IN_HBM, ANY],
        out_specs=WHOLE,
        scratch_shapes=[
            pltpu.VMEM((2, depth, width), jnp.bfloat16),
            pltpu.VMEM((2, rows, width), jnp.float32),
            pltpu.SemaphoreType.DMA((2, len(pieces_of(depth, STEP)))),
        ],
        compiler_params=params(18),
        cost_estimate=SMALL,
    )(start, features, in_hbm(gate_weight), in_hbm(up_weight), after)


def hidden_tail(rows, width):
    half = pl.cdiv(width // 2, 128) * 128
    return half if rows % 8 else 0


def activate_kernel(rows, width, summed, near, out):
    def pair(at):
        return summed[:, at : at + width] + near[:, at : at + width].astype(jnp.float32)

    for g in range(rows // 8):
        value = activate(pair(2 * g * width), pair((2 * g + 1) * width))
        out[:, g * width : (g + 1) * width] = value
    if rows % 8:
        last = pair((rows // 8) * 2 * width)
        value = activate(last[:4], last[4:]).astype(jnp.float32)
        half = hidden_tail(rows, width)
        right = jnp.concatenate([value[:, half:], jnp.zeros((4, 2 * half - width), jnp.float32)], axis=1)
        at = (rows // 8) * width
        out[:, at : at + half] = jnp.concatenate([value[:, :half], right], axis=0).astype(out.dtype)


def activate_packed(summed, near, rows, width):
    return pl.pallas_call(
        functools.partial(activate_kernel, rows, width),
        out_shape=jax.ShapeDtypeStruct(
            (8, (rows // 8) * width + hidden_tail(rows, width)), jnp.bfloat16
        ),
        in_specs=[WHOLE] * 2,
        out_specs=WHOLE,
        compiler_params=params(8),
        cost_estimate=SMALL,
    )(summed, near)


def down_kernel(first, rows, width, starts, *refs):
    blocks = starts.shape[0]
    hidden, refs = refs[:blocks], refs[blocks:]
    if not first:
        before, refs = refs[0], refs[1:]
    held, outs, (plain, total) = refs[0], refs[1:-2], refs[-2:]
    for b in range(blocks):
        for g in range(rows // 8):
            plain[8 * g : 8 * g + 8, :] = hidden[b][:, g * width : (g + 1) * width].astype(jnp.float32)
        if rows % 8:
            at, half = (rows // 8) * width, hidden_tail(rows, width)
            tail = hidden[b][:, at : at + half].astype(jnp.float32)
            plain[rows - 4 :, :half] = tail[:4]
            plain[rows - 4 :, half:] = tail[4:, : width - half]
        for row, tall in pieces_of(width, STEP):
            term = jnp.dot(
                plain[:, row : row + tall].astype(jnp.bfloat16),
                held[pl.ds(pl.multiple_of(starts[b] + row, 128), tall), :],
                preferred_element_type=jnp.float32,
            )
            if b == 0 and row == 0:
                total[...] = term if first else before[...] + term
            else:
                total[...] += term
    if len(outs) == 1:
        outs[0][...] = total[...]
    else:
        tall = outs[0].shape[0]
        for r, out in enumerate(outs):
            out[...] = total[r * tall : (r + 1) * tall, :].astype(out.dtype)


def down(hidden, starts, before, weight, rows, width, outs):
    columns = weight.shape[1]
    if outs == 1:
        shapes = [jax.ShapeDtypeStruct((rows, columns), jnp.float32)]
    else:
        shapes = [jax.ShapeDtypeStruct((rows // outs, columns), jnp.bfloat16)] * outs
    carried = [] if before is None else [before]
    return pl.pallas_call(
        functools.partial(down_kernel, before is None, rows, width),
        out_shape=shapes,
        in_specs=[SCALARS] + [WHOLE] * (len(hidden) + len(carried) + 1),
        out_specs=[WHOLE] * outs,
        scratch_shapes=[
            pltpu.VMEM((rows, width), jnp.float32),
            pltpu.VMEM((rows, columns), jnp.float32),
        ],
        compiler_params=params(8),
        cost_estimate=SMALL,
    )(starts, *hidden, *carried, in_vmem(weight))


def swap(value, axes, size, distance):
    return lax.ppermute(value, axes, [(i, i ^ distance) for i in range(size)])


def add(a, b):
    return a.astype(jnp.float32) + b.astype(jnp.float32)


def direct(tokens, gate_weight, up_weight, down_weight):
    n_gx = lax.axis_size("gx")
    n_token = lax.axis_size(TOKEN_AXES)
    me = lax.axis_index("gx")
    width = gate_weight.shape[1] // n_gx

    def starts_of(*distances):
        return jnp.stack([(me ^ d) * width for d in distances]).astype(jnp.int32)

    held = fetch(gate_weight, up_weight, starts_of(3), width)
    features = jnp.concatenate(
        [tokens] + [swap(tokens, TOKEN_AXES, n_token, r) for r in range(1, n_token)], axis=0
    )
    rows = features.shape[0]

    def block_for(d, after):
        return gate_up_stream(features, gate_weight, up_weight, starts_of(d), width, after)

    relayed = gate_up_held(features, held)
    arrived = swap(relayed, "gx", n_gx, 1)
    across = block_for(2, relayed)
    across = lax.optimization_barrier(add(across, arrived).astype(jnp.bfloat16))
    far = swap(across, "gx", n_gx, 2)
    beside = block_for(1, across)
    near = swap(beside, "gx", n_gx, 1)
    own = block_for(0, beside)
    summed = lax.optimization_barrier(add(own, far))
    hidden = activate_packed(summed, near, rows, width)

    first = [hidden, swap(hidden, "gx", n_gx, 1)]
    second = [swap(hidden, "gx", n_gx, d) for d in (2, 3)]
    (partial_sum,) = down(first, starts_of(0, 1), None, down_weight, rows, width, 1)
    outs = down(second, starts_of(2, 3), partial_sum, down_weight, rows, width, n_token)
    result = outs[0].astype(jnp.float32)
    for r in range(1, n_token):
        result = result + swap(outs[r], TOKEN_AXES, n_token, r).astype(jnp.float32)
    return result.astype(jnp.bfloat16)


def offloaded(tokens, gate_weight, up_weight, down_weight):
    features = lax.all_gather(tokens, TOKEN_AXES, axis=0, tiled=True)
    hidden_width = gate_weight.shape[1]
    gate_part = jnp.dot(features, gate_weight, preferred_element_type=jnp.float32)
    up_part = jnp.dot(features, up_weight, preferred_element_type=jnp.float32)
    summed = lax.psum(
        jnp.concatenate([gate_part, up_part], axis=1).astype(jnp.bfloat16), "gx"
    ).astype(jnp.float32)
    hidden = activate(summed[:, :hidden_width], summed[:, hidden_width:])
    partial_value = jnp.dot(hidden, down_weight, preferred_element_type=jnp.float32)
    return lax.psum_scatter(
        partial_value.astype(jnp.bfloat16), TOKEN_AXES, scatter_dimension=0, tiled=True
    )


def shards(tokens, gate_weight, up_weight, down_weight):
    n_gx = lax.axis_size("gx")
    n_token = lax.axis_size(TOKEN_AXES)
    rows = tokens.shape[0] * n_token
    tokens_fit = n_token > 1 and n_token & (n_token - 1) == 0 and rows % 4 == 0
    weights_fit = gate_weight.shape[1] % (128 * 4) == 0 and gate_weight.shape[0] % STEP == 0
    if n_gx == 4 and tokens_fit and weights_fit:
        return direct(tokens, gate_weight, up_weight, down_weight)
    return offloaded(tokens, gate_weight, up_weight, down_weight)


def solution(mesh):
    return jax.shard_map(
        shards,
        mesh=mesh,
        in_specs=(
            P(("grp", "gy", "gz"), "gx"),
            P("gx", ("gy", "gz")),
            P("gx", ("gy", "gz")),
            P(("gy", "gz"), "gx"),
        ),
        out_specs=P(("grp", "gy", "gz"), "gx"),
        check_vma=False,
    )
```

time: 145 us -> 60.5 us (0.42)
  waiting for transfers between devices: 84 us -> 11.1 us
  matrix products: 34.4 us -> 0 us
  Pallas kernels: 0 us -> 32 us
  starting transfers between devices: 0.04 us -> 16 us
  between operations: 14.1 us -> 0.18 us
  blocking collectives: 7.39 us -> 0 us
  local copies, waits for them, and re-layouts: 2.2 us -> 0.03 us
  other arithmetic: 2.46 us -> 1.01 us
    psum x1 -> x0, waiting for transfers between devices: 54.1 us -> none  [shards(): lax.psum(jnp.concatenate([gate_part, up_part], axis=1).astype(jnp.bfloat1...]
    dot_general x3 -> x0, matrix products: 34.4 us -> none  [the longest x1 11.9 us: shards(): jnp.dot(hidden, down_weight, preferred_element_type=jnp.float32)]
    pallas_call x0 -> x8, Pallas kernels: none -> 32 us  [the longest x3 18.4 us: gate_up_stream(): pl.pallas_call(functools.partial(stream_kernel, width), out_shape=jax.Sha...]
    unnamed x3 -> x0, waiting for transfers between devices: 29.9 us -> none
    ppermute x0 -> x12, starting transfers between devices: none -> 16 us  [swap(): return lax.ppermute(value, axes, [(i, i ^ distance) for i in range(size)])]
    ppermute x0 -> x12, waiting for transfers between devices: none -> 11.1 us  [swap(): return lax.ppermute(value, axes, [(i, i ^ distance) for i in range(size)])]
    all_gather x1 -> x0, blocking collectives: 7.39 us -> none  [shards(): features = lax.all_gather(tokens, ('gy', 'gz'), axis=0, tiled=True)]
    unnamed x5 -> x16, local copies, waits for them, and re-layouts: 2.2 us -> 0.03 us
  transfers between devices with their start and end apart: 2 -> 12, of which waited for: 2 -> 6; matrix products, arithmetic and copies ran while one was open for 0% -> 0% of each run, Pallas kernels for 0% -> 44%
where the time goes in v3:
time: 60.5 us; the launch traced here: 60.3 us
  Pallas kernels  32 us (53%)
  starting transfers between devices  16 us (26%)
  waiting for transfers between devices  11.1 us (18%)
  other arithmetic  1.01 us (2%)
    pallas_call x3, Pallas kernels, gate_up_stream(): pl.pallas_call(functools.partial(stream_kernel, width), out_shape=jax.Sha...  18.4 us
    ppermute x12, starting transfers between devices, swap(): return lax.ppermute(value, axes, [(i, i ^ distance) for i in range(size)])  16 us
    ppermute x12, waiting for transfers between devices, swap(): return lax.ppermute(value, axes, [(i, i ^ distance) for i in range(size)])  11.1 us
    pallas_call x2, Pallas kernels, down(): pl.pallas_call(functools.partial(down_kernel, before is None, rows, width...  6.09 us
    pallas_call x1, Pallas kernels, fetch(): pl.pallas_call(functools.partial(fetch_kernel, width), out_shape=pltpu.VM...  5.23 us
    pallas_call x1, Pallas kernels, gate_up_held(): pl.pallas_call(held_kernel, out_shape=jax.ShapeDtypeStruct((8, packed_pai...  2.17 us
  transfers between devices with their start and end apart: 12, of which 6 were waited for; matrix products, arithmetic and copies ran while one was open for 0% of the time, Pallas kernels for 44%

profile of v3, /device:TPU:0, one launch (start us, length us, event | category | flops | bytes accessed | tf_op | source)
XLA Modules:
  0.0 60.3 jit_solution(16225120996167249323)
XLA Ops:
  0.0 0.5 collective-permute-start
  0.5 2.5 %collective-permute-start.1 = (bf16[9,2048]{1,0:T(8,128)(2,1)}, bf16[9,2048]{1,0:T(8,128)(2,1)S(1)}, u32[]{:S(2)}, u32[]{:S(2)}) collective-permute-start(bf16[9,2048]{1,0:T(8,128)(2,1)} %param.4), channel_id=1, source_target_pairs={{0,2},{1,3},{2,0},{3,1},{4,6},{5,7},{6,4},{7,5},{8,10},{9,11},{10,... | collective-permute-start | bytes 110600 | tf_op jit(solution)/shard_map/ppermute | solution.py:232
  2.9 0.1 collective-permute-start.2
  3.1 0.0 copy-start
  3.1 5.2 %shard_map.46.held = bf16[2,2048,1664]{2,1,0:T(8,128)(2,1)S(1)} custom-call(s32[1]{0:T(128)} %bitcast.1.start_ref, bf16[2048,6656]{1,0:T(8,128)(2,1)} %gate_ref.7, bf16[2048,6656]{1,0:T(8,128)(2,1)} %up_ref.7), custom_call_target="tpu_custom_call" | custom-call | bytes 1048576 | tf_op jit(solution)/shard_map/pallas_call | solution.py:78
  8.3 0.0 collective-permute-done
  8.3 0.0 collective-permute-done.1
  8.3 0.0 collective-permute-done.2
  8.4 0.0 copy-done
  8.4 0.1 pad_maximum_fusion.x_ref
  8.5 2.2 %shard_map.47._ = bf16[8,14976]{1,0:T(8,128)(2,1)S(1)} custom-call(bf16[36,2048]{1,0:T(8,128)(2,1)S(1)} %pad_maximum_fusion.x_ref, bf16[2,2048,1664]{2,1,0:T(8,128)(2,1)S(1)} %shard_map.46.held), custom_call_target="tpu_custom_call" | custom-call | bytes 1048576 | tf_op jit(solution)/shard_map/pallas_call | solution.py:110
  10.6 1.7 %collective-permute-start.3 = (bf16[8,14976]{1,0:T(8,128)(2,1)S(1)}, bf16[8,14976]{1,0:T(8,128)(2,1)S(1)}, u32[]{:S(2)}, u32[]{:S(2)}) collective-permute-start(bf16[8,14976]{1,0:T(8,128)(2,1)S(1)} %shard_map.47._), channel_id=1, source_target_pairs={{0,4},{4,0},{8,12},{12,8},{1,5},{5,1},{9,13},{13,9},{2,6},{6,2},{1... | collective-permute-start | bytes 718856 | tf_op jit(solution)/shard_map/ppermute | solution.py:232
  12.3 5.8 %shard_map.48 = bf16[8,14976]{1,0:T(8,128)(2,1)S(1)} custom-call(s32[1]{0:T(128)} %bitcast.start_ref, bf16[36,2048]{1,0:T(8,128)(2,1)S(1)} %pad_maximum_fusion.x_ref, bf16[2048,6656]{1,0:T(8,128)(2,1)} %gate_ref.7, bf16[2048,6656]{1,0:T(8,128)(2,1)} %up_ref.7, bf16[8,14976]{1,0:T(8,128)(2,1)S(1)} %shard_map.47._), custom_call_target="tpu_custom_call" | custom-call | bytes 1048576 | tf_op jit(solution)/shard_map/pallas_call | solution.py:129
  18.1 0.5 collective-permute-done.3
  18.6 0.1 add_convert_fusion._
  18.7 2.8 %collective-permute-start.4 = (bf16[8,14976]{1,0:T(8,128)(2,1)S(1)}, bf16[8,14976]{1,0:T(8,128)(2,1)S(1)}, u32[]{:S(2)}, u32[]{:S(2)}) collective-permute-start(bf16[8,14976]{1,0:T(8,128)(2,1)S(1)} %add_convert_fusion._), channel_id=1, source_target_pairs={{0,8},{4,12},{8,0},{12,4},{1,9},{5,13},{9,1},{13,5},{2,10},{6,14},... | collective-permute-start | bytes 718856 | tf_op jit(solution)/shard_map/ppermute | solution.py:232
  21.5 0.0 slice-start
  21.5 0.0 slice-start.1
  21.5 0.0 slice-start.2
  21.5 0.0 slice-start.3
  21.5 6.0 %shard_map.49._ = bf16[8,14976]{1,0:T(8,128)(2,1)S(1)} custom-call(s32[1]{0:T(128)} %bitcast.3.start_ref, bf16[36,2048]{1,0:T(8,128)(2,1)S(1)} %pad_maximum_fusion.x_ref, bf16[2048,6656]{1,0:T(8,128)(2,1)} %gate_ref.7, bf16[2048,6656]{1,0:T(8,128)(2,1)} %up_ref.7, bf16[8,14976]{1,0:T(8,128)(2,1)S(1)} %add_convert_fusion._), custom_call_target="tpu_custom_call" | custom-call | bytes 1048576 | tf_op jit(solution)/shard_map/pallas_call | solution.py:129
  27.5 1.7 %collective-permute-start.5 = (bf16[8,14976]{1,0:T(8,128)(2,1)S(1)}, bf16[8,14976]{1,0:T(8,128)(2,1)S(1)}, u32[]{:S(2)}, u32[]{:S(2)}) collective-permute-start(bf16[8,14976]{1,0:T(8,128)(2,1)S(1)} %shard_map.49._), channel_id=1, source_target_pairs={{0,4},{4,0},{8,12},{12,8},{1,5},{5,1},{9,13},{13,9},{2,6},{6,2},{1... | collective-permute-start | bytes 718856 | tf_op jit(solution)/shard_map/ppermute | solution.py:232
  29.2 0.0 slice-start.4
  29.2 0.0 slice-start.5
  29.2 0.0 slice-start.6
  29.2 6.6 %shard_map.50 = bf16[8,14976]{1,0:T(8,128)(2,1)S(1)} custom-call(s32[1]{0:T(128)} %bitcast.2.start_ref, bf16[36,2048]{1,0:T(8,128)(2,1)S(1)} %pad_maximum_fusion.x_ref, bf16[2048,6656]{1,0:T(8,128)(2,1)} %gate_ref.7, bf16[2048,6656]{1,0:T(8,128)(2,1)} %up_ref.7, bf16[8,14976]{1,0:T(8,128)(2,1)S(1)} %shard_map.49._), custom_call_target="tpu_custom_call" | custom-call | bytes 1048576 | tf_op jit(solution)/shard_map/pallas_call | solution.py:129
  35.8 0.0 collective-permute-done.4
  35.8 0.1 convert_add_fusion.summed
  35.9 1.3 %collective-permute-done.5.near = bf16[8,14976]{1,0:T(8,128)(2,1)S(1)} collective-permute-done((bf16[8,14976]{1,0:T(8,128)(2,1)S(1)}, bf16[8,14976]{1,0:T(8,128)(2,1)S(1)}, u32[]{:S(2)}, u32[]{:S(2)}) %collective-permute-start.5) | collective-permute-done | bytes 239648 | tf_op jit(solution)/shard_map/ppermute | solution.py:232
  37.2 0.1 shard_map.51.refs_0_
  37.3 0.1 collective-permute-start.8
  37.4 4.1 %collective-permute-start.6 = (bf16[8,7552]{1,0:T(8,128)(2,1)S(1)}, bf16[8,7552]{1,0:T(8,128)(2,1)S(1)}, u32[]{:S(2)}, u32[]{:S(2)}) collective-permute-start(bf16[8,7552]{1,0:T(8,128)(2,1)S(1)} %shard_map.51.refs_0_), channel_id=1, source_target_pairs={{0,8},{4,12},{8,0},{12,4},{1,9},{5,13},{9,1},{13,5},{2,10},{6,14},... | collective-permute-start | bytes 362504 | tf_op jit(solution)/shard_map/ppermute | solution.py:232
  41.5 0.3 collective-permute-start.7
  41.8 0.1 pad_add_fusion.1.starts
  41.9 0.1 pad_add_fusion.starts
  41.9 2.5 %collective-permute-done.8.refs_1_ = bf16[8,7552]{1,0:T(8,128)(2,1)S(1)} collective-permute-done((bf16[8,7552]{1,0:T(8,128)(2,1)S(1)}, bf16[8,7552]{1,0:T(8,128)(2,1)S(1)}, u32[]{:S(2)}, u32[]{:S(2)}) %collective-permute-start.8) | collective-permute-done | bytes 120864 | tf_op jit(solution)/shard_map/ppermute | solution.py:232
  44.4 0.0 slice-done
  44.4 0.0 slice-done.1
  44.4 0.0 slice-done.2
  44.4 0.0 slice-done.3
  44.4 0.0 slice-done.4
  44.4 0.0 slice-done.5
  44.4 0.0 slice-done.6
  44.5 3.0 %shard_map.52.refs_2_ = f32[36,2048]{1,0:T(8,128)S(1)} custom-call(s32[2]{0:T(128)S(1)} %pad_add_fusion.1.starts, bf16[8,7552]{1,0:T(8,128)(2,1)S(1)} %shard_map.51.refs_0_, bf16[8,7552]{1,0:T(8,128)(2,1)S(1)} %collective-permute-done.8.refs_1_, bf16[6656,2048]{1,0:T(8,128)(2,1)S(1)} %bitcast.5), custom_call_target="tpu_custom_call" | custom-call | bytes 1048576 | tf_op jit(solution)/shard_map/pallas_call | solution.py:217
  47.5 3.3 %collective-permute-done.6.refs_0_ = bf16[8,7552]{1,0:T(8,128)(2,1)S(1)} collective-permute-done((bf16[8,7552]{1,0:T(8,128)(2,1)S(1)}, bf16[8,7552]{1,0:T(8,128)(2,1)S(1)}, u32[]{:S(2)}, u32[]{:S(2)}) %collective-permute-start.6) | collective-permute-done | bytes 120864 | tf_op jit(solution)/shard_map/ppermute | solution.py:232
  50.8 0.0 collective-permute-done.7.refs_1_
  50.8 3.1 %shard_map.53 = (bf16[9,2048]{1,0:T(8,128)(2,1)S(1)}, bf16[9,2048]{1,0:T(8,128)(2,1)S(1)}, bf16[9,2048]{1,0:T(8,128)(2,1)S(1)}, bf16[9,2048]{1,0:T(8,128)(2,1)S(1)}) custom-call(s32[2]{0:T(128)S(1)} %pad_add_fusion.starts, bf16[8,7552]{1,0:T(8,128)(2,1)S(1)} %collective-permute-done.6.refs_0_, bf16[8,7552]{1,0:T(8,128)(2,1)S(1)} %collective-permute-done.7.refs_1_, ...), custom_call_target="tpu_custom_call" | custom-call | bytes 1048576 | tf_op jit(solution)/shard_map/pallas_call | solution.py:217
  53.9 1.6 %collective-permute-start.10 = (bf16[9,2048]{1,0:T(8,128)(2,1)S(1)}, bf16[9,2048]{1,0:T(8,128)(2,1)S(1)}, u32[]{:S(2)}, u32[]{:S(2)}) collective-permute-start(bf16[9,2048]{1,0:T(8,128)(2,1)S(1)} %get-tuple-element.11), channel_id=1, source_target_pairs={{0,2},{1,3},{2,0},{3,1},{4,6},{5,7},{6,4},{7,5},{8,10},{9,11},{10,... | collective-permute-start | bytes 110600 | tf_op jit(solution)/shard_map/ppermute | solution.py:232
  55.5 0.0 collective-permute-start.11
  55.5 0.6 %collective-permute-start.9 = (bf16[9,2048]{1,0:T(8,128)(2,1)S(1)}, bf16[9,2048]{1,0:T(8,128)(2,1)S(1)}, u32[]{:S(2)}, u32[]{:S(2)}) collective-permute-start(bf16[9,2048]{1,0:T(8,128)(2,1)S(1)} %get-tuple-element.10), channel_id=1, source_target_pairs={{0,1},{1,0},{2,3},{3,2},{4,5},{5,4},{6,7},{7,6},{8,9},{9,8},{10,11... | collective-permute-start | bytes 110600 | tf_op jit(solution)/shard_map/ppermute | solution.py:232
  56.1 2.1 %collective-permute-done.10 = bf16[9,2048]{1,0:T(8,128)(2,1)S(1)} collective-permute-done((bf16[9,2048]{1,0:T(8,128)(2,1)S(1)}, bf16[9,2048]{1,0:T(8,128)(2,1)S(1)}, u32[]{:S(2)}, u32[]{:S(2)}) %collective-permute-start.10) | collective-permute-done | bytes 36896 | tf_op jit(solution)/shard_map/ppermute | solution.py:232
  58.2 1.4 %collective-permute-done.11 = bf16[9,2048]{1,0:T(8,128)(2,1)S(1)} collective-permute-done((bf16[9,2048]{1,0:T(8,128)(2,1)S(1)}, bf16[9,2048]{1,0:T(8,128)(2,1)S(1)}, u32[]{:S(2)}, u32[]{:S(2)}) %collective-permute-start.11) | collective-permute-done | bytes 36896 | tf_op jit(solution)/shard_map/ppermute | solution.py:232
  59.6 0.0 collective-permute-done.9
  59.6 0.7 %add_convert_fusion.1 = bf16[9,2048]{1,0:T(8,128)(2,1)} fusion(bf16[9,2048]{1,0:T(8,128)(2,1)S(1)} %collective-permute-done.11, bf16[9,2048]{1,0:T(8,128)(2,1)S(1)} %collective-permute-done.10, bf16[9,2048]{1,0:T(8,128)(2,1)S(1)} %collective-permute-done.9, bf16[9,2048]{1,0:T(8,128)(2,1)S(1)} %get-tuple-element.9), kind=kLoop, calls=%fused_computation.3 | loop fusion | flops 147456 | bytes 184320 | tf_op jit(solution)/shard_map/convert_element_type | solution.py:275
  (1 shorter events, 0.0 us)
Async XLA Ops:
  0.0 8.3 %collective-permute-start = (bf16[9,2048]{1,0:T(8,128)(2,1)}, bf16[9,2048]{1,0:T(8,128)(2,1)S(1)}, u32[]{:S(2)}, u32[]{:S(2)}) collective-permute-start(bf16[9,2048]{1,0:T(8,128)(2,1)} %param.4), channel_id=1, source_target_pairs={{0,1},{1,0},{2,3},{3,2},{4,5},{5,4},{6,7},{7,6},{8,9},{9,8},{10,11... | collective-permute-start | bytes 110600 | tf_op jit(solution)/shard_map/ppermute | solution.py:232
  0.5 7.9 %collective-permute-start.1 = (bf16[9,2048]{1,0:T(8,128)(2,1)}, bf16[9,2048]{1,0:T(8,128)(2,1)S(1)}, u32[]{:S(2)}, u32[]{:S(2)}) collective-permute-start(bf16[9,2048]{1,0:T(8,128)(2,1)} %param.4), channel_id=1, source_target_pairs={{0,2},{1,3},{2,0},{3,1},{4,6},{5,7},{6,4},{7,5},{8,10},{9,11},{10,... | collective-permute-start | bytes 110600 | tf_op jit(solution)/shard_map/ppermute | solution.py:232
  2.9 5.4 %collective-permute-start.2 = (bf16[9,2048]{1,0:T(8,128)(2,1)}, bf16[9,2048]{1,0:T(8,128)(2,1)S(1)}, u32[]{:S(2)}, u32[]{:S(2)}) collective-permute-start(bf16[9,2048]{1,0:T(8,128)(2,1)} %param.4), channel_id=1, source_target_pairs={{0,3},{1,2},{2,1},{3,0},{4,7},{5,6},{6,5},{7,4},{8,11},{9,10},{10,... | collective-permute-start | bytes 110600 | tf_op jit(solution)/shard_map/ppermute | solution.py:232
  3.1 5.3 %copy-start = (bf16[9,2048]{1,0:T(8,128)(2,1)S(1)}, bf16[9,2048]{1,0:T(8,128)(2,1)}, u32[]{:S(2)}) copy-start(bf16[9,2048]{1,0:T(8,128)(2,1)} %param.4) | copy-start | bytes 110596
  10.6 8.0 %collective-permute-start.3 = (bf16[8,14976]{1,0:T(8,128)(2,1)S(1)}, bf16[8,14976]{1,0:T(8,128)(2,1)S(1)}, u32[]{:S(2)}, u32[]{:S(2)}) collective-permute-start(bf16[8,14976]{1,0:T(8,128)(2,1)S(1)} %shard_map.47._), channel_id=1, source_target_pairs={{0,4},{4,0},{8,12},{12,8},{1,5},{5,1},{9,13},{13,9},{2,6},{6,2},{1... | collective-permute-start | bytes 718856 | tf_op jit(solution)/shard_map/ppermute | solution.py:232
  18.7 17.2 %collective-permute-start.4 = (bf16[8,14976]{1,0:T(8,128)(2,1)S(1)}, bf16[8,14976]{1,0:T(8,128)(2,1)S(1)}, u32[]{:S(2)}, u32[]{:S(2)}) collective-permute-start(bf16[8,14976]{1,0:T(8,128)(2,1)S(1)} %add_convert_fusion._), channel_id=1, source_target_pairs={{0,8},{4,12},{8,0},{12,4},{1,9},{5,13},{9,1},{13,5},{2,10},{6,14},... | collective-permute-start | bytes 718856 | tf_op jit(solution)/shard_map/ppermute | solution.py:232
  21.5 22.9 %slice-start = ((s8[27262976]{0:T(1024)(128)(4,1)}), s8[4194304]{0:T(1024)(128)(4,1)S(1)}, s32[]{:S(2)}) async-start(s8[27262976]{0:T(1024)(128)(4,1)} %bitcast.4), calls=%async_computation | async-start | bytes 8388608
  21.5 22.9 %slice-start.1 = ((s8[27262976]{0:T(1024)(128)(4,1)}), s8[4194304]{0:T(1024)(128)(4,1)S(1)}, s32[]{:S(2)}) async-start(s8[27262976]{0:T(1024)(128)(4,1)} %bitcast.4), calls=%async_computation.1 | async-start | bytes 8388608
  21.5 22.9 %slice-start.2 = ((s8[27262976]{0:T(1024)(128)(4,1)}), s8[4194304]{0:T(1024)(128)(4,1)S(1)}, s32[]{:S(2)}) async-start(s8[27262976]{0:T(1024)(128)(4,1)} %bitcast.4), calls=%async_computation.2 | async-start | bytes 8388608
  21.5 22.9 %slice-start.3 = ((s8[27262976]{0:T(1024)(128)(4,1)}), s8[4194304]{0:T(1024)(128)(4,1)S(1)}, s32[]{:S(2)}) async-start(s8[27262976]{0:T(1024)(128)(4,1)} %bitcast.4), calls=%async_computation.3 | async-start | bytes 8388608
  27.5 9.7 %collective-permute-start.5 = (bf16[8,14976]{1,0:T(8,128)(2,1)S(1)}, bf16[8,14976]{1,0:T(8,128)(2,1)S(1)}, u32[]{:S(2)}, u32[]{:S(2)}) collective-permute-start(bf16[8,14976]{1,0:T(8,128)(2,1)S(1)} %shard_map.49._), channel_id=1, source_target_pairs={{0,4},{4,0},{8,12},{12,8},{1,5},{5,1},{9,13},{13,9},{2,6},{6,2},{1... | collective-permute-start | bytes 718856 | tf_op jit(solution)/shard_map/ppermute | solution.py:232
  29.2 15.2 %slice-start.4 = ((s8[27262976]{0:T(1024)(128)(4,1)}), s8[4194304]{0:T(1024)(128)(4,1)S(1)}, s32[]{:S(2)}) async-start(s8[27262976]{0:T(1024)(128)(4,1)} %bitcast.4), calls=%async_computation.4 | async-start | bytes 8388608
  29.2 15.2 %slice-start.5 = ((s8[27262976]{0:T(1024)(128)(4,1)}), s8[4194304]{0:T(1024)(128)(4,1)S(1)}, s32[]{:S(2)}) async-start(s8[27262976]{0:T(1024)(128)(4,1)} %bitcast.4), calls=%async_computation.5 | async-start | bytes 8388608
  29.2 15.2 %slice-start.6 = ((s8[27262976]{0:T(1024)(128)(4,1)}), s8[2097152]{0:T(1024)(128)(4,1)S(1)}, s32[]{:S(2)}) async-start(s8[27262976]{0:T(1024)(128)(4,1)} %bitcast.4), calls=%async_computation.6 | async-start | bytes 4194304
  37.3 7.1 %collective-permute-start.8 = (bf16[8,7552]{1,0:T(8,128)(2,1)S(1)}, bf16[8,7552]{1,0:T(8,128)(2,1)S(1)}, u32[]{:S(2)}, u32[]{:S(2)}) collective-permute-start(bf16[8,7552]{1,0:T(8,128)(2,1)S(1)} %shard_map.51.refs_0_), channel_id=1, source_target_pairs={{0,4},{4,0},{8,12},{12,8},{1,5},{5,1},{9,13},{13,9},{2,6},{6,2},{1... | collective-permute-start | bytes 362504 | tf_op jit(solution)/shard_map/ppermute | solution.py:232
  37.4 13.4 %collective-permute-start.6 = (bf16[8,7552]{1,0:T(8,128)(2,1)S(1)}, bf16[8,7552]{1,0:T(8,128)(2,1)S(1)}, u32[]{:S(2)}, u32[]{:S(2)}) collective-permute-start(bf16[8,7552]{1,0:T(8,128)(2,1)S(1)} %shard_map.51.refs_0_), channel_id=1, source_target_pairs={{0,8},{4,12},{8,0},{12,4},{1,9},{5,13},{9,1},{13,5},{2,10},{6,14},... | collective-permute-start | bytes 362504 | tf_op jit(solution)/shard_map/ppermute | solution.py:232
  41.5 9.3 %collective-permute-start.7 = (bf16[8,7552]{1,0:T(8,128)(2,1)S(1)}, bf16[8,7552]{1,0:T(8,128)(2,1)S(1)}, u32[]{:S(2)}, u32[]{:S(2)}) collective-permute-start(bf16[8,7552]{1,0:T(8,128)(2,1)S(1)} %shard_map.51.refs_0_), channel_id=1, source_target_pairs={{0,12},{4,8},{8,4},{12,0},{1,13},{5,9},{9,5},{13,1},{2,14},{6,10},... | collective-permute-start | bytes 362504 | tf_op jit(solution)/shard_map/ppermute | solution.py:232
  53.9 4.3 %collective-permute-start.10 = (bf16[9,2048]{1,0:T(8,128)(2,1)S(1)}, bf16[9,2048]{1,0:T(8,128)(2,1)S(1)}, u32[]{:S(2)}, u32[]{:S(2)}) collective-permute-start(bf16[9,2048]{1,0:T(8,128)(2,1)S(1)} %get-tuple-element.11), channel_id=1, source_target_pairs={{0,2},{1,3},{2,0},{3,1},{4,6},{5,7},{6,4},{7,5},{8,10},{9,11},{10,... | collective-permute-start | bytes 110600 | tf_op jit(solution)/shard_map/ppermute | solution.py:232
  55.5 4.2 %collective-permute-start.11 = (bf16[9,2048]{1,0:T(8,128)(2,1)S(1)}, bf16[9,2048]{1,0:T(8,128)(2,1)S(1)}, u32[]{:S(2)}, u32[]{:S(2)}) collective-permute-start(bf16[9,2048]{1,0:T(8,128)(2,1)S(1)} %get-tuple-element.12), channel_id=1, source_target_pairs={{0,3},{1,2},{2,1},{3,0},{4,7},{5,6},{6,5},{7,4},{8,11},{9,10},{10,... | collective-permute-start | bytes 110600 | tf_op jit(solution)/shard_map/ppermute | solution.py:232
  55.5 4.2 %collective-permute-start.9 = (bf16[9,2048]{1,0:T(8,128)(2,1)S(1)}, bf16[9,2048]{1,0:T(8,128)(2,1)S(1)}, u32[]{:S(2)}, u32[]{:S(2)}) collective-permute-start(bf16[9,2048]{1,0:T(8,128)(2,1)S(1)} %get-tuple-element.10), channel_id=1, source_target_pairs={{0,1},{1,0},{2,3},{3,2},{4,5},{5,4},{6,7},{7,6},{8,9},{9,8},{10,11... | collective-permute-start | bytes 110600 | tf_op jit(solution)/shard_map/ppermute | solution.py:232

commit v4 on v3

--- a/solution.py
+++ b/solution.py
@@ -175,57 +175,58 @@
     )(summed, near)
 
 
-def down_kernel(first, rows, width, starts, *refs):
-    blocks = starts.shape[0]
-    hidden, refs = refs[:blocks], refs[blocks:]
+def down_kernel(first, last, rows, width, start, *refs):
+    if last:
+        slots, refs = refs[0], refs[1:]
+    hidden, refs = refs[0], refs[1:]
     if not first:
         before, refs = refs[0], refs[1:]
-    held, outs, (plain, total) = refs[0], refs[1:-2], refs[-2:]
-    for b in range(blocks):
-        for g in range(rows // 8):
-            plain[8 * g : 8 * g + 8, :] = hidden[b][:, g * width : (g + 1) * width].astype(jnp.float32)
-        if rows % 8:
-            at, half = (rows // 8) * width, hidden_tail(rows, width)
-            tail = hidden[b][:, at : at + half].astype(jnp.float32)
-            plain[rows - 4 :, :half] = tail[:4]
-            plain[rows - 4 :, half:] = tail[4:, : width - half]
-        for row, tall in pieces_of(width, STEP):
-            term = jnp.dot(
-                plain[:, row : row + tall].astype(jnp.bfloat16),
-                held[pl.ds(pl.multiple_of(starts[b] + row, 128), tall), :],
-                preferred_element_type=jnp.float32,
-            )
-            if b == 0 and row == 0:
-                total[...] = term if first else before[...] + term
-            else:
-                total[...] += term
-    if len(outs) == 1:
-        outs[0][...] = total[...]
+    held, out, plain, total = refs
+    for g in range(rows // 8):
+        plain[8 * g : 8 * g + 8, :] = hidden[:, g * width : (g + 1) * width].astype(jnp.float32)
+    if rows % 8:
+        at, half = (rows // 8) * width, hidden_tail(rows, width)
+        tail = hidden[:, at : at + half].astype(jnp.float32)
+        plain[rows - 4 :, :half] = tail[:4]
+        plain[rows - 4 :, half:] = tail[4:, : width - half]
+    if not last:
+        total = out
+    for row, tall in pieces_of(width, STEP):
+        term = jnp.dot(
+            plain[:, row : row + tall].astype(jnp.bfloat16),
+            held[pl.ds(pl.multiple_of(start[0] + row, 128), tall), :],
+            preferred_element_type=jnp.float32,
+        )
+        if row == 0:
+            total[...] = term if first else before[...] + term
+        else:
+            total[...] += term
+    if last:
+        tall = out.shape[1]
+        for r in range(out.shape[0]):
+            out[slots[r]] = total[r * tall : (r + 1) * tall, :].astype(out.dtype)
+
+
+def down(hidden, start, before, weight, rows, width, slots):
+    columns = weight.shape[1]
+    scalars = [start] if slots is None else [start, slots]
+    if slots is None:
+        shape = jax.ShapeDtypeStruct((rows, columns), jnp.float32)
     else:
-        tall = outs[0].shape[0]
-        for r, out in enumerate(outs):
-            out[...] = total[r * tall : (r + 1) * tall, :].astype(out.dtype)
-
-
-def down(hidden, starts, before, weight, rows, width, outs):
-    columns = weight.shape[1]
-    if outs == 1:
-        shapes = [jax.ShapeDtypeStruct((rows, columns), jnp.float32)]
-    else:
-        shapes = [jax.ShapeDtypeStruct((rows // outs, columns), jnp.bfloat16)] * outs
+        shape = jax.ShapeDtypeStruct((slots.shape[0], rows // slots.shape[0], columns), jnp.bfloat16)
     carried = [] if before is None else [before]
     return pl.pallas_call(
-        functools.partial(down_kernel, before is None, rows, width),
-        out_shape=shapes,
-        in_specs=[SCALARS] + [WHOLE] * (len(hidden) + len(carried) + 1),
-        out_specs=[WHOLE] * outs,
+        functools.partial(down_kernel, before is None, slots is not None, rows, width),
+        out_shape=shape,
+        in_specs=[SCALARS] * len(scalars) + [WHOLE] * (2 + len(carried)),
+        out_specs=WHOLE,
         scratch_shapes=[
             pltpu.VMEM((rows, width), jnp.float32),
             pltpu.VMEM((rows, columns), jnp.float32),
         ],
         compiler_params=params(8),
         cost_estimate=SMALL,
-    )(starts, *hidden, *carried, in_vmem(weight))
+    )(*scalars, hidden, *carried, in_vmem(weight))
 
 
 def swap(value, axes, size, distance):
@@ -265,13 +266,18 @@
     summed = lax.optimization_barrier(add(own, far))
     hidden = activate_packed(summed, near, rows, width)
 
-    first = [hidden, swap(hidden, "gx", n_gx, 1)]
-    second = [swap(hidden, "gx", n_gx, d) for d in (2, 3)]
-    (partial_sum,) = down(first, starts_of(0, 1), None, down_weight, rows, width, 1)
-    outs = down(second, starts_of(2, 3), partial_sum, down_weight, rows, width, n_token)
-    result = outs[0].astype(jnp.float32)
+    total = None
+    for d in range(n_gx - 1):
+        block = swap(hidden, "gx", n_gx, d) if d else hidden
+        total = down(block, starts_of(d), total, down_weight, rows, width, None)
+    block = swap(hidden, "gx", n_gx, n_gx - 1)
+    token_me = lax.axis_index(TOKEN_AXES)
+    slots = jnp.stack([token_me ^ r for r in range(n_token)]).astype(jnp.int32)
+    terms = down(block, starts_of(n_gx - 1), total, down_weight, rows, width, slots)
+    terms = lax.all_to_all(terms, TOKEN_AXES, 0, 0, tiled=True)
+    result = terms[0].astype(jnp.float32)
     for r in range(1, n_token):
-        result = result + swap(outs[r], TOKEN_AXES, n_token, r).astype(jnp.float32)
+        result = result + terms[r].astype(jnp.float32)
     return result.astype(jnp.bfloat16)
 
 

time: 60.5 us -> 74.8 us (1.24)
  local copies, waits for them, and re-layouts: 0.03 us -> 17.5 us
  blocking collectives: 0 us -> 8.77 us
  waiting for transfers between devices: 11.1 us -> 2.95 us
  starting transfers between devices: 16 us -> 13.8 us
  Pallas kernels: 32 us -> 30.5 us
    unnamed x16 -> x6, local copies, waits for them, and re-layouts: 0.03 us -> 17.5 us
    all_to_all x0 -> x1, blocking collectives: none -> 8.77 us  [direct(): terms = lax.all_to_all(terms, TOKEN_AXES, 0, 0, tiled=True)]
    ppermute x12 -> x9, waiting for transfers between devices: 11.1 us -> 2.95 us  [swap(): return lax.ppermute(value, axes, [(i, i ^ distance) for i in range(size)])]
    ppermute x12 -> x9, starting transfers between devices: 16 us -> 13.8 us  [swap(): return lax.ppermute(value, axes, [(i, i ^ distance) for i in range(size)])]
    pallas_call x3, Pallas kernels: 18.4 us -> 17.3 us  [gate_up_stream(): pl.pallas_call(functools.partial(stream_kernel, width), out_shape=jax.Sha...]
    pallas_call x2 -> x4, Pallas kernels: 6.09 us -> 5.74 us  [down(): pl.pallas_call(functools.partial(down_kernel, before is None, slots is no...]
  transfers between devices with their start and end apart: 12 -> 9, of which waited for: 6 -> 2; matrix products, arithmetic and copies ran while one was open for 0% -> 0% of each run, Pallas kernels for 44% -> 35%
where the time goes in v4:
time: 74.8 us; the launch traced here: 74.6 us
  Pallas kernels  30.5 us (41%)
  local copies, waits for them, and re-layouts  17.5 us (23%)
  starting transfers between devices  13.8 us (18%)
  blocking collectives  8.77 us (12%)
  waiting for transfers between devices  2.95 us (4%)
  other arithmetic  0.93 us (1%)
    unnamed x6, local copies, waits for them, and re-layouts  17.5 us
    pallas_call x3, Pallas kernels, gate_up_stream(): pl.pallas_call(functools.partial(stream_kernel, width), out_shape=jax.Sha...  17.3 us
    ppermute x9, starting transfers between devices, swap(): return lax.ppermute(value, axes, [(i, i ^ distance) for i in range(size)])  13.8 us
    all_to_all x1, blocking collectives, direct(): terms = lax.all_to_all(terms, TOKEN_AXES, 0, 0, tiled=True)  8.77 us
    pallas_call x4, Pallas kernels, down(): pl.pallas_call(functools.partial(down_kernel, before is None, slots is no...  5.74 us
    pallas_call x1, Pallas kernels, fetch(): pl.pallas_call(functools.partial(fetch_kernel, width), out_shape=pltpu.VM...  5.23 us
    ppermute x9, waiting for transfers between devices, swap(): return lax.ppermute(value, axes, [(i, i ^ distance) for i in range(size)])  2.95 us
    pallas_call x1, Pallas kernels, gate_up_held(): pl.pallas_call(held_kernel, out_shape=jax.ShapeDtypeStruct((8, packed_pai...  2.18 us
  transfers between devices with their start and end apart: 9, of which 2 were waited for; matrix products, arithmetic and copies ran while one was open for 0% of the time, Pallas kernels for 35%

profile of v4, /device:TPU:0, one launch (start us, length us, event | category | flops | bytes accessed | tf_op | source)
XLA Modules:
  0.0 74.6 jit_solution(2273274810724606717)
XLA Ops:
  0.0 0.5 collective-permute-start
  0.5 2.5 %collective-permute-start.1 = (bf16[9,2048]{1,0:T(8,128)(2,1)}, bf16[9,2048]{1,0:T(8,128)(2,1)S(1)}, u32[]{:S(2)}, u32[]{:S(2)}) collective-permute-start(bf16[9,2048]{1,0:T(8,128)(2,1)} %param.4), channel_id=1, source_target_pairs={{0,2},{1,3},{2,0},{3,1},{4,6},{5,7},{6,4},{7,5},{8,10},{9,11},{10,... | collective-permute-start | bytes 110600 | tf_op jit(solution)/shard_map/ppermute | solution.py:233
  2.9 0.1 collective-permute-start.2
  3.1 0.0 copy-start.2
  3.1 5.2 %shard_map.46.held = bf16[2,2048,1664]{2,1,0:T(8,128)(2,1)S(1)} custom-call(s32[1]{0:T(128)} %bitcast.start_ref.start, bf16[2048,6656]{1,0:T(8,128)(2,1)} %gate_ref.7, bf16[2048,6656]{1,0:T(8,128)(2,1)} %up_ref.7), custom_call_target="tpu_custom_call" | custom-call | bytes 1048576 | tf_op jit(solution)/shard_map/pallas_call | solution.py:78
  8.3 0.0 collective-permute-done
  8.3 0.0 collective-permute-done.1
  8.3 0.0 collective-permute-done.2
  8.4 0.0 copy-done.2
  8.4 0.1 pad_maximum_fusion.x_ref
  8.5 2.2 %shard_map.47._ = bf16[8,14976]{1,0:T(8,128)(2,1)S(1)} custom-call(bf16[36,2048]{1,0:T(8,128)(2,1)S(1)} %pad_maximum_fusion.x_ref, bf16[2,2048,1664]{2,1,0:T(8,128)(2,1)S(1)} %shard_map.46.held), custom_call_target="tpu_custom_call" | custom-call | bytes 1048576 | tf_op jit(solution)/shard_map/pallas_call | solution.py:110
  10.6 1.7 %collective-permute-start.3 = (bf16[8,14976]{1,0:T(8,128)(2,1)S(1)}, bf16[8,14976]{1,0:T(8,128)(2,1)S(1)}, u32[]{:S(2)}, u32[]{:S(2)}) collective-permute-start(bf16[8,14976]{1,0:T(8,128)(2,1)S(1)} %shard_map.47._), channel_id=1, source_target_pairs={{0,4},{4,0},{8,12},{12,8},{1,5},{5,1},{9,13},{13,9},{2,6},{6,2},{1... | collective-permute-start | bytes 718856 | tf_op jit(solution)/shard_map/ppermute | solution.py:233
  12.4 5.8 %shard_map.48 = bf16[8,14976]{1,0:T(8,128)(2,1)S(1)} custom-call(s32[1]{0:T(128)} %bitcast.7.start_ref.start, bf16[36,2048]{1,0:T(8,128)(2,1)S(1)} %pad_maximum_fusion.x_ref, bf16[2048,6656]{1,0:T(8,128)(2,1)} %gate_ref.7, bf16[2048,6656]{1,0:T(8,128)(2,1)} %up_ref.7, bf16[8,14976]{1,0:T(8,128)(2,1)S(1)} %shard_map.47._), custom_call_target="tpu_custom_call" | custom-call | bytes 1048576 | tf_op jit(solution)/shard_map/pallas_call | solution.py:129
  18.1 0.5 collective-permute-done.3
  18.6 0.1 add_convert_fusion._
  18.7 2.8 %collective-permute-start.4 = (bf16[8,14976]{1,0:T(8,128)(2,1)S(1)}, bf16[8,14976]{1,0:T(8,128)(2,1)S(1)}, u32[]{:S(2)}, u32[]{:S(2)}) collective-permute-start(bf16[8,14976]{1,0:T(8,128)(2,1)S(1)} %add_convert_fusion._), channel_id=1, source_target_pairs={{0,8},{4,12},{8,0},{12,4},{1,9},{5,13},{9,1},{13,5},{2,10},{6,14},... | collective-permute-start | bytes 718856 | tf_op jit(solution)/shard_map/ppermute | solution.py:233
  21.5 5.8 %shard_map.49._ = bf16[8,14976]{1,0:T(8,128)(2,1)S(1)} custom-call(s32[1]{0:T(128)} %bitcast.6.start_ref.start, bf16[36,2048]{1,0:T(8,128)(2,1)S(1)} %pad_maximum_fusion.x_ref, bf16[2048,6656]{1,0:T(8,128)(2,1)} %gate_ref.7, bf16[2048,6656]{1,0:T(8,128)(2,1)} %up_ref.7, bf16[8,14976]{1,0:T(8,128)(2,1)S(1)} %add_convert_fusion._), custom_call_target="tpu_custom_call" | custom-call | bytes 1048576 | tf_op jit(solution)/shard_map/pallas_call | solution.py:129
  27.3 1.7 %collective-permute-start.5 = (bf16[8,14976]{1,0:T(8,128)(2,1)S(1)}, bf16[8,14976]{1,0:T(8,128)(2,1)S(1)}, u32[]{:S(2)}, u32[]{:S(2)}) collective-permute-start(bf16[8,14976]{1,0:T(8,128)(2,1)S(1)} %shard_map.49._), channel_id=1, source_target_pairs={{0,4},{4,0},{8,12},{12,8},{1,5},{5,1},{9,13},{13,9},{2,6},{6,2},{1... | collective-permute-start | bytes 718856 | tf_op jit(solution)/shard_map/ppermute | solution.py:233
  29.0 5.8 %shard_map.50 = bf16[8,14976]{1,0:T(8,128)(2,1)S(1)} custom-call(s32[1]{0:T(128)} %bitcast.5.start_ref.start, bf16[36,2048]{1,0:T(8,128)(2,1)S(1)} %pad_maximum_fusion.x_ref, bf16[2048,6656]{1,0:T(8,128)(2,1)} %gate_ref.7, bf16[2048,6656]{1,0:T(8,128)(2,1)} %up_ref.7, bf16[8,14976]{1,0:T(8,128)(2,1)S(1)} %shard_map.49._), custom_call_target="tpu_custom_call" | custom-call | bytes 1048576 | tf_op jit(solution)/shard_map/pallas_call | solution.py:129
  34.8 0.0 collective-permute-done.4
  34.8 0.1 convert_add_fusion.summed
  34.8 2.4 %collective-permute-done.5.near = bf16[8,14976]{1,0:T(8,128)(2,1)S(1)} collective-permute-done((bf16[8,14976]{1,0:T(8,128)(2,1)S(1)}, bf16[8,14976]{1,0:T(8,128)(2,1)S(1)}, u32[]{:S(2)}, u32[]{:S(2)}) %collective-permute-start.5) | collective-permute-done | bytes 239648 | tf_op jit(solution)/shard_map/ppermute | solution.py:233
  37.3 0.1 shard_map.51.refs_0_
  37.3 0.1 collective-permute-start.8
  37.4 4.0 %collective-permute-start.7 = (bf16[8,7552]{1,0:T(8,128)(2,1)S(1)}, bf16[8,7552]{1,0:T(8,128)(2,1)S(1)}, u32[]{:S(2)}, u32[]{:S(2)}) collective-permute-start(bf16[8,7552]{1,0:T(8,128)(2,1)S(1)} %shard_map.51.refs_0_), channel_id=1, source_target_pairs={{0,8},{4,12},{8,0},{12,4},{1,9},{5,13},{9,1},{13,5},{2,10},{6,14},... | collective-permute-start | bytes 362504 | tf_op jit(solution)/shard_map/ppermute | solution.py:233
  41.4 0.4 collective-permute-start.6
  41.8 0.1 pad_add_fusion.refs_0_
  41.9 0.0 copy-start
  41.9 8.8 %copy-done = bf16[6656,2048]{1,0:T(8,128)(2,1)S(1)} copy-done((bf16[6656,2048]{1,0:T(8,128)(2,1)S(1)}, bf16[6656,2048]{1,0:T(8,128)(2,1)}, u32[]{:S(2)}) %copy-start) | copy-done | bytes 27263000
  50.6 1.3 %shard_map.52.refs_1_ = f32[36,2048]{1,0:T(8,128)S(1)} custom-call(s32[1]{0:T(128)} %bitcast.5.start_ref.start, bf16[8,7552]{1,0:T(8,128)(2,1)S(1)} %shard_map.51.refs_0_, bf16[6656,2048]{1,0:T(8,128)(2,1)S(1)} %copy-done), custom_call_target="tpu_custom_call" | custom-call | bytes 1048576 | tf_op jit(solution)/shard_map/pallas_call | solution.py:218
  51.9 0.0 collective-permute-done.8.refs_0_
  51.9 0.0 copy-start.1
  51.9 8.7 %copy-done.1 = bf16[6656,2048]{1,0:T(8,128)(2,1)S(1)} copy-done((bf16[6656,2048]{1,0:T(8,128)(2,1)S(1)}, bf16[6656,2048]{1,0:T(8,128)(2,1)}, u32[]{:S(2)}) %copy-start.1) | copy-done | bytes 27263000
  60.7 1.3 %shard_map.53.refs_1_ = f32[36,2048]{1,0:T(8,128)S(1)} custom-call(s32[1]{0:T(128)} %bitcast.6.start_ref.start, bf16[8,7552]{1,0:T(8,128)(2,1)S(1)} %collective-permute-done.8.refs_0_, f32[36,2048]{1,0:T(8,128)S(1)} %shard_map.52.refs_1_, bf16[6656,2048]{1,0:T(8,128)(2,1)S(1)} %copy-done.1), custom_call_target="tpu_custom_call" | custom-call | bytes 1048576 | tf_op jit(solution)/shard_map/pallas_call | solution.py:218
  62.0 0.0 collective-permute-done.7.refs_0_
  62.0 1.3 %shard_map.54.refs_2_ = f32[36,2048]{1,0:T(8,128)S(1)} custom-call(s32[1]{0:T(128)} %bitcast.7.start_ref.start, bf16[8,7552]{1,0:T(8,128)(2,1)S(1)} %collective-permute-done.7.refs_0_, f32[36,2048]{1,0:T(8,128)S(1)} %shard_map.53.refs_1_, bf16[6656,2048]{1,0:T(8,128)(2,1)S(1)} %copy-done.1), custom_call_target="tpu_custom_call" | custom-call | bytes 1048576 | tf_op jit(solution)/shard_map/pallas_call | solution.py:218
  63.3 0.0 collective-permute-done.6.refs_1_
  63.3 1.9 %shard_map.55 = bf16[4,9,2048]{2,1,0:T(8,128)(2,1)S(1)} custom-call(s32[1]{0:T(128)} %bitcast.start_ref.start, s32[4]{0:T(128)S(1)} %pad_add_fusion.refs_0_, bf16[8,7552]{1,0:T(8,128)(2,1)S(1)} %collective-permute-done.6.refs_1_, f32[36,2048]{1,0:T(8,128)S(1)} %shard_map.54.refs_2_, bf16[6656,2048]{1,0:T(8,128)(2,1)S(1)} %copy-done.1), custom_call_target="tpu_custom_call" | custom-call | bytes 1048576 | tf_op jit(solution)/shard_map/pallas_call | solution.py:218
  65.2 8.8 %all_to_all.5 = bf16[4,9,2048]{2,1,0:T(8,128)(2,1)S(1)} all-to-all(bf16[4,9,2048]{2,1,0:T(8,128)(2,1)S(1)} %shard_map.55), channel_id=1, replica_groups=mesh['grp'=2,'gx'=4,'gy'=2,'gz'=2] {'gy','gz'}, dimensions={0} | all-to-all | bytes 294912 | tf_op jit(solution)/shard_map/all_to_all | solution.py:277
  74.0 0.7 fusion
Async XLA Ops:
  0.0 8.3 %collective-permute-start = (bf16[9,2048]{1,0:T(8,128)(2,1)}, bf16[9,2048]{1,0:T(8,128)(2,1)S(1)}, u32[]{:S(2)}, u32[]{:S(2)}) collective-permute-start(bf16[9,2048]{1,0:T(8,128)(2,1)} %param.4), channel_id=1, source_target_pairs={{0,1},{1,0},{2,3},{3,2},{4,5},{5,4},{6,7},{7,6},{8,9},{9,8},{10,11... | collective-permute-start | bytes 110600 | tf_op jit(solution)/shard_map/ppermute | solution.py:233
  0.5 7.9 %collective-permute-start.1 = (bf16[9,2048]{1,0:T(8,128)(2,1)}, bf16[9,2048]{1,0:T(8,128)(2,1)S(1)}, u32[]{:S(2)}, u32[]{:S(2)}) collective-permute-start(bf16[9,2048]{1,0:T(8,128)(2,1)} %param.4), channel_id=1, source_target_pairs={{0,2},{1,3},{2,0},{3,1},{4,6},{5,7},{6,4},{7,5},{8,10},{9,11},{10,... | collective-permute-start | bytes 110600 | tf_op jit(solution)/shard_map/ppermute | solution.py:233
  2.9 5.4 %collective-permute-start.2 = (bf16[9,2048]{1,0:T(8,128)(2,1)}, bf16[9,2048]{1,0:T(8,128)(2,1)S(1)}, u32[]{:S(2)}, u32[]{:S(2)}) collective-permute-start(bf16[9,2048]{1,0:T(8,128)(2,1)} %param.4), channel_id=1, source_target_pairs={{0,3},{1,2},{2,1},{3,0},{4,7},{5,6},{6,5},{7,4},{8,11},{9,10},{10,... | collective-permute-start | bytes 110600 | tf_op jit(solution)/shard_map/ppermute | solution.py:233
  3.1 5.3 %copy-start.2 = (bf16[9,2048]{1,0:T(8,128)(2,1)S(1)}, bf16[9,2048]{1,0:T(8,128)(2,1)}, u32[]{:S(2)}) copy-start(bf16[9,2048]{1,0:T(8,128)(2,1)} %param.4) | copy-start | bytes 110596
  10.6 8.0 %collective-permute-start.3 = (bf16[8,14976]{1,0:T(8,128)(2,1)S(1)}, bf16[8,14976]{1,0:T(8,128)(2,1)S(1)}, u32[]{:S(2)}, u32[]{:S(2)}) collective-permute-start(bf16[8,14976]{1,0:T(8,128)(2,1)S(1)} %shard_map.47._), channel_id=1, source_target_pairs={{0,4},{4,0},{8,12},{12,8},{1,5},{5,1},{9,13},{13,9},{2,6},{6,2},{1... | collective-permute-start | bytes 718856 | tf_op jit(solution)/shard_map/ppermute | solution.py:233
  18.7 16.1 %collective-permute-start.4 = (bf16[8,14976]{1,0:T(8,128)(2,1)S(1)}, bf16[8,14976]{1,0:T(8,128)(2,1)S(1)}, u32[]{:S(2)}, u32[]{:S(2)}) collective-permute-start(bf16[8,14976]{1,0:T(8,128)(2,1)S(1)} %add_convert_fusion._), channel_id=1, source_target_pairs={{0,8},{4,12},{8,0},{12,4},{1,9},{5,13},{9,1},{13,5},{2,10},{6,14},... | collective-permute-start | bytes 718856 | tf_op jit(solution)/shard_map/ppermute | solution.py:233
  27.3 10.0 %collective-permute-start.5 = (bf16[8,14976]{1,0:T(8,128)(2,1)S(1)}, bf16[8,14976]{1,0:T(8,128)(2,1)S(1)}, u32[]{:S(2)}, u32[]{:S(2)}) collective-permute-start(bf16[8,14976]{1,0:T(8,128)(2,1)S(1)} %shard_map.49._), channel_id=1, source_target_pairs={{0,4},{4,0},{8,12},{12,8},{1,5},{5,1},{9,13},{13,9},{2,6},{6,2},{1... | collective-permute-start | bytes 718856 | tf_op jit(solution)/shard_map/ppermute | solution.py:233
  37.3 14.6 %collective-permute-start.8 = (bf16[8,7552]{1,0:T(8,128)(2,1)S(1)}, bf16[8,7552]{1,0:T(8,128)(2,1)S(1)}, u32[]{:S(2)}, u32[]{:S(2)}) collective-permute-start(bf16[8,7552]{1,0:T(8,128)(2,1)S(1)} %shard_map.51.refs_0_), channel_id=1, source_target_pairs={{0,4},{4,0},{8,12},{12,8},{1,5},{5,1},{9,13},{13,9},{2,6},{6,2},{1... | collective-permute-start | bytes 362504 | tf_op jit(solution)/shard_map/ppermute | solution.py:233
  37.4 24.6 %collective-permute-start.7 = (bf16[8,7552]{1,0:T(8,128)(2,1)S(1)}, bf16[8,7552]{1,0:T(8,128)(2,1)S(1)}, u32[]{:S(2)}, u32[]{:S(2)}) collective-permute-start(bf16[8,7552]{1,0:T(8,128)(2,1)S(1)} %shard_map.51.refs_0_), channel_id=1, source_target_pairs={{0,8},{4,12},{8,0},{12,4},{1,9},{5,13},{9,1},{13,5},{2,10},{6,14},... | collective-permute-start | bytes 362504 | tf_op jit(solution)/shard_map/ppermute | solution.py:233
  41.4 21.9 %collective-permute-start.6 = (bf16[8,7552]{1,0:T(8,128)(2,1)S(1)}, bf16[8,7552]{1,0:T(8,128)(2,1)S(1)}, u32[]{:S(2)}, u32[]{:S(2)}) collective-permute-start(bf16[8,7552]{1,0:T(8,128)(2,1)S(1)} %shard_map.51.refs_0_), channel_id=1, source_target_pairs={{0,12},{4,8},{8,4},{12,0},{1,13},{5,9},{9,5},{13,1},{2,14},{6,10},... | collective-permute-start | bytes 362504 | tf_op jit(solution)/shard_map/ppermute | solution.py:233
  41.9 8.8 %copy-start = (bf16[6656,2048]{1,0:T(8,128)(2,1)S(1)}, bf16[6656,2048]{1,0:T(8,128)(2,1)}, u32[]{:S(2)}) copy-start(bf16[6656,2048]{1,0:T(8,128)(2,1)} %refs_3_.1) | copy-start | bytes 81788928
  51.9 8.8 %copy-start.1 = (bf16[6656,2048]{1,0:T(8,128)(2,1)S(1)}, bf16[6656,2048]{1,0:T(8,128)(2,1)}, u32[]{:S(2)}) copy-start(bf16[6656,2048]{1,0:T(8,128)(2,1)} %refs_3_.1) | copy-start | bytes 81788928

commit v5 on v3

--- a/solution.py
+++ b/solution.py
@@ -175,12 +175,38 @@
     )(summed, near)
 
 
+def pack_rows(out, value):
+    rows, width = value.shape
+    for g in range(rows // 8):
+        out[:, g * width : (g + 1) * width] = value[8 * g : 8 * g + 8].astype(out.dtype)
+    piece = width // 8
+    for r in range(rows // 8 * 8, rows):
+        at = (rows // 8) * width + (r % 8) * piece
+        row = jnp.concatenate(
+            [value[r : r + 1, i * piece : (i + 1) * piece] for i in range(8)], axis=0
+        )
+        out[:, at : at + piece] = row.astype(out.dtype)
+
+
+def unpack_rows(out, packed):
+    rows, width = out.shape
+    for g in range(rows // 8):
+        out[8 * g : 8 * g + 8, :] = packed[:, g * width : (g + 1) * width]
+    piece = width // 8
+    for r in range(rows // 8 * 8, rows):
+        at = (rows // 8) * width + (r % 8) * piece
+        for i in range(8):
+            out[r : r + 1, i * piece : (i + 1) * piece] = packed[i : i + 1, at : at + piece]
+
+
 def down_kernel(first, rows, width, starts, *refs):
     blocks = starts.shape[0]
     hidden, refs = refs[:blocks], refs[blocks:]
     if not first:
         before, refs = refs[0], refs[1:]
     held, outs, (plain, total) = refs[0], refs[1:-2], refs[-2:]
+    if first:
+        total = outs[0]
     for b in range(blocks):
         for g in range(rows // 8):
             plain[8 * g : 8 * g + 8, :] = hidden[b][:, g * width : (g + 1) * width].astype(jnp.float32)
@@ -199,26 +225,25 @@
                 total[...] = term if first else before[...] + term
             else:
                 total[...] += term
-    if len(outs) == 1:
-        outs[0][...] = total[...]
-    else:
-        tall = outs[0].shape[0]
+    if not first:
+        tall = rows // len(outs)
         for r, out in enumerate(outs):
-            out[...] = total[r * tall : (r + 1) * tall, :].astype(out.dtype)
+            pack_rows(out, total[r * tall : (r + 1) * tall, :])
 
 
 def down(hidden, starts, before, weight, rows, width, outs):
     columns = weight.shape[1]
-    if outs == 1:
+    if before is None:
         shapes = [jax.ShapeDtypeStruct((rows, columns), jnp.float32)]
     else:
-        shapes = [jax.ShapeDtypeStruct((rows // outs, columns), jnp.bfloat16)] * outs
+        packed = (8, rows // outs * columns // 8)
+        shapes = [jax.ShapeDtypeStruct(packed, jnp.bfloat16 if r else jnp.float32) for r in range(outs)]
     carried = [] if before is None else [before]
     return pl.pallas_call(
         functools.partial(down_kernel, before is None, rows, width),
         out_shape=shapes,
         in_specs=[SCALARS] + [WHOLE] * (len(hidden) + len(carried) + 1),
-        out_specs=[WHOLE] * outs,
+        out_specs=[WHOLE] * len(shapes),
         scratch_shapes=[
             pltpu.VMEM((rows, width), jnp.float32),
             pltpu.VMEM((rows, columns), jnp.float32),
@@ -226,6 +251,27 @@
         compiler_params=params(8),
         cost_estimate=SMALL,
     )(starts, *hidden, *carried, in_vmem(weight))
+
+
+def finish_kernel(*refs):
+    terms, out, plain = refs[:-2], refs[-2], refs[-1]
+    packed = terms[0][...]
+    for term in terms[1:]:
+        packed = packed + term[...].astype(jnp.float32)
+    unpack_rows(plain, packed)
+    out[...] = plain[...].astype(out.dtype)
+
+
+def finish(terms, shape):
+    return pl.pallas_call(
+        finish_kernel,
+        out_shape=jax.ShapeDtypeStruct(shape, jnp.bfloat16),
+        in_specs=[WHOLE] * len(terms),
+        out_specs=WHOLE,
+        scratch_shapes=[pltpu.VMEM(shape, jnp.float32)],
+        compiler_params=params(4),
+        cost_estimate=SMALL,
+    )(*terms)
 
 
 def swap(value, axes, size, distance):
@@ -265,14 +311,13 @@
     summed = lax.optimization_barrier(add(own, far))
     hidden = activate_packed(summed, near, rows, width)
 
-    first = [hidden, swap(hidden, "gx", n_gx, 1)]
-    second = [swap(hidden, "gx", n_gx, d) for d in (2, 3)]
-    (partial_sum,) = down(first, starts_of(0, 1), None, down_weight, rows, width, 1)
-    outs = down(second, starts_of(2, 3), partial_sum, down_weight, rows, width, n_token)
-    result = outs[0].astype(jnp.float32)
-    for r in range(1, n_token):
-        result = result + swap(outs[r], TOKEN_AXES, n_token, r).astype(jnp.float32)
-    return result.astype(jnp.bfloat16)
+    opposite = swap(hidden, "gx", n_gx, 2)
+    first = [hidden, swap(hidden, "gx", n_gx, 1), opposite]
+    second = [swap(opposite, "gx", n_gx, 1)]
+    (partial_sum,) = down(first, starts_of(0, 1, 2), None, down_weight, rows, width, 1)
+    outs = down(second, starts_of(3), partial_sum, down_weight, rows, width, n_token)
+    terms = [outs[0]] + [swap(outs[r], TOKEN_AXES, n_token, r) for r in range(1, n_token)]
+    return finish(terms, tokens.shape)
 
 
 def offloaded(tokens, gate_weight, up_weight, down_weight):
@@ -296,7 +341,8 @@
     rows = tokens.shape[0] * n_token
     tokens_fit = n_token > 1 and n_token & (n_token - 1) == 0 and rows % 4 == 0
     weights_fit = gate_weight.shape[1] % (128 * 4) == 0 and gate_weight.shape[0] % STEP == 0
-    if n_gx == 4 and tokens_fit and weights_fit:
+    columns_fit = down_weight.shape[1] % (128 * 8) == 0
+    if n_gx == 4 and tokens_fit and weights_fit and columns_fit:
         return direct(tokens, gate_weight, up_weight, down_weight)
     return offloaded(tokens, gate_weight, up_weight, down_weight)
 

time: 60.5 us -> 58.3 us (0.964)
  waiting for transfers between devices: 11.1 us -> 9.94 us
  other arithmetic: 1.01 us -> 0.26 us
    ppermute x12, waiting for transfers between devices: 11.1 us -> 9.94 us  [swap(): return lax.ppermute(value, axes, [(i, i ^ distance) for i in range(size)])]
    convert_element_type x1 -> x0, other arithmetic: 0.67 us -> none  [direct(): return result.astype(jnp.bfloat16)]
    pallas_call x0 -> x1, Pallas kernels: none -> 0.66 us  [finish(): pl.pallas_call(finish_kernel, out_shape=jax.ShapeDtypeStruct(shape, jnp.b...]
    pallas_call x2, Pallas kernels: 6.09 us -> 5.48 us  [down(): pl.pallas_call(functools.partial(down_kernel, before is None, rows, width...]
  transfers between devices with their start and end apart: 12 -> 12, of which waited for: 6 -> 6; matrix products, arithmetic and copies ran while one was open for 0% -> 0% of each run, Pallas kernels for 44% -> 48%
where the time goes in v5:
time: 58.3 us; the launch traced here: 58.1 us
  Pallas kernels  32 us (55%)
  starting transfers between devices  15.7 us (27%)
  waiting for transfers between devices  9.94 us (17%)
    pallas_call x3, Pallas kernels, gate_up_stream(): pl.pallas_call(functools.partial(stream_kernel, width), out_shape=jax.Sha...  18.4 us
    ppermute x12, starting transfers between devices, swap(): return lax.ppermute(value, axes, [(i, i ^ distance) for i in range(size)])  15.7 us
    ppermute x12, waiting for transfers between devices, swap(): return lax.ppermute(value, axes, [(i, i ^ distance) for i in range(size)])  9.94 us
    pallas_call x2, Pallas kernels, down(): pl.pallas_call(functools.partial(down_kernel, before is None, rows, width...  5.48 us
    pallas_call x1, Pallas kernels, fetch(): pl.pallas_call(functools.partial(fetch_kernel, width), out_shape=pltpu.VM...  5.23 us
    pallas_call x1, Pallas kernels, gate_up_held(): pl.pallas_call(held_kernel, out_shape=jax.ShapeDtypeStruct((8, packed_pai...  2.15 us
  transfers between devices with their start and end apart: 12, of which 6 were waited for; matrix products, arithmetic and copies ran while one was open for 0% of the time, Pallas kernels for 48%

profile of v5, /device:TPU:0, one launch (start us, length us, event | category | flops | bytes accessed | tf_op | source)
XLA Modules:
  0.0 58.1 jit_solution(15156454693660700436)
XLA Ops:
  0.0 0.5 collective-permute-start
  0.5 2.5 %collective-permute-start.1 = (bf16[9,2048]{1,0:T(8,128)(2,1)}, bf16[9,2048]{1,0:T(8,128)(2,1)S(1)}, u32[]{:S(2)}, u32[]{:S(2)}) collective-permute-start(bf16[9,2048]{1,0:T(8,128)(2,1)} %param.4), channel_id=1, source_target_pairs={{0,2},{1,3},{2,0},{3,1},{4,6},{5,7},{6,4},{7,5},{8,10},{9,11},{10,... | collective-permute-start | bytes 110600 | tf_op jit(solution)/shard_map/ppermute | solution.py:278
  2.9 0.1 collective-permute-start.2
  3.1 0.0 copy-start
  3.1 5.2 %shard_map.46.held = bf16[2,2048,1664]{2,1,0:T(8,128)(2,1)S(1)} custom-call(s32[1]{0:T(128)} %bitcast.start_ref.starts, bf16[2048,6656]{1,0:T(8,128)(2,1)} %gate_ref.7, bf16[2048,6656]{1,0:T(8,128)(2,1)} %up_ref.7), custom_call_target="tpu_custom_call" | custom-call | bytes 1048576 | tf_op jit(solution)/shard_map/pallas_call | solution.py:78
  8.3 0.0 collective-permute-done
  8.3 0.0 collective-permute-done.1
  8.3 0.0 collective-permute-done.2
  8.4 0.0 copy-done
  8.4 0.1 pad_maximum_fusion.x_ref
  8.5 2.2 %shard_map.47._ = bf16[8,14976]{1,0:T(8,128)(2,1)S(1)} custom-call(bf16[36,2048]{1,0:T(8,128)(2,1)S(1)} %pad_maximum_fusion.x_ref, bf16[2,2048,1664]{2,1,0:T(8,128)(2,1)S(1)} %shard_map.46.held), custom_call_target="tpu_custom_call" | custom-call | bytes 1048576 | tf_op jit(solution)/shard_map/pallas_call | solution.py:110
  10.6 1.7 %collective-permute-start.3 = (bf16[8,14976]{1,0:T(8,128)(2,1)S(1)}, bf16[8,14976]{1,0:T(8,128)(2,1)S(1)}, u32[]{:S(2)}, u32[]{:S(2)}) collective-permute-start(bf16[8,14976]{1,0:T(8,128)(2,1)S(1)} %shard_map.47._), channel_id=1, source_target_pairs={{0,4},{4,0},{8,12},{12,8},{1,5},{5,1},{9,13},{13,9},{2,6},{6,2},{1... | collective-permute-start | bytes 718856 | tf_op jit(solution)/shard_map/ppermute | solution.py:278
  12.3 5.8 %shard_map.48 = bf16[8,14976]{1,0:T(8,128)(2,1)S(1)} custom-call(s32[1]{0:T(128)} %bitcast.3.start_ref, bf16[36,2048]{1,0:T(8,128)(2,1)S(1)} %pad_maximum_fusion.x_ref, bf16[2048,6656]{1,0:T(8,128)(2,1)} %gate_ref.7, bf16[2048,6656]{1,0:T(8,128)(2,1)} %up_ref.7, bf16[8,14976]{1,0:T(8,128)(2,1)S(1)} %shard_map.47._), custom_call_target="tpu_custom_call" | custom-call | bytes 1048576 | tf_op jit(solution)/shard_map/pallas_call | solution.py:129
  18.1 0.5 collective-permute-done.3
  18.6 0.1 add_convert_fusion._
  18.7 2.8 %collective-permute-start.4 = (bf16[8,14976]{1,0:T(8,128)(2,1)S(1)}, bf16[8,14976]{1,0:T(8,128)(2,1)S(1)}, u32[]{:S(2)}, u32[]{:S(2)}) collective-permute-start(bf16[8,14976]{1,0:T(8,128)(2,1)S(1)} %add_convert_fusion._), channel_id=1, source_target_pairs={{0,8},{4,12},{8,0},{12,4},{1,9},{5,13},{9,1},{13,5},{2,10},{6,14},... | collective-permute-start | bytes 718856 | tf_op jit(solution)/shard_map/ppermute | solution.py:278
  21.5 0.0 slice-start
  21.5 0.0 slice-start.1
  21.5 0.0 slice-start.2
  21.5 0.0 slice-start.3
  21.5 6.0 %shard_map.49._ = bf16[8,14976]{1,0:T(8,128)(2,1)S(1)} custom-call(s32[1]{0:T(128)} %bitcast.2.start_ref, bf16[36,2048]{1,0:T(8,128)(2,1)S(1)} %pad_maximum_fusion.x_ref, bf16[2048,6656]{1,0:T(8,128)(2,1)} %gate_ref.7, bf16[2048,6656]{1,0:T(8,128)(2,1)} %up_ref.7, bf16[8,14976]{1,0:T(8,128)(2,1)S(1)} %add_convert_fusion._), custom_call_target="tpu_custom_call" | custom-call | bytes 1048576 | tf_op jit(solution)/shard_map/pallas_call | solution.py:129
  27.5 1.7 %collective-permute-start.5 = (bf16[8,14976]{1,0:T(8,128)(2,1)S(1)}, bf16[8,14976]{1,0:T(8,128)(2,1)S(1)}, u32[]{:S(2)}, u32[]{:S(2)}) collective-permute-start(bf16[8,14976]{1,0:T(8,128)(2,1)S(1)} %shard_map.49._), channel_id=1, source_target_pairs={{0,4},{4,0},{8,12},{12,8},{1,5},{5,1},{9,13},{13,9},{2,6},{6,2},{1... | collective-permute-start | bytes 718856 | tf_op jit(solution)/shard_map/ppermute | solution.py:278
  29.2 0.0 slice-start.4
  29.2 0.0 slice-start.5
  29.2 0.0 slice-start.6
  29.2 6.6 %shard_map.50 = bf16[8,14976]{1,0:T(8,128)(2,1)S(1)} custom-call(s32[1]{0:T(128)} %bitcast.1.start_ref, bf16[36,2048]{1,0:T(8,128)(2,1)S(1)} %pad_maximum_fusion.x_ref, bf16[2048,6656]{1,0:T(8,128)(2,1)} %gate_ref.7, bf16[2048,6656]{1,0:T(8,128)(2,1)} %up_ref.7, bf16[8,14976]{1,0:T(8,128)(2,1)S(1)} %shard_map.49._), custom_call_target="tpu_custom_call" | custom-call | bytes 1048576 | tf_op jit(solution)/shard_map/pallas_call | solution.py:129
  35.8 0.0 collective-permute-done.4
  35.8 0.1 convert_add_fusion.summed
  35.9 1.3 %collective-permute-done.5.near = bf16[8,14976]{1,0:T(8,128)(2,1)S(1)} collective-permute-done((bf16[8,14976]{1,0:T(8,128)(2,1)S(1)}, bf16[8,14976]{1,0:T(8,128)(2,1)S(1)}, u32[]{:S(2)}, u32[]{:S(2)}) %collective-permute-start.5) | collective-permute-done | bytes 239648 | tf_op jit(solution)/shard_map/ppermute | solution.py:278
  37.2 0.1 shard_map.51.refs_0_
  37.3 1.7 %collective-permute-start.6 = (bf16[8,7552]{1,0:T(8,128)(2,1)S(1)}, bf16[8,7552]{1,0:T(8,128)(2,1)S(1)}, u32[]{:S(2)}, u32[]{:S(2)}) collective-permute-start(bf16[8,7552]{1,0:T(8,128)(2,1)S(1)} %shard_map.51.refs_0_), channel_id=1, source_target_pairs={{0,8},{4,12},{8,0},{12,4},{1,9},{5,13},{9,1},{13,5},{2,10},{6,14},... | collective-permute-start | bytes 362504 | tf_op jit(solution)/shard_map/ppermute | solution.py:278
  39.0 2.5 %collective-permute-start.8 = (bf16[8,7552]{1,0:T(8,128)(2,1)S(1)}, bf16[8,7552]{1,0:T(8,128)(2,1)S(1)}, u32[]{:S(2)}, u32[]{:S(2)}) collective-permute-start(bf16[8,7552]{1,0:T(8,128)(2,1)S(1)} %shard_map.51.refs_0_), channel_id=1, source_target_pairs={{0,4},{4,0},{8,12},{12,8},{1,5},{5,1},{9,13},{13,9},{2,6},{6,2},{1... | collective-permute-start | bytes 362504 | tf_op jit(solution)/shard_map/ppermute | solution.py:278
  41.5 4.7 %collective-permute-done.6.refs_2_ = bf16[8,7552]{1,0:T(8,128)(2,1)S(1)} collective-permute-done((bf16[8,7552]{1,0:T(8,128)(2,1)S(1)}, bf16[8,7552]{1,0:T(8,128)(2,1)S(1)}, u32[]{:S(2)}, u32[]{:S(2)}) %collective-permute-start.6) | collective-permute-done | bytes 120864 | tf_op jit(solution)/shard_map/ppermute | solution.py:278
  46.2 0.0 collective-permute-start.7
  46.2 0.1 pad_add_fusion.starts
  46.3 0.0 collective-permute-done.8.refs_1_
  46.3 0.0 slice-done
  46.3 0.0 slice-done.1
  46.3 0.0 slice-done.2
  46.3 0.0 slice-done.3
  46.3 0.0 slice-done.4
  46.3 0.0 slice-done.5
  46.3 0.0 slice-done.6
  46.3 4.2 %shard_map.52.refs_1_ = f32[36,2048]{1,0:T(8,128)S(1)} custom-call(s32[3]{0:T(128)S(1)} %pad_add_fusion.starts, bf16[8,7552]{1,0:T(8,128)(2,1)S(1)} %shard_map.51.refs_0_, bf16[8,7552]{1,0:T(8,128)(2,1)S(1)} %collective-permute-done.8.refs_1_, bf16[8,7552]{1,0:T(8,128)(2,1)S(1)} %collective-permute-done.6.refs_2_, bf16[6656,2048]{1,0:T(8,128)(2,1)S(1)} %bitcast.5), custom_call_target="tpu_custom_call" | custom-call | bytes 1048576 | tf_op jit(solution)/shard_map/pallas_call | solution.py:242
  50.5 0.5 collective-permute-done.7.refs_0_
  51.0 1.3 %shard_map.53 = (f32[8,2304]{1,0:T(8,128)S(1)}, bf16[8,2304]{1,0:T(8,128)(2,1)S(1)}, bf16[8,2304]{1,0:T(8,128)(2,1)S(1)}, bf16[8,2304]{1,0:T(8,128)(2,1)S(1)}) custom-call(s32[1]{0:T(128)} %bitcast.start_ref.starts, bf16[8,7552]{1,0:T(8,128)(2,1)S(1)} %collective-permute-done.7.refs_0_, f32[36,2048]{1,0:T(8,128)S(1)} %shard_map.52.refs_1_, ...), custom_call_target="tpu_custom_call" | custom-call | bytes 1048576 | tf_op jit(solution)/shard_map/pallas_call | solution.py:242
  52.4 1.7 %collective-permute-start.10 = (bf16[8,2304]{1,0:T(8,128)(2,1)S(1)}, bf16[8,2304]{1,0:T(8,128)(2,1)S(1)}, u32[]{:S(2)}, u32[]{:S(2)}) collective-permute-start(bf16[8,2304]{1,0:T(8,128)(2,1)S(1)} %get-tuple-element.11), channel_id=1, source_target_pairs={{0,2},{1,3},{2,0},{3,1},{4,6},{5,7},{6,4},{7,5},{8,10},{9,11},{10,... | collective-permute-start | bytes 110600 | tf_op jit(solution)/shard_map/ppermute | solution.py:278
  54.1 0.0 collective-permute-start.11
  54.1 0.5 collective-permute-start.9
  54.6 1.8 %collective-permute-done.10.refs_2_ = bf16[8,2304]{1,0:T(8,128)(2,1)S(1)} collective-permute-done((bf16[8,2304]{1,0:T(8,128)(2,1)S(1)}, bf16[8,2304]{1,0:T(8,128)(2,1)S(1)}, u32[]{:S(2)}, u32[]{:S(2)}) %collective-permute-start.10) | collective-permute-done | bytes 36896 | tf_op jit(solution)/shard_map/ppermute | solution.py:278
  56.4 1.1 %collective-permute-done.11.refs_3_ = bf16[8,2304]{1,0:T(8,128)(2,1)S(1)} collective-permute-done((bf16[8,2304]{1,0:T(8,128)(2,1)S(1)}, bf16[8,2304]{1,0:T(8,128)(2,1)S(1)}, u32[]{:S(2)}, u32[]{:S(2)}) %collective-permute-start.11) | collective-permute-done | bytes 36896 | tf_op jit(solution)/shard_map/ppermute | solution.py:278
  57.5 0.0 collective-permute-done.9.refs_1_
  57.5 0.7 %shard_map.54 = bf16[9,2048]{1,0:T(8,128)(2,1)} custom-call(f32[8,2304]{1,0:T(8,128)S(1)} %get-tuple-element.9.refs_0_, bf16[8,2304]{1,0:T(8,128)(2,1)S(1)} %collective-permute-done.9.refs_1_, bf16[8,2304]{1,0:T(8,128)(2,1)S(1)} %collective-permute-done.10.refs_2_, bf16[8,2304]{1,0:T(8,128)(2,1)S(1)} %collective-permute-done.11.refs_3_), custom_call_target="tpu_custom_call" | custom-call | bytes 1048576 | tf_op jit(solution)/shard_map/pallas_call | solution.py:266
  (1 shorter events, 0.0 us)
Async XLA Ops:
  0.0 8.3 %collective-permute-start = (bf16[9,2048]{1,0:T(8,128)(2,1)}, bf16[9,2048]{1,0:T(8,128)(2,1)S(1)}, u32[]{:S(2)}, u32[]{:S(2)}) collective-permute-start(bf16[9,2048]{1,0:T(8,128)(2,1)} %param.4), channel_id=1, source_target_pairs={{0,1},{1,0},{2,3},{3,2},{4,5},{5,4},{6,7},{7,6},{8,9},{9,8},{10,11... | collective-permute-start | bytes 110600 | tf_op jit(solution)/shard_map/ppermute | solution.py:278
  0.5 7.9 %collective-permute-start.1 = (bf16[9,2048]{1,0:T(8,128)(2,1)}, bf16[9,2048]{1,0:T(8,128)(2,1)S(1)}, u32[]{:S(2)}, u32[]{:S(2)}) collective-permute-start(bf16[9,2048]{1,0:T(8,128)(2,1)} %param.4), channel_id=1, source_target_pairs={{0,2},{1,3},{2,0},{3,1},{4,6},{5,7},{6,4},{7,5},{8,10},{9,11},{10,... | collective-permute-start | bytes 110600 | tf_op jit(solution)/shard_map/ppermute | solution.py:278
  2.9 5.4 %collective-permute-start.2 = (bf16[9,2048]{1,0:T(8,128)(2,1)}, bf16[9,2048]{1,0:T(8,128)(2,1)S(1)}, u32[]{:S(2)}, u32[]{:S(2)}) collective-permute-start(bf16[9,2048]{1,0:T(8,128)(2,1)} %param.4), channel_id=1, source_target_pairs={{0,3},{1,2},{2,1},{3,0},{4,7},{5,6},{6,5},{7,4},{8,11},{9,10},{10,... | collective-permute-start | bytes 110600 | tf_op jit(solution)/shard_map/ppermute | solution.py:278
  3.1 5.3 %copy-start = (bf16[9,2048]{1,0:T(8,128)(2,1)S(1)}, bf16[9,2048]{1,0:T(8,128)(2,1)}, u32[]{:S(2)}) copy-start(bf16[9,2048]{1,0:T(8,128)(2,1)} %param.4) | copy-start | bytes 110596
  10.6 8.0 %collective-permute-start.3 = (bf16[8,14976]{1,0:T(8,128)(2,1)S(1)}, bf16[8,14976]{1,0:T(8,128)(2,1)S(1)}, u32[]{:S(2)}, u32[]{:S(2)}) collective-permute-start(bf16[8,14976]{1,0:T(8,128)(2,1)S(1)} %shard_map.47._), channel_id=1, source_target_pairs={{0,4},{4,0},{8,12},{12,8},{1,5},{5,1},{9,13},{13,9},{2,6},{6,2},{1... | collective-permute-start | bytes 718856 | tf_op jit(solution)/shard_map/ppermute | solution.py:278
  18.7 17.2 %collective-permute-start.4 = (bf16[8,14976]{1,0:T(8,128)(2,1)S(1)}, bf16[8,14976]{1,0:T(8,128)(2,1)S(1)}, u32[]{:S(2)}, u32[]{:S(2)}) collective-permute-start(bf16[8,14976]{1,0:T(8,128)(2,1)S(1)} %add_convert_fusion._), channel_id=1, source_target_pairs={{0,8},{4,12},{8,0},{12,4},{1,9},{5,13},{9,1},{13,5},{2,10},{6,14},... | collective-permute-start | bytes 718856 | tf_op jit(solution)/shard_map/ppermute | solution.py:278
  21.5 24.8 %slice-start = ((s8[27262976]{0:T(1024)(128)(4,1)}), s8[4194304]{0:T(1024)(128)(4,1)S(1)}, s32[]{:S(2)}) async-start(s8[27262976]{0:T(1024)(128)(4,1)} %bitcast.4), calls=%async_computation | async-start | bytes 8388608
  21.5 24.8 %slice-start.1 = ((s8[27262976]{0:T(1024)(128)(4,1)}), s8[4194304]{0:T(1024)(128)(4,1)S(1)}, s32[]{:S(2)}) async-start(s8[27262976]{0:T(1024)(128)(4,1)} %bitcast.4), calls=%async_computation.1 | async-start | bytes 8388608
  21.5 24.8 %slice-start.2 = ((s8[27262976]{0:T(1024)(128)(4,1)}), s8[4194304]{0:T(1024)(128)(4,1)S(1)}, s32[]{:S(2)}) async-start(s8[27262976]{0:T(1024)(128)(4,1)} %bitcast.4), calls=%async_computation.2 | async-start | bytes 8388608
  21.5 24.8 %slice-start.3 = ((s8[27262976]{0:T(1024)(128)(4,1)}), s8[4194304]{0:T(1024)(128)(4,1)S(1)}, s32[]{:S(2)}) async-start(s8[27262976]{0:T(1024)(128)(4,1)} %bitcast.4), calls=%async_computation.3 | async-start | bytes 8388608
  27.5 9.7 %collective-permute-start.5 = (bf16[8,14976]{1,0:T(8,128)(2,1)S(1)}, bf16[8,14976]{1,0:T(8,128)(2,1)S(1)}, u32[]{:S(2)}, u32[]{:S(2)}) collective-permute-start(bf16[8,14976]{1,0:T(8,128)(2,1)S(1)} %shard_map.49._), channel_id=1, source_target_pairs={{0,4},{4,0},{8,12},{12,8},{1,5},{5,1},{9,13},{13,9},{2,6},{6,2},{1... | collective-permute-start | bytes 718856 | tf_op jit(solution)/shard_map/ppermute | solution.py:278
  29.2 17.1 %slice-start.4 = ((s8[27262976]{0:T(1024)(128)(4,1)}), s8[4194304]{0:T(1024)(128)(4,1)S(1)}, s32[]{:S(2)}) async-start(s8[27262976]{0:T(1024)(128)(4,1)} %bitcast.4), calls=%async_computation.4 | async-start | bytes 8388608
  29.2 17.1 %slice-start.5 = ((s8[27262976]{0:T(1024)(128)(4,1)}), s8[4194304]{0:T(1024)(128)(4,1)S(1)}, s32[]{:S(2)}) async-start(s8[27262976]{0:T(1024)(128)(4,1)} %bitcast.4), calls=%async_computation.5 | async-start | bytes 8388608
  29.2 17.1 %slice-start.6 = ((s8[27262976]{0:T(1024)(128)(4,1)}), s8[2097152]{0:T(1024)(128)(4,1)S(1)}, s32[]{:S(2)}) async-start(s8[27262976]{0:T(1024)(128)(4,1)} %bitcast.4), calls=%async_computation.6 | async-start | bytes 4194304
  37.3 8.9 %collective-permute-start.6 = (bf16[8,7552]{1,0:T(8,128)(2,1)S(1)}, bf16[8,7552]{1,0:T(8,128)(2,1)S(1)}, u32[]{:S(2)}, u32[]{:S(2)}) collective-permute-start(bf16[8,7552]{1,0:T(8,128)(2,1)S(1)} %shard_map.51.refs_0_), channel_id=1, source_target_pairs={{0,8},{4,12},{8,0},{12,4},{1,9},{5,13},{9,1},{13,5},{2,10},{6,14},... | collective-permute-start | bytes 362504 | tf_op jit(solution)/shard_map/ppermute | solution.py:278
  39.0 7.3 %collective-permute-start.8 = (bf16[8,7552]{1,0:T(8,128)(2,1)S(1)}, bf16[8,7552]{1,0:T(8,128)(2,1)S(1)}, u32[]{:S(2)}, u32[]{:S(2)}) collective-permute-start(bf16[8,7552]{1,0:T(8,128)(2,1)S(1)} %shard_map.51.refs_0_), channel_id=1, source_target_pairs={{0,4},{4,0},{8,12},{12,8},{1,5},{5,1},{9,13},{13,9},{2,6},{6,2},{1... | collective-permute-start | bytes 362504 | tf_op jit(solution)/shard_map/ppermute | solution.py:278
  46.2 4.9 %collective-permute-start.7 = (bf16[8,7552]{1,0:T(8,128)(2,1)S(1)}, bf16[8,7552]{1,0:T(8,128)(2,1)S(1)}, u32[]{:S(2)}, u32[]{:S(2)}) collective-permute-start(bf16[8,7552]{1,0:T(8,128)(2,1)S(1)} %collective-permute-done.6.refs_2_), channel_id=1, source_target_pairs={{0,4},{4,0},{8,12},{12,8},{1,5},{5,1},{9,13},{13,9},{2,6},{6,2},{1... | collective-permute-start | bytes 362504 | tf_op jit(solution)/shard_map/ppermute | solution.py:278
  52.4 4.0 %collective-permute-start.10 = (bf16[8,2304]{1,0:T(8,128)(2,1)S(1)}, bf16[8,2304]{1,0:T(8,128)(2,1)S(1)}, u32[]{:S(2)}, u32[]{:S(2)}) collective-permute-start(bf16[8,2304]{1,0:T(8,128)(2,1)S(1)} %get-tuple-element.11), channel_id=1, source_target_pairs={{0,2},{1,3},{2,0},{3,1},{4,6},{5,7},{6,4},{7,5},{8,10},{9,11},{10,... | collective-permute-start | bytes 110600 | tf_op jit(solution)/shard_map/ppermute | solution.py:278
  54.1 3.4 %collective-permute-start.11 = (bf16[8,2304]{1,0:T(8,128)(2,1)S(1)}, bf16[8,2304]{1,0:T(8,128)(2,1)S(1)}, u32[]{:S(2)}, u32[]{:S(2)}) collective-permute-start(bf16[8,2304]{1,0:T(8,128)(2,1)S(1)} %get-tuple-element.12), channel_id=1, source_target_pairs={{0,3},{1,2},{2,1},{3,0},{4,7},{5,6},{6,5},{7,4},{8,11},{9,10},{10,... | collective-permute-start | bytes 110600 | tf_op jit(solution)/shard_map/ppermute | solution.py:278
  54.1 3.4 %collective-permute-start.9 = (bf16[8,2304]{1,0:T(8,128)(2,1)S(1)}, bf16[8,2304]{1,0:T(8,128)(2,1)S(1)}, u32[]{:S(2)}, u32[]{:S(2)}) collective-permute-start(bf16[8,2304]{1,0:T(8,128)(2,1)S(1)} %get-tuple-element.10), channel_id=1, source_target_pairs={{0,1},{1,0},{2,3},{3,2},{4,5},{5,4},{6,7},{7,6},{8,9},{9,8},{10,11... | collective-permute-start | bytes 110600 | tf_op jit(solution)/shard_map/ppermute | solution.py:278

commit v6 on v5

v6 whole, which is shorter than its diff:
```python
import functools

import jax
import jax.numpy as jnp
from jax import lax
from jax.experimental import pallas as pl
from jax.experimental.pallas import tpu as pltpu
from jax.sharding import PartitionSpec as P

MIB = 1 << 20
STEP = 256
TOKEN_AXES = ("gy", "gz")
IN_HBM = pl.BlockSpec(memory_space=pltpu.HBM)
ANY = pl.BlockSpec(memory_space=pl.ANY)
WHOLE = pl.BlockSpec(memory_space=pltpu.VMEM)
SCALARS = pl.BlockSpec(memory_space=pltpu.SMEM)


def activate(gate, up):
    return (jax.nn.silu(gate) * up).astype(jnp.bfloat16)


def pieces_of(total, step):
    return [(start, min(step, total - start)) for start in range(0, total, step)]


def in_hbm(value):
    return pltpu.with_memory_space_constraint(value, pltpu.HBM)


def in_vmem(value):
    return pltpu.with_memory_space_constraint(value, pltpu.VMEM)


SMALL = pl.CostEstimate(flops=0, bytes_accessed=MIB, transcendentals=0)


def params(mib):
    return pltpu.CompilerParams(vmem_limit_bytes=mib * MIB)


def packed_pair_width(rows, width):
    return (rows // 8) * 2 * width + (width if rows % 8 else 0)


def pack_one(out, value, w):
    rows, width = value.shape
    for g in range(rows // 8):
        at = (2 * g + w) * width
        out[:, at : at + width] = value[8 * g : 8 * g + 8].astype(out.dtype)


def pack_last(out, gate, up):
    rows, width = gate.shape
    if rows % 8:
        at = (rows // 8) * 2 * width
        tail = jnp.concatenate([gate[rows - 4 :], up[rows - 4 :]], axis=0)
        out[:, at : at + width] = tail.astype(out.dtype)


def start_copies(width, start, first, weights, held, sems):
    columns = pl.ds(pl.multiple_of(start, 128), width)
    copies = []
    for w, weight in enumerate(weights):
        for k, (row, rows) in enumerate(pieces_of(held.shape[1], STEP)):
            copy = pltpu.make_async_copy(
                weight.at[pl.ds(first + row, rows), columns],
                held.at[w, pl.ds(row, rows)],
                sems.at[w, k],
            )
            copy.start()
            copies.append((w, row, rows, copy))
    return copies


def fetch_kernel(width, start_ref, gate_ref, up_ref, held, sems):
    for _, _, _, copy in start_copies(width, start_ref[0], 0, (gate_ref, up_ref), held, sems):
        copy.wait()


def fetch(weights, start, depth, width):
    return pl.pallas_call(
        functools.partial(fetch_kernel, width),
        out_shape=pltpu.VMEM((2, depth, width), jnp.bfloat16),
        in_specs=[SCALARS, IN_HBM, IN_HBM],
        out_specs=WHOLE,
        scratch_shapes=[pltpu.SemaphoreType.DMA((2, len(pieces_of(depth, STEP))))],
        compiler_params=params(4),
        cost_estimate=SMALL,
    )(start, *[in_hbm(w) for w in weights])


def block_kernel(width, ahead, has_held, has_partial, starts, x_ref, *refs):
    refs = list(refs)
    held = refs.pop(0) if has_held else None
    partial = refs.pop(0) if has_partial else None
    weights = refs[:2]
    refs = refs[3:]
    out = refs.pop(0)
    next_total = refs.pop(0) if ahead else None
    stream, total, sems = refs[:3]
    first = x_ref.shape[1] - stream.shape[1]
    copies = start_copies(width, starts[0], first, weights, stream, sems)
    if ahead:
        next_stream, next_sems = refs[3:]
        next_copies = start_copies(width, starts[1], 0, weights, next_stream, next_sems)

    def product(row, rows, weight):
        return jnp.dot(x_ref[:, row : row + rows], weight, preferred_element_type=jnp.float32)

    for w in range(2):
        if has_held:
            for row, rows in pieces_of(first, STEP):
                term = product(row, rows, held[w, row : row + rows, :])
                total[w] = total[w] + term if row else term
        if has_partial:
            total[w] = partial[w]
    for w, row, rows, copy in copies:
        copy.wait()
        term = product(first + row, rows, stream[w, row : row + rows, :])
        total[w] = total[w] + term if first + row else term
        if row + rows == stream.shape[1]:
            pack_one(out, total[w], w)
    pack_last(out, total[0], total[1])
    if ahead:
        for w, row, rows, copy in next_copies:
            copy.wait()
            term = product(row, rows, next_stream[w, row : row + rows, :])
            next_total[w] = next_total[w] + term if row else term


def gate_up(features, weights, starts, width, after, held=None, partial=None, summed=0, ahead=0):
    rows, depth = features.shape
    below = depth - (held.shape[1] if held is not None else summed)
    out_shape = [jax.ShapeDtypeStruct((8, packed_pair_width(rows, width)), jnp.bfloat16)]
    scratch = [
        pltpu.VMEM((2, below, width), jnp.bfloat16),
        pltpu.VMEM((2, rows, width), jnp.float32),
        pltpu.SemaphoreType.DMA((2, len(pieces_of(below, STEP)))),
    ]
    if ahead:
        out_shape.append(jax.ShapeDtypeStruct((2, rows, width), jnp.float32))
        scratch += [
            pltpu.VMEM((2, ahead, width), jnp.bfloat16),
            pltpu.SemaphoreType.DMA((2, len(pieces_of(ahead, STEP)))),
        ]
    before = [] if held is None else [in_vmem(held)]
    before += [] if partial is None else [partial]
    mib = 4 + -(-(below + ahead) * width * 4 // MIB)
    return pl.pallas_call(
        functools.partial(block_kernel, width, ahead, held is not None, partial is not None),
        out_shape=out_shape,
        in_specs=[SCALARS, WHOLE] + [WHOLE] * len(before) + [IN_HBM, IN_HBM, ANY],
        out_specs=[WHOLE] * len(out_shape),
        scratch_shapes=scratch,
        compiler_params=params(mib),
        cost_estimate=SMALL,
    )(starts, features, *before, *[in_hbm(w) for w in weights], after)


def hidden_tail(rows, width):
    half = pl.cdiv(width // 2, 128) * 128
    return half if rows % 8 else 0


def packed_hidden_shape(rows, width):
    return (8, (rows // 8) * width + hidden_tail(rows, width))


def pack_hidden_last(out, value, rows):
    width = value.shape[1]
    half = hidden_tail(rows, width)
    right = value[:, half:]
    if 2 * half > width:
        right = jnp.concatenate([right, jnp.zeros((4, 2 * half - width), jnp.float32)], axis=1)
    at = (rows // 8) * width
    out[:, at : at + half] = jnp.concatenate([value[:, :half], right], axis=0).astype(out.dtype)


def unpack_hidden(plain, hidden, column, width):
    rows = plain.shape[0]
    for g in range(rows // 8):
        value = hidden[:, g * width : (g + 1) * width].astype(jnp.float32)
        plain[8 * g : 8 * g + 8, column : column + width] = value
    if rows % 8:
        at, half = (rows // 8) * width, hidden_tail(rows, width)
        tail = hidden[:, at : at + half].astype(jnp.float32)
        plain[rows - 4 :, column : column + half] = tail[:4]
        plain[rows - 4 :, column + half : column + width] = tail[4:, : width - half]


def activate_kernel(rows, cuts, summed, near, *outs):
    width = cuts[-1]
    parts = [(0, width)] + list(zip(cuts[:-1], cuts[1:]))

    def pair(at):
        return summed[:, at : at + width] + near[:, at : at + width].astype(jnp.float32)

    for g in range(rows // 8):
        value = activate(pair(2 * g * width), pair((2 * g + 1) * width))
        for out, (left, right) in zip(outs, parts):
            wide = right - left
            out[:, g * wide : (g + 1) * wide] = value[:, left:right]
    if rows % 8:
        last = pair((rows // 8) * 2 * width)
        value = activate(last[:4], last[4:]).astype(jnp.float32)
        for out, (left, right) in zip(outs, parts):
            pack_hidden_last(out, value[:, left:right], rows)


def activate_packed(summed, near, rows, cuts):
    widths = [cuts[-1]] + [right - left for left, right in zip(cuts[:-1], cuts[1:])]
    return pl.pallas_call(
        functools.partial(activate_kernel, rows, cuts),
        out_shape=[jax.ShapeDtypeStruct(packed_hidden_shape(rows, w), jnp.bfloat16) for w in widths],
        in_specs=[WHOLE] * 2,
        out_specs=[WHOLE] * len(widths),
        compiler_params=params(8),
        cost_estimate=SMALL,
    )(summed, near)


def pack_rows(out, value):
    rows, width = value.shape
    for g in range(rows // 8):
        out[:, g * width : (g + 1) * width] = value[8 * g : 8 * g + 8].astype(out.dtype)
    piece = width // 8
    for r in range(rows // 8 * 8, rows):
        at = (rows // 8) * width + (r % 8) * piece
        row = jnp.concatenate(
            [value[r : r + 1, i * piece : (i + 1) * piece] for i in range(8)], axis=0
        )
        out[:, at : at + piece] = row.astype(out.dtype)


def unpack_rows(out, packed):
    rows, width = out.shape
    for g in range(rows // 8):
        out[8 * g : 8 * g + 8, :] = packed[:, g * width : (g + 1) * width]
    piece = width // 8
    for r in range(rows // 8 * 8, rows):
        at = (rows // 8) * width + (r % 8) * piece
        for i in range(8):
            out[r : r + 1, i * piece : (i + 1) * piece] = packed[i : i + 1, at : at + piece]


def down_kernel(layout, first, last, starts, *refs):
    refs = list(refs)
    hidden = [[refs.pop(0) for _ in widths] for widths in layout]
    before = None if first else refs.pop(0)
    held, outs, (plain, total) = refs[0], refs[1:-2], refs[-2:]
    if not last:
        total = outs[0]
    width = plain.shape[1]
    for b, widths in enumerate(layout):
        column = 0
        for part, wide in zip(hidden[b], widths):
            unpack_hidden(plain, part, column, wide)
            column += wide
        for row, tall in pieces_of(width, STEP):
            term = jnp.dot(
                plain[:, row : row + tall].astype(jnp.bfloat16),
                held[pl.ds(pl.multiple_of(starts[b] + row, 128), tall), :],
                preferred_element_type=jnp.float32,
            )
            if b == 0 and row == 0:
                total[...] = term if first else before[...] + term
            else:
                total[...] += term
    if last:
        tall = plain.shape[0] // len(outs)
        for r, out in enumerate(outs):
            pack_rows(out, total[r * tall : (r + 1) * tall, :])


def down(hidden, layout, starts, before, weight, rows, outs):
    columns = weight.shape[1]
    if outs == 1:
        shapes = [jax.ShapeDtypeStruct((rows, columns), jnp.float32)]
    else:
        packed = (8, rows // outs * columns // 8)
        shapes = [jax.ShapeDtypeStruct(packed, jnp.bfloat16 if r else jnp.float32) for r in range(outs)]
    arrays = [part for parts in hidden for part in parts]
    arrays += [] if before is None else [before]
    return pl.pallas_call(
        functools.partial(down_kernel, layout, before is None, outs > 1),
        out_shape=shapes,
        in_specs=[SCALARS] + [WHOLE] * (len(arrays) + 1),
        out_specs=[WHOLE] * len(shapes),
        scratch_shapes=[
            pltpu.VMEM((rows, sum(layout[0])), jnp.float32),
            pltpu.VMEM((rows, columns), jnp.float32),
        ],
        compiler_params=params(8),
        cost_estimate=SMALL,
    )(starts, *arrays, in_vmem(weight))


def finish_kernel(*refs):
    terms, out, plain = refs[:-2], refs[-2], refs[-1]
    packed = terms[0][...]
    for term in terms[1:]:
        packed = packed + term[...].astype(jnp.float32)
    unpack_rows(plain, packed)
    out[...] = plain[...].astype(out.dtype)


def finish(terms, shape):
    return pl.pallas_call(
        finish_kernel,
        out_shape=jax.ShapeDtypeStruct(shape, jnp.bfloat16),
        in_specs=[WHOLE] * len(terms),
        out_specs=WHOLE,
        scratch_shapes=[pltpu.VMEM(shape, jnp.float32)],
        compiler_params=params(4),
        cost_estimate=SMALL,
    )(*terms)


def swap(value, axes, size, distance):
    return lax.ppermute(value, axes, [(i, i ^ distance) for i in range(size)])


def add(a, b):
    return a.astype(jnp.float32) + b.astype(jnp.float32)


def direct(tokens, gate_weight, up_weight, down_weight):
    n_gx = lax.axis_size("gx")
    n_token = lax.axis_size(TOKEN_AXES)
    me = lax.axis_index("gx")
    width = gate_weight.shape[1] // n_gx

    def starts_of(*distances):
        return jnp.stack([(me ^ d) * width for d in distances]).astype(jnp.int32)

    weights = (gate_weight, up_weight)
    early = gate_weight.shape[0] // STEP * 3 // 4 * STEP
    ahead = gate_weight.shape[0] // STEP // 4 * STEP
    held = fetch(weights, starts_of(3), early, width)
    features = jnp.concatenate(
        [tokens] + [swap(tokens, TOKEN_AXES, n_token, r) for r in range(1, n_token)], axis=0
    )
    rows = features.shape[0]

    (relayed,) = gate_up(features, weights, starts_of(3), width, features, held=held)
    arrived = swap(relayed, "gx", n_gx, 1)
    across, partial = gate_up(features, weights, starts_of(2, 1), width, relayed, ahead=ahead)
    across = lax.optimization_barrier(add(across, arrived).astype(jnp.bfloat16))
    far = swap(across, "gx", n_gx, 2)
    (beside,) = gate_up(
        features, weights, starts_of(1), width, across, partial=partial, summed=ahead
    )
    near = swap(beside, "gx", n_gx, 1)
    (own,) = gate_up(features, weights, starts_of(0), width, beside)
    summed = lax.optimization_barrier(add(own, far))

    middle = (width // 128 + 1) // 2 * 128
    whole, halves = (width,), (middle, width - middle)
    hidden, *parts = activate_packed(summed, near, rows, (0, middle, width))
    opposite = [swap(part, "gx", n_gx, 2) for part in parts]
    beside = swap(hidden, "gx", n_gx, 1)
    (total,) = down(
        [[hidden], [beside]], [whole, whole], starts_of(0, 1), None, down_weight, rows, 1
    )
    diagonal = []
    for i, part in enumerate(opposite):
        opposite[i], total = lax.optimization_barrier((part, total))
        diagonal.append(swap(opposite[i], "gx", n_gx, 1))
    (total,) = down([opposite], [halves], starts_of(2), total, down_weight, rows, 1)
    outs = down([diagonal], [halves], starts_of(3), total, down_weight, rows, n_token)
    terms = [outs[0]] + [swap(outs[r], TOKEN_AXES, n_token, r) for r in range(1, n_token)]
    return finish(terms, tokens.shape)


def offloaded(tokens, gate_weight, up_weight, down_weight):
    features = lax.all_gather(tokens, TOKEN_AXES, axis=0, tiled=True)
    hidden_width = gate_weight.shape[1]
    gate_part = jnp.dot(features, gate_weight, preferred_element_type=jnp.float32)
    up_part = jnp.dot(features, up_weight, preferred_element_type=jnp.float32)
    summed = lax.psum(
        jnp.concatenate([gate_part, up_part], axis=1).astype(jnp.bfloat16), "gx"
    ).astype(jnp.float32)
    hidden = activate(summed[:, :hidden_width], summed[:, hidden_width:])
    partial_value = jnp.dot(hidden, down_weight, preferred_element_type=jnp.float32)
    return lax.psum_scatter(
        partial_value.astype(jnp.bfloat16), TOKEN_AXES, scatter_dimension=0, tiled=True
    )


def shards(tokens, gate_weight, up_weight, down_weight):
    n_gx = lax.axis_size("gx")
    n_token = lax.axis_size(TOKEN_AXES)
    rows = tokens.shape[0] * n_token
    tokens_fit = n_token > 1 and n_token & (n_token - 1) == 0 and rows % 4 == 0
    weights_fit = gate_weight.shape[1] % (128 * 4) == 0 and gate_weight.shape[0] % (4 * STEP) == 0
    columns_fit = down_weight.shape[1] % (128 * 8) == 0
    if n_gx == 4 and tokens_fit and weights_fit and columns_fit:
        return direct(tokens, gate_weight, up_weight, down_weight)
    return offloaded(tokens, gate_weight, up_weight, down_weight)


def solution(mesh):
    return jax.shard_map(
        shards,
        mesh=mesh,
        in_specs=(
            P(("grp", "gy", "gz"), "gx"),
            P("gx", ("gy", "gz")),
            P("gx", ("gy", "gz")),
            P(("gy", "gz"), "gx"),
        ),
        out_specs=P(("grp", "gy", "gz"), "gx"),
        check_vma=False,
    )
```

time: 58.3 us -> 60.7 us (1.041)
  waiting for transfers between devices: 9.94 us -> 12.3 us
  starting transfers between devices: 15.7 us -> 15 us
    ppermute x12 -> x14, waiting for transfers between devices: 9.94 us -> 12.3 us  [swap(): return lax.ppermute(value, axes, [(i, i ^ distance) for i in range(size)])]
    pallas_call x7 -> x8, Pallas kernels: 26.1 us -> 27.8 us  [the longest x4 22.1 us: gate_up(): pl.pallas_call(functools.partial(block_kernel, width, ahead, held is not...]
    pallas_call x1, Pallas kernels: 5.23 us -> 4.18 us  [fetch(): pl.pallas_call(functools.partial(fetch_kernel, width), out_shape=pltpu.VM...]
    ppermute x12 -> x14, starting transfers between devices: 15.7 us -> 15 us  [swap(): return lax.ppermute(value, axes, [(i, i ^ distance) for i in range(size)])]
  transfers between devices with their start and end apart: 12 -> 14, of which waited for: 6 -> 5; matrix products, arithmetic and copies ran while one was open for 0% -> 0% of each run, Pallas kernels for 48% -> 46%
where the time goes in v6:
time: 60.7 us; the launch traced here: 60.6 us
  Pallas kernels  32.6 us (54%)
  starting transfers between devices  15 us (25%)
  waiting for transfers between devices  12.3 us (20%)
    pallas_call x4, Pallas kernels, gate_up(): pl.pallas_call(functools.partial(block_kernel, width, ahead, held is not...  22.1 us
    ppermute x14, starting transfers between devices, swap(): return lax.ppermute(value, axes, [(i, i ^ distance) for i in range(size)])  15 us
    ppermute x14, waiting for transfers between devices, swap(): return lax.ppermute(value, axes, [(i, i ^ distance) for i in range(size)])  12.3 us
    pallas_call x3, Pallas kernels, down(): pl.pallas_call(functools.partial(down_kernel, layout, before is None, out...  5.62 us
    pallas_call x1, Pallas kernels, fetch(): pl.pallas_call(functools.partial(fetch_kernel, width), out_shape=pltpu.VM...  4.18 us
  transfers between devices with their start and end apart: 14, of which 5 were waited for; matrix products, arithmetic and copies ran while one was open for 0% of the time, Pallas kernels for 46%

profile of v6, /device:TPU:0, one launch (start us, length us, event | category | flops | bytes accessed | tf_op | source)
XLA Modules:
  0.0 60.6 jit_solution(16874535504458858208)
XLA Ops:
  0.0 0.5 collective-permute-start
  0.5 2.5 %collective-permute-start.1 = (bf16[9,2048]{1,0:T(8,128)(2,1)}, bf16[9,2048]{1,0:T(8,128)(2,1)S(1)}, u32[]{:S(2)}, u32[]{:S(2)}) collective-permute-start(bf16[9,2048]{1,0:T(8,128)(2,1)} %param.4), channel_id=1, source_target_pairs={{0,2},{1,3},{2,0},{3,1},{4,6},{5,7},{6,4},{7,5},{8,10},{9,11},{10,... | collective-permute-start | bytes 110600 | tf_op jit(solution)/shard_map/ppermute | solution.py:321
  2.9 0.1 collective-permute-start.2
  3.1 0.0 copy-start
  3.1 4.2 %shard_map.46.refs_0_ = bf16[2,1536,1664]{2,1,0:T(8,128)(2,1)S(1)} custom-call(s32[1]{0:T(128)} %bitcast.start_ref.starts, bf16[2048,6656]{1,0:T(8,128)(2,1)} %refs_0_.3, bf16[2048,6656]{1,0:T(8,128)(2,1)} %refs_1_.7), custom_call_target="tpu_custom_call" | custom-call | bytes 1048576 | tf_op jit(solution)/shard_map/pallas_call | solution.py:82
  7.3 0.0 collective-permute-done
  7.3 0.0 collective-permute-done.1
  7.3 0.0 collective-permute-done.2
  7.3 0.0 copy-done
  7.3 0.1 pad_maximum_fusion.x_ref.refs_3_
  7.4 2.8 %shard_map.47.refs_2_ = bf16[8,14976]{1,0:T(8,128)(2,1)S(1)} custom-call(s32[1]{0:T(128)} %bitcast.start_ref.starts, bf16[36,2048]{1,0:T(8,128)(2,1)S(1)} %pad_maximum_fusion.x_ref.refs_3_, bf16[2,1536,1664]{2,1,0:T(8,128)(2,1)S(1)} %shard_map.46.refs_0_, bf16[2048,6656]{1,0:T(8,128)(2,1)} %refs_0_.3, bf16[2048,6656]{1,0:T(8,128)(2,1)} %refs_1_.7, ...), custom_call_target="tpu_custom_call" | custom-call | bytes 1048576 | tf_op jit(solution)/shard_map/pallas_call | solution.py:150
  10.2 1.8 %collective-permute-start.3 = (bf16[8,14976]{1,0:T(8,128)(2,1)S(1)}, bf16[8,14976]{1,0:T(8,128)(2,1)S(1)}, u32[]{:S(2)}, u32[]{:S(2)}) collective-permute-start(bf16[8,14976]{1,0:T(8,128)(2,1)S(1)} %shard_map.47.refs_2_), channel_id=1, source_target_pairs={{0,4},{4,0},{8,12},{12,8},{1,5},{5,1},{9,13},{13,9},{2,6},{6,2},{1... | collective-permute-start | bytes 718856 | tf_op jit(solution)/shard_map/ppermute | solution.py:321
  12.0 0.1 pad_add_fusion.starts
  12.1 7.9 %shard_map.48 = (bf16[8,14976]{1,0:T(8,128)(2,1)S(1)}, f32[2,36,1664]{2,1,0:T(8,128)S(1)}) custom-call(s32[2]{0:T(128)S(1)} %pad_add_fusion.starts, bf16[36,2048]{1,0:T(8,128)(2,1)S(1)} %pad_maximum_fusion.x_ref.refs_3_, bf16[2048,6656]{1,0:T(8,128)(2,1)} %refs_0_.3, bf16[2048,6656]{1,0:T(8,128)(2,1)} %refs_1_.7, bf16[8,14976]{1,0:T(8,128)(2,1)S(1)} %shard_map.47.refs_2_), custom_call_target="tpu_custom_call" | custom-call | bytes 1048576 | tf_op jit(solution)/shard_map/pallas_call | solution.py:150
  19.9 0.0 collective-permute-done.3
  19.9 0.1 add_convert_fusion.refs_3_
  20.0 2.6 %collective-permute-start.4 = (bf16[8,14976]{1,0:T(8,128)(2,1)S(1)}, bf16[8,14976]{1,0:T(8,128)(2,1)S(1)}, u32[]{:S(2)}, u32[]{:S(2)}) collective-permute-start(bf16[8,14976]{1,0:T(8,128)(2,1)S(1)} %add_convert_fusion.refs_3_), channel_id=1, source_target_pairs={{0,8},{4,12},{8,0},{12,4},{1,9},{5,13},{9,1},{13,5},{2,10},{6,14},... | collective-permute-start | bytes 718856 | tf_op jit(solution)/shard_map/ppermute | solution.py:321
  22.6 0.0 slice-start
  22.6 0.0 slice-start.1
  22.6 0.0 slice-start.2
  22.6 0.0 slice-start.3
  22.6 4.8 %shard_map.49.refs_2_ = bf16[8,14976]{1,0:T(8,128)(2,1)S(1)} custom-call(s32[1]{0:T(128)} %bitcast.2.starts, bf16[36,2048]{1,0:T(8,128)(2,1)S(1)} %pad_maximum_fusion.x_ref.refs_3_, f32[2,36,1664]{2,1,0:T(8,128)S(1)} %get-tuple-element.18.refs_0_, bf16[2048,6656]{1,0:T(8,128)(2,1)} %refs_0_.3, bf16[2048,6656]{1,0:T(8,128)(2,1)} %refs_1_.7, ...), custom_call_target="tpu_custom_call" | custom-call | bytes 1048576 | tf_op jit(solution)/shard_map/pallas_call | solution.py:150
  27.4 0.5 collective-permute-start.5
  28.0 0.0 slice-start.4
  28.0 0.0 slice-start.5
  28.0 0.0 slice-start.6
  28.0 6.6 %shard_map.50 = bf16[8,14976]{1,0:T(8,128)(2,1)S(1)} custom-call(s32[1]{0:T(128)} %bitcast.1.starts, bf16[36,2048]{1,0:T(8,128)(2,1)S(1)} %pad_maximum_fusion.x_ref.refs_3_, bf16[2048,6656]{1,0:T(8,128)(2,1)} %refs_0_.3, bf16[2048,6656]{1,0:T(8,128)(2,1)} %refs_1_.7, bf16[8,14976]{1,0:T(8,128)(2,1)S(1)} %shard_map.49.refs_2_), custom_call_target="tpu_custom_call" | custom-call | bytes 1048576 | tf_op jit(solution)/shard_map/pallas_call | solution.py:150
  34.6 0.0 collective-permute-done.4
  34.6 0.1 convert_add_fusion.summed
  34.6 4.2 %collective-permute-done.5.near = bf16[8,14976]{1,0:T(8,128)(2,1)S(1)} collective-permute-done((bf16[8,14976]{1,0:T(8,128)(2,1)S(1)}, bf16[8,14976]{1,0:T(8,128)(2,1)S(1)}, u32[]{:S(2)}, u32[]{:S(2)}) %collective-permute-start.5) | collective-permute-done | bytes 239648 | tf_op jit(solution)/shard_map/ppermute | solution.py:321
  38.8 0.1 shard_map.51
  38.9 0.1 collective-permute-start.7
  39.0 0.9 %collective-permute-start.6 = (bf16[8,4096]{1,0:T(8,128)(2,1)S(1)}, bf16[8,4096]{1,0:T(8,128)(2,1)S(1)}, u32[]{:S(2)}, u32[]{:S(2)}) collective-permute-start(bf16[8,4096]{1,0:T(8,128)(2,1)S(1)} %get-tuple-element.20), channel_id=1, source_target_pairs={{0,8},{4,12},{8,0},{12,4},{1,9},{5,13},{9,1},{13,5},{2,10},{6,14},... | collective-permute-start | bytes 196616 | tf_op jit(solution)/shard_map/ppermute | solution.py:321
  39.9 2.1 %collective-permute-start.9 = (bf16[8,3456]{1,0:T(8,128)(2,1)S(1)}, bf16[8,3456]{1,0:T(8,128)(2,1)S(1)}, u32[]{:S(2)}, u32[]{:S(2)}) collective-permute-start(bf16[8,3456]{1,0:T(8,128)(2,1)S(1)} %get-tuple-element.23), channel_id=1, source_target_pairs={{0,8},{4,12},{8,0},{12,4},{1,9},{5,13},{9,1},{13,5},{2,10},{6,14},... | collective-permute-start | bytes 165896 | tf_op jit(solution)/shard_map/ppermute | solution.py:321
  42.0 0.1 pad_add_fusion.1.starts
  42.1 3.3 %collective-permute-done.7.refs_1_ = bf16[8,7552]{1,0:T(8,128)(2,1)S(1)} collective-permute-done((bf16[8,7552]{1,0:T(8,128)(2,1)S(1)}, bf16[8,7552]{1,0:T(8,128)(2,1)S(1)}, u32[]{:S(2)}, u32[]{:S(2)}) %collective-permute-start.7) | collective-permute-done | bytes 120864 | tf_op jit(solution)/shard_map/ppermute | solution.py:321
  45.3 0.0 slice-done
  45.3 0.0 slice-done.1
  45.3 0.0 slice-done.2
  45.3 0.0 slice-done.3
  45.4 0.0 slice-done.4
  45.4 0.0 slice-done.5
  45.4 0.0 slice-done.6
  45.4 3.0 %shard_map.52.refs_2_ = f32[36,2048]{1,0:T(8,128)S(1)} custom-call(s32[2]{0:T(128)S(1)} %pad_add_fusion.1.starts, bf16[8,7552]{1,0:T(8,128)(2,1)S(1)} %get-tuple-element.21.refs_0_, bf16[8,7552]{1,0:T(8,128)(2,1)S(1)} %collective-permute-done.7.refs_1_, bf16[6656,2048]{1,0:T(8,128)(2,1)S(1)} %bitcast.5), custom_call_target="tpu_custom_call" | custom-call | bytes 1048576 | tf_op jit(solution)/shard_map/pallas_call | solution.py:285
  48.4 0.0 collective-permute-done.6.refs_0_
  48.4 0.1 collective-permute-start.8
  48.5 0.0 collective-permute-done.9.refs_1_
  48.5 2.0 %collective-permute-start.10 = (bf16[8,3456]{1,0:T(8,128)(2,1)S(1)}, bf16[8,3456]{1,0:T(8,128)(2,1)S(1)}, u32[]{:S(2)}, u32[]{:S(2)}) collective-permute-start(bf16[8,3456]{1,0:T(8,128)(2,1)S(1)} %collective-permute-done.9.refs_1_), channel_id=1, source_target_pairs={{0,4},{4,0},{8,12},{12,8},{1,5},{5,1},{9,13},{13,9},{2,6},{6,2},{1... | collective-permute-start | bytes 165896 | tf_op jit(solution)/shard_map/ppermute | solution.py:321
  50.5 1.3 %shard_map.53.refs_2_ = f32[36,2048]{1,0:T(8,128)S(1)} custom-call(s32[1]{0:T(128)} %bitcast.3.starts, bf16[8,4096]{1,0:T(8,128)(2,1)S(1)} %collective-permute-done.6.refs_0_, bf16[8,3456]{1,0:T(8,128)(2,1)S(1)} %collective-permute-done.9.refs_1_, f32[36,2048]{1,0:T(8,128)S(1)} %shard_map.52.refs_2_, bf16[6656,2048]{1,0:T(8,128)(2,1)S(1)} %bitcast.5), custom_call_target="tpu_custom_call" | custom-call | bytes 1048576 | tf_op jit(solution)/shard_map/pallas_call | solution.py:285
  51.8 1.5 %collective-permute-done.10.refs_1_ = bf16[8,3456]{1,0:T(8,128)(2,1)S(1)} collective-permute-done((bf16[8,3456]{1,0:T(8,128)(2,1)S(1)}, bf16[8,3456]{1,0:T(8,128)(2,1)S(1)}, u32[]{:S(2)}, u32[]{:S(2)}) %collective-permute-start.10) | collective-permute-done | bytes 55328 | tf_op jit(solution)/shard_map/ppermute | solution.py:321
  53.3 0.0 collective-permute-done.8.refs_0_
  53.3 1.3 %shard_map.54 = (f32[8,2304]{1,0:T(8,128)S(1)}, bf16[8,2304]{1,0:T(8,128)(2,1)S(1)}, bf16[8,2304]{1,0:T(8,128)(2,1)S(1)}, bf16[8,2304]{1,0:T(8,128)(2,1)S(1)}) custom-call(s32[1]{0:T(128)} %bitcast.start_ref.starts, bf16[8,4096]{1,0:T(8,128)(2,1)S(1)} %collective-permute-done.8.refs_0_, bf16[8,3456]{1,0:T(8,128)(2,1)S(1)} %collective-permute-done.10.refs_1_, ...), custom_call_target="tpu_custom_call" | custom-call | bytes 1048576 | tf_op jit(solution)/shard_map/pallas_call | solution.py:285
  54.7 0.1 collective-permute-start.11
  54.7 1.7 %collective-permute-start.12 = (bf16[8,2304]{1,0:T(8,128)(2,1)S(1)}, bf16[8,2304]{1,0:T(8,128)(2,1)S(1)}, u32[]{:S(2)}, u32[]{:S(2)}) collective-permute-start(bf16[8,2304]{1,0:T(8,128)(2,1)S(1)} %get-tuple-element.29), channel_id=1, source_target_pairs={{0,2},{1,3},{2,0},{3,1},{4,6},{5,7},{6,4},{7,5},{8,10},{9,11},{10,... | collective-permute-start | bytes 110600 | tf_op jit(solution)/shard_map/ppermute | solution.py:321
  56.5 0.1 collective-permute-start.13
  56.6 0.0 collective-permute-done.11.refs_1_
  56.6 2.2 %collective-permute-done.12.refs_2_ = bf16[8,2304]{1,0:T(8,128)(2,1)S(1)} collective-permute-done((bf16[8,2304]{1,0:T(8,128)(2,1)S(1)}, bf16[8,2304]{1,0:T(8,128)(2,1)S(1)}, u32[]{:S(2)}, u32[]{:S(2)}) %collective-permute-start.12) | collective-permute-done | bytes 36896 | tf_op jit(solution)/shard_map/ppermute | solution.py:321
  58.8 1.1 %collective-permute-done.13.refs_3_ = bf16[8,2304]{1,0:T(8,128)(2,1)S(1)} collective-permute-done((bf16[8,2304]{1,0:T(8,128)(2,1)S(1)}, bf16[8,2304]{1,0:T(8,128)(2,1)S(1)}, u32[]{:S(2)}, u32[]{:S(2)}) %collective-permute-start.13) | collective-permute-done | bytes 36896 | tf_op jit(solution)/shard_map/ppermute | solution.py:321
  59.9 0.7 %shard_map.55 = bf16[9,2048]{1,0:T(8,128)(2,1)} custom-call(f32[8,2304]{1,0:T(8,128)S(1)} %get-tuple-element.27.refs_0_, bf16[8,2304]{1,0:T(8,128)(2,1)S(1)} %collective-permute-done.11.refs_1_, bf16[8,2304]{1,0:T(8,128)(2,1)S(1)} %collective-permute-done.12.refs_2_, bf16[8,2304]{1,0:T(8,128)(2,1)S(1)} %collective-permute-done.13.refs_3_), custom_call_target="tpu_custom_call" | custom-call | bytes 1048576 | tf_op jit(solution)/shard_map/pallas_call | solution.py:309
  (1 shorter events, 0.0 us)
Async XLA Ops:
  0.0 7.3 %collective-permute-start = (bf16[9,2048]{1,0:T(8,128)(2,1)}, bf16[9,2048]{1,0:T(8,128)(2,1)S(1)}, u32[]{:S(2)}, u32[]{:S(2)}) collective-permute-start(bf16[9,2048]{1,0:T(8,128)(2,1)} %param.4), channel_id=1, source_target_pairs={{0,1},{1,0},{2,3},{3,2},{4,5},{5,4},{6,7},{7,6},{8,9},{9,8},{10,11... | collective-permute-start | bytes 110600 | tf_op jit(solution)/shard_map/ppermute | solution.py:321
  0.5 6.8 %collective-permute-start.1 = (bf16[9,2048]{1,0:T(8,128)(2,1)}, bf16[9,2048]{1,0:T(8,128)(2,1)S(1)}, u32[]{:S(2)}, u32[]{:S(2)}) collective-permute-start(bf16[9,2048]{1,0:T(8,128)(2,1)} %param.4), channel_id=1, source_target_pairs={{0,2},{1,3},{2,0},{3,1},{4,6},{5,7},{6,4},{7,5},{8,10},{9,11},{10,... | collective-permute-start | bytes 110600 | tf_op jit(solution)/shard_map/ppermute | solution.py:321
  2.9 4.4 %collective-permute-start.2 = (bf16[9,2048]{1,0:T(8,128)(2,1)}, bf16[9,2048]{1,0:T(8,128)(2,1)S(1)}, u32[]{:S(2)}, u32[]{:S(2)}) collective-permute-start(bf16[9,2048]{1,0:T(8,128)(2,1)} %param.4), channel_id=1, source_target_pairs={{0,3},{1,2},{2,1},{3,0},{4,7},{5,6},{6,5},{7,4},{8,11},{9,10},{10,... | collective-permute-start | bytes 110600 | tf_op jit(solution)/shard_map/ppermute | solution.py:321
  3.1 4.2 %copy-start = (bf16[9,2048]{1,0:T(8,128)(2,1)S(1)}, bf16[9,2048]{1,0:T(8,128)(2,1)}, u32[]{:S(2)}) copy-start(bf16[9,2048]{1,0:T(8,128)(2,1)} %param.4) | copy-start | bytes 110596
  10.2 9.7 %collective-permute-start.3 = (bf16[8,14976]{1,0:T(8,128)(2,1)S(1)}, bf16[8,14976]{1,0:T(8,128)(2,1)S(1)}, u32[]{:S(2)}, u32[]{:S(2)}) collective-permute-start(bf16[8,14976]{1,0:T(8,128)(2,1)S(1)} %shard_map.47.refs_2_), channel_id=1, source_target_pairs={{0,4},{4,0},{8,12},{12,8},{1,5},{5,1},{9,13},{13,9},{2,6},{6,2},{1... | collective-permute-start | bytes 718856 | tf_op jit(solution)/shard_map/ppermute | solution.py:321
  20.0 14.6 %collective-permute-start.4 = (bf16[8,14976]{1,0:T(8,128)(2,1)S(1)}, bf16[8,14976]{1,0:T(8,128)(2,1)S(1)}, u32[]{:S(2)}, u32[]{:S(2)}) collective-permute-start(bf16[8,14976]{1,0:T(8,128)(2,1)S(1)} %add_convert_fusion.refs_3_), channel_id=1, source_target_pairs={{0,8},{4,12},{8,0},{12,4},{1,9},{5,13},{9,1},{13,5},{2,10},{6,14},... | collective-permute-start | bytes 718856 | tf_op jit(solution)/shard_map/ppermute | solution.py:321
  22.6 22.7 %slice-start = ((s8[27262976]{0:T(1024)(128)(4,1)}), s8[4194304]{0:T(1024)(128)(4,1)S(1)}, s32[]{:S(2)}) async-start(s8[27262976]{0:T(1024)(128)(4,1)} %bitcast.4), calls=%async_computation | async-start | bytes 8388608
  22.6 22.7 %slice-start.1 = ((s8[27262976]{0:T(1024)(128)(4,1)}), s8[4194304]{0:T(1024)(128)(4,1)S(1)}, s32[]{:S(2)}) async-start(s8[27262976]{0:T(1024)(128)(4,1)} %bitcast.4), calls=%async_computation.1 | async-start | bytes 8388608
  22.6 22.7 %slice-start.2 = ((s8[27262976]{0:T(1024)(128)(4,1)}), s8[4194304]{0:T(1024)(128)(4,1)S(1)}, s32[]{:S(2)}) async-start(s8[27262976]{0:T(1024)(128)(4,1)} %bitcast.4), calls=%async_computation.2 | async-start | bytes 8388608
  22.6 22.7 %slice-start.3 = ((s8[27262976]{0:T(1024)(128)(4,1)}), s8[4194304]{0:T(1024)(128)(4,1)S(1)}, s32[]{:S(2)}) async-start(s8[27262976]{0:T(1024)(128)(4,1)} %bitcast.4), calls=%async_computation.3 | async-start | bytes 8388608
  27.4 11.4 %collective-permute-start.5 = (bf16[8,14976]{1,0:T(8,128)(2,1)S(1)}, bf16[8,14976]{1,0:T(8,128)(2,1)S(1)}, u32[]{:S(2)}, u32[]{:S(2)}) collective-permute-start(bf16[8,14976]{1,0:T(8,128)(2,1)S(1)} %shard_map.49.refs_2_), channel_id=1, source_target_pairs={{0,4},{4,0},{8,12},{12,8},{1,5},{5,1},{9,13},{13,9},{2,6},{6,2},{1... | collective-permute-start | bytes 718856 | tf_op jit(solution)/shard_map/ppermute | solution.py:321
  28.0 17.4 %slice-start.4 = ((s8[27262976]{0:T(1024)(128)(4,1)}), s8[4194304]{0:T(1024)(128)(4,1)S(1)}, s32[]{:S(2)}) async-start(s8[27262976]{0:T(1024)(128)(4,1)} %bitcast.4), calls=%async_computation.4 | async-start | bytes 8388608
  28.0 17.4 %slice-start.5 = ((s8[27262976]{0:T(1024)(128)(4,1)}), s8[4194304]{0:T(1024)(128)(4,1)S(1)}, s32[]{:S(2)}) async-start(s8[27262976]{0:T(1024)(128)(4,1)} %bitcast.4), calls=%async_computation.5 | async-start | bytes 8388608
  28.0 17.4 %slice-start.6 = ((s8[27262976]{0:T(1024)(128)(4,1)}), s8[2097152]{0:T(1024)(128)(4,1)S(1)}, s32[]{:S(2)}) async-start(s8[27262976]{0:T(1024)(128)(4,1)} %bitcast.4), calls=%async_computation.6 | async-start | bytes 4194304
  38.9 6.4 %collective-permute-start.7 = (bf16[8,7552]{1,0:T(8,128)(2,1)S(1)}, bf16[8,7552]{1,0:T(8,128)(2,1)S(1)}, u32[]{:S(2)}, u32[]{:S(2)}) collective-permute-start(bf16[8,7552]{1,0:T(8,128)(2,1)S(1)} %get-tuple-element.21.refs_0_), channel_id=1, source_target_pairs={{0,4},{4,0},{8,12},{12,8},{1,5},{5,1},{9,13},{13,9},{2,6},{6,2},{1... | collective-permute-start | bytes 362504 | tf_op jit(solution)/shard_map/ppermute | solution.py:321
  39.0 9.4 %collective-permute-start.6 = (bf16[8,4096]{1,0:T(8,128)(2,1)S(1)}, bf16[8,4096]{1,0:T(8,128)(2,1)S(1)}, u32[]{:S(2)}, u32[]{:S(2)}) collective-permute-start(bf16[8,4096]{1,0:T(8,128)(2,1)S(1)} %get-tuple-element.20), channel_id=1, source_target_pairs={{0,8},{4,12},{8,0},{12,4},{1,9},{5,13},{9,1},{13,5},{2,10},{6,14},... | collective-permute-start | bytes 196616 | tf_op jit(solution)/shard_map/ppermute | solution.py:321
  39.9 8.6 %collective-permute-start.9 = (bf16[8,3456]{1,0:T(8,128)(2,1)S(1)}, bf16[8,3456]{1,0:T(8,128)(2,1)S(1)}, u32[]{:S(2)}, u32[]{:S(2)}) collective-permute-start(bf16[8,3456]{1,0:T(8,128)(2,1)S(1)} %get-tuple-element.23), channel_id=1, source_target_pairs={{0,8},{4,12},{8,0},{12,4},{1,9},{5,13},{9,1},{13,5},{2,10},{6,14},... | collective-permute-start | bytes 165896 | tf_op jit(solution)/shard_map/ppermute | solution.py:321
  48.4 4.9 %collective-permute-start.8 = (bf16[8,4096]{1,0:T(8,128)(2,1)S(1)}, bf16[8,4096]{1,0:T(8,128)(2,1)S(1)}, u32[]{:S(2)}, u32[]{:S(2)}) collective-permute-start(bf16[8,4096]{1,0:T(8,128)(2,1)S(1)} %collective-permute-done.6.refs_0_), channel_id=1, source_target_pairs={{0,4},{4,0},{8,12},{12,8},{1,5},{5,1},{9,13},{13,9},{2,6},{6,2},{1... | collective-permute-start | bytes 196616 | tf_op jit(solution)/shard_map/ppermute | solution.py:321
  48.5 4.8 %collective-permute-start.10 = (bf16[8,3456]{1,0:T(8,128)(2,1)S(1)}, bf16[8,3456]{1,0:T(8,128)(2,1)S(1)}, u32[]{:S(2)}, u32[]{:S(2)}) collective-permute-start(bf16[8,3456]{1,0:T(8,128)(2,1)S(1)} %collective-permute-done.9.refs_1_), channel_id=1, source_target_pairs={{0,4},{4,0},{8,12},{12,8},{1,5},{5,1},{9,13},{13,9},{2,6},{6,2},{1... | collective-permute-start | bytes 165896 | tf_op jit(solution)/shard_map/ppermute | solution.py:321
  54.7 1.9 %collective-permute-start.11 = (bf16[8,2304]{1,0:T(8,128)(2,1)S(1)}, bf16[8,2304]{1,0:T(8,128)(2,1)S(1)}, u32[]{:S(2)}, u32[]{:S(2)}) collective-permute-start(bf16[8,2304]{1,0:T(8,128)(2,1)S(1)} %get-tuple-element.28), channel_id=1, source_target_pairs={{0,1},{1,0},{2,3},{3,2},{4,5},{5,4},{6,7},{7,6},{8,9},{9,8},{10,11... | collective-permute-start | bytes 110600 | tf_op jit(solution)/shard_map/ppermute | solution.py:321
  54.7 4.0 %collective-permute-start.12 = (bf16[8,2304]{1,0:T(8,128)(2,1)S(1)}, bf16[8,2304]{1,0:T(8,128)(2,1)S(1)}, u32[]{:S(2)}, u32[]{:S(2)}) collective-permute-start(bf16[8,2304]{1,0:T(8,128)(2,1)S(1)} %get-tuple-element.29), channel_id=1, source_target_pairs={{0,2},{1,3},{2,0},{3,1},{4,6},{5,7},{6,4},{7,5},{8,10},{9,11},{10,... | collective-permute-start | bytes 110600 | tf_op jit(solution)/shard_map/ppermute | solution.py:321
  56.5 3.4 %collective-permute-start.13 = (bf16[8,2304]{1,0:T(8,128)(2,1)S(1)}, bf16[8,2304]{1,0:T(8,128)(2,1)S(1)}, u32[]{:S(2)}, u32[]{:S(2)}) collective-permute-start(bf16[8,2304]{1,0:T(8,128)(2,1)S(1)} %get-tuple-element.30), channel_id=1, source_target_pairs={{0,3},{1,2},{2,1},{3,0},{4,7},{5,6},{6,5},{7,4},{8,11},{9,10},{10,... | collective-permute-start | bytes 110600 | tf_op jit(solution)/shard_map/ppermute | solution.py:321

commit v7 on v5

--- a/solution.py
+++ b/solution.py
@@ -9,6 +9,7 @@
 
 MIB = 1 << 20
 STEP = 256
+IN_FLIGHT = 5
 TOKEN_AXES = ("gy", "gz")
 IN_HBM = pl.BlockSpec(memory_space=pltpu.HBM)
 ANY = pl.BlockSpec(memory_space=pl.ANY)
@@ -55,26 +56,29 @@
         out[:, at : at + width] = tail.astype(out.dtype)
 
 
-def start_copies(width, start_ref, gate_ref, up_ref, held, sems):
+def block_copies(width, first, start_ref, gate_ref, up_ref, held, sems):
     columns = pl.ds(pl.multiple_of(start_ref[0], 128), width)
     copies = []
     for k, (row, rows) in enumerate(pieces_of(held.shape[1], STEP)):
         for w, weight in enumerate((gate_ref, up_ref)):
             copy = pltpu.make_async_copy(
-                weight.at[pl.ds(row, rows), columns], held.at[w, pl.ds(row, rows)], sems.at[w, k]
+                weight.at[pl.ds(first + row, rows), columns],
+                held.at[w, pl.ds(row, rows)],
+                sems.at[w, k],
             )
-            copy.start()
             copies.append((w, row, rows, copy))
     return copies
 
 
 def fetch_kernel(width, start_ref, gate_ref, up_ref, held, sems):
-    for _, _, _, copy in start_copies(width, start_ref, gate_ref, up_ref, held, sems):
+    copies = block_copies(width, 0, start_ref, gate_ref, up_ref, held, sems)
+    for _, _, _, copy in copies:
+        copy.start()
+    for _, _, _, copy in copies:
         copy.wait()
 
 
-def fetch(gate_weight, up_weight, start, width):
-    depth = gate_weight.shape[0]
+def fetch(gate_weight, up_weight, start, depth, width):
     return pl.pallas_call(
         functools.partial(fetch_kernel, width),
         out_shape=pltpu.VMEM((2, depth, width), jnp.bfloat16),
@@ -86,59 +90,51 @@
     )(start, in_hbm(gate_weight), in_hbm(up_weight))
 
 
-def multiply(x_ref, held, total, steps):
-    for w, row, rows, copy in steps:
-        if copy is not None:
-            copy.wait()
-        term = jnp.dot(
-            x_ref[:, row : row + rows], held[w, row : row + rows, :], preferred_element_type=jnp.float32
-        )
+def block_kernel(width, has_held, start_ref, x_ref, *refs):
+    refs = list(refs)
+    held = refs.pop(0) if has_held else None
+    gate_ref, up_ref, _, out, stream, total, sems = refs
+    first = x_ref.shape[1] - stream.shape[1]
+    copies = block_copies(width, first, start_ref, gate_ref, up_ref, stream, sems)
+    for _, _, _, copy in copies[:IN_FLIGHT]:
+        copy.start()
+
+    def accumulate(w, row, rows, weight):
+        term = jnp.dot(x_ref[:, row : row + rows], weight, preferred_element_type=jnp.float32)
         if row == 0:
             total[w] = term
         else:
             total[w] += term
 
-
-def held_kernel(x_ref, held, out, total):
-    parts = pieces_of(x_ref.shape[1], STEP)
-    multiply(x_ref, held, total, [(w, row, rows, None) for w in range(2) for row, rows in parts])
+    if has_held:
+        for row, rows in pieces_of(first, STEP):
+            for w in range(2):
+                accumulate(w, row, rows, held[w, row : row + rows, :])
+    for i, (w, row, rows, copy) in enumerate(copies):
+        copy.wait()
+        if i + IN_FLIGHT < len(copies):
+            copies[i + IN_FLIGHT][-1].start()
+        accumulate(w, first + row, rows, stream[w, row : row + rows, :])
     pack_pair(out, total[0], total[1])
 
 
-def gate_up_held(features, held):
-    rows, width = features.shape[0], held.shape[2]
-    return pl.pallas_call(
-        held_kernel,
+def gate_up(features, gate_weight, up_weight, start, width, after, held=None):
+    rows, depth = features.shape
+    below = depth if held is None else depth - held.shape[1]
+    before = [] if held is None else [in_vmem(held)]
+    return pl.pallas_call(
+        functools.partial(block_kernel, width, held is not None),
         out_shape=jax.ShapeDtypeStruct((8, packed_pair_width(rows, width)), jnp.bfloat16),
-        in_specs=[WHOLE, WHOLE],
-        out_specs=WHOLE,
-        scratch_shapes=[pltpu.VMEM((2, rows, width), jnp.float32)],
-        compiler_params=params(8),
-        cost_estimate=SMALL,
-    )(features, in_vmem(held))
-
-
-def stream_kernel(width, start_ref, x_ref, gate_ref, up_ref, _, out, held, total, sems):
-    copies = start_copies(width, start_ref, gate_ref, up_ref, held, sems)
-    multiply(x_ref, held, total, copies)
-    pack_pair(out, total[0], total[1])
-
-
-def gate_up_stream(features, gate_weight, up_weight, start, width, after):
-    rows, depth = features.shape
-    return pl.pallas_call(
-        functools.partial(stream_kernel, width),
-        out_shape=jax.ShapeDtypeStruct((8, packed_pair_width(rows, width)), jnp.bfloat16),
-        in_specs=[SCALARS, WHOLE, IN_HBM, IN_HBM, ANY],
+        in_specs=[SCALARS, WHOLE] + [WHOLE] * len(before) + [IN_HBM, IN_HBM, ANY],
         out_specs=WHOLE,
         scratch_shapes=[
-            pltpu.VMEM((2, depth, width), jnp.bfloat16),
+            pltpu.VMEM((2, below, width), jnp.bfloat16),
             pltpu.VMEM((2, rows, width), jnp.float32),
-            pltpu.SemaphoreType.DMA((2, len(pieces_of(depth, STEP)))),
+            pltpu.SemaphoreType.DMA((2, len(pieces_of(below, STEP)))),
         ],
-        compiler_params=params(18),
-        cost_estimate=SMALL,
-    )(start, features, in_hbm(gate_weight), in_hbm(up_weight), after)
+        compiler_params=params(5 + -(-below * width * 4 // MIB)),
+        cost_estimate=SMALL,
+    )(start, features, *before, in_hbm(gate_weight), in_hbm(up_weight), after)
 
 
 def hidden_tail(rows, width):
@@ -291,16 +287,17 @@
     def starts_of(*distances):
         return jnp.stack([(me ^ d) * width for d in distances]).astype(jnp.int32)
 
-    held = fetch(gate_weight, up_weight, starts_of(3), width)
+    early = gate_weight.shape[0] - STEP
+    held = fetch(gate_weight, up_weight, starts_of(3), early, width)
     features = jnp.concatenate(
         [tokens] + [swap(tokens, TOKEN_AXES, n_token, r) for r in range(1, n_token)], axis=0
     )
     rows = features.shape[0]
 
-    def block_for(d, after):
-        return gate_up_stream(features, gate_weight, up_weight, starts_of(d), width, after)
-
-    relayed = gate_up_held(features, held)
+    def block_for(d, after, held=None):
+        return gate_up(features, gate_weight, up_weight, starts_of(d), width, after, held)
+
+    relayed = block_for(3, features, held)
     arrived = swap(relayed, "gx", n_gx, 1)
     across = block_for(2, relayed)
     across = lax.optimization_barrier(add(across, arrived).astype(jnp.bfloat16))
@@ -340,7 +337,7 @@
     n_token = lax.axis_size(TOKEN_AXES)
     rows = tokens.shape[0] * n_token
     tokens_fit = n_token > 1 and n_token & (n_token - 1) == 0 and rows % 4 == 0
-    weights_fit = gate_weight.shape[1] % (128 * 4) == 0 and gate_weight.shape[0] % STEP == 0
+    weights_fit = gate_weight.shape[1] % (128 * 4) == 0 and gate_weight.shape[0] % STEP == 0 and gate_weight.shape[0] > STEP
     columns_fit = down_weight.shape[1] % (128 * 8) == 0
     if n_gx == 4 and tokens_fit and weights_fit and columns_fit:
         return direct(tokens, gate_weight, up_weight, down_weight)

time: 58.3 us -> 58.9 us (1.010)
  Pallas kernels: 32 us -> 35.5 us
  starting transfers between devices: 15.7 us -> 13.6 us
  waiting for transfers between devices: 9.94 us -> 9.25 us
    pallas_call x4, Pallas kernels: 20.5 us -> 24.6 us  [gate_up(): pl.pallas_call(functools.partial(block_kernel, width, held is not None),...]
    ppermute x12, starting transfers between devices: 15.7 us -> 13.6 us  [swap(): return lax.ppermute(value, axes, [(i, i ^ distance) for i in range(size)])]
    ppermute x12, waiting for transfers between devices: 9.94 us -> 9.25 us  [swap(): return lax.ppermute(value, axes, [(i, i ^ distance) for i in range(size)])]
  transfers between devices with their start and end apart: 12 -> 12, of which waited for: 6 -> 5; matrix products, arithmetic and copies ran while one was open for 0% -> 0% of each run, Pallas kernels for 48% -> 53%
where the time goes in v7:
time: 58.9 us; the launch traced here: 58.8 us
  Pallas kernels  35.5 us (60%)
  starting transfers between devices  13.6 us (23%)
  waiting for transfers between devices  9.25 us (16%)
    pallas_call x4, Pallas kernels, gate_up(): pl.pallas_call(functools.partial(block_kernel, width, held is not None),...  24.6 us
    ppermute x12, starting transfers between devices, swap(): return lax.ppermute(value, axes, [(i, i ^ distance) for i in range(size)])  13.6 us
    ppermute x12, waiting for transfers between devices, swap(): return lax.ppermute(value, axes, [(i, i ^ distance) for i in range(size)])  9.25 us
    pallas_call x2, Pallas kernels, down(): pl.pallas_call(functools.partial(down_kernel, before is None, rows, width...  5.48 us
    pallas_call x1, Pallas kernels, fetch(): pl.pallas_call(functools.partial(fetch_kernel, width), out_shape=pltpu.VM...  4.65 us
  transfers between devices with their start and end apart: 12, of which 5 were waited for; matrix products, arithmetic and copies ran while one was open for 0% of the time, Pallas kernels for 53%

profile of v7, /device:TPU:0, one launch (start us, length us, event | category | flops | bytes accessed | tf_op | source)
XLA Modules:
  0.0 58.8 jit_solution(2001935949844660243)
XLA Ops:
  0.0 0.5 collective-permute-start
  0.5 2.5 %collective-permute-start.1 = (bf16[9,2048]{1,0:T(8,128)(2,1)}, bf16[9,2048]{1,0:T(8,128)(2,1)S(1)}, u32[]{:S(2)}, u32[]{:S(2)}) collective-permute-start(bf16[9,2048]{1,0:T(8,128)(2,1)} %param.4), channel_id=1, source_target_pairs={{0,2},{1,3},{2,0},{3,1},{4,6},{5,7},{6,4},{7,5},{8,10},{9,11},{10,... | collective-permute-start | bytes 110600 | tf_op jit(solution)/shard_map/ppermute | solution.py:274
  2.9 0.1 collective-permute-start.2
  3.1 0.0 copy-start
  3.1 4.6 %shard_map.46.refs_0_ = bf16[2,1792,1664]{2,1,0:T(8,128)(2,1)S(1)} custom-call(s32[1]{0:T(128)} %bitcast.start_ref.starts, bf16[2048,6656]{1,0:T(8,128)(2,1)} %refs_0_.5, bf16[2048,6656]{1,0:T(8,128)(2,1)} %refs_1_.7), custom_call_target="tpu_custom_call" | custom-call | bytes 1048576 | tf_op jit(solution)/shard_map/pallas_call | solution.py:82
  7.7 0.0 collective-permute-done
  7.8 0.0 collective-permute-done.1
  7.8 0.0 collective-permute-done.2
  7.8 0.0 copy-done
  7.8 0.1 pad_maximum_fusion.x_ref.refs_3_
  7.9 2.5 %shard_map.47.refs_2_ = bf16[8,14976]{1,0:T(8,128)(2,1)S(1)} custom-call(s32[1]{0:T(128)} %bitcast.start_ref.starts, bf16[36,2048]{1,0:T(8,128)(2,1)S(1)} %pad_maximum_fusion.x_ref.refs_3_, bf16[2,1792,1664]{2,1,0:T(8,128)(2,1)S(1)} %shard_map.46.refs_0_, bf16[2048,6656]{1,0:T(8,128)(2,1)} %refs_0_.5, bf16[2048,6656]{1,0:T(8,128)(2,1)} %refs_1_.7, ...), custom_call_target="tpu_custom_call" | custom-call | bytes 1048576 | tf_op jit(solution)/shard_map/pallas_call | solution.py:125
  10.4 1.8 %collective-permute-start.3 = (bf16[8,14976]{1,0:T(8,128)(2,1)S(1)}, bf16[8,14976]{1,0:T(8,128)(2,1)S(1)}, u32[]{:S(2)}, u32[]{:S(2)}) collective-permute-start(bf16[8,14976]{1,0:T(8,128)(2,1)S(1)} %shard_map.47.refs_2_), channel_id=1, source_target_pairs={{0,4},{4,0},{8,12},{12,8},{1,5},{5,1},{9,13},{13,9},{2,6},{6,2},{1... | collective-permute-start | bytes 718856 | tf_op jit(solution)/shard_map/ppermute | solution.py:274
  12.2 5.9 %shard_map.48 = bf16[8,14976]{1,0:T(8,128)(2,1)S(1)} custom-call(s32[1]{0:T(128)} %bitcast.3.start_ref, bf16[36,2048]{1,0:T(8,128)(2,1)S(1)} %pad_maximum_fusion.x_ref.refs_3_, bf16[2048,6656]{1,0:T(8,128)(2,1)} %refs_0_.5, bf16[2048,6656]{1,0:T(8,128)(2,1)} %refs_1_.7, bf16[8,14976]{1,0:T(8,128)(2,1)S(1)} %shard_map.47.refs_2_), custom_call_target="tpu_custom_call" | custom-call | bytes 1048576 | tf_op jit(solution)/shard_map/pallas_call | solution.py:125
  18.1 0.3 collective-permute-done.3
  18.5 0.1 add_convert_fusion.refs_2_
  18.5 2.8 %collective-permute-start.4 = (bf16[8,14976]{1,0:T(8,128)(2,1)S(1)}, bf16[8,14976]{1,0:T(8,128)(2,1)S(1)}, u32[]{:S(2)}, u32[]{:S(2)}) collective-permute-start(bf16[8,14976]{1,0:T(8,128)(2,1)S(1)} %add_convert_fusion.refs_2_), channel_id=1, source_target_pairs={{0,8},{4,12},{8,0},{12,4},{1,9},{5,13},{9,1},{13,5},{2,10},{6,14},... | collective-permute-start | bytes 718856 | tf_op jit(solution)/shard_map/ppermute | solution.py:274
  21.3 0.0 slice-start
  21.3 0.0 slice-start.1
  21.3 0.0 slice-start.2
  21.3 0.0 slice-start.3
  21.3 8.1 %shard_map.49.refs_2_ = bf16[8,14976]{1,0:T(8,128)(2,1)S(1)} custom-call(s32[1]{0:T(128)} %bitcast.2.start_ref, bf16[36,2048]{1,0:T(8,128)(2,1)S(1)} %pad_maximum_fusion.x_ref.refs_3_, bf16[2048,6656]{1,0:T(8,128)(2,1)} %refs_0_.5, bf16[2048,6656]{1,0:T(8,128)(2,1)} %refs_1_.7, bf16[8,14976]{1,0:T(8,128)(2,1)S(1)} %add_convert_fusion.refs_2_), custom_call_target="tpu_custom_call" | custom-call | bytes 1048576 | tf_op jit(solution)/shard_map/pallas_call | solution.py:125
  29.5 1.6 %collective-permute-start.5 = (bf16[8,14976]{1,0:T(8,128)(2,1)S(1)}, bf16[8,14976]{1,0:T(8,128)(2,1)S(1)}, u32[]{:S(2)}, u32[]{:S(2)}) collective-permute-start(bf16[8,14976]{1,0:T(8,128)(2,1)S(1)} %shard_map.49.refs_2_), channel_id=1, source_target_pairs={{0,4},{4,0},{8,12},{12,8},{1,5},{5,1},{9,13},{13,9},{2,6},{6,2},{1... | collective-permute-start | bytes 718856 | tf_op jit(solution)/shard_map/ppermute | solution.py:274
  31.1 0.0 slice-start.4
  31.1 0.0 slice-start.5
  31.1 0.0 slice-start.6
  31.1 8.0 %shard_map.50 = bf16[8,14976]{1,0:T(8,128)(2,1)S(1)} custom-call(s32[1]{0:T(128)} %bitcast.1.start_ref, bf16[36,2048]{1,0:T(8,128)(2,1)S(1)} %pad_maximum_fusion.x_ref.refs_3_, bf16[2048,6656]{1,0:T(8,128)(2,1)} %refs_0_.5, bf16[2048,6656]{1,0:T(8,128)(2,1)} %refs_1_.7, bf16[8,14976]{1,0:T(8,128)(2,1)S(1)} %shard_map.49.refs_2_), custom_call_target="tpu_custom_call" | custom-call | bytes 1048576 | tf_op jit(solution)/shard_map/pallas_call | solution.py:125
  39.2 0.0 collective-permute-done.4
  39.2 0.1 convert_add_fusion.summed
  39.2 0.0 collective-permute-done.5.near
  39.3 0.1 shard_map.51.refs_0_
  39.3 0.4 collective-permute-start.6
  39.7 1.6 %collective-permute-start.8 = (bf16[8,7552]{1,0:T(8,128)(2,1)S(1)}, bf16[8,7552]{1,0:T(8,128)(2,1)S(1)}, u32[]{:S(2)}, u32[]{:S(2)}) collective-permute-start(bf16[8,7552]{1,0:T(8,128)(2,1)S(1)} %shard_map.51.refs_0_), channel_id=1, source_target_pairs={{0,4},{4,0},{8,12},{12,8},{1,5},{5,1},{9,13},{13,9},{2,6},{6,2},{1... | collective-permute-start | bytes 362504 | tf_op jit(solution)/shard_map/ppermute | solution.py:274
  41.4 5.6 %collective-permute-done.6.refs_2_ = bf16[8,7552]{1,0:T(8,128)(2,1)S(1)} collective-permute-done((bf16[8,7552]{1,0:T(8,128)(2,1)S(1)}, bf16[8,7552]{1,0:T(8,128)(2,1)S(1)}, u32[]{:S(2)}, u32[]{:S(2)}) %collective-permute-start.6) | collective-permute-done | bytes 120864 | tf_op jit(solution)/shard_map/ppermute | solution.py:274
  47.0 0.0 collective-permute-start.7
  47.0 0.1 pad_add_fusion.starts
  47.1 0.0 collective-permute-done.8.refs_1_
  47.1 0.0 slice-done
  47.1 0.0 slice-done.1
  47.1 0.0 slice-done.2
  47.1 0.0 slice-done.3
  47.1 0.0 slice-done.4
  47.1 0.0 slice-done.5
  47.1 0.0 slice-done.6
  47.1 4.2 %shard_map.52.refs_1_ = f32[36,2048]{1,0:T(8,128)S(1)} custom-call(s32[3]{0:T(128)S(1)} %pad_add_fusion.starts, bf16[8,7552]{1,0:T(8,128)(2,1)S(1)} %shard_map.51.refs_0_, bf16[8,7552]{1,0:T(8,128)(2,1)S(1)} %collective-permute-done.8.refs_1_, bf16[8,7552]{1,0:T(8,128)(2,1)S(1)} %collective-permute-done.6.refs_2_, bf16[6656,2048]{1,0:T(8,128)(2,1)S(1)} %bitcast.5), custom_call_target="tpu_custom_call" | custom-call | bytes 1048576 | tf_op jit(solution)/shard_map/pallas_call | solution.py:238
  51.3 0.5 collective-permute-done.7.refs_0_
  51.8 1.3 %shard_map.53 = (f32[8,2304]{1,0:T(8,128)S(1)}, bf16[8,2304]{1,0:T(8,128)(2,1)S(1)}, bf16[8,2304]{1,0:T(8,128)(2,1)S(1)}, bf16[8,2304]{1,0:T(8,128)(2,1)S(1)}) custom-call(s32[1]{0:T(128)} %bitcast.start_ref.starts, bf16[8,7552]{1,0:T(8,128)(2,1)S(1)} %collective-permute-done.7.refs_0_, f32[36,2048]{1,0:T(8,128)S(1)} %shard_map.52.refs_1_, ...), custom_call_target="tpu_custom_call" | custom-call | bytes 1048576 | tf_op jit(solution)/shard_map/pallas_call | solution.py:238
  53.2 1.6 %collective-permute-start.10 = (bf16[8,2304]{1,0:T(8,128)(2,1)S(1)}, bf16[8,2304]{1,0:T(8,128)(2,1)S(1)}, u32[]{:S(2)}, u32[]{:S(2)}) collective-permute-start(bf16[8,2304]{1,0:T(8,128)(2,1)S(1)} %get-tuple-element.11), channel_id=1, source_target_pairs={{0,2},{1,3},{2,0},{3,1},{4,6},{5,7},{6,4},{7,5},{8,10},{9,11},{10,... | collective-permute-start | bytes 110600 | tf_op jit(solution)/shard_map/ppermute | solution.py:274
  54.7 0.0 collective-permute-start.11
  54.7 0.6 %collective-permute-start.9 = (bf16[8,2304]{1,0:T(8,128)(2,1)S(1)}, bf16[8,2304]{1,0:T(8,128)(2,1)S(1)}, u32[]{:S(2)}, u32[]{:S(2)}) collective-permute-start(bf16[8,2304]{1,0:T(8,128)(2,1)S(1)} %get-tuple-element.10), channel_id=1, source_target_pairs={{0,1},{1,0},{2,3},{3,2},{4,5},{5,4},{6,7},{7,6},{8,9},{9,8},{10,11... | collective-permute-start | bytes 110600 | tf_op jit(solution)/shard_map/ppermute | solution.py:274
  55.4 1.8 %collective-permute-done.10.refs_2_ = bf16[8,2304]{1,0:T(8,128)(2,1)S(1)} collective-permute-done((bf16[8,2304]{1,0:T(8,128)(2,1)S(1)}, bf16[8,2304]{1,0:T(8,128)(2,1)S(1)}, u32[]{:S(2)}, u32[]{:S(2)}) %collective-permute-start.10) | collective-permute-done | bytes 36896 | tf_op jit(solution)/shard_map/ppermute | solution.py:274
  57.2 0.9 %collective-permute-done.11.refs_3_ = bf16[8,2304]{1,0:T(8,128)(2,1)S(1)} collective-permute-done((bf16[8,2304]{1,0:T(8,128)(2,1)S(1)}, bf16[8,2304]{1,0:T(8,128)(2,1)S(1)}, u32[]{:S(2)}, u32[]{:S(2)}) %collective-permute-start.11) | collective-permute-done | bytes 36896 | tf_op jit(solution)/shard_map/ppermute | solution.py:274
  58.1 0.0 collective-permute-done.9.refs_1_
  58.1 0.7 %shard_map.54 = bf16[9,2048]{1,0:T(8,128)(2,1)} custom-call(f32[8,2304]{1,0:T(8,128)S(1)} %get-tuple-element.9.refs_0_, bf16[8,2304]{1,0:T(8,128)(2,1)S(1)} %collective-permute-done.9.refs_1_, bf16[8,2304]{1,0:T(8,128)(2,1)S(1)} %collective-permute-done.10.refs_2_, bf16[8,2304]{1,0:T(8,128)(2,1)S(1)} %collective-permute-done.11.refs_3_), custom_call_target="tpu_custom_call" | custom-call | bytes 1048576 | tf_op jit(solution)/shard_map/pallas_call | solution.py:262
  (1 shorter events, 0.0 us)
Async XLA Ops:
  0.0 7.7 %collective-permute-start = (bf16[9,2048]{1,0:T(8,128)(2,1)}, bf16[9,2048]{1,0:T(8,128)(2,1)S(1)}, u32[]{:S(2)}, u32[]{:S(2)}) collective-permute-start(bf16[9,2048]{1,0:T(8,128)(2,1)} %param.4), channel_id=1, source_target_pairs={{0,1},{1,0},{2,3},{3,2},{4,5},{5,4},{6,7},{7,6},{8,9},{9,8},{10,11... | collective-permute-start | bytes 110600 | tf_op jit(solution)/shard_map/ppermute | solution.py:274
  0.5 7.3 %collective-permute-start.1 = (bf16[9,2048]{1,0:T(8,128)(2,1)}, bf16[9,2048]{1,0:T(8,128)(2,1)S(1)}, u32[]{:S(2)}, u32[]{:S(2)}) collective-permute-start(bf16[9,2048]{1,0:T(8,128)(2,1)} %param.4), channel_id=1, source_target_pairs={{0,2},{1,3},{2,0},{3,1},{4,6},{5,7},{6,4},{7,5},{8,10},{9,11},{10,... | collective-permute-start | bytes 110600 | tf_op jit(solution)/shard_map/ppermute | solution.py:274
  2.9 4.8 %collective-permute-start.2 = (bf16[9,2048]{1,0:T(8,128)(2,1)}, bf16[9,2048]{1,0:T(8,128)(2,1)S(1)}, u32[]{:S(2)}, u32[]{:S(2)}) collective-permute-start(bf16[9,2048]{1,0:T(8,128)(2,1)} %param.4), channel_id=1, source_target_pairs={{0,3},{1,2},{2,1},{3,0},{4,7},{5,6},{6,5},{7,4},{8,11},{9,10},{10,... | collective-permute-start | bytes 110600 | tf_op jit(solution)/shard_map/ppermute | solution.py:274
  3.1 4.7 %copy-start = (bf16[9,2048]{1,0:T(8,128)(2,1)S(1)}, bf16[9,2048]{1,0:T(8,128)(2,1)}, u32[]{:S(2)}) copy-start(bf16[9,2048]{1,0:T(8,128)(2,1)} %param.4) | copy-start | bytes 110596
  10.4 8.1 %collective-permute-start.3 = (bf16[8,14976]{1,0:T(8,128)(2,1)S(1)}, bf16[8,14976]{1,0:T(8,128)(2,1)S(1)}, u32[]{:S(2)}, u32[]{:S(2)}) collective-permute-start(bf16[8,14976]{1,0:T(8,128)(2,1)S(1)} %shard_map.47.refs_2_), channel_id=1, source_target_pairs={{0,4},{4,0},{8,12},{12,8},{1,5},{5,1},{9,13},{13,9},{2,6},{6,2},{1... | collective-permute-start | bytes 718856 | tf_op jit(solution)/shard_map/ppermute | solution.py:274
  18.5 20.7 %collective-permute-start.4 = (bf16[8,14976]{1,0:T(8,128)(2,1)S(1)}, bf16[8,14976]{1,0:T(8,128)(2,1)S(1)}, u32[]{:S(2)}, u32[]{:S(2)}) collective-permute-start(bf16[8,14976]{1,0:T(8,128)(2,1)S(1)} %add_convert_fusion.refs_2_), channel_id=1, source_target_pairs={{0,8},{4,12},{8,0},{12,4},{1,9},{5,13},{9,1},{13,5},{2,10},{6,14},... | collective-permute-start | bytes 718856 | tf_op jit(solution)/shard_map/ppermute | solution.py:274
  21.3 25.7 %slice-start = ((s8[27262976]{0:T(1024)(128)(4,1)}), s8[4194304]{0:T(1024)(128)(4,1)S(1)}, s32[]{:S(2)}) async-start(s8[27262976]{0:T(1024)(128)(4,1)} %bitcast.4), calls=%async_computation | async-start | bytes 8388608
  21.3 25.7 %slice-start.1 = ((s8[27262976]{0:T(1024)(128)(4,1)}), s8[4194304]{0:T(1024)(128)(4,1)S(1)}, s32[]{:S(2)}) async-start(s8[27262976]{0:T(1024)(128)(4,1)} %bitcast.4), calls=%async_computation.1 | async-start | bytes 8388608
  21.3 25.7 %slice-start.2 = ((s8[27262976]{0:T(1024)(128)(4,1)}), s8[4194304]{0:T(1024)(128)(4,1)S(1)}, s32[]{:S(2)}) async-start(s8[27262976]{0:T(1024)(128)(4,1)} %bitcast.4), calls=%async_computation.2 | async-start | bytes 8388608
  21.3 25.8 %slice-start.3 = ((s8[27262976]{0:T(1024)(128)(4,1)}), s8[4194304]{0:T(1024)(128)(4,1)S(1)}, s32[]{:S(2)}) async-start(s8[27262976]{0:T(1024)(128)(4,1)} %bitcast.4), calls=%async_computation.3 | async-start | bytes 8388608
  29.5 9.8 %collective-permute-start.5 = (bf16[8,14976]{1,0:T(8,128)(2,1)S(1)}, bf16[8,14976]{1,0:T(8,128)(2,1)S(1)}, u32[]{:S(2)}, u32[]{:S(2)}) collective-permute-start(bf16[8,14976]{1,0:T(8,128)(2,1)S(1)} %shard_map.49.refs_2_), channel_id=1, source_target_pairs={{0,4},{4,0},{8,12},{12,8},{1,5},{5,1},{9,13},{13,9},{2,6},{6,2},{1... | collective-permute-start | bytes 718856 | tf_op jit(solution)/shard_map/ppermute | solution.py:274
  31.1 16.0 %slice-start.4 = ((s8[27262976]{0:T(1024)(128)(4,1)}), s8[4194304]{0:T(1024)(128)(4,1)S(1)}, s32[]{:S(2)}) async-start(s8[27262976]{0:T(1024)(128)(4,1)} %bitcast.4), calls=%async_computation.4 | async-start | bytes 8388608
  31.1 16.0 %slice-start.5 = ((s8[27262976]{0:T(1024)(128)(4,1)}), s8[4194304]{0:T(1024)(128)(4,1)S(1)}, s32[]{:S(2)}) async-start(s8[27262976]{0:T(1024)(128)(4,1)} %bitcast.4), calls=%async_computation.5 | async-start | bytes 8388608
  31.1 16.0 %slice-start.6 = ((s8[27262976]{0:T(1024)(128)(4,1)}), s8[2097152]{0:T(1024)(128)(4,1)S(1)}, s32[]{:S(2)}) async-start(s8[27262976]{0:T(1024)(128)(4,1)} %bitcast.4), calls=%async_computation.6 | async-start | bytes 4194304
  39.3 7.6 %collective-permute-start.6 = (bf16[8,7552]{1,0:T(8,128)(2,1)S(1)}, bf16[8,7552]{1,0:T(8,128)(2,1)S(1)}, u32[]{:S(2)}, u32[]{:S(2)}) collective-permute-start(bf16[8,7552]{1,0:T(8,128)(2,1)S(1)} %shard_map.51.refs_0_), channel_id=1, source_target_pairs={{0,8},{4,12},{8,0},{12,4},{1,9},{5,13},{9,1},{13,5},{2,10},{6,14},... | collective-permute-start | bytes 362504 | tf_op jit(solution)/shard_map/ppermute | solution.py:274
  39.7 7.3 %collective-permute-start.8 = (bf16[8,7552]{1,0:T(8,128)(2,1)S(1)}, bf16[8,7552]{1,0:T(8,128)(2,1)S(1)}, u32[]{:S(2)}, u32[]{:S(2)}) collective-permute-start(bf16[8,7552]{1,0:T(8,128)(2,1)S(1)} %shard_map.51.refs_0_), channel_id=1, source_target_pairs={{0,4},{4,0},{8,12},{12,8},{1,5},{5,1},{9,13},{13,9},{2,6},{6,2},{1... | collective-permute-start | bytes 362504 | tf_op jit(solution)/shard_map/ppermute | solution.py:274
  47.0 4.9 %collective-permute-start.7 = (bf16[8,7552]{1,0:T(8,128)(2,1)S(1)}, bf16[8,7552]{1,0:T(8,128)(2,1)S(1)}, u32[]{:S(2)}, u32[]{:S(2)}) collective-permute-start(bf16[8,7552]{1,0:T(8,128)(2,1)S(1)} %collective-permute-done.6.refs_2_), channel_id=1, source_target_pairs={{0,4},{4,0},{8,12},{12,8},{1,5},{5,1},{9,13},{13,9},{2,6},{6,2},{1... | collective-permute-start | bytes 362504 | tf_op jit(solution)/shard_map/ppermute | solution.py:274
  53.2 4.0 %collective-permute-start.10 = (bf16[8,2304]{1,0:T(8,128)(2,1)S(1)}, bf16[8,2304]{1,0:T(8,128)(2,1)S(1)}, u32[]{:S(2)}, u32[]{:S(2)}) collective-permute-start(bf16[8,2304]{1,0:T(8,128)(2,1)S(1)} %get-tuple-element.11), channel_id=1, source_target_pairs={{0,2},{1,3},{2,0},{3,1},{4,6},{5,7},{6,4},{7,5},{8,10},{9,11},{10,... | collective-permute-start | bytes 110600 | tf_op jit(solution)/shard_map/ppermute | solution.py:274
  54.7 3.4 %collective-permute-start.11 = (bf16[8,2304]{1,0:T(8,128)(2,1)S(1)}, bf16[8,2304]{1,0:T(8,128)(2,1)S(1)}, u32[]{:S(2)}, u32[]{:S(2)}) collective-permute-start(bf16[8,2304]{1,0:T(8,128)(2,1)S(1)} %get-tuple-element.12), channel_id=1, source_target_pairs={{0,3},{1,2},{2,1},{3,0},{4,7},{5,6},{6,5},{7,4},{8,11},{9,10},{10,... | collective-permute-start | bytes 110600 | tf_op jit(solution)/shard_map/ppermute | solution.py:274
  54.7 3.4 %collective-permute-start.9 = (bf16[8,2304]{1,0:T(8,128)(2,1)S(1)}, bf16[8,2304]{1,0:T(8,128)(2,1)S(1)}, u32[]{:S(2)}, u32[]{:S(2)}) collective-permute-start(bf16[8,2304]{1,0:T(8,128)(2,1)S(1)} %get-tuple-element.10), channel_id=1, source_target_pairs={{0,1},{1,0},{2,3},{3,2},{4,5},{5,4},{6,7},{7,6},{8,9},{9,8},{10,11... | collective-permute-start | bytes 110600 | tf_op jit(solution)/shard_map/ppermute | solution.py:274

commit v8 on v5

--- a/solution.py
+++ b/solution.py
@@ -55,22 +55,29 @@
         out[:, at : at + width] = tail.astype(out.dtype)
 
 
-def start_copies(width, start_ref, gate_ref, up_ref, held, sems):
-    columns = pl.ds(pl.multiple_of(start_ref[0], 128), width)
-    copies = []
-    for k, (row, rows) in enumerate(pieces_of(held.shape[1], STEP)):
-        for w, weight in enumerate((gate_ref, up_ref)):
-            copy = pltpu.make_async_copy(
-                weight.at[pl.ds(row, rows), columns], held.at[w, pl.ds(row, rows)], sems.at[w, k]
-            )
-            copy.start()
-            copies.append((w, row, rows, copy))
-    return copies
+def piece_copy(width, start_ref, weight, held, sems, w, k):
+    return pltpu.make_async_copy(
+        weight.at[pl.ds(k * STEP, STEP), pl.ds(pl.multiple_of(start_ref[0], 128), width)],
+        held.at[w, pl.ds(k * STEP, STEP)],
+        sems.at[w, k],
+    )
+
+
+def start_copies(width, start_ref, weights, held, sems):
+    @pl.loop(0, held.shape[1] // STEP)
+    def _(k):
+        for w, weight in enumerate(weights):
+            piece_copy(width, start_ref, weight, held, sems, w, k).start()
 
 
 def fetch_kernel(width, start_ref, gate_ref, up_ref, held, sems):
-    for _, _, _, copy in start_copies(width, start_ref, gate_ref, up_ref, held, sems):
-        copy.wait()
+    weights = (gate_ref, up_ref)
+    start_copies(width, start_ref, weights, held, sems)
+
+    @pl.loop(0, held.shape[1] // STEP)
+    def _(k):
+        for w, weight in enumerate(weights):
+            piece_copy(width, start_ref, weight, held, sems, w, k).wait()
 
 
 def fetch(gate_weight, up_weight, start, width):
@@ -80,28 +87,25 @@
         out_shape=pltpu.VMEM((2, depth, width), jnp.bfloat16),
         in_specs=[SCALARS, IN_HBM, IN_HBM],
         out_specs=WHOLE,
-        scratch_shapes=[pltpu.SemaphoreType.DMA((2, len(pieces_of(depth, STEP))))],
+        scratch_shapes=[pltpu.SemaphoreType.DMA((2, depth // STEP))],
         compiler_params=params(4),
         cost_estimate=SMALL,
     )(start, in_hbm(gate_weight), in_hbm(up_weight))
 
 
-def multiply(x_ref, held, total, steps):
-    for w, row, rows, copy in steps:
-        if copy is not None:
-            copy.wait()
-        term = jnp.dot(
-            x_ref[:, row : row + rows], held[w, row : row + rows, :], preferred_element_type=jnp.float32
-        )
-        if row == 0:
-            total[w] = term
-        else:
-            total[w] += term
+def accumulate(x_ref, held, total, w, k):
+    rows = pl.ds(pl.multiple_of(k * STEP, STEP), STEP)
+    total[w] += jnp.dot(x_ref[:, rows], held[w, rows, :], preferred_element_type=jnp.float32)
 
 
 def held_kernel(x_ref, held, out, total):
-    parts = pieces_of(x_ref.shape[1], STEP)
-    multiply(x_ref, held, total, [(w, row, rows, None) for w in range(2) for row, rows in parts])
+    total[...] = jnp.zeros_like(total)
+
+    @pl.loop(0, held.shape[1] // STEP)
+    def _(k):
+        for w in range(2):
+            accumulate(x_ref, held, total, w, k)
+
     pack_pair(out, total[0], total[1])
 
 
@@ -119,8 +123,16 @@
 
 
 def stream_kernel(width, start_ref, x_ref, gate_ref, up_ref, _, out, held, total, sems):
-    copies = start_copies(width, start_ref, gate_ref, up_ref, held, sems)
-    multiply(x_ref, held, total, copies)
+    weights = (gate_ref, up_ref)
+    start_copies(width, start_ref, weights, held, sems)
+    total[...] = jnp.zeros_like(total)
+
+    @pl.loop(0, held.shape[1] // STEP)
+    def _(k):
+        for w, weight in enumerate(weights):
+            piece_copy(width, start_ref, weight, held, sems, w, k).wait()
+            accumulate(x_ref, held, total, w, k)
+
     pack_pair(out, total[0], total[1])
 
 
@@ -134,7 +146,7 @@
         scratch_shapes=[
             pltpu.VMEM((2, depth, width), jnp.bfloat16),
             pltpu.VMEM((2, rows, width), jnp.float32),
-            pltpu.SemaphoreType.DMA((2, len(pieces_of(depth, STEP)))),
+            pltpu.SemaphoreType.DMA((2, depth // STEP)),
         ],
         compiler_params=params(18),
         cost_estimate=SMALL,
@@ -207,6 +219,9 @@
     held, outs, (plain, total) = refs[0], refs[1:-2], refs[-2:]
     if first:
         total = outs[0]
+        total[...] = jnp.zeros_like(total)
+    else:
+        total[...] = before[...]
     for b in range(blocks):
         for g in range(rows // 8):
             plain[8 * g : 8 * g + 8, :] = hidden[b][:, g * width : (g + 1) * width].astype(jnp.float32)
@@ -215,16 +230,20 @@
             tail = hidden[b][:, at : at + half].astype(jnp.float32)
             plain[rows - 4 :, :half] = tail[:4]
             plain[rows - 4 :, half:] = tail[4:, : width - half]
-        for row, tall in pieces_of(width, STEP):
-            term = jnp.dot(
-                plain[:, row : row + tall].astype(jnp.bfloat16),
+
+        def accumulate_down(row, tall):
+            total[...] += jnp.dot(
+                plain[:, pl.ds(row, tall)].astype(jnp.bfloat16),
                 held[pl.ds(pl.multiple_of(starts[b] + row, 128), tall), :],
                 preferred_element_type=jnp.float32,
             )
-            if b == 0 and row == 0:
-                total[...] = term if first else before[...] + term
-            else:
-                total[...] += term
+
+        @pl.loop(0, width // STEP)
+        def _(k):
+            accumulate_down(pl.multiple_of(k * STEP, STEP), STEP)
+
+        if width % STEP:
+            accumulate_down(width // STEP * STEP, width % STEP)
     if not first:
         tall = rows // len(outs)
         for r, out in enumerate(outs):

time: 58.3 us -> 61.9 us (1.062)
  Pallas kernels: 32 us -> 36.1 us
    pallas_call x2, Pallas kernels: 5.48 us -> 8.63 us  [down(): pl.pallas_call(functools.partial(down_kernel, before is None, rows, width...]
    pallas_call x1, Pallas kernels: 2.15 us -> 3.15 us  [gate_up_held(): pl.pallas_call(held_kernel, out_shape=jax.ShapeDtypeStruct((8, packed_pai...]
  transfers between devices with their start and end apart: 12 -> 12, of which waited for: 6 -> 5; matrix products, arithmetic and copies ran while one was open for 0% -> 0% of each run, Pallas kernels for 48% -> 49%
where the time goes in v8:
time: 61.9 us; the launch traced here: 61.8 us
  Pallas kernels  36.1 us (58%)
  starting transfers between devices  15.7 us (25%)
  waiting for transfers between devices  9.45 us (15%)
    pallas_call x3, Pallas kernels, gate_up_stream(): pl.pallas_call(functools.partial(stream_kernel, width), out_shape=jax.Sha...  18.4 us
    ppermute x12, starting transfers between devices, swap(): return lax.ppermute(value, axes, [(i, i ^ distance) for i in range(size)])  15.7 us
    ppermute x12, waiting for transfers between devices, swap(): return lax.ppermute(value, axes, [(i, i ^ distance) for i in range(size)])  9.45 us
    pallas_call x2, Pallas kernels, down(): pl.pallas_call(functools.partial(down_kernel, before is None, rows, width...  8.63 us
    pallas_call x1, Pallas kernels, fetch(): pl.pallas_call(functools.partial(fetch_kernel, width), out_shape=pltpu.VM...  5.23 us
    pallas_call x1, Pallas kernels, gate_up_held(): pl.pallas_call(held_kernel, out_shape=jax.ShapeDtypeStruct((8, packed_pai...  3.15 us
  transfers between devices with their start and end apart: 12, of which 5 were waited for; matrix products, arithmetic and copies ran while one was open for 0% of the time, Pallas kernels for 49%

profile of v8, /device:TPU:0, one launch (start us, length us, event | category | flops | bytes accessed | tf_op | source)
XLA Modules:
  0.0 61.8 jit_solution(2666077230071480046)
XLA Ops:
  0.0 0.5 collective-permute-start
  0.5 2.5 %collective-permute-start.1 = (bf16[9,2048]{1,0:T(8,128)(2,1)}, bf16[9,2048]{1,0:T(8,128)(2,1)S(1)}, u32[]{:S(2)}, u32[]{:S(2)}) collective-permute-start(bf16[9,2048]{1,0:T(8,128)(2,1)} %param.4), channel_id=1, source_target_pairs={{0,2},{1,3},{2,0},{3,1},{4,6},{5,7},{6,4},{7,5},{8,10},{9,11},{10,... | collective-permute-start | bytes 110600 | tf_op jit(solution)/shard_map/ppermute | solution.py:297
  2.9 0.1 collective-permute-start.2
  3.1 0.0 copy-start
  3.1 5.2 %shard_map.46.held = bf16[2,2048,1664]{2,1,0:T(8,128)(2,1)S(1)} custom-call(s32[1]{0:T(128)} %bitcast.start_ref.starts, bf16[2048,6656]{1,0:T(8,128)(2,1)} %gate_ref.7, bf16[2048,6656]{1,0:T(8,128)(2,1)} %up_ref.7), custom_call_target="tpu_custom_call" | custom-call | bytes 1048576 | tf_op jit(solution)/shard_map/pallas_call | solution.py:85
  8.3 0.0 collective-permute-done
  8.3 0.0 collective-permute-done.1
  8.3 0.0 collective-permute-done.2
  8.4 0.0 copy-done
  8.4 0.1 pad_maximum_fusion.x_ref
  8.5 3.1 %shard_map.47._ = bf16[8,14976]{1,0:T(8,128)(2,1)S(1)} custom-call(bf16[36,2048]{1,0:T(8,128)(2,1)S(1)} %pad_maximum_fusion.x_ref, bf16[2,2048,1664]{2,1,0:T(8,128)(2,1)S(1)} %shard_map.46.held), custom_call_target="tpu_custom_call" | custom-call | bytes 1048576 | tf_op jit(solution)/shard_map/pallas_call | solution.py:114
  11.6 1.7 %collective-permute-start.3 = (bf16[8,14976]{1,0:T(8,128)(2,1)S(1)}, bf16[8,14976]{1,0:T(8,128)(2,1)S(1)}, u32[]{:S(2)}, u32[]{:S(2)}) collective-permute-start(bf16[8,14976]{1,0:T(8,128)(2,1)S(1)} %shard_map.47._), channel_id=1, source_target_pairs={{0,4},{4,0},{8,12},{12,8},{1,5},{5,1},{9,13},{13,9},{2,6},{6,2},{1... | collective-permute-start | bytes 718856 | tf_op jit(solution)/shard_map/ppermute | solution.py:297
  13.3 5.8 %shard_map.48 = bf16[8,14976]{1,0:T(8,128)(2,1)S(1)} custom-call(s32[1]{0:T(128)} %bitcast.3.start_ref, bf16[36,2048]{1,0:T(8,128)(2,1)S(1)} %pad_maximum_fusion.x_ref, bf16[2048,6656]{1,0:T(8,128)(2,1)} %gate_ref.7, bf16[2048,6656]{1,0:T(8,128)(2,1)} %up_ref.7, bf16[8,14976]{1,0:T(8,128)(2,1)S(1)} %shard_map.47._), custom_call_target="tpu_custom_call" | custom-call | bytes 1048576 | tf_op jit(solution)/shard_map/pallas_call | solution.py:141
  19.1 0.5 collective-permute-done.3
  19.6 0.1 add_convert_fusion._
  19.7 2.8 %collective-permute-start.4 = (bf16[8,14976]{1,0:T(8,128)(2,1)S(1)}, bf16[8,14976]{1,0:T(8,128)(2,1)S(1)}, u32[]{:S(2)}, u32[]{:S(2)}) collective-permute-start(bf16[8,14976]{1,0:T(8,128)(2,1)S(1)} %add_convert_fusion._), channel_id=1, source_target_pairs={{0,8},{4,12},{8,0},{12,4},{1,9},{5,13},{9,1},{13,5},{2,10},{6,14},... | collective-permute-start | bytes 718856 | tf_op jit(solution)/shard_map/ppermute | solution.py:297
  22.5 0.0 slice-start
  22.5 0.0 slice-start.1
  22.5 0.0 slice-start.2
  22.5 0.0 slice-start.3
  22.5 5.9 %shard_map.49._ = bf16[8,14976]{1,0:T(8,128)(2,1)S(1)} custom-call(s32[1]{0:T(128)} %bitcast.2.start_ref, bf16[36,2048]{1,0:T(8,128)(2,1)S(1)} %pad_maximum_fusion.x_ref, bf16[2048,6656]{1,0:T(8,128)(2,1)} %gate_ref.7, bf16[2048,6656]{1,0:T(8,128)(2,1)} %up_ref.7, bf16[8,14976]{1,0:T(8,128)(2,1)S(1)} %add_convert_fusion._), custom_call_target="tpu_custom_call" | custom-call | bytes 1048576 | tf_op jit(solution)/shard_map/pallas_call | solution.py:141
  28.5 1.7 %collective-permute-start.5 = (bf16[8,14976]{1,0:T(8,128)(2,1)S(1)}, bf16[8,14976]{1,0:T(8,128)(2,1)S(1)}, u32[]{:S(2)}, u32[]{:S(2)}) collective-permute-start(bf16[8,14976]{1,0:T(8,128)(2,1)S(1)} %shard_map.49._), channel_id=1, source_target_pairs={{0,4},{4,0},{8,12},{12,8},{1,5},{5,1},{9,13},{13,9},{2,6},{6,2},{1... | collective-permute-start | bytes 718856 | tf_op jit(solution)/shard_map/ppermute | solution.py:297
  30.2 0.0 slice-start.4
  30.2 0.0 slice-start.5
  30.2 0.0 slice-start.6
  30.2 6.6 %shard_map.50 = bf16[8,14976]{1,0:T(8,128)(2,1)S(1)} custom-call(s32[1]{0:T(128)} %bitcast.1.start_ref, bf16[36,2048]{1,0:T(8,128)(2,1)S(1)} %pad_maximum_fusion.x_ref, bf16[2048,6656]{1,0:T(8,128)(2,1)} %gate_ref.7, bf16[2048,6656]{1,0:T(8,128)(2,1)} %up_ref.7, bf16[8,14976]{1,0:T(8,128)(2,1)S(1)} %shard_map.49._), custom_call_target="tpu_custom_call" | custom-call | bytes 1048576 | tf_op jit(solution)/shard_map/pallas_call | solution.py:141
  36.8 0.0 collective-permute-done.4
  36.8 0.1 convert_add_fusion.summed
  36.9 1.4 %collective-permute-done.5.near = bf16[8,14976]{1,0:T(8,128)(2,1)S(1)} collective-permute-done((bf16[8,14976]{1,0:T(8,128)(2,1)S(1)}, bf16[8,14976]{1,0:T(8,128)(2,1)S(1)}, u32[]{:S(2)}, u32[]{:S(2)}) %collective-permute-start.5) | collective-permute-done | bytes 239648 | tf_op jit(solution)/shard_map/ppermute | solution.py:297
  38.2 0.1 shard_map.51.refs_0_
  38.3 1.7 %collective-permute-start.6 = (bf16[8,7552]{1,0:T(8,128)(2,1)S(1)}, bf16[8,7552]{1,0:T(8,128)(2,1)S(1)}, u32[]{:S(2)}, u32[]{:S(2)}) collective-permute-start(bf16[8,7552]{1,0:T(8,128)(2,1)S(1)} %shard_map.51.refs_0_), channel_id=1, source_target_pairs={{0,8},{4,12},{8,0},{12,4},{1,9},{5,13},{9,1},{13,5},{2,10},{6,14},... | collective-permute-start | bytes 362504 | tf_op jit(solution)/shard_map/ppermute | solution.py:297
  40.0 2.5 %collective-permute-start.8 = (bf16[8,7552]{1,0:T(8,128)(2,1)S(1)}, bf16[8,7552]{1,0:T(8,128)(2,1)S(1)}, u32[]{:S(2)}, u32[]{:S(2)}) collective-permute-start(bf16[8,7552]{1,0:T(8,128)(2,1)S(1)} %shard_map.51.refs_0_), channel_id=1, source_target_pairs={{0,4},{4,0},{8,12},{12,8},{1,5},{5,1},{9,13},{13,9},{2,6},{6,2},{1... | collective-permute-start | bytes 362504 | tf_op jit(solution)/shard_map/ppermute | solution.py:297
  42.5 4.7 %collective-permute-done.6.refs_2_ = bf16[8,7552]{1,0:T(8,128)(2,1)S(1)} collective-permute-done((bf16[8,7552]{1,0:T(8,128)(2,1)S(1)}, bf16[8,7552]{1,0:T(8,128)(2,1)S(1)}, u32[]{:S(2)}, u32[]{:S(2)}) %collective-permute-start.6) | collective-permute-done | bytes 120864 | tf_op jit(solution)/shard_map/ppermute | solution.py:297
  47.2 0.0 collective-permute-start.7
  47.2 0.1 pad_add_fusion.starts
  47.3 0.0 collective-permute-done.8.refs_1_
  47.3 0.0 slice-done
  47.3 0.0 slice-done.1
  47.3 0.0 slice-done.2
  47.3 0.0 slice-done.3
  47.3 0.0 slice-done.4
  47.3 0.0 slice-done.5
  47.3 0.0 slice-done.6
  47.3 6.6 %shard_map.52.refs_1_ = f32[36,2048]{1,0:T(8,128)S(1)} custom-call(s32[3]{0:T(128)S(1)} %pad_add_fusion.starts, bf16[8,7552]{1,0:T(8,128)(2,1)S(1)} %shard_map.51.refs_0_, bf16[8,7552]{1,0:T(8,128)(2,1)S(1)} %collective-permute-done.8.refs_1_, bf16[8,7552]{1,0:T(8,128)(2,1)S(1)} %collective-permute-done.6.refs_2_, bf16[6656,2048]{1,0:T(8,128)(2,1)S(1)} %bitcast.5), custom_call_target="tpu_custom_call" | custom-call | bytes 1048576 | tf_op jit(solution)/shard_map/pallas_call | solution.py:261
  53.9 0.0 collective-permute-done.7.refs_0_
  53.9 2.1 %shard_map.53 = (f32[8,2304]{1,0:T(8,128)S(1)}, bf16[8,2304]{1,0:T(8,128)(2,1)S(1)}, bf16[8,2304]{1,0:T(8,128)(2,1)S(1)}, bf16[8,2304]{1,0:T(8,128)(2,1)S(1)}) custom-call(s32[1]{0:T(128)} %bitcast.start_ref.starts, bf16[8,7552]{1,0:T(8,128)(2,1)S(1)} %collective-permute-done.7.refs_0_, f32[36,2048]{1,0:T(8,128)S(1)} %shard_map.52.refs_1_, ...), custom_call_target="tpu_custom_call" | custom-call | bytes 1048576 | tf_op jit(solution)/shard_map/pallas_call | solution.py:261
  56.0 1.7 %collective-permute-start.10 = (bf16[8,2304]{1,0:T(8,128)(2,1)S(1)}, bf16[8,2304]{1,0:T(8,128)(2,1)S(1)}, u32[]{:S(2)}, u32[]{:S(2)}) collective-permute-start(bf16[8,2304]{1,0:T(8,128)(2,1)S(1)} %get-tuple-element.11), channel_id=1, source_target_pairs={{0,2},{1,3},{2,0},{3,1},{4,6},{5,7},{6,4},{7,5},{8,10},{9,11},{10,... | collective-permute-start | bytes 110600 | tf_op jit(solution)/shard_map/ppermute | solution.py:297
  57.7 0.0 collective-permute-start.11
  57.7 0.5 collective-permute-start.9
  58.2 1.8 %collective-permute-done.10.refs_2_ = bf16[8,2304]{1,0:T(8,128)(2,1)S(1)} collective-permute-done((bf16[8,2304]{1,0:T(8,128)(2,1)S(1)}, bf16[8,2304]{1,0:T(8,128)(2,1)S(1)}, u32[]{:S(2)}, u32[]{:S(2)}) %collective-permute-start.10) | collective-permute-done | bytes 36896 | tf_op jit(solution)/shard_map/ppermute | solution.py:297
  60.0 1.1 %collective-permute-done.11.refs_3_ = bf16[8,2304]{1,0:T(8,128)(2,1)S(1)} collective-permute-done((bf16[8,2304]{1,0:T(8,128)(2,1)S(1)}, bf16[8,2304]{1,0:T(8,128)(2,1)S(1)}, u32[]{:S(2)}, u32[]{:S(2)}) %collective-permute-start.11) | collective-permute-done | bytes 36896 | tf_op jit(solution)/shard_map/ppermute | solution.py:297
  61.1 0.0 collective-permute-done.9.refs_1_
  61.1 0.7 %shard_map.54 = bf16[9,2048]{1,0:T(8,128)(2,1)} custom-call(f32[8,2304]{1,0:T(8,128)S(1)} %get-tuple-element.9.refs_0_, bf16[8,2304]{1,0:T(8,128)(2,1)S(1)} %collective-permute-done.9.refs_1_, bf16[8,2304]{1,0:T(8,128)(2,1)S(1)} %collective-permute-done.10.refs_2_, bf16[8,2304]{1,0:T(8,128)(2,1)S(1)} %collective-permute-done.11.refs_3_), custom_call_target="tpu_custom_call" | custom-call | bytes 1048576 | tf_op jit(solution)/shard_map/pallas_call | solution.py:285
  (1 shorter events, 0.0 us)
Async XLA Ops:
  0.0 8.3 %collective-permute-start = (bf16[9,2048]{1,0:T(8,128)(2,1)}, bf16[9,2048]{1,0:T(8,128)(2,1)S(1)}, u32[]{:S(2)}, u32[]{:S(2)}) collective-permute-start(bf16[9,2048]{1,0:T(8,128)(2,1)} %param.4), channel_id=1, source_target_pairs={{0,1},{1,0},{2,3},{3,2},{4,5},{5,4},{6,7},{7,6},{8,9},{9,8},{10,11... | collective-permute-start | bytes 110600 | tf_op jit(solution)/shard_map/ppermute | solution.py:297
  0.5 7.9 %collective-permute-start.1 = (bf16[9,2048]{1,0:T(8,128)(2,1)}, bf16[9,2048]{1,0:T(8,128)(2,1)S(1)}, u32[]{:S(2)}, u32[]{:S(2)}) collective-permute-start(bf16[9,2048]{1,0:T(8,128)(2,1)} %param.4), channel_id=1, source_target_pairs={{0,2},{1,3},{2,0},{3,1},{4,6},{5,7},{6,4},{7,5},{8,10},{9,11},{10,... | collective-permute-start | bytes 110600 | tf_op jit(solution)/shard_map/ppermute | solution.py:297
  2.9 5.4 %collective-permute-start.2 = (bf16[9,2048]{1,0:T(8,128)(2,1)}, bf16[9,2048]{1,0:T(8,128)(2,1)S(1)}, u32[]{:S(2)}, u32[]{:S(2)}) collective-permute-start(bf16[9,2048]{1,0:T(8,128)(2,1)} %param.4), channel_id=1, source_target_pairs={{0,3},{1,2},{2,1},{3,0},{4,7},{5,6},{6,5},{7,4},{8,11},{9,10},{10,... | collective-permute-start | bytes 110600 | tf_op jit(solution)/shard_map/ppermute | solution.py:297
  3.1 5.3 %copy-start = (bf16[9,2048]{1,0:T(8,128)(2,1)S(1)}, bf16[9,2048]{1,0:T(8,128)(2,1)}, u32[]{:S(2)}) copy-start(bf16[9,2048]{1,0:T(8,128)(2,1)} %param.4) | copy-start | bytes 110596
  11.6 8.0 %collective-permute-start.3 = (bf16[8,14976]{1,0:T(8,128)(2,1)S(1)}, bf16[8,14976]{1,0:T(8,128)(2,1)S(1)}, u32[]{:S(2)}, u32[]{:S(2)}) collective-permute-start(bf16[8,14976]{1,0:T(8,128)(2,1)S(1)} %shard_map.47._), channel_id=1, source_target_pairs={{0,4},{4,0},{8,12},{12,8},{1,5},{5,1},{9,13},{13,9},{2,6},{6,2},{1... | collective-permute-start | bytes 718856 | tf_op jit(solution)/shard_map/ppermute | solution.py:297
  19.7 17.1 %collective-permute-start.4 = (bf16[8,14976]{1,0:T(8,128)(2,1)S(1)}, bf16[8,14976]{1,0:T(8,128)(2,1)S(1)}, u32[]{:S(2)}, u32[]{:S(2)}) collective-permute-start(bf16[8,14976]{1,0:T(8,128)(2,1)S(1)} %add_convert_fusion._), channel_id=1, source_target_pairs={{0,8},{4,12},{8,0},{12,4},{1,9},{5,13},{9,1},{13,5},{2,10},{6,14},... | collective-permute-start | bytes 718856 | tf_op jit(solution)/shard_map/ppermute | solution.py:297
  22.5 24.8 %slice-start = ((s8[27262976]{0:T(1024)(128)(4,1)}), s8[4194304]{0:T(1024)(128)(4,1)S(1)}, s32[]{:S(2)}) async-start(s8[27262976]{0:T(1024)(128)(4,1)} %bitcast.4), calls=%async_computation | async-start | bytes 8388608
  22.5 24.8 %slice-start.1 = ((s8[27262976]{0:T(1024)(128)(4,1)}), s8[4194304]{0:T(1024)(128)(4,1)S(1)}, s32[]{:S(2)}) async-start(s8[27262976]{0:T(1024)(128)(4,1)} %bitcast.4), calls=%async_computation.1 | async-start | bytes 8388608
  22.5 24.8 %slice-start.2 = ((s8[27262976]{0:T(1024)(128)(4,1)}), s8[4194304]{0:T(1024)(128)(4,1)S(1)}, s32[]{:S(2)}) async-start(s8[27262976]{0:T(1024)(128)(4,1)} %bitcast.4), calls=%async_computation.2 | async-start | bytes 8388608
  22.5 24.8 %slice-start.3 = ((s8[27262976]{0:T(1024)(128)(4,1)}), s8[4194304]{0:T(1024)(128)(4,1)S(1)}, s32[]{:S(2)}) async-start(s8[27262976]{0:T(1024)(128)(4,1)} %bitcast.4), calls=%async_computation.3 | async-start | bytes 8388608
  28.5 9.8 %collective-permute-start.5 = (bf16[8,14976]{1,0:T(8,128)(2,1)S(1)}, bf16[8,14976]{1,0:T(8,128)(2,1)S(1)}, u32[]{:S(2)}, u32[]{:S(2)}) collective-permute-start(bf16[8,14976]{1,0:T(8,128)(2,1)S(1)} %shard_map.49._), channel_id=1, source_target_pairs={{0,4},{4,0},{8,12},{12,8},{1,5},{5,1},{9,13},{13,9},{2,6},{6,2},{1... | collective-permute-start | bytes 718856 | tf_op jit(solution)/shard_map/ppermute | solution.py:297
  30.2 17.1 %slice-start.4 = ((s8[27262976]{0:T(1024)(128)(4,1)}), s8[4194304]{0:T(1024)(128)(4,1)S(1)}, s32[]{:S(2)}) async-start(s8[27262976]{0:T(1024)(128)(4,1)} %bitcast.4), calls=%async_computation.4 | async-start | bytes 8388608
  30.2 17.1 %slice-start.5 = ((s8[27262976]{0:T(1024)(128)(4,1)}), s8[4194304]{0:T(1024)(128)(4,1)S(1)}, s32[]{:S(2)}) async-start(s8[27262976]{0:T(1024)(128)(4,1)} %bitcast.4), calls=%async_computation.5 | async-start | bytes 8388608
  30.2 17.1 %slice-start.6 = ((s8[27262976]{0:T(1024)(128)(4,1)}), s8[2097152]{0:T(1024)(128)(4,1)S(1)}, s32[]{:S(2)}) async-start(s8[27262976]{0:T(1024)(128)(4,1)} %bitcast.4), calls=%async_computation.6 | async-start | bytes 4194304
  38.3 8.9 %collective-permute-start.6 = (bf16[8,7552]{1,0:T(8,128)(2,1)S(1)}, bf16[8,7552]{1,0:T(8,128)(2,1)S(1)}, u32[]{:S(2)}, u32[]{:S(2)}) collective-permute-start(bf16[8,7552]{1,0:T(8,128)(2,1)S(1)} %shard_map.51.refs_0_), channel_id=1, source_target_pairs={{0,8},{4,12},{8,0},{12,4},{1,9},{5,13},{9,1},{13,5},{2,10},{6,14},... | collective-permute-start | bytes 362504 | tf_op jit(solution)/shard_map/ppermute | solution.py:297
  40.0 7.3 %collective-permute-start.8 = (bf16[8,7552]{1,0:T(8,128)(2,1)S(1)}, bf16[8,7552]{1,0:T(8,128)(2,1)S(1)}, u32[]{:S(2)}, u32[]{:S(2)}) collective-permute-start(bf16[8,7552]{1,0:T(8,128)(2,1)S(1)} %shard_map.51.refs_0_), channel_id=1, source_target_pairs={{0,4},{4,0},{8,12},{12,8},{1,5},{5,1},{9,13},{13,9},{2,6},{6,2},{1... | collective-permute-start | bytes 362504 | tf_op jit(solution)/shard_map/ppermute | solution.py:297
  47.2 6.7 %collective-permute-start.7 = (bf16[8,7552]{1,0:T(8,128)(2,1)S(1)}, bf16[8,7552]{1,0:T(8,128)(2,1)S(1)}, u32[]{:S(2)}, u32[]{:S(2)}) collective-permute-start(bf16[8,7552]{1,0:T(8,128)(2,1)S(1)} %collective-permute-done.6.refs_2_), channel_id=1, source_target_pairs={{0,4},{4,0},{8,12},{12,8},{1,5},{5,1},{9,13},{13,9},{2,6},{6,2},{1... | collective-permute-start | bytes 362504 | tf_op jit(solution)/shard_map/ppermute | solution.py:297
  56.0 4.0 %collective-permute-start.10 = (bf16[8,2304]{1,0:T(8,128)(2,1)S(1)}, bf16[8,2304]{1,0:T(8,128)(2,1)S(1)}, u32[]{:S(2)}, u32[]{:S(2)}) collective-permute-start(bf16[8,2304]{1,0:T(8,128)(2,1)S(1)} %get-tuple-element.11), channel_id=1, source_target_pairs={{0,2},{1,3},{2,0},{3,1},{4,6},{5,7},{6,4},{7,5},{8,10},{9,11},{10,... | collective-permute-start | bytes 110600 | tf_op jit(solution)/shard_map/ppermute | solution.py:297
  57.7 3.4 %collective-permute-start.11 = (bf16[8,2304]{1,0:T(8,128)(2,1)S(1)}, bf16[8,2304]{1,0:T(8,128)(2,1)S(1)}, u32[]{:S(2)}, u32[]{:S(2)}) collective-permute-start(bf16[8,2304]{1,0:T(8,128)(2,1)S(1)} %get-tuple-element.12), channel_id=1, source_target_pairs={{0,3},{1,2},{2,1},{3,0},{4,7},{5,6},{6,5},{7,4},{8,11},{9,10},{10,... | collective-permute-start | bytes 110600 | tf_op jit(solution)/shard_map/ppermute | solution.py:297
  57.7 3.4 %collective-permute-start.9 = (bf16[8,2304]{1,0:T(8,128)(2,1)S(1)}, bf16[8,2304]{1,0:T(8,128)(2,1)S(1)}, u32[]{:S(2)}, u32[]{:S(2)}) collective-permute-start(bf16[8,2304]{1,0:T(8,128)(2,1)S(1)} %get-tuple-element.10), channel_id=1, source_target_pairs={{0,1},{1,0},{2,3},{3,2},{4,5},{5,4},{6,7},{7,6},{8,9},{9,8},{10,11... | collective-permute-start | bytes 110600 | tf_op jit(solution)/shard_map/ppermute | solution.py:297

commit v9 on v5

--- a/solution.py
+++ b/solution.py
@@ -55,8 +55,8 @@
         out[:, at : at + width] = tail.astype(out.dtype)
 
 
-def start_copies(width, start_ref, gate_ref, up_ref, held, sems):
-    columns = pl.ds(pl.multiple_of(start_ref[0], 128), width)
+def start_copies(width, starts, b, gate_ref, up_ref, held, sems):
+    columns = pl.ds(pl.multiple_of(starts[b], 128), width)
     copies = []
     for k, (row, rows) in enumerate(pieces_of(held.shape[1], STEP)):
         for w, weight in enumerate((gate_ref, up_ref)):
@@ -69,7 +69,7 @@
 
 
 def fetch_kernel(width, start_ref, gate_ref, up_ref, held, sems):
-    for _, _, _, copy in start_copies(width, start_ref, gate_ref, up_ref, held, sems):
+    for _, _, _, copy in start_copies(width, start_ref, 0, gate_ref, up_ref, held, sems):
         copy.wait()
 
 
@@ -118,27 +118,38 @@
     )(features, in_vmem(held))
 
 
-def stream_kernel(width, start_ref, x_ref, gate_ref, up_ref, _, out, held, total, sems):
-    copies = start_copies(width, start_ref, gate_ref, up_ref, held, sems)
-    multiply(x_ref, held, total, copies)
-    pack_pair(out, total[0], total[1])
-
-
-def gate_up_stream(features, gate_weight, up_weight, start, width, after):
+def stream_kernel(widths, starts, x_ref, gate_ref, up_ref, _, *refs):
+    outs, refs = refs[: len(widths)], refs[len(widths) :]
+    blocks = []
+    for b, width in enumerate(widths):
+        held, total, sems = refs[3 * b : 3 * b + 3]
+        copies = start_copies(width, starts, b, gate_ref, up_ref, held, sems)
+        blocks.append((outs[b], held, total, copies))
+    for out, held, total, copies in blocks:
+        multiply(x_ref, held, total, copies)
+        pack_pair(out, total[0], total[1])
+
+
+def gate_up_stream(features, gate_weight, up_weight, starts, widths, after):
     rows, depth = features.shape
-    return pl.pallas_call(
-        functools.partial(stream_kernel, width),
-        out_shape=jax.ShapeDtypeStruct((8, packed_pair_width(rows, width)), jnp.bfloat16),
-        in_specs=[SCALARS, WHOLE, IN_HBM, IN_HBM, ANY],
-        out_specs=WHOLE,
-        scratch_shapes=[
+    scratch = []
+    for width in widths:
+        scratch += [
             pltpu.VMEM((2, depth, width), jnp.bfloat16),
             pltpu.VMEM((2, rows, width), jnp.float32),
             pltpu.SemaphoreType.DMA((2, len(pieces_of(depth, STEP)))),
+        ]
+    return pl.pallas_call(
+        functools.partial(stream_kernel, widths),
+        out_shape=[
+            jax.ShapeDtypeStruct((8, packed_pair_width(rows, w)), jnp.bfloat16) for w in widths
         ],
-        compiler_params=params(18),
-        cost_estimate=SMALL,
-    )(start, features, in_hbm(gate_weight), in_hbm(up_weight), after)
+        in_specs=[SCALARS, WHOLE, IN_HBM, IN_HBM, ANY],
+        out_specs=[WHOLE] * len(widths),
+        scratch_shapes=scratch,
+        compiler_params=params(5 + -(-depth * sum(widths) * 4 // MIB)),
+        cost_estimate=SMALL,
+    )(starts, features, in_hbm(gate_weight), in_hbm(up_weight), after)
 
 
 def hidden_tail(rows, width):
@@ -146,15 +157,25 @@
     return half if rows % 8 else 0
 
 
-def activate_kernel(rows, width, summed, near, out):
-    def pair(at):
-        return summed[:, at : at + width] + near[:, at : at + width].astype(jnp.float32)
+def activate_kernel(rows, widths, summed, *refs):
+    near, out = refs[:-1], refs[-1]
+    width = sum(widths)
+
+    def pair(w, g):
+        column = (2 * g + w) * width
+        parts = []
+        for part, wide in zip(near, widths):
+            at = (2 * g + w) * wide
+            parts.append(
+                summed[:, column : column + wide] + part[:, at : at + wide].astype(jnp.float32)
+            )
+            column += wide
+        return jnp.concatenate(parts, axis=1)
 
     for g in range(rows // 8):
-        value = activate(pair(2 * g * width), pair((2 * g + 1) * width))
-        out[:, g * width : (g + 1) * width] = value
+        out[:, g * width : (g + 1) * width] = activate(pair(0, g), pair(1, g))
     if rows % 8:
-        last = pair((rows // 8) * 2 * width)
+        last = pair(0, rows // 8)
         value = activate(last[:4], last[4:]).astype(jnp.float32)
         half = hidden_tail(rows, width)
         right = jnp.concatenate([value[:, half:], jnp.zeros((4, 2 * half - width), jnp.float32)], axis=1)
@@ -162,17 +183,18 @@
         out[:, at : at + half] = jnp.concatenate([value[:, :half], right], axis=0).astype(out.dtype)
 
 
-def activate_packed(summed, near, rows, width):
-    return pl.pallas_call(
-        functools.partial(activate_kernel, rows, width),
+def activate_packed(summed, near, rows, widths):
+    width = sum(widths)
+    return pl.pallas_call(
+        functools.partial(activate_kernel, rows, widths),
         out_shape=jax.ShapeDtypeStruct(
             (8, (rows // 8) * width + hidden_tail(rows, width)), jnp.bfloat16
         ),
-        in_specs=[WHOLE] * 2,
+        in_specs=[WHOLE] * (1 + len(near)),
         out_specs=WHOLE,
         compiler_params=params(8),
         cost_estimate=SMALL,
-    )(summed, near)
+    )(summed, *near)
 
 
 def pack_rows(out, value):
@@ -297,19 +319,21 @@
     )
     rows = features.shape[0]
 
-    def block_for(d, after):
-        return gate_up_stream(features, gate_weight, up_weight, starts_of(d), width, after)
-
+    def blocks_for(starts, widths, after):
+        return gate_up_stream(features, gate_weight, up_weight, starts, widths, after)
+
+    ahead = width // 128 * 2 // 5 * 128
     relayed = gate_up_held(features, held)
     arrived = swap(relayed, "gx", n_gx, 1)
-    across = block_for(2, relayed)
+    across, beside = blocks_for(starts_of(2, 1), (width, ahead), relayed)
     across = lax.optimization_barrier(add(across, arrived).astype(jnp.bfloat16))
     far = swap(across, "gx", n_gx, 2)
-    beside = block_for(1, across)
-    near = swap(beside, "gx", n_gx, 1)
-    own = block_for(0, beside)
+    near = [swap(beside, "gx", n_gx, 1)]
+    (beside,) = blocks_for(starts_of(1) + ahead, (width - ahead,), across)
+    near.append(swap(beside, "gx", n_gx, 1))
+    (own,) = blocks_for(starts_of(0), (width,), beside)
     summed = lax.optimization_barrier(add(own, far))
-    hidden = activate_packed(summed, near, rows, width)
+    hidden = activate_packed(summed, near, rows, (ahead, width - ahead))
 
     opposite = swap(hidden, "gx", n_gx, 2)
     first = [hidden, swap(hidden, "gx", n_gx, 1), opposite]

time: 58.3 us -> 60.1 us (1.031)
  Pallas kernels: 32 us -> 35.4 us
  starting transfers between devices: 15.7 us -> 13.7 us
    pallas_call x4, Pallas kernels: 18.5 us -> 21.9 us  [the longest x3 21.8 us: gate_up_stream(): pl.pallas_call(functools.partial(stream_kernel, widths), out_shape=[jax.S...]
    ppermute x12 -> x13, starting transfers between devices: 15.7 us -> 13.7 us  [swap(): return lax.ppermute(value, axes, [(i, i ^ distance) for i in range(size)])]
    ppermute x12 -> x13, waiting for transfers between devices: 9.94 us -> 10.3 us  [swap(): return lax.ppermute(value, axes, [(i, i ^ distance) for i in range(size)])]
  transfers between devices with their start and end apart: 12 -> 13, of which waited for: 6 -> 5; matrix products, arithmetic and copies ran while one was open for 0% -> 0% of each run, Pallas kernels for 48% -> 52%
where the time goes in v9:
time: 60.1 us; the launch traced here: 60 us
  Pallas kernels  35.4 us (59%)
  starting transfers between devices  13.7 us (23%)
  waiting for transfers between devices  10.3 us (17%)
    pallas_call x3, Pallas kernels, gate_up_stream(): pl.pallas_call(functools.partial(stream_kernel, widths), out_shape=[jax.S...  21.8 us
    ppermute x13, starting transfers between devices, swap(): return lax.ppermute(value, axes, [(i, i ^ distance) for i in range(size)])  13.7 us
    ppermute x13, waiting for transfers between devices, swap(): return lax.ppermute(value, axes, [(i, i ^ distance) for i in range(size)])  10.3 us
    pallas_call x2, Pallas kernels, down(): pl.pallas_call(functools.partial(down_kernel, before is None, rows, width...  5.48 us
    pallas_call x1, Pallas kernels, fetch(): pl.pallas_call(functools.partial(fetch_kernel, width), out_shape=pltpu.VM...  5.23 us
    pallas_call x1, Pallas kernels, gate_up_held(): pl.pallas_call(held_kernel, out_shape=jax.ShapeDtypeStruct((8, packed_pai...  2.15 us
  transfers between devices with their start and end apart: 13, of which 5 were waited for; matrix products, arithmetic and copies ran while one was open for 0% of the time, Pallas kernels for 52%

profile of v9, /device:TPU:0, one launch (start us, length us, event | category | flops | bytes accessed | tf_op | source)
XLA Modules:
  0.0 60.0 jit_solution(5138633868607692440)
XLA Ops:
  0.0 2.4 %collective-permute-start.2 = (bf16[9,2048]{1,0:T(8,128)(2,1)}, bf16[9,2048]{1,0:T(8,128)(2,1)S(1)}, u32[]{:S(2)}, u32[]{:S(2)}) collective-permute-start(bf16[9,2048]{1,0:T(8,128)(2,1)} %param.4), channel_id=1, source_target_pairs={{0,3},{1,2},{2,1},{3,0},{4,7},{5,6},{6,5},{7,4},{8,11},{9,10},{10,... | collective-permute-start | bytes 110600 | tf_op jit(solution)/shard_map/ppermute | solution.py:300
  2.4 0.6 collective-permute-start.1
  3.0 0.1 collective-permute-start
  3.1 0.0 copy-start
  3.1 5.2 %shard_map.46.held = bf16[2,2048,1664]{2,1,0:T(8,128)(2,1)S(1)} custom-call(s32[1]{0:T(128)} %bitcast.start_ref.starts, bf16[2048,6656]{1,0:T(8,128)(2,1)} %gate_ref.7, bf16[2048,6656]{1,0:T(8,128)(2,1)} %up_ref.7), custom_call_target="tpu_custom_call" | custom-call | bytes 1048576 | tf_op jit(solution)/shard_map/pallas_call | solution.py:78
  8.3 0.0 collective-permute-done.2
  8.3 0.0 collective-permute-done.1
  8.3 0.0 collective-permute-done
  8.3 0.0 copy-done
  8.3 0.1 pad_maximum_fusion.x_ref
  8.4 2.2 %shard_map.47._ = bf16[8,14976]{1,0:T(8,128)(2,1)S(1)} custom-call(bf16[36,2048]{1,0:T(8,128)(2,1)S(1)} %pad_maximum_fusion.x_ref, bf16[2,2048,1664]{2,1,0:T(8,128)(2,1)S(1)} %shard_map.46.held), custom_call_target="tpu_custom_call" | custom-call | bytes 1048576 | tf_op jit(solution)/shard_map/pallas_call | solution.py:110
  10.6 1.7 %collective-permute-start.3 = (bf16[8,14976]{1,0:T(8,128)(2,1)S(1)}, bf16[8,14976]{1,0:T(8,128)(2,1)S(1)}, u32[]{:S(2)}, u32[]{:S(2)}) collective-permute-start(bf16[8,14976]{1,0:T(8,128)(2,1)S(1)} %shard_map.47._), channel_id=1, source_target_pairs={{0,4},{4,0},{8,12},{12,8},{1,5},{5,1},{9,13},{13,9},{2,6},{6,2},{1... | collective-permute-start | bytes 718856 | tf_op jit(solution)/shard_map/ppermute | solution.py:300
  12.3 0.1 pad_add_fusion.starts
  12.4 10.5 %shard_map.48 = (bf16[8,14976]{1,0:T(8,128)(2,1)S(1)}, bf16[8,5760]{1,0:T(8,128)(2,1)S(1)}) custom-call(s32[2]{0:T(128)S(1)} %pad_add_fusion.starts, bf16[36,2048]{1,0:T(8,128)(2,1)S(1)} %pad_maximum_fusion.x_ref, bf16[2048,6656]{1,0:T(8,128)(2,1)} %gate_ref.7, bf16[2048,6656]{1,0:T(8,128)(2,1)} %up_ref.7, bf16[8,14976]{1,0:T(8,128)(2,1)S(1)} %shard_map.47._), custom_call_target="tpu_custom_call" | custom-call | bytes 1048576 | tf_op jit(solution)/shard_map/pallas_call | solution.py:142
  23.0 0.0 collective-permute-done.3
  23.0 0.1 add_convert_fusion._
  23.0 2.7 %collective-permute-start.4 = (bf16[8,14976]{1,0:T(8,128)(2,1)S(1)}, bf16[8,14976]{1,0:T(8,128)(2,1)S(1)}, u32[]{:S(2)}, u32[]{:S(2)}) collective-permute-start(bf16[8,14976]{1,0:T(8,128)(2,1)S(1)} %add_convert_fusion._), channel_id=1, source_target_pairs={{0,8},{4,12},{8,0},{12,4},{1,9},{5,13},{9,1},{13,5},{2,10},{6,14},... | collective-permute-start | bytes 718856 | tf_op jit(solution)/shard_map/ppermute | solution.py:300
  25.8 0.4 collective-permute-start.5
  26.2 0.0 slice-start
  26.2 0.0 slice-start.1
  26.2 0.0 slice-start.2
  26.2 0.0 slice-start.3
  26.2 4.7 %shard_map.49._ = bf16[8,9216]{1,0:T(8,128)(2,1)S(1)} custom-call(s32[1]{0:T(128)S(6)} %add.9.starts, bf16[36,2048]{1,0:T(8,128)(2,1)S(1)} %pad_maximum_fusion.x_ref, bf16[2048,6656]{1,0:T(8,128)(2,1)} %gate_ref.7, bf16[2048,6656]{1,0:T(8,128)(2,1)} %up_ref.7, bf16[8,14976]{1,0:T(8,128)(2,1)S(1)} %add_convert_fusion._), custom_call_target="tpu_custom_call" | custom-call | bytes 1048576 | tf_op jit(solution)/shard_map/pallas_call | solution.py:142
  30.9 1.7 %collective-permute-start.6 = (bf16[8,9216]{1,0:T(8,128)(2,1)S(1)}, bf16[8,9216]{1,0:T(8,128)(2,1)S(1)}, u32[]{:S(2)}, u32[]{:S(2)}) collective-permute-start(bf16[8,9216]{1,0:T(8,128)(2,1)S(1)} %shard_map.49._), channel_id=1, source_target_pairs={{0,4},{4,0},{8,12},{12,8},{1,5},{5,1},{9,13},{13,9},{2,6},{6,2},{1... | collective-permute-start | bytes 442376 | tf_op jit(solution)/shard_map/ppermute | solution.py:300
  32.5 0.0 slice-start.4
  32.5 0.0 slice-start.5
  32.5 0.0 slice-start.6
  32.5 6.6 %shard_map.50 = bf16[8,14976]{1,0:T(8,128)(2,1)S(1)} custom-call(s32[1]{0:T(128)} %bitcast.1.starts, bf16[36,2048]{1,0:T(8,128)(2,1)S(1)} %pad_maximum_fusion.x_ref, bf16[2048,6656]{1,0:T(8,128)(2,1)} %gate_ref.7, bf16[2048,6656]{1,0:T(8,128)(2,1)} %up_ref.7, bf16[8,9216]{1,0:T(8,128)(2,1)S(1)} %shard_map.49._), custom_call_target="tpu_custom_call" | custom-call | bytes 1048576 | tf_op jit(solution)/shard_map/pallas_call | solution.py:142
  39.2 0.0 collective-permute-done.4
  39.2 0.1 convert_add_fusion.summed
  39.2 0.0 collective-permute-done.5.refs_0_
  39.3 0.7 %collective-permute-done.6.refs_1_ = bf16[8,9216]{1,0:T(8,128)(2,1)S(1)} collective-permute-done((bf16[8,9216]{1,0:T(8,128)(2,1)S(1)}, bf16[8,9216]{1,0:T(8,128)(2,1)S(1)}, u32[]{:S(2)}, u32[]{:S(2)}) %collective-permute-start.6) | collective-permute-done | bytes 147488 | tf_op jit(solution)/shard_map/ppermute | solution.py:300
  39.9 0.1 shard_map.51.refs_0_
  40.0 0.1 collective-permute-start.7
  40.1 2.1 %collective-permute-start.9 = (bf16[8,7552]{1,0:T(8,128)(2,1)S(1)}, bf16[8,7552]{1,0:T(8,128)(2,1)S(1)}, u32[]{:S(2)}, u32[]{:S(2)}) collective-permute-start(bf16[8,7552]{1,0:T(8,128)(2,1)S(1)} %shard_map.51.refs_0_), channel_id=1, source_target_pairs={{0,4},{4,0},{8,12},{12,8},{1,5},{5,1},{9,13},{13,9},{2,6},{6,2},{1... | collective-permute-start | bytes 362504 | tf_op jit(solution)/shard_map/ppermute | solution.py:300
  42.2 5.7 %collective-permute-done.7.refs_2_ = bf16[8,7552]{1,0:T(8,128)(2,1)S(1)} collective-permute-done((bf16[8,7552]{1,0:T(8,128)(2,1)S(1)}, bf16[8,7552]{1,0:T(8,128)(2,1)S(1)}, u32[]{:S(2)}, u32[]{:S(2)}) %collective-permute-start.7) | collective-permute-done | bytes 120864 | tf_op jit(solution)/shard_map/ppermute | solution.py:300
  47.9 0.0 collective-permute-start.8
  47.9 0.1 pad_add_fusion.1.starts
  48.0 0.0 collective-permute-done.9.refs_1_
  48.0 0.0 slice-done
  48.0 0.0 slice-done.1
  48.0 0.0 slice-done.2
  48.0 0.0 slice-done.3
  48.0 0.0 slice-done.4
  48.0 0.0 slice-done.5
  48.0 0.0 slice-done.6
  48.0 4.2 %shard_map.52.refs_1_ = f32[36,2048]{1,0:T(8,128)S(1)} custom-call(s32[3]{0:T(128)S(1)} %pad_add_fusion.1.starts, bf16[8,7552]{1,0:T(8,128)(2,1)S(1)} %shard_map.51.refs_0_, bf16[8,7552]{1,0:T(8,128)(2,1)S(1)} %collective-permute-done.9.refs_1_, bf16[8,7552]{1,0:T(8,128)(2,1)S(1)} %collective-permute-done.7.refs_2_, bf16[6656,2048]{1,0:T(8,128)(2,1)S(1)} %bitcast.5), custom_call_target="tpu_custom_call" | custom-call | bytes 1048576 | tf_op jit(solution)/shard_map/pallas_call | solution.py:264
  52.2 0.8 %collective-permute-done.8.refs_0_ = bf16[8,7552]{1,0:T(8,128)(2,1)S(1)} collective-permute-done((bf16[8,7552]{1,0:T(8,128)(2,1)S(1)}, bf16[8,7552]{1,0:T(8,128)(2,1)S(1)}, u32[]{:S(2)}, u32[]{:S(2)}) %collective-permute-start.8) | collective-permute-done | bytes 120864 | tf_op jit(solution)/shard_map/ppermute | solution.py:300
  53.0 1.3 %shard_map.53 = (f32[8,2304]{1,0:T(8,128)S(1)}, bf16[8,2304]{1,0:T(8,128)(2,1)S(1)}, bf16[8,2304]{1,0:T(8,128)(2,1)S(1)}, bf16[8,2304]{1,0:T(8,128)(2,1)S(1)}) custom-call(s32[1]{0:T(128)} %bitcast.start_ref.starts, bf16[8,7552]{1,0:T(8,128)(2,1)S(1)} %collective-permute-done.8.refs_0_, f32[36,2048]{1,0:T(8,128)S(1)} %shard_map.52.refs_1_, ...), custom_call_target="tpu_custom_call" | custom-call | bytes 1048576 | tf_op jit(solution)/shard_map/pallas_call | solution.py:264
  54.3 0.1 collective-permute-start.10
  54.4 1.5 %collective-permute-start.11 = (bf16[8,2304]{1,0:T(8,128)(2,1)S(1)}, bf16[8,2304]{1,0:T(8,128)(2,1)S(1)}, u32[]{:S(2)}, u32[]{:S(2)}) collective-permute-start(bf16[8,2304]{1,0:T(8,128)(2,1)S(1)} %get-tuple-element.15), channel_id=1, source_target_pairs={{0,2},{1,3},{2,0},{3,1},{4,6},{5,7},{6,4},{7,5},{8,10},{9,11},{10,... | collective-permute-start | bytes 110600 | tf_op jit(solution)/shard_map/ppermute | solution.py:300
  55.9 0.4 collective-permute-start.12
  56.3 0.0 collective-permute-done.10.refs_1_
  56.3 2.2 %collective-permute-done.11.refs_2_ = bf16[8,2304]{1,0:T(8,128)(2,1)S(1)} collective-permute-done((bf16[8,2304]{1,0:T(8,128)(2,1)S(1)}, bf16[8,2304]{1,0:T(8,128)(2,1)S(1)}, u32[]{:S(2)}, u32[]{:S(2)}) %collective-permute-start.11) | collective-permute-done | bytes 36896 | tf_op jit(solution)/shard_map/ppermute | solution.py:300
  58.4 0.9 %collective-permute-done.12.refs_3_ = bf16[8,2304]{1,0:T(8,128)(2,1)S(1)} collective-permute-done((bf16[8,2304]{1,0:T(8,128)(2,1)S(1)}, bf16[8,2304]{1,0:T(8,128)(2,1)S(1)}, u32[]{:S(2)}, u32[]{:S(2)}) %collective-permute-start.12) | collective-permute-done | bytes 36896 | tf_op jit(solution)/shard_map/ppermute | solution.py:300
  59.3 0.7 %shard_map.54 = bf16[9,2048]{1,0:T(8,128)(2,1)} custom-call(f32[8,2304]{1,0:T(8,128)S(1)} %get-tuple-element.13.refs_0_, bf16[8,2304]{1,0:T(8,128)(2,1)S(1)} %collective-permute-done.10.refs_1_, bf16[8,2304]{1,0:T(8,128)(2,1)S(1)} %collective-permute-done.11.refs_2_, bf16[8,2304]{1,0:T(8,128)(2,1)S(1)} %collective-permute-done.12.refs_3_), custom_call_target="tpu_custom_call" | custom-call | bytes 1048576 | tf_op jit(solution)/shard_map/pallas_call | solution.py:288
  (1 shorter events, 0.0 us)
Async XLA Ops:
  0.0 8.3 %collective-permute-start.2 = (bf16[9,2048]{1,0:T(8,128)(2,1)}, bf16[9,2048]{1,0:T(8,128)(2,1)S(1)}, u32[]{:S(2)}, u32[]{:S(2)}) collective-permute-start(bf16[9,2048]{1,0:T(8,128)(2,1)} %param.4), channel_id=1, source_target_pairs={{0,3},{1,2},{2,1},{3,0},{4,7},{5,6},{6,5},{7,4},{8,11},{9,10},{10,... | collective-permute-start | bytes 110600 | tf_op jit(solution)/shard_map/ppermute | solution.py:300
  2.4 5.9 %collective-permute-start.1 = (bf16[9,2048]{1,0:T(8,128)(2,1)}, bf16[9,2048]{1,0:T(8,128)(2,1)S(1)}, u32[]{:S(2)}, u32[]{:S(2)}) collective-permute-start(bf16[9,2048]{1,0:T(8,128)(2,1)} %param.4), channel_id=1, source_target_pairs={{0,2},{1,3},{2,0},{3,1},{4,6},{5,7},{6,4},{7,5},{8,10},{9,11},{10,... | collective-permute-start | bytes 110600 | tf_op jit(solution)/shard_map/ppermute | solution.py:300
  3.0 5.3 %collective-permute-start = (bf16[9,2048]{1,0:T(8,128)(2,1)}, bf16[9,2048]{1,0:T(8,128)(2,1)S(1)}, u32[]{:S(2)}, u32[]{:S(2)}) collective-permute-start(bf16[9,2048]{1,0:T(8,128)(2,1)} %param.4), channel_id=1, source_target_pairs={{0,1},{1,0},{2,3},{3,2},{4,5},{5,4},{6,7},{7,6},{8,9},{9,8},{10,11... | collective-permute-start | bytes 110600 | tf_op jit(solution)/shard_map/ppermute | solution.py:300
  3.1 5.3 %copy-start = (bf16[9,2048]{1,0:T(8,128)(2,1)S(1)}, bf16[9,2048]{1,0:T(8,128)(2,1)}, u32[]{:S(2)}) copy-start(bf16[9,2048]{1,0:T(8,128)(2,1)} %param.4) | copy-start | bytes 110596
  10.6 12.4 %collective-permute-start.3 = (bf16[8,14976]{1,0:T(8,128)(2,1)S(1)}, bf16[8,14976]{1,0:T(8,128)(2,1)S(1)}, u32[]{:S(2)}, u32[]{:S(2)}) collective-permute-start(bf16[8,14976]{1,0:T(8,128)(2,1)S(1)} %shard_map.47._), channel_id=1, source_target_pairs={{0,4},{4,0},{8,12},{12,8},{1,5},{5,1},{9,13},{13,9},{2,6},{6,2},{1... | collective-permute-start | bytes 718856 | tf_op jit(solution)/shard_map/ppermute | solution.py:300
  23.0 16.1 %collective-permute-start.4 = (bf16[8,14976]{1,0:T(8,128)(2,1)S(1)}, bf16[8,14976]{1,0:T(8,128)(2,1)S(1)}, u32[]{:S(2)}, u32[]{:S(2)}) collective-permute-start(bf16[8,14976]{1,0:T(8,128)(2,1)S(1)} %add_convert_fusion._), channel_id=1, source_target_pairs={{0,8},{4,12},{8,0},{12,4},{1,9},{5,13},{9,1},{13,5},{2,10},{6,14},... | collective-permute-start | bytes 718856 | tf_op jit(solution)/shard_map/ppermute | solution.py:300
  25.8 13.5 %collective-permute-start.5 = (bf16[8,5760]{1,0:T(8,128)(2,1)S(1)}, bf16[8,5760]{1,0:T(8,128)(2,1)S(1)}, u32[]{:S(2)}, u32[]{:S(2)}) collective-permute-start(bf16[8,5760]{1,0:T(8,128)(2,1)S(1)} %get-tuple-element.12), channel_id=1, source_target_pairs={{0,4},{4,0},{8,12},{12,8},{1,5},{5,1},{9,13},{13,9},{2,6},{6,2},{1... | collective-permute-start | bytes 276488 | tf_op jit(solution)/shard_map/ppermute | solution.py:300
  26.2 21.8 %slice-start = ((s8[27262976]{0:T(1024)(128)(4,1)}), s8[4194304]{0:T(1024)(128)(4,1)S(1)}, s32[]{:S(2)}) async-start(s8[27262976]{0:T(1024)(128)(4,1)} %bitcast.4), calls=%async_computation | async-start | bytes 8388608
  26.2 21.8 %slice-start.1 = ((s8[27262976]{0:T(1024)(128)(4,1)}), s8[4194304]{0:T(1024)(128)(4,1)S(1)}, s32[]{:S(2)}) async-start(s8[27262976]{0:T(1024)(128)(4,1)} %bitcast.4), calls=%async_computation.1 | async-start | bytes 8388608
  26.2 21.8 %slice-start.2 = ((s8[27262976]{0:T(1024)(128)(4,1)}), s8[4194304]{0:T(1024)(128)(4,1)S(1)}, s32[]{:S(2)}) async-start(s8[27262976]{0:T(1024)(128)(4,1)} %bitcast.4), calls=%async_computation.2 | async-start | bytes 8388608
  26.2 21.8 %slice-start.3 = ((s8[27262976]{0:T(1024)(128)(4,1)}), s8[4194304]{0:T(1024)(128)(4,1)S(1)}, s32[]{:S(2)}) async-start(s8[27262976]{0:T(1024)(128)(4,1)} %bitcast.4), calls=%async_computation.3 | async-start | bytes 8388608
  30.9 9.1 %collective-permute-start.6 = (bf16[8,9216]{1,0:T(8,128)(2,1)S(1)}, bf16[8,9216]{1,0:T(8,128)(2,1)S(1)}, u32[]{:S(2)}, u32[]{:S(2)}) collective-permute-start(bf16[8,9216]{1,0:T(8,128)(2,1)S(1)} %shard_map.49._), channel_id=1, source_target_pairs={{0,4},{4,0},{8,12},{12,8},{1,5},{5,1},{9,13},{13,9},{2,6},{6,2},{1... | collective-permute-start | bytes 442376 | tf_op jit(solution)/shard_map/ppermute | solution.py:300
  32.5 15.5 %slice-start.4 = ((s8[27262976]{0:T(1024)(128)(4,1)}), s8[4194304]{0:T(1024)(128)(4,1)S(1)}, s32[]{:S(2)}) async-start(s8[27262976]{0:T(1024)(128)(4,1)} %bitcast.4), calls=%async_computation.4 | async-start | bytes 8388608
  32.5 15.5 %slice-start.5 = ((s8[27262976]{0:T(1024)(128)(4,1)}), s8[4194304]{0:T(1024)(128)(4,1)S(1)}, s32[]{:S(2)}) async-start(s8[27262976]{0:T(1024)(128)(4,1)} %bitcast.4), calls=%async_computation.5 | async-start | bytes 8388608
  32.5 15.5 %slice-start.6 = ((s8[27262976]{0:T(1024)(128)(4,1)}), s8[2097152]{0:T(1024)(128)(4,1)S(1)}, s32[]{:S(2)}) async-start(s8[27262976]{0:T(1024)(128)(4,1)} %bitcast.4), calls=%async_computation.6 | async-start | bytes 4194304
  40.0 7.8 %collective-permute-start.7 = (bf16[8,7552]{1,0:T(8,128)(2,1)S(1)}, bf16[8,7552]{1,0:T(8,128)(2,1)S(1)}, u32[]{:S(2)}, u32[]{:S(2)}) collective-permute-start(bf16[8,7552]{1,0:T(8,128)(2,1)S(1)} %shard_map.51.refs_0_), channel_id=1, source_target_pairs={{0,8},{4,12},{8,0},{12,4},{1,9},{5,13},{9,1},{13,5},{2,10},{6,14},... | collective-permute-start | bytes 362504 | tf_op jit(solution)/shard_map/ppermute | solution.py:300
  40.1 7.9 %collective-permute-start.9 = (bf16[8,7552]{1,0:T(8,128)(2,1)S(1)}, bf16[8,7552]{1,0:T(8,128)(2,1)S(1)}, u32[]{:S(2)}, u32[]{:S(2)}) collective-permute-start(bf16[8,7552]{1,0:T(8,128)(2,1)S(1)} %shard_map.51.refs_0_), channel_id=1, source_target_pairs={{0,4},{4,0},{8,12},{12,8},{1,5},{5,1},{9,13},{13,9},{2,6},{6,2},{1... | collective-permute-start | bytes 362504 | tf_op jit(solution)/shard_map/ppermute | solution.py:300
  47.9 5.1 %collective-permute-start.8 = (bf16[8,7552]{1,0:T(8,128)(2,1)S(1)}, bf16[8,7552]{1,0:T(8,128)(2,1)S(1)}, u32[]{:S(2)}, u32[]{:S(2)}) collective-permute-start(bf16[8,7552]{1,0:T(8,128)(2,1)S(1)} %collective-permute-done.7.refs_2_), channel_id=1, source_target_pairs={{0,4},{4,0},{8,12},{12,8},{1,5},{5,1},{9,13},{13,9},{2,6},{6,2},{1... | collective-permute-start | bytes 362504 | tf_op jit(solution)/shard_map/ppermute | solution.py:300
  54.3 1.9 %collective-permute-start.10 = (bf16[8,2304]{1,0:T(8,128)(2,1)S(1)}, bf16[8,2304]{1,0:T(8,128)(2,1)S(1)}, u32[]{:S(2)}, u32[]{:S(2)}) collective-permute-start(bf16[8,2304]{1,0:T(8,128)(2,1)S(1)} %get-tuple-element.14), channel_id=1, source_target_pairs={{0,1},{1,0},{2,3},{3,2},{4,5},{5,4},{6,7},{7,6},{8,9},{9,8},{10,11... | collective-permute-start | bytes 110600 | tf_op jit(solution)/shard_map/ppermute | solution.py:300
  54.4 4.0 %collective-permute-start.11 = (bf16[8,2304]{1,0:T(8,128)(2,1)S(1)}, bf16[8,2304]{1,0:T(8,128)(2,1)S(1)}, u32[]{:S(2)}, u32[]{:S(2)}) collective-permute-start(bf16[8,2304]{1,0:T(8,128)(2,1)S(1)} %get-tuple-element.15), channel_id=1, source_target_pairs={{0,2},{1,3},{2,0},{3,1},{4,6},{5,7},{6,4},{7,5},{8,10},{9,11},{10,... | collective-permute-start | bytes 110600 | tf_op jit(solution)/shard_map/ppermute | solution.py:300
  55.9 3.4 %collective-permute-start.12 = (bf16[8,2304]{1,0:T(8,128)(2,1)S(1)}, bf16[8,2304]{1,0:T(8,128)(2,1)S(1)}, u32[]{:S(2)}, u32[]{:S(2)}) collective-permute-start(bf16[8,2304]{1,0:T(8,128)(2,1)S(1)} %get-tuple-element.16), channel_id=1, source_target_pairs={{0,3},{1,2},{2,1},{3,0},{4,7},{5,6},{6,5},{7,4},{8,11},{9,10},{10,... | collective-permute-start | bytes 110600 | tf_op jit(solution)/shard_map/ppermute | solution.py:300

commit v10 on v9

--- a/solution.py
+++ b/solution.py
@@ -9,6 +9,7 @@
 
 MIB = 1 << 20
 STEP = 256
+IN_FLIGHT = 8
 TOKEN_AXES = ("gy", "gz")
 IN_HBM = pl.BlockSpec(memory_space=pltpu.HBM)
 ANY = pl.BlockSpec(memory_space=pl.ANY)
@@ -55,7 +56,7 @@
         out[:, at : at + width] = tail.astype(out.dtype)
 
 
-def start_copies(width, starts, b, gate_ref, up_ref, held, sems):
+def block_copies(width, starts, b, gate_ref, up_ref, held, sems):
     columns = pl.ds(pl.multiple_of(starts[b], 128), width)
     copies = []
     for k, (row, rows) in enumerate(pieces_of(held.shape[1], STEP)):
@@ -63,13 +64,15 @@
             copy = pltpu.make_async_copy(
                 weight.at[pl.ds(row, rows), columns], held.at[w, pl.ds(row, rows)], sems.at[w, k]
             )
-            copy.start()
             copies.append((w, row, rows, copy))
     return copies
 
 
 def fetch_kernel(width, start_ref, gate_ref, up_ref, held, sems):
-    for _, _, _, copy in start_copies(width, start_ref, 0, gate_ref, up_ref, held, sems):
+    copies = block_copies(width, start_ref, 0, gate_ref, up_ref, held, sems)
+    for _, _, _, copy in copies:
+        copy.start()
+    for _, _, _, copy in copies:
         copy.wait()
 
 
@@ -86,10 +89,12 @@
     )(start, in_hbm(gate_weight), in_hbm(up_weight))
 
 
-def multiply(x_ref, held, total, steps):
+def multiply(x_ref, held, total, steps, waiting=()):
     for w, row, rows, copy in steps:
         if copy is not None:
             copy.wait()
+        if waiting:
+            waiting.pop(0).start()
         term = jnp.dot(
             x_ref[:, row : row + rows], held[w, row : row + rows, :], preferred_element_type=jnp.float32
         )
@@ -123,10 +128,15 @@
     blocks = []
     for b, width in enumerate(widths):
         held, total, sems = refs[3 * b : 3 * b + 3]
-        copies = start_copies(width, starts, b, gate_ref, up_ref, held, sems)
+        copies = block_copies(width, starts, b, gate_ref, up_ref, held, sems)
         blocks.append((outs[b], held, total, copies))
+    waiting = [step[-1] for block in blocks for step in block[-1]]
+    in_flight = IN_FLIGHT if len(widths) > 1 else len(waiting)
+    for copy in waiting[:in_flight]:
+        copy.start()
+    waiting = waiting[in_flight:]
     for out, held, total, copies in blocks:
-        multiply(x_ref, held, total, copies)
+        multiply(x_ref, held, total, copies, waiting)
         pack_pair(out, total[0], total[1])
 
 

time: 60.1 us -> 59.2 us (0.985)
  Pallas kernels: 35.4 us -> 34.5 us
    pallas_call x3, Pallas kernels: 21.8 us -> 20.8 us  [gate_up_stream(): pl.pallas_call(functools.partial(stream_kernel, widths), out_shape=[jax.S...]
  transfers between devices with their start and end apart: 13 -> 13, of which waited for: 5 -> 5; matrix products, arithmetic and copies ran while one was open for 0% -> 0% of each run, Pallas kernels for 52% -> 51%
where the time goes in v10:
time: 59.2 us; the launch traced here: 59 us
  Pallas kernels  34.5 us (58%)
  starting transfers between devices  13.7 us (23%)
  waiting for transfers between devices  10.3 us (17%)
    pallas_call x3, Pallas kernels, gate_up_stream(): pl.pallas_call(functools.partial(stream_kernel, widths), out_shape=[jax.S...  20.8 us
    ppermute x13, starting transfers between devices, swap(): return lax.ppermute(value, axes, [(i, i ^ distance) for i in range(size)])  13.7 us
    ppermute x13, waiting for transfers between devices, swap(): return lax.ppermute(value, axes, [(i, i ^ distance) for i in range(size)])  10.3 us
    pallas_call x2, Pallas kernels, down(): pl.pallas_call(functools.partial(down_kernel, before is None, rows, width...  5.48 us
    pallas_call x1, Pallas kernels, fetch(): pl.pallas_call(functools.partial(fetch_kernel, width), out_shape=pltpu.VM...  5.23 us
    pallas_call x1, Pallas kernels, gate_up_held(): pl.pallas_call(held_kernel, out_shape=jax.ShapeDtypeStruct((8, packed_pai...  2.15 us
  transfers between devices with their start and end apart: 13, of which 5 were waited for; matrix products, arithmetic and copies ran while one was open for 0% of the time, Pallas kernels for 51%

profile of v10, /device:TPU:0, one launch (start us, length us, event | category | flops | bytes accessed | tf_op | source)
XLA Modules:
  0.0 59.0 jit_solution(1579251884958005092)
XLA Ops:
  0.0 2.4 %collective-permute-start.2 = (bf16[9,2048]{1,0:T(8,128)(2,1)}, bf16[9,2048]{1,0:T(8,128)(2,1)S(1)}, u32[]{:S(2)}, u32[]{:S(2)}) collective-permute-start(bf16[9,2048]{1,0:T(8,128)(2,1)} %param.4), channel_id=1, source_target_pairs={{0,3},{1,2},{2,1},{3,0},{4,7},{5,6},{6,5},{7,4},{8,11},{9,10},{10,... | collective-permute-start | bytes 110600 | tf_op jit(solution)/shard_map/ppermute | solution.py:310
  2.4 0.6 %collective-permute-start.1 = (bf16[9,2048]{1,0:T(8,128)(2,1)}, bf16[9,2048]{1,0:T(8,128)(2,1)S(1)}, u32[]{:S(2)}, u32[]{:S(2)}) collective-permute-start(bf16[9,2048]{1,0:T(8,128)(2,1)} %param.4), channel_id=1, source_target_pairs={{0,2},{1,3},{2,0},{3,1},{4,6},{5,7},{6,4},{7,5},{8,10},{9,11},{10,... | collective-permute-start | bytes 110600 | tf_op jit(solution)/shard_map/ppermute | solution.py:310
  3.0 0.1 collective-permute-start
  3.1 0.0 copy-start
  3.1 5.2 %shard_map.46.held = bf16[2,2048,1664]{2,1,0:T(8,128)(2,1)S(1)} custom-call(s32[1]{0:T(128)} %bitcast.start_ref.starts, bf16[2048,6656]{1,0:T(8,128)(2,1)} %gate_ref.7, bf16[2048,6656]{1,0:T(8,128)(2,1)} %up_ref.7), custom_call_target="tpu_custom_call" | custom-call | bytes 1048576 | tf_op jit(solution)/shard_map/pallas_call | solution.py:81
  8.3 0.0 collective-permute-done.2
  8.3 0.0 collective-permute-done.1
  8.3 0.0 collective-permute-done
  8.3 0.0 copy-done
  8.3 0.1 pad_maximum_fusion.x_ref
  8.4 2.2 %shard_map.47._ = bf16[8,14976]{1,0:T(8,128)(2,1)S(1)} custom-call(bf16[36,2048]{1,0:T(8,128)(2,1)S(1)} %pad_maximum_fusion.x_ref, bf16[2,2048,1664]{2,1,0:T(8,128)(2,1)S(1)} %shard_map.46.held), custom_call_target="tpu_custom_call" | custom-call | bytes 1048576 | tf_op jit(solution)/shard_map/pallas_call | solution.py:115
  10.6 1.7 %collective-permute-start.3 = (bf16[8,14976]{1,0:T(8,128)(2,1)S(1)}, bf16[8,14976]{1,0:T(8,128)(2,1)S(1)}, u32[]{:S(2)}, u32[]{:S(2)}) collective-permute-start(bf16[8,14976]{1,0:T(8,128)(2,1)S(1)} %shard_map.47._), channel_id=1, source_target_pairs={{0,4},{4,0},{8,12},{12,8},{1,5},{5,1},{9,13},{13,9},{2,6},{6,2},{1... | collective-permute-start | bytes 718856 | tf_op jit(solution)/shard_map/ppermute | solution.py:310
  12.3 0.1 pad_add_fusion.starts
  12.4 9.6 %shard_map.48 = (bf16[8,14976]{1,0:T(8,128)(2,1)S(1)}, bf16[8,5760]{1,0:T(8,128)(2,1)S(1)}) custom-call(s32[2]{0:T(128)S(1)} %pad_add_fusion.starts, bf16[36,2048]{1,0:T(8,128)(2,1)S(1)} %pad_maximum_fusion.x_ref, bf16[2048,6656]{1,0:T(8,128)(2,1)} %gate_ref.7, bf16[2048,6656]{1,0:T(8,128)(2,1)} %up_ref.7, bf16[8,14976]{1,0:T(8,128)(2,1)S(1)} %shard_map.47._), custom_call_target="tpu_custom_call" | custom-call | bytes 1048576 | tf_op jit(solution)/shard_map/pallas_call | solution.py:152
  22.0 0.0 collective-permute-done.3
  22.0 0.1 add_convert_fusion._
  22.1 2.7 %collective-permute-start.4 = (bf16[8,14976]{1,0:T(8,128)(2,1)S(1)}, bf16[8,14976]{1,0:T(8,128)(2,1)S(1)}, u32[]{:S(2)}, u32[]{:S(2)}) collective-permute-start(bf16[8,14976]{1,0:T(8,128)(2,1)S(1)} %add_convert_fusion._), channel_id=1, source_target_pairs={{0,8},{4,12},{8,0},{12,4},{1,9},{5,13},{9,1},{13,5},{2,10},{6,14},... | collective-permute-start | bytes 718856 | tf_op jit(solution)/shard_map/ppermute | solution.py:310
  24.8 0.4 collective-permute-start.5
  25.2 0.0 slice-start
  25.2 0.0 slice-start.1
  25.2 0.0 slice-start.2
  25.2 0.0 slice-start.3
  25.2 4.7 %shard_map.49._ = bf16[8,9216]{1,0:T(8,128)(2,1)S(1)} custom-call(s32[1]{0:T(128)S(6)} %add.9.starts, bf16[36,2048]{1,0:T(8,128)(2,1)S(1)} %pad_maximum_fusion.x_ref, bf16[2048,6656]{1,0:T(8,128)(2,1)} %gate_ref.7, bf16[2048,6656]{1,0:T(8,128)(2,1)} %up_ref.7, bf16[8,14976]{1,0:T(8,128)(2,1)S(1)} %add_convert_fusion._), custom_call_target="tpu_custom_call" | custom-call | bytes 1048576 | tf_op jit(solution)/shard_map/pallas_call | solution.py:152
  29.9 1.7 %collective-permute-start.6 = (bf16[8,9216]{1,0:T(8,128)(2,1)S(1)}, bf16[8,9216]{1,0:T(8,128)(2,1)S(1)}, u32[]{:S(2)}, u32[]{:S(2)}) collective-permute-start(bf16[8,9216]{1,0:T(8,128)(2,1)S(1)} %shard_map.49._), channel_id=1, source_target_pairs={{0,4},{4,0},{8,12},{12,8},{1,5},{5,1},{9,13},{13,9},{2,6},{6,2},{1... | collective-permute-start | bytes 442376 | tf_op jit(solution)/shard_map/ppermute | solution.py:310
  31.6 0.0 slice-start.4
  31.6 0.0 slice-start.5
  31.6 0.0 slice-start.6
  31.6 6.6 %shard_map.50 = bf16[8,14976]{1,0:T(8,128)(2,1)S(1)} custom-call(s32[1]{0:T(128)} %bitcast.1.starts, bf16[36,2048]{1,0:T(8,128)(2,1)S(1)} %pad_maximum_fusion.x_ref, bf16[2048,6656]{1,0:T(8,128)(2,1)} %gate_ref.7, bf16[2048,6656]{1,0:T(8,128)(2,1)} %up_ref.7, bf16[8,9216]{1,0:T(8,128)(2,1)S(1)} %shard_map.49._), custom_call_target="tpu_custom_call" | custom-call | bytes 1048576 | tf_op jit(solution)/shard_map/pallas_call | solution.py:152
  38.2 0.0 collective-permute-done.4
  38.2 0.1 convert_add_fusion.summed
  38.3 0.0 collective-permute-done.5.refs_0_
  38.3 0.7 %collective-permute-done.6.refs_1_ = bf16[8,9216]{1,0:T(8,128)(2,1)S(1)} collective-permute-done((bf16[8,9216]{1,0:T(8,128)(2,1)S(1)}, bf16[8,9216]{1,0:T(8,128)(2,1)S(1)}, u32[]{:S(2)}, u32[]{:S(2)}) %collective-permute-start.6) | collective-permute-done | bytes 147488 | tf_op jit(solution)/shard_map/ppermute | solution.py:310
  39.0 0.1 shard_map.51.refs_0_
  39.1 0.1 collective-permute-start.7
  39.1 2.0 %collective-permute-start.9 = (bf16[8,7552]{1,0:T(8,128)(2,1)S(1)}, bf16[8,7552]{1,0:T(8,128)(2,1)S(1)}, u32[]{:S(2)}, u32[]{:S(2)}) collective-permute-start(bf16[8,7552]{1,0:T(8,128)(2,1)S(1)} %shard_map.51.refs_0_), channel_id=1, source_target_pairs={{0,4},{4,0},{8,12},{12,8},{1,5},{5,1},{9,13},{13,9},{2,6},{6,2},{1... | collective-permute-start | bytes 362504 | tf_op jit(solution)/shard_map/ppermute | solution.py:310
  41.2 5.7 %collective-permute-done.7.refs_2_ = bf16[8,7552]{1,0:T(8,128)(2,1)S(1)} collective-permute-done((bf16[8,7552]{1,0:T(8,128)(2,1)S(1)}, bf16[8,7552]{1,0:T(8,128)(2,1)S(1)}, u32[]{:S(2)}, u32[]{:S(2)}) %collective-permute-start.7) | collective-permute-done | bytes 120864 | tf_op jit(solution)/shard_map/ppermute | solution.py:310
  46.9 0.0 collective-permute-start.8
  46.9 0.1 pad_add_fusion.1.starts
  47.0 0.0 collective-permute-done.9.refs_1_
  47.0 0.0 slice-done
  47.0 0.0 slice-done.1
  47.0 0.0 slice-done.2
  47.0 0.0 slice-done.3
  47.0 0.0 slice-done.4
  47.0 0.0 slice-done.5
  47.0 0.0 slice-done.6
  47.0 4.2 %shard_map.52.refs_1_ = f32[36,2048]{1,0:T(8,128)S(1)} custom-call(s32[3]{0:T(128)S(1)} %pad_add_fusion.1.starts, bf16[8,7552]{1,0:T(8,128)(2,1)S(1)} %shard_map.51.refs_0_, bf16[8,7552]{1,0:T(8,128)(2,1)S(1)} %collective-permute-done.9.refs_1_, bf16[8,7552]{1,0:T(8,128)(2,1)S(1)} %collective-permute-done.7.refs_2_, bf16[6656,2048]{1,0:T(8,128)(2,1)S(1)} %bitcast.5), custom_call_target="tpu_custom_call" | custom-call | bytes 1048576 | tf_op jit(solution)/shard_map/pallas_call | solution.py:274
  51.2 0.8 %collective-permute-done.8.refs_0_ = bf16[8,7552]{1,0:T(8,128)(2,1)S(1)} collective-permute-done((bf16[8,7552]{1,0:T(8,128)(2,1)S(1)}, bf16[8,7552]{1,0:T(8,128)(2,1)S(1)}, u32[]{:S(2)}, u32[]{:S(2)}) %collective-permute-start.8) | collective-permute-done | bytes 120864 | tf_op jit(solution)/shard_map/ppermute | solution.py:310
  52.0 1.3 %shard_map.53 = (f32[8,2304]{1,0:T(8,128)S(1)}, bf16[8,2304]{1,0:T(8,128)(2,1)S(1)}, bf16[8,2304]{1,0:T(8,128)(2,1)S(1)}, bf16[8,2304]{1,0:T(8,128)(2,1)S(1)}) custom-call(s32[1]{0:T(128)} %bitcast.start_ref.starts, bf16[8,7552]{1,0:T(8,128)(2,1)S(1)} %collective-permute-done.8.refs_0_, f32[36,2048]{1,0:T(8,128)S(1)} %shard_map.52.refs_1_, ...), custom_call_target="tpu_custom_call" | custom-call | bytes 1048576 | tf_op jit(solution)/shard_map/pallas_call | solution.py:274
  53.4 0.1 collective-permute-start.10
  53.4 1.5 %collective-permute-start.11 = (bf16[8,2304]{1,0:T(8,128)(2,1)S(1)}, bf16[8,2304]{1,0:T(8,128)(2,1)S(1)}, u32[]{:S(2)}, u32[]{:S(2)}) collective-permute-start(bf16[8,2304]{1,0:T(8,128)(2,1)S(1)} %get-tuple-element.15), channel_id=1, source_target_pairs={{0,2},{1,3},{2,0},{3,1},{4,6},{5,7},{6,4},{7,5},{8,10},{9,11},{10,... | collective-permute-start | bytes 110600 | tf_op jit(solution)/shard_map/ppermute | solution.py:310
  54.9 0.4 collective-permute-start.12
  55.3 0.0 collective-permute-done.10.refs_1_
  55.3 2.2 %collective-permute-done.11.refs_2_ = bf16[8,2304]{1,0:T(8,128)(2,1)S(1)} collective-permute-done((bf16[8,2304]{1,0:T(8,128)(2,1)S(1)}, bf16[8,2304]{1,0:T(8,128)(2,1)S(1)}, u32[]{:S(2)}, u32[]{:S(2)}) %collective-permute-start.11) | collective-permute-done | bytes 36896 | tf_op jit(solution)/shard_map/ppermute | solution.py:310
  57.5 0.9 %collective-permute-done.12.refs_3_ = bf16[8,2304]{1,0:T(8,128)(2,1)S(1)} collective-permute-done((bf16[8,2304]{1,0:T(8,128)(2,1)S(1)}, bf16[8,2304]{1,0:T(8,128)(2,1)S(1)}, u32[]{:S(2)}, u32[]{:S(2)}) %collective-permute-start.12) | collective-permute-done | bytes 36896 | tf_op jit(solution)/shard_map/ppermute | solution.py:310
  58.4 0.7 %shard_map.54 = bf16[9,2048]{1,0:T(8,128)(2,1)} custom-call(f32[8,2304]{1,0:T(8,128)S(1)} %get-tuple-element.13.refs_0_, bf16[8,2304]{1,0:T(8,128)(2,1)S(1)} %collective-permute-done.10.refs_1_, bf16[8,2304]{1,0:T(8,128)(2,1)S(1)} %collective-permute-done.11.refs_2_, bf16[8,2304]{1,0:T(8,128)(2,1)S(1)} %collective-permute-done.12.refs_3_), custom_call_target="tpu_custom_call" | custom-call | bytes 1048576 | tf_op jit(solution)/shard_map/pallas_call | solution.py:298
  (1 shorter events, 0.0 us)
Async XLA Ops:
  0.0 8.3 %collective-permute-start.2 = (bf16[9,2048]{1,0:T(8,128)(2,1)}, bf16[9,2048]{1,0:T(8,128)(2,1)S(1)}, u32[]{:S(2)}, u32[]{:S(2)}) collective-permute-start(bf16[9,2048]{1,0:T(8,128)(2,1)} %param.4), channel_id=1, source_target_pairs={{0,3},{1,2},{2,1},{3,0},{4,7},{5,6},{6,5},{7,4},{8,11},{9,10},{10,... | collective-permute-start | bytes 110600 | tf_op jit(solution)/shard_map/ppermute | solution.py:310
  2.4 5.9 %collective-permute-start.1 = (bf16[9,2048]{1,0:T(8,128)(2,1)}, bf16[9,2048]{1,0:T(8,128)(2,1)S(1)}, u32[]{:S(2)}, u32[]{:S(2)}) collective-permute-start(bf16[9,2048]{1,0:T(8,128)(2,1)} %param.4), channel_id=1, source_target_pairs={{0,2},{1,3},{2,0},{3,1},{4,6},{5,7},{6,4},{7,5},{8,10},{9,11},{10,... | collective-permute-start | bytes 110600 | tf_op jit(solution)/shard_map/ppermute | solution.py:310
  3.0 5.3 %collective-permute-start = (bf16[9,2048]{1,0:T(8,128)(2,1)}, bf16[9,2048]{1,0:T(8,128)(2,1)S(1)}, u32[]{:S(2)}, u32[]{:S(2)}) collective-permute-start(bf16[9,2048]{1,0:T(8,128)(2,1)} %param.4), channel_id=1, source_target_pairs={{0,1},{1,0},{2,3},{3,2},{4,5},{5,4},{6,7},{7,6},{8,9},{9,8},{10,11... | collective-permute-start | bytes 110600 | tf_op jit(solution)/shard_map/ppermute | solution.py:310
  3.1 5.3 %copy-start = (bf16[9,2048]{1,0:T(8,128)(2,1)S(1)}, bf16[9,2048]{1,0:T(8,128)(2,1)}, u32[]{:S(2)}) copy-start(bf16[9,2048]{1,0:T(8,128)(2,1)} %param.4) | copy-start | bytes 110596
  10.6 11.4 %collective-permute-start.3 = (bf16[8,14976]{1,0:T(8,128)(2,1)S(1)}, bf16[8,14976]{1,0:T(8,128)(2,1)S(1)}, u32[]{:S(2)}, u32[]{:S(2)}) collective-permute-start(bf16[8,14976]{1,0:T(8,128)(2,1)S(1)} %shard_map.47._), channel_id=1, source_target_pairs={{0,4},{4,0},{8,12},{12,8},{1,5},{5,1},{9,13},{13,9},{2,6},{6,2},{1... | collective-permute-start | bytes 718856 | tf_op jit(solution)/shard_map/ppermute | solution.py:310
  22.1 16.1 %collective-permute-start.4 = (bf16[8,14976]{1,0:T(8,128)(2,1)S(1)}, bf16[8,14976]{1,0:T(8,128)(2,1)S(1)}, u32[]{:S(2)}, u32[]{:S(2)}) collective-permute-start(bf16[8,14976]{1,0:T(8,128)(2,1)S(1)} %add_convert_fusion._), channel_id=1, source_target_pairs={{0,8},{4,12},{8,0},{12,4},{1,9},{5,13},{9,1},{13,5},{2,10},{6,14},... | collective-permute-start | bytes 718856 | tf_op jit(solution)/shard_map/ppermute | solution.py:310
  24.8 13.5 %collective-permute-start.5 = (bf16[8,5760]{1,0:T(8,128)(2,1)S(1)}, bf16[8,5760]{1,0:T(8,128)(2,1)S(1)}, u32[]{:S(2)}, u32[]{:S(2)}) collective-permute-start(bf16[8,5760]{1,0:T(8,128)(2,1)S(1)} %get-tuple-element.12), channel_id=1, source_target_pairs={{0,4},{4,0},{8,12},{12,8},{1,5},{5,1},{9,13},{13,9},{2,6},{6,2},{1... | collective-permute-start | bytes 276488 | tf_op jit(solution)/shard_map/ppermute | solution.py:310
  25.2 21.8 %slice-start = ((s8[27262976]{0:T(1024)(128)(4,1)}), s8[4194304]{0:T(1024)(128)(4,1)S(1)}, s32[]{:S(2)}) async-start(s8[27262976]{0:T(1024)(128)(4,1)} %bitcast.4), calls=%async_computation | async-start | bytes 8388608
  25.2 21.8 %slice-start.1 = ((s8[27262976]{0:T(1024)(128)(4,1)}), s8[4194304]{0:T(1024)(128)(4,1)S(1)}, s32[]{:S(2)}) async-start(s8[27262976]{0:T(1024)(128)(4,1)} %bitcast.4), calls=%async_computation.1 | async-start | bytes 8388608
  25.2 21.8 %slice-start.2 = ((s8[27262976]{0:T(1024)(128)(4,1)}), s8[4194304]{0:T(1024)(128)(4,1)S(1)}, s32[]{:S(2)}) async-start(s8[27262976]{0:T(1024)(128)(4,1)} %bitcast.4), calls=%async_computation.2 | async-start | bytes 8388608
  25.2 21.8 %slice-start.3 = ((s8[27262976]{0:T(1024)(128)(4,1)}), s8[4194304]{0:T(1024)(128)(4,1)S(1)}, s32[]{:S(2)}) async-start(s8[27262976]{0:T(1024)(128)(4,1)} %bitcast.4), calls=%async_computation.3 | async-start | bytes 8388608
  29.9 9.1 %collective-permute-start.6 = (bf16[8,9216]{1,0:T(8,128)(2,1)S(1)}, bf16[8,9216]{1,0:T(8,128)(2,1)S(1)}, u32[]{:S(2)}, u32[]{:S(2)}) collective-permute-start(bf16[8,9216]{1,0:T(8,128)(2,1)S(1)} %shard_map.49._), channel_id=1, source_target_pairs={{0,4},{4,0},{8,12},{12,8},{1,5},{5,1},{9,13},{13,9},{2,6},{6,2},{1... | collective-permute-start | bytes 442376 | tf_op jit(solution)/shard_map/ppermute | solution.py:310
  31.6 15.5 %slice-start.4 = ((s8[27262976]{0:T(1024)(128)(4,1)}), s8[4194304]{0:T(1024)(128)(4,1)S(1)}, s32[]{:S(2)}) async-start(s8[27262976]{0:T(1024)(128)(4,1)} %bitcast.4), calls=%async_computation.4 | async-start | bytes 8388608
  31.6 15.5 %slice-start.5 = ((s8[27262976]{0:T(1024)(128)(4,1)}), s8[4194304]{0:T(1024)(128)(4,1)S(1)}, s32[]{:S(2)}) async-start(s8[27262976]{0:T(1024)(128)(4,1)} %bitcast.4), calls=%async_computation.5 | async-start | bytes 8388608
  31.6 15.5 %slice-start.6 = ((s8[27262976]{0:T(1024)(128)(4,1)}), s8[2097152]{0:T(1024)(128)(4,1)S(1)}, s32[]{:S(2)}) async-start(s8[27262976]{0:T(1024)(128)(4,1)} %bitcast.4), calls=%async_computation.6 | async-start | bytes 4194304
  39.1 7.8 %collective-permute-start.7 = (bf16[8,7552]{1,0:T(8,128)(2,1)S(1)}, bf16[8,7552]{1,0:T(8,128)(2,1)S(1)}, u32[]{:S(2)}, u32[]{:S(2)}) collective-permute-start(bf16[8,7552]{1,0:T(8,128)(2,1)S(1)} %shard_map.51.refs_0_), channel_id=1, source_target_pairs={{0,8},{4,12},{8,0},{12,4},{1,9},{5,13},{9,1},{13,5},{2,10},{6,14},... | collective-permute-start | bytes 362504 | tf_op jit(solution)/shard_map/ppermute | solution.py:310
  39.1 7.9 %collective-permute-start.9 = (bf16[8,7552]{1,0:T(8,128)(2,1)S(1)}, bf16[8,7552]{1,0:T(8,128)(2,1)S(1)}, u32[]{:S(2)}, u32[]{:S(2)}) collective-permute-start(bf16[8,7552]{1,0:T(8,128)(2,1)S(1)} %shard_map.51.refs_0_), channel_id=1, source_target_pairs={{0,4},{4,0},{8,12},{12,8},{1,5},{5,1},{9,13},{13,9},{2,6},{6,2},{1... | collective-permute-start | bytes 362504 | tf_op jit(solution)/shard_map/ppermute | solution.py:310
  46.9 5.1 %collective-permute-start.8 = (bf16[8,7552]{1,0:T(8,128)(2,1)S(1)}, bf16[8,7552]{1,0:T(8,128)(2,1)S(1)}, u32[]{:S(2)}, u32[]{:S(2)}) collective-permute-start(bf16[8,7552]{1,0:T(8,128)(2,1)S(1)} %collective-permute-done.7.refs_2_), channel_id=1, source_target_pairs={{0,4},{4,0},{8,12},{12,8},{1,5},{5,1},{9,13},{13,9},{2,6},{6,2},{1... | collective-permute-start | bytes 362504 | tf_op jit(solution)/shard_map/ppermute | solution.py:310
  53.4 1.9 %collective-permute-start.10 = (bf16[8,2304]{1,0:T(8,128)(2,1)S(1)}, bf16[8,2304]{1,0:T(8,128)(2,1)S(1)}, u32[]{:S(2)}, u32[]{:S(2)}) collective-permute-start(bf16[8,2304]{1,0:T(8,128)(2,1)S(1)} %get-tuple-element.14), channel_id=1, source_target_pairs={{0,1},{1,0},{2,3},{3,2},{4,5},{5,4},{6,7},{7,6},{8,9},{9,8},{10,11... | collective-permute-start | bytes 110600 | tf_op jit(solution)/shard_map/ppermute | solution.py:310
  53.4 4.0 %collective-permute-start.11 = (bf16[8,2304]{1,0:T(8,128)(2,1)S(1)}, bf16[8,2304]{1,0:T(8,128)(2,1)S(1)}, u32[]{:S(2)}, u32[]{:S(2)}) collective-permute-start(bf16[8,2304]{1,0:T(8,128)(2,1)S(1)} %get-tuple-element.15), channel_id=1, source_target_pairs={{0,2},{1,3},{2,0},{3,1},{4,6},{5,7},{6,4},{7,5},{8,10},{9,11},{10,... | collective-permute-start | bytes 110600 | tf_op jit(solution)/shard_map/ppermute | solution.py:310
  54.9 3.4 %collective-permute-start.12 = (bf16[8,2304]{1,0:T(8,128)(2,1)S(1)}, bf16[8,2304]{1,0:T(8,128)(2,1)S(1)}, u32[]{:S(2)}, u32[]{:S(2)}) collective-permute-start(bf16[8,2304]{1,0:T(8,128)(2,1)S(1)} %get-tuple-element.16), channel_id=1, source_target_pairs={{0,3},{1,2},{2,1},{3,0},{4,7},{5,6},{6,5},{7,4},{8,11},{9,10},{10,... | collective-permute-start | bytes 110600 | tf_op jit(solution)/shard_map/ppermute | solution.py:310

commit v11 on v5

--- a/solution.py
+++ b/solution.py
@@ -9,6 +9,7 @@
 
 MIB = 1 << 20
 STEP = 256
+IN_FLIGHT = 8
 TOKEN_AXES = ("gy", "gz")
 IN_HBM = pl.BlockSpec(memory_space=pltpu.HBM)
 ANY = pl.BlockSpec(memory_space=pl.ANY)
@@ -55,21 +56,23 @@
         out[:, at : at + width] = tail.astype(out.dtype)
 
 
-def start_copies(width, start_ref, gate_ref, up_ref, held, sems):
-    columns = pl.ds(pl.multiple_of(start_ref[0], 128), width)
+def block_copies(width, start, weights, held, sems):
+    columns = pl.ds(pl.multiple_of(start, 128), width)
     copies = []
     for k, (row, rows) in enumerate(pieces_of(held.shape[1], STEP)):
-        for w, weight in enumerate((gate_ref, up_ref)):
+        for w, weight in enumerate(weights):
             copy = pltpu.make_async_copy(
                 weight.at[pl.ds(row, rows), columns], held.at[w, pl.ds(row, rows)], sems.at[w, k]
             )
-            copy.start()
             copies.append((w, row, rows, copy))
     return copies
 
 
 def fetch_kernel(width, start_ref, gate_ref, up_ref, held, sems):
-    for _, _, _, copy in start_copies(width, start_ref, gate_ref, up_ref, held, sems):
+    copies = block_copies(width, start_ref[0], (gate_ref, up_ref), held, sems)
+    for _, _, _, copy in copies:
+        copy.start()
+    for _, _, _, copy in copies:
         copy.wait()
 
 
@@ -86,10 +89,12 @@
     )(start, in_hbm(gate_weight), in_hbm(up_weight))
 
 
-def multiply(x_ref, held, total, steps):
+def multiply(x_ref, held, total, steps, waiting=()):
     for w, row, rows, copy in steps:
         if copy is not None:
             copy.wait()
+        if waiting:
+            waiting.pop(0).start()
         term = jnp.dot(
             x_ref[:, row : row + rows], held[w, row : row + rows, :], preferred_element_type=jnp.float32
         )
@@ -118,27 +123,48 @@
     )(features, in_vmem(held))
 
 
-def stream_kernel(width, start_ref, x_ref, gate_ref, up_ref, _, out, held, total, sems):
-    copies = start_copies(width, start_ref, gate_ref, up_ref, held, sems)
-    multiply(x_ref, held, total, copies)
-    pack_pair(out, total[0], total[1])
-
-
-def gate_up_stream(features, gate_weight, up_weight, start, width, after):
+def stream_kernel(width, blocks, starts, x_ref, gate_ref, up_ref, _, *refs):
+    outs, refs = refs[: len(blocks)], refs[len(blocks) :]
+    work = []
+    for b, which in enumerate(blocks):
+        held, total, sems = refs[3 * b : 3 * b + 3]
+        weights = [(gate_ref, up_ref)[w] for w in which]
+        copies = block_copies(width, starts[b], weights, held, sems)
+        work.append((outs[b], held, total, copies))
+    waiting = [step[-1] for block in work for step in block[-1]]
+    in_flight = IN_FLIGHT if len(blocks) > 1 else len(waiting)
+    for copy in waiting[:in_flight]:
+        copy.start()
+    waiting = waiting[in_flight:]
+    for (out, held, total, copies), which in zip(work, blocks):
+        multiply(x_ref, held, total, copies, waiting)
+        if len(which) == 2:
+            pack_pair(out, total[0], total[1])
+        else:
+            pack_single(out, total[0])
+
+
+def gate_up_stream(features, gate_weight, up_weight, starts, blocks, width, after):
     rows, depth = features.shape
-    return pl.pallas_call(
-        functools.partial(stream_kernel, width),
-        out_shape=jax.ShapeDtypeStruct((8, packed_pair_width(rows, width)), jnp.bfloat16),
+    scratch, shapes = [], []
+    for which in blocks:
+        packed = packed_pair_width(rows, width) if len(which) == 2 else packed_width(rows, width)
+        shapes.append(jax.ShapeDtypeStruct((8, packed), jnp.bfloat16))
+        scratch += [
+            pltpu.VMEM((len(which), depth, width), jnp.bfloat16),
+            pltpu.VMEM((len(which), rows, width), jnp.float32),
+            pltpu.SemaphoreType.DMA((len(which), len(pieces_of(depth, STEP)))),
+        ]
+    held_mib = -(-depth * width * 2 * sum(len(which) for which in blocks) // MIB)
+    return pl.pallas_call(
+        functools.partial(stream_kernel, width, blocks),
+        out_shape=shapes,
         in_specs=[SCALARS, WHOLE, IN_HBM, IN_HBM, ANY],
-        out_specs=WHOLE,
-        scratch_shapes=[
-            pltpu.VMEM((2, depth, width), jnp.bfloat16),
-            pltpu.VMEM((2, rows, width), jnp.float32),
-            pltpu.SemaphoreType.DMA((2, len(pieces_of(depth, STEP)))),
-        ],
-        compiler_params=params(18),
-        cost_estimate=SMALL,
-    )(start, features, in_hbm(gate_weight), in_hbm(up_weight), after)
+        out_specs=[WHOLE] * len(blocks),
+        scratch_shapes=scratch,
+        compiler_params=params(5 + held_mib),
+        cost_estimate=SMALL,
+    )(starts, features, in_hbm(gate_weight), in_hbm(up_weight), after)
 
 
 def hidden_tail(rows, width):
@@ -146,17 +172,42 @@
     return half if rows % 8 else 0
 
 
-def activate_kernel(rows, width, summed, near, out):
-    def pair(at):
-        return summed[:, at : at + width] + near[:, at : at + width].astype(jnp.float32)
-
+def packed_width(rows, width):
+    return (rows // 8) * width + hidden_tail(rows, width)
+
+
+def pack_single(out, value):
+    rows, width = value.shape
     for g in range(rows // 8):
-        value = activate(pair(2 * g * width), pair((2 * g + 1) * width))
-        out[:, g * width : (g + 1) * width] = value
+        out[:, g * width : (g + 1) * width] = value[8 * g : 8 * g + 8].astype(out.dtype)
     if rows % 8:
-        last = pair((rows // 8) * 2 * width)
-        value = activate(last[:4], last[4:]).astype(jnp.float32)
-        half = hidden_tail(rows, width)
+        at, half = (rows // 8) * width, hidden_tail(rows, width)
+        left, right = value[rows - 4 :, :half], value[rows - 4 :, half:]
+        if 2 * half > width:
+            right = jnp.concatenate([right, jnp.zeros((4, 2 * half - width), jnp.float32)], axis=1)
+        out[:, at : at + half] = jnp.concatenate([left, right], axis=0).astype(out.dtype)
+
+
+def last_rows(packed, rows, width):
+    at, half = (rows // 8) * width, hidden_tail(rows, width)
+    tail = packed[:, at : at + half].astype(jnp.float32)
+    return jnp.concatenate([tail[:4], tail[4:, : width - half]], axis=1)
+
+
+def activate_kernel(rows, width, summed, gate_near, up_near, out):
+    for g in range(rows // 8):
+        near = slice(g * width, (g + 1) * width)
+        gate, up = ((2 * g + w) * width for w in range(2))
+        out[:, near] = activate(
+            summed[:, gate : gate + width] + gate_near[:, near].astype(jnp.float32),
+            summed[:, up : up + width] + up_near[:, near].astype(jnp.float32),
+        )
+    if rows % 8:
+        at, half = (rows // 8) * 2 * width, hidden_tail(rows, width)
+        value = activate(
+            summed[:4, at : at + width] + last_rows(gate_near, rows, width),
+            summed[4:, at : at + width] + last_rows(up_near, rows, width),
+        ).astype(jnp.float32)
         right = jnp.concatenate([value[:, half:], jnp.zeros((4, 2 * half - width), jnp.float32)], axis=1)
         at = (rows // 8) * width
         out[:, at : at + half] = jnp.concatenate([value[:, :half], right], axis=0).astype(out.dtype)
@@ -165,14 +216,12 @@
 def activate_packed(summed, near, rows, width):
     return pl.pallas_call(
         functools.partial(activate_kernel, rows, width),
-        out_shape=jax.ShapeDtypeStruct(
-            (8, (rows // 8) * width + hidden_tail(rows, width)), jnp.bfloat16
-        ),
-        in_specs=[WHOLE] * 2,
+        out_shape=jax.ShapeDtypeStruct((8, packed_width(rows, width)), jnp.bfloat16),
+        in_specs=[WHOLE] * 3,
         out_specs=WHOLE,
         compiler_params=params(8),
         cost_estimate=SMALL,
-    )(summed, near)
+    )(summed, *near)
 
 
 def pack_rows(out, value):
@@ -297,17 +346,18 @@
     )
     rows = features.shape[0]
 
-    def block_for(d, after):
-        return gate_up_stream(features, gate_weight, up_weight, starts_of(d), width, after)
+    def blocks_for(starts, blocks, after):
+        return gate_up_stream(features, gate_weight, up_weight, starts, blocks, width, after)
 
     relayed = gate_up_held(features, held)
     arrived = swap(relayed, "gx", n_gx, 1)
-    across = block_for(2, relayed)
+    across, beside = blocks_for(starts_of(2, 1), ((0, 1), (0,)), relayed)
     across = lax.optimization_barrier(add(across, arrived).astype(jnp.bfloat16))
     far = swap(across, "gx", n_gx, 2)
-    beside = block_for(1, across)
-    near = swap(beside, "gx", n_gx, 1)
-    own = block_for(0, beside)
+    near = [swap(beside, "gx", n_gx, 1)]
+    (beside,) = blocks_for(starts_of(1), ((1,),), across)
+    near.append(swap(beside, "gx", n_gx, 1))
+    (own,) = blocks_for(starts_of(0), ((0, 1),), beside)
     summed = lax.optimization_barrier(add(own, far))
     hidden = activate_packed(summed, near, rows, width)
 

time: 58.3 us -> 56.3 us (0.966)
  starting transfers between devices: 15.7 us -> 13 us
  Pallas kernels: 32 us -> 32.6 us
    ppermute x12 -> x13, starting transfers between devices: 15.7 us -> 13 us  [swap(): return lax.ppermute(value, axes, [(i, i ^ distance) for i in range(size)])]
    ppermute x12 -> x13, waiting for transfers between devices: 9.94 us -> 10 us  [swap(): return lax.ppermute(value, axes, [(i, i ^ distance) for i in range(size)])]
  transfers between devices with their start and end apart: 12 -> 13, of which waited for: 6 -> 6; matrix products, arithmetic and copies ran while one was open for 0% -> 0% of each run, Pallas kernels for 48% -> 50%
where the time goes in v11:
time: 56.3 us; the launch traced here: 56.2 us
  Pallas kernels  32.6 us (58%)
  starting transfers between devices  13 us (23%)
  waiting for transfers between devices  10 us (18%)
    pallas_call x3, Pallas kernels, gate_up_stream(): pl.pallas_call(functools.partial(stream_kernel, width, blocks), out_shape...  18.9 us
    ppermute x13, starting transfers between devices, swap(): return lax.ppermute(value, axes, [(i, i ^ distance) for i in range(size)])  13 us
    ppermute x13, waiting for transfers between devices, swap(): return lax.ppermute(value, axes, [(i, i ^ distance) for i in range(size)])  10 us
    pallas_call x2, Pallas kernels, down(): pl.pallas_call(functools.partial(down_kernel, before is None, rows, width...  5.48 us
    pallas_call x1, Pallas kernels, fetch(): pl.pallas_call(functools.partial(fetch_kernel, width), out_shape=pltpu.VM...  5.23 us
    pallas_call x1, Pallas kernels, gate_up_held(): pl.pallas_call(held_kernel, out_shape=jax.ShapeDtypeStruct((8, packed_pai...  2.15 us
  transfers between devices with their start and end apart: 13, of which 6 were waited for; matrix products, arithmetic and copies ran while one was open for 0% of the time, Pallas kernels for 50%

profile of v11, /device:TPU:0, one launch (start us, length us, event | category | flops | bytes accessed | tf_op | source)
XLA Modules:
  0.0 56.2 jit_solution(12426195699826380306)
XLA Ops:
  0.0 2.4 %collective-permute-start.2 = (bf16[9,2048]{1,0:T(8,128)(2,1)}, bf16[9,2048]{1,0:T(8,128)(2,1)S(1)}, u32[]{:S(2)}, u32[]{:S(2)}) collective-permute-start(bf16[9,2048]{1,0:T(8,128)(2,1)} %param.4), channel_id=1, source_target_pairs={{0,3},{1,2},{2,1},{3,0},{4,7},{5,6},{6,5},{7,4},{8,11},{9,10},{10,... | collective-permute-start | bytes 110600 | tf_op jit(solution)/shard_map/ppermute | solution.py:327
  2.4 0.6 %collective-permute-start.1 = (bf16[9,2048]{1,0:T(8,128)(2,1)}, bf16[9,2048]{1,0:T(8,128)(2,1)S(1)}, u32[]{:S(2)}, u32[]{:S(2)}) collective-permute-start(bf16[9,2048]{1,0:T(8,128)(2,1)} %param.4), channel_id=1, source_target_pairs={{0,2},{1,3},{2,0},{3,1},{4,6},{5,7},{6,4},{7,5},{8,10},{9,11},{10,... | collective-permute-start | bytes 110600 | tf_op jit(solution)/shard_map/ppermute | solution.py:327
  3.0 0.1 collective-permute-start
  3.1 0.0 copy-start
  3.1 5.2 %shard_map.46.held = bf16[2,2048,1664]{2,1,0:T(8,128)(2,1)S(1)} custom-call(s32[1]{0:T(128)} %bitcast.start_ref.starts, bf16[2048,6656]{1,0:T(8,128)(2,1)} %gate_ref.7, bf16[2048,6656]{1,0:T(8,128)(2,1)} %up_ref.7), custom_call_target="tpu_custom_call" | custom-call | bytes 1048576 | tf_op jit(solution)/shard_map/pallas_call | solution.py:81
  8.3 0.0 collective-permute-done.2
  8.3 0.0 collective-permute-done.1
  8.3 0.0 collective-permute-done
  8.3 0.0 copy-done
  8.3 0.1 pad_maximum_fusion.x_ref
  8.4 2.2 %shard_map.47._ = bf16[8,14976]{1,0:T(8,128)(2,1)S(1)} custom-call(bf16[36,2048]{1,0:T(8,128)(2,1)S(1)} %pad_maximum_fusion.x_ref, bf16[2,2048,1664]{2,1,0:T(8,128)(2,1)S(1)} %shard_map.46.held), custom_call_target="tpu_custom_call" | custom-call | bytes 1048576 | tf_op jit(solution)/shard_map/pallas_call | solution.py:115
  10.6 1.7 %collective-permute-start.3 = (bf16[8,14976]{1,0:T(8,128)(2,1)S(1)}, bf16[8,14976]{1,0:T(8,128)(2,1)S(1)}, u32[]{:S(2)}, u32[]{:S(2)}) collective-permute-start(bf16[8,14976]{1,0:T(8,128)(2,1)S(1)} %shard_map.47._), channel_id=1, source_target_pairs={{0,4},{4,0},{8,12},{12,8},{1,5},{5,1},{9,13},{13,9},{2,6},{6,2},{1... | collective-permute-start | bytes 718856 | tf_op jit(solution)/shard_map/ppermute | solution.py:327
  12.3 0.1 pad_add_fusion.starts
  12.4 8.7 %shard_map.48 = (bf16[8,14976]{1,0:T(8,128)(2,1)S(1)}, bf16[8,7552]{1,0:T(8,128)(2,1)S(1)}) custom-call(s32[2]{0:T(128)S(1)} %pad_add_fusion.starts, bf16[36,2048]{1,0:T(8,128)(2,1)S(1)} %pad_maximum_fusion.x_ref, bf16[2048,6656]{1,0:T(8,128)(2,1)} %gate_ref.7, bf16[2048,6656]{1,0:T(8,128)(2,1)} %up_ref.7, bf16[8,14976]{1,0:T(8,128)(2,1)S(1)} %shard_map.47._), custom_call_target="tpu_custom_call" | custom-call | bytes 1048576 | tf_op jit(solution)/shard_map/pallas_call | solution.py:159
  21.1 0.0 collective-permute-done.3
  21.1 0.1 add_convert_fusion._
  21.2 2.7 %collective-permute-start.4 = (bf16[8,14976]{1,0:T(8,128)(2,1)S(1)}, bf16[8,14976]{1,0:T(8,128)(2,1)S(1)}, u32[]{:S(2)}, u32[]{:S(2)}) collective-permute-start(bf16[8,14976]{1,0:T(8,128)(2,1)S(1)} %add_convert_fusion._), channel_id=1, source_target_pairs={{0,8},{4,12},{8,0},{12,4},{1,9},{5,13},{9,1},{13,5},{2,10},{6,14},... | collective-permute-start | bytes 718856 | tf_op jit(solution)/shard_map/ppermute | solution.py:327
  23.9 0.4 collective-permute-start.5
  24.3 0.0 slice-start
  24.3 0.0 slice-start.1
  24.3 0.0 slice-start.2
  24.3 0.0 slice-start.3
  24.3 3.6 %shard_map.49._ = bf16[8,7552]{1,0:T(8,128)(2,1)S(1)} custom-call(s32[1]{0:T(128)} %bitcast.2.starts, bf16[36,2048]{1,0:T(8,128)(2,1)S(1)} %pad_maximum_fusion.x_ref, bf16[2048,6656]{1,0:T(8,128)(2,1)} %gate_ref.7, bf16[2048,6656]{1,0:T(8,128)(2,1)} %up_ref.7, bf16[8,14976]{1,0:T(8,128)(2,1)S(1)} %add_convert_fusion._), custom_call_target="tpu_custom_call" | custom-call | bytes 1048576 | tf_op jit(solution)/shard_map/pallas_call | solution.py:159
  28.0 1.7 %collective-permute-start.6 = (bf16[8,7552]{1,0:T(8,128)(2,1)S(1)}, bf16[8,7552]{1,0:T(8,128)(2,1)S(1)}, u32[]{:S(2)}, u32[]{:S(2)}) collective-permute-start(bf16[8,7552]{1,0:T(8,128)(2,1)S(1)} %shard_map.49._), channel_id=1, source_target_pairs={{0,4},{4,0},{8,12},{12,8},{1,5},{5,1},{9,13},{13,9},{2,6},{6,2},{1... | collective-permute-start | bytes 362504 | tf_op jit(solution)/shard_map/ppermute | solution.py:327
  29.7 0.0 slice-start.4
  29.7 0.0 slice-start.5
  29.7 0.0 slice-start.6
  29.7 6.6 %shard_map.50 = bf16[8,14976]{1,0:T(8,128)(2,1)S(1)} custom-call(s32[1]{0:T(128)} %bitcast.1.starts, bf16[36,2048]{1,0:T(8,128)(2,1)S(1)} %pad_maximum_fusion.x_ref, bf16[2048,6656]{1,0:T(8,128)(2,1)} %gate_ref.7, bf16[2048,6656]{1,0:T(8,128)(2,1)} %up_ref.7, bf16[8,7552]{1,0:T(8,128)(2,1)S(1)} %shard_map.49._), custom_call_target="tpu_custom_call" | custom-call | bytes 1048576 | tf_op jit(solution)/shard_map/pallas_call | solution.py:159
  36.3 0.0 collective-permute-done.4
  36.3 0.1 convert_add_fusion.summed
  36.4 0.0 collective-permute-done.5.gate_near
  36.4 0.8 %collective-permute-done.6.up_near = bf16[8,7552]{1,0:T(8,128)(2,1)S(1)} collective-permute-done((bf16[8,7552]{1,0:T(8,128)(2,1)S(1)}, bf16[8,7552]{1,0:T(8,128)(2,1)S(1)}, u32[]{:S(2)}, u32[]{:S(2)}) %collective-permute-start.6) | collective-permute-done | bytes 120864 | tf_op jit(solution)/shard_map/ppermute | solution.py:327
  37.2 0.1 shard_map.51.refs_0_
  37.3 0.1 collective-permute-start.7
  37.3 1.4 %collective-permute-start.9 = (bf16[8,7552]{1,0:T(8,128)(2,1)S(1)}, bf16[8,7552]{1,0:T(8,128)(2,1)S(1)}, u32[]{:S(2)}, u32[]{:S(2)}) collective-permute-start(bf16[8,7552]{1,0:T(8,128)(2,1)S(1)} %shard_map.51.refs_0_), channel_id=1, source_target_pairs={{0,4},{4,0},{8,12},{12,8},{1,5},{5,1},{9,13},{13,9},{2,6},{6,2},{1... | collective-permute-start | bytes 362504 | tf_op jit(solution)/shard_map/ppermute | solution.py:327
  38.7 5.9 %collective-permute-done.7.refs_2_ = bf16[8,7552]{1,0:T(8,128)(2,1)S(1)} collective-permute-done((bf16[8,7552]{1,0:T(8,128)(2,1)S(1)}, bf16[8,7552]{1,0:T(8,128)(2,1)S(1)}, u32[]{:S(2)}, u32[]{:S(2)}) %collective-permute-start.7) | collective-permute-done | bytes 120864 | tf_op jit(solution)/shard_map/ppermute | solution.py:327
  44.6 0.0 collective-permute-start.8
  44.6 0.1 pad_add_fusion.1.starts
  44.7 0.1 collective-permute-done.9.refs_1_
  44.8 0.0 slice-done
  44.8 0.0 slice-done.1
  44.8 0.0 slice-done.2
  44.8 0.0 slice-done.3
  44.8 0.0 slice-done.4
  44.8 0.0 slice-done.5
  44.8 0.0 slice-done.6
  44.8 4.2 %shard_map.52.refs_1_ = f32[36,2048]{1,0:T(8,128)S(1)} custom-call(s32[3]{0:T(128)S(1)} %pad_add_fusion.1.starts, bf16[8,7552]{1,0:T(8,128)(2,1)S(1)} %shard_map.51.refs_0_, bf16[8,7552]{1,0:T(8,128)(2,1)S(1)} %collective-permute-done.9.refs_1_, bf16[8,7552]{1,0:T(8,128)(2,1)S(1)} %collective-permute-done.7.refs_2_, bf16[6656,2048]{1,0:T(8,128)(2,1)S(1)} %bitcast.5), custom_call_target="tpu_custom_call" | custom-call | bytes 1048576 | tf_op jit(solution)/shard_map/pallas_call | solution.py:291
  49.0 0.6 %collective-permute-done.8.refs_0_ = bf16[8,7552]{1,0:T(8,128)(2,1)S(1)} collective-permute-done((bf16[8,7552]{1,0:T(8,128)(2,1)S(1)}, bf16[8,7552]{1,0:T(8,128)(2,1)S(1)}, u32[]{:S(2)}, u32[]{:S(2)}) %collective-permute-start.8) | collective-permute-done | bytes 120864 | tf_op jit(solution)/shard_map/ppermute | solution.py:327
  49.6 1.3 %shard_map.53 = (f32[8,2304]{1,0:T(8,128)S(1)}, bf16[8,2304]{1,0:T(8,128)(2,1)S(1)}, bf16[8,2304]{1,0:T(8,128)(2,1)S(1)}, bf16[8,2304]{1,0:T(8,128)(2,1)S(1)}) custom-call(s32[1]{0:T(128)} %bitcast.start_ref.starts, bf16[8,7552]{1,0:T(8,128)(2,1)S(1)} %collective-permute-done.8.refs_0_, f32[36,2048]{1,0:T(8,128)S(1)} %shard_map.52.refs_1_, ...), custom_call_target="tpu_custom_call" | custom-call | bytes 1048576 | tf_op jit(solution)/shard_map/pallas_call | solution.py:291
  51.0 0.1 collective-permute-start.10
  51.0 1.0 %collective-permute-start.11 = (bf16[8,2304]{1,0:T(8,128)(2,1)S(1)}, bf16[8,2304]{1,0:T(8,128)(2,1)S(1)}, u32[]{:S(2)}, u32[]{:S(2)}) collective-permute-start(bf16[8,2304]{1,0:T(8,128)(2,1)S(1)} %get-tuple-element.15), channel_id=1, source_target_pairs={{0,2},{1,3},{2,0},{3,1},{4,6},{5,7},{6,4},{7,5},{8,10},{9,11},{10,... | collective-permute-start | bytes 110600 | tf_op jit(solution)/shard_map/ppermute | solution.py:327
  52.1 0.8 %collective-permute-start.12 = (bf16[8,2304]{1,0:T(8,128)(2,1)S(1)}, bf16[8,2304]{1,0:T(8,128)(2,1)S(1)}, u32[]{:S(2)}, u32[]{:S(2)}) collective-permute-start(bf16[8,2304]{1,0:T(8,128)(2,1)S(1)} %get-tuple-element.16), channel_id=1, source_target_pairs={{0,3},{1,2},{2,1},{3,0},{4,7},{5,6},{6,5},{7,4},{8,11},{9,10},{10,... | collective-permute-start | bytes 110600 | tf_op jit(solution)/shard_map/ppermute | solution.py:327
  52.9 0.0 collective-permute-done.10.refs_1_
  52.9 2.2 %collective-permute-done.11.refs_2_ = bf16[8,2304]{1,0:T(8,128)(2,1)S(1)} collective-permute-done((bf16[8,2304]{1,0:T(8,128)(2,1)S(1)}, bf16[8,2304]{1,0:T(8,128)(2,1)S(1)}, u32[]{:S(2)}, u32[]{:S(2)}) %collective-permute-start.11) | collective-permute-done | bytes 36896 | tf_op jit(solution)/shard_map/ppermute | solution.py:327
  55.1 0.4 collective-permute-done.12.refs_3_
  55.5 0.7 %shard_map.54 = bf16[9,2048]{1,0:T(8,128)(2,1)} custom-call(f32[8,2304]{1,0:T(8,128)S(1)} %get-tuple-element.13.refs_0_, bf16[8,2304]{1,0:T(8,128)(2,1)S(1)} %collective-permute-done.10.refs_1_, bf16[8,2304]{1,0:T(8,128)(2,1)S(1)} %collective-permute-done.11.refs_2_, bf16[8,2304]{1,0:T(8,128)(2,1)S(1)} %collective-permute-done.12.refs_3_), custom_call_target="tpu_custom_call" | custom-call | bytes 1048576 | tf_op jit(solution)/shard_map/pallas_call | solution.py:315
  (1 shorter events, 0.0 us)
Async XLA Ops:
  0.0 8.3 %collective-permute-start.2 = (bf16[9,2048]{1,0:T(8,128)(2,1)}, bf16[9,2048]{1,0:T(8,128)(2,1)S(1)}, u32[]{:S(2)}, u32[]{:S(2)}) collective-permute-start(bf16[9,2048]{1,0:T(8,128)(2,1)} %param.4), channel_id=1, source_target_pairs={{0,3},{1,2},{2,1},{3,0},{4,7},{5,6},{6,5},{7,4},{8,11},{9,10},{10,... | collective-permute-start | bytes 110600 | tf_op jit(solution)/shard_map/ppermute | solution.py:327
  2.4 5.9 %collective-permute-start.1 = (bf16[9,2048]{1,0:T(8,128)(2,1)}, bf16[9,2048]{1,0:T(8,128)(2,1)S(1)}, u32[]{:S(2)}, u32[]{:S(2)}) collective-permute-start(bf16[9,2048]{1,0:T(8,128)(2,1)} %param.4), channel_id=1, source_target_pairs={{0,2},{1,3},{2,0},{3,1},{4,6},{5,7},{6,4},{7,5},{8,10},{9,11},{10,... | collective-permute-start | bytes 110600 | tf_op jit(solution)/shard_map/ppermute | solution.py:327
  3.0 5.3 %collective-permute-start = (bf16[9,2048]{1,0:T(8,128)(2,1)}, bf16[9,2048]{1,0:T(8,128)(2,1)S(1)}, u32[]{:S(2)}, u32[]{:S(2)}) collective-permute-start(bf16[9,2048]{1,0:T(8,128)(2,1)} %param.4), channel_id=1, source_target_pairs={{0,1},{1,0},{2,3},{3,2},{4,5},{5,4},{6,7},{7,6},{8,9},{9,8},{10,11... | collective-permute-start | bytes 110600 | tf_op jit(solution)/shard_map/ppermute | solution.py:327
  3.1 5.3 %copy-start = (bf16[9,2048]{1,0:T(8,128)(2,1)S(1)}, bf16[9,2048]{1,0:T(8,128)(2,1)}, u32[]{:S(2)}) copy-start(bf16[9,2048]{1,0:T(8,128)(2,1)} %param.4) | copy-start | bytes 110596
  10.6 10.5 %collective-permute-start.3 = (bf16[8,14976]{1,0:T(8,128)(2,1)S(1)}, bf16[8,14976]{1,0:T(8,128)(2,1)S(1)}, u32[]{:S(2)}, u32[]{:S(2)}) collective-permute-start(bf16[8,14976]{1,0:T(8,128)(2,1)S(1)} %shard_map.47._), channel_id=1, source_target_pairs={{0,4},{4,0},{8,12},{12,8},{1,5},{5,1},{9,13},{13,9},{2,6},{6,2},{1... | collective-permute-start | bytes 718856 | tf_op jit(solution)/shard_map/ppermute | solution.py:327
  21.2 15.1 %collective-permute-start.4 = (bf16[8,14976]{1,0:T(8,128)(2,1)S(1)}, bf16[8,14976]{1,0:T(8,128)(2,1)S(1)}, u32[]{:S(2)}, u32[]{:S(2)}) collective-permute-start(bf16[8,14976]{1,0:T(8,128)(2,1)S(1)} %add_convert_fusion._), channel_id=1, source_target_pairs={{0,8},{4,12},{8,0},{12,4},{1,9},{5,13},{9,1},{13,5},{2,10},{6,14},... | collective-permute-start | bytes 718856 | tf_op jit(solution)/shard_map/ppermute | solution.py:327
  23.9 12.4 %collective-permute-start.5 = (bf16[8,7552]{1,0:T(8,128)(2,1)S(1)}, bf16[8,7552]{1,0:T(8,128)(2,1)S(1)}, u32[]{:S(2)}, u32[]{:S(2)}) collective-permute-start(bf16[8,7552]{1,0:T(8,128)(2,1)S(1)} %get-tuple-element.12), channel_id=1, source_target_pairs={{0,4},{4,0},{8,12},{12,8},{1,5},{5,1},{9,13},{13,9},{2,6},{6,2},{1... | collective-permute-start | bytes 362504 | tf_op jit(solution)/shard_map/ppermute | solution.py:327
  24.3 20.5 %slice-start = ((s8[27262976]{0:T(1024)(128)(4,1)}), s8[4194304]{0:T(1024)(128)(4,1)S(1)}, s32[]{:S(2)}) async-start(s8[27262976]{0:T(1024)(128)(4,1)} %bitcast.4), calls=%async_computation | async-start | bytes 8388608
  24.3 20.5 %slice-start.1 = ((s8[27262976]{0:T(1024)(128)(4,1)}), s8[4194304]{0:T(1024)(128)(4,1)S(1)}, s32[]{:S(2)}) async-start(s8[27262976]{0:T(1024)(128)(4,1)} %bitcast.4), calls=%async_computation.1 | async-start | bytes 8388608
  24.3 20.5 %slice-start.2 = ((s8[27262976]{0:T(1024)(128)(4,1)}), s8[4194304]{0:T(1024)(128)(4,1)S(1)}, s32[]{:S(2)}) async-start(s8[27262976]{0:T(1024)(128)(4,1)} %bitcast.4), calls=%async_computation.2 | async-start | bytes 8388608
  24.3 20.5 %slice-start.3 = ((s8[27262976]{0:T(1024)(128)(4,1)}), s8[4194304]{0:T(1024)(128)(4,1)S(1)}, s32[]{:S(2)}) async-start(s8[27262976]{0:T(1024)(128)(4,1)} %bitcast.4), calls=%async_computation.3 | async-start | bytes 8388608
  28.0 9.2 %collective-permute-start.6 = (bf16[8,7552]{1,0:T(8,128)(2,1)S(1)}, bf16[8,7552]{1,0:T(8,128)(2,1)S(1)}, u32[]{:S(2)}, u32[]{:S(2)}) collective-permute-start(bf16[8,7552]{1,0:T(8,128)(2,1)S(1)} %shard_map.49._), channel_id=1, source_target_pairs={{0,4},{4,0},{8,12},{12,8},{1,5},{5,1},{9,13},{13,9},{2,6},{6,2},{1... | collective-permute-start | bytes 362504 | tf_op jit(solution)/shard_map/ppermute | solution.py:327
  29.7 15.2 %slice-start.4 = ((s8[27262976]{0:T(1024)(128)(4,1)}), s8[4194304]{0:T(1024)(128)(4,1)S(1)}, s32[]{:S(2)}) async-start(s8[27262976]{0:T(1024)(128)(4,1)} %bitcast.4), calls=%async_computation.4 | async-start | bytes 8388608
  29.7 15.2 %slice-start.5 = ((s8[27262976]{0:T(1024)(128)(4,1)}), s8[4194304]{0:T(1024)(128)(4,1)S(1)}, s32[]{:S(2)}) async-start(s8[27262976]{0:T(1024)(128)(4,1)} %bitcast.4), calls=%async_computation.5 | async-start | bytes 8388608
  29.7 15.2 %slice-start.6 = ((s8[27262976]{0:T(1024)(128)(4,1)}), s8[2097152]{0:T(1024)(128)(4,1)S(1)}, s32[]{:S(2)}) async-start(s8[27262976]{0:T(1024)(128)(4,1)} %bitcast.4), calls=%async_computation.6 | async-start | bytes 4194304
  37.3 7.4 %collective-permute-start.7 = (bf16[8,7552]{1,0:T(8,128)(2,1)S(1)}, bf16[8,7552]{1,0:T(8,128)(2,1)S(1)}, u32[]{:S(2)}, u32[]{:S(2)}) collective-permute-start(bf16[8,7552]{1,0:T(8,128)(2,1)S(1)} %shard_map.51.refs_0_), channel_id=1, source_target_pairs={{0,8},{4,12},{8,0},{12,4},{1,9},{5,13},{9,1},{13,5},{2,10},{6,14},... | collective-permute-start | bytes 362504 | tf_op jit(solution)/shard_map/ppermute | solution.py:327
  37.3 7.4 %collective-permute-start.9 = (bf16[8,7552]{1,0:T(8,128)(2,1)S(1)}, bf16[8,7552]{1,0:T(8,128)(2,1)S(1)}, u32[]{:S(2)}, u32[]{:S(2)}) collective-permute-start(bf16[8,7552]{1,0:T(8,128)(2,1)S(1)} %shard_map.51.refs_0_), channel_id=1, source_target_pairs={{0,4},{4,0},{8,12},{12,8},{1,5},{5,1},{9,13},{13,9},{2,6},{6,2},{1... | collective-permute-start | bytes 362504 | tf_op jit(solution)/shard_map/ppermute | solution.py:327
  44.6 5.0 %collective-permute-start.8 = (bf16[8,7552]{1,0:T(8,128)(2,1)S(1)}, bf16[8,7552]{1,0:T(8,128)(2,1)S(1)}, u32[]{:S(2)}, u32[]{:S(2)}) collective-permute-start(bf16[8,7552]{1,0:T(8,128)(2,1)S(1)} %collective-permute-done.7.refs_2_), channel_id=1, source_target_pairs={{0,4},{4,0},{8,12},{12,8},{1,5},{5,1},{9,13},{13,9},{2,6},{6,2},{1... | collective-permute-start | bytes 362504 | tf_op jit(solution)/shard_map/ppermute | solution.py:327
  51.0 1.9 %collective-permute-start.10 = (bf16[8,2304]{1,0:T(8,128)(2,1)S(1)}, bf16[8,2304]{1,0:T(8,128)(2,1)S(1)}, u32[]{:S(2)}, u32[]{:S(2)}) collective-permute-start(bf16[8,2304]{1,0:T(8,128)(2,1)S(1)} %get-tuple-element.14), channel_id=1, source_target_pairs={{0,1},{1,0},{2,3},{3,2},{4,5},{5,4},{6,7},{7,6},{8,9},{9,8},{10,11... | collective-permute-start | bytes 110600 | tf_op jit(solution)/shard_map/ppermute | solution.py:327
  51.0 4.0 %collective-permute-start.11 = (bf16[8,2304]{1,0:T(8,128)(2,1)S(1)}, bf16[8,2304]{1,0:T(8,128)(2,1)S(1)}, u32[]{:S(2)}, u32[]{:S(2)}) collective-permute-start(bf16[8,2304]{1,0:T(8,128)(2,1)S(1)} %get-tuple-element.15), channel_id=1, source_target_pairs={{0,2},{1,3},{2,0},{3,1},{4,6},{5,7},{6,4},{7,5},{8,10},{9,11},{10,... | collective-permute-start | bytes 110600 | tf_op jit(solution)/shard_map/ppermute | solution.py:327
  52.1 3.4 %collective-permute-start.12 = (bf16[8,2304]{1,0:T(8,128)(2,1)S(1)}, bf16[8,2304]{1,0:T(8,128)(2,1)S(1)}, u32[]{:S(2)}, u32[]{:S(2)}) collective-permute-start(bf16[8,2304]{1,0:T(8,128)(2,1)S(1)} %get-tuple-element.16), channel_id=1, source_target_pairs={{0,3},{1,2},{2,1},{3,0},{4,7},{5,6},{6,5},{7,4},{8,11},{9,10},{10,... | collective-permute-start | bytes 110600 | tf_op jit(solution)/shard_map/ppermute | solution.py:327

commit v12 on v11

--- a/solution.py
+++ b/solution.py
@@ -9,7 +9,8 @@
 
 MIB = 1 << 20
 STEP = 256
-IN_FLIGHT = 8
+COPY_STEP = 512
+IN_FLIGHT = 6
 TOKEN_AXES = ("gy", "gz")
 IN_HBM = pl.BlockSpec(memory_space=pltpu.HBM)
 ANY = pl.BlockSpec(memory_space=pl.ANY)
@@ -59,7 +60,7 @@
 def block_copies(width, start, weights, held, sems):
     columns = pl.ds(pl.multiple_of(start, 128), width)
     copies = []
-    for k, (row, rows) in enumerate(pieces_of(held.shape[1], STEP)):
+    for k, (row, rows) in enumerate(pieces_of(held.shape[1], COPY_STEP)):
         for w, weight in enumerate(weights):
             copy = pltpu.make_async_copy(
                 weight.at[pl.ds(row, rows), columns], held.at[w, pl.ds(row, rows)], sems.at[w, k]
@@ -83,25 +84,25 @@
         out_shape=pltpu.VMEM((2, depth, width), jnp.bfloat16),
         in_specs=[SCALARS, IN_HBM, IN_HBM],
         out_specs=WHOLE,
-        scratch_shapes=[pltpu.SemaphoreType.DMA((2, len(pieces_of(depth, STEP))))],
+        scratch_shapes=[pltpu.SemaphoreType.DMA((2, len(pieces_of(depth, COPY_STEP))))],
         compiler_params=params(4),
         cost_estimate=SMALL,
     )(start, in_hbm(gate_weight), in_hbm(up_weight))
 
 
 def multiply(x_ref, held, total, steps, waiting=()):
-    for w, row, rows, copy in steps:
+    for w, first, tall, copy in steps:
         if copy is not None:
             copy.wait()
         if waiting:
             waiting.pop(0).start()
-        term = jnp.dot(
-            x_ref[:, row : row + rows], held[w, row : row + rows, :], preferred_element_type=jnp.float32
-        )
-        if row == 0:
-            total[w] = term
-        else:
-            total[w] += term
+        for row, rows in pieces_of(tall, STEP):
+            rows = slice(first + row, first + row + rows)
+            term = jnp.dot(x_ref[:, rows], held[w, rows, :], preferred_element_type=jnp.float32)
+            if rows.start == 0:
+                total[w] = term
+            else:
+                total[w] += term
 
 
 def held_kernel(x_ref, held, out, total):
@@ -153,7 +154,7 @@
         scratch += [
             pltpu.VMEM((len(which), depth, width), jnp.bfloat16),
             pltpu.VMEM((len(which), rows, width), jnp.float32),
-            pltpu.SemaphoreType.DMA((len(which), len(pieces_of(depth, STEP)))),
+            pltpu.SemaphoreType.DMA((len(which), len(pieces_of(depth, COPY_STEP)))),
         ]
     held_mib = -(-depth * width * 2 * sum(len(which) for which in blocks) // MIB)
     return pl.pallas_call(

time: 56.3 us -> 55.6 us (0.988)
  Pallas kernels: 32.6 us -> 31.5 us
    pallas_call x3, Pallas kernels: 18.9 us -> 17.9 us  [gate_up_stream(): pl.pallas_call(functools.partial(stream_kernel, width, blocks), out_shape...]
  transfers between devices with their start and end apart: 13 -> 13, of which waited for: 6 -> 6; matrix products, arithmetic and copies ran while one was open for 0% -> 0% of each run, Pallas kernels for 50% -> 49%
where the time goes in v12:
time: 55.6 us; the launch traced here: 55.5 us
  Pallas kernels  31.5 us (57%)
  starting transfers between devices  13 us (23%)
  waiting for transfers between devices  10.4 us (19%)
    pallas_call x3, Pallas kernels, gate_up_stream(): pl.pallas_call(functools.partial(stream_kernel, width, blocks), out_shape...  17.9 us
    ppermute x13, starting transfers between devices, swap(): return lax.ppermute(value, axes, [(i, i ^ distance) for i in range(size)])  13 us
    ppermute x13, waiting for transfers between devices, swap(): return lax.ppermute(value, axes, [(i, i ^ distance) for i in range(size)])  10.4 us
    pallas_call x2, Pallas kernels, down(): pl.pallas_call(functools.partial(down_kernel, before is None, rows, width...  5.48 us
    pallas_call x1, Pallas kernels, fetch(): pl.pallas_call(functools.partial(fetch_kernel, width), out_shape=pltpu.VM...  5.16 us
    pallas_call x1, Pallas kernels, gate_up_held(): pl.pallas_call(held_kernel, out_shape=jax.ShapeDtypeStruct((8, packed_pai...  2.15 us
  transfers between devices with their start and end apart: 13, of which 6 were waited for; matrix products, arithmetic and copies ran while one was open for 0% of the time, Pallas kernels for 49%

profile of v12, /device:TPU:0, one launch (start us, length us, event | category | flops | bytes accessed | tf_op | source)
XLA Modules:
  0.0 55.5 jit_solution(3640350926837547128)
XLA Ops:
  0.0 2.4 %collective-permute-start.2 = (bf16[9,2048]{1,0:T(8,128)(2,1)}, bf16[9,2048]{1,0:T(8,128)(2,1)S(1)}, u32[]{:S(2)}, u32[]{:S(2)}) collective-permute-start(bf16[9,2048]{1,0:T(8,128)(2,1)} %param.4), channel_id=1, source_target_pairs={{0,3},{1,2},{2,1},{3,0},{4,7},{5,6},{6,5},{7,4},{8,11},{9,10},{10,... | collective-permute-start | bytes 110600 | tf_op jit(solution)/shard_map/ppermute | solution.py:328
  2.4 0.6 %collective-permute-start.1 = (bf16[9,2048]{1,0:T(8,128)(2,1)}, bf16[9,2048]{1,0:T(8,128)(2,1)S(1)}, u32[]{:S(2)}, u32[]{:S(2)}) collective-permute-start(bf16[9,2048]{1,0:T(8,128)(2,1)} %param.4), channel_id=1, source_target_pairs={{0,2},{1,3},{2,0},{3,1},{4,6},{5,7},{6,4},{7,5},{8,10},{9,11},{10,... | collective-permute-start | bytes 110600 | tf_op jit(solution)/shard_map/ppermute | solution.py:328
  3.0 0.1 collective-permute-start
  3.1 0.0 copy-start
  3.1 5.2 %shard_map.46.held = bf16[2,2048,1664]{2,1,0:T(8,128)(2,1)S(1)} custom-call(s32[1]{0:T(128)} %bitcast.start_ref.starts, bf16[2048,6656]{1,0:T(8,128)(2,1)} %gate_ref.7, bf16[2048,6656]{1,0:T(8,128)(2,1)} %up_ref.7), custom_call_target="tpu_custom_call" | custom-call | bytes 1048576 | tf_op jit(solution)/shard_map/pallas_call | solution.py:82
  8.2 0.0 collective-permute-done.2
  8.2 0.0 collective-permute-done.1
  8.2 0.0 collective-permute-done
  8.3 0.0 copy-done
  8.3 0.1 pad_maximum_fusion.x_ref
  8.4 2.1 %shard_map.47._ = bf16[8,14976]{1,0:T(8,128)(2,1)S(1)} custom-call(bf16[36,2048]{1,0:T(8,128)(2,1)S(1)} %pad_maximum_fusion.x_ref, bf16[2,2048,1664]{2,1,0:T(8,128)(2,1)S(1)} %shard_map.46.held), custom_call_target="tpu_custom_call" | custom-call | bytes 1048576 | tf_op jit(solution)/shard_map/pallas_call | solution.py:116
  10.5 1.8 %collective-permute-start.3 = (bf16[8,14976]{1,0:T(8,128)(2,1)S(1)}, bf16[8,14976]{1,0:T(8,128)(2,1)S(1)}, u32[]{:S(2)}, u32[]{:S(2)}) collective-permute-start(bf16[8,14976]{1,0:T(8,128)(2,1)S(1)} %shard_map.47._), channel_id=1, source_target_pairs={{0,4},{4,0},{8,12},{12,8},{1,5},{5,1},{9,13},{13,9},{2,6},{6,2},{1... | collective-permute-start | bytes 718856 | tf_op jit(solution)/shard_map/ppermute | solution.py:328
  12.3 0.1 pad_add_fusion.starts
  12.4 8.1 %shard_map.48 = (bf16[8,14976]{1,0:T(8,128)(2,1)S(1)}, bf16[8,7552]{1,0:T(8,128)(2,1)S(1)}) custom-call(s32[2]{0:T(128)S(1)} %pad_add_fusion.starts, bf16[36,2048]{1,0:T(8,128)(2,1)S(1)} %pad_maximum_fusion.x_ref, bf16[2048,6656]{1,0:T(8,128)(2,1)} %gate_ref.7, bf16[2048,6656]{1,0:T(8,128)(2,1)} %up_ref.7, bf16[8,14976]{1,0:T(8,128)(2,1)S(1)} %shard_map.47._), custom_call_target="tpu_custom_call" | custom-call | bytes 1048576 | tf_op jit(solution)/shard_map/pallas_call | solution.py:160
  20.5 0.0 collective-permute-done.3
  20.5 0.1 add_convert_fusion._
  20.6 2.7 %collective-permute-start.4 = (bf16[8,14976]{1,0:T(8,128)(2,1)S(1)}, bf16[8,14976]{1,0:T(8,128)(2,1)S(1)}, u32[]{:S(2)}, u32[]{:S(2)}) collective-permute-start(bf16[8,14976]{1,0:T(8,128)(2,1)S(1)} %add_convert_fusion._), channel_id=1, source_target_pairs={{0,8},{4,12},{8,0},{12,4},{1,9},{5,13},{9,1},{13,5},{2,10},{6,14},... | collective-permute-start | bytes 718856 | tf_op jit(solution)/shard_map/ppermute | solution.py:328
  23.3 0.4 collective-permute-start.5
  23.7 0.0 slice-start
  23.7 0.0 slice-start.1
  23.7 0.0 slice-start.2
  23.7 0.0 slice-start.3
  23.7 3.6 %shard_map.49._ = bf16[8,7552]{1,0:T(8,128)(2,1)S(1)} custom-call(s32[1]{0:T(128)} %bitcast.2.starts, bf16[36,2048]{1,0:T(8,128)(2,1)S(1)} %pad_maximum_fusion.x_ref, bf16[2048,6656]{1,0:T(8,128)(2,1)} %gate_ref.7, bf16[2048,6656]{1,0:T(8,128)(2,1)} %up_ref.7, bf16[8,14976]{1,0:T(8,128)(2,1)S(1)} %add_convert_fusion._), custom_call_target="tpu_custom_call" | custom-call | bytes 1048576 | tf_op jit(solution)/shard_map/pallas_call | solution.py:160
  27.3 1.7 %collective-permute-start.6 = (bf16[8,7552]{1,0:T(8,128)(2,1)S(1)}, bf16[8,7552]{1,0:T(8,128)(2,1)S(1)}, u32[]{:S(2)}, u32[]{:S(2)}) collective-permute-start(bf16[8,7552]{1,0:T(8,128)(2,1)S(1)} %shard_map.49._), channel_id=1, source_target_pairs={{0,4},{4,0},{8,12},{12,8},{1,5},{5,1},{9,13},{13,9},{2,6},{6,2},{1... | collective-permute-start | bytes 362504 | tf_op jit(solution)/shard_map/ppermute | solution.py:328
  29.0 0.0 slice-start.4
  29.0 0.0 slice-start.5
  29.0 0.0 slice-start.6
  29.0 6.2 %shard_map.50 = bf16[8,14976]{1,0:T(8,128)(2,1)S(1)} custom-call(s32[1]{0:T(128)} %bitcast.1.starts, bf16[36,2048]{1,0:T(8,128)(2,1)S(1)} %pad_maximum_fusion.x_ref, bf16[2048,6656]{1,0:T(8,128)(2,1)} %gate_ref.7, bf16[2048,6656]{1,0:T(8,128)(2,1)} %up_ref.7, bf16[8,7552]{1,0:T(8,128)(2,1)S(1)} %shard_map.49._), custom_call_target="tpu_custom_call" | custom-call | bytes 1048576 | tf_op jit(solution)/shard_map/pallas_call | solution.py:160
  35.2 0.0 collective-permute-done.4
  35.2 0.1 convert_add_fusion.summed
  35.3 0.0 collective-permute-done.5.gate_near
  35.3 1.2 %collective-permute-done.6.up_near = bf16[8,7552]{1,0:T(8,128)(2,1)S(1)} collective-permute-done((bf16[8,7552]{1,0:T(8,128)(2,1)S(1)}, bf16[8,7552]{1,0:T(8,128)(2,1)S(1)}, u32[]{:S(2)}, u32[]{:S(2)}) %collective-permute-start.6) | collective-permute-done | bytes 120864 | tf_op jit(solution)/shard_map/ppermute | solution.py:328
  36.5 0.1 shard_map.51.refs_0_
  36.6 0.1 collective-permute-start.7
  36.7 1.4 %collective-permute-start.9 = (bf16[8,7552]{1,0:T(8,128)(2,1)S(1)}, bf16[8,7552]{1,0:T(8,128)(2,1)S(1)}, u32[]{:S(2)}, u32[]{:S(2)}) collective-permute-start(bf16[8,7552]{1,0:T(8,128)(2,1)S(1)} %shard_map.51.refs_0_), channel_id=1, source_target_pairs={{0,4},{4,0},{8,12},{12,8},{1,5},{5,1},{9,13},{13,9},{2,6},{6,2},{1... | collective-permute-start | bytes 362504 | tf_op jit(solution)/shard_map/ppermute | solution.py:328
  38.1 5.9 %collective-permute-done.7.refs_2_ = bf16[8,7552]{1,0:T(8,128)(2,1)S(1)} collective-permute-done((bf16[8,7552]{1,0:T(8,128)(2,1)S(1)}, bf16[8,7552]{1,0:T(8,128)(2,1)S(1)}, u32[]{:S(2)}, u32[]{:S(2)}) %collective-permute-start.7) | collective-permute-done | bytes 120864 | tf_op jit(solution)/shard_map/ppermute | solution.py:328
  44.0 0.0 collective-permute-start.8
  44.0 0.1 pad_add_fusion.1.starts
  44.1 0.1 collective-permute-done.9.refs_1_
  44.1 0.0 slice-done
  44.1 0.0 slice-done.1
  44.1 0.0 slice-done.2
  44.1 0.0 slice-done.3
  44.1 0.0 slice-done.4
  44.1 0.0 slice-done.5
  44.2 0.0 slice-done.6
  44.2 4.2 %shard_map.52.refs_1_ = f32[36,2048]{1,0:T(8,128)S(1)} custom-call(s32[3]{0:T(128)S(1)} %pad_add_fusion.1.starts, bf16[8,7552]{1,0:T(8,128)(2,1)S(1)} %shard_map.51.refs_0_, bf16[8,7552]{1,0:T(8,128)(2,1)S(1)} %collective-permute-done.9.refs_1_, bf16[8,7552]{1,0:T(8,128)(2,1)S(1)} %collective-permute-done.7.refs_2_, bf16[6656,2048]{1,0:T(8,128)(2,1)S(1)} %bitcast.5), custom_call_target="tpu_custom_call" | custom-call | bytes 1048576 | tf_op jit(solution)/shard_map/pallas_call | solution.py:292
  48.4 0.6 %collective-permute-done.8.refs_0_ = bf16[8,7552]{1,0:T(8,128)(2,1)S(1)} collective-permute-done((bf16[8,7552]{1,0:T(8,128)(2,1)S(1)}, bf16[8,7552]{1,0:T(8,128)(2,1)S(1)}, u32[]{:S(2)}, u32[]{:S(2)}) %collective-permute-start.8) | collective-permute-done | bytes 120864 | tf_op jit(solution)/shard_map/ppermute | solution.py:328
  48.9 1.3 %shard_map.53 = (f32[8,2304]{1,0:T(8,128)S(1)}, bf16[8,2304]{1,0:T(8,128)(2,1)S(1)}, bf16[8,2304]{1,0:T(8,128)(2,1)S(1)}, bf16[8,2304]{1,0:T(8,128)(2,1)S(1)}) custom-call(s32[1]{0:T(128)} %bitcast.start_ref.starts, bf16[8,7552]{1,0:T(8,128)(2,1)S(1)} %collective-permute-done.8.refs_0_, f32[36,2048]{1,0:T(8,128)S(1)} %shard_map.52.refs_1_, ...), custom_call_target="tpu_custom_call" | custom-call | bytes 1048576 | tf_op jit(solution)/shard_map/pallas_call | solution.py:292
  50.3 0.1 collective-permute-start.10
  50.3 1.1 %collective-permute-start.11 = (bf16[8,2304]{1,0:T(8,128)(2,1)S(1)}, bf16[8,2304]{1,0:T(8,128)(2,1)S(1)}, u32[]{:S(2)}, u32[]{:S(2)}) collective-permute-start(bf16[8,2304]{1,0:T(8,128)(2,1)S(1)} %get-tuple-element.15), channel_id=1, source_target_pairs={{0,2},{1,3},{2,0},{3,1},{4,6},{5,7},{6,4},{7,5},{8,10},{9,11},{10,... | collective-permute-start | bytes 110600 | tf_op jit(solution)/shard_map/ppermute | solution.py:328
  51.4 0.8 %collective-permute-start.12 = (bf16[8,2304]{1,0:T(8,128)(2,1)S(1)}, bf16[8,2304]{1,0:T(8,128)(2,1)S(1)}, u32[]{:S(2)}, u32[]{:S(2)}) collective-permute-start(bf16[8,2304]{1,0:T(8,128)(2,1)S(1)} %get-tuple-element.16), channel_id=1, source_target_pairs={{0,3},{1,2},{2,1},{3,0},{4,7},{5,6},{6,5},{7,4},{8,11},{9,10},{10,... | collective-permute-start | bytes 110600 | tf_op jit(solution)/shard_map/ppermute | solution.py:328
  52.2 0.0 collective-permute-done.10.refs_1_
  52.2 2.2 %collective-permute-done.11.refs_2_ = bf16[8,2304]{1,0:T(8,128)(2,1)S(1)} collective-permute-done((bf16[8,2304]{1,0:T(8,128)(2,1)S(1)}, bf16[8,2304]{1,0:T(8,128)(2,1)S(1)}, u32[]{:S(2)}, u32[]{:S(2)}) %collective-permute-start.11) | collective-permute-done | bytes 36896 | tf_op jit(solution)/shard_map/ppermute | solution.py:328
  54.4 0.5 collective-permute-done.12.refs_3_
  54.8 0.7 %shard_map.54 = bf16[9,2048]{1,0:T(8,128)(2,1)} custom-call(f32[8,2304]{1,0:T(8,128)S(1)} %get-tuple-element.13.refs_0_, bf16[8,2304]{1,0:T(8,128)(2,1)S(1)} %collective-permute-done.10.refs_1_, bf16[8,2304]{1,0:T(8,128)(2,1)S(1)} %collective-permute-done.11.refs_2_, bf16[8,2304]{1,0:T(8,128)(2,1)S(1)} %collective-permute-done.12.refs_3_), custom_call_target="tpu_custom_call" | custom-call | bytes 1048576 | tf_op jit(solution)/shard_map/pallas_call | solution.py:316
  (1 shorter events, 0.0 us)
Async XLA Ops:
  0.0 8.2 %collective-permute-start.2 = (bf16[9,2048]{1,0:T(8,128)(2,1)}, bf16[9,2048]{1,0:T(8,128)(2,1)S(1)}, u32[]{:S(2)}, u32[]{:S(2)}) collective-permute-start(bf16[9,2048]{1,0:T(8,128)(2,1)} %param.4), channel_id=1, source_target_pairs={{0,3},{1,2},{2,1},{3,0},{4,7},{5,6},{6,5},{7,4},{8,11},{9,10},{10,... | collective-permute-start | bytes 110600 | tf_op jit(solution)/shard_map/ppermute | solution.py:328
  2.4 5.9 %collective-permute-start.1 = (bf16[9,2048]{1,0:T(8,128)(2,1)}, bf16[9,2048]{1,0:T(8,128)(2,1)S(1)}, u32[]{:S(2)}, u32[]{:S(2)}) collective-permute-start(bf16[9,2048]{1,0:T(8,128)(2,1)} %param.4), channel_id=1, source_target_pairs={{0,2},{1,3},{2,0},{3,1},{4,6},{5,7},{6,4},{7,5},{8,10},{9,11},{10,... | collective-permute-start | bytes 110600 | tf_op jit(solution)/shard_map/ppermute | solution.py:328
  3.0 5.3 %collective-permute-start = (bf16[9,2048]{1,0:T(8,128)(2,1)}, bf16[9,2048]{1,0:T(8,128)(2,1)S(1)}, u32[]{:S(2)}, u32[]{:S(2)}) collective-permute-start(bf16[9,2048]{1,0:T(8,128)(2,1)} %param.4), channel_id=1, source_target_pairs={{0,1},{1,0},{2,3},{3,2},{4,5},{5,4},{6,7},{7,6},{8,9},{9,8},{10,11... | collective-permute-start | bytes 110600 | tf_op jit(solution)/shard_map/ppermute | solution.py:328
  3.1 5.2 %copy-start = (bf16[9,2048]{1,0:T(8,128)(2,1)S(1)}, bf16[9,2048]{1,0:T(8,128)(2,1)}, u32[]{:S(2)}) copy-start(bf16[9,2048]{1,0:T(8,128)(2,1)} %param.4) | copy-start | bytes 110596
  10.5 10.0 %collective-permute-start.3 = (bf16[8,14976]{1,0:T(8,128)(2,1)S(1)}, bf16[8,14976]{1,0:T(8,128)(2,1)S(1)}, u32[]{:S(2)}, u32[]{:S(2)}) collective-permute-start(bf16[8,14976]{1,0:T(8,128)(2,1)S(1)} %shard_map.47._), channel_id=1, source_target_pairs={{0,4},{4,0},{8,12},{12,8},{1,5},{5,1},{9,13},{13,9},{2,6},{6,2},{1... | collective-permute-start | bytes 718856 | tf_op jit(solution)/shard_map/ppermute | solution.py:328
  20.6 14.6 %collective-permute-start.4 = (bf16[8,14976]{1,0:T(8,128)(2,1)S(1)}, bf16[8,14976]{1,0:T(8,128)(2,1)S(1)}, u32[]{:S(2)}, u32[]{:S(2)}) collective-permute-start(bf16[8,14976]{1,0:T(8,128)(2,1)S(1)} %add_convert_fusion._), channel_id=1, source_target_pairs={{0,8},{4,12},{8,0},{12,4},{1,9},{5,13},{9,1},{13,5},{2,10},{6,14},... | collective-permute-start | bytes 718856 | tf_op jit(solution)/shard_map/ppermute | solution.py:328
  23.3 12.0 %collective-permute-start.5 = (bf16[8,7552]{1,0:T(8,128)(2,1)S(1)}, bf16[8,7552]{1,0:T(8,128)(2,1)S(1)}, u32[]{:S(2)}, u32[]{:S(2)}) collective-permute-start(bf16[8,7552]{1,0:T(8,128)(2,1)S(1)} %get-tuple-element.12), channel_id=1, source_target_pairs={{0,4},{4,0},{8,12},{12,8},{1,5},{5,1},{9,13},{13,9},{2,6},{6,2},{1... | collective-permute-start | bytes 362504 | tf_op jit(solution)/shard_map/ppermute | solution.py:328
  23.7 20.4 %slice-start = ((s8[27262976]{0:T(1024)(128)(4,1)}), s8[4194304]{0:T(1024)(128)(4,1)S(1)}, s32[]{:S(2)}) async-start(s8[27262976]{0:T(1024)(128)(4,1)} %bitcast.4), calls=%async_computation | async-start | bytes 8388608
  23.7 20.4 %slice-start.1 = ((s8[27262976]{0:T(1024)(128)(4,1)}), s8[4194304]{0:T(1024)(128)(4,1)S(1)}, s32[]{:S(2)}) async-start(s8[27262976]{0:T(1024)(128)(4,1)} %bitcast.4), calls=%async_computation.1 | async-start | bytes 8388608
  23.7 20.4 %slice-start.2 = ((s8[27262976]{0:T(1024)(128)(4,1)}), s8[4194304]{0:T(1024)(128)(4,1)S(1)}, s32[]{:S(2)}) async-start(s8[27262976]{0:T(1024)(128)(4,1)} %bitcast.4), calls=%async_computation.2 | async-start | bytes 8388608
  23.7 20.4 %slice-start.3 = ((s8[27262976]{0:T(1024)(128)(4,1)}), s8[4194304]{0:T(1024)(128)(4,1)S(1)}, s32[]{:S(2)}) async-start(s8[27262976]{0:T(1024)(128)(4,1)} %bitcast.4), calls=%async_computation.3 | async-start | bytes 8388608
  27.3 9.2 %collective-permute-start.6 = (bf16[8,7552]{1,0:T(8,128)(2,1)S(1)}, bf16[8,7552]{1,0:T(8,128)(2,1)S(1)}, u32[]{:S(2)}, u32[]{:S(2)}) collective-permute-start(bf16[8,7552]{1,0:T(8,128)(2,1)S(1)} %shard_map.49._), channel_id=1, source_target_pairs={{0,4},{4,0},{8,12},{12,8},{1,5},{5,1},{9,13},{13,9},{2,6},{6,2},{1... | collective-permute-start | bytes 362504 | tf_op jit(solution)/shard_map/ppermute | solution.py:328
  29.0 15.2 %slice-start.4 = ((s8[27262976]{0:T(1024)(128)(4,1)}), s8[4194304]{0:T(1024)(128)(4,1)S(1)}, s32[]{:S(2)}) async-start(s8[27262976]{0:T(1024)(128)(4,1)} %bitcast.4), calls=%async_computation.4 | async-start | bytes 8388608
  29.0 15.2 %slice-start.5 = ((s8[27262976]{0:T(1024)(128)(4,1)}), s8[4194304]{0:T(1024)(128)(4,1)S(1)}, s32[]{:S(2)}) async-start(s8[27262976]{0:T(1024)(128)(4,1)} %bitcast.4), calls=%async_computation.5 | async-start | bytes 8388608
  29.0 15.2 %slice-start.6 = ((s8[27262976]{0:T(1024)(128)(4,1)}), s8[2097152]{0:T(1024)(128)(4,1)S(1)}, s32[]{:S(2)}) async-start(s8[27262976]{0:T(1024)(128)(4,1)} %bitcast.4), calls=%async_computation.6 | async-start | bytes 4194304
  36.6 7.3 %collective-permute-start.7 = (bf16[8,7552]{1,0:T(8,128)(2,1)S(1)}, bf16[8,7552]{1,0:T(8,128)(2,1)S(1)}, u32[]{:S(2)}, u32[]{:S(2)}) collective-permute-start(bf16[8,7552]{1,0:T(8,128)(2,1)S(1)} %shard_map.51.refs_0_), channel_id=1, source_target_pairs={{0,8},{4,12},{8,0},{12,4},{1,9},{5,13},{9,1},{13,5},{2,10},{6,14},... | collective-permute-start | bytes 362504 | tf_op jit(solution)/shard_map/ppermute | solution.py:328
  36.7 7.4 %collective-permute-start.9 = (bf16[8,7552]{1,0:T(8,128)(2,1)S(1)}, bf16[8,7552]{1,0:T(8,128)(2,1)S(1)}, u32[]{:S(2)}, u32[]{:S(2)}) collective-permute-start(bf16[8,7552]{1,0:T(8,128)(2,1)S(1)} %shard_map.51.refs_0_), channel_id=1, source_target_pairs={{0,4},{4,0},{8,12},{12,8},{1,5},{5,1},{9,13},{13,9},{2,6},{6,2},{1... | collective-permute-start | bytes 362504 | tf_op jit(solution)/shard_map/ppermute | solution.py:328
  44.0 5.0 %collective-permute-start.8 = (bf16[8,7552]{1,0:T(8,128)(2,1)S(1)}, bf16[8,7552]{1,0:T(8,128)(2,1)S(1)}, u32[]{:S(2)}, u32[]{:S(2)}) collective-permute-start(bf16[8,7552]{1,0:T(8,128)(2,1)S(1)} %collective-permute-done.7.refs_2_), channel_id=1, source_target_pairs={{0,4},{4,0},{8,12},{12,8},{1,5},{5,1},{9,13},{13,9},{2,6},{6,2},{1... | collective-permute-start | bytes 362504 | tf_op jit(solution)/shard_map/ppermute | solution.py:328
  50.3 1.9 %collective-permute-start.10 = (bf16[8,2304]{1,0:T(8,128)(2,1)S(1)}, bf16[8,2304]{1,0:T(8,128)(2,1)S(1)}, u32[]{:S(2)}, u32[]{:S(2)}) collective-permute-start(bf16[8,2304]{1,0:T(8,128)(2,1)S(1)} %get-tuple-element.14), channel_id=1, source_target_pairs={{0,1},{1,0},{2,3},{3,2},{4,5},{5,4},{6,7},{7,6},{8,9},{9,8},{10,11... | collective-permute-start | bytes 110600 | tf_op jit(solution)/shard_map/ppermute | solution.py:328
  50.3 4.0 %collective-permute-start.11 = (bf16[8,2304]{1,0:T(8,128)(2,1)S(1)}, bf16[8,2304]{1,0:T(8,128)(2,1)S(1)}, u32[]{:S(2)}, u32[]{:S(2)}) collective-permute-start(bf16[8,2304]{1,0:T(8,128)(2,1)S(1)} %get-tuple-element.15), channel_id=1, source_target_pairs={{0,2},{1,3},{2,0},{3,1},{4,6},{5,7},{6,4},{7,5},{8,10},{9,11},{10,... | collective-permute-start | bytes 110600 | tf_op jit(solution)/shard_map/ppermute | solution.py:328
  51.4 3.4 %collective-permute-start.12 = (bf16[8,2304]{1,0:T(8,128)(2,1)S(1)}, bf16[8,2304]{1,0:T(8,128)(2,1)S(1)}, u32[]{:S(2)}, u32[]{:S(2)}) collective-permute-start(bf16[8,2304]{1,0:T(8,128)(2,1)S(1)} %get-tuple-element.16), channel_id=1, source_target_pairs={{0,3},{1,2},{2,1},{3,0},{4,7},{5,6},{6,5},{7,4},{8,11},{9,10},{10,... | collective-permute-start | bytes 110600 | tf_op jit(solution)/shard_map/ppermute | solution.py:328

commit v13 on v12

--- a/solution.py
+++ b/solution.py
@@ -57,20 +57,26 @@
         out[:, at : at + width] = tail.astype(out.dtype)
 
 
-def block_copies(width, start, weights, held, sems):
+def block_copies(width, start, weights, first, held, sems):
     columns = pl.ds(pl.multiple_of(start, 128), width)
     copies = []
     for k, (row, rows) in enumerate(pieces_of(held.shape[1], COPY_STEP)):
         for w, weight in enumerate(weights):
             copy = pltpu.make_async_copy(
-                weight.at[pl.ds(row, rows), columns], held.at[w, pl.ds(row, rows)], sems.at[w, k]
+                weight.at[pl.ds(first + row, rows), columns],
+                held.at[w, pl.ds(row, rows)],
+                sems.at[w, k],
             )
             copies.append((w, row, rows, copy))
     return copies
 
 
+def copy_sems(weights, depth):
+    return pltpu.SemaphoreType.DMA((weights, len(pieces_of(depth, COPY_STEP))))
+
+
 def fetch_kernel(width, start_ref, gate_ref, up_ref, held, sems):
-    copies = block_copies(width, start_ref[0], (gate_ref, up_ref), held, sems)
+    copies = block_copies(width, start_ref[0], (gate_ref, up_ref), 0, held, sems)
     for _, _, _, copy in copies:
         copy.start()
     for _, _, _, copy in copies:
@@ -84,88 +90,111 @@
         out_shape=pltpu.VMEM((2, depth, width), jnp.bfloat16),
         in_specs=[SCALARS, IN_HBM, IN_HBM],
         out_specs=WHOLE,
-        scratch_shapes=[pltpu.SemaphoreType.DMA((2, len(pieces_of(depth, COPY_STEP))))],
+        scratch_shapes=[copy_sems(2, depth)],
         compiler_params=params(4),
         cost_estimate=SMALL,
     )(start, in_hbm(gate_weight), in_hbm(up_weight))
 
 
-def multiply(x_ref, held, total, steps, waiting=()):
-    for w, first, tall, copy in steps:
+def multiply(x_ref, first, held, total, steps, waiting=()):
+    for w, top, tall, copy in steps:
         if copy is not None:
             copy.wait()
         if waiting:
             waiting.pop(0).start()
         for row, rows in pieces_of(tall, STEP):
-            rows = slice(first + row, first + row + rows)
-            term = jnp.dot(x_ref[:, rows], held[w, rows, :], preferred_element_type=jnp.float32)
-            if rows.start == 0:
+            at, rows = first + top + row, slice(top + row, top + row + rows)
+            term = jnp.dot(
+                x_ref[:, at : at + rows.stop - rows.start],
+                held[w, rows, :],
+                preferred_element_type=jnp.float32,
+            )
+            if at == 0:
                 total[w] = term
             else:
                 total[w] += term
 
 
-def held_kernel(x_ref, held, out, total):
-    parts = pieces_of(x_ref.shape[1], STEP)
-    multiply(x_ref, held, total, [(w, row, rows, None) for w in range(2) for row, rows in parts])
+def held_steps(held):
+    return [(w, row, rows, None) for row, rows in pieces_of(held.shape[1], STEP) for w in range(2)]
+
+
+def held_kernel(width, start_ref, x_ref, held, gate_ref, up_ref, out, ahead, total, sems):
+    copies = block_copies(width, start_ref[0], (gate_ref, up_ref), 0, ahead, sems)
+    for _, _, _, copy in copies:
+        copy.start()
+    multiply(x_ref, 0, held, total, held_steps(held))
     pack_pair(out, total[0], total[1])
-
-
-def gate_up_held(features, held):
+    for _, _, _, copy in copies:
+        copy.wait()
+
+
+def gate_up_held(features, held, gate_weight, up_weight, start, ahead):
     rows, width = features.shape[0], held.shape[2]
     return pl.pallas_call(
-        held_kernel,
-        out_shape=jax.ShapeDtypeStruct((8, packed_pair_width(rows, width)), jnp.bfloat16),
-        in_specs=[WHOLE, WHOLE],
-        out_specs=WHOLE,
-        scratch_shapes=[pltpu.VMEM((2, rows, width), jnp.float32)],
+        functools.partial(held_kernel, width),
+        out_shape=(
+            jax.ShapeDtypeStruct((8, packed_pair_width(rows, width)), jnp.bfloat16),
+            pltpu.VMEM((2, ahead, width), jnp.bfloat16),
+        ),
+        in_specs=[SCALARS, WHOLE, WHOLE, IN_HBM, IN_HBM],
+        out_specs=(WHOLE, WHOLE),
+        scratch_shapes=[pltpu.VMEM((2, rows, width), jnp.float32), copy_sems(2, ahead)],
         compiler_params=params(8),
         cost_estimate=SMALL,
-    )(features, in_vmem(held))
-
-
-def stream_kernel(width, blocks, starts, x_ref, gate_ref, up_ref, _, *refs):
-    outs, refs = refs[: len(blocks)], refs[len(blocks) :]
+    )(start, features, in_vmem(held), in_hbm(gate_weight), in_hbm(up_weight))
+
+
+def stream_kernel(width, blocks, has_held, starts, x_ref, *refs):
+    refs = list(refs)
+    held_top = refs.pop(0) if has_held else None
+    gate_ref, up_ref, _ = refs[:3]
+    outs, refs = refs[3 : 3 + len(blocks)], refs[3 + len(blocks) :]
     work = []
     for b, which in enumerate(blocks):
         held, total, sems = refs[3 * b : 3 * b + 3]
         weights = [(gate_ref, up_ref)[w] for w in which]
-        copies = block_copies(width, starts[b], weights, held, sems)
-        work.append((outs[b], held, total, copies))
+        first = x_ref.shape[1] - held.shape[1]
+        copies = block_copies(width, starts[b], weights, first, held, sems)
+        work.append((outs[b], first, held, total, copies))
     waiting = [step[-1] for block in work for step in block[-1]]
     in_flight = IN_FLIGHT if len(blocks) > 1 else len(waiting)
     for copy in waiting[:in_flight]:
         copy.start()
     waiting = waiting[in_flight:]
-    for (out, held, total, copies), which in zip(work, blocks):
-        multiply(x_ref, held, total, copies, waiting)
+    if has_held:
+        multiply(x_ref, 0, held_top, work[0][3], held_steps(held_top))
+    for (out, first, held, total, copies), which in zip(work, blocks):
+        multiply(x_ref, first, held, total, copies, waiting)
         if len(which) == 2:
             pack_pair(out, total[0], total[1])
         else:
             pack_single(out, total[0])
 
 
-def gate_up_stream(features, gate_weight, up_weight, starts, blocks, width, after):
+def gate_up_stream(features, gate_weight, up_weight, starts, blocks, width, after, held=None):
     rows, depth = features.shape
-    scratch, shapes = [], []
-    for which in blocks:
+    scratch, shapes, held_bytes = [], [], 0
+    for b, which in enumerate(blocks):
         packed = packed_pair_width(rows, width) if len(which) == 2 else packed_width(rows, width)
         shapes.append(jax.ShapeDtypeStruct((8, packed), jnp.bfloat16))
+        below = depth - (held.shape[1] if held is not None and b == 0 else 0)
+        held_bytes += len(which) * below * width * 2
         scratch += [
-            pltpu.VMEM((len(which), depth, width), jnp.bfloat16),
+            pltpu.VMEM((len(which), below, width), jnp.bfloat16),
             pltpu.VMEM((len(which), rows, width), jnp.float32),
-            pltpu.SemaphoreType.DMA((len(which), len(pieces_of(depth, COPY_STEP)))),
+            copy_sems(len(which), below),
         ]
-    held_mib = -(-depth * width * 2 * sum(len(which) for which in blocks) // MIB)
-    return pl.pallas_call(
-        functools.partial(stream_kernel, width, blocks),
+    before = [] if held is None else [in_vmem(held)]
+    return pl.pallas_call(
+        functools.partial(stream_kernel, width, blocks, held is not None),
         out_shape=shapes,
-        in_specs=[SCALARS, WHOLE, IN_HBM, IN_HBM, ANY],
+        in_specs=[SCALARS, WHOLE] + [WHOLE] * len(before) + [IN_HBM, IN_HBM, ANY],
         out_specs=[WHOLE] * len(blocks),
         scratch_shapes=scratch,
-        compiler_params=params(5 + held_mib),
-        cost_estimate=SMALL,
-    )(starts, features, in_hbm(gate_weight), in_hbm(up_weight), after)
+        compiler_params=params(5 + -(-held_bytes // MIB)),
+        cost_estimate=SMALL,
+    )(starts, features, *before, in_hbm(gate_weight), in_hbm(up_weight), after)
 
 
 def hidden_tail(rows, width):
@@ -347,12 +376,13 @@
     )
     rows = features.shape[0]
 
-    def blocks_for(starts, blocks, after):
-        return gate_up_stream(features, gate_weight, up_weight, starts, blocks, width, after)
-
-    relayed = gate_up_held(features, held)
+    def blocks_for(starts, blocks, after, held=None):
+        return gate_up_stream(features, gate_weight, up_weight, starts, blocks, width, after, held)
+
+    ahead = gate_weight.shape[0] // 4 // STEP * STEP
+    relayed, held = gate_up_held(features, held, gate_weight, up_weight, starts_of(2), ahead)
     arrived = swap(relayed, "gx", n_gx, 1)
-    across, beside = blocks_for(starts_of(2, 1), ((0, 1), (0,)), relayed)
+    across, beside = blocks_for(starts_of(2, 1), ((0, 1), (0,)), relayed, held)
     across = lax.optimization_barrier(add(across, arrived).astype(jnp.bfloat16))
     far = swap(across, "gx", n_gx, 2)
     near = [swap(beside, "gx", n_gx, 1)]
@@ -391,7 +421,7 @@
     n_token = lax.axis_size(TOKEN_AXES)
     rows = tokens.shape[0] * n_token
     tokens_fit = n_token > 1 and n_token & (n_token - 1) == 0 and rows % 4 == 0
-    weights_fit = gate_weight.shape[1] % (128 * 4) == 0 and gate_weight.shape[0] % STEP == 0
+    weights_fit = gate_weight.shape[1] % (128 * 4) == 0 and gate_weight.shape[0] % (4 * STEP) == 0
     columns_fit = down_weight.shape[1] % (128 * 8) == 0
     if n_gx == 4 and tokens_fit and weights_fit and columns_fit:
         return direct(tokens, gate_weight, up_weight, down_weight)

time: 55.6 us -> 59.2 us (1.065)
  local copies, waits for them, and re-layouts: 0.03 us -> 3.7 us
    unnamed x16 -> x20, local copies, waits for them, and re-layouts: 0.03 us -> 3.7 us
  transfers between devices with their start and end apart: 13 -> 13, of which waited for: 6 -> 6; matrix products, arithmetic and copies ran while one was open for 0% -> 0% of each run, Pallas kernels for 49% -> 45%
where the time goes in v13:
time: 59.2 us; the launch traced here: 59.1 us
  Pallas kernels  31.1 us (53%)
  starting transfers between devices  13.1 us (22%)
  waiting for transfers between devices  10.7 us (18%)
  local copies, waits for them, and re-layouts  3.7 us (6%)
    pallas_call x3, Pallas kernels, gate_up_stream(): pl.pallas_call(functools.partial(stream_kernel, width, blocks, held is no...  17.5 us
    ppermute x13, starting transfers between devices, swap(): return lax.ppermute(value, axes, [(i, i ^ distance) for i in range(size)])  13.1 us
    ppermute x13, waiting for transfers between devices, swap(): return lax.ppermute(value, axes, [(i, i ^ distance) for i in range(size)])  10.7 us
    pallas_call x2, Pallas kernels, down(): pl.pallas_call(functools.partial(down_kernel, before is None, rows, width...  5.48 us
    pallas_call x1, Pallas kernels, fetch(): pl.pallas_call(functools.partial(fetch_kernel, width), out_shape=pltpu.VM...  5.16 us
    unnamed x20, local copies, waits for them, and re-layouts  3.7 us
    pallas_call x1, Pallas kernels, gate_up_held(): pl.pallas_call(functools.partial(held_kernel, width), out_shape=(jax.Shap...  2.2 us
  transfers between devices with their start and end apart: 13, of which 6 were waited for; matrix products, arithmetic and copies ran while one was open for 0% of the time, Pallas kernels for 45%

profile of v13, /device:TPU:0, one launch (start us, length us, event | category | flops | bytes accessed | tf_op | source)
XLA Modules:
  0.0 59.1 jit_solution(8730913754615355332)
XLA Ops:
  0.0 0.5 collective-permute-start
  0.5 2.5 %collective-permute-start.1 = (bf16[9,2048]{1,0:T(8,128)(2,1)}, bf16[9,2048]{1,0:T(8,128)(2,1)S(1)}, u32[]{:S(2)}, u32[]{:S(2)}) collective-permute-start(bf16[9,2048]{1,0:T(8,128)(2,1)} %param.4), channel_id=1, source_target_pairs={{0,2},{1,3},{2,0},{3,1},{4,6},{5,7},{6,4},{7,5},{8,10},{9,11},{10,... | collective-permute-start | bytes 110600 | tf_op jit(solution)/shard_map/ppermute | solution.py:357
  2.9 0.1 collective-permute-start.2
  3.1 0.0 copy-start.2
  3.1 5.2 %shard_map.46.held = bf16[2,2048,1664]{2,1,0:T(8,128)(2,1)S(1)} custom-call(s32[1]{0:T(128)} %bitcast.start_ref.starts, bf16[2048,6656]{1,0:T(8,128)(2,1)} %refs_0_.3, bf16[2048,6656]{1,0:T(8,128)(2,1)} %refs_1_.5), custom_call_target="tpu_custom_call" | custom-call | bytes 1048576 | tf_op jit(solution)/shard_map/pallas_call | solution.py:88
  8.3 0.0 collective-permute-done
  8.3 0.0 collective-permute-done.1
  8.3 0.0 collective-permute-done.2
  8.3 0.0 copy-done.2
  8.3 0.1 pad_maximum_fusion.x_ref
  8.4 2.2 %shard_map.47 = (bf16[8,14976]{1,0:T(8,128)(2,1)S(1)}, bf16[2,512,1664]{2,1,0:T(8,128)(2,1)S(1)}) custom-call(s32[1]{0:T(128)} %bitcast.3.start_ref, bf16[36,2048]{1,0:T(8,128)(2,1)S(1)} %pad_maximum_fusion.x_ref, bf16[2,2048,1664]{2,1,0:T(8,128)(2,1)S(1)} %shard_map.46.held, bf16[2048,6656]{1,0:T(8,128)(2,1)} %refs_0_.3, bf16[2048,6656]{1,0:T(8,128)(2,1)} %refs_1_.5), custom_call_target="tpu_custom_call" | custom-call | bytes 1048576 | tf_op jit(solution)/shard_map/pallas_call | solution.py:134
  10.6 0.0 copy-start
  10.6 1.7 %copy-done = bf16[2,512,1664]{2,1,0:T(8,128)(2,1)} copy-done((bf16[2,512,1664]{2,1,0:T(8,128)(2,1)}, bf16[2,512,1664]{2,1,0:T(8,128)(2,1)S(1)}, u32[]{:S(2)}) %copy-start) | copy-done | bytes 3407896
  12.3 1.7 %collective-permute-start.3 = (bf16[8,14976]{1,0:T(8,128)(2,1)S(1)}, bf16[8,14976]{1,0:T(8,128)(2,1)S(1)}, u32[]{:S(2)}, u32[]{:S(2)}) collective-permute-start(bf16[8,14976]{1,0:T(8,128)(2,1)S(1)} %get-tuple-element.14.refs_3_), channel_id=1, source_target_pairs={{0,4},{4,0},{8,12},{12,8},{1,5},{5,1},{9,13},{13,9},{2,6},{6,2},{1... | collective-permute-start | bytes 718856 | tf_op jit(solution)/shard_map/ppermute | solution.py:357
  14.0 0.1 pad_add_fusion.starts
  14.1 0.0 copy-start.1
  14.1 2.0 %copy-done.1 = bf16[2,512,1664]{2,1,0:T(8,128)(2,1)S(1)} copy-done((bf16[2,512,1664]{2,1,0:T(8,128)(2,1)S(1)}, bf16[2,512,1664]{2,1,0:T(8,128)(2,1)}, u32[]{:S(2)}) %copy-start.1) | copy-done | bytes 3407896
  16.0 7.7 %shard_map.48 = (bf16[8,14976]{1,0:T(8,128)(2,1)S(1)}, bf16[8,7552]{1,0:T(8,128)(2,1)S(1)}) custom-call(s32[2]{0:T(128)S(1)} %pad_add_fusion.starts, bf16[36,2048]{1,0:T(8,128)(2,1)S(1)} %pad_maximum_fusion.x_ref, bf16[2,512,1664]{2,1,0:T(8,128)(2,1)S(1)} %copy-done.1, bf16[2048,6656]{1,0:T(8,128)(2,1)} %refs_0_.3, bf16[2048,6656]{1,0:T(8,128)(2,1)} %refs_1_.5, ...), custom_call_target="tpu_custom_call" | custom-call | bytes 1048576 | tf_op jit(solution)/shard_map/pallas_call | solution.py:189
  23.7 0.0 collective-permute-done.3
  23.7 0.1 add_convert_fusion.refs_2_
  23.8 2.7 %collective-permute-start.4 = (bf16[8,14976]{1,0:T(8,128)(2,1)S(1)}, bf16[8,14976]{1,0:T(8,128)(2,1)S(1)}, u32[]{:S(2)}, u32[]{:S(2)}) collective-permute-start(bf16[8,14976]{1,0:T(8,128)(2,1)S(1)} %add_convert_fusion.refs_2_), channel_id=1, source_target_pairs={{0,8},{4,12},{8,0},{12,4},{1,9},{5,13},{9,1},{13,5},{2,10},{6,14},... | collective-permute-start | bytes 718856 | tf_op jit(solution)/shard_map/ppermute | solution.py:357
  26.5 0.4 collective-permute-start.5
  26.9 0.0 slice-start
  26.9 0.0 slice-start.1
  26.9 0.0 slice-start.2
  26.9 0.0 slice-start.3
  26.9 3.6 %shard_map.49.refs_2_ = bf16[8,7552]{1,0:T(8,128)(2,1)S(1)} custom-call(s32[1]{0:T(128)} %bitcast.2.starts, bf16[36,2048]{1,0:T(8,128)(2,1)S(1)} %pad_maximum_fusion.x_ref, bf16[2048,6656]{1,0:T(8,128)(2,1)} %refs_0_.3, bf16[2048,6656]{1,0:T(8,128)(2,1)} %refs_1_.5, bf16[8,14976]{1,0:T(8,128)(2,1)S(1)} %add_convert_fusion.refs_2_), custom_call_target="tpu_custom_call" | custom-call | bytes 1048576 | tf_op jit(solution)/shard_map/pallas_call | solution.py:189
  30.5 1.7 %collective-permute-start.6 = (bf16[8,7552]{1,0:T(8,128)(2,1)S(1)}, bf16[8,7552]{1,0:T(8,128)(2,1)S(1)}, u32[]{:S(2)}, u32[]{:S(2)}) collective-permute-start(bf16[8,7552]{1,0:T(8,128)(2,1)S(1)} %shard_map.49.refs_2_), channel_id=1, source_target_pairs={{0,4},{4,0},{8,12},{12,8},{1,5},{5,1},{9,13},{13,9},{2,6},{6,2},{1... | collective-permute-start | bytes 362504 | tf_op jit(solution)/shard_map/ppermute | solution.py:357
  32.2 0.0 slice-start.4
  32.2 0.0 slice-start.5
  32.2 0.0 slice-start.6
  32.2 6.2 %shard_map.50 = bf16[8,14976]{1,0:T(8,128)(2,1)S(1)} custom-call(s32[1]{0:T(128)} %bitcast.1.starts, bf16[36,2048]{1,0:T(8,128)(2,1)S(1)} %pad_maximum_fusion.x_ref, bf16[2048,6656]{1,0:T(8,128)(2,1)} %refs_0_.3, bf16[2048,6656]{1,0:T(8,128)(2,1)} %refs_1_.5, bf16[8,7552]{1,0:T(8,128)(2,1)S(1)} %shard_map.49.refs_2_), custom_call_target="tpu_custom_call" | custom-call | bytes 1048576 | tf_op jit(solution)/shard_map/pallas_call | solution.py:189
  38.4 0.0 collective-permute-done.4
  38.4 0.1 convert_add_fusion.summed
  38.5 0.0 collective-permute-done.5.gate_near
  38.5 1.2 %collective-permute-done.6.up_near = bf16[8,7552]{1,0:T(8,128)(2,1)S(1)} collective-permute-done((bf16[8,7552]{1,0:T(8,128)(2,1)S(1)}, bf16[8,7552]{1,0:T(8,128)(2,1)S(1)}, u32[]{:S(2)}, u32[]{:S(2)}) %collective-permute-start.6) | collective-permute-done | bytes 120864 | tf_op jit(solution)/shard_map/ppermute | solution.py:357
  39.8 0.1 shard_map.51.refs_0_
  39.8 0.1 collective-permute-start.7
  39.9 1.5 %collective-permute-start.9 = (bf16[8,7552]{1,0:T(8,128)(2,1)S(1)}, bf16[8,7552]{1,0:T(8,128)(2,1)S(1)}, u32[]{:S(2)}, u32[]{:S(2)}) collective-permute-start(bf16[8,7552]{1,0:T(8,128)(2,1)S(1)} %shard_map.51.refs_0_), channel_id=1, source_target_pairs={{0,4},{4,0},{8,12},{12,8},{1,5},{5,1},{9,13},{13,9},{2,6},{6,2},{1... | collective-permute-start | bytes 362504 | tf_op jit(solution)/shard_map/ppermute | solution.py:357
  41.4 5.8 %collective-permute-done.7.refs_2_ = bf16[8,7552]{1,0:T(8,128)(2,1)S(1)} collective-permute-done((bf16[8,7552]{1,0:T(8,128)(2,1)S(1)}, bf16[8,7552]{1,0:T(8,128)(2,1)S(1)}, u32[]{:S(2)}, u32[]{:S(2)}) %collective-permute-start.7) | collective-permute-done | bytes 120864 | tf_op jit(solution)/shard_map/ppermute | solution.py:357
  47.2 0.0 collective-permute-start.8
  47.2 0.1 pad_add_fusion.1.starts
  47.3 0.1 collective-permute-done.9.refs_1_
  47.4 0.0 slice-done
  47.4 0.0 slice-done.1
  47.4 0.0 slice-done.2
  47.4 0.0 slice-done.3
  47.4 0.0 slice-done.4
  47.4 0.0 slice-done.5
  47.4 0.0 slice-done.6
  47.4 4.2 %shard_map.52.refs_1_ = f32[36,2048]{1,0:T(8,128)S(1)} custom-call(s32[3]{0:T(128)S(1)} %pad_add_fusion.1.starts, bf16[8,7552]{1,0:T(8,128)(2,1)S(1)} %shard_map.51.refs_0_, bf16[8,7552]{1,0:T(8,128)(2,1)S(1)} %collective-permute-done.9.refs_1_, bf16[8,7552]{1,0:T(8,128)(2,1)S(1)} %collective-permute-done.7.refs_2_, bf16[6656,2048]{1,0:T(8,128)(2,1)S(1)} %bitcast.5), custom_call_target="tpu_custom_call" | custom-call | bytes 1048576 | tf_op jit(solution)/shard_map/pallas_call | solution.py:321
  51.6 0.5 collective-permute-done.8.refs_0_
  52.2 1.3 %shard_map.53 = (f32[8,2304]{1,0:T(8,128)S(1)}, bf16[8,2304]{1,0:T(8,128)(2,1)S(1)}, bf16[8,2304]{1,0:T(8,128)(2,1)S(1)}, bf16[8,2304]{1,0:T(8,128)(2,1)S(1)}) custom-call(s32[1]{0:T(128)} %bitcast.start_ref.starts, bf16[8,7552]{1,0:T(8,128)(2,1)S(1)} %collective-permute-done.8.refs_0_, f32[36,2048]{1,0:T(8,128)S(1)} %shard_map.52.refs_1_, ...), custom_call_target="tpu_custom_call" | custom-call | bytes 1048576 | tf_op jit(solution)/shard_map/pallas_call | solution.py:321
  53.5 0.1 collective-permute-start.10
  53.6 1.4 %collective-permute-start.11 = (bf16[8,2304]{1,0:T(8,128)(2,1)S(1)}, bf16[8,2304]{1,0:T(8,128)(2,1)S(1)}, u32[]{:S(2)}, u32[]{:S(2)}) collective-permute-start(bf16[8,2304]{1,0:T(8,128)(2,1)S(1)} %get-tuple-element.19), channel_id=1, source_target_pairs={{0,2},{1,3},{2,0},{3,1},{4,6},{5,7},{6,4},{7,5},{8,10},{9,11},{10,... | collective-permute-start | bytes 110600 | tf_op jit(solution)/shard_map/ppermute | solution.py:357
  55.0 0.4 collective-permute-start.12
  55.4 0.0 collective-permute-done.10.refs_1_
  55.4 2.2 %collective-permute-done.11.refs_2_ = bf16[8,2304]{1,0:T(8,128)(2,1)S(1)} collective-permute-done((bf16[8,2304]{1,0:T(8,128)(2,1)S(1)}, bf16[8,2304]{1,0:T(8,128)(2,1)S(1)}, u32[]{:S(2)}, u32[]{:S(2)}) %collective-permute-start.11) | collective-permute-done | bytes 36896 | tf_op jit(solution)/shard_map/ppermute | solution.py:357
  57.6 0.8 %collective-permute-done.12.refs_3_ = bf16[8,2304]{1,0:T(8,128)(2,1)S(1)} collective-permute-done((bf16[8,2304]{1,0:T(8,128)(2,1)S(1)}, bf16[8,2304]{1,0:T(8,128)(2,1)S(1)}, u32[]{:S(2)}, u32[]{:S(2)}) %collective-permute-start.12) | collective-permute-done | bytes 36896 | tf_op jit(solution)/shard_map/ppermute | solution.py:357
  58.4 0.7 %shard_map.54 = bf16[9,2048]{1,0:T(8,128)(2,1)} custom-call(f32[8,2304]{1,0:T(8,128)S(1)} %get-tuple-element.17.refs_0_, bf16[8,2304]{1,0:T(8,128)(2,1)S(1)} %collective-permute-done.10.refs_1_, bf16[8,2304]{1,0:T(8,128)(2,1)S(1)} %collective-permute-done.11.refs_2_, bf16[8,2304]{1,0:T(8,128)(2,1)S(1)} %collective-permute-done.12.refs_3_), custom_call_target="tpu_custom_call" | custom-call | bytes 1048576 | tf_op jit(solution)/shard_map/pallas_call | solution.py:345
  (1 shorter events, 0.0 us)
Async XLA Ops:
  0.0 8.3 %collective-permute-start = (bf16[9,2048]{1,0:T(8,128)(2,1)}, bf16[9,2048]{1,0:T(8,128)(2,1)S(1)}, u32[]{:S(2)}, u32[]{:S(2)}) collective-permute-start(bf16[9,2048]{1,0:T(8,128)(2,1)} %param.4), channel_id=1, source_target_pairs={{0,1},{1,0},{2,3},{3,2},{4,5},{5,4},{6,7},{7,6},{8,9},{9,8},{10,11... | collective-permute-start | bytes 110600 | tf_op jit(solution)/shard_map/ppermute | solution.py:357
  0.5 7.8 %collective-permute-start.1 = (bf16[9,2048]{1,0:T(8,128)(2,1)}, bf16[9,2048]{1,0:T(8,128)(2,1)S(1)}, u32[]{:S(2)}, u32[]{:S(2)}) collective-permute-start(bf16[9,2048]{1,0:T(8,128)(2,1)} %param.4), channel_id=1, source_target_pairs={{0,2},{1,3},{2,0},{3,1},{4,6},{5,7},{6,4},{7,5},{8,10},{9,11},{10,... | collective-permute-start | bytes 110600 | tf_op jit(solution)/shard_map/ppermute | solution.py:357
  2.9 5.3 %collective-permute-start.2 = (bf16[9,2048]{1,0:T(8,128)(2,1)}, bf16[9,2048]{1,0:T(8,128)(2,1)S(1)}, u32[]{:S(2)}, u32[]{:S(2)}) collective-permute-start(bf16[9,2048]{1,0:T(8,128)(2,1)} %param.4), channel_id=1, source_target_pairs={{0,3},{1,2},{2,1},{3,0},{4,7},{5,6},{6,5},{7,4},{8,11},{9,10},{10,... | collective-permute-start | bytes 110600 | tf_op jit(solution)/shard_map/ppermute | solution.py:357
  3.1 5.2 %copy-start.2 = (bf16[9,2048]{1,0:T(8,128)(2,1)S(1)}, bf16[9,2048]{1,0:T(8,128)(2,1)}, u32[]{:S(2)}) copy-start(bf16[9,2048]{1,0:T(8,128)(2,1)} %param.4) | copy-start | bytes 110596
  10.6 1.7 %copy-start = (bf16[2,512,1664]{2,1,0:T(8,128)(2,1)}, bf16[2,512,1664]{2,1,0:T(8,128)(2,1)S(1)}, u32[]{:S(2)}) copy-start(bf16[2,512,1664]{2,1,0:T(8,128)(2,1)S(1)} %get-tuple-element.13.refs_0_) | copy-start | bytes 10223620
  12.3 11.4 %collective-permute-start.3 = (bf16[8,14976]{1,0:T(8,128)(2,1)S(1)}, bf16[8,14976]{1,0:T(8,128)(2,1)S(1)}, u32[]{:S(2)}, u32[]{:S(2)}) collective-permute-start(bf16[8,14976]{1,0:T(8,128)(2,1)S(1)} %get-tuple-element.14.refs_3_), channel_id=1, source_target_pairs={{0,4},{4,0},{8,12},{12,8},{1,5},{5,1},{9,13},{13,9},{2,6},{6,2},{1... | collective-permute-start | bytes 718856 | tf_op jit(solution)/shard_map/ppermute | solution.py:357
  14.1 2.0 %copy-start.1 = (bf16[2,512,1664]{2,1,0:T(8,128)(2,1)S(1)}, bf16[2,512,1664]{2,1,0:T(8,128)(2,1)}, u32[]{:S(2)}) copy-start(bf16[2,512,1664]{2,1,0:T(8,128)(2,1)} %copy-done) | copy-start | bytes 10223620
  23.8 14.6 %collective-permute-start.4 = (bf16[8,14976]{1,0:T(8,128)(2,1)S(1)}, bf16[8,14976]{1,0:T(8,128)(2,1)S(1)}, u32[]{:S(2)}, u32[]{:S(2)}) collective-permute-start(bf16[8,14976]{1,0:T(8,128)(2,1)S(1)} %add_convert_fusion.refs_2_), channel_id=1, source_target_pairs={{0,8},{4,12},{8,0},{12,4},{1,9},{5,13},{9,1},{13,5},{2,10},{6,14},... | collective-permute-start | bytes 718856 | tf_op jit(solution)/shard_map/ppermute | solution.py:357
  26.5 12.0 %collective-permute-start.5 = (bf16[8,7552]{1,0:T(8,128)(2,1)S(1)}, bf16[8,7552]{1,0:T(8,128)(2,1)S(1)}, u32[]{:S(2)}, u32[]{:S(2)}) collective-permute-start(bf16[8,7552]{1,0:T(8,128)(2,1)S(1)} %get-tuple-element.16), channel_id=1, source_target_pairs={{0,4},{4,0},{8,12},{12,8},{1,5},{5,1},{9,13},{13,9},{2,6},{6,2},{1... | collective-permute-start | bytes 362504 | tf_op jit(solution)/shard_map/ppermute | solution.py:357
  26.9 20.5 %slice-start = ((s8[27262976]{0:T(1024)(128)(4,1)}), s8[4194304]{0:T(1024)(128)(4,1)S(1)}, s32[]{:S(2)}) async-start(s8[27262976]{0:T(1024)(128)(4,1)} %bitcast.4), calls=%async_computation | async-start | bytes 8388608
  26.9 20.5 %slice-start.1 = ((s8[27262976]{0:T(1024)(128)(4,1)}), s8[4194304]{0:T(1024)(128)(4,1)S(1)}, s32[]{:S(2)}) async-start(s8[27262976]{0:T(1024)(128)(4,1)} %bitcast.4), calls=%async_computation.1 | async-start | bytes 8388608
  26.9 20.5 %slice-start.2 = ((s8[27262976]{0:T(1024)(128)(4,1)}), s8[4194304]{0:T(1024)(128)(4,1)S(1)}, s32[]{:S(2)}) async-start(s8[27262976]{0:T(1024)(128)(4,1)} %bitcast.4), calls=%async_computation.2 | async-start | bytes 8388608
  26.9 20.5 %slice-start.3 = ((s8[27262976]{0:T(1024)(128)(4,1)}), s8[4194304]{0:T(1024)(128)(4,1)S(1)}, s32[]{:S(2)}) async-start(s8[27262976]{0:T(1024)(128)(4,1)} %bitcast.4), calls=%async_computation.3 | async-start | bytes 8388608
  30.5 9.2 %collective-permute-start.6 = (bf16[8,7552]{1,0:T(8,128)(2,1)S(1)}, bf16[8,7552]{1,0:T(8,128)(2,1)S(1)}, u32[]{:S(2)}, u32[]{:S(2)}) collective-permute-start(bf16[8,7552]{1,0:T(8,128)(2,1)S(1)} %shard_map.49.refs_2_), channel_id=1, source_target_pairs={{0,4},{4,0},{8,12},{12,8},{1,5},{5,1},{9,13},{13,9},{2,6},{6,2},{1... | collective-permute-start | bytes 362504 | tf_op jit(solution)/shard_map/ppermute | solution.py:357
  32.2 15.2 %slice-start.4 = ((s8[27262976]{0:T(1024)(128)(4,1)}), s8[4194304]{0:T(1024)(128)(4,1)S(1)}, s32[]{:S(2)}) async-start(s8[27262976]{0:T(1024)(128)(4,1)} %bitcast.4), calls=%async_computation.4 | async-start | bytes 8388608
  32.2 15.2 %slice-start.5 = ((s8[27262976]{0:T(1024)(128)(4,1)}), s8[4194304]{0:T(1024)(128)(4,1)S(1)}, s32[]{:S(2)}) async-start(s8[27262976]{0:T(1024)(128)(4,1)} %bitcast.4), calls=%async_computation.5 | async-start | bytes 8388608
  32.2 15.2 %slice-start.6 = ((s8[27262976]{0:T(1024)(128)(4,1)}), s8[2097152]{0:T(1024)(128)(4,1)S(1)}, s32[]{:S(2)}) async-start(s8[27262976]{0:T(1024)(128)(4,1)} %bitcast.4), calls=%async_computation.6 | async-start | bytes 4194304
  39.8 7.4 %collective-permute-start.7 = (bf16[8,7552]{1,0:T(8,128)(2,1)S(1)}, bf16[8,7552]{1,0:T(8,128)(2,1)S(1)}, u32[]{:S(2)}, u32[]{:S(2)}) collective-permute-start(bf16[8,7552]{1,0:T(8,128)(2,1)S(1)} %shard_map.51.refs_0_), channel_id=1, source_target_pairs={{0,8},{4,12},{8,0},{12,4},{1,9},{5,13},{9,1},{13,5},{2,10},{6,14},... | collective-permute-start | bytes 362504 | tf_op jit(solution)/shard_map/ppermute | solution.py:357
  39.9 7.5 %collective-permute-start.9 = (bf16[8,7552]{1,0:T(8,128)(2,1)S(1)}, bf16[8,7552]{1,0:T(8,128)(2,1)S(1)}, u32[]{:S(2)}, u32[]{:S(2)}) collective-permute-start(bf16[8,7552]{1,0:T(8,128)(2,1)S(1)} %shard_map.51.refs_0_), channel_id=1, source_target_pairs={{0,4},{4,0},{8,12},{12,8},{1,5},{5,1},{9,13},{13,9},{2,6},{6,2},{1... | collective-permute-start | bytes 362504 | tf_op jit(solution)/shard_map/ppermute | solution.py:357
  47.2 4.9 %collective-permute-start.8 = (bf16[8,7552]{1,0:T(8,128)(2,1)S(1)}, bf16[8,7552]{1,0:T(8,128)(2,1)S(1)}, u32[]{:S(2)}, u32[]{:S(2)}) collective-permute-start(bf16[8,7552]{1,0:T(8,128)(2,1)S(1)} %collective-permute-done.7.refs_2_), channel_id=1, source_target_pairs={{0,4},{4,0},{8,12},{12,8},{1,5},{5,1},{9,13},{13,9},{2,6},{6,2},{1... | collective-permute-start | bytes 362504 | tf_op jit(solution)/shard_map/ppermute | solution.py:357
  53.5 1.9 %collective-permute-start.10 = (bf16[8,2304]{1,0:T(8,128)(2,1)S(1)}, bf16[8,2304]{1,0:T(8,128)(2,1)S(1)}, u32[]{:S(2)}, u32[]{:S(2)}) collective-permute-start(bf16[8,2304]{1,0:T(8,128)(2,1)S(1)} %get-tuple-element.18), channel_id=1, source_target_pairs={{0,1},{1,0},{2,3},{3,2},{4,5},{5,4},{6,7},{7,6},{8,9},{9,8},{10,11... | collective-permute-start | bytes 110600 | tf_op jit(solution)/shard_map/ppermute | solution.py:357
  53.6 4.0 %collective-permute-start.11 = (bf16[8,2304]{1,0:T(8,128)(2,1)S(1)}, bf16[8,2304]{1,0:T(8,128)(2,1)S(1)}, u32[]{:S(2)}, u32[]{:S(2)}) collective-permute-start(bf16[8,2304]{1,0:T(8,128)(2,1)S(1)} %get-tuple-element.19), channel_id=1, source_target_pairs={{0,2},{1,3},{2,0},{3,1},{4,6},{5,7},{6,4},{7,5},{8,10},{9,11},{10,... | collective-permute-start | bytes 110600 | tf_op jit(solution)/shard_map/ppermute | solution.py:357
  55.0 3.4 %collective-permute-start.12 = (bf16[8,2304]{1,0:T(8,128)(2,1)S(1)}, bf16[8,2304]{1,0:T(8,128)(2,1)S(1)}, u32[]{:S(2)}, u32[]{:S(2)}) collective-permute-start(bf16[8,2304]{1,0:T(8,128)(2,1)S(1)} %get-tuple-element.20), channel_id=1, source_target_pairs={{0,3},{1,2},{2,1},{3,0},{4,7},{5,6},{6,5},{7,4},{8,11},{9,10},{10,... | collective-permute-start | bytes 110600 | tf_op jit(solution)/shard_map/ppermute | solution.py:357

commit v14 on v12

--- a/solution.py
+++ b/solution.py
@@ -15,7 +15,6 @@
 IN_HBM = pl.BlockSpec(memory_space=pltpu.HBM)
 ANY = pl.BlockSpec(memory_space=pl.ANY)
 WHOLE = pl.BlockSpec(memory_space=pltpu.VMEM)
-SCALARS = pl.BlockSpec(memory_space=pltpu.SMEM)
 
 
 def activate(gate, up):
@@ -35,6 +34,10 @@
 
 
 SMALL = pl.CostEstimate(flops=0, bytes_accessed=MIB, transcendentals=0)
+
+
+def block_start(distance, width):
+    return pl.multiple_of((lax.axis_index("gx") ^ distance) * width, 128)
 
 
 def params(mib):
@@ -57,8 +60,8 @@
         out[:, at : at + width] = tail.astype(out.dtype)
 
 
-def block_copies(width, start, weights, held, sems):
-    columns = pl.ds(pl.multiple_of(start, 128), width)
+def block_copies(width, distance, weights, held, sems):
+    columns = pl.ds(block_start(distance, width), width)
     copies = []
     for k, (row, rows) in enumerate(pieces_of(held.shape[1], COPY_STEP)):
         for w, weight in enumerate(weights):
@@ -69,25 +72,25 @@
     return copies
 
 
-def fetch_kernel(width, start_ref, gate_ref, up_ref, held, sems):
-    copies = block_copies(width, start_ref[0], (gate_ref, up_ref), held, sems)
+def fetch_kernel(width, distance, gate_ref, up_ref, held, sems):
+    copies = block_copies(width, distance, (gate_ref, up_ref), held, sems)
     for _, _, _, copy in copies:
         copy.start()
     for _, _, _, copy in copies:
         copy.wait()
 
 
-def fetch(gate_weight, up_weight, start, width):
+def fetch(gate_weight, up_weight, distance, width):
     depth = gate_weight.shape[0]
     return pl.pallas_call(
-        functools.partial(fetch_kernel, width),
+        functools.partial(fetch_kernel, width, distance),
         out_shape=pltpu.VMEM((2, depth, width), jnp.bfloat16),
-        in_specs=[SCALARS, IN_HBM, IN_HBM],
+        in_specs=[IN_HBM, IN_HBM],
         out_specs=WHOLE,
         scratch_shapes=[pltpu.SemaphoreType.DMA((2, len(pieces_of(depth, COPY_STEP))))],
         compiler_params=params(4),
         cost_estimate=SMALL,
-    )(start, in_hbm(gate_weight), in_hbm(up_weight))
+    )(in_hbm(gate_weight), in_hbm(up_weight))
 
 
 def multiply(x_ref, held, total, steps, waiting=()):
@@ -124,13 +127,13 @@
     )(features, in_vmem(held))
 
 
-def stream_kernel(width, blocks, starts, x_ref, gate_ref, up_ref, _, *refs):
+def stream_kernel(width, blocks, distances, x_ref, gate_ref, up_ref, _, *refs):
     outs, refs = refs[: len(blocks)], refs[len(blocks) :]
     work = []
     for b, which in enumerate(blocks):
         held, total, sems = refs[3 * b : 3 * b + 3]
         weights = [(gate_ref, up_ref)[w] for w in which]
-        copies = block_copies(width, starts[b], weights, held, sems)
+        copies = block_copies(width, distances[b], weights, held, sems)
         work.append((outs[b], held, total, copies))
     waiting = [step[-1] for block in work for step in block[-1]]
     in_flight = IN_FLIGHT if len(blocks) > 1 else len(waiting)
@@ -145,7 +148,7 @@
             pack_single(out, total[0])
 
 
-def gate_up_stream(features, gate_weight, up_weight, starts, blocks, width, after):
+def gate_up_stream(features, gate_weight, up_weight, distances, blocks, width, after):
     rows, depth = features.shape
     scratch, shapes = [], []
     for which in blocks:
@@ -158,14 +161,14 @@
         ]
     held_mib = -(-depth * width * 2 * sum(len(which) for which in blocks) // MIB)
     return pl.pallas_call(
-        functools.partial(stream_kernel, width, blocks),
+        functools.partial(stream_kernel, width, blocks, distances),
         out_shape=shapes,
-        in_specs=[SCALARS, WHOLE, IN_HBM, IN_HBM, ANY],
+        in_specs=[WHOLE, IN_HBM, IN_HBM, ANY],
         out_specs=[WHOLE] * len(blocks),
         scratch_shapes=scratch,
         compiler_params=params(5 + held_mib),
         cost_estimate=SMALL,
-    )(starts, features, in_hbm(gate_weight), in_hbm(up_weight), after)
+    )(features, in_hbm(gate_weight), in_hbm(up_weight), after)
 
 
 def hidden_tail(rows, width):
@@ -195,34 +198,38 @@
     return jnp.concatenate([tail[:4], tail[4:, : width - half]], axis=1)
 
 
-def activate_kernel(rows, width, summed, gate_near, up_near, out):
+def activate_kernel(rows, width, own, far, gate_near, up_near, out):
+    def pair(at):
+        columns = slice(at, at + width)
+        return own[:, columns].astype(jnp.float32) + far[:, columns].astype(jnp.float32)
+
     for g in range(rows // 8):
         near = slice(g * width, (g + 1) * width)
-        gate, up = ((2 * g + w) * width for w in range(2))
         out[:, near] = activate(
-            summed[:, gate : gate + width] + gate_near[:, near].astype(jnp.float32),
-            summed[:, up : up + width] + up_near[:, near].astype(jnp.float32),
+            pair(2 * g * width) + gate_near[:, near].astype(jnp.float32),
+            pair((2 * g + 1) * width) + up_near[:, near].astype(jnp.float32),
         )
     if rows % 8:
-        at, half = (rows // 8) * 2 * width, hidden_tail(rows, width)
+        half = hidden_tail(rows, width)
+        last = pair((rows // 8) * 2 * width)
         value = activate(
-            summed[:4, at : at + width] + last_rows(gate_near, rows, width),
-            summed[4:, at : at + width] + last_rows(up_near, rows, width),
+            last[:4] + last_rows(gate_near, rows, width),
+            last[4:] + last_rows(up_near, rows, width),
         ).astype(jnp.float32)
         right = jnp.concatenate([value[:, half:], jnp.zeros((4, 2 * half - width), jnp.float32)], axis=1)
         at = (rows // 8) * width
         out[:, at : at + half] = jnp.concatenate([value[:, :half], right], axis=0).astype(out.dtype)
 
 
-def activate_packed(summed, near, rows, width):
+def activate_packed(own, far, near, rows, width):
     return pl.pallas_call(
         functools.partial(activate_kernel, rows, width),
         out_shape=jax.ShapeDtypeStruct((8, packed_width(rows, width)), jnp.bfloat16),
-        in_specs=[WHOLE] * 3,
+        in_specs=[WHOLE] * 4,
         out_specs=WHOLE,
         compiler_params=params(8),
         cost_estimate=SMALL,
-    )(summed, *near)
+    )(own, far, *near)
 
 
 def pack_rows(out, value):
@@ -249,8 +256,8 @@
             out[r : r + 1, i * piece : (i + 1) * piece] = packed[i : i + 1, at : at + piece]
 
 
-def down_kernel(first, rows, width, starts, *refs):
-    blocks = starts.shape[0]
+def down_kernel(first, rows, width, distances, *refs):
+    blocks = len(distances)
     hidden, refs = refs[:blocks], refs[blocks:]
     if not first:
         before, refs = refs[0], refs[1:]
@@ -268,7 +275,7 @@
         for row, tall in pieces_of(width, STEP):
             term = jnp.dot(
                 plain[:, row : row + tall].astype(jnp.bfloat16),
-                held[pl.ds(pl.multiple_of(starts[b] + row, 128), tall), :],
+                held[pl.ds(pl.multiple_of(block_start(distances[b], width) + row, 128), tall), :],
                 preferred_element_type=jnp.float32,
             )
             if b == 0 and row == 0:
@@ -281,7 +288,7 @@
             pack_rows(out, total[r * tall : (r + 1) * tall, :])
 
 
-def down(hidden, starts, before, weight, rows, width, outs):
+def down(hidden, distances, before, weight, rows, width, outs):
     columns = weight.shape[1]
     if before is None:
         shapes = [jax.ShapeDtypeStruct((rows, columns), jnp.float32)]
@@ -290,9 +297,9 @@
         shapes = [jax.ShapeDtypeStruct(packed, jnp.bfloat16 if r else jnp.float32) for r in range(outs)]
     carried = [] if before is None else [before]
     return pl.pallas_call(
-        functools.partial(down_kernel, before is None, rows, width),
+        functools.partial(down_kernel, before is None, rows, width, distances),
         out_shape=shapes,
-        in_specs=[SCALARS] + [WHOLE] * (len(hidden) + len(carried) + 1),
+        in_specs=[WHOLE] * (len(hidden) + len(carried) + 1),
         out_specs=[WHOLE] * len(shapes),
         scratch_shapes=[
             pltpu.VMEM((rows, width), jnp.float32),
@@ -300,7 +307,7 @@
         ],
         compiler_params=params(8),
         cost_estimate=SMALL,
-    )(starts, *hidden, *carried, in_vmem(weight))
+    )(*hidden, *carried, in_vmem(weight))
 
 
 def finish_kernel(*refs):
@@ -335,38 +342,33 @@
 def direct(tokens, gate_weight, up_weight, down_weight):
     n_gx = lax.axis_size("gx")
     n_token = lax.axis_size(TOKEN_AXES)
-    me = lax.axis_index("gx")
     width = gate_weight.shape[1] // n_gx
 
-    def starts_of(*distances):
-        return jnp.stack([(me ^ d) * width for d in distances]).astype(jnp.int32)
-
-    held = fetch(gate_weight, up_weight, starts_of(3), width)
+    held = fetch(gate_weight, up_weight, 3, width)
     features = jnp.concatenate(
         [tokens] + [swap(tokens, TOKEN_AXES, n_token, r) for r in range(1, n_token)], axis=0
     )
     rows = features.shape[0]
 
-    def blocks_for(starts, blocks, after):
-        return gate_up_stream(features, gate_weight, up_weight, starts, blocks, width, after)
+    def blocks_for(distances, blocks, after):
+        return gate_up_stream(features, gate_weight, up_weight, distances, blocks, width, after)
 
     relayed = gate_up_held(features, held)
     arrived = swap(relayed, "gx", n_gx, 1)
-    across, beside = blocks_for(starts_of(2, 1), ((0, 1), (0,)), relayed)
+    across, beside = blocks_for((2, 1), ((0, 1), (0,)), relayed)
     across = lax.optimization_barrier(add(across, arrived).astype(jnp.bfloat16))
     far = swap(across, "gx", n_gx, 2)
     near = [swap(beside, "gx", n_gx, 1)]
-    (beside,) = blocks_for(starts_of(1), ((1,),), across)
+    (beside,) = blocks_for((1,), ((1,),), across)
     near.append(swap(beside, "gx", n_gx, 1))
-    (own,) = blocks_for(starts_of(0), ((0, 1),), beside)
-    summed = lax.optimization_barrier(add(own, far))
-    hidden = activate_packed(summed, near, rows, width)
+    (own,) = blocks_for((0,), ((0, 1),), beside)
+    hidden = activate_packed(own, far, near, rows, width)
 
     opposite = swap(hidden, "gx", n_gx, 2)
     first = [hidden, swap(hidden, "gx", n_gx, 1), opposite]
     second = [swap(opposite, "gx", n_gx, 1)]
-    (partial_sum,) = down(first, starts_of(0, 1, 2), None, down_weight, rows, width, 1)
-    outs = down(second, starts_of(3), partial_sum, down_weight, rows, width, n_token)
+    (partial_sum,) = down(first, (0, 1, 2), None, down_weight, rows, width, 1)
+    outs = down(second, (3,), partial_sum, down_weight, rows, width, n_token)
     terms = [outs[0]] + [swap(outs[r], TOKEN_AXES, n_token, r) for r in range(1, n_token)]
     return finish(terms, tokens.shape)
 

time: 55.6 us -> 55.1 us (level)
  Pallas kernels: 31.5 us -> 30.5 us
  transfers between devices with their start and end apart: 13 -> 13, of which waited for: 6 -> 6; matrix products, arithmetic and copies ran while one was open for 0% -> 0% of each run, Pallas kernels for 49% -> 48%
where the time goes in v14:
time: 55.1 us; the launch traced here: 55 us
  Pallas kernels  30.5 us (55%)
  starting transfers between devices  13.4 us (24%)
  waiting for transfers between devices  10.7 us (19%)
    pallas_call x3, Pallas kernels, gate_up_stream(): pl.pallas_call(functools.partial(stream_kernel, width, blocks, distances)...  17.4 us
    ppermute x13, starting transfers between devices, swap(): return lax.ppermute(value, axes, [(i, i ^ distance) for i in range(size)])  13.4 us
    ppermute x13, waiting for transfers between devices, swap(): return lax.ppermute(value, axes, [(i, i ^ distance) for i in range(size)])  10.7 us
    pallas_call x1, Pallas kernels, fetch(): pl.pallas_call(functools.partial(fetch_kernel, width, distance), out_shap...  5.16 us
    pallas_call x2, Pallas kernels, down(): pl.pallas_call(functools.partial(down_kernel, before is None, rows, width...  4.94 us
    pallas_call x1, Pallas kernels, gate_up_held(): pl.pallas_call(held_kernel, out_shape=jax.ShapeDtypeStruct((8, packed_pai...  2.15 us
  transfers between devices with their start and end apart: 13, of which 6 were waited for; matrix products, arithmetic and copies ran while one was open for 0% of the time, Pallas kernels for 48%

profile of v14, /device:TPU:0, one launch (start us, length us, event | category | flops | bytes accessed | tf_op | source)
XLA Modules:
  0.0 55.0 jit_solution(17160153235079795748)
XLA Ops:
  0.0 0.0 copy-start
  0.0 2.9 %collective-permute-start.1 = (bf16[9,2048]{1,0:T(8,128)(2,1)}, bf16[9,2048]{1,0:T(8,128)(2,1)S(1)}, u32[]{:S(2)}, u32[]{:S(2)}) collective-permute-start(bf16[9,2048]{1,0:T(8,128)(2,1)} %param.4), channel_id=1, source_target_pairs={{0,2},{1,3},{2,0},{3,1},{4,6},{5,7},{6,4},{7,5},{8,10},{9,11},{10,... | collective-permute-start | bytes 110600 | tf_op jit(solution)/shard_map/ppermute | solution.py:335
  2.9 0.0 collective-permute-start
  2.9 0.2 collective-permute-start.2
  3.1 5.2 %shard_map.46.held = bf16[2,2048,1664]{2,1,0:T(8,128)(2,1)S(1)} custom-call(bf16[2048,6656]{1,0:T(8,128)(2,1)} %gate_ref.7, bf16[2048,6656]{1,0:T(8,128)(2,1)} %up_ref.7), custom_call_target="tpu_custom_call" | custom-call | bytes 1048576 | tf_op jit(solution)/shard_map/pallas_call | solution.py:85
  8.3 0.0 collective-permute-done.1
  8.3 0.0 collective-permute-done
  8.3 0.0 collective-permute-done.2
  8.3 0.0 copy-done
  8.3 0.1 pad_maximum_fusion.x_ref
  8.4 2.2 %shard_map.47._ = bf16[8,14976]{1,0:T(8,128)(2,1)S(1)} custom-call(bf16[36,2048]{1,0:T(8,128)(2,1)S(1)} %pad_maximum_fusion.x_ref, bf16[2,2048,1664]{2,1,0:T(8,128)(2,1)S(1)} %shard_map.46.held), custom_call_target="tpu_custom_call" | custom-call | bytes 1048576 | tf_op jit(solution)/shard_map/pallas_call | solution.py:119
  10.6 2.0 %collective-permute-start.3 = (bf16[8,14976]{1,0:T(8,128)(2,1)S(1)}, bf16[8,14976]{1,0:T(8,128)(2,1)S(1)}, u32[]{:S(2)}, u32[]{:S(2)}) collective-permute-start(bf16[8,14976]{1,0:T(8,128)(2,1)S(1)} %shard_map.47._), channel_id=1, source_target_pairs={{0,4},{4,0},{8,12},{12,8},{1,5},{5,1},{9,13},{13,9},{2,6},{6,2},{1... | collective-permute-start | bytes 718856 | tf_op jit(solution)/shard_map/ppermute | solution.py:335
  12.6 7.6 %shard_map.48 = (bf16[8,14976]{1,0:T(8,128)(2,1)S(1)}, bf16[8,7552]{1,0:T(8,128)(2,1)S(1)}) custom-call(bf16[36,2048]{1,0:T(8,128)(2,1)S(1)} %pad_maximum_fusion.x_ref, bf16[2048,6656]{1,0:T(8,128)(2,1)} %gate_ref.7, bf16[2048,6656]{1,0:T(8,128)(2,1)} %up_ref.7, bf16[8,14976]{1,0:T(8,128)(2,1)S(1)} %shard_map.47._), custom_call_target="tpu_custom_call" | custom-call | bytes 1048576 | tf_op jit(solution)/shard_map/pallas_call | solution.py:163
  20.2 0.0 collective-permute-done.3
  20.2 0.1 add_convert_fusion._
  20.2 2.7 %collective-permute-start.4 = (bf16[8,14976]{1,0:T(8,128)(2,1)S(1)}, bf16[8,14976]{1,0:T(8,128)(2,1)S(1)}, u32[]{:S(2)}, u32[]{:S(2)}) collective-permute-start(bf16[8,14976]{1,0:T(8,128)(2,1)S(1)} %add_convert_fusion._), channel_id=1, source_target_pairs={{0,8},{4,12},{8,0},{12,4},{1,9},{5,13},{9,1},{13,5},{2,10},{6,14},... | collective-permute-start | bytes 718856 | tf_op jit(solution)/shard_map/ppermute | solution.py:335
  22.9 0.4 collective-permute-start.5
  23.3 0.0 slice-start
  23.3 0.0 slice-start.1
  23.3 0.0 slice-start.2
  23.3 0.0 slice-start.3
  23.4 3.6 %shard_map.49._ = bf16[8,7552]{1,0:T(8,128)(2,1)S(1)} custom-call(bf16[36,2048]{1,0:T(8,128)(2,1)S(1)} %pad_maximum_fusion.x_ref, bf16[2048,6656]{1,0:T(8,128)(2,1)} %gate_ref.7, bf16[2048,6656]{1,0:T(8,128)(2,1)} %up_ref.7, bf16[8,14976]{1,0:T(8,128)(2,1)S(1)} %add_convert_fusion._), custom_call_target="tpu_custom_call" | custom-call | bytes 1048576 | tf_op jit(solution)/shard_map/pallas_call | solution.py:163
  26.9 0.0 slice-start.4
  27.0 0.0 slice-start.5
  27.0 0.0 slice-start.6
  27.0 1.7 %collective-permute-start.6 = (bf16[8,7552]{1,0:T(8,128)(2,1)S(1)}, bf16[8,7552]{1,0:T(8,128)(2,1)S(1)}, u32[]{:S(2)}, u32[]{:S(2)}) collective-permute-start(bf16[8,7552]{1,0:T(8,128)(2,1)S(1)} %shard_map.49._), channel_id=1, source_target_pairs={{0,4},{4,0},{8,12},{12,8},{1,5},{5,1},{9,13},{13,9},{2,6},{6,2},{1... | collective-permute-start | bytes 362504 | tf_op jit(solution)/shard_map/ppermute | solution.py:335
  28.7 6.2 %shard_map.50.own = bf16[8,14976]{1,0:T(8,128)(2,1)S(1)} custom-call(bf16[36,2048]{1,0:T(8,128)(2,1)S(1)} %pad_maximum_fusion.x_ref, bf16[2048,6656]{1,0:T(8,128)(2,1)} %gate_ref.7, bf16[2048,6656]{1,0:T(8,128)(2,1)} %up_ref.7, bf16[8,7552]{1,0:T(8,128)(2,1)S(1)} %shard_map.49._), custom_call_target="tpu_custom_call" | custom-call | bytes 1048576 | tf_op jit(solution)/shard_map/pallas_call | solution.py:163
  34.9 0.0 collective-permute-done.5.gate_near
  34.9 1.0 %collective-permute-done.6.up_near = bf16[8,7552]{1,0:T(8,128)(2,1)S(1)} collective-permute-done((bf16[8,7552]{1,0:T(8,128)(2,1)S(1)}, bf16[8,7552]{1,0:T(8,128)(2,1)S(1)}, u32[]{:S(2)}, u32[]{:S(2)}) %collective-permute-start.6) | collective-permute-done | bytes 120864 | tf_op jit(solution)/shard_map/ppermute | solution.py:335
  35.9 0.0 collective-permute-done.4.far
  35.9 0.1 shard_map.51.refs_0_
  36.1 0.1 collective-permute-start.7
  36.2 1.5 %collective-permute-start.9 = (bf16[8,7552]{1,0:T(8,128)(2,1)S(1)}, bf16[8,7552]{1,0:T(8,128)(2,1)S(1)}, u32[]{:S(2)}, u32[]{:S(2)}) collective-permute-start(bf16[8,7552]{1,0:T(8,128)(2,1)S(1)} %shard_map.51.refs_0_), channel_id=1, source_target_pairs={{0,4},{4,0},{8,12},{12,8},{1,5},{5,1},{9,13},{13,9},{2,6},{6,2},{1... | collective-permute-start | bytes 362504 | tf_op jit(solution)/shard_map/ppermute | solution.py:335
  37.6 5.8 %collective-permute-done.7.refs_2_ = bf16[8,7552]{1,0:T(8,128)(2,1)S(1)} collective-permute-done((bf16[8,7552]{1,0:T(8,128)(2,1)S(1)}, bf16[8,7552]{1,0:T(8,128)(2,1)S(1)}, u32[]{:S(2)}, u32[]{:S(2)}) %collective-permute-start.7) | collective-permute-done | bytes 120864 | tf_op jit(solution)/shard_map/ppermute | solution.py:335
  43.4 0.0 collective-permute-start.8
  43.4 0.1 collective-permute-done.9.refs_1_
  43.6 0.0 slice-done
  43.6 0.0 slice-done.1
  43.6 0.0 slice-done.2
  43.6 0.0 slice-done.3
  43.6 0.0 slice-done.4
  43.6 0.0 slice-done.5
  43.6 0.0 slice-done.6
  43.6 3.6 %shard_map.52.refs_1_ = f32[36,2048]{1,0:T(8,128)S(1)} custom-call(bf16[8,7552]{1,0:T(8,128)(2,1)S(1)} %shard_map.51.refs_0_, bf16[8,7552]{1,0:T(8,128)(2,1)S(1)} %collective-permute-done.9.refs_1_, bf16[8,7552]{1,0:T(8,128)(2,1)S(1)} %collective-permute-done.7.refs_2_, bf16[6656,2048]{1,0:T(8,128)(2,1)S(1)} %bitcast.1), custom_call_target="tpu_custom_call" | custom-call | bytes 1048576 | tf_op jit(solution)/shard_map/pallas_call | solution.py:299
  47.3 1.0 %collective-permute-done.8.refs_0_ = bf16[8,7552]{1,0:T(8,128)(2,1)S(1)} collective-permute-done((bf16[8,7552]{1,0:T(8,128)(2,1)S(1)}, bf16[8,7552]{1,0:T(8,128)(2,1)S(1)}, u32[]{:S(2)}, u32[]{:S(2)}) %collective-permute-start.8) | collective-permute-done | bytes 120864 | tf_op jit(solution)/shard_map/ppermute | solution.py:335
  48.3 1.3 %shard_map.53 = (f32[8,2304]{1,0:T(8,128)S(1)}, bf16[8,2304]{1,0:T(8,128)(2,1)S(1)}, bf16[8,2304]{1,0:T(8,128)(2,1)S(1)}, bf16[8,2304]{1,0:T(8,128)(2,1)S(1)}) custom-call(bf16[8,7552]{1,0:T(8,128)(2,1)S(1)} %collective-permute-done.8.refs_0_, f32[36,2048]{1,0:T(8,128)S(1)} %shard_map.52.refs_1_, bf16[6656,2048]{1,0:T(8,128)(2,1)S(1)} %bitcast.1), custom_call_target="tpu_custom_call" | custom-call | bytes 1048576 | tf_op jit(solution)/shard_map/pallas_call | solution.py:299
  49.6 0.1 collective-permute-start.10
  49.7 1.2 %collective-permute-start.11 = (bf16[8,2304]{1,0:T(8,128)(2,1)S(1)}, bf16[8,2304]{1,0:T(8,128)(2,1)S(1)}, u32[]{:S(2)}, u32[]{:S(2)}) collective-permute-start(bf16[8,2304]{1,0:T(8,128)(2,1)S(1)} %get-tuple-element.15), channel_id=1, source_target_pairs={{0,2},{1,3},{2,0},{3,1},{4,6},{5,7},{6,4},{7,5},{8,10},{9,11},{10,... | collective-permute-start | bytes 110600 | tf_op jit(solution)/shard_map/ppermute | solution.py:335
  50.9 0.7 %collective-permute-start.12 = (bf16[8,2304]{1,0:T(8,128)(2,1)S(1)}, bf16[8,2304]{1,0:T(8,128)(2,1)S(1)}, u32[]{:S(2)}, u32[]{:S(2)}) collective-permute-start(bf16[8,2304]{1,0:T(8,128)(2,1)S(1)} %get-tuple-element.16), channel_id=1, source_target_pairs={{0,3},{1,2},{2,1},{3,0},{4,7},{5,6},{6,5},{7,4},{8,11},{9,10},{10,... | collective-permute-start | bytes 110600 | tf_op jit(solution)/shard_map/ppermute | solution.py:335
  51.6 0.0 collective-permute-done.10.refs_1_
  51.6 2.2 %collective-permute-done.11.refs_2_ = bf16[8,2304]{1,0:T(8,128)(2,1)S(1)} collective-permute-done((bf16[8,2304]{1,0:T(8,128)(2,1)S(1)}, bf16[8,2304]{1,0:T(8,128)(2,1)S(1)}, u32[]{:S(2)}, u32[]{:S(2)}) %collective-permute-start.11) | collective-permute-done | bytes 36896 | tf_op jit(solution)/shard_map/ppermute | solution.py:335
  53.7 0.6 %collective-permute-done.12.refs_3_ = bf16[8,2304]{1,0:T(8,128)(2,1)S(1)} collective-permute-done((bf16[8,2304]{1,0:T(8,128)(2,1)S(1)}, bf16[8,2304]{1,0:T(8,128)(2,1)S(1)}, u32[]{:S(2)}, u32[]{:S(2)}) %collective-permute-start.12) | collective-permute-done | bytes 36896 | tf_op jit(solution)/shard_map/ppermute | solution.py:335
  54.3 0.7 %shard_map.54 = bf16[9,2048]{1,0:T(8,128)(2,1)} custom-call(f32[8,2304]{1,0:T(8,128)S(1)} %get-tuple-element.13.refs_0_, bf16[8,2304]{1,0:T(8,128)(2,1)S(1)} %collective-permute-done.10.refs_1_, bf16[8,2304]{1,0:T(8,128)(2,1)S(1)} %collective-permute-done.11.refs_2_, bf16[8,2304]{1,0:T(8,128)(2,1)S(1)} %collective-permute-done.12.refs_3_), custom_call_target="tpu_custom_call" | custom-call | bytes 1048576 | tf_op jit(solution)/shard_map/pallas_call | solution.py:323
  (1 shorter events, 0.0 us)
Async XLA Ops:
  0.0 8.3 %copy-start = (bf16[9,2048]{1,0:T(8,128)(2,1)S(1)}, bf16[9,2048]{1,0:T(8,128)(2,1)}, u32[]{:S(2)}) copy-start(bf16[9,2048]{1,0:T(8,128)(2,1)} %param.4) | copy-start | bytes 110596
  0.0 8.3 %collective-permute-start.1 = (bf16[9,2048]{1,0:T(8,128)(2,1)}, bf16[9,2048]{1,0:T(8,128)(2,1)S(1)}, u32[]{:S(2)}, u32[]{:S(2)}) collective-permute-start(bf16[9,2048]{1,0:T(8,128)(2,1)} %param.4), channel_id=1, source_target_pairs={{0,2},{1,3},{2,0},{3,1},{4,6},{5,7},{6,4},{7,5},{8,10},{9,11},{10,... | collective-permute-start | bytes 110600 | tf_op jit(solution)/shard_map/ppermute | solution.py:335
  2.9 5.4 %collective-permute-start = (bf16[9,2048]{1,0:T(8,128)(2,1)}, bf16[9,2048]{1,0:T(8,128)(2,1)S(1)}, u32[]{:S(2)}, u32[]{:S(2)}) collective-permute-start(bf16[9,2048]{1,0:T(8,128)(2,1)} %param.4), channel_id=1, source_target_pairs={{0,1},{1,0},{2,3},{3,2},{4,5},{5,4},{6,7},{7,6},{8,9},{9,8},{10,11... | collective-permute-start | bytes 110600 | tf_op jit(solution)/shard_map/ppermute | solution.py:335
  2.9 5.4 %collective-permute-start.2 = (bf16[9,2048]{1,0:T(8,128)(2,1)}, bf16[9,2048]{1,0:T(8,128)(2,1)S(1)}, u32[]{:S(2)}, u32[]{:S(2)}) collective-permute-start(bf16[9,2048]{1,0:T(8,128)(2,1)} %param.4), channel_id=1, source_target_pairs={{0,3},{1,2},{2,1},{3,0},{4,7},{5,6},{6,5},{7,4},{8,11},{9,10},{10,... | collective-permute-start | bytes 110600 | tf_op jit(solution)/shard_map/ppermute | solution.py:335
  10.6 9.6 %collective-permute-start.3 = (bf16[8,14976]{1,0:T(8,128)(2,1)S(1)}, bf16[8,14976]{1,0:T(8,128)(2,1)S(1)}, u32[]{:S(2)}, u32[]{:S(2)}) collective-permute-start(bf16[8,14976]{1,0:T(8,128)(2,1)S(1)} %shard_map.47._), channel_id=1, source_target_pairs={{0,4},{4,0},{8,12},{12,8},{1,5},{5,1},{9,13},{13,9},{2,6},{6,2},{1... | collective-permute-start | bytes 718856 | tf_op jit(solution)/shard_map/ppermute | solution.py:335
  20.2 15.7 %collective-permute-start.4 = (bf16[8,14976]{1,0:T(8,128)(2,1)S(1)}, bf16[8,14976]{1,0:T(8,128)(2,1)S(1)}, u32[]{:S(2)}, u32[]{:S(2)}) collective-permute-start(bf16[8,14976]{1,0:T(8,128)(2,1)S(1)} %add_convert_fusion._), channel_id=1, source_target_pairs={{0,8},{4,12},{8,0},{12,4},{1,9},{5,13},{9,1},{13,5},{2,10},{6,14},... | collective-permute-start | bytes 718856 | tf_op jit(solution)/shard_map/ppermute | solution.py:335
  22.9 12.0 %collective-permute-start.5 = (bf16[8,7552]{1,0:T(8,128)(2,1)S(1)}, bf16[8,7552]{1,0:T(8,128)(2,1)S(1)}, u32[]{:S(2)}, u32[]{:S(2)}) collective-permute-start(bf16[8,7552]{1,0:T(8,128)(2,1)S(1)} %get-tuple-element.12), channel_id=1, source_target_pairs={{0,4},{4,0},{8,12},{12,8},{1,5},{5,1},{9,13},{13,9},{2,6},{6,2},{1... | collective-permute-start | bytes 362504 | tf_op jit(solution)/shard_map/ppermute | solution.py:335
  23.3 20.2 %slice-start = ((s8[27262976]{0:T(1024)(128)(4,1)}), s8[4194304]{0:T(1024)(128)(4,1)S(1)}, s32[]{:S(2)}) async-start(s8[27262976]{0:T(1024)(128)(4,1)} %bitcast), calls=%async_computation | async-start | bytes 8388608
  23.3 20.2 %slice-start.1 = ((s8[27262976]{0:T(1024)(128)(4,1)}), s8[4194304]{0:T(1024)(128)(4,1)S(1)}, s32[]{:S(2)}) async-start(s8[27262976]{0:T(1024)(128)(4,1)} %bitcast), calls=%async_computation.1 | async-start | bytes 8388608
  23.3 20.2 %slice-start.2 = ((s8[27262976]{0:T(1024)(128)(4,1)}), s8[4194304]{0:T(1024)(128)(4,1)S(1)}, s32[]{:S(2)}) async-start(s8[27262976]{0:T(1024)(128)(4,1)} %bitcast), calls=%async_computation.2 | async-start | bytes 8388608
  23.3 20.2 %slice-start.3 = ((s8[27262976]{0:T(1024)(128)(4,1)}), s8[4194304]{0:T(1024)(128)(4,1)S(1)}, s32[]{:S(2)}) async-start(s8[27262976]{0:T(1024)(128)(4,1)} %bitcast), calls=%async_computation.3 | async-start | bytes 8388608
  26.9 16.7 %slice-start.4 = ((s8[27262976]{0:T(1024)(128)(4,1)}), s8[4194304]{0:T(1024)(128)(4,1)S(1)}, s32[]{:S(2)}) async-start(s8[27262976]{0:T(1024)(128)(4,1)} %bitcast), calls=%async_computation.4 | async-start | bytes 8388608
  27.0 16.7 %slice-start.5 = ((s8[27262976]{0:T(1024)(128)(4,1)}), s8[4194304]{0:T(1024)(128)(4,1)S(1)}, s32[]{:S(2)}) async-start(s8[27262976]{0:T(1024)(128)(4,1)} %bitcast), calls=%async_computation.5 | async-start | bytes 8388608
  27.0 16.7 %slice-start.6 = ((s8[27262976]{0:T(1024)(128)(4,1)}), s8[2097152]{0:T(1024)(128)(4,1)S(1)}, s32[]{:S(2)}) async-start(s8[27262976]{0:T(1024)(128)(4,1)} %bitcast), calls=%async_computation.6 | async-start | bytes 4194304
  27.0 9.0 %collective-permute-start.6 = (bf16[8,7552]{1,0:T(8,128)(2,1)S(1)}, bf16[8,7552]{1,0:T(8,128)(2,1)S(1)}, u32[]{:S(2)}, u32[]{:S(2)}) collective-permute-start(bf16[8,7552]{1,0:T(8,128)(2,1)S(1)} %shard_map.49._), channel_id=1, source_target_pairs={{0,4},{4,0},{8,12},{12,8},{1,5},{5,1},{9,13},{13,9},{2,6},{6,2},{1... | collective-permute-start | bytes 362504 | tf_op jit(solution)/shard_map/ppermute | solution.py:335
  36.1 7.4 %collective-permute-start.7 = (bf16[8,7552]{1,0:T(8,128)(2,1)S(1)}, bf16[8,7552]{1,0:T(8,128)(2,1)S(1)}, u32[]{:S(2)}, u32[]{:S(2)}) collective-permute-start(bf16[8,7552]{1,0:T(8,128)(2,1)S(1)} %shard_map.51.refs_0_), channel_id=1, source_target_pairs={{0,8},{4,12},{8,0},{12,4},{1,9},{5,13},{9,1},{13,5},{2,10},{6,14},... | collective-permute-start | bytes 362504 | tf_op jit(solution)/shard_map/ppermute | solution.py:335
  36.2 7.4 %collective-permute-start.9 = (bf16[8,7552]{1,0:T(8,128)(2,1)S(1)}, bf16[8,7552]{1,0:T(8,128)(2,1)S(1)}, u32[]{:S(2)}, u32[]{:S(2)}) collective-permute-start(bf16[8,7552]{1,0:T(8,128)(2,1)S(1)} %shard_map.51.refs_0_), channel_id=1, source_target_pairs={{0,4},{4,0},{8,12},{12,8},{1,5},{5,1},{9,13},{13,9},{2,6},{6,2},{1... | collective-permute-start | bytes 362504 | tf_op jit(solution)/shard_map/ppermute | solution.py:335
  43.4 4.9 %collective-permute-start.8 = (bf16[8,7552]{1,0:T(8,128)(2,1)S(1)}, bf16[8,7552]{1,0:T(8,128)(2,1)S(1)}, u32[]{:S(2)}, u32[]{:S(2)}) collective-permute-start(bf16[8,7552]{1,0:T(8,128)(2,1)S(1)} %collective-permute-done.7.refs_2_), channel_id=1, source_target_pairs={{0,4},{4,0},{8,12},{12,8},{1,5},{5,1},{9,13},{13,9},{2,6},{6,2},{1... | collective-permute-start | bytes 362504 | tf_op jit(solution)/shard_map/ppermute | solution.py:335
  49.6 1.9 %collective-permute-start.10 = (bf16[8,2304]{1,0:T(8,128)(2,1)S(1)}, bf16[8,2304]{1,0:T(8,128)(2,1)S(1)}, u32[]{:S(2)}, u32[]{:S(2)}) collective-permute-start(bf16[8,2304]{1,0:T(8,128)(2,1)S(1)} %get-tuple-element.14), channel_id=1, source_target_pairs={{0,1},{1,0},{2,3},{3,2},{4,5},{5,4},{6,7},{7,6},{8,9},{9,8},{10,11... | collective-permute-start | bytes 110600 | tf_op jit(solution)/shard_map/ppermute | solution.py:335
  49.7 4.0 %collective-permute-start.11 = (bf16[8,2304]{1,0:T(8,128)(2,1)S(1)}, bf16[8,2304]{1,0:T(8,128)(2,1)S(1)}, u32[]{:S(2)}, u32[]{:S(2)}) collective-permute-start(bf16[8,2304]{1,0:T(8,128)(2,1)S(1)} %get-tuple-element.15), channel_id=1, source_target_pairs={{0,2},{1,3},{2,0},{3,1},{4,6},{5,7},{6,4},{7,5},{8,10},{9,11},{10,... | collective-permute-start | bytes 110600 | tf_op jit(solution)/shard_map/ppermute | solution.py:335
  50.9 3.4 %collective-permute-start.12 = (bf16[8,2304]{1,0:T(8,128)(2,1)S(1)}, bf16[8,2304]{1,0:T(8,128)(2,1)S(1)}, u32[]{:S(2)}, u32[]{:S(2)}) collective-permute-start(bf16[8,2304]{1,0:T(8,128)(2,1)S(1)} %get-tuple-element.16), channel_id=1, source_target_pairs={{0,3},{1,2},{2,1},{3,0},{4,7},{5,6},{6,5},{7,4},{8,11},{9,10},{10,... | collective-permute-start | bytes 110600 | tf_op jit(solution)/shard_map/ppermute | solution.py:335

commit v15 on v14

--- a/solution.py
+++ b/solution.py
@@ -10,7 +10,6 @@
 MIB = 1 << 20
 STEP = 256
 COPY_STEP = 512
-IN_FLIGHT = 6
 TOKEN_AXES = ("gy", "gz")
 IN_HBM = pl.BlockSpec(memory_space=pltpu.HBM)
 ANY = pl.BlockSpec(memory_space=pl.ANY)
@@ -23,6 +22,15 @@
 
 def pieces_of(total, step):
     return [(start, min(step, total - start)) for start in range(0, total, step)]
+
+
+def graded_pieces(total):
+    pieces, row = [], 0
+    while total - row > STEP:
+        rows = max(STEP, (total - row) // (2 * STEP) * STEP)
+        pieces.append((row, rows))
+        row += rows
+    return pieces + [(row, total - row)]
 
 
 def in_hbm(value):
@@ -60,10 +68,10 @@
         out[:, at : at + width] = tail.astype(out.dtype)
 
 
-def block_copies(width, distance, weights, held, sems):
+def block_copies(width, distance, weights, pieces, held, sems):
     columns = pl.ds(block_start(distance, width), width)
     copies = []
-    for k, (row, rows) in enumerate(pieces_of(held.shape[1], COPY_STEP)):
+    for k, (row, rows) in enumerate(pieces):
         for w, weight in enumerate(weights):
             copy = pltpu.make_async_copy(
                 weight.at[pl.ds(row, rows), columns], held.at[w, pl.ds(row, rows)], sems.at[w, k]
@@ -72,33 +80,32 @@
     return copies
 
 
-def fetch_kernel(width, distance, gate_ref, up_ref, held, sems):
-    copies = block_copies(width, distance, (gate_ref, up_ref), held, sems)
+def fetch_kernel(width, distance, weight, held, sems):
+    pieces = pieces_of(held.shape[1], COPY_STEP)
+    copies = block_copies(width, distance, (weight,), pieces, held, sems)
     for _, _, _, copy in copies:
         copy.start()
     for _, _, _, copy in copies:
         copy.wait()
 
 
-def fetch(gate_weight, up_weight, distance, width):
-    depth = gate_weight.shape[0]
+def fetch(weight, distance, width):
+    depth = weight.shape[0]
     return pl.pallas_call(
         functools.partial(fetch_kernel, width, distance),
-        out_shape=pltpu.VMEM((2, depth, width), jnp.bfloat16),
-        in_specs=[IN_HBM, IN_HBM],
+        out_shape=pltpu.VMEM((1, depth, width), jnp.bfloat16),
+        in_specs=[IN_HBM],
         out_specs=WHOLE,
-        scratch_shapes=[pltpu.SemaphoreType.DMA((2, len(pieces_of(depth, COPY_STEP))))],
+        scratch_shapes=[pltpu.SemaphoreType.DMA((1, len(pieces_of(depth, COPY_STEP))))],
         compiler_params=params(4),
         cost_estimate=SMALL,
-    )(in_hbm(gate_weight), in_hbm(up_weight))
-
-
-def multiply(x_ref, held, total, steps, waiting=()):
+    )(in_hbm(weight))
+
+
+def multiply(x_ref, held, total, steps):
     for w, first, tall, copy in steps:
         if copy is not None:
             copy.wait()
-        if waiting:
-            waiting.pop(0).start()
         for row, rows in pieces_of(tall, STEP):
             rows = slice(first + row, first + row + rows)
             term = jnp.dot(x_ref[:, rows], held[w, rows, :], preferred_element_type=jnp.float32)
@@ -108,23 +115,32 @@
                 total[w] += term
 
 
-def held_kernel(x_ref, held, out, total):
-    parts = pieces_of(x_ref.shape[1], STEP)
-    multiply(x_ref, held, total, [(w, row, rows, None) for w in range(2) for row, rows in parts])
+def held_kernel(width, distance, x_ref, held, up_ref, out, stream, total, sems):
+    pieces = graded_pieces(stream.shape[1])
+    copies = block_copies(width, distance, (up_ref,), pieces, stream, sems)
+    for _, _, _, copy in copies:
+        copy.start()
+    multiply(x_ref, held, total.at[pl.ds(0, 1)], [(0, 0, held.shape[1], None)])
+    multiply(x_ref, stream, total.at[pl.ds(1, 1)], copies)
     pack_pair(out, total[0], total[1])
 
 
-def gate_up_held(features, held):
-    rows, width = features.shape[0], held.shape[2]
-    return pl.pallas_call(
-        held_kernel,
+def gate_up_held(features, held, up_weight, distance):
+    rows, depth = features.shape
+    width = held.shape[2]
+    return pl.pallas_call(
+        functools.partial(held_kernel, width, distance),
         out_shape=jax.ShapeDtypeStruct((8, packed_pair_width(rows, width)), jnp.bfloat16),
-        in_specs=[WHOLE, WHOLE],
+        in_specs=[WHOLE, WHOLE, IN_HBM],
         out_specs=WHOLE,
-        scratch_shapes=[pltpu.VMEM((2, rows, width), jnp.float32)],
-        compiler_params=params(8),
-        cost_estimate=SMALL,
-    )(features, in_vmem(held))
+        scratch_shapes=[
+            pltpu.VMEM((1, depth, width), jnp.bfloat16),
+            pltpu.VMEM((2, rows, width), jnp.float32),
+            pltpu.SemaphoreType.DMA((1, len(graded_pieces(depth)))),
+        ],
+        compiler_params=params(5 + -(-depth * width * 2 // MIB)),
+        cost_estimate=SMALL,
+    )(features, in_vmem(held), in_hbm(up_weight))
 
 
 def stream_kernel(width, blocks, distances, x_ref, gate_ref, up_ref, _, *refs):
@@ -133,19 +149,21 @@
     for b, which in enumerate(blocks):
         held, total, sems = refs[3 * b : 3 * b + 3]
         weights = [(gate_ref, up_ref)[w] for w in which]
-        copies = block_copies(width, distances[b], weights, held, sems)
+        pieces = stream_pieces(held.shape[1], blocks)
+        copies = block_copies(width, distances[b], weights, pieces, held, sems)
+        for _, _, _, copy in copies:
+            copy.start()
         work.append((outs[b], held, total, copies))
-    waiting = [step[-1] for block in work for step in block[-1]]
-    in_flight = IN_FLIGHT if len(blocks) > 1 else len(waiting)
-    for copy in waiting[:in_flight]:
-        copy.start()
-    waiting = waiting[in_flight:]
     for (out, held, total, copies), which in zip(work, blocks):
-        multiply(x_ref, held, total, copies, waiting)
+        multiply(x_ref, held, total, copies)
         if len(which) == 2:
             pack_pair(out, total[0], total[1])
         else:
             pack_single(out, total[0])
+
+
+def stream_pieces(depth, blocks):
+    return pieces_of(depth, COPY_STEP) if len(blocks) > 1 else graded_pieces(depth)
 
 
 def gate_up_stream(features, gate_weight, up_weight, distances, blocks, width, after):
@@ -157,7 +175,7 @@
         scratch += [
             pltpu.VMEM((len(which), depth, width), jnp.bfloat16),
             pltpu.VMEM((len(which), rows, width), jnp.float32),
-            pltpu.SemaphoreType.DMA((len(which), len(pieces_of(depth, COPY_STEP)))),
+            pltpu.SemaphoreType.DMA((len(which), len(stream_pieces(depth, blocks)))),
         ]
     held_mib = -(-depth * width * 2 * sum(len(which) for which in blocks) // MIB)
     return pl.pallas_call(
@@ -344,7 +362,7 @@
     n_token = lax.axis_size(TOKEN_AXES)
     width = gate_weight.shape[1] // n_gx
 
-    held = fetch(gate_weight, up_weight, 3, width)
+    held = fetch(gate_weight, 3, width)
     features = jnp.concatenate(
         [tokens] + [swap(tokens, TOKEN_AXES, n_token, r) for r in range(1, n_token)], axis=0
     )
@@ -353,7 +371,7 @@
     def blocks_for(distances, blocks, after):
         return gate_up_stream(features, gate_weight, up_weight, distances, blocks, width, after)
 
-    relayed = gate_up_held(features, held)
+    relayed = gate_up_held(features, held, up_weight, 3)
     arrived = swap(relayed, "gx", n_gx, 1)
     across, beside = blocks_for((2, 1), ((0, 1), (0,)), relayed)
     across = lax.optimization_barrier(add(across, arrived).astype(jnp.bfloat16))

time: 55.1 us -> 58.1 us (1.054)
  waiting for transfers between devices: 10.7 us -> 12.6 us
  Pallas kernels: 30.5 us -> 32 us
    pallas_call x1, Pallas kernels: 2.15 us -> 4.61 us  [gate_up_held(): pl.pallas_call(functools.partial(held_kernel, width, distance), out_shape...]
    pallas_call x1, Pallas kernels: 5.16 us -> 3.04 us  [fetch(): pl.pallas_call(functools.partial(fetch_kernel, width, distance), out_shap...]
    ppermute x13, waiting for transfers between devices: 10.7 us -> 12.6 us  [swap(): return lax.ppermute(value, axes, [(i, i ^ distance) for i in range(size)])]
    pallas_call x3, Pallas kernels: 17.4 us -> 18.6 us  [gate_up_stream(): pl.pallas_call(functools.partial(stream_kernel, width, blocks, distances)...]
  transfers between devices with their start and end apart: 13 -> 13, of which waited for: 6 -> 7; matrix products, arithmetic and copies ran while one was open for 0% -> 0% of each run, Pallas kernels for 48% -> 44%
where the time goes in v15:
time: 58.1 us; the launch traced here: 57.9 us
  Pallas kernels  32 us (55%)
  starting transfers between devices  13 us (22%)
  waiting for transfers between devices  12.6 us (22%)
    pallas_call x3, Pallas kernels, gate_up_stream(): pl.pallas_call(functools.partial(stream_kernel, width, blocks, distances)...  18.6 us
    ppermute x13, starting transfers between devices, swap(): return lax.ppermute(value, axes, [(i, i ^ distance) for i in range(size)])  13 us
    ppermute x13, waiting for transfers between devices, swap(): return lax.ppermute(value, axes, [(i, i ^ distance) for i in range(size)])  12.6 us
    pallas_call x2, Pallas kernels, down(): pl.pallas_call(functools.partial(down_kernel, before is None, rows, width...  4.94 us
    pallas_call x1, Pallas kernels, gate_up_held(): pl.pallas_call(functools.partial(held_kernel, width, distance), out_shape...  4.61 us
    pallas_call x1, Pallas kernels, fetch(): pl.pallas_call(functools.partial(fetch_kernel, width, distance), out_shap...  3.04 us
  transfers between devices with their start and end apart: 13, of which 7 were waited for; matrix products, arithmetic and copies ran while one was open for 0% of the time, Pallas kernels for 44%

profile of v15, /device:TPU:0, one launch (start us, length us, event | category | flops | bytes accessed | tf_op | source)
XLA Modules:
  0.0 57.9 jit_solution(10216381432479862544)
XLA Ops:
  0.0 0.0 copy-start
  0.0 2.9 %collective-permute-start.1 = (bf16[9,2048]{1,0:T(8,128)(2,1)}, bf16[9,2048]{1,0:T(8,128)(2,1)S(1)}, u32[]{:S(2)}, u32[]{:S(2)}) collective-permute-start(bf16[9,2048]{1,0:T(8,128)(2,1)} %param.4), channel_id=1, source_target_pairs={{0,2},{1,3},{2,0},{3,1},{4,6},{5,7},{6,4},{7,5},{8,10},{9,11},{10,... | collective-permute-start | bytes 110600 | tf_op jit(solution)/shard_map/ppermute | solution.py:353
  2.9 0.0 collective-permute-start
  2.9 0.2 collective-permute-start.2
  3.1 3.0 %shard_map.46.held = bf16[1,2048,1664]{2,1,0:T(8,128)(2,1)S(1)} custom-call(bf16[2048,6656]{1,0:T(8,128)(2,1)} %gate_ref.5), custom_call_target="tpu_custom_call" | custom-call | bytes 1048576 | tf_op jit(solution)/shard_map/pallas_call | solution.py:94
  6.2 0.0 collective-permute-done.1
  6.2 0.0 collective-permute-done
  6.2 0.7 %collective-permute-done.2 = bf16[9,2048]{1,0:T(8,128)(2,1)S(1)} collective-permute-done((bf16[9,2048]{1,0:T(8,128)(2,1)}, bf16[9,2048]{1,0:T(8,128)(2,1)S(1)}, u32[]{:S(2)}, u32[]{:S(2)}) %collective-permute-start.2) | collective-permute-done | bytes 36896 | tf_op jit(solution)/shard_map/ppermute | solution.py:353
  6.9 0.0 copy-done
  6.9 0.1 pad_maximum_fusion.x_ref
  7.0 4.6 %shard_map.47._ = bf16[8,14976]{1,0:T(8,128)(2,1)S(1)} custom-call(bf16[36,2048]{1,0:T(8,128)(2,1)S(1)} %pad_maximum_fusion.x_ref, bf16[1,2048,1664]{2,1,0:T(8,128)(2,1)S(1)} %shard_map.46.held, bf16[2048,6656]{1,0:T(8,128)(2,1)} %up_ref.7), custom_call_target="tpu_custom_call" | custom-call | bytes 1048576 | tf_op jit(solution)/shard_map/pallas_call | solution.py:131
  11.6 1.6 %collective-permute-start.3 = (bf16[8,14976]{1,0:T(8,128)(2,1)S(1)}, bf16[8,14976]{1,0:T(8,128)(2,1)S(1)}, u32[]{:S(2)}, u32[]{:S(2)}) collective-permute-start(bf16[8,14976]{1,0:T(8,128)(2,1)S(1)} %shard_map.47._), channel_id=1, source_target_pairs={{0,4},{4,0},{8,12},{12,8},{1,5},{5,1},{9,13},{13,9},{2,6},{6,2},{1... | collective-permute-start | bytes 718856 | tf_op jit(solution)/shard_map/ppermute | solution.py:353
  13.2 8.5 %shard_map.48 = (bf16[8,14976]{1,0:T(8,128)(2,1)S(1)}, bf16[8,7552]{1,0:T(8,128)(2,1)S(1)}) custom-call(bf16[36,2048]{1,0:T(8,128)(2,1)S(1)} %pad_maximum_fusion.x_ref, bf16[2048,6656]{1,0:T(8,128)(2,1)} %gate_ref.5, bf16[2048,6656]{1,0:T(8,128)(2,1)} %up_ref.7, bf16[8,14976]{1,0:T(8,128)(2,1)S(1)} %shard_map.47._), custom_call_target="tpu_custom_call" | custom-call | bytes 1048576 | tf_op jit(solution)/shard_map/pallas_call | solution.py:181
  21.7 0.0 collective-permute-done.3
  21.7 0.1 add_convert_fusion._
  21.8 2.7 %collective-permute-start.4 = (bf16[8,14976]{1,0:T(8,128)(2,1)S(1)}, bf16[8,14976]{1,0:T(8,128)(2,1)S(1)}, u32[]{:S(2)}, u32[]{:S(2)}) collective-permute-start(bf16[8,14976]{1,0:T(8,128)(2,1)S(1)} %add_convert_fusion._), channel_id=1, source_target_pairs={{0,8},{4,12},{8,0},{12,4},{1,9},{5,13},{9,1},{13,5},{2,10},{6,14},... | collective-permute-start | bytes 718856 | tf_op jit(solution)/shard_map/ppermute | solution.py:353
  24.5 0.6 %collective-permute-start.5 = (bf16[8,7552]{1,0:T(8,128)(2,1)S(1)}, bf16[8,7552]{1,0:T(8,128)(2,1)S(1)}, u32[]{:S(2)}, u32[]{:S(2)}) collective-permute-start(bf16[8,7552]{1,0:T(8,128)(2,1)S(1)} %get-tuple-element.12), channel_id=1, source_target_pairs={{0,4},{4,0},{8,12},{12,8},{1,5},{5,1},{9,13},{13,9},{2,6},{6,2},{1... | collective-permute-start | bytes 362504 | tf_op jit(solution)/shard_map/ppermute | solution.py:353
  25.0 0.0 slice-start
  25.0 0.0 slice-start.1
  25.1 0.0 slice-start.2
  25.1 0.0 slice-start.3
  25.1 3.7 %shard_map.49._ = bf16[8,7552]{1,0:T(8,128)(2,1)S(1)} custom-call(bf16[36,2048]{1,0:T(8,128)(2,1)S(1)} %pad_maximum_fusion.x_ref, bf16[2048,6656]{1,0:T(8,128)(2,1)} %gate_ref.5, bf16[2048,6656]{1,0:T(8,128)(2,1)} %up_ref.7, bf16[8,14976]{1,0:T(8,128)(2,1)S(1)} %add_convert_fusion._), custom_call_target="tpu_custom_call" | custom-call | bytes 1048576 | tf_op jit(solution)/shard_map/pallas_call | solution.py:181
  28.8 0.0 slice-start.4
  28.8 0.0 slice-start.5
  28.8 0.0 slice-start.6
  28.8 1.5 %collective-permute-start.6 = (bf16[8,7552]{1,0:T(8,128)(2,1)S(1)}, bf16[8,7552]{1,0:T(8,128)(2,1)S(1)}, u32[]{:S(2)}, u32[]{:S(2)}) collective-permute-start(bf16[8,7552]{1,0:T(8,128)(2,1)S(1)} %shard_map.49._), channel_id=1, source_target_pairs={{0,4},{4,0},{8,12},{12,8},{1,5},{5,1},{9,13},{13,9},{2,6},{6,2},{1... | collective-permute-start | bytes 362504 | tf_op jit(solution)/shard_map/ppermute | solution.py:353
  30.3 6.4 %shard_map.50.own = bf16[8,14976]{1,0:T(8,128)(2,1)S(1)} custom-call(bf16[36,2048]{1,0:T(8,128)(2,1)S(1)} %pad_maximum_fusion.x_ref, bf16[2048,6656]{1,0:T(8,128)(2,1)} %gate_ref.5, bf16[2048,6656]{1,0:T(8,128)(2,1)} %up_ref.7, bf16[8,7552]{1,0:T(8,128)(2,1)S(1)} %shard_map.49._), custom_call_target="tpu_custom_call" | custom-call | bytes 1048576 | tf_op jit(solution)/shard_map/pallas_call | solution.py:181
  36.7 0.0 collective-permute-done.5.gate_near
  36.7 1.5 %collective-permute-done.6.up_near = bf16[8,7552]{1,0:T(8,128)(2,1)S(1)} collective-permute-done((bf16[8,7552]{1,0:T(8,128)(2,1)S(1)}, bf16[8,7552]{1,0:T(8,128)(2,1)S(1)}, u32[]{:S(2)}, u32[]{:S(2)}) %collective-permute-start.6) | collective-permute-done | bytes 120864 | tf_op jit(solution)/shard_map/ppermute | solution.py:353
  38.2 0.0 collective-permute-done.4.far
  38.2 0.1 shard_map.51.refs_0_
  38.4 0.1 collective-permute-start.7
  38.4 1.4 %collective-permute-start.9 = (bf16[8,7552]{1,0:T(8,128)(2,1)S(1)}, bf16[8,7552]{1,0:T(8,128)(2,1)S(1)}, u32[]{:S(2)}, u32[]{:S(2)}) collective-permute-start(bf16[8,7552]{1,0:T(8,128)(2,1)S(1)} %shard_map.51.refs_0_), channel_id=1, source_target_pairs={{0,4},{4,0},{8,12},{12,8},{1,5},{5,1},{9,13},{13,9},{2,6},{6,2},{1... | collective-permute-start | bytes 362504 | tf_op jit(solution)/shard_map/ppermute | solution.py:353
  39.9 6.1 %collective-permute-done.7.refs_2_ = bf16[8,7552]{1,0:T(8,128)(2,1)S(1)} collective-permute-done((bf16[8,7552]{1,0:T(8,128)(2,1)S(1)}, bf16[8,7552]{1,0:T(8,128)(2,1)S(1)}, u32[]{:S(2)}, u32[]{:S(2)}) %collective-permute-start.7) | collective-permute-done | bytes 120864 | tf_op jit(solution)/shard_map/ppermute | solution.py:353
  46.0 0.0 collective-permute-start.8
  46.0 0.1 collective-permute-done.9.refs_1_
  46.1 0.0 slice-done
  46.1 0.0 slice-done.1
  46.1 0.0 slice-done.2
  46.1 0.0 slice-done.3
  46.1 0.0 slice-done.4
  46.1 0.0 slice-done.5
  46.2 0.0 slice-done.6
  46.2 3.6 %shard_map.52.refs_1_ = f32[36,2048]{1,0:T(8,128)S(1)} custom-call(bf16[8,7552]{1,0:T(8,128)(2,1)S(1)} %shard_map.51.refs_0_, bf16[8,7552]{1,0:T(8,128)(2,1)S(1)} %collective-permute-done.9.refs_1_, bf16[8,7552]{1,0:T(8,128)(2,1)S(1)} %collective-permute-done.7.refs_2_, bf16[6656,2048]{1,0:T(8,128)(2,1)S(1)} %bitcast.1), custom_call_target="tpu_custom_call" | custom-call | bytes 1048576 | tf_op jit(solution)/shard_map/pallas_call | solution.py:317
  49.8 1.3 %collective-permute-done.8.refs_0_ = bf16[8,7552]{1,0:T(8,128)(2,1)S(1)} collective-permute-done((bf16[8,7552]{1,0:T(8,128)(2,1)S(1)}, bf16[8,7552]{1,0:T(8,128)(2,1)S(1)}, u32[]{:S(2)}, u32[]{:S(2)}) %collective-permute-start.8) | collective-permute-done | bytes 120864 | tf_op jit(solution)/shard_map/ppermute | solution.py:353
  51.2 1.3 %shard_map.53 = (f32[8,2304]{1,0:T(8,128)S(1)}, bf16[8,2304]{1,0:T(8,128)(2,1)S(1)}, bf16[8,2304]{1,0:T(8,128)(2,1)S(1)}, bf16[8,2304]{1,0:T(8,128)(2,1)S(1)}) custom-call(bf16[8,7552]{1,0:T(8,128)(2,1)S(1)} %collective-permute-done.8.refs_0_, f32[36,2048]{1,0:T(8,128)S(1)} %shard_map.52.refs_1_, bf16[6656,2048]{1,0:T(8,128)(2,1)S(1)} %bitcast.1), custom_call_target="tpu_custom_call" | custom-call | bytes 1048576 | tf_op jit(solution)/shard_map/pallas_call | solution.py:317
  52.5 0.1 collective-permute-start.10
  52.6 1.3 %collective-permute-start.11 = (bf16[8,2304]{1,0:T(8,128)(2,1)S(1)}, bf16[8,2304]{1,0:T(8,128)(2,1)S(1)}, u32[]{:S(2)}, u32[]{:S(2)}) collective-permute-start(bf16[8,2304]{1,0:T(8,128)(2,1)S(1)} %get-tuple-element.15), channel_id=1, source_target_pairs={{0,2},{1,3},{2,0},{3,1},{4,6},{5,7},{6,4},{7,5},{8,10},{9,11},{10,... | collective-permute-start | bytes 110600 | tf_op jit(solution)/shard_map/ppermute | solution.py:353
  53.8 0.6 collective-permute-start.12
  54.4 0.0 collective-permute-done.10.refs_1_
  54.4 2.2 %collective-permute-done.11.refs_2_ = bf16[8,2304]{1,0:T(8,128)(2,1)S(1)} collective-permute-done((bf16[8,2304]{1,0:T(8,128)(2,1)S(1)}, bf16[8,2304]{1,0:T(8,128)(2,1)S(1)}, u32[]{:S(2)}, u32[]{:S(2)}) %collective-permute-start.11) | collective-permute-done | bytes 36896 | tf_op jit(solution)/shard_map/ppermute | solution.py:353
  56.6 0.7 %collective-permute-done.12.refs_3_ = bf16[8,2304]{1,0:T(8,128)(2,1)S(1)} collective-permute-done((bf16[8,2304]{1,0:T(8,128)(2,1)S(1)}, bf16[8,2304]{1,0:T(8,128)(2,1)S(1)}, u32[]{:S(2)}, u32[]{:S(2)}) %collective-permute-start.12) | collective-permute-done | bytes 36896 | tf_op jit(solution)/shard_map/ppermute | solution.py:353
  57.3 0.7 %shard_map.54 = bf16[9,2048]{1,0:T(8,128)(2,1)} custom-call(f32[8,2304]{1,0:T(8,128)S(1)} %get-tuple-element.13.refs_0_, bf16[8,2304]{1,0:T(8,128)(2,1)S(1)} %collective-permute-done.10.refs_1_, bf16[8,2304]{1,0:T(8,128)(2,1)S(1)} %collective-permute-done.11.refs_2_, bf16[8,2304]{1,0:T(8,128)(2,1)S(1)} %collective-permute-done.12.refs_3_), custom_call_target="tpu_custom_call" | custom-call | bytes 1048576 | tf_op jit(solution)/shard_map/pallas_call | solution.py:341
  (1 shorter events, 0.0 us)
Async XLA Ops:
  0.0 6.9 %copy-start = (bf16[9,2048]{1,0:T(8,128)(2,1)S(1)}, bf16[9,2048]{1,0:T(8,128)(2,1)}, u32[]{:S(2)}) copy-start(bf16[9,2048]{1,0:T(8,128)(2,1)} %param.4) | copy-start | bytes 110596
  0.0 6.2 %collective-permute-start.1 = (bf16[9,2048]{1,0:T(8,128)(2,1)}, bf16[9,2048]{1,0:T(8,128)(2,1)S(1)}, u32[]{:S(2)}, u32[]{:S(2)}) collective-permute-start(bf16[9,2048]{1,0:T(8,128)(2,1)} %param.4), channel_id=1, source_target_pairs={{0,2},{1,3},{2,0},{3,1},{4,6},{5,7},{6,4},{7,5},{8,10},{9,11},{10,... | collective-permute-start | bytes 110600 | tf_op jit(solution)/shard_map/ppermute | solution.py:353
  2.9 3.3 %collective-permute-start = (bf16[9,2048]{1,0:T(8,128)(2,1)}, bf16[9,2048]{1,0:T(8,128)(2,1)S(1)}, u32[]{:S(2)}, u32[]{:S(2)}) collective-permute-start(bf16[9,2048]{1,0:T(8,128)(2,1)} %param.4), channel_id=1, source_target_pairs={{0,1},{1,0},{2,3},{3,2},{4,5},{5,4},{6,7},{7,6},{8,9},{9,8},{10,11... | collective-permute-start | bytes 110600 | tf_op jit(solution)/shard_map/ppermute | solution.py:353
  2.9 4.0 %collective-permute-start.2 = (bf16[9,2048]{1,0:T(8,128)(2,1)}, bf16[9,2048]{1,0:T(8,128)(2,1)S(1)}, u32[]{:S(2)}, u32[]{:S(2)}) collective-permute-start(bf16[9,2048]{1,0:T(8,128)(2,1)} %param.4), channel_id=1, source_target_pairs={{0,3},{1,2},{2,1},{3,0},{4,7},{5,6},{6,5},{7,4},{8,11},{9,10},{10,... | collective-permute-start | bytes 110600 | tf_op jit(solution)/shard_map/ppermute | solution.py:353
  11.6 10.1 %collective-permute-start.3 = (bf16[8,14976]{1,0:T(8,128)(2,1)S(1)}, bf16[8,14976]{1,0:T(8,128)(2,1)S(1)}, u32[]{:S(2)}, u32[]{:S(2)}) collective-permute-start(bf16[8,14976]{1,0:T(8,128)(2,1)S(1)} %shard_map.47._), channel_id=1, source_target_pairs={{0,4},{4,0},{8,12},{12,8},{1,5},{5,1},{9,13},{13,9},{2,6},{6,2},{1... | collective-permute-start | bytes 718856 | tf_op jit(solution)/shard_map/ppermute | solution.py:353
  21.8 16.4 %collective-permute-start.4 = (bf16[8,14976]{1,0:T(8,128)(2,1)S(1)}, bf16[8,14976]{1,0:T(8,128)(2,1)S(1)}, u32[]{:S(2)}, u32[]{:S(2)}) collective-permute-start(bf16[8,14976]{1,0:T(8,128)(2,1)S(1)} %add_convert_fusion._), channel_id=1, source_target_pairs={{0,8},{4,12},{8,0},{12,4},{1,9},{5,13},{9,1},{13,5},{2,10},{6,14},... | collective-permute-start | bytes 718856 | tf_op jit(solution)/shard_map/ppermute | solution.py:353
  24.5 12.3 %collective-permute-start.5 = (bf16[8,7552]{1,0:T(8,128)(2,1)S(1)}, bf16[8,7552]{1,0:T(8,128)(2,1)S(1)}, u32[]{:S(2)}, u32[]{:S(2)}) collective-permute-start(bf16[8,7552]{1,0:T(8,128)(2,1)S(1)} %get-tuple-element.12), channel_id=1, source_target_pairs={{0,4},{4,0},{8,12},{12,8},{1,5},{5,1},{9,13},{13,9},{2,6},{6,2},{1... | collective-permute-start | bytes 362504 | tf_op jit(solution)/shard_map/ppermute | solution.py:353
  25.0 21.1 %slice-start = ((s8[27262976]{0:T(1024)(128)(4,1)}), s8[4194304]{0:T(1024)(128)(4,1)S(1)}, s32[]{:S(2)}) async-start(s8[27262976]{0:T(1024)(128)(4,1)} %bitcast), calls=%async_computation | async-start | bytes 8388608
  25.0 21.1 %slice-start.1 = ((s8[27262976]{0:T(1024)(128)(4,1)}), s8[4194304]{0:T(1024)(128)(4,1)S(1)}, s32[]{:S(2)}) async-start(s8[27262976]{0:T(1024)(128)(4,1)} %bitcast), calls=%async_computation.1 | async-start | bytes 8388608
  25.1 21.1 %slice-start.2 = ((s8[27262976]{0:T(1024)(128)(4,1)}), s8[4194304]{0:T(1024)(128)(4,1)S(1)}, s32[]{:S(2)}) async-start(s8[27262976]{0:T(1024)(128)(4,1)} %bitcast), calls=%async_computation.2 | async-start | bytes 8388608
  25.1 21.1 %slice-start.3 = ((s8[27262976]{0:T(1024)(128)(4,1)}), s8[4194304]{0:T(1024)(128)(4,1)S(1)}, s32[]{:S(2)}) async-start(s8[27262976]{0:T(1024)(128)(4,1)} %bitcast), calls=%async_computation.3 | async-start | bytes 8388608
  28.8 17.3 %slice-start.4 = ((s8[27262976]{0:T(1024)(128)(4,1)}), s8[4194304]{0:T(1024)(128)(4,1)S(1)}, s32[]{:S(2)}) async-start(s8[27262976]{0:T(1024)(128)(4,1)} %bitcast), calls=%async_computation.4 | async-start | bytes 8388608
  28.8 17.3 %slice-start.5 = ((s8[27262976]{0:T(1024)(128)(4,1)}), s8[4194304]{0:T(1024)(128)(4,1)S(1)}, s32[]{:S(2)}) async-start(s8[27262976]{0:T(1024)(128)(4,1)} %bitcast), calls=%async_computation.5 | async-start | bytes 8388608
  28.8 17.3 %slice-start.6 = ((s8[27262976]{0:T(1024)(128)(4,1)}), s8[2097152]{0:T(1024)(128)(4,1)S(1)}, s32[]{:S(2)}) async-start(s8[27262976]{0:T(1024)(128)(4,1)} %bitcast), calls=%async_computation.6 | async-start | bytes 4194304
  28.8 9.4 %collective-permute-start.6 = (bf16[8,7552]{1,0:T(8,128)(2,1)S(1)}, bf16[8,7552]{1,0:T(8,128)(2,1)S(1)}, u32[]{:S(2)}, u32[]{:S(2)}) collective-permute-start(bf16[8,7552]{1,0:T(8,128)(2,1)S(1)} %shard_map.49._), channel_id=1, source_target_pairs={{0,4},{4,0},{8,12},{12,8},{1,5},{5,1},{9,13},{13,9},{2,6},{6,2},{1... | collective-permute-start | bytes 362504 | tf_op jit(solution)/shard_map/ppermute | solution.py:353
  38.4 7.7 %collective-permute-start.7 = (bf16[8,7552]{1,0:T(8,128)(2,1)S(1)}, bf16[8,7552]{1,0:T(8,128)(2,1)S(1)}, u32[]{:S(2)}, u32[]{:S(2)}) collective-permute-start(bf16[8,7552]{1,0:T(8,128)(2,1)S(1)} %shard_map.51.refs_0_), channel_id=1, source_target_pairs={{0,8},{4,12},{8,0},{12,4},{1,9},{5,13},{9,1},{13,5},{2,10},{6,14},... | collective-permute-start | bytes 362504 | tf_op jit(solution)/shard_map/ppermute | solution.py:353
  38.4 7.7 %collective-permute-start.9 = (bf16[8,7552]{1,0:T(8,128)(2,1)S(1)}, bf16[8,7552]{1,0:T(8,128)(2,1)S(1)}, u32[]{:S(2)}, u32[]{:S(2)}) collective-permute-start(bf16[8,7552]{1,0:T(8,128)(2,1)S(1)} %shard_map.51.refs_0_), channel_id=1, source_target_pairs={{0,4},{4,0},{8,12},{12,8},{1,5},{5,1},{9,13},{13,9},{2,6},{6,2},{1... | collective-permute-start | bytes 362504 | tf_op jit(solution)/shard_map/ppermute | solution.py:353
  46.0 5.1 %collective-permute-start.8 = (bf16[8,7552]{1,0:T(8,128)(2,1)S(1)}, bf16[8,7552]{1,0:T(8,128)(2,1)S(1)}, u32[]{:S(2)}, u32[]{:S(2)}) collective-permute-start(bf16[8,7552]{1,0:T(8,128)(2,1)S(1)} %collective-permute-done.7.refs_2_), channel_id=1, source_target_pairs={{0,4},{4,0},{8,12},{12,8},{1,5},{5,1},{9,13},{13,9},{2,6},{6,2},{1... | collective-permute-start | bytes 362504 | tf_op jit(solution)/shard_map/ppermute | solution.py:353
  52.5 1.9 %collective-permute-start.10 = (bf16[8,2304]{1,0:T(8,128)(2,1)S(1)}, bf16[8,2304]{1,0:T(8,128)(2,1)S(1)}, u32[]{:S(2)}, u32[]{:S(2)}) collective-permute-start(bf16[8,2304]{1,0:T(8,128)(2,1)S(1)} %get-tuple-element.14), channel_id=1, source_target_pairs={{0,1},{1,0},{2,3},{3,2},{4,5},{5,4},{6,7},{7,6},{8,9},{9,8},{10,11... | collective-permute-start | bytes 110600 | tf_op jit(solution)/shard_map/ppermute | solution.py:353
  52.6 4.0 %collective-permute-start.11 = (bf16[8,2304]{1,0:T(8,128)(2,1)S(1)}, bf16[8,2304]{1,0:T(8,128)(2,1)S(1)}, u32[]{:S(2)}, u32[]{:S(2)}) collective-permute-start(bf16[8,2304]{1,0:T(8,128)(2,1)S(1)} %get-tuple-element.15), channel_id=1, source_target_pairs={{0,2},{1,3},{2,0},{3,1},{4,6},{5,7},{6,4},{7,5},{8,10},{9,11},{10,... | collective-permute-start | bytes 110600 | tf_op jit(solution)/shard_map/ppermute | solution.py:353
  53.8 3.4 %collective-permute-start.12 = (bf16[8,2304]{1,0:T(8,128)(2,1)S(1)}, bf16[8,2304]{1,0:T(8,128)(2,1)S(1)}, u32[]{:S(2)}, u32[]{:S(2)}) collective-permute-start(bf16[8,2304]{1,0:T(8,128)(2,1)S(1)} %get-tuple-element.16), channel_id=1, source_target_pairs={{0,3},{1,2},{2,1},{3,0},{4,7},{5,6},{6,5},{7,4},{8,11},{9,10},{10,... | collective-permute-start | bytes 110600 | tf_op jit(solution)/shard_map/ppermute | solution.py:353

commit v16 on v14

--- a/solution.py
+++ b/solution.py
@@ -11,6 +11,7 @@
 STEP = 256
 COPY_STEP = 512
 IN_FLIGHT = 6
+HELD_STEP = 512
 TOKEN_AXES = ("gy", "gz")
 IN_HBM = pl.BlockSpec(memory_space=pltpu.HBM)
 ANY = pl.BlockSpec(memory_space=pl.ANY)
@@ -23,6 +24,14 @@
 
 def pieces_of(total, step):
     return [(start, min(step, total - start)) for start in range(0, total, step)]
+
+
+def copy_pieces(depth, last):
+    if not last:
+        return pieces_of(depth, COPY_STEP)
+    cut = depth // 4 // STEP * STEP
+    small = pieces_of(cut, STEP // 2)
+    return pieces_of(depth - cut, STEP) + [(depth - cut + row, rows) for row, rows in small]
 
 
 def in_hbm(value):
@@ -60,10 +69,10 @@
         out[:, at : at + width] = tail.astype(out.dtype)
 
 
-def block_copies(width, distance, weights, held, sems):
+def block_copies(width, distance, weights, held, sems, last=False):
     columns = pl.ds(block_start(distance, width), width)
     copies = []
-    for k, (row, rows) in enumerate(pieces_of(held.shape[1], COPY_STEP)):
+    for k, (row, rows) in enumerate(copy_pieces(held.shape[1], last)):
         for w, weight in enumerate(weights):
             copy = pltpu.make_async_copy(
                 weight.at[pl.ds(row, rows), columns], held.at[w, pl.ds(row, rows)], sems.at[w, k]
@@ -93,13 +102,13 @@
     )(in_hbm(gate_weight), in_hbm(up_weight))
 
 
-def multiply(x_ref, held, total, steps, waiting=()):
+def multiply(x_ref, held, total, steps, waiting=(), step=STEP):
     for w, first, tall, copy in steps:
         if copy is not None:
             copy.wait()
         if waiting:
             waiting.pop(0).start()
-        for row, rows in pieces_of(tall, STEP):
+        for row, rows in pieces_of(tall, step):
             rows = slice(first + row, first + row + rows)
             term = jnp.dot(x_ref[:, rows], held[w, rows, :], preferred_element_type=jnp.float32)
             if rows.start == 0:
@@ -109,8 +118,7 @@
 
 
 def held_kernel(x_ref, held, out, total):
-    parts = pieces_of(x_ref.shape[1], STEP)
-    multiply(x_ref, held, total, [(w, row, rows, None) for w in range(2) for row, rows in parts])
+    multiply(x_ref, held, total, [(w, 0, held.shape[1], None) for w in range(2)], step=HELD_STEP)
     pack_pair(out, total[0], total[1])
 
 
@@ -133,7 +141,7 @@
     for b, which in enumerate(blocks):
         held, total, sems = refs[3 * b : 3 * b + 3]
         weights = [(gate_ref, up_ref)[w] for w in which]
-        copies = block_copies(width, distances[b], weights, held, sems)
+        copies = block_copies(width, distances[b], weights, held, sems, last=b > 0)
         work.append((outs[b], held, total, copies))
     waiting = [step[-1] for block in work for step in block[-1]]
     in_flight = IN_FLIGHT if len(blocks) > 1 else len(waiting)
@@ -151,13 +159,13 @@
 def gate_up_stream(features, gate_weight, up_weight, distances, blocks, width, after):
     rows, depth = features.shape
     scratch, shapes = [], []
-    for which in blocks:
+    for b, which in enumerate(blocks):
         packed = packed_pair_width(rows, width) if len(which) == 2 else packed_width(rows, width)
         shapes.append(jax.ShapeDtypeStruct((8, packed), jnp.bfloat16))
         scratch += [
             pltpu.VMEM((len(which), depth, width), jnp.bfloat16),
             pltpu.VMEM((len(which), rows, width), jnp.float32),
-            pltpu.SemaphoreType.DMA((len(which), len(pieces_of(depth, COPY_STEP)))),
+            pltpu.SemaphoreType.DMA((len(which), len(copy_pieces(depth, b > 0)))),
         ]
     held_mib = -(-depth * width * 2 * sum(len(which) for which in blocks) // MIB)
     return pl.pallas_call(
@@ -272,7 +280,7 @@
             tail = hidden[b][:, at : at + half].astype(jnp.float32)
             plain[rows - 4 :, :half] = tail[:4]
             plain[rows - 4 :, half:] = tail[4:, : width - half]
-        for row, tall in pieces_of(width, STEP):
+        for row, tall in pieces_of(width, HELD_STEP):
             term = jnp.dot(
                 plain[:, row : row + tall].astype(jnp.bfloat16),
                 held[pl.ds(pl.multiple_of(block_start(distances[b], width) + row, 128), tall), :],

time: 55.1 us -> 56.2 us (1.020)
  Pallas kernels: 30.5 us -> 31.5 us
    pallas_call x3, Pallas kernels: 17.4 us -> 18.1 us  [gate_up_stream(): pl.pallas_call(functools.partial(stream_kernel, width, blocks, distances)...]
where the time goes in v16:
time: 56.2 us; the launch traced here: 56 us
  Pallas kernels  31.5 us (56%)
  starting transfers between devices  13.4 us (24%)
  waiting for transfers between devices  10.8 us (19%)
    pallas_call x3, Pallas kernels, gate_up_stream(): pl.pallas_call(functools.partial(stream_kernel, width, blocks, distances)...  18.1 us
    ppermute x13, starting transfers between devices, swap(): return lax.ppermute(value, axes, [(i, i ^ distance) for i in range(size)])  13.4 us
    ppermute x13, waiting for transfers between devices, swap(): return lax.ppermute(value, axes, [(i, i ^ distance) for i in range(size)])  10.8 us
    pallas_call x1, Pallas kernels, fetch(): pl.pallas_call(functools.partial(fetch_kernel, width, distance), out_shap...  5.16 us
    pallas_call x2, Pallas kernels, down(): pl.pallas_call(functools.partial(down_kernel, before is None, rows, width...  4.92 us
    pallas_call x1, Pallas kernels, gate_up_held(): pl.pallas_call(held_kernel, out_shape=jax.ShapeDtypeStruct((8, packed_pai...  2.47 us
  transfers between devices with their start and end apart: 13, of which 6 were waited for; matrix products, arithmetic and copies ran while one was open for 0% of the time, Pallas kernels for 48%

profile of v16, /device:TPU:0, one launch (start us, length us, event | category | flops | bytes accessed | tf_op | source)
XLA Modules:
  0.0 56.0 jit_solution(12808472050512429484)
XLA Ops:
  0.0 0.0 copy-start
  0.0 2.9 %collective-permute-start.1 = (bf16[9,2048]{1,0:T(8,128)(2,1)}, bf16[9,2048]{1,0:T(8,128)(2,1)S(1)}, u32[]{:S(2)}, u32[]{:S(2)}) collective-permute-start(bf16[9,2048]{1,0:T(8,128)(2,1)} %param.4), channel_id=1, source_target_pairs={{0,2},{1,3},{2,0},{3,1},{4,6},{5,7},{6,4},{7,5},{8,10},{9,11},{10,... | collective-permute-start | bytes 110600 | tf_op jit(solution)/shard_map/ppermute | solution.py:343
  2.9 0.0 collective-permute-start
  2.9 0.2 collective-permute-start.2
  3.1 5.2 %shard_map.46.held = bf16[2,2048,1664]{2,1,0:T(8,128)(2,1)S(1)} custom-call(bf16[2048,6656]{1,0:T(8,128)(2,1)} %gate_ref.7, bf16[2048,6656]{1,0:T(8,128)(2,1)} %up_ref.7), custom_call_target="tpu_custom_call" | custom-call | bytes 1048576 | tf_op jit(solution)/shard_map/pallas_call | solution.py:94
  8.3 0.0 collective-permute-done.1
  8.3 0.0 collective-permute-done
  8.3 0.0 collective-permute-done.2
  8.3 0.0 copy-done
  8.3 0.1 pad_maximum_fusion.x_ref
  8.4 2.5 %shard_map.47._ = bf16[8,14976]{1,0:T(8,128)(2,1)S(1)} custom-call(bf16[36,2048]{1,0:T(8,128)(2,1)S(1)} %pad_maximum_fusion.x_ref, bf16[2,2048,1664]{2,1,0:T(8,128)(2,1)S(1)} %shard_map.46.held), custom_call_target="tpu_custom_call" | custom-call | bytes 1048576 | tf_op jit(solution)/shard_map/pallas_call | solution.py:127
  10.9 2.0 %collective-permute-start.3 = (bf16[8,14976]{1,0:T(8,128)(2,1)S(1)}, bf16[8,14976]{1,0:T(8,128)(2,1)S(1)}, u32[]{:S(2)}, u32[]{:S(2)}) collective-permute-start(bf16[8,14976]{1,0:T(8,128)(2,1)S(1)} %shard_map.47._), channel_id=1, source_target_pairs={{0,4},{4,0},{8,12},{12,8},{1,5},{5,1},{9,13},{13,9},{2,6},{6,2},{1... | collective-permute-start | bytes 718856 | tf_op jit(solution)/shard_map/ppermute | solution.py:343
  12.9 8.3 %shard_map.48 = (bf16[8,14976]{1,0:T(8,128)(2,1)S(1)}, bf16[8,7552]{1,0:T(8,128)(2,1)S(1)}) custom-call(bf16[36,2048]{1,0:T(8,128)(2,1)S(1)} %pad_maximum_fusion.x_ref, bf16[2048,6656]{1,0:T(8,128)(2,1)} %gate_ref.7, bf16[2048,6656]{1,0:T(8,128)(2,1)} %up_ref.7, bf16[8,14976]{1,0:T(8,128)(2,1)S(1)} %shard_map.47._), custom_call_target="tpu_custom_call" | custom-call | bytes 1048576 | tf_op jit(solution)/shard_map/pallas_call | solution.py:171
  21.2 0.0 collective-permute-done.3
  21.2 0.1 add_convert_fusion._
  21.3 2.7 %collective-permute-start.4 = (bf16[8,14976]{1,0:T(8,128)(2,1)S(1)}, bf16[8,14976]{1,0:T(8,128)(2,1)S(1)}, u32[]{:S(2)}, u32[]{:S(2)}) collective-permute-start(bf16[8,14976]{1,0:T(8,128)(2,1)S(1)} %add_convert_fusion._), channel_id=1, source_target_pairs={{0,8},{4,12},{8,0},{12,4},{1,9},{5,13},{9,1},{13,5},{2,10},{6,14},... | collective-permute-start | bytes 718856 | tf_op jit(solution)/shard_map/ppermute | solution.py:343
  24.0 0.4 collective-permute-start.5
  24.4 0.0 slice-start
  24.4 0.0 slice-start.1
  24.4 0.0 slice-start.2
  24.4 0.0 slice-start.3
  24.4 3.6 %shard_map.49._ = bf16[8,7552]{1,0:T(8,128)(2,1)S(1)} custom-call(bf16[36,2048]{1,0:T(8,128)(2,1)S(1)} %pad_maximum_fusion.x_ref, bf16[2048,6656]{1,0:T(8,128)(2,1)} %gate_ref.7, bf16[2048,6656]{1,0:T(8,128)(2,1)} %up_ref.7, bf16[8,14976]{1,0:T(8,128)(2,1)S(1)} %add_convert_fusion._), custom_call_target="tpu_custom_call" | custom-call | bytes 1048576 | tf_op jit(solution)/shard_map/pallas_call | solution.py:171
  28.0 0.0 slice-start.4
  28.0 0.0 slice-start.5
  28.0 0.0 slice-start.6
  28.0 1.7 %collective-permute-start.6 = (bf16[8,7552]{1,0:T(8,128)(2,1)S(1)}, bf16[8,7552]{1,0:T(8,128)(2,1)S(1)}, u32[]{:S(2)}, u32[]{:S(2)}) collective-permute-start(bf16[8,7552]{1,0:T(8,128)(2,1)S(1)} %shard_map.49._), channel_id=1, source_target_pairs={{0,4},{4,0},{8,12},{12,8},{1,5},{5,1},{9,13},{13,9},{2,6},{6,2},{1... | collective-permute-start | bytes 362504 | tf_op jit(solution)/shard_map/ppermute | solution.py:343
  29.7 6.2 %shard_map.50.own = bf16[8,14976]{1,0:T(8,128)(2,1)S(1)} custom-call(bf16[36,2048]{1,0:T(8,128)(2,1)S(1)} %pad_maximum_fusion.x_ref, bf16[2048,6656]{1,0:T(8,128)(2,1)} %gate_ref.7, bf16[2048,6656]{1,0:T(8,128)(2,1)} %up_ref.7, bf16[8,7552]{1,0:T(8,128)(2,1)S(1)} %shard_map.49._), custom_call_target="tpu_custom_call" | custom-call | bytes 1048576 | tf_op jit(solution)/shard_map/pallas_call | solution.py:171
  35.9 0.0 collective-permute-done.5.gate_near
  35.9 1.0 %collective-permute-done.6.up_near = bf16[8,7552]{1,0:T(8,128)(2,1)S(1)} collective-permute-done((bf16[8,7552]{1,0:T(8,128)(2,1)S(1)}, bf16[8,7552]{1,0:T(8,128)(2,1)S(1)}, u32[]{:S(2)}, u32[]{:S(2)}) %collective-permute-start.6) | collective-permute-done | bytes 120864 | tf_op jit(solution)/shard_map/ppermute | solution.py:343
  36.9 0.0 collective-permute-done.4.far
  36.9 0.1 shard_map.51.refs_0_
  37.1 0.1 collective-permute-start.7
  37.2 1.5 %collective-permute-start.9 = (bf16[8,7552]{1,0:T(8,128)(2,1)S(1)}, bf16[8,7552]{1,0:T(8,128)(2,1)S(1)}, u32[]{:S(2)}, u32[]{:S(2)}) collective-permute-start(bf16[8,7552]{1,0:T(8,128)(2,1)S(1)} %shard_map.51.refs_0_), channel_id=1, source_target_pairs={{0,4},{4,0},{8,12},{12,8},{1,5},{5,1},{9,13},{13,9},{2,6},{6,2},{1... | collective-permute-start | bytes 362504 | tf_op jit(solution)/shard_map/ppermute | solution.py:343
  38.6 5.8 %collective-permute-done.7.refs_2_ = bf16[8,7552]{1,0:T(8,128)(2,1)S(1)} collective-permute-done((bf16[8,7552]{1,0:T(8,128)(2,1)S(1)}, bf16[8,7552]{1,0:T(8,128)(2,1)S(1)}, u32[]{:S(2)}, u32[]{:S(2)}) %collective-permute-start.7) | collective-permute-done | bytes 120864 | tf_op jit(solution)/shard_map/ppermute | solution.py:343
  44.5 0.0 collective-permute-start.8
  44.5 0.1 collective-permute-done.9.refs_1_
  44.6 0.0 slice-done
  44.6 0.0 slice-done.1
  44.6 0.0 slice-done.2
  44.6 0.0 slice-done.3
  44.6 0.0 slice-done.4
  44.6 0.0 slice-done.5
  44.6 0.0 slice-done.6
  44.7 3.6 %shard_map.52.refs_1_ = f32[36,2048]{1,0:T(8,128)S(1)} custom-call(bf16[8,7552]{1,0:T(8,128)(2,1)S(1)} %shard_map.51.refs_0_, bf16[8,7552]{1,0:T(8,128)(2,1)S(1)} %collective-permute-done.9.refs_1_, bf16[8,7552]{1,0:T(8,128)(2,1)S(1)} %collective-permute-done.7.refs_2_, bf16[6656,2048]{1,0:T(8,128)(2,1)S(1)} %bitcast.1), custom_call_target="tpu_custom_call" | custom-call | bytes 1048576 | tf_op jit(solution)/shard_map/pallas_call | solution.py:307
  48.3 1.0 %collective-permute-done.8.refs_0_ = bf16[8,7552]{1,0:T(8,128)(2,1)S(1)} collective-permute-done((bf16[8,7552]{1,0:T(8,128)(2,1)S(1)}, bf16[8,7552]{1,0:T(8,128)(2,1)S(1)}, u32[]{:S(2)}, u32[]{:S(2)}) %collective-permute-start.8) | collective-permute-done | bytes 120864 | tf_op jit(solution)/shard_map/ppermute | solution.py:343
  49.3 1.3 %shard_map.53 = (f32[8,2304]{1,0:T(8,128)S(1)}, bf16[8,2304]{1,0:T(8,128)(2,1)S(1)}, bf16[8,2304]{1,0:T(8,128)(2,1)S(1)}, bf16[8,2304]{1,0:T(8,128)(2,1)S(1)}) custom-call(bf16[8,7552]{1,0:T(8,128)(2,1)S(1)} %collective-permute-done.8.refs_0_, f32[36,2048]{1,0:T(8,128)S(1)} %shard_map.52.refs_1_, bf16[6656,2048]{1,0:T(8,128)(2,1)S(1)} %bitcast.1), custom_call_target="tpu_custom_call" | custom-call | bytes 1048576 | tf_op jit(solution)/shard_map/pallas_call | solution.py:307
  50.6 0.1 collective-permute-start.10
  50.7 1.2 %collective-permute-start.11 = (bf16[8,2304]{1,0:T(8,128)(2,1)S(1)}, bf16[8,2304]{1,0:T(8,128)(2,1)S(1)}, u32[]{:S(2)}, u32[]{:S(2)}) collective-permute-start(bf16[8,2304]{1,0:T(8,128)(2,1)S(1)} %get-tuple-element.15), channel_id=1, source_target_pairs={{0,2},{1,3},{2,0},{3,1},{4,6},{5,7},{6,4},{7,5},{8,10},{9,11},{10,... | collective-permute-start | bytes 110600 | tf_op jit(solution)/shard_map/ppermute | solution.py:343
  51.9 0.6 %collective-permute-start.12 = (bf16[8,2304]{1,0:T(8,128)(2,1)S(1)}, bf16[8,2304]{1,0:T(8,128)(2,1)S(1)}, u32[]{:S(2)}, u32[]{:S(2)}) collective-permute-start(bf16[8,2304]{1,0:T(8,128)(2,1)S(1)} %get-tuple-element.16), channel_id=1, source_target_pairs={{0,3},{1,2},{2,1},{3,0},{4,7},{5,6},{6,5},{7,4},{8,11},{9,10},{10,... | collective-permute-start | bytes 110600 | tf_op jit(solution)/shard_map/ppermute | solution.py:343
  52.6 0.0 collective-permute-done.10.refs_1_
  52.6 2.2 %collective-permute-done.11.refs_2_ = bf16[8,2304]{1,0:T(8,128)(2,1)S(1)} collective-permute-done((bf16[8,2304]{1,0:T(8,128)(2,1)S(1)}, bf16[8,2304]{1,0:T(8,128)(2,1)S(1)}, u32[]{:S(2)}, u32[]{:S(2)}) %collective-permute-start.11) | collective-permute-done | bytes 36896 | tf_op jit(solution)/shard_map/ppermute | solution.py:343
  54.7 0.6 %collective-permute-done.12.refs_3_ = bf16[8,2304]{1,0:T(8,128)(2,1)S(1)} collective-permute-done((bf16[8,2304]{1,0:T(8,128)(2,1)S(1)}, bf16[8,2304]{1,0:T(8,128)(2,1)S(1)}, u32[]{:S(2)}, u32[]{:S(2)}) %collective-permute-start.12) | collective-permute-done | bytes 36896 | tf_op jit(solution)/shard_map/ppermute | solution.py:343
  55.4 0.7 %shard_map.54 = bf16[9,2048]{1,0:T(8,128)(2,1)} custom-call(f32[8,2304]{1,0:T(8,128)S(1)} %get-tuple-element.13.refs_0_, bf16[8,2304]{1,0:T(8,128)(2,1)S(1)} %collective-permute-done.10.refs_1_, bf16[8,2304]{1,0:T(8,128)(2,1)S(1)} %collective-permute-done.11.refs_2_, bf16[8,2304]{1,0:T(8,128)(2,1)S(1)} %collective-permute-done.12.refs_3_), custom_call_target="tpu_custom_call" | custom-call | bytes 1048576 | tf_op jit(solution)/shard_map/pallas_call | solution.py:331
  (1 shorter events, 0.0 us)
Async XLA Ops:
  0.0 8.3 %copy-start = (bf16[9,2048]{1,0:T(8,128)(2,1)S(1)}, bf16[9,2048]{1,0:T(8,128)(2,1)}, u32[]{:S(2)}) copy-start(bf16[9,2048]{1,0:T(8,128)(2,1)} %param.4) | copy-start | bytes 110596
  0.0 8.3 %collective-permute-start.1 = (bf16[9,2048]{1,0:T(8,128)(2,1)}, bf16[9,2048]{1,0:T(8,128)(2,1)S(1)}, u32[]{:S(2)}, u32[]{:S(2)}) collective-permute-start(bf16[9,2048]{1,0:T(8,128)(2,1)} %param.4), channel_id=1, source_target_pairs={{0,2},{1,3},{2,0},{3,1},{4,6},{5,7},{6,4},{7,5},{8,10},{9,11},{10,... | collective-permute-start | bytes 110600 | tf_op jit(solution)/shard_map/ppermute | solution.py:343
  2.9 5.4 %collective-permute-start = (bf16[9,2048]{1,0:T(8,128)(2,1)}, bf16[9,2048]{1,0:T(8,128)(2,1)S(1)}, u32[]{:S(2)}, u32[]{:S(2)}) collective-permute-start(bf16[9,2048]{1,0:T(8,128)(2,1)} %param.4), channel_id=1, source_target_pairs={{0,1},{1,0},{2,3},{3,2},{4,5},{5,4},{6,7},{7,6},{8,9},{9,8},{10,11... | collective-permute-start | bytes 110600 | tf_op jit(solution)/shard_map/ppermute | solution.py:343
  2.9 5.4 %collective-permute-start.2 = (bf16[9,2048]{1,0:T(8,128)(2,1)}, bf16[9,2048]{1,0:T(8,128)(2,1)S(1)}, u32[]{:S(2)}, u32[]{:S(2)}) collective-permute-start(bf16[9,2048]{1,0:T(8,128)(2,1)} %param.4), channel_id=1, source_target_pairs={{0,3},{1,2},{2,1},{3,0},{4,7},{5,6},{6,5},{7,4},{8,11},{9,10},{10,... | collective-permute-start | bytes 110600 | tf_op jit(solution)/shard_map/ppermute | solution.py:343
  10.9 10.3 %collective-permute-start.3 = (bf16[8,14976]{1,0:T(8,128)(2,1)S(1)}, bf16[8,14976]{1,0:T(8,128)(2,1)S(1)}, u32[]{:S(2)}, u32[]{:S(2)}) collective-permute-start(bf16[8,14976]{1,0:T(8,128)(2,1)S(1)} %shard_map.47._), channel_id=1, source_target_pairs={{0,4},{4,0},{8,12},{12,8},{1,5},{5,1},{9,13},{13,9},{2,6},{6,2},{1... | collective-permute-start | bytes 718856 | tf_op jit(solution)/shard_map/ppermute | solution.py:343
  21.3 15.7 %collective-permute-start.4 = (bf16[8,14976]{1,0:T(8,128)(2,1)S(1)}, bf16[8,14976]{1,0:T(8,128)(2,1)S(1)}, u32[]{:S(2)}, u32[]{:S(2)}) collective-permute-start(bf16[8,14976]{1,0:T(8,128)(2,1)S(1)} %add_convert_fusion._), channel_id=1, source_target_pairs={{0,8},{4,12},{8,0},{12,4},{1,9},{5,13},{9,1},{13,5},{2,10},{6,14},... | collective-permute-start | bytes 718856 | tf_op jit(solution)/shard_map/ppermute | solution.py:343
  24.0 12.0 %collective-permute-start.5 = (bf16[8,7552]{1,0:T(8,128)(2,1)S(1)}, bf16[8,7552]{1,0:T(8,128)(2,1)S(1)}, u32[]{:S(2)}, u32[]{:S(2)}) collective-permute-start(bf16[8,7552]{1,0:T(8,128)(2,1)S(1)} %get-tuple-element.12), channel_id=1, source_target_pairs={{0,4},{4,0},{8,12},{12,8},{1,5},{5,1},{9,13},{13,9},{2,6},{6,2},{1... | collective-permute-start | bytes 362504 | tf_op jit(solution)/shard_map/ppermute | solution.py:343
  24.4 20.2 %slice-start = ((s8[27262976]{0:T(1024)(128)(4,1)}), s8[4194304]{0:T(1024)(128)(4,1)S(1)}, s32[]{:S(2)}) async-start(s8[27262976]{0:T(1024)(128)(4,1)} %bitcast), calls=%async_computation | async-start | bytes 8388608
  24.4 20.2 %slice-start.1 = ((s8[27262976]{0:T(1024)(128)(4,1)}), s8[4194304]{0:T(1024)(128)(4,1)S(1)}, s32[]{:S(2)}) async-start(s8[27262976]{0:T(1024)(128)(4,1)} %bitcast), calls=%async_computation.1 | async-start | bytes 8388608
  24.4 20.2 %slice-start.2 = ((s8[27262976]{0:T(1024)(128)(4,1)}), s8[4194304]{0:T(1024)(128)(4,1)S(1)}, s32[]{:S(2)}) async-start(s8[27262976]{0:T(1024)(128)(4,1)} %bitcast), calls=%async_computation.2 | async-start | bytes 8388608
  24.4 20.2 %slice-start.3 = ((s8[27262976]{0:T(1024)(128)(4,1)}), s8[4194304]{0:T(1024)(128)(4,1)S(1)}, s32[]{:S(2)}) async-start(s8[27262976]{0:T(1024)(128)(4,1)} %bitcast), calls=%async_computation.3 | async-start | bytes 8388608
  28.0 16.7 %slice-start.4 = ((s8[27262976]{0:T(1024)(128)(4,1)}), s8[4194304]{0:T(1024)(128)(4,1)S(1)}, s32[]{:S(2)}) async-start(s8[27262976]{0:T(1024)(128)(4,1)} %bitcast), calls=%async_computation.4 | async-start | bytes 8388608
  28.0 16.7 %slice-start.5 = ((s8[27262976]{0:T(1024)(128)(4,1)}), s8[4194304]{0:T(1024)(128)(4,1)S(1)}, s32[]{:S(2)}) async-start(s8[27262976]{0:T(1024)(128)(4,1)} %bitcast), calls=%async_computation.5 | async-start | bytes 8388608
  28.0 16.7 %slice-start.6 = ((s8[27262976]{0:T(1024)(128)(4,1)}), s8[2097152]{0:T(1024)(128)(4,1)S(1)}, s32[]{:S(2)}) async-start(s8[27262976]{0:T(1024)(128)(4,1)} %bitcast), calls=%async_computation.6 | async-start | bytes 4194304
  28.0 8.9 %collective-permute-start.6 = (bf16[8,7552]{1,0:T(8,128)(2,1)S(1)}, bf16[8,7552]{1,0:T(8,128)(2,1)S(1)}, u32[]{:S(2)}, u32[]{:S(2)}) collective-permute-start(bf16[8,7552]{1,0:T(8,128)(2,1)S(1)} %shard_map.49._), channel_id=1, source_target_pairs={{0,4},{4,0},{8,12},{12,8},{1,5},{5,1},{9,13},{13,9},{2,6},{6,2},{1... | collective-permute-start | bytes 362504 | tf_op jit(solution)/shard_map/ppermute | solution.py:343
  37.1 7.4 %collective-permute-start.7 = (bf16[8,7552]{1,0:T(8,128)(2,1)S(1)}, bf16[8,7552]{1,0:T(8,128)(2,1)S(1)}, u32[]{:S(2)}, u32[]{:S(2)}) collective-permute-start(bf16[8,7552]{1,0:T(8,128)(2,1)S(1)} %shard_map.51.refs_0_), channel_id=1, source_target_pairs={{0,8},{4,12},{8,0},{12,4},{1,9},{5,13},{9,1},{13,5},{2,10},{6,14},... | collective-permute-start | bytes 362504 | tf_op jit(solution)/shard_map/ppermute | solution.py:343
  37.2 7.4 %collective-permute-start.9 = (bf16[8,7552]{1,0:T(8,128)(2,1)S(1)}, bf16[8,7552]{1,0:T(8,128)(2,1)S(1)}, u32[]{:S(2)}, u32[]{:S(2)}) collective-permute-start(bf16[8,7552]{1,0:T(8,128)(2,1)S(1)} %shard_map.51.refs_0_), channel_id=1, source_target_pairs={{0,4},{4,0},{8,12},{12,8},{1,5},{5,1},{9,13},{13,9},{2,6},{6,2},{1... | collective-permute-start | bytes 362504 | tf_op jit(solution)/shard_map/ppermute | solution.py:343
  44.5 4.9 %collective-permute-start.8 = (bf16[8,7552]{1,0:T(8,128)(2,1)S(1)}, bf16[8,7552]{1,0:T(8,128)(2,1)S(1)}, u32[]{:S(2)}, u32[]{:S(2)}) collective-permute-start(bf16[8,7552]{1,0:T(8,128)(2,1)S(1)} %collective-permute-done.7.refs_2_), channel_id=1, source_target_pairs={{0,4},{4,0},{8,12},{12,8},{1,5},{5,1},{9,13},{13,9},{2,6},{6,2},{1... | collective-permute-start | bytes 362504 | tf_op jit(solution)/shard_map/ppermute | solution.py:343
  50.6 1.9 %collective-permute-start.10 = (bf16[8,2304]{1,0:T(8,128)(2,1)S(1)}, bf16[8,2304]{1,0:T(8,128)(2,1)S(1)}, u32[]{:S(2)}, u32[]{:S(2)}) collective-permute-start(bf16[8,2304]{1,0:T(8,128)(2,1)S(1)} %get-tuple-element.14), channel_id=1, source_target_pairs={{0,1},{1,0},{2,3},{3,2},{4,5},{5,4},{6,7},{7,6},{8,9},{9,8},{10,11... | collective-permute-start | bytes 110600 | tf_op jit(solution)/shard_map/ppermute | solution.py:343
  50.7 4.0 %collective-permute-start.11 = (bf16[8,2304]{1,0:T(8,128)(2,1)S(1)}, bf16[8,2304]{1,0:T(8,128)(2,1)S(1)}, u32[]{:S(2)}, u32[]{:S(2)}) collective-permute-start(bf16[8,2304]{1,0:T(8,128)(2,1)S(1)} %get-tuple-element.15), channel_id=1, source_target_pairs={{0,2},{1,3},{2,0},{3,1},{4,6},{5,7},{6,4},{7,5},{8,10},{9,11},{10,... | collective-permute-start | bytes 110600 | tf_op jit(solution)/shard_map/ppermute | solution.py:343
  51.9 3.4 %collective-permute-start.12 = (bf16[8,2304]{1,0:T(8,128)(2,1)S(1)}, bf16[8,2304]{1,0:T(8,128)(2,1)S(1)}, u32[]{:S(2)}, u32[]{:S(2)}) collective-permute-start(bf16[8,2304]{1,0:T(8,128)(2,1)S(1)} %get-tuple-element.16), channel_id=1, source_target_pairs={{0,3},{1,2},{2,1},{3,0},{4,7},{5,6},{6,5},{7,4},{8,11},{9,10},{10,... | collective-permute-start | bytes 110600 | tf_op jit(solution)/shard_map/ppermute | solution.py:343

commit v17 on v14

--- a/solution.py
+++ b/solution.py
@@ -10,7 +10,9 @@
 MIB = 1 << 20
 STEP = 256
 COPY_STEP = 512
-IN_FLIGHT = 6
+LARGE_STEP = 1024
+IN_FLIGHT = 4
+DOWN_STEP = 512
 TOKEN_AXES = ("gy", "gz")
 IN_HBM = pl.BlockSpec(memory_space=pltpu.HBM)
 ANY = pl.BlockSpec(memory_space=pl.ANY)
@@ -60,10 +62,10 @@
         out[:, at : at + width] = tail.astype(out.dtype)
 
 
-def block_copies(width, distance, weights, held, sems):
+def block_copies(width, distance, weights, held, sems, step=COPY_STEP):
     columns = pl.ds(block_start(distance, width), width)
     copies = []
-    for k, (row, rows) in enumerate(pieces_of(held.shape[1], COPY_STEP)):
+    for k, (row, rows) in enumerate(pieces_of(held.shape[1], step)):
         for w, weight in enumerate(weights):
             copy = pltpu.make_async_copy(
                 weight.at[pl.ds(row, rows), columns], held.at[w, pl.ds(row, rows)], sems.at[w, k]
@@ -127,18 +129,23 @@
     )(features, in_vmem(held))
 
 
+def stream_step(blocks):
+    return COPY_STEP if len(blocks) == 1 else LARGE_STEP
+
+
 def stream_kernel(width, blocks, distances, x_ref, gate_ref, up_ref, _, *refs):
     outs, refs = refs[: len(blocks)], refs[len(blocks) :]
     work = []
     for b, which in enumerate(blocks):
         held, total, sems = refs[3 * b : 3 * b + 3]
         weights = [(gate_ref, up_ref)[w] for w in which]
-        copies = block_copies(width, distances[b], weights, held, sems)
+        copies = block_copies(width, distances[b], weights, held, sems, stream_step(blocks))
         work.append((outs[b], held, total, copies))
     waiting = [step[-1] for block in work for step in block[-1]]
-    in_flight = IN_FLIGHT if len(blocks) > 1 else len(waiting)
+    alone = len(blocks) == 1
+    in_flight = len(waiting) if alone else IN_FLIGHT
     for copy in waiting[:in_flight]:
-        copy.start()
+        copy.start(priority=int(alone))
     waiting = waiting[in_flight:]
     for (out, held, total, copies), which in zip(work, blocks):
         multiply(x_ref, held, total, copies, waiting)
@@ -157,7 +164,7 @@
         scratch += [
             pltpu.VMEM((len(which), depth, width), jnp.bfloat16),
             pltpu.VMEM((len(which), rows, width), jnp.float32),
-            pltpu.SemaphoreType.DMA((len(which), len(pieces_of(depth, COPY_STEP)))),
+            pltpu.SemaphoreType.DMA((len(which), len(pieces_of(depth, stream_step(blocks))))),
         ]
     held_mib = -(-depth * width * 2 * sum(len(which) for which in blocks) // MIB)
     return pl.pallas_call(
@@ -272,7 +279,7 @@
             tail = hidden[b][:, at : at + half].astype(jnp.float32)
             plain[rows - 4 :, :half] = tail[:4]
             plain[rows - 4 :, half:] = tail[4:, : width - half]
-        for row, tall in pieces_of(width, STEP):
+        for row, tall in pieces_of(width, DOWN_STEP):
             term = jnp.dot(
                 plain[:, row : row + tall].astype(jnp.bfloat16),
                 held[pl.ds(pl.multiple_of(block_start(distances[b], width) + row, 128), tall), :],

time: 55.1 us -> 55.4 us (level)
  no operation moved by 1% of the time
where the time goes in v17:
time: 55.4 us; the launch traced here: 55.3 us
  Pallas kernels  30.7 us (55%)
  starting transfers between devices  13.4 us (24%)
  waiting for transfers between devices  10.8 us (19%)
    pallas_call x3, Pallas kernels, gate_up_stream(): pl.pallas_call(functools.partial(stream_kernel, width, blocks, distances)...  17.7 us
    ppermute x13, starting transfers between devices, swap(): return lax.ppermute(value, axes, [(i, i ^ distance) for i in range(size)])  13.4 us
    ppermute x13, waiting for transfers between devices, swap(): return lax.ppermute(value, axes, [(i, i ^ distance) for i in range(size)])  10.8 us
    pallas_call x1, Pallas kernels, fetch(): pl.pallas_call(functools.partial(fetch_kernel, width, distance), out_shap...  5.16 us
    pallas_call x2, Pallas kernels, down(): pl.pallas_call(functools.partial(down_kernel, before is None, rows, width...  4.92 us
    pallas_call x1, Pallas kernels, gate_up_held(): pl.pallas_call(held_kernel, out_shape=jax.ShapeDtypeStruct((8, packed_pai...  2.15 us
  transfers between devices with their start and end apart: 13, of which 6 were waited for; matrix products, arithmetic and copies ran while one was open for 0% of the time, Pallas kernels for 48%

profile of v17, /device:TPU:0, one launch (start us, length us, event | category | flops | bytes accessed | tf_op | source)
XLA Modules:
  0.0 55.3 jit_solution(11973656612587789323)
XLA Ops:
  0.0 0.0 copy-start
  0.0 2.9 %collective-permute-start.1 = (bf16[9,2048]{1,0:T(8,128)(2,1)}, bf16[9,2048]{1,0:T(8,128)(2,1)S(1)}, u32[]{:S(2)}, u32[]{:S(2)}) collective-permute-start(bf16[9,2048]{1,0:T(8,128)(2,1)} %param.4), channel_id=1, source_target_pairs={{0,2},{1,3},{2,0},{3,1},{4,6},{5,7},{6,4},{7,5},{8,10},{9,11},{10,... | collective-permute-start | bytes 110600 | tf_op jit(solution)/shard_map/ppermute | solution.py:342
  2.9 0.0 collective-permute-start
  2.9 0.2 collective-permute-start.2
  3.1 5.2 %shard_map.46.held = bf16[2,2048,1664]{2,1,0:T(8,128)(2,1)S(1)} custom-call(bf16[2048,6656]{1,0:T(8,128)(2,1)} %gate_ref.7, bf16[2048,6656]{1,0:T(8,128)(2,1)} %up_ref.7), custom_call_target="tpu_custom_call" | custom-call | bytes 1048576 | tf_op jit(solution)/shard_map/pallas_call | solution.py:87
  8.3 0.0 collective-permute-done.1
  8.3 0.0 collective-permute-done
  8.3 0.0 collective-permute-done.2
  8.3 0.0 copy-done
  8.3 0.1 pad_maximum_fusion.x_ref
  8.4 2.2 %shard_map.47._ = bf16[8,14976]{1,0:T(8,128)(2,1)S(1)} custom-call(bf16[36,2048]{1,0:T(8,128)(2,1)S(1)} %pad_maximum_fusion.x_ref, bf16[2,2048,1664]{2,1,0:T(8,128)(2,1)S(1)} %shard_map.46.held), custom_call_target="tpu_custom_call" | custom-call | bytes 1048576 | tf_op jit(solution)/shard_map/pallas_call | solution.py:121
  10.6 2.0 %collective-permute-start.3 = (bf16[8,14976]{1,0:T(8,128)(2,1)S(1)}, bf16[8,14976]{1,0:T(8,128)(2,1)S(1)}, u32[]{:S(2)}, u32[]{:S(2)}) collective-permute-start(bf16[8,14976]{1,0:T(8,128)(2,1)S(1)} %shard_map.47._), channel_id=1, source_target_pairs={{0,4},{4,0},{8,12},{12,8},{1,5},{5,1},{9,13},{13,9},{2,6},{6,2},{1... | collective-permute-start | bytes 718856 | tf_op jit(solution)/shard_map/ppermute | solution.py:342
  12.6 7.8 %shard_map.48 = (bf16[8,14976]{1,0:T(8,128)(2,1)S(1)}, bf16[8,7552]{1,0:T(8,128)(2,1)S(1)}) custom-call(bf16[36,2048]{1,0:T(8,128)(2,1)S(1)} %pad_maximum_fusion.x_ref, bf16[2048,6656]{1,0:T(8,128)(2,1)} %gate_ref.7, bf16[2048,6656]{1,0:T(8,128)(2,1)} %up_ref.7, bf16[8,14976]{1,0:T(8,128)(2,1)S(1)} %shard_map.47._), custom_call_target="tpu_custom_call" | custom-call | bytes 1048576 | tf_op jit(solution)/shard_map/pallas_call | solution.py:170
  20.4 0.0 collective-permute-done.3
  20.4 0.1 add_convert_fusion._
  20.5 2.7 %collective-permute-start.4 = (bf16[8,14976]{1,0:T(8,128)(2,1)S(1)}, bf16[8,14976]{1,0:T(8,128)(2,1)S(1)}, u32[]{:S(2)}, u32[]{:S(2)}) collective-permute-start(bf16[8,14976]{1,0:T(8,128)(2,1)S(1)} %add_convert_fusion._), channel_id=1, source_target_pairs={{0,8},{4,12},{8,0},{12,4},{1,9},{5,13},{9,1},{13,5},{2,10},{6,14},... | collective-permute-start | bytes 718856 | tf_op jit(solution)/shard_map/ppermute | solution.py:342
  23.2 0.4 collective-permute-start.5
  23.6 0.0 slice-start
  23.6 0.0 slice-start.1
  23.6 0.0 slice-start.2
  23.6 0.0 slice-start.3
  23.6 3.6 %shard_map.49._ = bf16[8,7552]{1,0:T(8,128)(2,1)S(1)} custom-call(bf16[36,2048]{1,0:T(8,128)(2,1)S(1)} %pad_maximum_fusion.x_ref, bf16[2048,6656]{1,0:T(8,128)(2,1)} %gate_ref.7, bf16[2048,6656]{1,0:T(8,128)(2,1)} %up_ref.7, bf16[8,14976]{1,0:T(8,128)(2,1)S(1)} %add_convert_fusion._), custom_call_target="tpu_custom_call" | custom-call | bytes 1048576 | tf_op jit(solution)/shard_map/pallas_call | solution.py:170
  27.2 0.0 slice-start.4
  27.2 0.0 slice-start.5
  27.2 0.0 slice-start.6
  27.2 1.7 %collective-permute-start.6 = (bf16[8,7552]{1,0:T(8,128)(2,1)S(1)}, bf16[8,7552]{1,0:T(8,128)(2,1)S(1)}, u32[]{:S(2)}, u32[]{:S(2)}) collective-permute-start(bf16[8,7552]{1,0:T(8,128)(2,1)S(1)} %shard_map.49._), channel_id=1, source_target_pairs={{0,4},{4,0},{8,12},{12,8},{1,5},{5,1},{9,13},{13,9},{2,6},{6,2},{1... | collective-permute-start | bytes 362504 | tf_op jit(solution)/shard_map/ppermute | solution.py:342
  28.9 6.2 %shard_map.50.own = bf16[8,14976]{1,0:T(8,128)(2,1)S(1)} custom-call(bf16[36,2048]{1,0:T(8,128)(2,1)S(1)} %pad_maximum_fusion.x_ref, bf16[2048,6656]{1,0:T(8,128)(2,1)} %gate_ref.7, bf16[2048,6656]{1,0:T(8,128)(2,1)} %up_ref.7, bf16[8,7552]{1,0:T(8,128)(2,1)S(1)} %shard_map.49._), custom_call_target="tpu_custom_call" | custom-call | bytes 1048576 | tf_op jit(solution)/shard_map/pallas_call | solution.py:170
  35.2 0.0 collective-permute-done.5.gate_near
  35.2 1.0 %collective-permute-done.6.up_near = bf16[8,7552]{1,0:T(8,128)(2,1)S(1)} collective-permute-done((bf16[8,7552]{1,0:T(8,128)(2,1)S(1)}, bf16[8,7552]{1,0:T(8,128)(2,1)S(1)}, u32[]{:S(2)}, u32[]{:S(2)}) %collective-permute-start.6) | collective-permute-done | bytes 120864 | tf_op jit(solution)/shard_map/ppermute | solution.py:342
  36.2 0.0 collective-permute-done.4.far
  36.2 0.1 shard_map.51.refs_0_
  36.3 0.1 collective-permute-start.7
  36.4 1.5 %collective-permute-start.9 = (bf16[8,7552]{1,0:T(8,128)(2,1)S(1)}, bf16[8,7552]{1,0:T(8,128)(2,1)S(1)}, u32[]{:S(2)}, u32[]{:S(2)}) collective-permute-start(bf16[8,7552]{1,0:T(8,128)(2,1)S(1)} %shard_map.51.refs_0_), channel_id=1, source_target_pairs={{0,4},{4,0},{8,12},{12,8},{1,5},{5,1},{9,13},{13,9},{2,6},{6,2},{1... | collective-permute-start | bytes 362504 | tf_op jit(solution)/shard_map/ppermute | solution.py:342
  37.9 5.8 %collective-permute-done.7.refs_2_ = bf16[8,7552]{1,0:T(8,128)(2,1)S(1)} collective-permute-done((bf16[8,7552]{1,0:T(8,128)(2,1)S(1)}, bf16[8,7552]{1,0:T(8,128)(2,1)S(1)}, u32[]{:S(2)}, u32[]{:S(2)}) %collective-permute-start.7) | collective-permute-done | bytes 120864 | tf_op jit(solution)/shard_map/ppermute | solution.py:342
  43.7 0.0 collective-permute-start.8
  43.7 0.1 collective-permute-done.9.refs_1_
  43.8 0.0 slice-done
  43.8 0.0 slice-done.1
  43.8 0.0 slice-done.2
  43.8 0.0 slice-done.3
  43.8 0.0 slice-done.4
  43.9 0.0 slice-done.5
  43.9 0.0 slice-done.6
  43.9 3.6 %shard_map.52.refs_1_ = f32[36,2048]{1,0:T(8,128)S(1)} custom-call(bf16[8,7552]{1,0:T(8,128)(2,1)S(1)} %shard_map.51.refs_0_, bf16[8,7552]{1,0:T(8,128)(2,1)S(1)} %collective-permute-done.9.refs_1_, bf16[8,7552]{1,0:T(8,128)(2,1)S(1)} %collective-permute-done.7.refs_2_, bf16[6656,2048]{1,0:T(8,128)(2,1)S(1)} %bitcast.1), custom_call_target="tpu_custom_call" | custom-call | bytes 1048576 | tf_op jit(solution)/shard_map/pallas_call | solution.py:306
  47.5 1.0 %collective-permute-done.8.refs_0_ = bf16[8,7552]{1,0:T(8,128)(2,1)S(1)} collective-permute-done((bf16[8,7552]{1,0:T(8,128)(2,1)S(1)}, bf16[8,7552]{1,0:T(8,128)(2,1)S(1)}, u32[]{:S(2)}, u32[]{:S(2)}) %collective-permute-start.8) | collective-permute-done | bytes 120864 | tf_op jit(solution)/shard_map/ppermute | solution.py:342
  48.5 1.3 %shard_map.53 = (f32[8,2304]{1,0:T(8,128)S(1)}, bf16[8,2304]{1,0:T(8,128)(2,1)S(1)}, bf16[8,2304]{1,0:T(8,128)(2,1)S(1)}, bf16[8,2304]{1,0:T(8,128)(2,1)S(1)}) custom-call(bf16[8,7552]{1,0:T(8,128)(2,1)S(1)} %collective-permute-done.8.refs_0_, f32[36,2048]{1,0:T(8,128)S(1)} %shard_map.52.refs_1_, bf16[6656,2048]{1,0:T(8,128)(2,1)S(1)} %bitcast.1), custom_call_target="tpu_custom_call" | custom-call | bytes 1048576 | tf_op jit(solution)/shard_map/pallas_call | solution.py:306
  49.9 0.1 collective-permute-start.10
  49.9 1.2 %collective-permute-start.11 = (bf16[8,2304]{1,0:T(8,128)(2,1)S(1)}, bf16[8,2304]{1,0:T(8,128)(2,1)S(1)}, u32[]{:S(2)}, u32[]{:S(2)}) collective-permute-start(bf16[8,2304]{1,0:T(8,128)(2,1)S(1)} %get-tuple-element.15), channel_id=1, source_target_pairs={{0,2},{1,3},{2,0},{3,1},{4,6},{5,7},{6,4},{7,5},{8,10},{9,11},{10,... | collective-permute-start | bytes 110600 | tf_op jit(solution)/shard_map/ppermute | solution.py:342
  51.2 0.6 %collective-permute-start.12 = (bf16[8,2304]{1,0:T(8,128)(2,1)S(1)}, bf16[8,2304]{1,0:T(8,128)(2,1)S(1)}, u32[]{:S(2)}, u32[]{:S(2)}) collective-permute-start(bf16[8,2304]{1,0:T(8,128)(2,1)S(1)} %get-tuple-element.16), channel_id=1, source_target_pairs={{0,3},{1,2},{2,1},{3,0},{4,7},{5,6},{6,5},{7,4},{8,11},{9,10},{10,... | collective-permute-start | bytes 110600 | tf_op jit(solution)/shard_map/ppermute | solution.py:342
  51.8 0.0 collective-permute-done.10.refs_1_
  51.8 2.2 %collective-permute-done.11.refs_2_ = bf16[8,2304]{1,0:T(8,128)(2,1)S(1)} collective-permute-done((bf16[8,2304]{1,0:T(8,128)(2,1)S(1)}, bf16[8,2304]{1,0:T(8,128)(2,1)S(1)}, u32[]{:S(2)}, u32[]{:S(2)}) %collective-permute-start.11) | collective-permute-done | bytes 36896 | tf_op jit(solution)/shard_map/ppermute | solution.py:342
  54.0 0.7 %collective-permute-done.12.refs_3_ = bf16[8,2304]{1,0:T(8,128)(2,1)S(1)} collective-permute-done((bf16[8,2304]{1,0:T(8,128)(2,1)S(1)}, bf16[8,2304]{1,0:T(8,128)(2,1)S(1)}, u32[]{:S(2)}, u32[]{:S(2)}) %collective-permute-start.12) | collective-permute-done | bytes 36896 | tf_op jit(solution)/shard_map/ppermute | solution.py:342
  54.6 0.7 %shard_map.54 = bf16[9,2048]{1,0:T(8,128)(2,1)} custom-call(f32[8,2304]{1,0:T(8,128)S(1)} %get-tuple-element.13.refs_0_, bf16[8,2304]{1,0:T(8,128)(2,1)S(1)} %collective-permute-done.10.refs_1_, bf16[8,2304]{1,0:T(8,128)(2,1)S(1)} %collective-permute-done.11.refs_2_, bf16[8,2304]{1,0:T(8,128)(2,1)S(1)} %collective-permute-done.12.refs_3_), custom_call_target="tpu_custom_call" | custom-call | bytes 1048576 | tf_op jit(solution)/shard_map/pallas_call | solution.py:330
  (1 shorter events, 0.0 us)
Async XLA Ops:
  0.0 8.3 %copy-start = (bf16[9,2048]{1,0:T(8,128)(2,1)S(1)}, bf16[9,2048]{1,0:T(8,128)(2,1)}, u32[]{:S(2)}) copy-start(bf16[9,2048]{1,0:T(8,128)(2,1)} %param.4) | copy-start | bytes 110596
  0.0 8.3 %collective-permute-start.1 = (bf16[9,2048]{1,0:T(8,128)(2,1)}, bf16[9,2048]{1,0:T(8,128)(2,1)S(1)}, u32[]{:S(2)}, u32[]{:S(2)}) collective-permute-start(bf16[9,2048]{1,0:T(8,128)(2,1)} %param.4), channel_id=1, source_target_pairs={{0,2},{1,3},{2,0},{3,1},{4,6},{5,7},{6,4},{7,5},{8,10},{9,11},{10,... | collective-permute-start | bytes 110600 | tf_op jit(solution)/shard_map/ppermute | solution.py:342
  2.9 5.4 %collective-permute-start = (bf16[9,2048]{1,0:T(8,128)(2,1)}, bf16[9,2048]{1,0:T(8,128)(2,1)S(1)}, u32[]{:S(2)}, u32[]{:S(2)}) collective-permute-start(bf16[9,2048]{1,0:T(8,128)(2,1)} %param.4), channel_id=1, source_target_pairs={{0,1},{1,0},{2,3},{3,2},{4,5},{5,4},{6,7},{7,6},{8,9},{9,8},{10,11... | collective-permute-start | bytes 110600 | tf_op jit(solution)/shard_map/ppermute | solution.py:342
  2.9 5.4 %collective-permute-start.2 = (bf16[9,2048]{1,0:T(8,128)(2,1)}, bf16[9,2048]{1,0:T(8,128)(2,1)S(1)}, u32[]{:S(2)}, u32[]{:S(2)}) collective-permute-start(bf16[9,2048]{1,0:T(8,128)(2,1)} %param.4), channel_id=1, source_target_pairs={{0,3},{1,2},{2,1},{3,0},{4,7},{5,6},{6,5},{7,4},{8,11},{9,10},{10,... | collective-permute-start | bytes 110600 | tf_op jit(solution)/shard_map/ppermute | solution.py:342
  10.6 9.8 %collective-permute-start.3 = (bf16[8,14976]{1,0:T(8,128)(2,1)S(1)}, bf16[8,14976]{1,0:T(8,128)(2,1)S(1)}, u32[]{:S(2)}, u32[]{:S(2)}) collective-permute-start(bf16[8,14976]{1,0:T(8,128)(2,1)S(1)} %shard_map.47._), channel_id=1, source_target_pairs={{0,4},{4,0},{8,12},{12,8},{1,5},{5,1},{9,13},{13,9},{2,6},{6,2},{1... | collective-permute-start | bytes 718856 | tf_op jit(solution)/shard_map/ppermute | solution.py:342
  20.5 15.7 %collective-permute-start.4 = (bf16[8,14976]{1,0:T(8,128)(2,1)S(1)}, bf16[8,14976]{1,0:T(8,128)(2,1)S(1)}, u32[]{:S(2)}, u32[]{:S(2)}) collective-permute-start(bf16[8,14976]{1,0:T(8,128)(2,1)S(1)} %add_convert_fusion._), channel_id=1, source_target_pairs={{0,8},{4,12},{8,0},{12,4},{1,9},{5,13},{9,1},{13,5},{2,10},{6,14},... | collective-permute-start | bytes 718856 | tf_op jit(solution)/shard_map/ppermute | solution.py:342
  23.2 12.0 %collective-permute-start.5 = (bf16[8,7552]{1,0:T(8,128)(2,1)S(1)}, bf16[8,7552]{1,0:T(8,128)(2,1)S(1)}, u32[]{:S(2)}, u32[]{:S(2)}) collective-permute-start(bf16[8,7552]{1,0:T(8,128)(2,1)S(1)} %get-tuple-element.12), channel_id=1, source_target_pairs={{0,4},{4,0},{8,12},{12,8},{1,5},{5,1},{9,13},{13,9},{2,6},{6,2},{1... | collective-permute-start | bytes 362504 | tf_op jit(solution)/shard_map/ppermute | solution.py:342
  23.6 20.2 %slice-start = ((s8[27262976]{0:T(1024)(128)(4,1)}), s8[4194304]{0:T(1024)(128)(4,1)S(1)}, s32[]{:S(2)}) async-start(s8[27262976]{0:T(1024)(128)(4,1)} %bitcast), calls=%async_computation | async-start | bytes 8388608
  23.6 20.2 %slice-start.1 = ((s8[27262976]{0:T(1024)(128)(4,1)}), s8[4194304]{0:T(1024)(128)(4,1)S(1)}, s32[]{:S(2)}) async-start(s8[27262976]{0:T(1024)(128)(4,1)} %bitcast), calls=%async_computation.1 | async-start | bytes 8388608
  23.6 20.2 %slice-start.2 = ((s8[27262976]{0:T(1024)(128)(4,1)}), s8[4194304]{0:T(1024)(128)(4,1)S(1)}, s32[]{:S(2)}) async-start(s8[27262976]{0:T(1024)(128)(4,1)} %bitcast), calls=%async_computation.2 | async-start | bytes 8388608
  23.6 20.2 %slice-start.3 = ((s8[27262976]{0:T(1024)(128)(4,1)}), s8[4194304]{0:T(1024)(128)(4,1)S(1)}, s32[]{:S(2)}) async-start(s8[27262976]{0:T(1024)(128)(4,1)} %bitcast), calls=%async_computation.3 | async-start | bytes 8388608
  27.2 16.6 %slice-start.4 = ((s8[27262976]{0:T(1024)(128)(4,1)}), s8[4194304]{0:T(1024)(128)(4,1)S(1)}, s32[]{:S(2)}) async-start(s8[27262976]{0:T(1024)(128)(4,1)} %bitcast), calls=%async_computation.4 | async-start | bytes 8388608
  27.2 16.6 %slice-start.5 = ((s8[27262976]{0:T(1024)(128)(4,1)}), s8[4194304]{0:T(1024)(128)(4,1)S(1)}, s32[]{:S(2)}) async-start(s8[27262976]{0:T(1024)(128)(4,1)} %bitcast), calls=%async_computation.5 | async-start | bytes 8388608
  27.2 16.6 %slice-start.6 = ((s8[27262976]{0:T(1024)(128)(4,1)}), s8[2097152]{0:T(1024)(128)(4,1)S(1)}, s32[]{:S(2)}) async-start(s8[27262976]{0:T(1024)(128)(4,1)} %bitcast), calls=%async_computation.6 | async-start | bytes 4194304
  27.2 8.9 %collective-permute-start.6 = (bf16[8,7552]{1,0:T(8,128)(2,1)S(1)}, bf16[8,7552]{1,0:T(8,128)(2,1)S(1)}, u32[]{:S(2)}, u32[]{:S(2)}) collective-permute-start(bf16[8,7552]{1,0:T(8,128)(2,1)S(1)} %shard_map.49._), channel_id=1, source_target_pairs={{0,4},{4,0},{8,12},{12,8},{1,5},{5,1},{9,13},{13,9},{2,6},{6,2},{1... | collective-permute-start | bytes 362504 | tf_op jit(solution)/shard_map/ppermute | solution.py:342
  36.3 7.4 %collective-permute-start.7 = (bf16[8,7552]{1,0:T(8,128)(2,1)S(1)}, bf16[8,7552]{1,0:T(8,128)(2,1)S(1)}, u32[]{:S(2)}, u32[]{:S(2)}) collective-permute-start(bf16[8,7552]{1,0:T(8,128)(2,1)S(1)} %shard_map.51.refs_0_), channel_id=1, source_target_pairs={{0,8},{4,12},{8,0},{12,4},{1,9},{5,13},{9,1},{13,5},{2,10},{6,14},... | collective-permute-start | bytes 362504 | tf_op jit(solution)/shard_map/ppermute | solution.py:342
  36.4 7.4 %collective-permute-start.9 = (bf16[8,7552]{1,0:T(8,128)(2,1)S(1)}, bf16[8,7552]{1,0:T(8,128)(2,1)S(1)}, u32[]{:S(2)}, u32[]{:S(2)}) collective-permute-start(bf16[8,7552]{1,0:T(8,128)(2,1)S(1)} %shard_map.51.refs_0_), channel_id=1, source_target_pairs={{0,4},{4,0},{8,12},{12,8},{1,5},{5,1},{9,13},{13,9},{2,6},{6,2},{1... | collective-permute-start | bytes 362504 | tf_op jit(solution)/shard_map/ppermute | solution.py:342
  43.7 4.9 %collective-permute-start.8 = (bf16[8,7552]{1,0:T(8,128)(2,1)S(1)}, bf16[8,7552]{1,0:T(8,128)(2,1)S(1)}, u32[]{:S(2)}, u32[]{:S(2)}) collective-permute-start(bf16[8,7552]{1,0:T(8,128)(2,1)S(1)} %collective-permute-done.7.refs_2_), channel_id=1, source_target_pairs={{0,4},{4,0},{8,12},{12,8},{1,5},{5,1},{9,13},{13,9},{2,6},{6,2},{1... | collective-permute-start | bytes 362504 | tf_op jit(solution)/shard_map/ppermute | solution.py:342
  49.9 1.9 %collective-permute-start.10 = (bf16[8,2304]{1,0:T(8,128)(2,1)S(1)}, bf16[8,2304]{1,0:T(8,128)(2,1)S(1)}, u32[]{:S(2)}, u32[]{:S(2)}) collective-permute-start(bf16[8,2304]{1,0:T(8,128)(2,1)S(1)} %get-tuple-element.14), channel_id=1, source_target_pairs={{0,1},{1,0},{2,3},{3,2},{4,5},{5,4},{6,7},{7,6},{8,9},{9,8},{10,11... | collective-permute-start | bytes 110600 | tf_op jit(solution)/shard_map/ppermute | solution.py:342
  49.9 4.0 %collective-permute-start.11 = (bf16[8,2304]{1,0:T(8,128)(2,1)S(1)}, bf16[8,2304]{1,0:T(8,128)(2,1)S(1)}, u32[]{:S(2)}, u32[]{:S(2)}) collective-permute-start(bf16[8,2304]{1,0:T(8,128)(2,1)S(1)} %get-tuple-element.15), channel_id=1, source_target_pairs={{0,2},{1,3},{2,0},{3,1},{4,6},{5,7},{6,4},{7,5},{8,10},{9,11},{10,... | collective-permute-start | bytes 110600 | tf_op jit(solution)/shard_map/ppermute | solution.py:342
  51.2 3.4 %collective-permute-start.12 = (bf16[8,2304]{1,0:T(8,128)(2,1)S(1)}, bf16[8,2304]{1,0:T(8,128)(2,1)S(1)}, u32[]{:S(2)}, u32[]{:S(2)}) collective-permute-start(bf16[8,2304]{1,0:T(8,128)(2,1)S(1)} %get-tuple-element.16), channel_id=1, source_target_pairs={{0,3},{1,2},{2,1},{3,0},{4,7},{5,6},{6,5},{7,4},{8,11},{9,10},{10,... | collective-permute-start | bytes 110600 | tf_op jit(solution)/shard_map/ppermute | solution.py:342

commit v18 on v14

--- a/solution.py
+++ b/solution.py
@@ -11,6 +11,7 @@
 STEP = 256
 COPY_STEP = 512
 IN_FLIGHT = 6
+DOWN_STEP = 512
 TOKEN_AXES = ("gy", "gz")
 IN_HBM = pl.BlockSpec(memory_space=pltpu.HBM)
 ANY = pl.BlockSpec(memory_space=pl.ANY)
@@ -256,23 +257,20 @@
             out[r : r + 1, i * piece : (i + 1) * piece] = packed[i : i + 1, at : at + piece]
 
 
-def down_kernel(first, rows, width, distances, *refs):
+def down_kernel(first, last, rows, width, distances, *refs):
     blocks = len(distances)
     hidden, refs = refs[:blocks], refs[blocks:]
     if not first:
         before, refs = refs[0], refs[1:]
     held, outs, (plain, total) = refs[0], refs[1:-2], refs[-2:]
-    if first:
+    if not last:
         total = outs[0]
     for b in range(blocks):
         for g in range(rows // 8):
             plain[8 * g : 8 * g + 8, :] = hidden[b][:, g * width : (g + 1) * width].astype(jnp.float32)
         if rows % 8:
-            at, half = (rows // 8) * width, hidden_tail(rows, width)
-            tail = hidden[b][:, at : at + half].astype(jnp.float32)
-            plain[rows - 4 :, :half] = tail[:4]
-            plain[rows - 4 :, half:] = tail[4:, : width - half]
-        for row, tall in pieces_of(width, STEP):
+            plain[rows - 4 :, :] = last_rows(hidden[b], rows, width)
+        for row, tall in pieces_of(width, DOWN_STEP):
             term = jnp.dot(
                 plain[:, row : row + tall].astype(jnp.bfloat16),
                 held[pl.ds(pl.multiple_of(block_start(distances[b], width) + row, 128), tall), :],
@@ -282,7 +280,7 @@
                 total[...] = term if first else before[...] + term
             else:
                 total[...] += term
-    if not first:
+    if last:
         tall = rows // len(outs)
         for r, out in enumerate(outs):
             pack_rows(out, total[r * tall : (r + 1) * tall, :])
@@ -290,14 +288,14 @@
 
 def down(hidden, distances, before, weight, rows, width, outs):
     columns = weight.shape[1]
-    if before is None:
+    if outs == 1:
         shapes = [jax.ShapeDtypeStruct((rows, columns), jnp.float32)]
     else:
         packed = (8, rows // outs * columns // 8)
         shapes = [jax.ShapeDtypeStruct(packed, jnp.bfloat16 if r else jnp.float32) for r in range(outs)]
     carried = [] if before is None else [before]
     return pl.pallas_call(
-        functools.partial(down_kernel, before is None, rows, width, distances),
+        functools.partial(down_kernel, before is None, outs > 1, rows, width, distances),
         out_shape=shapes,
         in_specs=[WHOLE] * (len(hidden) + len(carried) + 1),
         out_specs=[WHOLE] * len(shapes),
@@ -364,11 +362,13 @@
     (own,) = blocks_for((0,), ((0, 1),), beside)
     hidden = activate_packed(own, far, near, rows, width)
 
+    neighbour = swap(hidden, "gx", n_gx, 1)
     opposite = swap(hidden, "gx", n_gx, 2)
-    first = [hidden, swap(hidden, "gx", n_gx, 1), opposite]
-    second = [swap(opposite, "gx", n_gx, 1)]
-    (partial_sum,) = down(first, (0, 1, 2), None, down_weight, rows, width, 1)
-    outs = down(second, (3,), partial_sum, down_weight, rows, width, n_token)
+    (total,) = down([hidden, neighbour], (0, 1), None, down_weight, rows, width, 1)
+    opposite, total = lax.optimization_barrier((opposite, total))
+    diagonal = swap(opposite, "gx", n_gx, 1)
+    (total,) = down([opposite], (2,), total, down_weight, rows, width, 1)
+    outs = down([diagonal], (3,), total, down_weight, rows, width, n_token)
     terms = [outs[0]] + [swap(outs[r], TOKEN_AXES, n_token, r) for r in range(1, n_token)]
     return finish(terms, tokens.shape)
 

time: 55.1 us -> 56.9 us (1.033)
  waiting for transfers between devices: 10.7 us -> 12.4 us
    ppermute x13, waiting for transfers between devices: 10.7 us -> 12.4 us  [swap(): return lax.ppermute(value, axes, [(i, i ^ distance) for i in range(size)])]
    pallas_call x2 -> x3, Pallas kernels: 4.94 us -> 5.05 us  [down(): pl.pallas_call(functools.partial(down_kernel, before is None, outs > 1, r...]
  transfers between devices with their start and end apart: 13 -> 13, of which waited for: 6 -> 5; matrix products, arithmetic and copies ran while one was open for 0% -> 0% of each run, Pallas kernels for 48% -> 46%
where the time goes in v18:
time: 56.9 us; the launch traced here: 56.8 us
  Pallas kernels  30.6 us (54%)
  starting transfers between devices  13.4 us (24%)
  waiting for transfers between devices  12.4 us (22%)
    pallas_call x3, Pallas kernels, gate_up_stream(): pl.pallas_call(functools.partial(stream_kernel, width, blocks, distances)...  17.4 us
    ppermute x13, starting transfers between devices, swap(): return lax.ppermute(value, axes, [(i, i ^ distance) for i in range(size)])  13.4 us
    ppermute x13, waiting for transfers between devices, swap(): return lax.ppermute(value, axes, [(i, i ^ distance) for i in range(size)])  12.4 us
    pallas_call x1, Pallas kernels, fetch(): pl.pallas_call(functools.partial(fetch_kernel, width, distance), out_shap...  5.16 us
    pallas_call x3, Pallas kernels, down(): pl.pallas_call(functools.partial(down_kernel, before is None, outs > 1, r...  5.05 us
    pallas_call x1, Pallas kernels, gate_up_held(): pl.pallas_call(held_kernel, out_shape=jax.ShapeDtypeStruct((8, packed_pai...  2.15 us
  transfers between devices with their start and end apart: 13, of which 5 were waited for; matrix products, arithmetic and copies ran while one was open for 0% of the time, Pallas kernels for 46%

profile of v18, /device:TPU:0, one launch (start us, length us, event | category | flops | bytes accessed | tf_op | source)
XLA Modules:
  0.0 56.8 jit_solution(9363458397320343768)
XLA Ops:
  0.0 0.0 copy-start
  0.0 2.9 %collective-permute-start.1 = (bf16[9,2048]{1,0:T(8,128)(2,1)}, bf16[9,2048]{1,0:T(8,128)(2,1)S(1)}, u32[]{:S(2)}, u32[]{:S(2)}) collective-permute-start(bf16[9,2048]{1,0:T(8,128)(2,1)} %param.4), channel_id=1, source_target_pairs={{0,2},{1,3},{2,0},{3,1},{4,6},{5,7},{6,4},{7,5},{8,10},{9,11},{10,... | collective-permute-start | bytes 110600 | tf_op jit(solution)/shard_map/ppermute | solution.py:333
  2.9 0.0 collective-permute-start
  2.9 0.2 collective-permute-start.2
  3.1 5.2 %shard_map.46.held = bf16[2,2048,1664]{2,1,0:T(8,128)(2,1)S(1)} custom-call(bf16[2048,6656]{1,0:T(8,128)(2,1)} %gate_ref.7, bf16[2048,6656]{1,0:T(8,128)(2,1)} %up_ref.7), custom_call_target="tpu_custom_call" | custom-call | bytes 1048576 | tf_op jit(solution)/shard_map/pallas_call | solution.py:86
  8.3 0.0 collective-permute-done.1
  8.3 0.0 collective-permute-done
  8.3 0.0 collective-permute-done.2
  8.3 0.0 copy-done
  8.3 0.1 pad_maximum_fusion.x_ref
  8.4 2.2 %shard_map.47._ = bf16[8,14976]{1,0:T(8,128)(2,1)S(1)} custom-call(bf16[36,2048]{1,0:T(8,128)(2,1)S(1)} %pad_maximum_fusion.x_ref, bf16[2,2048,1664]{2,1,0:T(8,128)(2,1)S(1)} %shard_map.46.held), custom_call_target="tpu_custom_call" | custom-call | bytes 1048576 | tf_op jit(solution)/shard_map/pallas_call | solution.py:120
  10.6 2.0 %collective-permute-start.3 = (bf16[8,14976]{1,0:T(8,128)(2,1)S(1)}, bf16[8,14976]{1,0:T(8,128)(2,1)S(1)}, u32[]{:S(2)}, u32[]{:S(2)}) collective-permute-start(bf16[8,14976]{1,0:T(8,128)(2,1)S(1)} %shard_map.47._), channel_id=1, source_target_pairs={{0,4},{4,0},{8,12},{12,8},{1,5},{5,1},{9,13},{13,9},{2,6},{6,2},{1... | collective-permute-start | bytes 718856 | tf_op jit(solution)/shard_map/ppermute | solution.py:333
  12.6 7.6 %shard_map.48 = (bf16[8,14976]{1,0:T(8,128)(2,1)S(1)}, bf16[8,7552]{1,0:T(8,128)(2,1)S(1)}) custom-call(bf16[36,2048]{1,0:T(8,128)(2,1)S(1)} %pad_maximum_fusion.x_ref, bf16[2048,6656]{1,0:T(8,128)(2,1)} %gate_ref.7, bf16[2048,6656]{1,0:T(8,128)(2,1)} %up_ref.7, bf16[8,14976]{1,0:T(8,128)(2,1)S(1)} %shard_map.47._), custom_call_target="tpu_custom_call" | custom-call | bytes 1048576 | tf_op jit(solution)/shard_map/pallas_call | solution.py:164
  20.2 0.0 collective-permute-done.3
  20.2 0.1 add_convert_fusion._
  20.2 2.7 %collective-permute-start.4 = (bf16[8,14976]{1,0:T(8,128)(2,1)S(1)}, bf16[8,14976]{1,0:T(8,128)(2,1)S(1)}, u32[]{:S(2)}, u32[]{:S(2)}) collective-permute-start(bf16[8,14976]{1,0:T(8,128)(2,1)S(1)} %add_convert_fusion._), channel_id=1, source_target_pairs={{0,8},{4,12},{8,0},{12,4},{1,9},{5,13},{9,1},{13,5},{2,10},{6,14},... | collective-permute-start | bytes 718856 | tf_op jit(solution)/shard_map/ppermute | solution.py:333
  22.9 0.4 collective-permute-start.5
  23.3 0.0 slice-start
  23.3 0.0 slice-start.1
  23.3 0.0 slice-start.2
  23.3 0.0 slice-start.3
  23.4 3.6 %shard_map.49._ = bf16[8,7552]{1,0:T(8,128)(2,1)S(1)} custom-call(bf16[36,2048]{1,0:T(8,128)(2,1)S(1)} %pad_maximum_fusion.x_ref, bf16[2048,6656]{1,0:T(8,128)(2,1)} %gate_ref.7, bf16[2048,6656]{1,0:T(8,128)(2,1)} %up_ref.7, bf16[8,14976]{1,0:T(8,128)(2,1)S(1)} %add_convert_fusion._), custom_call_target="tpu_custom_call" | custom-call | bytes 1048576 | tf_op jit(solution)/shard_map/pallas_call | solution.py:164
  26.9 0.0 slice-start.4
  27.0 0.0 slice-start.5
  27.0 0.0 slice-start.6
  27.0 1.7 %collective-permute-start.6 = (bf16[8,7552]{1,0:T(8,128)(2,1)S(1)}, bf16[8,7552]{1,0:T(8,128)(2,1)S(1)}, u32[]{:S(2)}, u32[]{:S(2)}) collective-permute-start(bf16[8,7552]{1,0:T(8,128)(2,1)S(1)} %shard_map.49._), channel_id=1, source_target_pairs={{0,4},{4,0},{8,12},{12,8},{1,5},{5,1},{9,13},{13,9},{2,6},{6,2},{1... | collective-permute-start | bytes 362504 | tf_op jit(solution)/shard_map/ppermute | solution.py:333
  28.7 6.2 %shard_map.50.own = bf16[8,14976]{1,0:T(8,128)(2,1)S(1)} custom-call(bf16[36,2048]{1,0:T(8,128)(2,1)S(1)} %pad_maximum_fusion.x_ref, bf16[2048,6656]{1,0:T(8,128)(2,1)} %gate_ref.7, bf16[2048,6656]{1,0:T(8,128)(2,1)} %up_ref.7, bf16[8,7552]{1,0:T(8,128)(2,1)S(1)} %shard_map.49._), custom_call_target="tpu_custom_call" | custom-call | bytes 1048576 | tf_op jit(solution)/shard_map/pallas_call | solution.py:164
  34.9 0.0 collective-permute-done.5.gate_near
  34.9 1.0 %collective-permute-done.6.up_near = bf16[8,7552]{1,0:T(8,128)(2,1)S(1)} collective-permute-done((bf16[8,7552]{1,0:T(8,128)(2,1)S(1)}, bf16[8,7552]{1,0:T(8,128)(2,1)S(1)}, u32[]{:S(2)}, u32[]{:S(2)}) %collective-permute-start.6) | collective-permute-done | bytes 120864 | tf_op jit(solution)/shard_map/ppermute | solution.py:333
  35.9 0.0 collective-permute-done.4.far
  35.9 0.1 shard_map.51.refs_0_
  36.1 0.1 collective-permute-start.8
  36.1 1.5 %collective-permute-start.7 = (bf16[8,7552]{1,0:T(8,128)(2,1)S(1)}, bf16[8,7552]{1,0:T(8,128)(2,1)S(1)}, u32[]{:S(2)}, u32[]{:S(2)}) collective-permute-start(bf16[8,7552]{1,0:T(8,128)(2,1)S(1)} %shard_map.51.refs_0_), channel_id=1, source_target_pairs={{0,8},{4,12},{8,0},{12,4},{1,9},{5,13},{9,1},{13,5},{2,10},{6,14},... | collective-permute-start | bytes 362504 | tf_op jit(solution)/shard_map/ppermute | solution.py:333
  37.6 4.7 %collective-permute-done.8.refs_1_ = bf16[8,7552]{1,0:T(8,128)(2,1)S(1)} collective-permute-done((bf16[8,7552]{1,0:T(8,128)(2,1)S(1)}, bf16[8,7552]{1,0:T(8,128)(2,1)S(1)}, u32[]{:S(2)}, u32[]{:S(2)}) %collective-permute-start.8) | collective-permute-done | bytes 120864 | tf_op jit(solution)/shard_map/ppermute | solution.py:333
  42.3 0.0 slice-done
  42.3 0.0 slice-done.1
  42.3 0.0 slice-done.2
  42.3 0.0 slice-done.3
  42.4 0.0 slice-done.4
  42.4 0.0 slice-done.5
  42.4 0.0 slice-done.6
  42.4 2.5 %shard_map.52.refs_1_ = f32[36,2048]{1,0:T(8,128)S(1)} custom-call(bf16[8,7552]{1,0:T(8,128)(2,1)S(1)} %shard_map.51.refs_0_, bf16[8,7552]{1,0:T(8,128)(2,1)S(1)} %collective-permute-done.8.refs_1_, bf16[6656,2048]{1,0:T(8,128)(2,1)S(1)} %bitcast.1), custom_call_target="tpu_custom_call" | custom-call | bytes 1048576 | tf_op jit(solution)/shard_map/pallas_call | solution.py:297
  44.9 0.0 collective-permute-done.7.refs_0_
  44.9 0.1 collective-permute-start.9
  44.9 1.3 %shard_map.53.refs_1_ = f32[36,2048]{1,0:T(8,128)S(1)} custom-call(bf16[8,7552]{1,0:T(8,128)(2,1)S(1)} %collective-permute-done.7.refs_0_, f32[36,2048]{1,0:T(8,128)S(1)} %shard_map.52.refs_1_, bf16[6656,2048]{1,0:T(8,128)(2,1)S(1)} %bitcast.1), custom_call_target="tpu_custom_call" | custom-call | bytes 1048576 | tf_op jit(solution)/shard_map/pallas_call | solution.py:297
  46.2 3.5 %collective-permute-done.9.refs_0_ = bf16[8,7552]{1,0:T(8,128)(2,1)S(1)} collective-permute-done((bf16[8,7552]{1,0:T(8,128)(2,1)S(1)}, bf16[8,7552]{1,0:T(8,128)(2,1)S(1)}, u32[]{:S(2)}, u32[]{:S(2)}) %collective-permute-start.9) | collective-permute-done | bytes 120864 | tf_op jit(solution)/shard_map/ppermute | solution.py:333
  49.8 1.3 %shard_map.54 = (f32[8,2304]{1,0:T(8,128)S(1)}, bf16[8,2304]{1,0:T(8,128)(2,1)S(1)}, bf16[8,2304]{1,0:T(8,128)(2,1)S(1)}, bf16[8,2304]{1,0:T(8,128)(2,1)S(1)}) custom-call(bf16[8,7552]{1,0:T(8,128)(2,1)S(1)} %collective-permute-done.9.refs_0_, f32[36,2048]{1,0:T(8,128)S(1)} %shard_map.53.refs_1_, bf16[6656,2048]{1,0:T(8,128)(2,1)S(1)} %bitcast.1), custom_call_target="tpu_custom_call" | custom-call | bytes 1048576 | tf_op jit(solution)/shard_map/pallas_call | solution.py:297
  51.1 0.1 collective-permute-start.10
  51.2 1.5 %collective-permute-start.11 = (bf16[8,2304]{1,0:T(8,128)(2,1)S(1)}, bf16[8,2304]{1,0:T(8,128)(2,1)S(1)}, u32[]{:S(2)}, u32[]{:S(2)}) collective-permute-start(bf16[8,2304]{1,0:T(8,128)(2,1)S(1)} %get-tuple-element.19), channel_id=1, source_target_pairs={{0,2},{1,3},{2,0},{3,1},{4,6},{5,7},{6,4},{7,5},{8,10},{9,11},{10,... | collective-permute-start | bytes 110600 | tf_op jit(solution)/shard_map/ppermute | solution.py:333
  52.7 0.3 collective-permute-start.12
  53.0 0.0 collective-permute-done.10.refs_1_
  53.0 2.2 %collective-permute-done.11.refs_2_ = bf16[8,2304]{1,0:T(8,128)(2,1)S(1)} collective-permute-done((bf16[8,2304]{1,0:T(8,128)(2,1)S(1)}, bf16[8,2304]{1,0:T(8,128)(2,1)S(1)}, u32[]{:S(2)}, u32[]{:S(2)}) %collective-permute-start.11) | collective-permute-done | bytes 36896 | tf_op jit(solution)/shard_map/ppermute | solution.py:333
  55.2 0.9 %collective-permute-done.12.refs_3_ = bf16[8,2304]{1,0:T(8,128)(2,1)S(1)} collective-permute-done((bf16[8,2304]{1,0:T(8,128)(2,1)S(1)}, bf16[8,2304]{1,0:T(8,128)(2,1)S(1)}, u32[]{:S(2)}, u32[]{:S(2)}) %collective-permute-start.12) | collective-permute-done | bytes 36896 | tf_op jit(solution)/shard_map/ppermute | solution.py:333
  56.1 0.7 %shard_map.55 = bf16[9,2048]{1,0:T(8,128)(2,1)} custom-call(f32[8,2304]{1,0:T(8,128)S(1)} %get-tuple-element.17.refs_0_, bf16[8,2304]{1,0:T(8,128)(2,1)S(1)} %collective-permute-done.10.refs_1_, bf16[8,2304]{1,0:T(8,128)(2,1)S(1)} %collective-permute-done.11.refs_2_, bf16[8,2304]{1,0:T(8,128)(2,1)S(1)} %collective-permute-done.12.refs_3_), custom_call_target="tpu_custom_call" | custom-call | bytes 1048576 | tf_op jit(solution)/shard_map/pallas_call | solution.py:321
  (1 shorter events, 0.0 us)
Async XLA Ops:
  0.0 8.3 %copy-start = (bf16[9,2048]{1,0:T(8,128)(2,1)S(1)}, bf16[9,2048]{1,0:T(8,128)(2,1)}, u32[]{:S(2)}) copy-start(bf16[9,2048]{1,0:T(8,128)(2,1)} %param.4) | copy-start | bytes 110596
  0.0 8.3 %collective-permute-start.1 = (bf16[9,2048]{1,0:T(8,128)(2,1)}, bf16[9,2048]{1,0:T(8,128)(2,1)S(1)}, u32[]{:S(2)}, u32[]{:S(2)}) collective-permute-start(bf16[9,2048]{1,0:T(8,128)(2,1)} %param.4), channel_id=1, source_target_pairs={{0,2},{1,3},{2,0},{3,1},{4,6},{5,7},{6,4},{7,5},{8,10},{9,11},{10,... | collective-permute-start | bytes 110600 | tf_op jit(solution)/shard_map/ppermute | solution.py:333
  2.9 5.4 %collective-permute-start = (bf16[9,2048]{1,0:T(8,128)(2,1)}, bf16[9,2048]{1,0:T(8,128)(2,1)S(1)}, u32[]{:S(2)}, u32[]{:S(2)}) collective-permute-start(bf16[9,2048]{1,0:T(8,128)(2,1)} %param.4), channel_id=1, source_target_pairs={{0,1},{1,0},{2,3},{3,2},{4,5},{5,4},{6,7},{7,6},{8,9},{9,8},{10,11... | collective-permute-start | bytes 110600 | tf_op jit(solution)/shard_map/ppermute | solution.py:333
  2.9 5.4 %collective-permute-start.2 = (bf16[9,2048]{1,0:T(8,128)(2,1)}, bf16[9,2048]{1,0:T(8,128)(2,1)S(1)}, u32[]{:S(2)}, u32[]{:S(2)}) collective-permute-start(bf16[9,2048]{1,0:T(8,128)(2,1)} %param.4), channel_id=1, source_target_pairs={{0,3},{1,2},{2,1},{3,0},{4,7},{5,6},{6,5},{7,4},{8,11},{9,10},{10,... | collective-permute-start | bytes 110600 | tf_op jit(solution)/shard_map/ppermute | solution.py:333
  10.6 9.6 %collective-permute-start.3 = (bf16[8,14976]{1,0:T(8,128)(2,1)S(1)}, bf16[8,14976]{1,0:T(8,128)(2,1)S(1)}, u32[]{:S(2)}, u32[]{:S(2)}) collective-permute-start(bf16[8,14976]{1,0:T(8,128)(2,1)S(1)} %shard_map.47._), channel_id=1, source_target_pairs={{0,4},{4,0},{8,12},{12,8},{1,5},{5,1},{9,13},{13,9},{2,6},{6,2},{1... | collective-permute-start | bytes 718856 | tf_op jit(solution)/shard_map/ppermute | solution.py:333
  20.2 15.7 %collective-permute-start.4 = (bf16[8,14976]{1,0:T(8,128)(2,1)S(1)}, bf16[8,14976]{1,0:T(8,128)(2,1)S(1)}, u32[]{:S(2)}, u32[]{:S(2)}) collective-permute-start(bf16[8,14976]{1,0:T(8,128)(2,1)S(1)} %add_convert_fusion._), channel_id=1, source_target_pairs={{0,8},{4,12},{8,0},{12,4},{1,9},{5,13},{9,1},{13,5},{2,10},{6,14},... | collective-permute-start | bytes 718856 | tf_op jit(solution)/shard_map/ppermute | solution.py:333
  22.9 12.0 %collective-permute-start.5 = (bf16[8,7552]{1,0:T(8,128)(2,1)S(1)}, bf16[8,7552]{1,0:T(8,128)(2,1)S(1)}, u32[]{:S(2)}, u32[]{:S(2)}) collective-permute-start(bf16[8,7552]{1,0:T(8,128)(2,1)S(1)} %get-tuple-element.14), channel_id=1, source_target_pairs={{0,4},{4,0},{8,12},{12,8},{1,5},{5,1},{9,13},{13,9},{2,6},{6,2},{1... | collective-permute-start | bytes 362504 | tf_op jit(solution)/shard_map/ppermute | solution.py:333
  23.3 19.0 %slice-start = ((s8[27262976]{0:T(1024)(128)(4,1)}), s8[4194304]{0:T(1024)(128)(4,1)S(1)}, s32[]{:S(2)}) async-start(s8[27262976]{0:T(1024)(128)(4,1)} %bitcast), calls=%async_computation | async-start | bytes 8388608
  23.3 19.0 %slice-start.1 = ((s8[27262976]{0:T(1024)(128)(4,1)}), s8[4194304]{0:T(1024)(128)(4,1)S(1)}, s32[]{:S(2)}) async-start(s8[27262976]{0:T(1024)(128)(4,1)} %bitcast), calls=%async_computation.1 | async-start | bytes 8388608
  23.3 19.0 %slice-start.2 = ((s8[27262976]{0:T(1024)(128)(4,1)}), s8[4194304]{0:T(1024)(128)(4,1)S(1)}, s32[]{:S(2)}) async-start(s8[27262976]{0:T(1024)(128)(4,1)} %bitcast), calls=%async_computation.2 | async-start | bytes 8388608
  23.3 19.0 %slice-start.3 = ((s8[27262976]{0:T(1024)(128)(4,1)}), s8[4194304]{0:T(1024)(128)(4,1)S(1)}, s32[]{:S(2)}) async-start(s8[27262976]{0:T(1024)(128)(4,1)} %bitcast), calls=%async_computation.3 | async-start | bytes 8388608
  26.9 15.4 %slice-start.4 = ((s8[27262976]{0:T(1024)(128)(4,1)}), s8[4194304]{0:T(1024)(128)(4,1)S(1)}, s32[]{:S(2)}) async-start(s8[27262976]{0:T(1024)(128)(4,1)} %bitcast), calls=%async_computation.4 | async-start | bytes 8388608
  27.0 15.4 %slice-start.5 = ((s8[27262976]{0:T(1024)(128)(4,1)}), s8[4194304]{0:T(1024)(128)(4,1)S(1)}, s32[]{:S(2)}) async-start(s8[27262976]{0:T(1024)(128)(4,1)} %bitcast), calls=%async_computation.5 | async-start | bytes 8388608
  27.0 15.4 %slice-start.6 = ((s8[27262976]{0:T(1024)(128)(4,1)}), s8[2097152]{0:T(1024)(128)(4,1)S(1)}, s32[]{:S(2)}) async-start(s8[27262976]{0:T(1024)(128)(4,1)} %bitcast), calls=%async_computation.6 | async-start | bytes 4194304
  27.0 9.0 %collective-permute-start.6 = (bf16[8,7552]{1,0:T(8,128)(2,1)S(1)}, bf16[8,7552]{1,0:T(8,128)(2,1)S(1)}, u32[]{:S(2)}, u32[]{:S(2)}) collective-permute-start(bf16[8,7552]{1,0:T(8,128)(2,1)S(1)} %shard_map.49._), channel_id=1, source_target_pairs={{0,4},{4,0},{8,12},{12,8},{1,5},{5,1},{9,13},{13,9},{2,6},{6,2},{1... | collective-permute-start | bytes 362504 | tf_op jit(solution)/shard_map/ppermute | solution.py:333
  36.1 6.3 %collective-permute-start.8 = (bf16[8,7552]{1,0:T(8,128)(2,1)S(1)}, bf16[8,7552]{1,0:T(8,128)(2,1)S(1)}, u32[]{:S(2)}, u32[]{:S(2)}) collective-permute-start(bf16[8,7552]{1,0:T(8,128)(2,1)S(1)} %shard_map.51.refs_0_), channel_id=1, source_target_pairs={{0,4},{4,0},{8,12},{12,8},{1,5},{5,1},{9,13},{13,9},{2,6},{6,2},{1... | collective-permute-start | bytes 362504 | tf_op jit(solution)/shard_map/ppermute | solution.py:333
  36.1 8.7 %collective-permute-start.7 = (bf16[8,7552]{1,0:T(8,128)(2,1)S(1)}, bf16[8,7552]{1,0:T(8,128)(2,1)S(1)}, u32[]{:S(2)}, u32[]{:S(2)}) collective-permute-start(bf16[8,7552]{1,0:T(8,128)(2,1)S(1)} %shard_map.51.refs_0_), channel_id=1, source_target_pairs={{0,8},{4,12},{8,0},{12,4},{1,9},{5,13},{9,1},{13,5},{2,10},{6,14},... | collective-permute-start | bytes 362504 | tf_op jit(solution)/shard_map/ppermute | solution.py:333
  44.9 4.9 %collective-permute-start.9 = (bf16[8,7552]{1,0:T(8,128)(2,1)S(1)}, bf16[8,7552]{1,0:T(8,128)(2,1)S(1)}, u32[]{:S(2)}, u32[]{:S(2)}) collective-permute-start(bf16[8,7552]{1,0:T(8,128)(2,1)S(1)} %collective-permute-done.7.refs_0_), channel_id=1, source_target_pairs={{0,4},{4,0},{8,12},{12,8},{1,5},{5,1},{9,13},{13,9},{2,6},{6,2},{1... | collective-permute-start | bytes 362504 | tf_op jit(solution)/shard_map/ppermute | solution.py:333
  51.1 1.9 %collective-permute-start.10 = (bf16[8,2304]{1,0:T(8,128)(2,1)S(1)}, bf16[8,2304]{1,0:T(8,128)(2,1)S(1)}, u32[]{:S(2)}, u32[]{:S(2)}) collective-permute-start(bf16[8,2304]{1,0:T(8,128)(2,1)S(1)} %get-tuple-element.18), channel_id=1, source_target_pairs={{0,1},{1,0},{2,3},{3,2},{4,5},{5,4},{6,7},{7,6},{8,9},{9,8},{10,11... | collective-permute-start | bytes 110600 | tf_op jit(solution)/shard_map/ppermute | solution.py:333
  51.2 4.0 %collective-permute-start.11 = (bf16[8,2304]{1,0:T(8,128)(2,1)S(1)}, bf16[8,2304]{1,0:T(8,128)(2,1)S(1)}, u32[]{:S(2)}, u32[]{:S(2)}) collective-permute-start(bf16[8,2304]{1,0:T(8,128)(2,1)S(1)} %get-tuple-element.19), channel_id=1, source_target_pairs={{0,2},{1,3},{2,0},{3,1},{4,6},{5,7},{6,4},{7,5},{8,10},{9,11},{10,... | collective-permute-start | bytes 110600 | tf_op jit(solution)/shard_map/ppermute | solution.py:333
  52.7 3.4 %collective-permute-start.12 = (bf16[8,2304]{1,0:T(8,128)(2,1)S(1)}, bf16[8,2304]{1,0:T(8,128)(2,1)S(1)}, u32[]{:S(2)}, u32[]{:S(2)}) collective-permute-start(bf16[8,2304]{1,0:T(8,128)(2,1)S(1)} %get-tuple-element.20), channel_id=1, source_target_pairs={{0,3},{1,2},{2,1},{3,0},{4,7},{5,6},{6,5},{7,4},{8,11},{9,10},{10,... | collective-permute-start | bytes 110600 | tf_op jit(solution)/shard_map/ppermute | solution.py:333

commit v19 on v14

--- a/solution.py
+++ b/solution.py
@@ -11,6 +11,7 @@
 STEP = 256
 COPY_STEP = 512
 IN_FLIGHT = 6
+DOWN_STEP = 512
 TOKEN_AXES = ("gy", "gz")
 IN_HBM = pl.BlockSpec(memory_space=pltpu.HBM)
 ANY = pl.BlockSpec(memory_space=pl.ANY)
@@ -60,20 +61,26 @@
         out[:, at : at + width] = tail.astype(out.dtype)
 
 
-def block_copies(width, distance, weights, held, sems):
+def block_copies(width, distance, weights, first, held, sems):
     columns = pl.ds(block_start(distance, width), width)
     copies = []
     for k, (row, rows) in enumerate(pieces_of(held.shape[1], COPY_STEP)):
         for w, weight in enumerate(weights):
             copy = pltpu.make_async_copy(
-                weight.at[pl.ds(row, rows), columns], held.at[w, pl.ds(row, rows)], sems.at[w, k]
+                weight.at[pl.ds(first + row, rows), columns],
+                held.at[w, pl.ds(row, rows)],
+                sems.at[w, k],
             )
             copies.append((w, row, rows, copy))
     return copies
 
 
+def copy_sems(weights, depth):
+    return pltpu.SemaphoreType.DMA((weights, len(pieces_of(depth, COPY_STEP))))
+
+
 def fetch_kernel(width, distance, gate_ref, up_ref, held, sems):
-    copies = block_copies(width, distance, (gate_ref, up_ref), held, sems)
+    copies = block_copies(width, distance, (gate_ref, up_ref), 0, held, sems)
     for _, _, _, copy in copies:
         copy.start()
     for _, _, _, copy in copies:
@@ -87,88 +94,111 @@
         out_shape=pltpu.VMEM((2, depth, width), jnp.bfloat16),
         in_specs=[IN_HBM, IN_HBM],
         out_specs=WHOLE,
-        scratch_shapes=[pltpu.SemaphoreType.DMA((2, len(pieces_of(depth, COPY_STEP))))],
+        scratch_shapes=[copy_sems(2, depth)],
         compiler_params=params(4),
         cost_estimate=SMALL,
     )(in_hbm(gate_weight), in_hbm(up_weight))
 
 
-def multiply(x_ref, held, total, steps, waiting=()):
-    for w, first, tall, copy in steps:
+def multiply(x_ref, first, held, total, steps, waiting=()):
+    for w, top, tall, copy in steps:
         if copy is not None:
             copy.wait()
         if waiting:
             waiting.pop(0).start()
         for row, rows in pieces_of(tall, STEP):
-            rows = slice(first + row, first + row + rows)
-            term = jnp.dot(x_ref[:, rows], held[w, rows, :], preferred_element_type=jnp.float32)
-            if rows.start == 0:
+            at = first + top + row
+            term = jnp.dot(
+                x_ref[:, at : at + rows],
+                held[w, top + row : top + row + rows, :],
+                preferred_element_type=jnp.float32,
+            )
+            if at == 0:
                 total[w] = term
             else:
                 total[w] += term
 
 
-def held_kernel(x_ref, held, out, total):
-    parts = pieces_of(x_ref.shape[1], STEP)
-    multiply(x_ref, held, total, [(w, row, rows, None) for w in range(2) for row, rows in parts])
+def held_steps(held):
+    return [(w, row, rows, None) for row, rows in pieces_of(held.shape[1], STEP) for w in range(2)]
+
+
+def held_kernel(width, distance, x_ref, held, gate_ref, up_ref, out, ahead, total, sems):
+    copies = block_copies(width, distance, (gate_ref, up_ref), 0, ahead, sems)
+    for _, _, _, copy in copies:
+        copy.start()
+    multiply(x_ref, 0, held, total, held_steps(held))
     pack_pair(out, total[0], total[1])
-
-
-def gate_up_held(features, held):
+    for _, _, _, copy in copies:
+        copy.wait()
+
+
+def gate_up_held(features, held, gate_weight, up_weight, distance, ahead):
     rows, width = features.shape[0], held.shape[2]
     return pl.pallas_call(
-        held_kernel,
-        out_shape=jax.ShapeDtypeStruct((8, packed_pair_width(rows, width)), jnp.bfloat16),
-        in_specs=[WHOLE, WHOLE],
-        out_specs=WHOLE,
-        scratch_shapes=[pltpu.VMEM((2, rows, width), jnp.float32)],
+        functools.partial(held_kernel, width, distance),
+        out_shape=(
+            jax.ShapeDtypeStruct((8, packed_pair_width(rows, width)), jnp.bfloat16),
+            jax.ShapeDtypeStruct((2, ahead, width), jnp.bfloat16),
+        ),
+        in_specs=[WHOLE, WHOLE, IN_HBM, IN_HBM],
+        out_specs=(WHOLE, WHOLE),
+        scratch_shapes=[pltpu.VMEM((2, rows, width), jnp.float32), copy_sems(2, ahead)],
         compiler_params=params(8),
         cost_estimate=SMALL,
-    )(features, in_vmem(held))
-
-
-def stream_kernel(width, blocks, distances, x_ref, gate_ref, up_ref, _, *refs):
-    outs, refs = refs[: len(blocks)], refs[len(blocks) :]
+    )(features, in_vmem(held), in_hbm(gate_weight), in_hbm(up_weight))
+
+
+def stream_kernel(width, blocks, distances, has_held, x_ref, *refs):
+    refs = list(refs)
+    held_top = refs.pop(0) if has_held else None
+    gate_ref, up_ref, _ = refs[:3]
+    outs, refs = refs[3 : 3 + len(blocks)], refs[3 + len(blocks) :]
     work = []
     for b, which in enumerate(blocks):
         held, total, sems = refs[3 * b : 3 * b + 3]
         weights = [(gate_ref, up_ref)[w] for w in which]
-        copies = block_copies(width, distances[b], weights, held, sems)
-        work.append((outs[b], held, total, copies))
+        first = x_ref.shape[1] - held.shape[1]
+        copies = block_copies(width, distances[b], weights, first, held, sems)
+        work.append((outs[b], first, held, total, copies))
     waiting = [step[-1] for block in work for step in block[-1]]
     in_flight = IN_FLIGHT if len(blocks) > 1 else len(waiting)
     for copy in waiting[:in_flight]:
         copy.start()
     waiting = waiting[in_flight:]
-    for (out, held, total, copies), which in zip(work, blocks):
-        multiply(x_ref, held, total, copies, waiting)
+    if has_held:
+        multiply(x_ref, 0, held_top, work[0][3], held_steps(held_top))
+    for (out, first, held, total, copies), which in zip(work, blocks):
+        multiply(x_ref, first, held, total, copies, waiting)
         if len(which) == 2:
             pack_pair(out, total[0], total[1])
         else:
             pack_single(out, total[0])
 
 
-def gate_up_stream(features, gate_weight, up_weight, distances, blocks, width, after):
+def gate_up_stream(features, gate_weight, up_weight, distances, blocks, width, after, held=None):
     rows, depth = features.shape
-    scratch, shapes = [], []
-    for which in blocks:
+    scratch, shapes, held_bytes = [], [], 0
+    for b, which in enumerate(blocks):
         packed = packed_pair_width(rows, width) if len(which) == 2 else packed_width(rows, width)
         shapes.append(jax.ShapeDtypeStruct((8, packed), jnp.bfloat16))
+        below = depth - (held.shape[1] if held is not None and b == 0 else 0)
+        held_bytes += len(which) * below * width * 2
         scratch += [
-            pltpu.VMEM((len(which), depth, width), jnp.bfloat16),
+            pltpu.VMEM((len(which), below, width), jnp.bfloat16),
             pltpu.VMEM((len(which), rows, width), jnp.float32),
-            pltpu.SemaphoreType.DMA((len(which), len(pieces_of(depth, COPY_STEP)))),
+            copy_sems(len(which), below),
         ]
-    held_mib = -(-depth * width * 2 * sum(len(which) for which in blocks) // MIB)
-    return pl.pallas_call(
-        functools.partial(stream_kernel, width, blocks, distances),
+    before = [] if held is None else [held]
+    return pl.pallas_call(
+        functools.partial(stream_kernel, width, blocks, distances, held is not None),
         out_shape=shapes,
-        in_specs=[WHOLE, IN_HBM, IN_HBM, ANY],
+        in_specs=[WHOLE] * (1 + len(before)) + [IN_HBM, IN_HBM, ANY],
         out_specs=[WHOLE] * len(blocks),
         scratch_shapes=scratch,
-        compiler_params=params(5 + held_mib),
-        cost_estimate=SMALL,
-    )(features, in_hbm(gate_weight), in_hbm(up_weight), after)
+        compiler_params=params(8 + -(-held_bytes // MIB)),
+        cost_estimate=SMALL,
+    )(features, *before, in_hbm(gate_weight), in_hbm(up_weight), after)
 
 
 def hidden_tail(rows, width):
@@ -272,7 +302,7 @@
             tail = hidden[b][:, at : at + half].astype(jnp.float32)
             plain[rows - 4 :, :half] = tail[:4]
             plain[rows - 4 :, half:] = tail[4:, : width - half]
-        for row, tall in pieces_of(width, STEP):
+        for row, tall in pieces_of(width, DOWN_STEP):
             term = jnp.dot(
                 plain[:, row : row + tall].astype(jnp.bfloat16),
                 held[pl.ds(pl.multiple_of(block_start(distances[b], width) + row, 128), tall), :],
@@ -350,12 +380,15 @@
     )
     rows = features.shape[0]
 
-    def blocks_for(distances, blocks, after):
-        return gate_up_stream(features, gate_weight, up_weight, distances, blocks, width, after)
-
-    relayed = gate_up_held(features, held)
+    def blocks_for(distances, blocks, after, held=None):
+        return gate_up_stream(
+            features, gate_weight, up_weight, distances, blocks, width, after, held
+        )
+
+    ahead = gate_weight.shape[0] // 4 // STEP * STEP
+    relayed, held = gate_up_held(features, held, gate_weight, up_weight, 2, ahead)
     arrived = swap(relayed, "gx", n_gx, 1)
-    across, beside = blocks_for((2, 1), ((0, 1), (0,)), relayed)
+    across, beside = blocks_for((2, 1), ((0, 1), (0,)), relayed, held)
     across = lax.optimization_barrier(add(across, arrived).astype(jnp.bfloat16))
     far = swap(across, "gx", n_gx, 2)
     near = [swap(beside, "gx", n_gx, 1)]
@@ -393,7 +426,7 @@
     n_token = lax.axis_size(TOKEN_AXES)
     rows = tokens.shape[0] * n_token
     tokens_fit = n_token > 1 and n_token & (n_token - 1) == 0 and rows % 4 == 0
-    weights_fit = gate_weight.shape[1] % (128 * 4) == 0 and gate_weight.shape[0] % STEP == 0
+    weights_fit = gate_weight.shape[1] % (128 * 4) == 0 and gate_weight.shape[0] % (4 * STEP) == 0
     columns_fit = down_weight.shape[1] % (128 * 8) == 0
     if n_gx == 4 and tokens_fit and weights_fit and columns_fit:
         return direct(tokens, gate_weight, up_weight, down_weight)

time: 55.1 us -> 56.5 us (1.025)
  Pallas kernels: 30.5 us -> 31.8 us
    pallas_call x4, Pallas kernels: 19.6 us -> 20.9 us  [the longest x3 17 us: gate_up_stream(): pl.pallas_call(functools.partial(stream_kernel, width, blocks, distances,...]
  transfers between devices with their start and end apart: 13 -> 13, of which waited for: 6 -> 6; matrix products, arithmetic and copies ran while one was open for 0% -> 0% of each run, Pallas kernels for 48% -> 46%
where the time goes in v19:
time: 56.5 us; the launch traced here: 56.4 us
  Pallas kernels  31.8 us (56%)
  starting transfers between devices  13.6 us (24%)
  waiting for transfers between devices  10.6 us (19%)
    pallas_call x3, Pallas kernels, gate_up_stream(): pl.pallas_call(functools.partial(stream_kernel, width, blocks, distances,...  17 us
    ppermute x13, starting transfers between devices, swap(): return lax.ppermute(value, axes, [(i, i ^ distance) for i in range(size)])  13.6 us
    ppermute x13, waiting for transfers between devices, swap(): return lax.ppermute(value, axes, [(i, i ^ distance) for i in range(size)])  10.6 us
    pallas_call x1, Pallas kernels, fetch(): pl.pallas_call(functools.partial(fetch_kernel, width, distance), out_shap...  5.16 us
    pallas_call x2, Pallas kernels, down(): pl.pallas_call(functools.partial(down_kernel, before is None, rows, width...  4.92 us
    pallas_call x1, Pallas kernels, gate_up_held(): pl.pallas_call(functools.partial(held_kernel, width, distance), out_shape...  3.96 us
  transfers between devices with their start and end apart: 13, of which 6 were waited for; matrix products, arithmetic and copies ran while one was open for 0% of the time, Pallas kernels for 46%

profile of v19, /device:TPU:0, one launch (start us, length us, event | category | flops | bytes accessed | tf_op | source)
XLA Modules:
  0.0 56.4 jit_solution(16803418251041783419)
XLA Ops:
  0.0 0.0 copy-start
  0.0 2.9 %collective-permute-start.1 = (bf16[9,2048]{1,0:T(8,128)(2,1)}, bf16[9,2048]{1,0:T(8,128)(2,1)S(1)}, u32[]{:S(2)}, u32[]{:S(2)}) collective-permute-start(bf16[9,2048]{1,0:T(8,128)(2,1)} %param.4), channel_id=1, source_target_pairs={{0,2},{1,3},{2,0},{3,1},{4,6},{5,7},{6,4},{7,5},{8,10},{9,11},{10,... | collective-permute-start | bytes 110600 | tf_op jit(solution)/shard_map/ppermute | solution.py:365
  2.9 0.0 collective-permute-start
  2.9 0.2 collective-permute-start.2
  3.1 5.2 %shard_map.46.held = bf16[2,2048,1664]{2,1,0:T(8,128)(2,1)S(1)} custom-call(bf16[2048,6656]{1,0:T(8,128)(2,1)} %refs_0_.3, bf16[2048,6656]{1,0:T(8,128)(2,1)} %refs_1_.5), custom_call_target="tpu_custom_call" | custom-call | bytes 1048576 | tf_op jit(solution)/shard_map/pallas_call | solution.py:92
  8.3 0.0 collective-permute-done.1
  8.3 0.0 collective-permute-done
  8.3 0.0 collective-permute-done.2
  8.3 0.0 copy-done
  8.3 0.1 pad_maximum_fusion.x_ref
  8.4 4.0 %shard_map.47 = (bf16[8,14976]{1,0:T(8,128)(2,1)S(1)}, bf16[2,512,1664]{2,1,0:T(8,128)(2,1)S(1)}) custom-call(bf16[36,2048]{1,0:T(8,128)(2,1)S(1)} %pad_maximum_fusion.x_ref, bf16[2,2048,1664]{2,1,0:T(8,128)(2,1)S(1)} %shard_map.46.held, bf16[2048,6656]{1,0:T(8,128)(2,1)} %refs_0_.3, bf16[2048,6656]{1,0:T(8,128)(2,1)} %refs_1_.5), custom_call_target="tpu_custom_call" | custom-call | bytes 1048576 | tf_op jit(solution)/shard_map/pallas_call | solution.py:138
  12.4 2.0 %collective-permute-start.3 = (bf16[8,14976]{1,0:T(8,128)(2,1)S(1)}, bf16[8,14976]{1,0:T(8,128)(2,1)S(1)}, u32[]{:S(2)}, u32[]{:S(2)}) collective-permute-start(bf16[8,14976]{1,0:T(8,128)(2,1)S(1)} %get-tuple-element.14.refs_3_), channel_id=1, source_target_pairs={{0,4},{4,0},{8,12},{12,8},{1,5},{5,1},{9,13},{13,9},{2,6},{6,2},{1... | collective-permute-start | bytes 718856 | tf_op jit(solution)/shard_map/ppermute | solution.py:365
  14.4 7.1 %shard_map.48 = (bf16[8,14976]{1,0:T(8,128)(2,1)S(1)}, bf16[8,7552]{1,0:T(8,128)(2,1)S(1)}) custom-call(bf16[36,2048]{1,0:T(8,128)(2,1)S(1)} %pad_maximum_fusion.x_ref, bf16[2,512,1664]{2,1,0:T(8,128)(2,1)S(1)} %get-tuple-element.13.refs_0_, bf16[2048,6656]{1,0:T(8,128)(2,1)} %refs_0_.3, bf16[2048,6656]{1,0:T(8,128)(2,1)} %refs_1_.5, ...), custom_call_target="tpu_custom_call" | custom-call | bytes 1048576 | tf_op jit(solution)/shard_map/pallas_call | solution.py:193
  21.5 0.0 collective-permute-done.3
  21.5 0.1 add_convert_fusion.refs_2_
  21.6 2.7 %collective-permute-start.4 = (bf16[8,14976]{1,0:T(8,128)(2,1)S(1)}, bf16[8,14976]{1,0:T(8,128)(2,1)S(1)}, u32[]{:S(2)}, u32[]{:S(2)}) collective-permute-start(bf16[8,14976]{1,0:T(8,128)(2,1)S(1)} %add_convert_fusion.refs_2_), channel_id=1, source_target_pairs={{0,8},{4,12},{8,0},{12,4},{1,9},{5,13},{9,1},{13,5},{2,10},{6,14},... | collective-permute-start | bytes 718856 | tf_op jit(solution)/shard_map/ppermute | solution.py:365
  24.3 0.6 collective-permute-start.5
  24.9 0.0 slice-start
  24.9 0.0 slice-start.1
  24.9 0.0 slice-start.2
  24.9 0.0 slice-start.3
  24.9 3.6 %shard_map.49.refs_2_ = bf16[8,7552]{1,0:T(8,128)(2,1)S(1)} custom-call(bf16[36,2048]{1,0:T(8,128)(2,1)S(1)} %pad_maximum_fusion.x_ref, bf16[2048,6656]{1,0:T(8,128)(2,1)} %refs_0_.3, bf16[2048,6656]{1,0:T(8,128)(2,1)} %refs_1_.5, bf16[8,14976]{1,0:T(8,128)(2,1)S(1)} %add_convert_fusion.refs_2_), custom_call_target="tpu_custom_call" | custom-call | bytes 1048576 | tf_op jit(solution)/shard_map/pallas_call | solution.py:193
  28.5 0.0 slice-start.4
  28.5 0.0 slice-start.5
  28.5 0.0 slice-start.6
  28.5 1.5 %collective-permute-start.6 = (bf16[8,7552]{1,0:T(8,128)(2,1)S(1)}, bf16[8,7552]{1,0:T(8,128)(2,1)S(1)}, u32[]{:S(2)}, u32[]{:S(2)}) collective-permute-start(bf16[8,7552]{1,0:T(8,128)(2,1)S(1)} %shard_map.49.refs_2_), channel_id=1, source_target_pairs={{0,4},{4,0},{8,12},{12,8},{1,5},{5,1},{9,13},{13,9},{2,6},{6,2},{1... | collective-permute-start | bytes 362504 | tf_op jit(solution)/shard_map/ppermute | solution.py:365
  30.0 6.2 %shard_map.50.own = bf16[8,14976]{1,0:T(8,128)(2,1)S(1)} custom-call(bf16[36,2048]{1,0:T(8,128)(2,1)S(1)} %pad_maximum_fusion.x_ref, bf16[2048,6656]{1,0:T(8,128)(2,1)} %refs_0_.3, bf16[2048,6656]{1,0:T(8,128)(2,1)} %refs_1_.5, bf16[8,7552]{1,0:T(8,128)(2,1)S(1)} %shard_map.49.refs_2_), custom_call_target="tpu_custom_call" | custom-call | bytes 1048576 | tf_op jit(solution)/shard_map/pallas_call | solution.py:193
  36.3 0.0 collective-permute-done.5.gate_near
  36.3 0.7 %collective-permute-done.6.up_near = bf16[8,7552]{1,0:T(8,128)(2,1)S(1)} collective-permute-done((bf16[8,7552]{1,0:T(8,128)(2,1)S(1)}, bf16[8,7552]{1,0:T(8,128)(2,1)S(1)}, u32[]{:S(2)}, u32[]{:S(2)}) %collective-permute-start.6) | collective-permute-done | bytes 120864 | tf_op jit(solution)/shard_map/ppermute | solution.py:365
  37.0 0.0 collective-permute-done.4.far
  37.0 0.1 shard_map.51.refs_0_
  37.2 0.1 collective-permute-start.7
  37.3 1.7 %collective-permute-start.9 = (bf16[8,7552]{1,0:T(8,128)(2,1)S(1)}, bf16[8,7552]{1,0:T(8,128)(2,1)S(1)}, u32[]{:S(2)}, u32[]{:S(2)}) collective-permute-start(bf16[8,7552]{1,0:T(8,128)(2,1)S(1)} %shard_map.51.refs_0_), channel_id=1, source_target_pairs={{0,4},{4,0},{8,12},{12,8},{1,5},{5,1},{9,13},{13,9},{2,6},{6,2},{1... | collective-permute-start | bytes 362504 | tf_op jit(solution)/shard_map/ppermute | solution.py:365
  39.0 5.3 %collective-permute-done.7.refs_2_ = bf16[8,7552]{1,0:T(8,128)(2,1)S(1)} collective-permute-done((bf16[8,7552]{1,0:T(8,128)(2,1)S(1)}, bf16[8,7552]{1,0:T(8,128)(2,1)S(1)}, u32[]{:S(2)}, u32[]{:S(2)}) %collective-permute-start.7) | collective-permute-done | bytes 120864 | tf_op jit(solution)/shard_map/ppermute | solution.py:365
  44.3 0.0 collective-permute-start.8
  44.3 0.1 collective-permute-done.9.refs_1_
  44.5 0.0 slice-done
  44.5 0.0 slice-done.1
  44.5 0.0 slice-done.2
  44.5 0.0 slice-done.3
  44.5 0.0 slice-done.4
  44.5 0.0 slice-done.5
  44.5 0.0 slice-done.6
  44.5 3.6 %shard_map.52.refs_1_ = f32[36,2048]{1,0:T(8,128)S(1)} custom-call(bf16[8,7552]{1,0:T(8,128)(2,1)S(1)} %shard_map.51.refs_0_, bf16[8,7552]{1,0:T(8,128)(2,1)S(1)} %collective-permute-done.9.refs_1_, bf16[8,7552]{1,0:T(8,128)(2,1)S(1)} %collective-permute-done.7.refs_2_, bf16[6656,2048]{1,0:T(8,128)(2,1)S(1)} %bitcast.1), custom_call_target="tpu_custom_call" | custom-call | bytes 1048576 | tf_op jit(solution)/shard_map/pallas_call | solution.py:329
  48.1 1.0 %collective-permute-done.8.refs_0_ = bf16[8,7552]{1,0:T(8,128)(2,1)S(1)} collective-permute-done((bf16[8,7552]{1,0:T(8,128)(2,1)S(1)}, bf16[8,7552]{1,0:T(8,128)(2,1)S(1)}, u32[]{:S(2)}, u32[]{:S(2)}) %collective-permute-start.8) | collective-permute-done | bytes 120864 | tf_op jit(solution)/shard_map/ppermute | solution.py:365
  49.2 1.3 %shard_map.53 = (f32[8,2304]{1,0:T(8,128)S(1)}, bf16[8,2304]{1,0:T(8,128)(2,1)S(1)}, bf16[8,2304]{1,0:T(8,128)(2,1)S(1)}, bf16[8,2304]{1,0:T(8,128)(2,1)S(1)}) custom-call(bf16[8,7552]{1,0:T(8,128)(2,1)S(1)} %collective-permute-done.8.refs_0_, f32[36,2048]{1,0:T(8,128)S(1)} %shard_map.52.refs_1_, bf16[6656,2048]{1,0:T(8,128)(2,1)S(1)} %bitcast.1), custom_call_target="tpu_custom_call" | custom-call | bytes 1048576 | tf_op jit(solution)/shard_map/pallas_call | solution.py:329
  50.5 0.1 collective-permute-start.10
  50.6 1.7 %collective-permute-start.11 = (bf16[8,2304]{1,0:T(8,128)(2,1)S(1)}, bf16[8,2304]{1,0:T(8,128)(2,1)S(1)}, u32[]{:S(2)}, u32[]{:S(2)}) collective-permute-start(bf16[8,2304]{1,0:T(8,128)(2,1)S(1)} %get-tuple-element.19), channel_id=1, source_target_pairs={{0,2},{1,3},{2,0},{3,1},{4,6},{5,7},{6,4},{7,5},{8,10},{9,11},{10,... | collective-permute-start | bytes 110600 | tf_op jit(solution)/shard_map/ppermute | solution.py:365
  52.3 0.1 collective-permute-start.12
  52.4 0.0 collective-permute-done.10.refs_1_
  52.4 2.2 %collective-permute-done.11.refs_2_ = bf16[8,2304]{1,0:T(8,128)(2,1)S(1)} collective-permute-done((bf16[8,2304]{1,0:T(8,128)(2,1)S(1)}, bf16[8,2304]{1,0:T(8,128)(2,1)S(1)}, u32[]{:S(2)}, u32[]{:S(2)}) %collective-permute-start.11) | collective-permute-done | bytes 36896 | tf_op jit(solution)/shard_map/ppermute | solution.py:365
  54.6 1.1 %collective-permute-done.12.refs_3_ = bf16[8,2304]{1,0:T(8,128)(2,1)S(1)} collective-permute-done((bf16[8,2304]{1,0:T(8,128)(2,1)S(1)}, bf16[8,2304]{1,0:T(8,128)(2,1)S(1)}, u32[]{:S(2)}, u32[]{:S(2)}) %collective-permute-start.12) | collective-permute-done | bytes 36896 | tf_op jit(solution)/shard_map/ppermute | solution.py:365
  55.7 0.7 %shard_map.54 = bf16[9,2048]{1,0:T(8,128)(2,1)} custom-call(f32[8,2304]{1,0:T(8,128)S(1)} %get-tuple-element.17.refs_0_, bf16[8,2304]{1,0:T(8,128)(2,1)S(1)} %collective-permute-done.10.refs_1_, bf16[8,2304]{1,0:T(8,128)(2,1)S(1)} %collective-permute-done.11.refs_2_, bf16[8,2304]{1,0:T(8,128)(2,1)S(1)} %collective-permute-done.12.refs_3_), custom_call_target="tpu_custom_call" | custom-call | bytes 1048576 | tf_op jit(solution)/shard_map/pallas_call | solution.py:353
  (1 shorter events, 0.0 us)
Async XLA Ops:
  0.0 8.3 %copy-start = (bf16[9,2048]{1,0:T(8,128)(2,1)S(1)}, bf16[9,2048]{1,0:T(8,128)(2,1)}, u32[]{:S(2)}) copy-start(bf16[9,2048]{1,0:T(8,128)(2,1)} %param.4) | copy-start | bytes 110596
  0.0 8.3 %collective-permute-start.1 = (bf16[9,2048]{1,0:T(8,128)(2,1)}, bf16[9,2048]{1,0:T(8,128)(2,1)S(1)}, u32[]{:S(2)}, u32[]{:S(2)}) collective-permute-start(bf16[9,2048]{1,0:T(8,128)(2,1)} %param.4), channel_id=1, source_target_pairs={{0,2},{1,3},{2,0},{3,1},{4,6},{5,7},{6,4},{7,5},{8,10},{9,11},{10,... | collective-permute-start | bytes 110600 | tf_op jit(solution)/shard_map/ppermute | solution.py:365
  2.9 5.4 %collective-permute-start = (bf16[9,2048]{1,0:T(8,128)(2,1)}, bf16[9,2048]{1,0:T(8,128)(2,1)S(1)}, u32[]{:S(2)}, u32[]{:S(2)}) collective-permute-start(bf16[9,2048]{1,0:T(8,128)(2,1)} %param.4), channel_id=1, source_target_pairs={{0,1},{1,0},{2,3},{3,2},{4,5},{5,4},{6,7},{7,6},{8,9},{9,8},{10,11... | collective-permute-start | bytes 110600 | tf_op jit(solution)/shard_map/ppermute | solution.py:365
  2.9 5.4 %collective-permute-start.2 = (bf16[9,2048]{1,0:T(8,128)(2,1)}, bf16[9,2048]{1,0:T(8,128)(2,1)S(1)}, u32[]{:S(2)}, u32[]{:S(2)}) collective-permute-start(bf16[9,2048]{1,0:T(8,128)(2,1)} %param.4), channel_id=1, source_target_pairs={{0,3},{1,2},{2,1},{3,0},{4,7},{5,6},{6,5},{7,4},{8,11},{9,10},{10,... | collective-permute-start | bytes 110600 | tf_op jit(solution)/shard_map/ppermute | solution.py:365
  12.4 9.1 %collective-permute-start.3 = (bf16[8,14976]{1,0:T(8,128)(2,1)S(1)}, bf16[8,14976]{1,0:T(8,128)(2,1)S(1)}, u32[]{:S(2)}, u32[]{:S(2)}) collective-permute-start(bf16[8,14976]{1,0:T(8,128)(2,1)S(1)} %get-tuple-element.14.refs_3_), channel_id=1, source_target_pairs={{0,4},{4,0},{8,12},{12,8},{1,5},{5,1},{9,13},{13,9},{2,6},{6,2},{1... | collective-permute-start | bytes 718856 | tf_op jit(solution)/shard_map/ppermute | solution.py:365
  21.6 15.4 %collective-permute-start.4 = (bf16[8,14976]{1,0:T(8,128)(2,1)S(1)}, bf16[8,14976]{1,0:T(8,128)(2,1)S(1)}, u32[]{:S(2)}, u32[]{:S(2)}) collective-permute-start(bf16[8,14976]{1,0:T(8,128)(2,1)S(1)} %add_convert_fusion.refs_2_), channel_id=1, source_target_pairs={{0,8},{4,12},{8,0},{12,4},{1,9},{5,13},{9,1},{13,5},{2,10},{6,14},... | collective-permute-start | bytes 718856 | tf_op jit(solution)/shard_map/ppermute | solution.py:365
  24.3 12.0 %collective-permute-start.5 = (bf16[8,7552]{1,0:T(8,128)(2,1)S(1)}, bf16[8,7552]{1,0:T(8,128)(2,1)S(1)}, u32[]{:S(2)}, u32[]{:S(2)}) collective-permute-start(bf16[8,7552]{1,0:T(8,128)(2,1)S(1)} %get-tuple-element.16), channel_id=1, source_target_pairs={{0,4},{4,0},{8,12},{12,8},{1,5},{5,1},{9,13},{13,9},{2,6},{6,2},{1... | collective-permute-start | bytes 362504 | tf_op jit(solution)/shard_map/ppermute | solution.py:365
  24.9 19.6 %slice-start = ((s8[27262976]{0:T(1024)(128)(4,1)}), s8[4194304]{0:T(1024)(128)(4,1)S(1)}, s32[]{:S(2)}) async-start(s8[27262976]{0:T(1024)(128)(4,1)} %bitcast), calls=%async_computation | async-start | bytes 8388608
  24.9 19.6 %slice-start.1 = ((s8[27262976]{0:T(1024)(128)(4,1)}), s8[4194304]{0:T(1024)(128)(4,1)S(1)}, s32[]{:S(2)}) async-start(s8[27262976]{0:T(1024)(128)(4,1)} %bitcast), calls=%async_computation.1 | async-start | bytes 8388608
  24.9 19.6 %slice-start.2 = ((s8[27262976]{0:T(1024)(128)(4,1)}), s8[4194304]{0:T(1024)(128)(4,1)S(1)}, s32[]{:S(2)}) async-start(s8[27262976]{0:T(1024)(128)(4,1)} %bitcast), calls=%async_computation.2 | async-start | bytes 8388608
  24.9 19.6 %slice-start.3 = ((s8[27262976]{0:T(1024)(128)(4,1)}), s8[4194304]{0:T(1024)(128)(4,1)S(1)}, s32[]{:S(2)}) async-start(s8[27262976]{0:T(1024)(128)(4,1)} %bitcast), calls=%async_computation.3 | async-start | bytes 8388608
  28.5 16.0 %slice-start.4 = ((s8[27262976]{0:T(1024)(128)(4,1)}), s8[4194304]{0:T(1024)(128)(4,1)S(1)}, s32[]{:S(2)}) async-start(s8[27262976]{0:T(1024)(128)(4,1)} %bitcast), calls=%async_computation.4 | async-start | bytes 8388608
  28.5 16.0 %slice-start.5 = ((s8[27262976]{0:T(1024)(128)(4,1)}), s8[4194304]{0:T(1024)(128)(4,1)S(1)}, s32[]{:S(2)}) async-start(s8[27262976]{0:T(1024)(128)(4,1)} %bitcast), calls=%async_computation.5 | async-start | bytes 8388608
  28.5 16.0 %slice-start.6 = ((s8[27262976]{0:T(1024)(128)(4,1)}), s8[2097152]{0:T(1024)(128)(4,1)S(1)}, s32[]{:S(2)}) async-start(s8[27262976]{0:T(1024)(128)(4,1)} %bitcast), calls=%async_computation.6 | async-start | bytes 4194304
  28.5 8.5 %collective-permute-start.6 = (bf16[8,7552]{1,0:T(8,128)(2,1)S(1)}, bf16[8,7552]{1,0:T(8,128)(2,1)S(1)}, u32[]{:S(2)}, u32[]{:S(2)}) collective-permute-start(bf16[8,7552]{1,0:T(8,128)(2,1)S(1)} %shard_map.49.refs_2_), channel_id=1, source_target_pairs={{0,4},{4,0},{8,12},{12,8},{1,5},{5,1},{9,13},{13,9},{2,6},{6,2},{1... | collective-permute-start | bytes 362504 | tf_op jit(solution)/shard_map/ppermute | solution.py:365
  37.2 7.1 %collective-permute-start.7 = (bf16[8,7552]{1,0:T(8,128)(2,1)S(1)}, bf16[8,7552]{1,0:T(8,128)(2,1)S(1)}, u32[]{:S(2)}, u32[]{:S(2)}) collective-permute-start(bf16[8,7552]{1,0:T(8,128)(2,1)S(1)} %shard_map.51.refs_0_), channel_id=1, source_target_pairs={{0,8},{4,12},{8,0},{12,4},{1,9},{5,13},{9,1},{13,5},{2,10},{6,14},... | collective-permute-start | bytes 362504 | tf_op jit(solution)/shard_map/ppermute | solution.py:365
  37.3 7.2 %collective-permute-start.9 = (bf16[8,7552]{1,0:T(8,128)(2,1)S(1)}, bf16[8,7552]{1,0:T(8,128)(2,1)S(1)}, u32[]{:S(2)}, u32[]{:S(2)}) collective-permute-start(bf16[8,7552]{1,0:T(8,128)(2,1)S(1)} %shard_map.51.refs_0_), channel_id=1, source_target_pairs={{0,4},{4,0},{8,12},{12,8},{1,5},{5,1},{9,13},{13,9},{2,6},{6,2},{1... | collective-permute-start | bytes 362504 | tf_op jit(solution)/shard_map/ppermute | solution.py:365
  44.3 4.9 %collective-permute-start.8 = (bf16[8,7552]{1,0:T(8,128)(2,1)S(1)}, bf16[8,7552]{1,0:T(8,128)(2,1)S(1)}, u32[]{:S(2)}, u32[]{:S(2)}) collective-permute-start(bf16[8,7552]{1,0:T(8,128)(2,1)S(1)} %collective-permute-done.7.refs_2_), channel_id=1, source_target_pairs={{0,4},{4,0},{8,12},{12,8},{1,5},{5,1},{9,13},{13,9},{2,6},{6,2},{1... | collective-permute-start | bytes 362504 | tf_op jit(solution)/shard_map/ppermute | solution.py:365
  50.5 1.9 %collective-permute-start.10 = (bf16[8,2304]{1,0:T(8,128)(2,1)S(1)}, bf16[8,2304]{1,0:T(8,128)(2,1)S(1)}, u32[]{:S(2)}, u32[]{:S(2)}) collective-permute-start(bf16[8,2304]{1,0:T(8,128)(2,1)S(1)} %get-tuple-element.18), channel_id=1, source_target_pairs={{0,1},{1,0},{2,3},{3,2},{4,5},{5,4},{6,7},{7,6},{8,9},{9,8},{10,11... | collective-permute-start | bytes 110600 | tf_op jit(solution)/shard_map/ppermute | solution.py:365
  50.6 4.0 %collective-permute-start.11 = (bf16[8,2304]{1,0:T(8,128)(2,1)S(1)}, bf16[8,2304]{1,0:T(8,128)(2,1)S(1)}, u32[]{:S(2)}, u32[]{:S(2)}) collective-permute-start(bf16[8,2304]{1,0:T(8,128)(2,1)S(1)} %get-tuple-element.19), channel_id=1, source_target_pairs={{0,2},{1,3},{2,0},{3,1},{4,6},{5,7},{6,4},{7,5},{8,10},{9,11},{10,... | collective-permute-start | bytes 110600 | tf_op jit(solution)/shard_map/ppermute | solution.py:365
  52.3 3.4 %collective-permute-start.12 = (bf16[8,2304]{1,0:T(8,128)(2,1)S(1)}, bf16[8,2304]{1,0:T(8,128)(2,1)S(1)}, u32[]{:S(2)}, u32[]{:S(2)}) collective-permute-start(bf16[8,2304]{1,0:T(8,128)(2,1)S(1)} %get-tuple-element.20), channel_id=1, source_target_pairs={{0,3},{1,2},{2,1},{3,0},{4,7},{5,6},{6,5},{7,4},{8,11},{9,10},{10,... | collective-permute-start | bytes 110600 | tf_op jit(solution)/shard_map/ppermute | solution.py:365

commit v20 on v14

--- a/solution.py
+++ b/solution.py
@@ -11,6 +11,7 @@
 STEP = 256
 COPY_STEP = 512
 IN_FLIGHT = 6
+DOWN_STEP = 512
 TOKEN_AXES = ("gy", "gz")
 IN_HBM = pl.BlockSpec(memory_space=pltpu.HBM)
 ANY = pl.BlockSpec(memory_space=pl.ANY)
@@ -256,23 +257,24 @@
             out[r : r + 1, i * piece : (i + 1) * piece] = packed[i : i + 1, at : at + piece]
 
 
-def down_kernel(first, rows, width, distances, *refs):
-    blocks = len(distances)
-    hidden, refs = refs[:blocks], refs[blocks:]
-    if not first:
-        before, refs = refs[0], refs[1:]
+def down_kernel(first, rows, width, distances, counts, *refs):
+    refs = list(refs)
+    hidden = [[refs.pop(0) for _ in range(count)] for count in counts]
+    before = None if first else refs.pop(0)
     held, outs, (plain, total) = refs[0], refs[1:-2], refs[-2:]
     if first:
         total = outs[0]
-    for b in range(blocks):
+    for b, parts in enumerate(hidden):
+        packed = parts[0][...].astype(jnp.float32)
+        for part in parts[1:]:
+            packed = packed + part[...].astype(jnp.float32)
         for g in range(rows // 8):
-            plain[8 * g : 8 * g + 8, :] = hidden[b][:, g * width : (g + 1) * width].astype(jnp.float32)
+            plain[8 * g : 8 * g + 8, :] = packed[:, g * width : (g + 1) * width]
         if rows % 8:
             at, half = (rows // 8) * width, hidden_tail(rows, width)
-            tail = hidden[b][:, at : at + half].astype(jnp.float32)
-            plain[rows - 4 :, :half] = tail[:4]
-            plain[rows - 4 :, half:] = tail[4:, : width - half]
-        for row, tall in pieces_of(width, STEP):
+            plain[rows - 4 :, :half] = packed[:4, at : at + half]
+            plain[rows - 4 :, half:] = packed[4:, at : at + width - half]
+        for row, tall in pieces_of(width, DOWN_STEP):
             term = jnp.dot(
                 plain[:, row : row + tall].astype(jnp.bfloat16),
                 held[pl.ds(pl.multiple_of(block_start(distances[b], width) + row, 128), tall), :],
@@ -296,10 +298,12 @@
         packed = (8, rows // outs * columns // 8)
         shapes = [jax.ShapeDtypeStruct(packed, jnp.bfloat16 if r else jnp.float32) for r in range(outs)]
     carried = [] if before is None else [before]
-    return pl.pallas_call(
-        functools.partial(down_kernel, before is None, rows, width, distances),
+    counts = [len(parts) for parts in hidden]
+    arrays = [part for parts in hidden for part in parts]
+    return pl.pallas_call(
+        functools.partial(down_kernel, before is None, rows, width, distances, counts),
         out_shape=shapes,
-        in_specs=[WHOLE] * (len(hidden) + len(carried) + 1),
+        in_specs=[WHOLE] * (len(arrays) + len(carried) + 1),
         out_specs=[WHOLE] * len(shapes),
         scratch_shapes=[
             pltpu.VMEM((rows, width), jnp.float32),
@@ -307,7 +311,7 @@
         ],
         compiler_params=params(8),
         cost_estimate=SMALL,
-    )(*hidden, *carried, in_vmem(weight))
+    )(*arrays, *carried, in_vmem(weight))
 
 
 def finish_kernel(*refs):
@@ -329,6 +333,10 @@
         compiler_params=params(4),
         cost_estimate=SMALL,
     )(*terms)
+
+
+def send(value, axes, pairs):
+    return lax.ppermute(value, axes, pairs)
 
 
 def swap(value, axes, size, distance):
@@ -364,9 +372,16 @@
     (own,) = blocks_for((0,), ((0, 1),), beside)
     hidden = activate_packed(own, far, near, rows, width)
 
-    opposite = swap(hidden, "gx", n_gx, 2)
-    first = [hidden, swap(hidden, "gx", n_gx, 1), opposite]
-    second = [swap(opposite, "gx", n_gx, 1)]
+    inner, outer = (1, 2), (0, 3)
+    outward = send(hidden, "gx", [(i, i ^ 2) for i in inner])
+    inward = send(hidden, "gx", [(i, i ^ 2) for i in outer])
+    first = [(hidden,), (swap(hidden, "gx", n_gx, 1),), (outward, inward)]
+    second = [
+        (
+            send(outward, "gx", [(i, i ^ 1) for i in outer]),
+            send(inward, "gx", [(i, i ^ 1) for i in inner]),
+        )
+    ]
     (partial_sum,) = down(first, (0, 1, 2), None, down_weight, rows, width, 1)
     outs = down(second, (3,), partial_sum, down_weight, rows, width, n_token)
     terms = [outs[0]] + [swap(outs[r], TOKEN_AXES, n_token, r) for r in range(1, n_token)]

time: 55.1 us -> 59.9 us (1.087)
  starting transfers between devices: 13.4 us -> 23 us
  waiting for transfers between devices: 10.7 us -> 5.8 us
    ppermute x0 -> x4, starting transfers between devices: none -> 7.27 us  [send(): return lax.ppermute(value, axes, pairs)]
    ppermute x13 -> x11, waiting for transfers between devices: 10.7 us -> 4.14 us  [swap(): return lax.ppermute(value, axes, [(i, i ^ distance) for i in range(size)])]
    ppermute x13 -> x11, starting transfers between devices: 13.4 us -> 15.7 us  [swap(): return lax.ppermute(value, axes, [(i, i ^ distance) for i in range(size)])]
    ppermute x0 -> x4, waiting for transfers between devices: none -> 1.67 us  [send(): return lax.ppermute(value, axes, pairs)]
  transfers between devices with their start and end apart: 13 -> 15, of which waited for: 6 -> 4; matrix products, arithmetic and copies ran while one was open for 0% -> 0% of each run, Pallas kernels for 48% -> 44%
where the time goes in v20:
time: 59.9 us; the launch traced here: 59.7 us
  Pallas kernels  30.4 us (51%)
  starting transfers between devices  23 us (38%)
  waiting for transfers between devices  5.8 us (10%)
    pallas_call x3, Pallas kernels, gate_up_stream(): pl.pallas_call(functools.partial(stream_kernel, width, blocks, distances)...  17.4 us
    ppermute x11, starting transfers between devices, swap(): return lax.ppermute(value, axes, [(i, i ^ distance) for i in range(size)])  15.7 us
    ppermute x4, starting transfers between devices, send(): return lax.ppermute(value, axes, pairs)  7.27 us
    pallas_call x1, Pallas kernels, fetch(): pl.pallas_call(functools.partial(fetch_kernel, width, distance), out_shap...  5.16 us
    pallas_call x2, Pallas kernels, down(): pl.pallas_call(functools.partial(down_kernel, before is None, rows, width...  4.92 us
    ppermute x11, waiting for transfers between devices, swap(): return lax.ppermute(value, axes, [(i, i ^ distance) for i in range(size)])  4.14 us
    pallas_call x1, Pallas kernels, gate_up_held(): pl.pallas_call(held_kernel, out_shape=jax.ShapeDtypeStruct((8, packed_pai...  2.16 us
    ppermute x4, waiting for transfers between devices, send(): return lax.ppermute(value, axes, pairs)  1.67 us
  transfers between devices with their start and end apart: 15, of which 4 were waited for; matrix products, arithmetic and copies ran while one was open for 0% of the time, Pallas kernels for 44%

profile of v20, /device:TPU:0, one launch (start us, length us, event | category | flops | bytes accessed | tf_op | source)
XLA Modules:
  0.0 59.7 jit_solution(10831521232938671179)
XLA Ops:
  0.0 0.0 copy-start
  0.0 2.9 %collective-permute-start.1 = (bf16[9,2048]{1,0:T(8,128)(2,1)}, bf16[9,2048]{1,0:T(8,128)(2,1)S(1)}, u32[]{:S(2)}, u32[]{:S(2)}) collective-permute-start(bf16[9,2048]{1,0:T(8,128)(2,1)} %param.4), channel_id=1, source_target_pairs={{0,2},{1,3},{2,0},{3,1},{4,6},{5,7},{6,4},{7,5},{8,10},{9,11},{10,... | collective-permute-start | bytes 110600 | tf_op jit(solution)/shard_map/ppermute | solution.py:343
  2.9 0.0 collective-permute-start
  2.9 0.2 collective-permute-start.2
  3.1 5.2 %shard_map.46.held = bf16[2,2048,1664]{2,1,0:T(8,128)(2,1)S(1)} custom-call(bf16[2048,6656]{1,0:T(8,128)(2,1)} %gate_ref.7, bf16[2048,6656]{1,0:T(8,128)(2,1)} %up_ref.7), custom_call_target="tpu_custom_call" | custom-call | bytes 1048576 | tf_op jit(solution)/shard_map/pallas_call | solution.py:86
  8.3 0.0 collective-permute-done.1
  8.3 0.0 collective-permute-done
  8.3 0.0 collective-permute-done.2
  8.3 0.0 copy-done
  8.3 0.1 pad_maximum_fusion.x_ref
  8.4 2.2 %shard_map.47._ = bf16[8,14976]{1,0:T(8,128)(2,1)S(1)} custom-call(bf16[36,2048]{1,0:T(8,128)(2,1)S(1)} %pad_maximum_fusion.x_ref, bf16[2,2048,1664]{2,1,0:T(8,128)(2,1)S(1)} %shard_map.46.held), custom_call_target="tpu_custom_call" | custom-call | bytes 1048576 | tf_op jit(solution)/shard_map/pallas_call | solution.py:120
  10.6 2.0 %collective-permute-start.3 = (bf16[8,14976]{1,0:T(8,128)(2,1)S(1)}, bf16[8,14976]{1,0:T(8,128)(2,1)S(1)}, u32[]{:S(2)}, u32[]{:S(2)}) collective-permute-start(bf16[8,14976]{1,0:T(8,128)(2,1)S(1)} %shard_map.47._), channel_id=1, source_target_pairs={{0,4},{4,0},{8,12},{12,8},{1,5},{5,1},{9,13},{13,9},{2,6},{6,2},{1... | collective-permute-start | bytes 718856 | tf_op jit(solution)/shard_map/ppermute | solution.py:343
  12.6 7.6 %shard_map.48 = (bf16[8,14976]{1,0:T(8,128)(2,1)S(1)}, bf16[8,7552]{1,0:T(8,128)(2,1)S(1)}) custom-call(bf16[36,2048]{1,0:T(8,128)(2,1)S(1)} %pad_maximum_fusion.x_ref, bf16[2048,6656]{1,0:T(8,128)(2,1)} %gate_ref.7, bf16[2048,6656]{1,0:T(8,128)(2,1)} %up_ref.7, bf16[8,14976]{1,0:T(8,128)(2,1)S(1)} %shard_map.47._), custom_call_target="tpu_custom_call" | custom-call | bytes 1048576 | tf_op jit(solution)/shard_map/pallas_call | solution.py:164
  20.2 0.0 collective-permute-done.3
  20.2 0.1 add_convert_fusion._
  20.2 2.7 %collective-permute-start.4 = (bf16[8,14976]{1,0:T(8,128)(2,1)S(1)}, bf16[8,14976]{1,0:T(8,128)(2,1)S(1)}, u32[]{:S(2)}, u32[]{:S(2)}) collective-permute-start(bf16[8,14976]{1,0:T(8,128)(2,1)S(1)} %add_convert_fusion._), channel_id=1, source_target_pairs={{0,8},{4,12},{8,0},{12,4},{1,9},{5,13},{9,1},{13,5},{2,10},{6,14},... | collective-permute-start | bytes 718856 | tf_op jit(solution)/shard_map/ppermute | solution.py:343
  22.9 0.4 collective-permute-start.5
  23.3 0.0 slice-start
  23.3 0.0 slice-start.1
  23.3 0.0 slice-start.2
  23.3 0.0 slice-start.3
  23.3 3.6 %shard_map.49._ = bf16[8,7552]{1,0:T(8,128)(2,1)S(1)} custom-call(bf16[36,2048]{1,0:T(8,128)(2,1)S(1)} %pad_maximum_fusion.x_ref, bf16[2048,6656]{1,0:T(8,128)(2,1)} %gate_ref.7, bf16[2048,6656]{1,0:T(8,128)(2,1)} %up_ref.7, bf16[8,14976]{1,0:T(8,128)(2,1)S(1)} %add_convert_fusion._), custom_call_target="tpu_custom_call" | custom-call | bytes 1048576 | tf_op jit(solution)/shard_map/pallas_call | solution.py:164
  26.9 0.0 slice-start.4
  27.0 0.0 slice-start.5
  27.0 0.0 slice-start.6
  27.0 1.7 %collective-permute-start.6 = (bf16[8,7552]{1,0:T(8,128)(2,1)S(1)}, bf16[8,7552]{1,0:T(8,128)(2,1)S(1)}, u32[]{:S(2)}, u32[]{:S(2)}) collective-permute-start(bf16[8,7552]{1,0:T(8,128)(2,1)S(1)} %shard_map.49._), channel_id=1, source_target_pairs={{0,4},{4,0},{8,12},{12,8},{1,5},{5,1},{9,13},{13,9},{2,6},{6,2},{1... | collective-permute-start | bytes 362504 | tf_op jit(solution)/shard_map/ppermute | solution.py:343
  28.7 6.2 %shard_map.50.own = bf16[8,14976]{1,0:T(8,128)(2,1)S(1)} custom-call(bf16[36,2048]{1,0:T(8,128)(2,1)S(1)} %pad_maximum_fusion.x_ref, bf16[2048,6656]{1,0:T(8,128)(2,1)} %gate_ref.7, bf16[2048,6656]{1,0:T(8,128)(2,1)} %up_ref.7, bf16[8,7552]{1,0:T(8,128)(2,1)S(1)} %shard_map.49._), custom_call_target="tpu_custom_call" | custom-call | bytes 1048576 | tf_op jit(solution)/shard_map/pallas_call | solution.py:164
  34.9 0.0 collective-permute-done.5.gate_near
  34.9 1.0 %collective-permute-done.6.up_near = bf16[8,7552]{1,0:T(8,128)(2,1)S(1)} collective-permute-done((bf16[8,7552]{1,0:T(8,128)(2,1)S(1)}, bf16[8,7552]{1,0:T(8,128)(2,1)S(1)}, u32[]{:S(2)}, u32[]{:S(2)}) %collective-permute-start.6) | collective-permute-done | bytes 120864 | tf_op jit(solution)/shard_map/ppermute | solution.py:343
  35.9 0.0 collective-permute-done.4.far
  35.9 0.1 shard_map.51.refs_0_
  36.1 1.6 %collective-permute-start.9 = (bf16[8,7552]{1,0:T(8,128)(2,1)S(1)}, bf16[8,7552]{1,0:T(8,128)(2,1)S(1)}, u32[]{:S(2)}, u32[]{:S(2)}) collective-permute-start(bf16[8,7552]{1,0:T(8,128)(2,1)S(1)} %shard_map.51.refs_0_), channel_id=1, source_target_pairs={{0,8},{12,4},{1,9},{13,5},{2,10},{14,6},{3,11},{15,7},{16,24},{28,... | collective-permute-start | bytes 362504 | tf_op jit(solution)/shard_map/ppermute | solution.py:339
  37.7 1.3 %collective-permute-start.7 = (bf16[8,7552]{1,0:T(8,128)(2,1)S(1)}, bf16[8,7552]{1,0:T(8,128)(2,1)S(1)}, u32[]{:S(2)}, u32[]{:S(2)}) collective-permute-start(bf16[8,7552]{1,0:T(8,128)(2,1)S(1)} %shard_map.51.refs_0_), channel_id=1, source_target_pairs={{4,12},{8,0},{5,13},{9,1},{6,14},{10,2},{7,15},{11,3},{20,28},{24,... | collective-permute-start | bytes 362504 | tf_op jit(solution)/shard_map/ppermute | solution.py:339
  39.0 3.9 %collective-permute-start.11 = (bf16[8,7552]{1,0:T(8,128)(2,1)S(1)}, bf16[8,7552]{1,0:T(8,128)(2,1)S(1)}, u32[]{:S(2)}, u32[]{:S(2)}) collective-permute-start(bf16[8,7552]{1,0:T(8,128)(2,1)S(1)} %shard_map.51.refs_0_), channel_id=1, source_target_pairs={{0,4},{4,0},{8,12},{12,8},{1,5},{5,1},{9,13},{13,9},{2,6},{6,2},{1... | collective-permute-start | bytes 362504 | tf_op jit(solution)/shard_map/ppermute | solution.py:343
  42.9 0.0 collective-permute-done.9.refs_3_
  42.9 1.3 %collective-permute-start.10 = (bf16[8,7552]{1,0:T(8,128)(2,1)S(1)}, bf16[8,7552]{1,0:T(8,128)(2,1)S(1)}, u32[]{:S(2)}, u32[]{:S(2)}) collective-permute-start(bf16[8,7552]{1,0:T(8,128)(2,1)S(1)} %collective-permute-done.9.refs_3_), channel_id=1, source_target_pairs={{4,0},{8,12},{5,1},{9,13},{6,2},{10,14},{7,3},{11,15},{20,16},{24,... | collective-permute-start | bytes 362504 | tf_op jit(solution)/shard_map/ppermute | solution.py:339
  44.1 1.7 %collective-permute-done.7.refs_2_ = bf16[8,7552]{1,0:T(8,128)(2,1)S(1)} collective-permute-done((bf16[8,7552]{1,0:T(8,128)(2,1)S(1)}, bf16[8,7552]{1,0:T(8,128)(2,1)S(1)}, u32[]{:S(2)}, u32[]{:S(2)}) %collective-permute-start.7) | collective-permute-done | bytes 120864 | tf_op jit(solution)/shard_map/ppermute | solution.py:339
  45.8 3.1 %collective-permute-start.8 = (bf16[8,7552]{1,0:T(8,128)(2,1)S(1)}, bf16[8,7552]{1,0:T(8,128)(2,1)S(1)}, u32[]{:S(2)}, u32[]{:S(2)}) collective-permute-start(bf16[8,7552]{1,0:T(8,128)(2,1)S(1)} %collective-permute-done.7.refs_2_), channel_id=1, source_target_pairs={{0,4},{12,8},{1,5},{13,9},{2,6},{14,10},{3,7},{15,11},{16,20},{28,... | collective-permute-start | bytes 362504 | tf_op jit(solution)/shard_map/ppermute | solution.py:339
  48.9 0.0 collective-permute-done.11.refs_1_
  48.9 0.0 slice-done
  48.9 0.0 slice-done.1
  48.9 0.0 slice-done.2
  48.9 0.0 slice-done.3
  49.0 0.0 slice-done.4
  49.0 0.0 slice-done.5
  49.0 0.0 slice-done.6
  49.0 3.6 %shard_map.52.refs_2_ = f32[36,2048]{1,0:T(8,128)S(1)} custom-call(bf16[8,7552]{1,0:T(8,128)(2,1)S(1)} %shard_map.51.refs_0_, bf16[8,7552]{1,0:T(8,128)(2,1)S(1)} %collective-permute-done.11.refs_1_, bf16[8,7552]{1,0:T(8,128)(2,1)S(1)} %collective-permute-done.7.refs_2_, bf16[8,7552]{1,0:T(8,128)(2,1)S(1)} %collective-permute-done.9.refs_3_, ...), custom_call_target="tpu_custom_call" | custom-call | bytes 1048576 | tf_op jit(solution)/shard_map/pallas_call | solution.py:303
  52.6 0.0 collective-permute-done.10.refs_1_
  52.6 0.0 collective-permute-done.8.refs_0_
  52.6 1.3 %shard_map.53 = (f32[8,2304]{1,0:T(8,128)S(1)}, bf16[8,2304]{1,0:T(8,128)(2,1)S(1)}, bf16[8,2304]{1,0:T(8,128)(2,1)S(1)}, bf16[8,2304]{1,0:T(8,128)(2,1)S(1)}) custom-call(bf16[8,7552]{1,0:T(8,128)(2,1)S(1)} %collective-permute-done.8.refs_0_, bf16[8,7552]{1,0:T(8,128)(2,1)S(1)} %collective-permute-done.10.refs_1_, f32[36,2048]{1,0:T(8,128)S(1)} %shard_map.52.refs_2_, ...), custom_call_target="tpu_custom_call" | custom-call | bytes 1048576 | tf_op jit(solution)/shard_map/pallas_call | solution.py:303
  53.9 0.1 collective-permute-start.12
  54.0 1.6 %collective-permute-start.13 = (bf16[8,2304]{1,0:T(8,128)(2,1)S(1)}, bf16[8,2304]{1,0:T(8,128)(2,1)S(1)}, u32[]{:S(2)}, u32[]{:S(2)}) collective-permute-start(bf16[8,2304]{1,0:T(8,128)(2,1)S(1)} %get-tuple-element.15), channel_id=1, source_target_pairs={{0,2},{1,3},{2,0},{3,1},{4,6},{5,7},{6,4},{7,5},{8,10},{9,11},{10,... | collective-permute-start | bytes 110600 | tf_op jit(solution)/shard_map/ppermute | solution.py:343
  55.6 0.3 collective-permute-start.14
  55.9 0.0 collective-permute-done.12.refs_1_
  55.9 2.2 %collective-permute-done.13.refs_2_ = bf16[8,2304]{1,0:T(8,128)(2,1)S(1)} collective-permute-done((bf16[8,2304]{1,0:T(8,128)(2,1)S(1)}, bf16[8,2304]{1,0:T(8,128)(2,1)S(1)}, u32[]{:S(2)}, u32[]{:S(2)}) %collective-permute-start.13) | collective-permute-done | bytes 36896 | tf_op jit(solution)/shard_map/ppermute | solution.py:343
  58.0 1.0 %collective-permute-done.14.refs_3_ = bf16[8,2304]{1,0:T(8,128)(2,1)S(1)} collective-permute-done((bf16[8,2304]{1,0:T(8,128)(2,1)S(1)}, bf16[8,2304]{1,0:T(8,128)(2,1)S(1)}, u32[]{:S(2)}, u32[]{:S(2)}) %collective-permute-start.14) | collective-permute-done | bytes 36896 | tf_op jit(solution)/shard_map/ppermute | solution.py:343
  59.0 0.7 %shard_map.54 = bf16[9,2048]{1,0:T(8,128)(2,1)} custom-call(f32[8,2304]{1,0:T(8,128)S(1)} %get-tuple-element.13.refs_0_, bf16[8,2304]{1,0:T(8,128)(2,1)S(1)} %collective-permute-done.12.refs_1_, bf16[8,2304]{1,0:T(8,128)(2,1)S(1)} %collective-permute-done.13.refs_2_, bf16[8,2304]{1,0:T(8,128)(2,1)S(1)} %collective-permute-done.14.refs_3_), custom_call_target="tpu_custom_call" | custom-call | bytes 1048576 | tf_op jit(solution)/shard_map/pallas_call | solution.py:327
  (1 shorter events, 0.0 us)
Async XLA Ops:
  0.0 8.3 %copy-start = (bf16[9,2048]{1,0:T(8,128)(2,1)S(1)}, bf16[9,2048]{1,0:T(8,128)(2,1)}, u32[]{:S(2)}) copy-start(bf16[9,2048]{1,0:T(8,128)(2,1)} %param.4) | copy-start | bytes 110596
  0.0 8.3 %collective-permute-start.1 = (bf16[9,2048]{1,0:T(8,128)(2,1)}, bf16[9,2048]{1,0:T(8,128)(2,1)S(1)}, u32[]{:S(2)}, u32[]{:S(2)}) collective-permute-start(bf16[9,2048]{1,0:T(8,128)(2,1)} %param.4), channel_id=1, source_target_pairs={{0,2},{1,3},{2,0},{3,1},{4,6},{5,7},{6,4},{7,5},{8,10},{9,11},{10,... | collective-permute-start | bytes 110600 | tf_op jit(solution)/shard_map/ppermute | solution.py:343
  2.9 5.4 %collective-permute-start = (bf16[9,2048]{1,0:T(8,128)(2,1)}, bf16[9,2048]{1,0:T(8,128)(2,1)S(1)}, u32[]{:S(2)}, u32[]{:S(2)}) collective-permute-start(bf16[9,2048]{1,0:T(8,128)(2,1)} %param.4), channel_id=1, source_target_pairs={{0,1},{1,0},{2,3},{3,2},{4,5},{5,4},{6,7},{7,6},{8,9},{9,8},{10,11... | collective-permute-start | bytes 110600 | tf_op jit(solution)/shard_map/ppermute | solution.py:343
  2.9 5.4 %collective-permute-start.2 = (bf16[9,2048]{1,0:T(8,128)(2,1)}, bf16[9,2048]{1,0:T(8,128)(2,1)S(1)}, u32[]{:S(2)}, u32[]{:S(2)}) collective-permute-start(bf16[9,2048]{1,0:T(8,128)(2,1)} %param.4), channel_id=1, source_target_pairs={{0,3},{1,2},{2,1},{3,0},{4,7},{5,6},{6,5},{7,4},{8,11},{9,10},{10,... | collective-permute-start | bytes 110600 | tf_op jit(solution)/shard_map/ppermute | solution.py:343
  10.6 9.6 %collective-permute-start.3 = (bf16[8,14976]{1,0:T(8,128)(2,1)S(1)}, bf16[8,14976]{1,0:T(8,128)(2,1)S(1)}, u32[]{:S(2)}, u32[]{:S(2)}) collective-permute-start(bf16[8,14976]{1,0:T(8,128)(2,1)S(1)} %shard_map.47._), channel_id=1, source_target_pairs={{0,4},{4,0},{8,12},{12,8},{1,5},{5,1},{9,13},{13,9},{2,6},{6,2},{1... | collective-permute-start | bytes 718856 | tf_op jit(solution)/shard_map/ppermute | solution.py:343
  20.2 15.7 %collective-permute-start.4 = (bf16[8,14976]{1,0:T(8,128)(2,1)S(1)}, bf16[8,14976]{1,0:T(8,128)(2,1)S(1)}, u32[]{:S(2)}, u32[]{:S(2)}) collective-permute-start(bf16[8,14976]{1,0:T(8,128)(2,1)S(1)} %add_convert_fusion._), channel_id=1, source_target_pairs={{0,8},{4,12},{8,0},{12,4},{1,9},{5,13},{9,1},{13,5},{2,10},{6,14},... | collective-permute-start | bytes 718856 | tf_op jit(solution)/shard_map/ppermute | solution.py:343
  22.9 12.0 %collective-permute-start.5 = (bf16[8,7552]{1,0:T(8,128)(2,1)S(1)}, bf16[8,7552]{1,0:T(8,128)(2,1)S(1)}, u32[]{:S(2)}, u32[]{:S(2)}) collective-permute-start(bf16[8,7552]{1,0:T(8,128)(2,1)S(1)} %get-tuple-element.12), channel_id=1, source_target_pairs={{0,4},{4,0},{8,12},{12,8},{1,5},{5,1},{9,13},{13,9},{2,6},{6,2},{1... | collective-permute-start | bytes 362504 | tf_op jit(solution)/shard_map/ppermute | solution.py:343
  23.3 25.6 %slice-start = ((s8[27262976]{0:T(1024)(128)(4,1)}), s8[4194304]{0:T(1024)(128)(4,1)S(1)}, s32[]{:S(2)}) async-start(s8[27262976]{0:T(1024)(128)(4,1)} %bitcast), calls=%async_computation | async-start | bytes 8388608
  23.3 25.6 %slice-start.1 = ((s8[27262976]{0:T(1024)(128)(4,1)}), s8[4194304]{0:T(1024)(128)(4,1)S(1)}, s32[]{:S(2)}) async-start(s8[27262976]{0:T(1024)(128)(4,1)} %bitcast), calls=%async_computation.1 | async-start | bytes 8388608
  23.3 25.6 %slice-start.2 = ((s8[27262976]{0:T(1024)(128)(4,1)}), s8[4194304]{0:T(1024)(128)(4,1)S(1)}, s32[]{:S(2)}) async-start(s8[27262976]{0:T(1024)(128)(4,1)} %bitcast), calls=%async_computation.2 | async-start | bytes 8388608
  23.3 25.6 %slice-start.3 = ((s8[27262976]{0:T(1024)(128)(4,1)}), s8[4194304]{0:T(1024)(128)(4,1)S(1)}, s32[]{:S(2)}) async-start(s8[27262976]{0:T(1024)(128)(4,1)} %bitcast), calls=%async_computation.3 | async-start | bytes 8388608
  26.9 22.0 %slice-start.4 = ((s8[27262976]{0:T(1024)(128)(4,1)}), s8[4194304]{0:T(1024)(128)(4,1)S(1)}, s32[]{:S(2)}) async-start(s8[27262976]{0:T(1024)(128)(4,1)} %bitcast), calls=%async_computation.4 | async-start | bytes 8388608
  27.0 22.0 %slice-start.5 = ((s8[27262976]{0:T(1024)(128)(4,1)}), s8[4194304]{0:T(1024)(128)(4,1)S(1)}, s32[]{:S(2)}) async-start(s8[27262976]{0:T(1024)(128)(4,1)} %bitcast), calls=%async_computation.5 | async-start | bytes 8388608
  27.0 22.0 %slice-start.6 = ((s8[27262976]{0:T(1024)(128)(4,1)}), s8[2097152]{0:T(1024)(128)(4,1)S(1)}, s32[]{:S(2)}) async-start(s8[27262976]{0:T(1024)(128)(4,1)} %bitcast), calls=%async_computation.6 | async-start | bytes 4194304
  27.0 8.9 %collective-permute-start.6 = (bf16[8,7552]{1,0:T(8,128)(2,1)S(1)}, bf16[8,7552]{1,0:T(8,128)(2,1)S(1)}, u32[]{:S(2)}, u32[]{:S(2)}) collective-permute-start(bf16[8,7552]{1,0:T(8,128)(2,1)S(1)} %shard_map.49._), channel_id=1, source_target_pairs={{0,4},{4,0},{8,12},{12,8},{1,5},{5,1},{9,13},{13,9},{2,6},{6,2},{1... | collective-permute-start | bytes 362504 | tf_op jit(solution)/shard_map/ppermute | solution.py:343
  36.1 6.8 %collective-permute-start.9 = (bf16[8,7552]{1,0:T(8,128)(2,1)S(1)}, bf16[8,7552]{1,0:T(8,128)(2,1)S(1)}, u32[]{:S(2)}, u32[]{:S(2)}) collective-permute-start(bf16[8,7552]{1,0:T(8,128)(2,1)S(1)} %shard_map.51.refs_0_), channel_id=1, source_target_pairs={{0,8},{12,4},{1,9},{13,5},{2,10},{14,6},{3,11},{15,7},{16,24},{28,... | collective-permute-start | bytes 362504 | tf_op jit(solution)/shard_map/ppermute | solution.py:339
  37.7 8.1 %collective-permute-start.7 = (bf16[8,7552]{1,0:T(8,128)(2,1)S(1)}, bf16[8,7552]{1,0:T(8,128)(2,1)S(1)}, u32[]{:S(2)}, u32[]{:S(2)}) collective-permute-start(bf16[8,7552]{1,0:T(8,128)(2,1)S(1)} %shard_map.51.refs_0_), channel_id=1, source_target_pairs={{4,12},{8,0},{5,13},{9,1},{6,14},{10,2},{7,15},{11,3},{20,28},{24,... | collective-permute-start | bytes 362504 | tf_op jit(solution)/shard_map/ppermute | solution.py:339
  39.0 9.9 %collective-permute-start.11 = (bf16[8,7552]{1,0:T(8,128)(2,1)S(1)}, bf16[8,7552]{1,0:T(8,128)(2,1)S(1)}, u32[]{:S(2)}, u32[]{:S(2)}) collective-permute-start(bf16[8,7552]{1,0:T(8,128)(2,1)S(1)} %shard_map.51.refs_0_), channel_id=1, source_target_pairs={{0,4},{4,0},{8,12},{12,8},{1,5},{5,1},{9,13},{13,9},{2,6},{6,2},{1... | collective-permute-start | bytes 362504 | tf_op jit(solution)/shard_map/ppermute | solution.py:343
  42.9 9.7 %collective-permute-start.10 = (bf16[8,7552]{1,0:T(8,128)(2,1)S(1)}, bf16[8,7552]{1,0:T(8,128)(2,1)S(1)}, u32[]{:S(2)}, u32[]{:S(2)}) collective-permute-start(bf16[8,7552]{1,0:T(8,128)(2,1)S(1)} %collective-permute-done.9.refs_3_), channel_id=1, source_target_pairs={{4,0},{8,12},{5,1},{9,13},{6,2},{10,14},{7,3},{11,15},{20,16},{24,... | collective-permute-start | bytes 362504 | tf_op jit(solution)/shard_map/ppermute | solution.py:339
  45.8 6.8 %collective-permute-start.8 = (bf16[8,7552]{1,0:T(8,128)(2,1)S(1)}, bf16[8,7552]{1,0:T(8,128)(2,1)S(1)}, u32[]{:S(2)}, u32[]{:S(2)}) collective-permute-start(bf16[8,7552]{1,0:T(8,128)(2,1)S(1)} %collective-permute-done.7.refs_2_), channel_id=1, source_target_pairs={{0,4},{12,8},{1,5},{13,9},{2,6},{14,10},{3,7},{15,11},{16,20},{28,... | collective-permute-start | bytes 362504 | tf_op jit(solution)/shard_map/ppermute | solution.py:339
  53.9 1.9 %collective-permute-start.12 = (bf16[8,2304]{1,0:T(8,128)(2,1)S(1)}, bf16[8,2304]{1,0:T(8,128)(2,1)S(1)}, u32[]{:S(2)}, u32[]{:S(2)}) collective-permute-start(bf16[8,2304]{1,0:T(8,128)(2,1)S(1)} %get-tuple-element.14), channel_id=1, source_target_pairs={{0,1},{1,0},{2,3},{3,2},{4,5},{5,4},{6,7},{7,6},{8,9},{9,8},{10,11... | collective-permute-start | bytes 110600 | tf_op jit(solution)/shard_map/ppermute | solution.py:343
  54.0 4.0 %collective-permute-start.13 = (bf16[8,2304]{1,0:T(8,128)(2,1)S(1)}, bf16[8,2304]{1,0:T(8,128)(2,1)S(1)}, u32[]{:S(2)}, u32[]{:S(2)}) collective-permute-start(bf16[8,2304]{1,0:T(8,128)(2,1)S(1)} %get-tuple-element.15), channel_id=1, source_target_pairs={{0,2},{1,3},{2,0},{3,1},{4,6},{5,7},{6,4},{7,5},{8,10},{9,11},{10,... | collective-permute-start | bytes 110600 | tf_op jit(solution)/shard_map/ppermute | solution.py:343
  55.6 3.4 %collective-permute-start.14 = (bf16[8,2304]{1,0:T(8,128)(2,1)S(1)}, bf16[8,2304]{1,0:T(8,128)(2,1)S(1)}, u32[]{:S(2)}, u32[]{:S(2)}) collective-permute-start(bf16[8,2304]{1,0:T(8,128)(2,1)S(1)} %get-tuple-element.16), channel_id=1, source_target_pairs={{0,3},{1,2},{2,1},{3,0},{4,7},{5,6},{6,5},{7,4},{8,11},{9,10},{10,... | collective-permute-start | bytes 110600 | tf_op jit(solution)/shard_map/ppermute | solution.py:343

commit v21 on v14

--- a/solution.py
+++ b/solution.py
@@ -11,6 +11,7 @@
 STEP = 256
 COPY_STEP = 512
 IN_FLIGHT = 6
+DOWN_STEP = 512
 TOKEN_AXES = ("gy", "gz")
 IN_HBM = pl.BlockSpec(memory_space=pltpu.HBM)
 ANY = pl.BlockSpec(memory_space=pl.ANY)
@@ -272,7 +273,7 @@
             tail = hidden[b][:, at : at + half].astype(jnp.float32)
             plain[rows - 4 :, :half] = tail[:4]
             plain[rows - 4 :, half:] = tail[4:, : width - half]
-        for row, tall in pieces_of(width, STEP):
+        for row, tall in pieces_of(width, DOWN_STEP):
             term = jnp.dot(
                 plain[:, row : row + tall].astype(jnp.bfloat16),
                 held[pl.ds(pl.multiple_of(block_start(distances[b], width) + row, 128), tall), :],
@@ -344,7 +345,7 @@
     n_token = lax.axis_size(TOKEN_AXES)
     width = gate_weight.shape[1] // n_gx
 
-    held = fetch(gate_weight, up_weight, 3, width)
+    held = fetch(gate_weight, up_weight, 2, width)
     features = jnp.concatenate(
         [tokens] + [swap(tokens, TOKEN_AXES, n_token, r) for r in range(1, n_token)], axis=0
     )
@@ -355,20 +356,20 @@
 
     relayed = gate_up_held(features, held)
     arrived = swap(relayed, "gx", n_gx, 1)
-    across, beside = blocks_for((2, 1), ((0, 1), (0,)), relayed)
+    across, beside = blocks_for((3, 1), ((0, 1), (0,)), relayed)
     across = lax.optimization_barrier(add(across, arrived).astype(jnp.bfloat16))
-    far = swap(across, "gx", n_gx, 2)
+    far = swap(across, "gx", n_gx, 3)
     near = [swap(beside, "gx", n_gx, 1)]
     (beside,) = blocks_for((1,), ((1,),), across)
     near.append(swap(beside, "gx", n_gx, 1))
     (own,) = blocks_for((0,), ((0, 1),), beside)
     hidden = activate_packed(own, far, near, rows, width)
 
-    opposite = swap(hidden, "gx", n_gx, 2)
+    opposite = swap(hidden, "gx", n_gx, 3)
     first = [hidden, swap(hidden, "gx", n_gx, 1), opposite]
     second = [swap(opposite, "gx", n_gx, 1)]
-    (partial_sum,) = down(first, (0, 1, 2), None, down_weight, rows, width, 1)
-    outs = down(second, (3,), partial_sum, down_weight, rows, width, n_token)
+    (partial_sum,) = down(first, (0, 1, 3), None, down_weight, rows, width, 1)
+    outs = down(second, (2,), partial_sum, down_weight, rows, width, n_token)
     terms = [outs[0]] + [swap(outs[r], TOKEN_AXES, n_token, r) for r in range(1, n_token)]
     return finish(terms, tokens.shape)
 

time: 55.1 us -> 55.2 us (level)
  transfers between devices with their start and end apart: 13 -> 13, of which waited for: 6 -> 6; matrix products, arithmetic and copies ran while one was open for 0% -> 0% of each run, Pallas kernels for 48% -> 47%
where the time goes in v21:
time: 55.2 us; the launch traced here: 55.1 us
  Pallas kernels  30.4 us (55%)
  starting transfers between devices  13.5 us (24%)
  waiting for transfers between devices  10.9 us (20%)
    pallas_call x3, Pallas kernels, gate_up_stream(): pl.pallas_call(functools.partial(stream_kernel, width, blocks, distances)...  17.5 us
    ppermute x13, starting transfers between devices, swap(): return lax.ppermute(value, axes, [(i, i ^ distance) for i in range(size)])  13.5 us
    ppermute x13, waiting for transfers between devices, swap(): return lax.ppermute(value, axes, [(i, i ^ distance) for i in range(size)])  10.9 us
    pallas_call x1, Pallas kernels, fetch(): pl.pallas_call(functools.partial(fetch_kernel, width, distance), out_shap...  5.03 us
    pallas_call x2, Pallas kernels, down(): pl.pallas_call(functools.partial(down_kernel, before is None, rows, width...  4.91 us
    pallas_call x1, Pallas kernels, gate_up_held(): pl.pallas_call(held_kernel, out_shape=jax.ShapeDtypeStruct((8, packed_pai...  2.15 us
  transfers between devices with their start and end apart: 13, of which 6 were waited for; matrix products, arithmetic and copies ran while one was open for 0% of the time, Pallas kernels for 47%

profile of v21, /device:TPU:0, one launch (start us, length us, event | category | flops | bytes accessed | tf_op | source)
XLA Modules:
  0.0 55.1 jit_solution(7419507760644913923)
XLA Ops:
  0.0 0.0 copy-start
  0.0 2.9 %collective-permute-start.1 = (bf16[9,2048]{1,0:T(8,128)(2,1)}, bf16[9,2048]{1,0:T(8,128)(2,1)S(1)}, u32[]{:S(2)}, u32[]{:S(2)}) collective-permute-start(bf16[9,2048]{1,0:T(8,128)(2,1)} %param.4), channel_id=1, source_target_pairs={{0,2},{1,3},{2,0},{3,1},{4,6},{5,7},{6,4},{7,5},{8,10},{9,11},{10,... | collective-permute-start | bytes 110600 | tf_op jit(solution)/shard_map/ppermute | solution.py:336
  2.9 0.0 collective-permute-start
  2.9 0.2 collective-permute-start.2
  3.1 5.0 %shard_map.46.held = bf16[2,2048,1664]{2,1,0:T(8,128)(2,1)S(1)} custom-call(bf16[2048,6656]{1,0:T(8,128)(2,1)} %gate_ref.7, bf16[2048,6656]{1,0:T(8,128)(2,1)} %up_ref.7), custom_call_target="tpu_custom_call" | custom-call | bytes 1048576 | tf_op jit(solution)/shard_map/pallas_call | solution.py:86
  8.2 0.0 collective-permute-done.1
  8.2 0.0 collective-permute-done
  8.2 0.0 collective-permute-done.2
  8.2 0.0 copy-done
  8.2 0.1 pad_maximum_fusion.x_ref
  8.3 2.2 %shard_map.47._ = bf16[8,14976]{1,0:T(8,128)(2,1)S(1)} custom-call(bf16[36,2048]{1,0:T(8,128)(2,1)S(1)} %pad_maximum_fusion.x_ref, bf16[2,2048,1664]{2,1,0:T(8,128)(2,1)S(1)} %shard_map.46.held), custom_call_target="tpu_custom_call" | custom-call | bytes 1048576 | tf_op jit(solution)/shard_map/pallas_call | solution.py:120
  10.5 2.2 %collective-permute-start.3 = (bf16[8,14976]{1,0:T(8,128)(2,1)S(1)}, bf16[8,14976]{1,0:T(8,128)(2,1)S(1)}, u32[]{:S(2)}, u32[]{:S(2)}) collective-permute-start(bf16[8,14976]{1,0:T(8,128)(2,1)S(1)} %shard_map.47._), channel_id=1, source_target_pairs={{0,4},{4,0},{8,12},{12,8},{1,5},{5,1},{9,13},{13,9},{2,6},{6,2},{1... | collective-permute-start | bytes 718856 | tf_op jit(solution)/shard_map/ppermute | solution.py:336
  12.7 7.6 %shard_map.48 = (bf16[8,14976]{1,0:T(8,128)(2,1)S(1)}, bf16[8,7552]{1,0:T(8,128)(2,1)S(1)}) custom-call(bf16[36,2048]{1,0:T(8,128)(2,1)S(1)} %pad_maximum_fusion.x_ref, bf16[2048,6656]{1,0:T(8,128)(2,1)} %gate_ref.7, bf16[2048,6656]{1,0:T(8,128)(2,1)} %up_ref.7, bf16[8,14976]{1,0:T(8,128)(2,1)S(1)} %shard_map.47._), custom_call_target="tpu_custom_call" | custom-call | bytes 1048576 | tf_op jit(solution)/shard_map/pallas_call | solution.py:164
  20.3 0.0 collective-permute-done.3
  20.3 0.1 add_convert_fusion._
  20.4 2.4 %collective-permute-start.4 = (bf16[8,14976]{1,0:T(8,128)(2,1)S(1)}, bf16[8,14976]{1,0:T(8,128)(2,1)S(1)}, u32[]{:S(2)}, u32[]{:S(2)}) collective-permute-start(bf16[8,14976]{1,0:T(8,128)(2,1)S(1)} %add_convert_fusion._), channel_id=1, source_target_pairs={{0,12},{4,8},{8,4},{12,0},{1,13},{5,9},{9,5},{13,1},{2,14},{6,10},... | collective-permute-start | bytes 718856 | tf_op jit(solution)/shard_map/ppermute | solution.py:336
  22.8 0.6 %collective-permute-start.5 = (bf16[8,7552]{1,0:T(8,128)(2,1)S(1)}, bf16[8,7552]{1,0:T(8,128)(2,1)S(1)}, u32[]{:S(2)}, u32[]{:S(2)}) collective-permute-start(bf16[8,7552]{1,0:T(8,128)(2,1)S(1)} %get-tuple-element.12), channel_id=1, source_target_pairs={{0,4},{4,0},{8,12},{12,8},{1,5},{5,1},{9,13},{13,9},{2,6},{6,2},{1... | collective-permute-start | bytes 362504 | tf_op jit(solution)/shard_map/ppermute | solution.py:336
  23.5 0.0 slice-start
  23.5 0.0 slice-start.1
  23.5 0.0 slice-start.2
  23.5 0.0 slice-start.3
  23.5 3.6 %shard_map.49._ = bf16[8,7552]{1,0:T(8,128)(2,1)S(1)} custom-call(bf16[36,2048]{1,0:T(8,128)(2,1)S(1)} %pad_maximum_fusion.x_ref, bf16[2048,6656]{1,0:T(8,128)(2,1)} %gate_ref.7, bf16[2048,6656]{1,0:T(8,128)(2,1)} %up_ref.7, bf16[8,14976]{1,0:T(8,128)(2,1)S(1)} %add_convert_fusion._), custom_call_target="tpu_custom_call" | custom-call | bytes 1048576 | tf_op jit(solution)/shard_map/pallas_call | solution.py:164
  27.1 0.0 slice-start.4
  27.1 0.0 slice-start.5
  27.1 0.0 slice-start.6
  27.1 1.5 %collective-permute-start.6 = (bf16[8,7552]{1,0:T(8,128)(2,1)S(1)}, bf16[8,7552]{1,0:T(8,128)(2,1)S(1)}, u32[]{:S(2)}, u32[]{:S(2)}) collective-permute-start(bf16[8,7552]{1,0:T(8,128)(2,1)S(1)} %shard_map.49._), channel_id=1, source_target_pairs={{0,4},{4,0},{8,12},{12,8},{1,5},{5,1},{9,13},{13,9},{2,6},{6,2},{1... | collective-permute-start | bytes 362504 | tf_op jit(solution)/shard_map/ppermute | solution.py:336
  28.6 6.2 %shard_map.50.own = bf16[8,14976]{1,0:T(8,128)(2,1)S(1)} custom-call(bf16[36,2048]{1,0:T(8,128)(2,1)S(1)} %pad_maximum_fusion.x_ref, bf16[2048,6656]{1,0:T(8,128)(2,1)} %gate_ref.7, bf16[2048,6656]{1,0:T(8,128)(2,1)} %up_ref.7, bf16[8,7552]{1,0:T(8,128)(2,1)S(1)} %shard_map.49._), custom_call_target="tpu_custom_call" | custom-call | bytes 1048576 | tf_op jit(solution)/shard_map/pallas_call | solution.py:164
  34.8 0.0 collective-permute-done.5.gate_near
  34.8 0.2 collective-permute-done.6.up_near
  35.0 0.0 collective-permute-done.4.far
  35.0 0.1 shard_map.51.refs_0_
  35.1 1.7 %collective-permute-start.7 = (bf16[8,7552]{1,0:T(8,128)(2,1)S(1)}, bf16[8,7552]{1,0:T(8,128)(2,1)S(1)}, u32[]{:S(2)}, u32[]{:S(2)}) collective-permute-start(bf16[8,7552]{1,0:T(8,128)(2,1)S(1)} %shard_map.51.refs_0_), channel_id=1, source_target_pairs={{0,12},{4,8},{8,4},{12,0},{1,13},{5,9},{9,5},{13,1},{2,14},{6,10},... | collective-permute-start | bytes 362504 | tf_op jit(solution)/shard_map/ppermute | solution.py:336
  36.9 0.0 collective-permute-start.9
  36.9 6.3 %collective-permute-done.7.refs_2_ = bf16[8,7552]{1,0:T(8,128)(2,1)S(1)} collective-permute-done((bf16[8,7552]{1,0:T(8,128)(2,1)S(1)}, bf16[8,7552]{1,0:T(8,128)(2,1)S(1)}, u32[]{:S(2)}, u32[]{:S(2)}) %collective-permute-start.7) | collective-permute-done | bytes 120864 | tf_op jit(solution)/shard_map/ppermute | solution.py:336
  43.2 0.0 collective-permute-start.8
  43.2 0.4 collective-permute-done.9.refs_1_
  43.6 0.0 slice-done
  43.6 0.0 slice-done.1
  43.7 0.0 slice-done.2
  43.7 0.0 slice-done.3
  43.7 0.0 slice-done.4
  43.7 0.0 slice-done.5
  43.7 0.0 slice-done.6
  43.7 3.6 %shard_map.52.refs_1_ = f32[36,2048]{1,0:T(8,128)S(1)} custom-call(bf16[8,7552]{1,0:T(8,128)(2,1)S(1)} %shard_map.51.refs_0_, bf16[8,7552]{1,0:T(8,128)(2,1)S(1)} %collective-permute-done.9.refs_1_, bf16[8,7552]{1,0:T(8,128)(2,1)S(1)} %collective-permute-done.7.refs_2_, bf16[6656,2048]{1,0:T(8,128)(2,1)S(1)} %bitcast.1), custom_call_target="tpu_custom_call" | custom-call | bytes 1048576 | tf_op jit(solution)/shard_map/pallas_call | solution.py:300
  47.3 0.7 %collective-permute-done.8.refs_0_ = bf16[8,7552]{1,0:T(8,128)(2,1)S(1)} collective-permute-done((bf16[8,7552]{1,0:T(8,128)(2,1)S(1)}, bf16[8,7552]{1,0:T(8,128)(2,1)S(1)}, u32[]{:S(2)}, u32[]{:S(2)}) %collective-permute-start.8) | collective-permute-done | bytes 120864 | tf_op jit(solution)/shard_map/ppermute | solution.py:336
  48.1 1.3 %shard_map.53 = (f32[8,2304]{1,0:T(8,128)S(1)}, bf16[8,2304]{1,0:T(8,128)(2,1)S(1)}, bf16[8,2304]{1,0:T(8,128)(2,1)S(1)}, bf16[8,2304]{1,0:T(8,128)(2,1)S(1)}) custom-call(bf16[8,7552]{1,0:T(8,128)(2,1)S(1)} %collective-permute-done.8.refs_0_, f32[36,2048]{1,0:T(8,128)S(1)} %shard_map.52.refs_1_, bf16[6656,2048]{1,0:T(8,128)(2,1)S(1)} %bitcast.1), custom_call_target="tpu_custom_call" | custom-call | bytes 1048576 | tf_op jit(solution)/shard_map/pallas_call | solution.py:300
  49.4 0.1 collective-permute-start.10
  49.4 1.6 %collective-permute-start.11 = (bf16[8,2304]{1,0:T(8,128)(2,1)S(1)}, bf16[8,2304]{1,0:T(8,128)(2,1)S(1)}, u32[]{:S(2)}, u32[]{:S(2)}) collective-permute-start(bf16[8,2304]{1,0:T(8,128)(2,1)S(1)} %get-tuple-element.15), channel_id=1, source_target_pairs={{0,2},{1,3},{2,0},{3,1},{4,6},{5,7},{6,4},{7,5},{8,10},{9,11},{10,... | collective-permute-start | bytes 110600 | tf_op jit(solution)/shard_map/ppermute | solution.py:336
  51.0 0.3 collective-permute-start.12
  51.3 0.0 collective-permute-done.10.refs_1_
  51.3 2.2 %collective-permute-done.11.refs_2_ = bf16[8,2304]{1,0:T(8,128)(2,1)S(1)} collective-permute-done((bf16[8,2304]{1,0:T(8,128)(2,1)S(1)}, bf16[8,2304]{1,0:T(8,128)(2,1)S(1)}, u32[]{:S(2)}, u32[]{:S(2)}) %collective-permute-start.11) | collective-permute-done | bytes 36896 | tf_op jit(solution)/shard_map/ppermute | solution.py:336
  53.5 1.0 %collective-permute-done.12.refs_3_ = bf16[8,2304]{1,0:T(8,128)(2,1)S(1)} collective-permute-done((bf16[8,2304]{1,0:T(8,128)(2,1)S(1)}, bf16[8,2304]{1,0:T(8,128)(2,1)S(1)}, u32[]{:S(2)}, u32[]{:S(2)}) %collective-permute-start.12) | collective-permute-done | bytes 36896 | tf_op jit(solution)/shard_map/ppermute | solution.py:336
  54.4 0.7 %shard_map.54 = bf16[9,2048]{1,0:T(8,128)(2,1)} custom-call(f32[8,2304]{1,0:T(8,128)S(1)} %get-tuple-element.13.refs_0_, bf16[8,2304]{1,0:T(8,128)(2,1)S(1)} %collective-permute-done.10.refs_1_, bf16[8,2304]{1,0:T(8,128)(2,1)S(1)} %collective-permute-done.11.refs_2_, bf16[8,2304]{1,0:T(8,128)(2,1)S(1)} %collective-permute-done.12.refs_3_), custom_call_target="tpu_custom_call" | custom-call | bytes 1048576 | tf_op jit(solution)/shard_map/pallas_call | solution.py:324
  (1 shorter events, 0.0 us)
Async XLA Ops:
  0.0 8.2 %copy-start = (bf16[9,2048]{1,0:T(8,128)(2,1)S(1)}, bf16[9,2048]{1,0:T(8,128)(2,1)}, u32[]{:S(2)}) copy-start(bf16[9,2048]{1,0:T(8,128)(2,1)} %param.4) | copy-start | bytes 110596
  0.0 8.2 %collective-permute-start.1 = (bf16[9,2048]{1,0:T(8,128)(2,1)}, bf16[9,2048]{1,0:T(8,128)(2,1)S(1)}, u32[]{:S(2)}, u32[]{:S(2)}) collective-permute-start(bf16[9,2048]{1,0:T(8,128)(2,1)} %param.4), channel_id=1, source_target_pairs={{0,2},{1,3},{2,0},{3,1},{4,6},{5,7},{6,4},{7,5},{8,10},{9,11},{10,... | collective-permute-start | bytes 110600 | tf_op jit(solution)/shard_map/ppermute | solution.py:336
  2.9 5.2 %collective-permute-start = (bf16[9,2048]{1,0:T(8,128)(2,1)}, bf16[9,2048]{1,0:T(8,128)(2,1)S(1)}, u32[]{:S(2)}, u32[]{:S(2)}) collective-permute-start(bf16[9,2048]{1,0:T(8,128)(2,1)} %param.4), channel_id=1, source_target_pairs={{0,1},{1,0},{2,3},{3,2},{4,5},{5,4},{6,7},{7,6},{8,9},{9,8},{10,11... | collective-permute-start | bytes 110600 | tf_op jit(solution)/shard_map/ppermute | solution.py:336
  2.9 5.3 %collective-permute-start.2 = (bf16[9,2048]{1,0:T(8,128)(2,1)}, bf16[9,2048]{1,0:T(8,128)(2,1)S(1)}, u32[]{:S(2)}, u32[]{:S(2)}) collective-permute-start(bf16[9,2048]{1,0:T(8,128)(2,1)} %param.4), channel_id=1, source_target_pairs={{0,3},{1,2},{2,1},{3,0},{4,7},{5,6},{6,5},{7,4},{8,11},{9,10},{10,... | collective-permute-start | bytes 110600 | tf_op jit(solution)/shard_map/ppermute | solution.py:336
  10.5 9.9 %collective-permute-start.3 = (bf16[8,14976]{1,0:T(8,128)(2,1)S(1)}, bf16[8,14976]{1,0:T(8,128)(2,1)S(1)}, u32[]{:S(2)}, u32[]{:S(2)}) collective-permute-start(bf16[8,14976]{1,0:T(8,128)(2,1)S(1)} %shard_map.47._), channel_id=1, source_target_pairs={{0,4},{4,0},{8,12},{12,8},{1,5},{5,1},{9,13},{13,9},{2,6},{6,2},{1... | collective-permute-start | bytes 718856 | tf_op jit(solution)/shard_map/ppermute | solution.py:336
  20.4 14.6 %collective-permute-start.4 = (bf16[8,14976]{1,0:T(8,128)(2,1)S(1)}, bf16[8,14976]{1,0:T(8,128)(2,1)S(1)}, u32[]{:S(2)}, u32[]{:S(2)}) collective-permute-start(bf16[8,14976]{1,0:T(8,128)(2,1)S(1)} %add_convert_fusion._), channel_id=1, source_target_pairs={{0,12},{4,8},{8,4},{12,0},{1,13},{5,9},{9,5},{13,1},{2,14},{6,10},... | collective-permute-start | bytes 718856 | tf_op jit(solution)/shard_map/ppermute | solution.py:336
  22.8 12.0 %collective-permute-start.5 = (bf16[8,7552]{1,0:T(8,128)(2,1)S(1)}, bf16[8,7552]{1,0:T(8,128)(2,1)S(1)}, u32[]{:S(2)}, u32[]{:S(2)}) collective-permute-start(bf16[8,7552]{1,0:T(8,128)(2,1)S(1)} %get-tuple-element.12), channel_id=1, source_target_pairs={{0,4},{4,0},{8,12},{12,8},{1,5},{5,1},{9,13},{13,9},{2,6},{6,2},{1... | collective-permute-start | bytes 362504 | tf_op jit(solution)/shard_map/ppermute | solution.py:336
  23.5 20.2 %slice-start = ((s8[27262976]{0:T(1024)(128)(4,1)}), s8[4194304]{0:T(1024)(128)(4,1)S(1)}, s32[]{:S(2)}) async-start(s8[27262976]{0:T(1024)(128)(4,1)} %bitcast), calls=%async_computation | async-start | bytes 8388608
  23.5 20.2 %slice-start.1 = ((s8[27262976]{0:T(1024)(128)(4,1)}), s8[4194304]{0:T(1024)(128)(4,1)S(1)}, s32[]{:S(2)}) async-start(s8[27262976]{0:T(1024)(128)(4,1)} %bitcast), calls=%async_computation.1 | async-start | bytes 8388608
  23.5 20.2 %slice-start.2 = ((s8[27262976]{0:T(1024)(128)(4,1)}), s8[4194304]{0:T(1024)(128)(4,1)S(1)}, s32[]{:S(2)}) async-start(s8[27262976]{0:T(1024)(128)(4,1)} %bitcast), calls=%async_computation.2 | async-start | bytes 8388608
  23.5 20.2 %slice-start.3 = ((s8[27262976]{0:T(1024)(128)(4,1)}), s8[4194304]{0:T(1024)(128)(4,1)S(1)}, s32[]{:S(2)}) async-start(s8[27262976]{0:T(1024)(128)(4,1)} %bitcast), calls=%async_computation.3 | async-start | bytes 8388608
  27.1 16.6 %slice-start.4 = ((s8[27262976]{0:T(1024)(128)(4,1)}), s8[4194304]{0:T(1024)(128)(4,1)S(1)}, s32[]{:S(2)}) async-start(s8[27262976]{0:T(1024)(128)(4,1)} %bitcast), calls=%async_computation.4 | async-start | bytes 8388608
  27.1 16.6 %slice-start.5 = ((s8[27262976]{0:T(1024)(128)(4,1)}), s8[4194304]{0:T(1024)(128)(4,1)S(1)}, s32[]{:S(2)}) async-start(s8[27262976]{0:T(1024)(128)(4,1)} %bitcast), calls=%async_computation.5 | async-start | bytes 8388608
  27.1 16.6 %slice-start.6 = ((s8[27262976]{0:T(1024)(128)(4,1)}), s8[2097152]{0:T(1024)(128)(4,1)S(1)}, s32[]{:S(2)}) async-start(s8[27262976]{0:T(1024)(128)(4,1)} %bitcast), calls=%async_computation.6 | async-start | bytes 4194304
  27.1 7.9 %collective-permute-start.6 = (bf16[8,7552]{1,0:T(8,128)(2,1)S(1)}, bf16[8,7552]{1,0:T(8,128)(2,1)S(1)}, u32[]{:S(2)}, u32[]{:S(2)}) collective-permute-start(bf16[8,7552]{1,0:T(8,128)(2,1)S(1)} %shard_map.49._), channel_id=1, source_target_pairs={{0,4},{4,0},{8,12},{12,8},{1,5},{5,1},{9,13},{13,9},{2,6},{6,2},{1... | collective-permute-start | bytes 362504 | tf_op jit(solution)/shard_map/ppermute | solution.py:336
  35.1 8.0 %collective-permute-start.7 = (bf16[8,7552]{1,0:T(8,128)(2,1)S(1)}, bf16[8,7552]{1,0:T(8,128)(2,1)S(1)}, u32[]{:S(2)}, u32[]{:S(2)}) collective-permute-start(bf16[8,7552]{1,0:T(8,128)(2,1)S(1)} %shard_map.51.refs_0_), channel_id=1, source_target_pairs={{0,12},{4,8},{8,4},{12,0},{1,13},{5,9},{9,5},{13,1},{2,14},{6,10},... | collective-permute-start | bytes 362504 | tf_op jit(solution)/shard_map/ppermute | solution.py:336
  36.9 6.8 %collective-permute-start.9 = (bf16[8,7552]{1,0:T(8,128)(2,1)S(1)}, bf16[8,7552]{1,0:T(8,128)(2,1)S(1)}, u32[]{:S(2)}, u32[]{:S(2)}) collective-permute-start(bf16[8,7552]{1,0:T(8,128)(2,1)S(1)} %shard_map.51.refs_0_), channel_id=1, source_target_pairs={{0,4},{4,0},{8,12},{12,8},{1,5},{5,1},{9,13},{13,9},{2,6},{6,2},{1... | collective-permute-start | bytes 362504 | tf_op jit(solution)/shard_map/ppermute | solution.py:336
  43.2 4.9 %collective-permute-start.8 = (bf16[8,7552]{1,0:T(8,128)(2,1)S(1)}, bf16[8,7552]{1,0:T(8,128)(2,1)S(1)}, u32[]{:S(2)}, u32[]{:S(2)}) collective-permute-start(bf16[8,7552]{1,0:T(8,128)(2,1)S(1)} %collective-permute-done.7.refs_2_), channel_id=1, source_target_pairs={{0,4},{4,0},{8,12},{12,8},{1,5},{5,1},{9,13},{13,9},{2,6},{6,2},{1... | collective-permute-start | bytes 362504 | tf_op jit(solution)/shard_map/ppermute | solution.py:336
  49.4 1.9 %collective-permute-start.10 = (bf16[8,2304]{1,0:T(8,128)(2,1)S(1)}, bf16[8,2304]{1,0:T(8,128)(2,1)S(1)}, u32[]{:S(2)}, u32[]{:S(2)}) collective-permute-start(bf16[8,2304]{1,0:T(8,128)(2,1)S(1)} %get-tuple-element.14), channel_id=1, source_target_pairs={{0,1},{1,0},{2,3},{3,2},{4,5},{5,4},{6,7},{7,6},{8,9},{9,8},{10,11... | collective-permute-start | bytes 110600 | tf_op jit(solution)/shard_map/ppermute | solution.py:336
  49.4 4.0 %collective-permute-start.11 = (bf16[8,2304]{1,0:T(8,128)(2,1)S(1)}, bf16[8,2304]{1,0:T(8,128)(2,1)S(1)}, u32[]{:S(2)}, u32[]{:S(2)}) collective-permute-start(bf16[8,2304]{1,0:T(8,128)(2,1)S(1)} %get-tuple-element.15), channel_id=1, source_target_pairs={{0,2},{1,3},{2,0},{3,1},{4,6},{5,7},{6,4},{7,5},{8,10},{9,11},{10,... | collective-permute-start | bytes 110600 | tf_op jit(solution)/shard_map/ppermute | solution.py:336
  51.0 3.4 %collective-permute-start.12 = (bf16[8,2304]{1,0:T(8,128)(2,1)S(1)}, bf16[8,2304]{1,0:T(8,128)(2,1)S(1)}, u32[]{:S(2)}, u32[]{:S(2)}) collective-permute-start(bf16[8,2304]{1,0:T(8,128)(2,1)S(1)} %get-tuple-element.16), channel_id=1, source_target_pairs={{0,3},{1,2},{2,1},{3,0},{4,7},{5,6},{6,5},{7,4},{8,11},{9,10},{10,... | collective-permute-start | bytes 110600 | tf_op jit(solution)/shard_map/ppermute | solution.py:336

commit v22 on v21

--- a/solution.py
+++ b/solution.py
@@ -365,11 +365,11 @@
     (own,) = blocks_for((0,), ((0, 1),), beside)
     hidden = activate_packed(own, far, near, rows, width)
 
-    opposite = swap(hidden, "gx", n_gx, 3)
+    opposite = swap(hidden, "gx", n_gx, 2)
     first = [hidden, swap(hidden, "gx", n_gx, 1), opposite]
     second = [swap(opposite, "gx", n_gx, 1)]
-    (partial_sum,) = down(first, (0, 1, 3), None, down_weight, rows, width, 1)
-    outs = down(second, (2,), partial_sum, down_weight, rows, width, n_token)
+    (partial_sum,) = down(first, (0, 1, 2), None, down_weight, rows, width, 1)
+    outs = down(second, (3,), partial_sum, down_weight, rows, width, n_token)
     terms = [outs[0]] + [swap(outs[r], TOKEN_AXES, n_token, r) for r in range(1, n_token)]
     return finish(terms, tokens.shape)
 

time: 55.2 us -> 55 us (level)
  waiting for transfers between devices: 10.9 us -> 10 us
  starting transfers between devices: 13.5 us -> 14.1 us
    ppermute x13, waiting for transfers between devices: 10.9 us -> 10 us  [swap(): return lax.ppermute(value, axes, [(i, i ^ distance) for i in range(size)])]
    ppermute x13, starting transfers between devices: 13.5 us -> 14.1 us  [swap(): return lax.ppermute(value, axes, [(i, i ^ distance) for i in range(size)])]
  transfers between devices with their start and end apart: 13 -> 13, of which waited for: 6 -> 6; matrix products, arithmetic and copies ran while one was open for 0% -> 0% of each run, Pallas kernels for 47% -> 48%
where the time goes in v22:
time: 55 us; the launch traced here: 54.8 us
  Pallas kernels  30.4 us (55%)
  starting transfers between devices  14.1 us (26%)
  waiting for transfers between devices  10 us (18%)
    pallas_call x3, Pallas kernels, gate_up_stream(): pl.pallas_call(functools.partial(stream_kernel, width, blocks, distances)...  17.5 us
    ppermute x13, starting transfers between devices, swap(): return lax.ppermute(value, axes, [(i, i ^ distance) for i in range(size)])  14.1 us
    ppermute x13, waiting for transfers between devices, swap(): return lax.ppermute(value, axes, [(i, i ^ distance) for i in range(size)])  10 us
    pallas_call x1, Pallas kernels, fetch(): pl.pallas_call(functools.partial(fetch_kernel, width, distance), out_shap...  5.03 us
    pallas_call x2, Pallas kernels, down(): pl.pallas_call(functools.partial(down_kernel, before is None, rows, width...  4.92 us
    pallas_call x1, Pallas kernels, gate_up_held(): pl.pallas_call(held_kernel, out_shape=jax.ShapeDtypeStruct((8, packed_pai...  2.15 us
  transfers between devices with their start and end apart: 13, of which 6 were waited for; matrix products, arithmetic and copies ran while one was open for 0% of the time, Pallas kernels for 48%

profile of v22, /device:TPU:0, one launch (start us, length us, event | category | flops | bytes accessed | tf_op | source)
XLA Modules:
  0.0 54.8 jit_solution(12599887353078834206)
XLA Ops:
  0.0 0.0 copy-start
  0.0 2.9 %collective-permute-start.1 = (bf16[9,2048]{1,0:T(8,128)(2,1)}, bf16[9,2048]{1,0:T(8,128)(2,1)S(1)}, u32[]{:S(2)}, u32[]{:S(2)}) collective-permute-start(bf16[9,2048]{1,0:T(8,128)(2,1)} %param.4), channel_id=1, source_target_pairs={{0,2},{1,3},{2,0},{3,1},{4,6},{5,7},{6,4},{7,5},{8,10},{9,11},{10,... | collective-permute-start | bytes 110600 | tf_op jit(solution)/shard_map/ppermute | solution.py:336
  2.9 0.0 collective-permute-start
  2.9 0.2 collective-permute-start.2
  3.1 5.0 %shard_map.46.held = bf16[2,2048,1664]{2,1,0:T(8,128)(2,1)S(1)} custom-call(bf16[2048,6656]{1,0:T(8,128)(2,1)} %gate_ref.7, bf16[2048,6656]{1,0:T(8,128)(2,1)} %up_ref.7), custom_call_target="tpu_custom_call" | custom-call | bytes 1048576 | tf_op jit(solution)/shard_map/pallas_call | solution.py:86
  8.2 0.0 collective-permute-done.1
  8.2 0.0 collective-permute-done
  8.2 0.0 collective-permute-done.2
  8.2 0.0 copy-done
  8.2 0.1 pad_maximum_fusion.x_ref
  8.3 2.2 %shard_map.47._ = bf16[8,14976]{1,0:T(8,128)(2,1)S(1)} custom-call(bf16[36,2048]{1,0:T(8,128)(2,1)S(1)} %pad_maximum_fusion.x_ref, bf16[2,2048,1664]{2,1,0:T(8,128)(2,1)S(1)} %shard_map.46.held), custom_call_target="tpu_custom_call" | custom-call | bytes 1048576 | tf_op jit(solution)/shard_map/pallas_call | solution.py:120
  10.5 2.2 %collective-permute-start.3 = (bf16[8,14976]{1,0:T(8,128)(2,1)S(1)}, bf16[8,14976]{1,0:T(8,128)(2,1)S(1)}, u32[]{:S(2)}, u32[]{:S(2)}) collective-permute-start(bf16[8,14976]{1,0:T(8,128)(2,1)S(1)} %shard_map.47._), channel_id=1, source_target_pairs={{0,4},{4,0},{8,12},{12,8},{1,5},{5,1},{9,13},{13,9},{2,6},{6,2},{1... | collective-permute-start | bytes 718856 | tf_op jit(solution)/shard_map/ppermute | solution.py:336
  12.7 7.6 %shard_map.48 = (bf16[8,14976]{1,0:T(8,128)(2,1)S(1)}, bf16[8,7552]{1,0:T(8,128)(2,1)S(1)}) custom-call(bf16[36,2048]{1,0:T(8,128)(2,1)S(1)} %pad_maximum_fusion.x_ref, bf16[2048,6656]{1,0:T(8,128)(2,1)} %gate_ref.7, bf16[2048,6656]{1,0:T(8,128)(2,1)} %up_ref.7, bf16[8,14976]{1,0:T(8,128)(2,1)S(1)} %shard_map.47._), custom_call_target="tpu_custom_call" | custom-call | bytes 1048576 | tf_op jit(solution)/shard_map/pallas_call | solution.py:164
  20.3 0.0 collective-permute-done.3
  20.3 0.1 add_convert_fusion._
  20.4 2.4 %collective-permute-start.4 = (bf16[8,14976]{1,0:T(8,128)(2,1)S(1)}, bf16[8,14976]{1,0:T(8,128)(2,1)S(1)}, u32[]{:S(2)}, u32[]{:S(2)}) collective-permute-start(bf16[8,14976]{1,0:T(8,128)(2,1)S(1)} %add_convert_fusion._), channel_id=1, source_target_pairs={{0,12},{4,8},{8,4},{12,0},{1,13},{5,9},{9,5},{13,1},{2,14},{6,10},... | collective-permute-start | bytes 718856 | tf_op jit(solution)/shard_map/ppermute | solution.py:336
  22.8 0.6 %collective-permute-start.5 = (bf16[8,7552]{1,0:T(8,128)(2,1)S(1)}, bf16[8,7552]{1,0:T(8,128)(2,1)S(1)}, u32[]{:S(2)}, u32[]{:S(2)}) collective-permute-start(bf16[8,7552]{1,0:T(8,128)(2,1)S(1)} %get-tuple-element.12), channel_id=1, source_target_pairs={{0,4},{4,0},{8,12},{12,8},{1,5},{5,1},{9,13},{13,9},{2,6},{6,2},{1... | collective-permute-start | bytes 362504 | tf_op jit(solution)/shard_map/ppermute | solution.py:336
  23.5 0.0 slice-start
  23.5 0.0 slice-start.1
  23.5 0.0 slice-start.2
  23.5 0.0 slice-start.3
  23.5 3.6 %shard_map.49._ = bf16[8,7552]{1,0:T(8,128)(2,1)S(1)} custom-call(bf16[36,2048]{1,0:T(8,128)(2,1)S(1)} %pad_maximum_fusion.x_ref, bf16[2048,6656]{1,0:T(8,128)(2,1)} %gate_ref.7, bf16[2048,6656]{1,0:T(8,128)(2,1)} %up_ref.7, bf16[8,14976]{1,0:T(8,128)(2,1)S(1)} %add_convert_fusion._), custom_call_target="tpu_custom_call" | custom-call | bytes 1048576 | tf_op jit(solution)/shard_map/pallas_call | solution.py:164
  27.1 0.0 slice-start.4
  27.1 0.0 slice-start.5
  27.1 0.0 slice-start.6
  27.1 1.5 %collective-permute-start.6 = (bf16[8,7552]{1,0:T(8,128)(2,1)S(1)}, bf16[8,7552]{1,0:T(8,128)(2,1)S(1)}, u32[]{:S(2)}, u32[]{:S(2)}) collective-permute-start(bf16[8,7552]{1,0:T(8,128)(2,1)S(1)} %shard_map.49._), channel_id=1, source_target_pairs={{0,4},{4,0},{8,12},{12,8},{1,5},{5,1},{9,13},{13,9},{2,6},{6,2},{1... | collective-permute-start | bytes 362504 | tf_op jit(solution)/shard_map/ppermute | solution.py:336
  28.6 6.2 %shard_map.50.own = bf16[8,14976]{1,0:T(8,128)(2,1)S(1)} custom-call(bf16[36,2048]{1,0:T(8,128)(2,1)S(1)} %pad_maximum_fusion.x_ref, bf16[2048,6656]{1,0:T(8,128)(2,1)} %gate_ref.7, bf16[2048,6656]{1,0:T(8,128)(2,1)} %up_ref.7, bf16[8,7552]{1,0:T(8,128)(2,1)S(1)} %shard_map.49._), custom_call_target="tpu_custom_call" | custom-call | bytes 1048576 | tf_op jit(solution)/shard_map/pallas_call | solution.py:164
  34.8 0.0 collective-permute-done.5.gate_near
  34.8 0.2 collective-permute-done.6.up_near
  35.0 0.0 collective-permute-done.4.far
  35.0 0.1 shard_map.51.refs_0_
  35.1 0.6 %collective-permute-start.7 = (bf16[8,7552]{1,0:T(8,128)(2,1)S(1)}, bf16[8,7552]{1,0:T(8,128)(2,1)S(1)}, u32[]{:S(2)}, u32[]{:S(2)}) collective-permute-start(bf16[8,7552]{1,0:T(8,128)(2,1)S(1)} %shard_map.51.refs_0_), channel_id=1, source_target_pairs={{0,8},{4,12},{8,0},{12,4},{1,9},{5,13},{9,1},{13,5},{2,10},{6,14},... | collective-permute-start | bytes 362504 | tf_op jit(solution)/shard_map/ppermute | solution.py:336
  35.8 1.7 %collective-permute-start.9 = (bf16[8,7552]{1,0:T(8,128)(2,1)S(1)}, bf16[8,7552]{1,0:T(8,128)(2,1)S(1)}, u32[]{:S(2)}, u32[]{:S(2)}) collective-permute-start(bf16[8,7552]{1,0:T(8,128)(2,1)S(1)} %shard_map.51.refs_0_), channel_id=1, source_target_pairs={{0,4},{4,0},{8,12},{12,8},{1,5},{5,1},{9,13},{13,9},{2,6},{6,2},{1... | collective-permute-start | bytes 362504 | tf_op jit(solution)/shard_map/ppermute | solution.py:336
  37.4 5.5 %collective-permute-done.7.refs_2_ = bf16[8,7552]{1,0:T(8,128)(2,1)S(1)} collective-permute-done((bf16[8,7552]{1,0:T(8,128)(2,1)S(1)}, bf16[8,7552]{1,0:T(8,128)(2,1)S(1)}, u32[]{:S(2)}, u32[]{:S(2)}) %collective-permute-start.7) | collective-permute-done | bytes 120864 | tf_op jit(solution)/shard_map/ppermute | solution.py:336
  42.9 0.0 collective-permute-start.8
  42.9 0.1 collective-permute-done.9.refs_1_
  43.1 0.0 slice-done
  43.1 0.0 slice-done.1
  43.1 0.0 slice-done.2
  43.1 0.0 slice-done.3
  43.1 0.0 slice-done.4
  43.1 0.0 slice-done.5
  43.1 0.0 slice-done.6
  43.1 3.6 %shard_map.52.refs_1_ = f32[36,2048]{1,0:T(8,128)S(1)} custom-call(bf16[8,7552]{1,0:T(8,128)(2,1)S(1)} %shard_map.51.refs_0_, bf16[8,7552]{1,0:T(8,128)(2,1)S(1)} %collective-permute-done.9.refs_1_, bf16[8,7552]{1,0:T(8,128)(2,1)S(1)} %collective-permute-done.7.refs_2_, bf16[6656,2048]{1,0:T(8,128)(2,1)S(1)} %bitcast.1), custom_call_target="tpu_custom_call" | custom-call | bytes 1048576 | tf_op jit(solution)/shard_map/pallas_call | solution.py:300
  46.8 1.0 %collective-permute-done.8.refs_0_ = bf16[8,7552]{1,0:T(8,128)(2,1)S(1)} collective-permute-done((bf16[8,7552]{1,0:T(8,128)(2,1)S(1)}, bf16[8,7552]{1,0:T(8,128)(2,1)S(1)}, u32[]{:S(2)}, u32[]{:S(2)}) %collective-permute-start.8) | collective-permute-done | bytes 120864 | tf_op jit(solution)/shard_map/ppermute | solution.py:336
  47.8 1.3 %shard_map.53 = (f32[8,2304]{1,0:T(8,128)S(1)}, bf16[8,2304]{1,0:T(8,128)(2,1)S(1)}, bf16[8,2304]{1,0:T(8,128)(2,1)S(1)}, bf16[8,2304]{1,0:T(8,128)(2,1)S(1)}) custom-call(bf16[8,7552]{1,0:T(8,128)(2,1)S(1)} %collective-permute-done.8.refs_0_, f32[36,2048]{1,0:T(8,128)S(1)} %shard_map.52.refs_1_, bf16[6656,2048]{1,0:T(8,128)(2,1)S(1)} %bitcast.1), custom_call_target="tpu_custom_call" | custom-call | bytes 1048576 | tf_op jit(solution)/shard_map/pallas_call | solution.py:300
  49.1 0.1 collective-permute-start.10
  49.2 1.6 %collective-permute-start.11 = (bf16[8,2304]{1,0:T(8,128)(2,1)S(1)}, bf16[8,2304]{1,0:T(8,128)(2,1)S(1)}, u32[]{:S(2)}, u32[]{:S(2)}) collective-permute-start(bf16[8,2304]{1,0:T(8,128)(2,1)S(1)} %get-tuple-element.15), channel_id=1, source_target_pairs={{0,2},{1,3},{2,0},{3,1},{4,6},{5,7},{6,4},{7,5},{8,10},{9,11},{10,... | collective-permute-start | bytes 110600 | tf_op jit(solution)/shard_map/ppermute | solution.py:336
  50.8 0.3 collective-permute-start.12
  51.1 0.0 collective-permute-done.10.refs_1_
  51.1 2.2 %collective-permute-done.11.refs_2_ = bf16[8,2304]{1,0:T(8,128)(2,1)S(1)} collective-permute-done((bf16[8,2304]{1,0:T(8,128)(2,1)S(1)}, bf16[8,2304]{1,0:T(8,128)(2,1)S(1)}, u32[]{:S(2)}, u32[]{:S(2)}) %collective-permute-start.11) | collective-permute-done | bytes 36896 | tf_op jit(solution)/shard_map/ppermute | solution.py:336
  53.2 1.0 %collective-permute-done.12.refs_3_ = bf16[8,2304]{1,0:T(8,128)(2,1)S(1)} collective-permute-done((bf16[8,2304]{1,0:T(8,128)(2,1)S(1)}, bf16[8,2304]{1,0:T(8,128)(2,1)S(1)}, u32[]{:S(2)}, u32[]{:S(2)}) %collective-permute-start.12) | collective-permute-done | bytes 36896 | tf_op jit(solution)/shard_map/ppermute | solution.py:336
  54.2 0.7 %shard_map.54 = bf16[9,2048]{1,0:T(8,128)(2,1)} custom-call(f32[8,2304]{1,0:T(8,128)S(1)} %get-tuple-element.13.refs_0_, bf16[8,2304]{1,0:T(8,128)(2,1)S(1)} %collective-permute-done.10.refs_1_, bf16[8,2304]{1,0:T(8,128)(2,1)S(1)} %collective-permute-done.11.refs_2_, bf16[8,2304]{1,0:T(8,128)(2,1)S(1)} %collective-permute-done.12.refs_3_), custom_call_target="tpu_custom_call" | custom-call | bytes 1048576 | tf_op jit(solution)/shard_map/pallas_call | solution.py:324
  (1 shorter events, 0.0 us)
Async XLA Ops:
  0.0 8.2 %copy-start = (bf16[9,2048]{1,0:T(8,128)(2,1)S(1)}, bf16[9,2048]{1,0:T(8,128)(2,1)}, u32[]{:S(2)}) copy-start(bf16[9,2048]{1,0:T(8,128)(2,1)} %param.4) | copy-start | bytes 110596
  0.0 8.2 %collective-permute-start.1 = (bf16[9,2048]{1,0:T(8,128)(2,1)}, bf16[9,2048]{1,0:T(8,128)(2,1)S(1)}, u32[]{:S(2)}, u32[]{:S(2)}) collective-permute-start(bf16[9,2048]{1,0:T(8,128)(2,1)} %param.4), channel_id=1, source_target_pairs={{0,2},{1,3},{2,0},{3,1},{4,6},{5,7},{6,4},{7,5},{8,10},{9,11},{10,... | collective-permute-start | bytes 110600 | tf_op jit(solution)/shard_map/ppermute | solution.py:336
  2.9 5.2 %collective-permute-start = (bf16[9,2048]{1,0:T(8,128)(2,1)}, bf16[9,2048]{1,0:T(8,128)(2,1)S(1)}, u32[]{:S(2)}, u32[]{:S(2)}) collective-permute-start(bf16[9,2048]{1,0:T(8,128)(2,1)} %param.4), channel_id=1, source_target_pairs={{0,1},{1,0},{2,3},{3,2},{4,5},{5,4},{6,7},{7,6},{8,9},{9,8},{10,11... | collective-permute-start | bytes 110600 | tf_op jit(solution)/shard_map/ppermute | solution.py:336
  2.9 5.3 %collective-permute-start.2 = (bf16[9,2048]{1,0:T(8,128)(2,1)}, bf16[9,2048]{1,0:T(8,128)(2,1)S(1)}, u32[]{:S(2)}, u32[]{:S(2)}) collective-permute-start(bf16[9,2048]{1,0:T(8,128)(2,1)} %param.4), channel_id=1, source_target_pairs={{0,3},{1,2},{2,1},{3,0},{4,7},{5,6},{6,5},{7,4},{8,11},{9,10},{10,... | collective-permute-start | bytes 110600 | tf_op jit(solution)/shard_map/ppermute | solution.py:336
  10.5 9.9 %collective-permute-start.3 = (bf16[8,14976]{1,0:T(8,128)(2,1)S(1)}, bf16[8,14976]{1,0:T(8,128)(2,1)S(1)}, u32[]{:S(2)}, u32[]{:S(2)}) collective-permute-start(bf16[8,14976]{1,0:T(8,128)(2,1)S(1)} %shard_map.47._), channel_id=1, source_target_pairs={{0,4},{4,0},{8,12},{12,8},{1,5},{5,1},{9,13},{13,9},{2,6},{6,2},{1... | collective-permute-start | bytes 718856 | tf_op jit(solution)/shard_map/ppermute | solution.py:336
  20.4 14.6 %collective-permute-start.4 = (bf16[8,14976]{1,0:T(8,128)(2,1)S(1)}, bf16[8,14976]{1,0:T(8,128)(2,1)S(1)}, u32[]{:S(2)}, u32[]{:S(2)}) collective-permute-start(bf16[8,14976]{1,0:T(8,128)(2,1)S(1)} %add_convert_fusion._), channel_id=1, source_target_pairs={{0,12},{4,8},{8,4},{12,0},{1,13},{5,9},{9,5},{13,1},{2,14},{6,10},... | collective-permute-start | bytes 718856 | tf_op jit(solution)/shard_map/ppermute | solution.py:336
  22.8 12.0 %collective-permute-start.5 = (bf16[8,7552]{1,0:T(8,128)(2,1)S(1)}, bf16[8,7552]{1,0:T(8,128)(2,1)S(1)}, u32[]{:S(2)}, u32[]{:S(2)}) collective-permute-start(bf16[8,7552]{1,0:T(8,128)(2,1)S(1)} %get-tuple-element.12), channel_id=1, source_target_pairs={{0,4},{4,0},{8,12},{12,8},{1,5},{5,1},{9,13},{13,9},{2,6},{6,2},{1... | collective-permute-start | bytes 362504 | tf_op jit(solution)/shard_map/ppermute | solution.py:336
  23.5 19.6 %slice-start = ((s8[27262976]{0:T(1024)(128)(4,1)}), s8[4194304]{0:T(1024)(128)(4,1)S(1)}, s32[]{:S(2)}) async-start(s8[27262976]{0:T(1024)(128)(4,1)} %bitcast), calls=%async_computation | async-start | bytes 8388608
  23.5 19.6 %slice-start.1 = ((s8[27262976]{0:T(1024)(128)(4,1)}), s8[4194304]{0:T(1024)(128)(4,1)S(1)}, s32[]{:S(2)}) async-start(s8[27262976]{0:T(1024)(128)(4,1)} %bitcast), calls=%async_computation.1 | async-start | bytes 8388608
  23.5 19.6 %slice-start.2 = ((s8[27262976]{0:T(1024)(128)(4,1)}), s8[4194304]{0:T(1024)(128)(4,1)S(1)}, s32[]{:S(2)}) async-start(s8[27262976]{0:T(1024)(128)(4,1)} %bitcast), calls=%async_computation.2 | async-start | bytes 8388608
  23.5 19.6 %slice-start.3 = ((s8[27262976]{0:T(1024)(128)(4,1)}), s8[4194304]{0:T(1024)(128)(4,1)S(1)}, s32[]{:S(2)}) async-start(s8[27262976]{0:T(1024)(128)(4,1)} %bitcast), calls=%async_computation.3 | async-start | bytes 8388608
  27.1 16.0 %slice-start.4 = ((s8[27262976]{0:T(1024)(128)(4,1)}), s8[4194304]{0:T(1024)(128)(4,1)S(1)}, s32[]{:S(2)}) async-start(s8[27262976]{0:T(1024)(128)(4,1)} %bitcast), calls=%async_computation.4 | async-start | bytes 8388608
  27.1 16.0 %slice-start.5 = ((s8[27262976]{0:T(1024)(128)(4,1)}), s8[4194304]{0:T(1024)(128)(4,1)S(1)}, s32[]{:S(2)}) async-start(s8[27262976]{0:T(1024)(128)(4,1)} %bitcast), calls=%async_computation.5 | async-start | bytes 8388608
  27.1 16.0 %slice-start.6 = ((s8[27262976]{0:T(1024)(128)(4,1)}), s8[2097152]{0:T(1024)(128)(4,1)S(1)}, s32[]{:S(2)}) async-start(s8[27262976]{0:T(1024)(128)(4,1)} %bitcast), calls=%async_computation.6 | async-start | bytes 4194304
  27.1 7.9 %collective-permute-start.6 = (bf16[8,7552]{1,0:T(8,128)(2,1)S(1)}, bf16[8,7552]{1,0:T(8,128)(2,1)S(1)}, u32[]{:S(2)}, u32[]{:S(2)}) collective-permute-start(bf16[8,7552]{1,0:T(8,128)(2,1)S(1)} %shard_map.49._), channel_id=1, source_target_pairs={{0,4},{4,0},{8,12},{12,8},{1,5},{5,1},{9,13},{13,9},{2,6},{6,2},{1... | collective-permute-start | bytes 362504 | tf_op jit(solution)/shard_map/ppermute | solution.py:336
  35.1 7.8 %collective-permute-start.7 = (bf16[8,7552]{1,0:T(8,128)(2,1)S(1)}, bf16[8,7552]{1,0:T(8,128)(2,1)S(1)}, u32[]{:S(2)}, u32[]{:S(2)}) collective-permute-start(bf16[8,7552]{1,0:T(8,128)(2,1)S(1)} %shard_map.51.refs_0_), channel_id=1, source_target_pairs={{0,8},{4,12},{8,0},{12,4},{1,9},{5,13},{9,1},{13,5},{2,10},{6,14},... | collective-permute-start | bytes 362504 | tf_op jit(solution)/shard_map/ppermute | solution.py:336
  35.8 7.3 %collective-permute-start.9 = (bf16[8,7552]{1,0:T(8,128)(2,1)S(1)}, bf16[8,7552]{1,0:T(8,128)(2,1)S(1)}, u32[]{:S(2)}, u32[]{:S(2)}) collective-permute-start(bf16[8,7552]{1,0:T(8,128)(2,1)S(1)} %shard_map.51.refs_0_), channel_id=1, source_target_pairs={{0,4},{4,0},{8,12},{12,8},{1,5},{5,1},{9,13},{13,9},{2,6},{6,2},{1... | collective-permute-start | bytes 362504 | tf_op jit(solution)/shard_map/ppermute | solution.py:336
  42.9 4.9 %collective-permute-start.8 = (bf16[8,7552]{1,0:T(8,128)(2,1)S(1)}, bf16[8,7552]{1,0:T(8,128)(2,1)S(1)}, u32[]{:S(2)}, u32[]{:S(2)}) collective-permute-start(bf16[8,7552]{1,0:T(8,128)(2,1)S(1)} %collective-permute-done.7.refs_2_), channel_id=1, source_target_pairs={{0,4},{4,0},{8,12},{12,8},{1,5},{5,1},{9,13},{13,9},{2,6},{6,2},{1... | collective-permute-start | bytes 362504 | tf_op jit(solution)/shard_map/ppermute | solution.py:336
  49.1 1.9 %collective-permute-start.10 = (bf16[8,2304]{1,0:T(8,128)(2,1)S(1)}, bf16[8,2304]{1,0:T(8,128)(2,1)S(1)}, u32[]{:S(2)}, u32[]{:S(2)}) collective-permute-start(bf16[8,2304]{1,0:T(8,128)(2,1)S(1)} %get-tuple-element.14), channel_id=1, source_target_pairs={{0,1},{1,0},{2,3},{3,2},{4,5},{5,4},{6,7},{7,6},{8,9},{9,8},{10,11... | collective-permute-start | bytes 110600 | tf_op jit(solution)/shard_map/ppermute | solution.py:336
  49.2 4.0 %collective-permute-start.11 = (bf16[8,2304]{1,0:T(8,128)(2,1)S(1)}, bf16[8,2304]{1,0:T(8,128)(2,1)S(1)}, u32[]{:S(2)}, u32[]{:S(2)}) collective-permute-start(bf16[8,2304]{1,0:T(8,128)(2,1)S(1)} %get-tuple-element.15), channel_id=1, source_target_pairs={{0,2},{1,3},{2,0},{3,1},{4,6},{5,7},{6,4},{7,5},{8,10},{9,11},{10,... | collective-permute-start | bytes 110600 | tf_op jit(solution)/shard_map/ppermute | solution.py:336
  50.8 3.4 %collective-permute-start.12 = (bf16[8,2304]{1,0:T(8,128)(2,1)S(1)}, bf16[8,2304]{1,0:T(8,128)(2,1)S(1)}, u32[]{:S(2)}, u32[]{:S(2)}) collective-permute-start(bf16[8,2304]{1,0:T(8,128)(2,1)S(1)} %get-tuple-element.16), channel_id=1, source_target_pairs={{0,3},{1,2},{2,1},{3,0},{4,7},{5,6},{6,5},{7,4},{8,11},{9,10},{10,... | collective-permute-start | bytes 110600 | tf_op jit(solution)/shard_map/ppermute | solution.py:336

commit v23 on v22

--- a/solution.py
+++ b/solution.py
@@ -12,6 +12,7 @@
 COPY_STEP = 512
 IN_FLIGHT = 6
 DOWN_STEP = 512
+LARGE_STEP = 1024
 TOKEN_AXES = ("gy", "gz")
 IN_HBM = pl.BlockSpec(memory_space=pltpu.HBM)
 ANY = pl.BlockSpec(memory_space=pl.ANY)
@@ -61,71 +62,95 @@
         out[:, at : at + width] = tail.astype(out.dtype)
 
 
-def block_copies(width, distance, weights, held, sems):
+def block_copies(width, distance, weights, held, sems, step, first=0):
     columns = pl.ds(block_start(distance, width), width)
     copies = []
-    for k, (row, rows) in enumerate(pieces_of(held.shape[1], COPY_STEP)):
+    for k, (row, rows) in enumerate(pieces_of(held.shape[1], step)):
         for w, weight in enumerate(weights):
             copy = pltpu.make_async_copy(
-                weight.at[pl.ds(row, rows), columns], held.at[w, pl.ds(row, rows)], sems.at[w, k]
+                weight.at[pl.ds(first + row, rows), columns],
+                held.at[w, pl.ds(row, rows)],
+                sems.at[w, k],
             )
             copies.append((w, row, rows, copy))
     return copies
 
 
+def copy_sems(weights, depth, step):
+    return pltpu.SemaphoreType.DMA((weights, len(pieces_of(depth, step))))
+
+
 def fetch_kernel(width, distance, gate_ref, up_ref, held, sems):
-    copies = block_copies(width, distance, (gate_ref, up_ref), held, sems)
+    copies = block_copies(width, distance, (gate_ref, up_ref), held, sems, COPY_STEP)
     for _, _, _, copy in copies:
         copy.start()
     for _, _, _, copy in copies:
         copy.wait()
 
 
-def fetch(gate_weight, up_weight, distance, width):
-    depth = gate_weight.shape[0]
+def fetch(gate_weight, up_weight, distance, depth, width):
     return pl.pallas_call(
         functools.partial(fetch_kernel, width, distance),
         out_shape=pltpu.VMEM((2, depth, width), jnp.bfloat16),
         in_specs=[IN_HBM, IN_HBM],
         out_specs=WHOLE,
-        scratch_shapes=[pltpu.SemaphoreType.DMA((2, len(pieces_of(depth, COPY_STEP))))],
+        scratch_shapes=[copy_sems(2, depth, COPY_STEP)],
         compiler_params=params(4),
         cost_estimate=SMALL,
     )(in_hbm(gate_weight), in_hbm(up_weight))
 
 
-def multiply(x_ref, held, total, steps, waiting=()):
-    for w, first, tall, copy in steps:
+def multiply(x_ref, held, total, steps, waiting=(), first=0):
+    for w, top, tall, copy in steps:
         if copy is not None:
             copy.wait()
         if waiting:
             waiting.pop(0).start()
         for row, rows in pieces_of(tall, STEP):
-            rows = slice(first + row, first + row + rows)
-            term = jnp.dot(x_ref[:, rows], held[w, rows, :], preferred_element_type=jnp.float32)
-            if rows.start == 0:
+            at = first + top + row
+            term = jnp.dot(
+                x_ref[:, at : at + rows],
+                held[w, top + row : top + row + rows, :],
+                preferred_element_type=jnp.float32,
+            )
+            if at == 0:
                 total[w] = term
             else:
                 total[w] += term
 
 
-def held_kernel(x_ref, held, out, total):
-    parts = pieces_of(x_ref.shape[1], STEP)
-    multiply(x_ref, held, total, [(w, row, rows, None) for w in range(2) for row, rows in parts])
+def held_kernel(width, distance, x_ref, held, gate_ref, up_ref, out, stream, total, sems):
+    first = held.shape[1]
+    copies = block_copies(width, distance, (gate_ref, up_ref), stream, sems, COPY_STEP, first)
+    for _, _, _, copy in copies:
+        copy.start()
+    steps = [(w, row, rows, None) for row, rows in pieces_of(first, STEP) for w in range(2)]
+    multiply(x_ref, held, total, steps)
+    multiply(x_ref, stream, total, copies, first=first)
     pack_pair(out, total[0], total[1])
 
 
-def gate_up_held(features, held):
-    rows, width = features.shape[0], held.shape[2]
-    return pl.pallas_call(
-        held_kernel,
+def gate_up_held(features, held, gate_weight, up_weight, distance):
+    rows, depth = features.shape
+    width = held.shape[2]
+    below = depth - held.shape[1]
+    return pl.pallas_call(
+        functools.partial(held_kernel, width, distance),
         out_shape=jax.ShapeDtypeStruct((8, packed_pair_width(rows, width)), jnp.bfloat16),
-        in_specs=[WHOLE, WHOLE],
+        in_specs=[WHOLE, WHOLE, IN_HBM, IN_HBM],
         out_specs=WHOLE,
-        scratch_shapes=[pltpu.VMEM((2, rows, width), jnp.float32)],
-        compiler_params=params(8),
-        cost_estimate=SMALL,
-    )(features, in_vmem(held))
+        scratch_shapes=[
+            pltpu.VMEM((2, below, width), jnp.bfloat16),
+            pltpu.VMEM((2, rows, width), jnp.float32),
+            copy_sems(2, below, COPY_STEP),
+        ],
+        compiler_params=params(5 + -(-below * width * 4 // MIB)),
+        cost_estimate=SMALL,
+    )(features, in_vmem(held), in_hbm(gate_weight), in_hbm(up_weight))
+
+
+def stream_step(blocks):
+    return LARGE_STEP if blocks == ((0, 1),) else COPY_STEP
 
 
 def stream_kernel(width, blocks, distances, x_ref, gate_ref, up_ref, _, *refs):
@@ -134,7 +159,7 @@
     for b, which in enumerate(blocks):
         held, total, sems = refs[3 * b : 3 * b + 3]
         weights = [(gate_ref, up_ref)[w] for w in which]
-        copies = block_copies(width, distances[b], weights, held, sems)
+        copies = block_copies(width, distances[b], weights, held, sems, stream_step(blocks))
         work.append((outs[b], held, total, copies))
     waiting = [step[-1] for block in work for step in block[-1]]
     in_flight = IN_FLIGHT if len(blocks) > 1 else len(waiting)
@@ -158,7 +183,7 @@
         scratch += [
             pltpu.VMEM((len(which), depth, width), jnp.bfloat16),
             pltpu.VMEM((len(which), rows, width), jnp.float32),
-            pltpu.SemaphoreType.DMA((len(which), len(pieces_of(depth, COPY_STEP)))),
+            copy_sems(len(which), depth, stream_step(blocks)),
         ]
     held_mib = -(-depth * width * 2 * sum(len(which) for which in blocks) // MIB)
     return pl.pallas_call(
@@ -345,7 +370,8 @@
     n_token = lax.axis_size(TOKEN_AXES)
     width = gate_weight.shape[1] // n_gx
 
-    held = fetch(gate_weight, up_weight, 2, width)
+    early = gate_weight.shape[0] // 4 * 3 // STEP * STEP
+    held = fetch(gate_weight, up_weight, 2, early, width)
     features = jnp.concatenate(
         [tokens] + [swap(tokens, TOKEN_AXES, n_token, r) for r in range(1, n_token)], axis=0
     )
@@ -354,7 +380,7 @@
     def blocks_for(distances, blocks, after):
         return gate_up_stream(features, gate_weight, up_weight, distances, blocks, width, after)
 
-    relayed = gate_up_held(features, held)
+    relayed = gate_up_held(features, held, gate_weight, up_weight, 2)
     arrived = swap(relayed, "gx", n_gx, 1)
     across, beside = blocks_for((3, 1), ((0, 1), (0,)), relayed)
     across = lax.optimization_barrier(add(across, arrived).astype(jnp.bfloat16))
@@ -394,7 +420,7 @@
     n_token = lax.axis_size(TOKEN_AXES)
     rows = tokens.shape[0] * n_token
     tokens_fit = n_token > 1 and n_token & (n_token - 1) == 0 and rows % 4 == 0
-    weights_fit = gate_weight.shape[1] % (128 * 4) == 0 and gate_weight.shape[0] % STEP == 0
+    weights_fit = gate_weight.shape[1] % (128 * 4) == 0 and gate_weight.shape[0] % (4 * STEP) == 0
     columns_fit = down_weight.shape[1] % (128 * 8) == 0
     if n_gx == 4 and tokens_fit and weights_fit and columns_fit:
         return direct(tokens, gate_weight, up_weight, down_weight)

time: 55 us -> 55.7 us (1.013)
  Pallas kernels: 30.4 us -> 31.3 us
    pallas_call x1, Pallas kernels: 2.15 us -> 3.91 us  [gate_up_held(): pl.pallas_call(functools.partial(held_kernel, width, distance), out_shape...]
    pallas_call x1, Pallas kernels: 5.03 us -> 4.03 us  [fetch(): pl.pallas_call(functools.partial(fetch_kernel, width, distance), out_shap...]
  transfers between devices with their start and end apart: 13 -> 13, of which waited for: 6 -> 5; matrix products, arithmetic and copies ran while one was open for 0% -> 0% of each run, Pallas kernels for 48% -> 46%
where the time goes in v23:
time: 55.7 us; the launch traced here: 55.6 us
  Pallas kernels  31.3 us (56%)
  starting transfers between devices  14 us (25%)
  waiting for transfers between devices  9.85 us (18%)
    pallas_call x3, Pallas kernels, gate_up_stream(): pl.pallas_call(functools.partial(stream_kernel, width, blocks, distances)...  17.7 us
    ppermute x13, starting transfers between devices, swap(): return lax.ppermute(value, axes, [(i, i ^ distance) for i in range(size)])  14 us
    ppermute x13, waiting for transfers between devices, swap(): return lax.ppermute(value, axes, [(i, i ^ distance) for i in range(size)])  9.85 us
    pallas_call x2, Pallas kernels, down(): pl.pallas_call(functools.partial(down_kernel, before is None, rows, width...  4.92 us
    pallas_call x1, Pallas kernels, fetch(): pl.pallas_call(functools.partial(fetch_kernel, width, distance), out_shap...  4.03 us
    pallas_call x1, Pallas kernels, gate_up_held(): pl.pallas_call(functools.partial(held_kernel, width, distance), out_shape...  3.91 us
  transfers between devices with their start and end apart: 13, of which 5 were waited for; matrix products, arithmetic and copies ran while one was open for 0% of the time, Pallas kernels for 46%

profile of v23, /device:TPU:0, one launch (start us, length us, event | category | flops | bytes accessed | tf_op | source)
XLA Modules:
  0.0 55.6 jit_solution(7444221000149447161)
XLA Ops:
  0.0 0.0 copy-start
  0.0 2.9 %collective-permute-start.1 = (bf16[9,2048]{1,0:T(8,128)(2,1)}, bf16[9,2048]{1,0:T(8,128)(2,1)S(1)}, u32[]{:S(2)}, u32[]{:S(2)}) collective-permute-start(bf16[9,2048]{1,0:T(8,128)(2,1)} %param.4), channel_id=1, source_target_pairs={{0,2},{1,3},{2,0},{3,1},{4,6},{5,7},{6,4},{7,5},{8,10},{9,11},{10,... | collective-permute-start | bytes 110600 | tf_op jit(solution)/shard_map/ppermute | solution.py:361
  2.9 0.0 collective-permute-start
  2.9 0.2 collective-permute-start.2
  3.1 4.0 %shard_map.46.held = bf16[2,1536,1664]{2,1,0:T(8,128)(2,1)S(1)} custom-call(bf16[2048,6656]{1,0:T(8,128)(2,1)} %gate_ref.9, bf16[2048,6656]{1,0:T(8,128)(2,1)} %up_ref.9), custom_call_target="tpu_custom_call" | custom-call | bytes 1048576 | tf_op jit(solution)/shard_map/pallas_call | solution.py:92
  7.2 0.0 collective-permute-done.1
  7.2 0.0 collective-permute-done
  7.2 0.0 collective-permute-done.2
  7.2 0.0 copy-done
  7.2 0.1 pad_maximum_fusion.x_ref
  7.3 3.9 %shard_map.47._ = bf16[8,14976]{1,0:T(8,128)(2,1)S(1)} custom-call(bf16[36,2048]{1,0:T(8,128)(2,1)S(1)} %pad_maximum_fusion.x_ref, bf16[2,1536,1664]{2,1,0:T(8,128)(2,1)S(1)} %shard_map.46.held, bf16[2048,6656]{1,0:T(8,128)(2,1)} %gate_ref.9, bf16[2048,6656]{1,0:T(8,128)(2,1)} %up_ref.9), custom_call_target="tpu_custom_call" | custom-call | bytes 1048576 | tf_op jit(solution)/shard_map/pallas_call | solution.py:137
  11.2 2.2 %collective-permute-start.3 = (bf16[8,14976]{1,0:T(8,128)(2,1)S(1)}, bf16[8,14976]{1,0:T(8,128)(2,1)S(1)}, u32[]{:S(2)}, u32[]{:S(2)}) collective-permute-start(bf16[8,14976]{1,0:T(8,128)(2,1)S(1)} %shard_map.47._), channel_id=1, source_target_pairs={{0,4},{4,0},{8,12},{12,8},{1,5},{5,1},{9,13},{13,9},{2,6},{6,2},{1... | collective-permute-start | bytes 718856 | tf_op jit(solution)/shard_map/ppermute | solution.py:361
  13.4 7.6 %shard_map.48 = (bf16[8,14976]{1,0:T(8,128)(2,1)S(1)}, bf16[8,7552]{1,0:T(8,128)(2,1)S(1)}) custom-call(bf16[36,2048]{1,0:T(8,128)(2,1)S(1)} %pad_maximum_fusion.x_ref, bf16[2048,6656]{1,0:T(8,128)(2,1)} %gate_ref.9, bf16[2048,6656]{1,0:T(8,128)(2,1)} %up_ref.9, bf16[8,14976]{1,0:T(8,128)(2,1)S(1)} %shard_map.47._), custom_call_target="tpu_custom_call" | custom-call | bytes 1048576 | tf_op jit(solution)/shard_map/pallas_call | solution.py:189
  21.1 0.0 collective-permute-done.3
  21.1 0.1 add_convert_fusion._
  21.1 2.4 %collective-permute-start.4 = (bf16[8,14976]{1,0:T(8,128)(2,1)S(1)}, bf16[8,14976]{1,0:T(8,128)(2,1)S(1)}, u32[]{:S(2)}, u32[]{:S(2)}) collective-permute-start(bf16[8,14976]{1,0:T(8,128)(2,1)S(1)} %add_convert_fusion._), channel_id=1, source_target_pairs={{0,12},{4,8},{8,4},{12,0},{1,13},{5,9},{9,5},{13,1},{2,14},{6,10},... | collective-permute-start | bytes 718856 | tf_op jit(solution)/shard_map/ppermute | solution.py:361
  23.5 0.7 %collective-permute-start.5 = (bf16[8,7552]{1,0:T(8,128)(2,1)S(1)}, bf16[8,7552]{1,0:T(8,128)(2,1)S(1)}, u32[]{:S(2)}, u32[]{:S(2)}) collective-permute-start(bf16[8,7552]{1,0:T(8,128)(2,1)S(1)} %get-tuple-element.12), channel_id=1, source_target_pairs={{0,4},{4,0},{8,12},{12,8},{1,5},{5,1},{9,13},{13,9},{2,6},{6,2},{1... | collective-permute-start | bytes 362504 | tf_op jit(solution)/shard_map/ppermute | solution.py:361
  24.2 0.0 slice-start
  24.2 0.0 slice-start.1
  24.2 0.0 slice-start.2
  24.2 0.0 slice-start.3
  24.2 3.6 %shard_map.49._ = bf16[8,7552]{1,0:T(8,128)(2,1)S(1)} custom-call(bf16[36,2048]{1,0:T(8,128)(2,1)S(1)} %pad_maximum_fusion.x_ref, bf16[2048,6656]{1,0:T(8,128)(2,1)} %gate_ref.9, bf16[2048,6656]{1,0:T(8,128)(2,1)} %up_ref.9, bf16[8,14976]{1,0:T(8,128)(2,1)S(1)} %add_convert_fusion._), custom_call_target="tpu_custom_call" | custom-call | bytes 1048576 | tf_op jit(solution)/shard_map/pallas_call | solution.py:189
  27.8 0.0 slice-start.4
  27.8 0.0 slice-start.5
  27.8 0.0 slice-start.6
  27.9 1.4 %collective-permute-start.6 = (bf16[8,7552]{1,0:T(8,128)(2,1)S(1)}, bf16[8,7552]{1,0:T(8,128)(2,1)S(1)}, u32[]{:S(2)}, u32[]{:S(2)}) collective-permute-start(bf16[8,7552]{1,0:T(8,128)(2,1)S(1)} %shard_map.49._), channel_id=1, source_target_pairs={{0,4},{4,0},{8,12},{12,8},{1,5},{5,1},{9,13},{13,9},{2,6},{6,2},{1... | collective-permute-start | bytes 362504 | tf_op jit(solution)/shard_map/ppermute | solution.py:361
  29.3 6.5 %shard_map.50.own = bf16[8,14976]{1,0:T(8,128)(2,1)S(1)} custom-call(bf16[36,2048]{1,0:T(8,128)(2,1)S(1)} %pad_maximum_fusion.x_ref, bf16[2048,6656]{1,0:T(8,128)(2,1)} %gate_ref.9, bf16[2048,6656]{1,0:T(8,128)(2,1)} %up_ref.9, bf16[8,7552]{1,0:T(8,128)(2,1)S(1)} %shard_map.49._), custom_call_target="tpu_custom_call" | custom-call | bytes 1048576 | tf_op jit(solution)/shard_map/pallas_call | solution.py:189
  35.7 0.0 collective-permute-done.5.gate_near
  35.7 0.0 collective-permute-done.6.up_near
  35.7 0.0 collective-permute-done.4.far
  35.8 0.1 shard_map.51.refs_0_
  35.9 0.6 %collective-permute-start.7 = (bf16[8,7552]{1,0:T(8,128)(2,1)S(1)}, bf16[8,7552]{1,0:T(8,128)(2,1)S(1)}, u32[]{:S(2)}, u32[]{:S(2)}) collective-permute-start(bf16[8,7552]{1,0:T(8,128)(2,1)S(1)} %shard_map.51.refs_0_), channel_id=1, source_target_pairs={{0,8},{4,12},{8,0},{12,4},{1,9},{5,13},{9,1},{13,5},{2,10},{6,14},... | collective-permute-start | bytes 362504 | tf_op jit(solution)/shard_map/ppermute | solution.py:361
  36.5 1.7 %collective-permute-start.9 = (bf16[8,7552]{1,0:T(8,128)(2,1)S(1)}, bf16[8,7552]{1,0:T(8,128)(2,1)S(1)}, u32[]{:S(2)}, u32[]{:S(2)}) collective-permute-start(bf16[8,7552]{1,0:T(8,128)(2,1)S(1)} %shard_map.51.refs_0_), channel_id=1, source_target_pairs={{0,4},{4,0},{8,12},{12,8},{1,5},{5,1},{9,13},{13,9},{2,6},{6,2},{1... | collective-permute-start | bytes 362504 | tf_op jit(solution)/shard_map/ppermute | solution.py:361
  38.1 5.5 %collective-permute-done.7.refs_2_ = bf16[8,7552]{1,0:T(8,128)(2,1)S(1)} collective-permute-done((bf16[8,7552]{1,0:T(8,128)(2,1)S(1)}, bf16[8,7552]{1,0:T(8,128)(2,1)S(1)}, u32[]{:S(2)}, u32[]{:S(2)}) %collective-permute-start.7) | collective-permute-done | bytes 120864 | tf_op jit(solution)/shard_map/ppermute | solution.py:361
  43.7 0.0 collective-permute-start.8
  43.7 0.1 collective-permute-done.9.refs_1_
  43.8 0.0 slice-done
  43.8 0.0 slice-done.1
  43.8 0.0 slice-done.2
  43.8 0.0 slice-done.3
  43.8 0.0 slice-done.4
  43.8 0.0 slice-done.5
  43.8 0.0 slice-done.6
  43.9 3.6 %shard_map.52.refs_1_ = f32[36,2048]{1,0:T(8,128)S(1)} custom-call(bf16[8,7552]{1,0:T(8,128)(2,1)S(1)} %shard_map.51.refs_0_, bf16[8,7552]{1,0:T(8,128)(2,1)S(1)} %collective-permute-done.9.refs_1_, bf16[8,7552]{1,0:T(8,128)(2,1)S(1)} %collective-permute-done.7.refs_2_, bf16[6656,2048]{1,0:T(8,128)(2,1)S(1)} %bitcast.1), custom_call_target="tpu_custom_call" | custom-call | bytes 1048576 | tf_op jit(solution)/shard_map/pallas_call | solution.py:325
  47.5 1.1 %collective-permute-done.8.refs_0_ = bf16[8,7552]{1,0:T(8,128)(2,1)S(1)} collective-permute-done((bf16[8,7552]{1,0:T(8,128)(2,1)S(1)}, bf16[8,7552]{1,0:T(8,128)(2,1)S(1)}, u32[]{:S(2)}, u32[]{:S(2)}) %collective-permute-start.8) | collective-permute-done | bytes 120864 | tf_op jit(solution)/shard_map/ppermute | solution.py:361
  48.5 1.3 %shard_map.53 = (f32[8,2304]{1,0:T(8,128)S(1)}, bf16[8,2304]{1,0:T(8,128)(2,1)S(1)}, bf16[8,2304]{1,0:T(8,128)(2,1)S(1)}, bf16[8,2304]{1,0:T(8,128)(2,1)S(1)}) custom-call(bf16[8,7552]{1,0:T(8,128)(2,1)S(1)} %collective-permute-done.8.refs_0_, f32[36,2048]{1,0:T(8,128)S(1)} %shard_map.52.refs_1_, bf16[6656,2048]{1,0:T(8,128)(2,1)S(1)} %bitcast.1), custom_call_target="tpu_custom_call" | custom-call | bytes 1048576 | tf_op jit(solution)/shard_map/pallas_call | solution.py:325
  49.9 0.1 collective-permute-start.10
  49.9 1.6 %collective-permute-start.11 = (bf16[8,2304]{1,0:T(8,128)(2,1)S(1)}, bf16[8,2304]{1,0:T(8,128)(2,1)S(1)}, u32[]{:S(2)}, u32[]{:S(2)}) collective-permute-start(bf16[8,2304]{1,0:T(8,128)(2,1)S(1)} %get-tuple-element.15), channel_id=1, source_target_pairs={{0,2},{1,3},{2,0},{3,1},{4,6},{5,7},{6,4},{7,5},{8,10},{9,11},{10,... | collective-permute-start | bytes 110600 | tf_op jit(solution)/shard_map/ppermute | solution.py:361
  51.5 0.3 collective-permute-start.12
  51.8 0.0 collective-permute-done.10.refs_1_
  51.8 2.2 %collective-permute-done.11.refs_2_ = bf16[8,2304]{1,0:T(8,128)(2,1)S(1)} collective-permute-done((bf16[8,2304]{1,0:T(8,128)(2,1)S(1)}, bf16[8,2304]{1,0:T(8,128)(2,1)S(1)}, u32[]{:S(2)}, u32[]{:S(2)}) %collective-permute-start.11) | collective-permute-done | bytes 36896 | tf_op jit(solution)/shard_map/ppermute | solution.py:361
  54.0 1.0 %collective-permute-done.12.refs_3_ = bf16[8,2304]{1,0:T(8,128)(2,1)S(1)} collective-permute-done((bf16[8,2304]{1,0:T(8,128)(2,1)S(1)}, bf16[8,2304]{1,0:T(8,128)(2,1)S(1)}, u32[]{:S(2)}, u32[]{:S(2)}) %collective-permute-start.12) | collective-permute-done | bytes 36896 | tf_op jit(solution)/shard_map/ppermute | solution.py:361
  54.9 0.7 %shard_map.54 = bf16[9,2048]{1,0:T(8,128)(2,1)} custom-call(f32[8,2304]{1,0:T(8,128)S(1)} %get-tuple-element.13.refs_0_, bf16[8,2304]{1,0:T(8,128)(2,1)S(1)} %collective-permute-done.10.refs_1_, bf16[8,2304]{1,0:T(8,128)(2,1)S(1)} %collective-permute-done.11.refs_2_, bf16[8,2304]{1,0:T(8,128)(2,1)S(1)} %collective-permute-done.12.refs_3_), custom_call_target="tpu_custom_call" | custom-call | bytes 1048576 | tf_op jit(solution)/shard_map/pallas_call | solution.py:349
  (1 shorter events, 0.0 us)
Async XLA Ops:
  0.0 7.2 %copy-start = (bf16[9,2048]{1,0:T(8,128)(2,1)S(1)}, bf16[9,2048]{1,0:T(8,128)(2,1)}, u32[]{:S(2)}) copy-start(bf16[9,2048]{1,0:T(8,128)(2,1)} %param.4) | copy-start | bytes 110596
  0.0 7.2 %collective-permute-start.1 = (bf16[9,2048]{1,0:T(8,128)(2,1)}, bf16[9,2048]{1,0:T(8,128)(2,1)S(1)}, u32[]{:S(2)}, u32[]{:S(2)}) collective-permute-start(bf16[9,2048]{1,0:T(8,128)(2,1)} %param.4), channel_id=1, source_target_pairs={{0,2},{1,3},{2,0},{3,1},{4,6},{5,7},{6,4},{7,5},{8,10},{9,11},{10,... | collective-permute-start | bytes 110600 | tf_op jit(solution)/shard_map/ppermute | solution.py:361
  2.9 4.2 %collective-permute-start = (bf16[9,2048]{1,0:T(8,128)(2,1)}, bf16[9,2048]{1,0:T(8,128)(2,1)S(1)}, u32[]{:S(2)}, u32[]{:S(2)}) collective-permute-start(bf16[9,2048]{1,0:T(8,128)(2,1)} %param.4), channel_id=1, source_target_pairs={{0,1},{1,0},{2,3},{3,2},{4,5},{5,4},{6,7},{7,6},{8,9},{9,8},{10,11... | collective-permute-start | bytes 110600 | tf_op jit(solution)/shard_map/ppermute | solution.py:361
  2.9 4.3 %collective-permute-start.2 = (bf16[9,2048]{1,0:T(8,128)(2,1)}, bf16[9,2048]{1,0:T(8,128)(2,1)S(1)}, u32[]{:S(2)}, u32[]{:S(2)}) collective-permute-start(bf16[9,2048]{1,0:T(8,128)(2,1)} %param.4), channel_id=1, source_target_pairs={{0,3},{1,2},{2,1},{3,0},{4,7},{5,6},{6,5},{7,4},{8,11},{9,10},{10,... | collective-permute-start | bytes 110600 | tf_op jit(solution)/shard_map/ppermute | solution.py:361
  11.2 9.8 %collective-permute-start.3 = (bf16[8,14976]{1,0:T(8,128)(2,1)S(1)}, bf16[8,14976]{1,0:T(8,128)(2,1)S(1)}, u32[]{:S(2)}, u32[]{:S(2)}) collective-permute-start(bf16[8,14976]{1,0:T(8,128)(2,1)S(1)} %shard_map.47._), channel_id=1, source_target_pairs={{0,4},{4,0},{8,12},{12,8},{1,5},{5,1},{9,13},{13,9},{2,6},{6,2},{1... | collective-permute-start | bytes 718856 | tf_op jit(solution)/shard_map/ppermute | solution.py:361
  21.1 14.6 %collective-permute-start.4 = (bf16[8,14976]{1,0:T(8,128)(2,1)S(1)}, bf16[8,14976]{1,0:T(8,128)(2,1)S(1)}, u32[]{:S(2)}, u32[]{:S(2)}) collective-permute-start(bf16[8,14976]{1,0:T(8,128)(2,1)S(1)} %add_convert_fusion._), channel_id=1, source_target_pairs={{0,12},{4,8},{8,4},{12,0},{1,13},{5,9},{9,5},{13,1},{2,14},{6,10},... | collective-permute-start | bytes 718856 | tf_op jit(solution)/shard_map/ppermute | solution.py:361
  23.5 12.2 %collective-permute-start.5 = (bf16[8,7552]{1,0:T(8,128)(2,1)S(1)}, bf16[8,7552]{1,0:T(8,128)(2,1)S(1)}, u32[]{:S(2)}, u32[]{:S(2)}) collective-permute-start(bf16[8,7552]{1,0:T(8,128)(2,1)S(1)} %get-tuple-element.12), channel_id=1, source_target_pairs={{0,4},{4,0},{8,12},{12,8},{1,5},{5,1},{9,13},{13,9},{2,6},{6,2},{1... | collective-permute-start | bytes 362504 | tf_op jit(solution)/shard_map/ppermute | solution.py:361
  24.2 19.6 %slice-start = ((s8[27262976]{0:T(1024)(128)(4,1)}), s8[4194304]{0:T(1024)(128)(4,1)S(1)}, s32[]{:S(2)}) async-start(s8[27262976]{0:T(1024)(128)(4,1)} %bitcast), calls=%async_computation | async-start | bytes 8388608
  24.2 19.6 %slice-start.1 = ((s8[27262976]{0:T(1024)(128)(4,1)}), s8[4194304]{0:T(1024)(128)(4,1)S(1)}, s32[]{:S(2)}) async-start(s8[27262976]{0:T(1024)(128)(4,1)} %bitcast), calls=%async_computation.1 | async-start | bytes 8388608
  24.2 19.6 %slice-start.2 = ((s8[27262976]{0:T(1024)(128)(4,1)}), s8[4194304]{0:T(1024)(128)(4,1)S(1)}, s32[]{:S(2)}) async-start(s8[27262976]{0:T(1024)(128)(4,1)} %bitcast), calls=%async_computation.2 | async-start | bytes 8388608
  24.2 19.6 %slice-start.3 = ((s8[27262976]{0:T(1024)(128)(4,1)}), s8[4194304]{0:T(1024)(128)(4,1)S(1)}, s32[]{:S(2)}) async-start(s8[27262976]{0:T(1024)(128)(4,1)} %bitcast), calls=%async_computation.3 | async-start | bytes 8388608
  27.8 16.0 %slice-start.4 = ((s8[27262976]{0:T(1024)(128)(4,1)}), s8[4194304]{0:T(1024)(128)(4,1)S(1)}, s32[]{:S(2)}) async-start(s8[27262976]{0:T(1024)(128)(4,1)} %bitcast), calls=%async_computation.4 | async-start | bytes 8388608
  27.8 16.0 %slice-start.5 = ((s8[27262976]{0:T(1024)(128)(4,1)}), s8[4194304]{0:T(1024)(128)(4,1)S(1)}, s32[]{:S(2)}) async-start(s8[27262976]{0:T(1024)(128)(4,1)} %bitcast), calls=%async_computation.5 | async-start | bytes 8388608
  27.8 16.0 %slice-start.6 = ((s8[27262976]{0:T(1024)(128)(4,1)}), s8[2097152]{0:T(1024)(128)(4,1)S(1)}, s32[]{:S(2)}) async-start(s8[27262976]{0:T(1024)(128)(4,1)} %bitcast), calls=%async_computation.6 | async-start | bytes 4194304
  27.9 7.9 %collective-permute-start.6 = (bf16[8,7552]{1,0:T(8,128)(2,1)S(1)}, bf16[8,7552]{1,0:T(8,128)(2,1)S(1)}, u32[]{:S(2)}, u32[]{:S(2)}) collective-permute-start(bf16[8,7552]{1,0:T(8,128)(2,1)S(1)} %shard_map.49._), channel_id=1, source_target_pairs={{0,4},{4,0},{8,12},{12,8},{1,5},{5,1},{9,13},{13,9},{2,6},{6,2},{1... | collective-permute-start | bytes 362504 | tf_op jit(solution)/shard_map/ppermute | solution.py:361
  35.9 7.8 %collective-permute-start.7 = (bf16[8,7552]{1,0:T(8,128)(2,1)S(1)}, bf16[8,7552]{1,0:T(8,128)(2,1)S(1)}, u32[]{:S(2)}, u32[]{:S(2)}) collective-permute-start(bf16[8,7552]{1,0:T(8,128)(2,1)S(1)} %shard_map.51.refs_0_), channel_id=1, source_target_pairs={{0,8},{4,12},{8,0},{12,4},{1,9},{5,13},{9,1},{13,5},{2,10},{6,14},... | collective-permute-start | bytes 362504 | tf_op jit(solution)/shard_map/ppermute | solution.py:361
  36.5 7.3 %collective-permute-start.9 = (bf16[8,7552]{1,0:T(8,128)(2,1)S(1)}, bf16[8,7552]{1,0:T(8,128)(2,1)S(1)}, u32[]{:S(2)}, u32[]{:S(2)}) collective-permute-start(bf16[8,7552]{1,0:T(8,128)(2,1)S(1)} %shard_map.51.refs_0_), channel_id=1, source_target_pairs={{0,4},{4,0},{8,12},{12,8},{1,5},{5,1},{9,13},{13,9},{2,6},{6,2},{1... | collective-permute-start | bytes 362504 | tf_op jit(solution)/shard_map/ppermute | solution.py:361
  43.7 4.9 %collective-permute-start.8 = (bf16[8,7552]{1,0:T(8,128)(2,1)S(1)}, bf16[8,7552]{1,0:T(8,128)(2,1)S(1)}, u32[]{:S(2)}, u32[]{:S(2)}) collective-permute-start(bf16[8,7552]{1,0:T(8,128)(2,1)S(1)} %collective-permute-done.7.refs_2_), channel_id=1, source_target_pairs={{0,4},{4,0},{8,12},{12,8},{1,5},{5,1},{9,13},{13,9},{2,6},{6,2},{1... | collective-permute-start | bytes 362504 | tf_op jit(solution)/shard_map/ppermute | solution.py:361
  49.9 1.9 %collective-permute-start.10 = (bf16[8,2304]{1,0:T(8,128)(2,1)S(1)}, bf16[8,2304]{1,0:T(8,128)(2,1)S(1)}, u32[]{:S(2)}, u32[]{:S(2)}) collective-permute-start(bf16[8,2304]{1,0:T(8,128)(2,1)S(1)} %get-tuple-element.14), channel_id=1, source_target_pairs={{0,1},{1,0},{2,3},{3,2},{4,5},{5,4},{6,7},{7,6},{8,9},{9,8},{10,11... | collective-permute-start | bytes 110600 | tf_op jit(solution)/shard_map/ppermute | solution.py:361
  49.9 4.0 %collective-permute-start.11 = (bf16[8,2304]{1,0:T(8,128)(2,1)S(1)}, bf16[8,2304]{1,0:T(8,128)(2,1)S(1)}, u32[]{:S(2)}, u32[]{:S(2)}) collective-permute-start(bf16[8,2304]{1,0:T(8,128)(2,1)S(1)} %get-tuple-element.15), channel_id=1, source_target_pairs={{0,2},{1,3},{2,0},{3,1},{4,6},{5,7},{6,4},{7,5},{8,10},{9,11},{10,... | collective-permute-start | bytes 110600 | tf_op jit(solution)/shard_map/ppermute | solution.py:361
  51.5 3.4 %collective-permute-start.12 = (bf16[8,2304]{1,0:T(8,128)(2,1)S(1)}, bf16[8,2304]{1,0:T(8,128)(2,1)S(1)}, u32[]{:S(2)}, u32[]{:S(2)}) collective-permute-start(bf16[8,2304]{1,0:T(8,128)(2,1)S(1)} %get-tuple-element.16), channel_id=1, source_target_pairs={{0,3},{1,2},{2,1},{3,0},{4,7},{5,6},{6,5},{7,4},{8,11},{9,10},{10,... | collective-permute-start | bytes 110600 | tf_op jit(solution)/shard_map/ppermute | solution.py:361

commit v24 on v22

--- a/solution.py
+++ b/solution.py
@@ -10,7 +10,7 @@
 MIB = 1 << 20
 STEP = 256
 COPY_STEP = 512
-IN_FLIGHT = 6
+IN_FLIGHT = 5
 DOWN_STEP = 512
 TOKEN_AXES = ("gy", "gz")
 IN_HBM = pl.BlockSpec(memory_space=pltpu.HBM)

time: 55 us -> 55 us (level)
  no operation moved by 1% of the time
where the time goes in v24:
time: 55 us; the launch traced here: 54.9 us
  Pallas kernels  30.4 us (55%)
  starting transfers between devices  14.1 us (26%)
  waiting for transfers between devices  9.97 us (18%)
    pallas_call x3, Pallas kernels, gate_up_stream(): pl.pallas_call(functools.partial(stream_kernel, width, blocks, distances)...  17.5 us
    ppermute x13, starting transfers between devices, swap(): return lax.ppermute(value, axes, [(i, i ^ distance) for i in range(size)])  14.1 us
    ppermute x13, waiting for transfers between devices, swap(): return lax.ppermute(value, axes, [(i, i ^ distance) for i in range(size)])  9.97 us
    pallas_call x1, Pallas kernels, fetch(): pl.pallas_call(functools.partial(fetch_kernel, width, distance), out_shap...  5.03 us
    pallas_call x2, Pallas kernels, down(): pl.pallas_call(functools.partial(down_kernel, before is None, rows, width...  4.92 us
    pallas_call x1, Pallas kernels, gate_up_held(): pl.pallas_call(held_kernel, out_shape=jax.ShapeDtypeStruct((8, packed_pai...  2.15 us
  transfers between devices with their start and end apart: 13, of which 6 were waited for; matrix products, arithmetic and copies ran while one was open for 0% of the time, Pallas kernels for 48%

profile of v24, /device:TPU:0, one launch (start us, length us, event | category | flops | bytes accessed | tf_op | source)
XLA Modules:
  0.0 54.9 jit_solution(6615855542082834064)
XLA Ops:
  0.0 0.0 copy-start
  0.0 2.9 %collective-permute-start.1 = (bf16[9,2048]{1,0:T(8,128)(2,1)}, bf16[9,2048]{1,0:T(8,128)(2,1)S(1)}, u32[]{:S(2)}, u32[]{:S(2)}) collective-permute-start(bf16[9,2048]{1,0:T(8,128)(2,1)} %param.4), channel_id=1, source_target_pairs={{0,2},{1,3},{2,0},{3,1},{4,6},{5,7},{6,4},{7,5},{8,10},{9,11},{10,... | collective-permute-start | bytes 110600 | tf_op jit(solution)/shard_map/ppermute | solution.py:336
  2.9 0.0 collective-permute-start
  2.9 0.2 collective-permute-start.2
  3.1 5.0 %shard_map.46.held = bf16[2,2048,1664]{2,1,0:T(8,128)(2,1)S(1)} custom-call(bf16[2048,6656]{1,0:T(8,128)(2,1)} %gate_ref.7, bf16[2048,6656]{1,0:T(8,128)(2,1)} %up_ref.7), custom_call_target="tpu_custom_call" | custom-call | bytes 1048576 | tf_op jit(solution)/shard_map/pallas_call | solution.py:86
  8.2 0.0 collective-permute-done.1
  8.2 0.0 collective-permute-done
  8.2 0.0 collective-permute-done.2
  8.2 0.0 copy-done
  8.2 0.1 pad_maximum_fusion.x_ref
  8.3 2.2 %shard_map.47._ = bf16[8,14976]{1,0:T(8,128)(2,1)S(1)} custom-call(bf16[36,2048]{1,0:T(8,128)(2,1)S(1)} %pad_maximum_fusion.x_ref, bf16[2,2048,1664]{2,1,0:T(8,128)(2,1)S(1)} %shard_map.46.held), custom_call_target="tpu_custom_call" | custom-call | bytes 1048576 | tf_op jit(solution)/shard_map/pallas_call | solution.py:120
  10.5 2.2 %collective-permute-start.3 = (bf16[8,14976]{1,0:T(8,128)(2,1)S(1)}, bf16[8,14976]{1,0:T(8,128)(2,1)S(1)}, u32[]{:S(2)}, u32[]{:S(2)}) collective-permute-start(bf16[8,14976]{1,0:T(8,128)(2,1)S(1)} %shard_map.47._), channel_id=1, source_target_pairs={{0,4},{4,0},{8,12},{12,8},{1,5},{5,1},{9,13},{13,9},{2,6},{6,2},{1... | collective-permute-start | bytes 718856 | tf_op jit(solution)/shard_map/ppermute | solution.py:336
  12.7 7.6 %shard_map.48 = (bf16[8,14976]{1,0:T(8,128)(2,1)S(1)}, bf16[8,7552]{1,0:T(8,128)(2,1)S(1)}) custom-call(bf16[36,2048]{1,0:T(8,128)(2,1)S(1)} %pad_maximum_fusion.x_ref, bf16[2048,6656]{1,0:T(8,128)(2,1)} %gate_ref.7, bf16[2048,6656]{1,0:T(8,128)(2,1)} %up_ref.7, bf16[8,14976]{1,0:T(8,128)(2,1)S(1)} %shard_map.47._), custom_call_target="tpu_custom_call" | custom-call | bytes 1048576 | tf_op jit(solution)/shard_map/pallas_call | solution.py:164
  20.3 0.0 collective-permute-done.3
  20.3 0.1 add_convert_fusion._
  20.4 2.5 %collective-permute-start.4 = (bf16[8,14976]{1,0:T(8,128)(2,1)S(1)}, bf16[8,14976]{1,0:T(8,128)(2,1)S(1)}, u32[]{:S(2)}, u32[]{:S(2)}) collective-permute-start(bf16[8,14976]{1,0:T(8,128)(2,1)S(1)} %add_convert_fusion._), channel_id=1, source_target_pairs={{0,12},{4,8},{8,4},{12,0},{1,13},{5,9},{9,5},{13,1},{2,14},{6,10},... | collective-permute-start | bytes 718856 | tf_op jit(solution)/shard_map/ppermute | solution.py:336
  22.9 0.6 %collective-permute-start.5 = (bf16[8,7552]{1,0:T(8,128)(2,1)S(1)}, bf16[8,7552]{1,0:T(8,128)(2,1)S(1)}, u32[]{:S(2)}, u32[]{:S(2)}) collective-permute-start(bf16[8,7552]{1,0:T(8,128)(2,1)S(1)} %get-tuple-element.12), channel_id=1, source_target_pairs={{0,4},{4,0},{8,12},{12,8},{1,5},{5,1},{9,13},{13,9},{2,6},{6,2},{1... | collective-permute-start | bytes 362504 | tf_op jit(solution)/shard_map/ppermute | solution.py:336
  23.5 0.0 slice-start
  23.5 0.0 slice-start.1
  23.5 0.0 slice-start.2
  23.5 0.0 slice-start.3
  23.5 3.6 %shard_map.49._ = bf16[8,7552]{1,0:T(8,128)(2,1)S(1)} custom-call(bf16[36,2048]{1,0:T(8,128)(2,1)S(1)} %pad_maximum_fusion.x_ref, bf16[2048,6656]{1,0:T(8,128)(2,1)} %gate_ref.7, bf16[2048,6656]{1,0:T(8,128)(2,1)} %up_ref.7, bf16[8,14976]{1,0:T(8,128)(2,1)S(1)} %add_convert_fusion._), custom_call_target="tpu_custom_call" | custom-call | bytes 1048576 | tf_op jit(solution)/shard_map/pallas_call | solution.py:164
  27.1 0.0 slice-start.4
  27.1 0.0 slice-start.5
  27.1 0.0 slice-start.6
  27.2 1.5 %collective-permute-start.6 = (bf16[8,7552]{1,0:T(8,128)(2,1)S(1)}, bf16[8,7552]{1,0:T(8,128)(2,1)S(1)}, u32[]{:S(2)}, u32[]{:S(2)}) collective-permute-start(bf16[8,7552]{1,0:T(8,128)(2,1)S(1)} %shard_map.49._), channel_id=1, source_target_pairs={{0,4},{4,0},{8,12},{12,8},{1,5},{5,1},{9,13},{13,9},{2,6},{6,2},{1... | collective-permute-start | bytes 362504 | tf_op jit(solution)/shard_map/ppermute | solution.py:336
  28.6 6.2 %shard_map.50.own = bf16[8,14976]{1,0:T(8,128)(2,1)S(1)} custom-call(bf16[36,2048]{1,0:T(8,128)(2,1)S(1)} %pad_maximum_fusion.x_ref, bf16[2048,6656]{1,0:T(8,128)(2,1)} %gate_ref.7, bf16[2048,6656]{1,0:T(8,128)(2,1)} %up_ref.7, bf16[8,7552]{1,0:T(8,128)(2,1)S(1)} %shard_map.49._), custom_call_target="tpu_custom_call" | custom-call | bytes 1048576 | tf_op jit(solution)/shard_map/pallas_call | solution.py:164
  34.9 0.0 collective-permute-done.5.gate_near
  34.9 0.1 collective-permute-done.6.up_near
  35.0 0.0 collective-permute-done.4.far
  35.0 0.1 shard_map.51.refs_0_
  35.2 0.6 %collective-permute-start.7 = (bf16[8,7552]{1,0:T(8,128)(2,1)S(1)}, bf16[8,7552]{1,0:T(8,128)(2,1)S(1)}, u32[]{:S(2)}, u32[]{:S(2)}) collective-permute-start(bf16[8,7552]{1,0:T(8,128)(2,1)S(1)} %shard_map.51.refs_0_), channel_id=1, source_target_pairs={{0,8},{4,12},{8,0},{12,4},{1,9},{5,13},{9,1},{13,5},{2,10},{6,14},... | collective-permute-start | bytes 362504 | tf_op jit(solution)/shard_map/ppermute | solution.py:336
  35.8 1.7 %collective-permute-start.9 = (bf16[8,7552]{1,0:T(8,128)(2,1)S(1)}, bf16[8,7552]{1,0:T(8,128)(2,1)S(1)}, u32[]{:S(2)}, u32[]{:S(2)}) collective-permute-start(bf16[8,7552]{1,0:T(8,128)(2,1)S(1)} %shard_map.51.refs_0_), channel_id=1, source_target_pairs={{0,4},{4,0},{8,12},{12,8},{1,5},{5,1},{9,13},{13,9},{2,6},{6,2},{1... | collective-permute-start | bytes 362504 | tf_op jit(solution)/shard_map/ppermute | solution.py:336
  37.4 5.5 %collective-permute-done.7.refs_2_ = bf16[8,7552]{1,0:T(8,128)(2,1)S(1)} collective-permute-done((bf16[8,7552]{1,0:T(8,128)(2,1)S(1)}, bf16[8,7552]{1,0:T(8,128)(2,1)S(1)}, u32[]{:S(2)}, u32[]{:S(2)}) %collective-permute-start.7) | collective-permute-done | bytes 120864 | tf_op jit(solution)/shard_map/ppermute | solution.py:336
  43.0 0.0 collective-permute-start.8
  43.0 0.1 collective-permute-done.9.refs_1_
  43.1 0.0 slice-done
  43.1 0.0 slice-done.1
  43.1 0.0 slice-done.2
  43.1 0.0 slice-done.3
  43.1 0.0 slice-done.4
  43.1 0.0 slice-done.5
  43.1 0.0 slice-done.6
  43.2 3.6 %shard_map.52.refs_1_ = f32[36,2048]{1,0:T(8,128)S(1)} custom-call(bf16[8,7552]{1,0:T(8,128)(2,1)S(1)} %shard_map.51.refs_0_, bf16[8,7552]{1,0:T(8,128)(2,1)S(1)} %collective-permute-done.9.refs_1_, bf16[8,7552]{1,0:T(8,128)(2,1)S(1)} %collective-permute-done.7.refs_2_, bf16[6656,2048]{1,0:T(8,128)(2,1)S(1)} %bitcast.1), custom_call_target="tpu_custom_call" | custom-call | bytes 1048576 | tf_op jit(solution)/shard_map/pallas_call | solution.py:300
  46.8 1.0 %collective-permute-done.8.refs_0_ = bf16[8,7552]{1,0:T(8,128)(2,1)S(1)} collective-permute-done((bf16[8,7552]{1,0:T(8,128)(2,1)S(1)}, bf16[8,7552]{1,0:T(8,128)(2,1)S(1)}, u32[]{:S(2)}, u32[]{:S(2)}) %collective-permute-start.8) | collective-permute-done | bytes 120864 | tf_op jit(solution)/shard_map/ppermute | solution.py:336
  47.8 1.3 %shard_map.53 = (f32[8,2304]{1,0:T(8,128)S(1)}, bf16[8,2304]{1,0:T(8,128)(2,1)S(1)}, bf16[8,2304]{1,0:T(8,128)(2,1)S(1)}, bf16[8,2304]{1,0:T(8,128)(2,1)S(1)}) custom-call(bf16[8,7552]{1,0:T(8,128)(2,1)S(1)} %collective-permute-done.8.refs_0_, f32[36,2048]{1,0:T(8,128)S(1)} %shard_map.52.refs_1_, bf16[6656,2048]{1,0:T(8,128)(2,1)S(1)} %bitcast.1), custom_call_target="tpu_custom_call" | custom-call | bytes 1048576 | tf_op jit(solution)/shard_map/pallas_call | solution.py:300
  49.1 0.1 collective-permute-start.10
  49.2 1.6 %collective-permute-start.11 = (bf16[8,2304]{1,0:T(8,128)(2,1)S(1)}, bf16[8,2304]{1,0:T(8,128)(2,1)S(1)}, u32[]{:S(2)}, u32[]{:S(2)}) collective-permute-start(bf16[8,2304]{1,0:T(8,128)(2,1)S(1)} %get-tuple-element.15), channel_id=1, source_target_pairs={{0,2},{1,3},{2,0},{3,1},{4,6},{5,7},{6,4},{7,5},{8,10},{9,11},{10,... | collective-permute-start | bytes 110600 | tf_op jit(solution)/shard_map/ppermute | solution.py:336
  50.8 0.3 collective-permute-start.12
  51.1 0.0 collective-permute-done.10.refs_1_
  51.1 2.2 %collective-permute-done.11.refs_2_ = bf16[8,2304]{1,0:T(8,128)(2,1)S(1)} collective-permute-done((bf16[8,2304]{1,0:T(8,128)(2,1)S(1)}, bf16[8,2304]{1,0:T(8,128)(2,1)S(1)}, u32[]{:S(2)}, u32[]{:S(2)}) %collective-permute-start.11) | collective-permute-done | bytes 36896 | tf_op jit(solution)/shard_map/ppermute | solution.py:336
  53.2 1.0 %collective-permute-done.12.refs_3_ = bf16[8,2304]{1,0:T(8,128)(2,1)S(1)} collective-permute-done((bf16[8,2304]{1,0:T(8,128)(2,1)S(1)}, bf16[8,2304]{1,0:T(8,128)(2,1)S(1)}, u32[]{:S(2)}, u32[]{:S(2)}) %collective-permute-start.12) | collective-permute-done | bytes 36896 | tf_op jit(solution)/shard_map/ppermute | solution.py:336
  54.2 0.7 %shard_map.54 = bf16[9,2048]{1,0:T(8,128)(2,1)} custom-call(f32[8,2304]{1,0:T(8,128)S(1)} %get-tuple-element.13.refs_0_, bf16[8,2304]{1,0:T(8,128)(2,1)S(1)} %collective-permute-done.10.refs_1_, bf16[8,2304]{1,0:T(8,128)(2,1)S(1)} %collective-permute-done.11.refs_2_, bf16[8,2304]{1,0:T(8,128)(2,1)S(1)} %collective-permute-done.12.refs_3_), custom_call_target="tpu_custom_call" | custom-call | bytes 1048576 | tf_op jit(solution)/shard_map/pallas_call | solution.py:324
  (1 shorter events, 0.0 us)
Async XLA Ops:
  0.0 8.2 %copy-start = (bf16[9,2048]{1,0:T(8,128)(2,1)S(1)}, bf16[9,2048]{1,0:T(8,128)(2,1)}, u32[]{:S(2)}) copy-start(bf16[9,2048]{1,0:T(8,128)(2,1)} %param.4) | copy-start | bytes 110596
  0.0 8.2 %collective-permute-start.1 = (bf16[9,2048]{1,0:T(8,128)(2,1)}, bf16[9,2048]{1,0:T(8,128)(2,1)S(1)}, u32[]{:S(2)}, u32[]{:S(2)}) collective-permute-start(bf16[9,2048]{1,0:T(8,128)(2,1)} %param.4), channel_id=1, source_target_pairs={{0,2},{1,3},{2,0},{3,1},{4,6},{5,7},{6,4},{7,5},{8,10},{9,11},{10,... | collective-permute-start | bytes 110600 | tf_op jit(solution)/shard_map/ppermute | solution.py:336
  2.9 5.2 %collective-permute-start = (bf16[9,2048]{1,0:T(8,128)(2,1)}, bf16[9,2048]{1,0:T(8,128)(2,1)S(1)}, u32[]{:S(2)}, u32[]{:S(2)}) collective-permute-start(bf16[9,2048]{1,0:T(8,128)(2,1)} %param.4), channel_id=1, source_target_pairs={{0,1},{1,0},{2,3},{3,2},{4,5},{5,4},{6,7},{7,6},{8,9},{9,8},{10,11... | collective-permute-start | bytes 110600 | tf_op jit(solution)/shard_map/ppermute | solution.py:336
  2.9 5.3 %collective-permute-start.2 = (bf16[9,2048]{1,0:T(8,128)(2,1)}, bf16[9,2048]{1,0:T(8,128)(2,1)S(1)}, u32[]{:S(2)}, u32[]{:S(2)}) collective-permute-start(bf16[9,2048]{1,0:T(8,128)(2,1)} %param.4), channel_id=1, source_target_pairs={{0,3},{1,2},{2,1},{3,0},{4,7},{5,6},{6,5},{7,4},{8,11},{9,10},{10,... | collective-permute-start | bytes 110600 | tf_op jit(solution)/shard_map/ppermute | solution.py:336
  10.5 9.9 %collective-permute-start.3 = (bf16[8,14976]{1,0:T(8,128)(2,1)S(1)}, bf16[8,14976]{1,0:T(8,128)(2,1)S(1)}, u32[]{:S(2)}, u32[]{:S(2)}) collective-permute-start(bf16[8,14976]{1,0:T(8,128)(2,1)S(1)} %shard_map.47._), channel_id=1, source_target_pairs={{0,4},{4,0},{8,12},{12,8},{1,5},{5,1},{9,13},{13,9},{2,6},{6,2},{1... | collective-permute-start | bytes 718856 | tf_op jit(solution)/shard_map/ppermute | solution.py:336
  20.4 14.6 %collective-permute-start.4 = (bf16[8,14976]{1,0:T(8,128)(2,1)S(1)}, bf16[8,14976]{1,0:T(8,128)(2,1)S(1)}, u32[]{:S(2)}, u32[]{:S(2)}) collective-permute-start(bf16[8,14976]{1,0:T(8,128)(2,1)S(1)} %add_convert_fusion._), channel_id=1, source_target_pairs={{0,12},{4,8},{8,4},{12,0},{1,13},{5,9},{9,5},{13,1},{2,14},{6,10},... | collective-permute-start | bytes 718856 | tf_op jit(solution)/shard_map/ppermute | solution.py:336
  22.9 12.0 %collective-permute-start.5 = (bf16[8,7552]{1,0:T(8,128)(2,1)S(1)}, bf16[8,7552]{1,0:T(8,128)(2,1)S(1)}, u32[]{:S(2)}, u32[]{:S(2)}) collective-permute-start(bf16[8,7552]{1,0:T(8,128)(2,1)S(1)} %get-tuple-element.12), channel_id=1, source_target_pairs={{0,4},{4,0},{8,12},{12,8},{1,5},{5,1},{9,13},{13,9},{2,6},{6,2},{1... | collective-permute-start | bytes 362504 | tf_op jit(solution)/shard_map/ppermute | solution.py:336
  23.5 19.6 %slice-start = ((s8[27262976]{0:T(1024)(128)(4,1)}), s8[4194304]{0:T(1024)(128)(4,1)S(1)}, s32[]{:S(2)}) async-start(s8[27262976]{0:T(1024)(128)(4,1)} %bitcast), calls=%async_computation | async-start | bytes 8388608
  23.5 19.6 %slice-start.1 = ((s8[27262976]{0:T(1024)(128)(4,1)}), s8[4194304]{0:T(1024)(128)(4,1)S(1)}, s32[]{:S(2)}) async-start(s8[27262976]{0:T(1024)(128)(4,1)} %bitcast), calls=%async_computation.1 | async-start | bytes 8388608
  23.5 19.6 %slice-start.2 = ((s8[27262976]{0:T(1024)(128)(4,1)}), s8[4194304]{0:T(1024)(128)(4,1)S(1)}, s32[]{:S(2)}) async-start(s8[27262976]{0:T(1024)(128)(4,1)} %bitcast), calls=%async_computation.2 | async-start | bytes 8388608
  23.5 19.6 %slice-start.3 = ((s8[27262976]{0:T(1024)(128)(4,1)}), s8[4194304]{0:T(1024)(128)(4,1)S(1)}, s32[]{:S(2)}) async-start(s8[27262976]{0:T(1024)(128)(4,1)} %bitcast), calls=%async_computation.3 | async-start | bytes 8388608
  27.1 16.0 %slice-start.4 = ((s8[27262976]{0:T(1024)(128)(4,1)}), s8[4194304]{0:T(1024)(128)(4,1)S(1)}, s32[]{:S(2)}) async-start(s8[27262976]{0:T(1024)(128)(4,1)} %bitcast), calls=%async_computation.4 | async-start | bytes 8388608
  27.1 16.0 %slice-start.5 = ((s8[27262976]{0:T(1024)(128)(4,1)}), s8[4194304]{0:T(1024)(128)(4,1)S(1)}, s32[]{:S(2)}) async-start(s8[27262976]{0:T(1024)(128)(4,1)} %bitcast), calls=%async_computation.5 | async-start | bytes 8388608
  27.1 16.0 %slice-start.6 = ((s8[27262976]{0:T(1024)(128)(4,1)}), s8[2097152]{0:T(1024)(128)(4,1)S(1)}, s32[]{:S(2)}) async-start(s8[27262976]{0:T(1024)(128)(4,1)} %bitcast), calls=%async_computation.6 | async-start | bytes 4194304
  27.2 7.9 %collective-permute-start.6 = (bf16[8,7552]{1,0:T(8,128)(2,1)S(1)}, bf16[8,7552]{1,0:T(8,128)(2,1)S(1)}, u32[]{:S(2)}, u32[]{:S(2)}) collective-permute-start(bf16[8,7552]{1,0:T(8,128)(2,1)S(1)} %shard_map.49._), channel_id=1, source_target_pairs={{0,4},{4,0},{8,12},{12,8},{1,5},{5,1},{9,13},{13,9},{2,6},{6,2},{1... | collective-permute-start | bytes 362504 | tf_op jit(solution)/shard_map/ppermute | solution.py:336
  35.2 7.8 %collective-permute-start.7 = (bf16[8,7552]{1,0:T(8,128)(2,1)S(1)}, bf16[8,7552]{1,0:T(8,128)(2,1)S(1)}, u32[]{:S(2)}, u32[]{:S(2)}) collective-permute-start(bf16[8,7552]{1,0:T(8,128)(2,1)S(1)} %shard_map.51.refs_0_), channel_id=1, source_target_pairs={{0,8},{4,12},{8,0},{12,4},{1,9},{5,13},{9,1},{13,5},{2,10},{6,14},... | collective-permute-start | bytes 362504 | tf_op jit(solution)/shard_map/ppermute | solution.py:336
  35.8 7.3 %collective-permute-start.9 = (bf16[8,7552]{1,0:T(8,128)(2,1)S(1)}, bf16[8,7552]{1,0:T(8,128)(2,1)S(1)}, u32[]{:S(2)}, u32[]{:S(2)}) collective-permute-start(bf16[8,7552]{1,0:T(8,128)(2,1)S(1)} %shard_map.51.refs_0_), channel_id=1, source_target_pairs={{0,4},{4,0},{8,12},{12,8},{1,5},{5,1},{9,13},{13,9},{2,6},{6,2},{1... | collective-permute-start | bytes 362504 | tf_op jit(solution)/shard_map/ppermute | solution.py:336
  43.0 4.9 %collective-permute-start.8 = (bf16[8,7552]{1,0:T(8,128)(2,1)S(1)}, bf16[8,7552]{1,0:T(8,128)(2,1)S(1)}, u32[]{:S(2)}, u32[]{:S(2)}) collective-permute-start(bf16[8,7552]{1,0:T(8,128)(2,1)S(1)} %collective-permute-done.7.refs_2_), channel_id=1, source_target_pairs={{0,4},{4,0},{8,12},{12,8},{1,5},{5,1},{9,13},{13,9},{2,6},{6,2},{1... | collective-permute-start | bytes 362504 | tf_op jit(solution)/shard_map/ppermute | solution.py:336
  49.1 1.9 %collective-permute-start.10 = (bf16[8,2304]{1,0:T(8,128)(2,1)S(1)}, bf16[8,2304]{1,0:T(8,128)(2,1)S(1)}, u32[]{:S(2)}, u32[]{:S(2)}) collective-permute-start(bf16[8,2304]{1,0:T(8,128)(2,1)S(1)} %get-tuple-element.14), channel_id=1, source_target_pairs={{0,1},{1,0},{2,3},{3,2},{4,5},{5,4},{6,7},{7,6},{8,9},{9,8},{10,11... | collective-permute-start | bytes 110600 | tf_op jit(solution)/shard_map/ppermute | solution.py:336
  49.2 4.0 %collective-permute-start.11 = (bf16[8,2304]{1,0:T(8,128)(2,1)S(1)}, bf16[8,2304]{1,0:T(8,128)(2,1)S(1)}, u32[]{:S(2)}, u32[]{:S(2)}) collective-permute-start(bf16[8,2304]{1,0:T(8,128)(2,1)S(1)} %get-tuple-element.15), channel_id=1, source_target_pairs={{0,2},{1,3},{2,0},{3,1},{4,6},{5,7},{6,4},{7,5},{8,10},{9,11},{10,... | collective-permute-start | bytes 110600 | tf_op jit(solution)/shard_map/ppermute | solution.py:336
  50.8 3.4 %collective-permute-start.12 = (bf16[8,2304]{1,0:T(8,128)(2,1)S(1)}, bf16[8,2304]{1,0:T(8,128)(2,1)S(1)}, u32[]{:S(2)}, u32[]{:S(2)}) collective-permute-start(bf16[8,2304]{1,0:T(8,128)(2,1)S(1)} %get-tuple-element.16), channel_id=1, source_target_pairs={{0,3},{1,2},{2,1},{3,0},{4,7},{5,6},{6,5},{7,4},{8,11},{9,10},{10,... | collective-permute-start | bytes 110600 | tf_op jit(solution)/shard_map/ppermute | solution.py:336
